TPU v7x, 32 devices: a whole 2x2x4 slice. The times are simulated.
32 devices in a mesh: dp: 4 (over y, core), expert: 8 (over z, x).
Axes of the slice: x: 2, y: 2, z: 4, core: 2. Of those that a mesh axis runs over, the one named last changes fastest.
Arguments:
- tokens: bfloat16 [4096, 2048], P(('dp', 'expert')), may hold values from -6 to 6
- cotangent: bfloat16 [4096, 2048], P(('dp', 'expert')), may hold values from -1.1953125 to 1.1953125
- routes: int32 [4096, 1], P(('dp', 'expert')), may hold values from 0 to 7; in each aligned block of 128 rows (0 to 127, 128 to 255, ...) at most 18 rows name the same one
- expert_gates: float32 [4096, 1], P(('dp', 'expert')), may hold values from 0.1 to 1
- gate_proj: bfloat16 [2048, 6144], P(None, 'expert'), may hold values from -0.125 to 0.125
- up_proj: bfloat16 [2048, 6144], P(None, 'expert'), may hold values from -0.125 to 0.125
- down_proj: bfloat16 [6144, 2048], P('expert'), may hold values from -0.21875 to 0.21875
Outputs:
- grad_input: bfloat16 [4096, 2048], P(('dp', 'expert'))
- grad_gate: float32 [2048, 6144], P('dp', 'expert')
- grad_up: float32 [2048, 6144], P('dp', 'expert')
- grad_down: float32 [6144, 2048], P('expert', 'dp')
Inputs may be any that keep to these rules, and one draw needn't show every extreme that they name: `routes`: each row names exactly one expert. Among the rows of one device no expert is named more than 18 times.
All inputs are finite; a program needn't handle non-finite values.
Results may differ from a plain program's by a relative error of at most 0.022.
Values may be sent and summed in bfloat16 or wider, within the bound.
No kernel may reach another device: no remote copies, remote signals or barrier semaphores. Data moves between devices by JAX's collectives and lax.ppermute only.
A program may use at most 64 MiB of HBM per device.

v0:
```python
import jax
import jax.numpy as jnp
from jax import lax
from jax.sharding import PartitionSpec as P

EXPERTS = 8
MOST = 18


def build_slots(routes, capacity):
    flat_routes = routes.reshape(-1)
    one_hot = (flat_routes[:, None] == jnp.arange(EXPERTS, dtype=jnp.int32)[None, :]).astype(
        jnp.int32
    )
    before = jnp.cumsum(one_hot, axis=0) - one_hot
    position = jnp.sum(before * one_hot, axis=1)
    return flat_routes * capacity + position


def body(tokens, cotangent, routes, expert_gates, gate_proj, up_proj, down_proj):
    tok_dev, model_dim = tokens.shape
    top_k = routes.shape[1]
    expert_devs = lax.axis_size("expert")
    group_size = expert_devs // EXPERTS
    capacity = MOST
    slot_total = EXPERTS * capacity
    slot_of = build_slots(routes, capacity)
    owners = jnp.arange(tok_dev * top_k, dtype=jnp.int32) // top_k
    slot_table = jnp.full((slot_total,), tok_dev, jnp.int32).at[slot_of].set(owners)
    slot_gate = jnp.zeros((slot_total,), jnp.float32).at[slot_of].set(expert_gates.reshape(-1))
    x_slots = jnp.take(tokens, slot_table, axis=0, mode="fill", fill_value=0)
    dy_slots = (
        jnp.take(cotangent, slot_table, axis=0, mode="fill", fill_value=0).astype(jnp.float32)
        * slot_gate[:, None]
    ).astype(jnp.bfloat16)

    def copies(values):
        spread = values.reshape(EXPERTS, 1, capacity, model_dim)
        return jnp.broadcast_to(spread, (EXPERTS, group_size, capacity, model_dim)).reshape(
            expert_devs, capacity, model_dim
        )

    x_recv, dy_recv = (
        lax.all_to_all(copies(x_slots), "expert", split_axis=0, concat_axis=0, tiled=True),
        lax.all_to_all(copies(dy_slots), "expert", split_axis=0, concat_axis=0, tiled=True),
    )
    in_rows = x_recv.reshape(expert_devs * capacity, model_dim)
    scaled = dy_recv.reshape(expert_devs * capacity, model_dim)
    pre_gate = jnp.dot(in_rows, gate_proj, preferred_element_type=jnp.float32)
    pre_up = jnp.dot(in_rows, up_proj, preferred_element_type=jnp.float32)
    gate_sig = jax.nn.sigmoid(pre_gate)
    hidden = (pre_gate * gate_sig * pre_up).astype(jnp.bfloat16)
    by_width = (((1,), (1,)), ((), ()))
    by_rows = (((0,), (0,)), ((), ()))
    d_hidden = lax.dot_general(scaled, down_proj, by_width, preferred_element_type=jnp.float32)
    d_gate = (d_hidden * pre_up * gate_sig * (1.0 + pre_gate * (1.0 - gate_sig))).astype(
        jnp.bfloat16
    )
    d_up = (d_hidden * pre_gate * gate_sig).astype(jnp.bfloat16)
    grad_down = lax.dot_general(hidden, scaled, by_rows, preferred_element_type=jnp.float32)
    grad_gate = lax.dot_general(in_rows, d_gate, by_rows, preferred_element_type=jnp.float32)
    grad_up = lax.dot_general(in_rows, d_up, by_rows, preferred_element_type=jnp.float32)
    grad_gate, grad_up, grad_down = (
        lax.psum_scatter(
            grad_gate.astype(jnp.bfloat16), "dp", scatter_dimension=0, tiled=True
        ).astype(jnp.float32),
        lax.psum_scatter(
            grad_up.astype(jnp.bfloat16), "dp", scatter_dimension=0, tiled=True
        ).astype(jnp.float32),
        lax.psum_scatter(
            grad_down.astype(jnp.bfloat16), "dp", scatter_dimension=1, tiled=True
        ).astype(jnp.float32),
    )
    joined_grads = jnp.concatenate([d_gate, d_up], 1)
    joined_proj = jnp.concatenate([gate_proj, up_proj], 1)
    partial_value = lax.dot_general(
        joined_grads, joined_proj, by_width, preferred_element_type=jnp.float32
    ).astype(jnp.bfloat16)
    returned = lax.all_to_all(
        partial_value.reshape(expert_devs, capacity, model_dim),
        "expert",
        split_axis=0,
        concat_axis=0,
        tiled=True,
    )
    summed = jnp.sum(
        returned.reshape(EXPERTS, group_size, capacity, model_dim).astype(jnp.float32), axis=1
    )
    summed = summed.reshape(slot_total, model_dim)
    grad_input = jnp.take(summed, slot_of, axis=0).reshape(tok_dev, top_k, model_dim).sum(axis=1)
    return (grad_input.astype(jnp.bfloat16), grad_gate, grad_up, grad_down)


def solution(mesh):
    in_specs = (
        P(("dp", "expert"), None),
        P(("dp", "expert"), None),
        P(("dp", "expert"), None),
        P(("dp", "expert"), None),
        P(None, "expert"),
        P(None, "expert"),
        P("expert", None),
    )
    out_specs = (P(("dp", "expert"), None), P("dp", "expert"), P("dp", "expert"), P("expert", "dp"))
    return jax.shard_map(body, mesh=mesh, in_specs=in_specs, out_specs=out_specs, check_vma=False)
```

profile of v0, /device:TPU:0, one launch (start us, length us, event | category | flops | bytes accessed | tf_op | source)
XLA Modules:
  0.0 208.3 jit_solution(14934135738454633604)
XLA Ops:
  10.8 3.5 %gather_fusion.1 = bf16[144,2048]{1,0:T(8,128)(2,1)} fusion(bf16[128,2048]{1,0:T(8,128)(2,1)} %param.10, s32[1024]{0:T(1024)S(1)} %pad_clamp_fusion.1), kind=kCustom, calls=%fused_computation.clone | custom fusion | bytes 1180224 | tf_op jit(solution)/shard_map/jit(_take)/gather | solution.py:33
  15.4 2.2 %multiply_convert_fusion = bf16[144,2048]{1,0:T(8,128)(2,1)} fusion(bf16[144,2048]{1,0:T(8,128)(2,1)} %gather_fusion.1, f32[144]{0:T(256)S(1)} %scatter_custom_fusion.1, pred[144]{0:T(512)(128)(4,1)S(1)} %compare_and_fusion), kind=kLoop, calls=%fused_computation.13 | loop fusion | flops 1179648 | bytes 1180368 | tf_op jit(solution)/shard_map/convert_element_type | solution.py:35
  19.7 7.3 %all-to-all-start = ((bf16[8,18,2048]{2,1,0:T(8,128)(2,1)}), bf16[8,18,2048]{2,1,0:T(8,128)(2,1)}, u32[]{:S(2)}, u32[]{:S(2)}) async-start(bf16[8,18,2048]{2,1,0:T(8,128)(2,1)} %reshape_reshape.6), calls=%async_computation | async-start | bytes 1572864 | tf_op jit(solution)/shard_map/all_to_all | solution.py:45
  27.0 3.5 %gather_fusion.2 = bf16[144,2048]{1,0:T(8,128)(2,1)} fusion(bf16[128,2048]{1,0:T(8,128)(2,1)} %param.9, s32[1024]{0:T(1024)S(1)} %pad_clamp_fusion.1), kind=kCustom, calls=%fused_computation.1.clone | custom fusion | bytes 1180224 | tf_op jit(solution)/shard_map/jit(_take)/gather | solution.py:31
  34.6 12.7 %all-to-all-done = bf16[8,18,2048]{2,1,0:T(8,128)(2,1)} async-done(((bf16[8,18,2048]{2,1,0:T(8,128)(2,1)}), bf16[8,18,2048]{2,1,0:T(8,128)(2,1)}, u32[]{:S(2)}, u32[]{:S(2)}) %all-to-all-start) | async-done | bytes 589856 | tf_op jit(solution)/shard_map/all_to_all | solution.py:45
  47.3 4.2 %all-to-all-start.1 = ((bf16[8,18,2048]{2,1,0:T(8,128)(2,1)}), bf16[8,18,2048]{2,1,0:T(8,128)(2,1)}, u32[]{:S(2)}, u32[]{:S(2)}) async-start(bf16[8,18,2048]{2,1,0:T(8,128)(2,1)} %reshape_reshape.7), calls=%async_computation.1 | async-start | bytes 1572864 | tf_op jit(solution)/shard_map/all_to_all | solution.py:44
  51.5 2.1 %reshape.54 = bf16[144,2048]{1,0:T(8,128)(2,1)} reshape(bf16[8,18,2048]{2,1,0:T(8,128)(2,1)} %all-to-all-done) | data formatting | bytes 1179648 | tf_op jit(solution)/shard_map/reshape | solution.py:48
  53.7 3.0 %fusion.18 = f32[144,768]{1,0:T(8,128)} fusion(bf16[144,2048]{1,0:T(8,128)(2,1)} %reshape.54, bf16[768,2048]{1,0:T(8,128)(2,1)S(1)} %copy-done), kind=kOutput, calls=%fused_computation.40 | convolution fusion | flops 452984832 | bytes 4177920 | tf_op jit(solution)/shard_map/dot_general | solution.py:55
  56.7 14.7 %all-to-all-done.1 = bf16[8,18,2048]{2,1,0:T(8,128)(2,1)} async-done(((bf16[8,18,2048]{2,1,0:T(8,128)(2,1)}), bf16[8,18,2048]{2,1,0:T(8,128)(2,1)}, u32[]{:S(2)}, u32[]{:S(2)}) %all-to-all-start.1) | async-done | bytes 589856 | tf_op jit(solution)/shard_map/all_to_all | solution.py:44
  71.4 2.1 %reshape.55 = bf16[144,2048]{1,0:T(8,128)(2,1)} reshape(bf16[8,18,2048]{2,1,0:T(8,128)(2,1)} %all-to-all-done.1) | data formatting | bytes 1179648 | tf_op jit(solution)/shard_map/reshape | solution.py:47
  73.5 2.8 %fusion.19 = f32[144,768]{1,0:T(8,128)S(1)} fusion(bf16[144,2048]{1,0:T(8,128)(2,1)} %reshape.55, bf16[2048,768]{1,0:T(8,128)(2,1)} %param.14), kind=kOutput, calls=%fused_computation.41 | convolution fusion | flops 452984832 | bytes 4177920 | tf_op jit(solution)/shard_map/dot_general | solution.py:50
  78.3 2.8 %convolution_convert_fusion = bf16[768,2048]{1,0:T(8,128)(2,1)} fusion(bf16[144,2048]{1,0:T(8,128)(2,1)S(1)} %copy-done.2, f32[144,768]{1,0:T(8,128)S(1)} %fusion.19, f32[144,768]{1,0:T(8,128)S(1)} %get-tuple-element.9), kind=kOutput, calls=%fused_computation.9 | convolution fusion | flops 455221248 | bytes 4620288 | tf_op jit(solution)/shard_map/dot_general | solution.py:60
  81.1 3.8 %convolution_convert_fusion.2 = bf16[2048,768]{1,0:T(8,128)(2,1)} fusion(bf16[144,2048]{1,0:T(8,128)(2,1)} %reshape.55, bf16[144,768]{1,0:T(8,128)(2,1)S(1)} %get-tuple-element.7), kind=kOutput, calls=%fused_computation.11 | convolution fusion | flops 454557696 | bytes 3956736 | tf_op jit(solution)/shard_map/dot_general | solution.py:61
  85.0 4.0 %convolution_convert_fusion.1 = bf16[2048,768]{1,0:T(8,128)(2,1)} fusion(bf16[144,2048]{1,0:T(8,128)(2,1)} %reshape.55, bf16[144,768]{1,0:T(8,128)(2,1)} %get-tuple-element.8), kind=kOutput, calls=%fused_computation.10 | convolution fusion | flops 454557696 | bytes 3956736 | tf_op jit(solution)/shard_map/dot_general | solution.py:62
  88.9 6.2 %fusion.4 = bf16[144,2048]{1,0:T(8,128)(2,1)} fusion(bf16[2048,768]{1,0:T(8,128)(2,1)} %param.14, bf16[2048,768]{1,0:T(8,128)(2,1)} %param.13, bf16[144,768]{1,0:T(8,128)(2,1)} %get-tuple-element.8, bf16[144,768]{1,0:T(8,128)(2,1)S(1)} %get-tuple-element.7), kind=kOutput, calls=%fused_computation.12 | convolution fusion | flops 919732224 | bytes 7323648 | tf_op jit(solution)/shard_map/dot_general | solution.py:76
  97.3 4.2 %all-to-all-start.2 = ((bf16[8,18,2048]{2,1,0:T(8,128)(2,1)}), bf16[8,18,2048]{2,1,0:T(8,128)(2,1)}, u32[]{:S(2)}, u32[]{:S(2)}) async-start(bf16[8,18,2048]{2,1,0:T(8,128)(2,1)} %reshape.56), calls=%async_computation.2 | async-start | bytes 1572864 | tf_op jit(solution)/shard_map/all_to_all | solution.py:79
  101.5 20.2 %all-to-all-done.2 = bf16[8,18,2048]{2,1,0:T(8,128)(2,1)} async-done(((bf16[8,18,2048]{2,1,0:T(8,128)(2,1)}), bf16[8,18,2048]{2,1,0:T(8,128)(2,1)}, u32[]{:S(2)}, u32[]{:S(2)}) %all-to-all-start.2) | async-done | bytes 589856 | tf_op jit(solution)/shard_map/all_to_all | solution.py:79
  121.7 2.1 %reshape.60 = bf16[144,2048]{1,0:T(8,128)(2,1)} reshape(bf16[8,18,2048]{2,1,0:T(8,128)(2,1)} %all-to-all-done.2) | data formatting | bytes 1179648 | tf_op jit(solution)/shard_map/reshape | solution.py:89
  123.8 3.4 %gather_fusion = bf16[128,2048]{1,0:T(8,128)(2,1)} fusion(bf16[144,2048]{1,0:T(8,128)(2,1)} %reshape.60, s32[1024]{0:T(1024)S(1)} %pad_clamp_fusion), kind=kCustom, calls=%fused_computation.2 | custom fusion | bytes 1049088 | tf_op jit(solution)/shard_map/jit(_take)/gather | solution.py:90
  129.2 2.6 %convert_element_type.57 = f32[768,512]{1,0:T(8,128)} convert(bf16[768,512]{1,0:T(8,128)(2,1)} %reduce-scatter.8.cloned.1.call-done) | non-fusion elementwise | flops 393216 | bytes 2359296 | tf_op jit(solution)/shard_map/convert_element_type | solution.py:72
  131.8 27.0 %reduce-scatter.4.cloned.1.call-done = bf16[512,768]{1,0:T(8,128)(2,1)} async-done(((bf16[2048,768]{1,0:T(8,128)(2,1)}), bf16[512,768]{1,0:T(8,128)(2,1)}) %reduce-scatter.4.cloned.1.call-update) | async-done | bytes 786448 | tf_op jit(solution)/shard_map/reduce_scatter | solution.py:64
  158.8 2.4 %convert_element_type.52 = f32[512,768]{1,0:T(8,128)} convert(bf16[512,768]{1,0:T(8,128)(2,1)} %reduce-scatter.4.cloned.1.call-done) | non-fusion elementwise | flops 393216 | bytes 2359296 | tf_op jit(solution)/shard_map/convert_element_type | solution.py:66
  161.2 38.1 %reduce-scatter.6.cloned.1.call-done = bf16[512,768]{1,0:T(8,128)(2,1)} async-done(((bf16[2048,768]{1,0:T(8,128)(2,1)}), bf16[512,768]{1,0:T(8,128)(2,1)}) %reduce-scatter.6.cloned.1.call-update) | async-done | bytes 786448 | tf_op jit(solution)/shard_map/reduce_scatter | solution.py:67
  199.3 2.4 %convert_element_type.54 = f32[512,768]{1,0:T(8,128)} convert(bf16[512,768]{1,0:T(8,128)(2,1)} %reduce-scatter.6.cloned.1.call-done) | non-fusion elementwise | flops 393216 | bytes 2359296 | tf_op jit(solution)/shard_map/convert_element_type | solution.py:69
  (34 shorter events, 17.2 us)
Async XLA Ops:
  7.2 46.5 %copy-start = (bf16[768,2048]{1,0:T(8,128)(2,1)S(1)}, bf16[768,2048]{1,0:T(8,128)(2,1)}, u32[]{:S(2)}) copy-start(bf16[768,2048]{1,0:T(8,128)(2,1)} %param.15) | copy-start | bytes 9437188
  19.7 27.5 %all-to-all-start = ((bf16[8,18,2048]{2,1,0:T(8,128)(2,1)}), bf16[8,18,2048]{2,1,0:T(8,128)(2,1)}, u32[]{:S(2)}, u32[]{:S(2)}) async-start(bf16[8,18,2048]{2,1,0:T(8,128)(2,1)} %reshape_reshape.6), calls=%async_computation | async-start | bytes 1572864 | tf_op jit(solution)/shard_map/all_to_all | solution.py:45
  47.3 24.1 %all-to-all-start.1 = ((bf16[8,18,2048]{2,1,0:T(8,128)(2,1)}), bf16[8,18,2048]{2,1,0:T(8,128)(2,1)}, u32[]{:S(2)}, u32[]{:S(2)}) async-start(bf16[8,18,2048]{2,1,0:T(8,128)(2,1)} %reshape_reshape.7), calls=%async_computation.1 | async-start | bytes 1572864 | tf_op jit(solution)/shard_map/all_to_all | solution.py:44
  51.5 77.7 %reduce-scatter.8.cloned.1.call-start = ((), (), s32[]{:S(2)}) async-start(), calls=%async_computation.8 | async-start | bytes 3932160 | tf_op jit(solution)/shard_map/reduce_scatter | solution.py:70
  73.5 2.9 %copy-start.1 = (bf16[144,2048]{1,0:T(8,128)(2,1)S(1)}, bf16[144,2048]{1,0:T(8,128)(2,1)}, u32[]{:S(2)}) copy-start(bf16[144,2048]{1,0:T(8,128)(2,1)} %reshape.55) | copy-start | bytes 1769476
  73.5 2.9 %copy-start.3 = (f32[144,768]{1,0:T(8,128)S(1)}, f32[144,768]{1,0:T(8,128)}, u32[]{:S(2)}) copy-start(f32[144,768]{1,0:T(8,128)} %fusion.18) | copy-start | bytes 1327108
  73.5 3.3 %copy-start.4 = (bf16[2048,768]{1,0:T(8,128)(2,1)S(1)}, bf16[2048,768]{1,0:T(8,128)(2,1)}, u32[]{:S(2)}) copy-start(bf16[2048,768]{1,0:T(8,128)(2,1)} %param.13) | copy-start | bytes 9437188
  76.8 1.5 copy-start.2
  81.1 77.7 %reduce-scatter.4.cloned.1.call-start = ((), (), s32[]{:S(2)}) async-start(), calls=%async_computation.6 | async-start | bytes 3932160 | tf_op jit(solution)/shard_map/reduce_scatter | solution.py:64
  84.9 114.4 %reduce-scatter.6.cloned.1.call-start = ((), (), s32[]{:S(2)}) async-start(), calls=%async_computation.7 | async-start | bytes 3932160 | tf_op jit(solution)/shard_map/reduce_scatter | solution.py:67
  97.3 24.4 %all-to-all-start.2 = ((bf16[8,18,2048]{2,1,0:T(8,128)(2,1)}), bf16[8,18,2048]{2,1,0:T(8,128)(2,1)}, u32[]{:S(2)}, u32[]{:S(2)}) async-start(bf16[8,18,2048]{2,1,0:T(8,128)(2,1)} %reshape.56), calls=%async_computation.2 | async-start | bytes 1572864 | tf_op jit(solution)/shard_map/all_to_all | solution.py:79
Sparse Core Ops, SparseCore 0:
  81.2 36.8 reduce-scatter.7
  120.8 37.9 reduce-scatter.3
  161.4 37.9 reduce-scatter.5
where the time goes:
time: 209 us; the launch traced here: 208 us
  waiting for transfers between devices  113 us (54%)
  local copies, waits for them, and re-layouts  25.6 us (12%)
  matrix products  24 us (11%)
  other arithmetic  16.2 us (8%)
  starting transfers between devices  15.8 us (8%)
  between operations  13.9 us (7%)
    reduce_scatter x1, waiting for transfers between devices, body(): lax.psum_scatter(grad_up.astype(jnp.bfloat16), 'dp', scatter_dimension=0,...  38.1 us
    reduce_scatter x1, waiting for transfers between devices, body(): lax.psum_scatter(grad_gate.astype(jnp.bfloat16), 'dp', scatter_dimension=...  27 us
    all_to_all x1, waiting for transfers between devices, body(): lax.all_to_all(partial_value.reshape(expert_devs, capacity, model_dim), '...  20.2 us
    all_to_all x1, waiting for transfers between devices, body(): lax.all_to_all(copies(x_slots), 'expert', split_axis=0, concat_axis=0, ti...  14.7 us
    all_to_all x1, waiting for transfers between devices, body(): lax.all_to_all(copies(dy_slots), 'expert', split_axis=0, concat_axis=0, t...  12.7 us
    convert_element_type x3, other arithmetic, body(): grad_gate, grad_up, grad_down = (lax.psum_scatter(grad_gate.astype(jnp.bf...  7.34 us
    all_to_all x1, starting transfers between devices, body(): lax.all_to_all(copies(dy_slots), 'expert', split_axis=0, concat_axis=0, t...  7.25 us
    dot_general x1, matrix products, body(): lax.dot_general(joined_grads, joined_proj, by_width, preferred_element_ty...  6.2 us
  transfers between devices with their start and end apart: 6, of which 5 were waited for; matrix products, arithmetic and copies ran while one was open for 20% of the time, Pallas kernels for 0%

commit v1 on v0

--- a/solution.py
+++ b/solution.py
@@ -1,10 +1,14 @@
 import jax
 import jax.numpy as jnp
 from jax import lax
+from jax.experimental import pallas as pl
+from jax.experimental.pallas import tpu as pltpu
 from jax.sharding import PartitionSpec as P
 
 EXPERTS = 8
 MOST = 18
+ROWS = 16
+VMEM_LIMIT = 48 * 1024 * 1024
 
 
 def build_slots(routes, capacity):
@@ -17,7 +21,7 @@
     return flat_routes * capacity + position
 
 
-def body(tokens, cotangent, routes, expert_gates, gate_proj, up_proj, down_proj):
+def scatter_body(tokens, cotangent, routes, expert_gates, gate_proj, up_proj, down_proj):
     tok_dev, model_dim = tokens.shape
     top_k = routes.shape[1]
     expert_devs = lax.axis_size("expert")
@@ -91,6 +95,357 @@
     return (grad_input.astype(jnp.bfloat16), grad_gate, grad_up, grad_down)
 
 
+def cut(width):
+    pieces = ROWS // (MOST - ROWS)
+    return pieces, width // pieces
+
+
+def params(limit=VMEM_LIMIT):
+    return pltpu.CompilerParams(vmem_limit_bytes=limit)
+
+
+def cost(flops, moved):
+    return pl.CostEstimate(flops=flops, bytes_accessed=moved, transcendentals=0)
+
+
+def whole(count):
+    return [pl.BlockSpec(memory_space=pltpu.VMEM)] * count
+
+
+def slot_masks(me, routes, blocks, width):
+    tokens = routes.shape[1]
+    pieces, _ = cut(width)
+    experts = lax.broadcasted_iota(jnp.int32, (EXPERTS, tokens), 0)
+    named = jnp.where(experts == routes, 1.0, 0.0)
+    earlier = lax.broadcasted_iota(jnp.int32, (tokens, tokens), 0) < lax.broadcasted_iota(
+        jnp.int32, (tokens, tokens), 1
+    )
+    before = jnp.dot(
+        named.astype(jnp.bfloat16),
+        jnp.where(earlier, 1.0, 0.0).astype(jnp.bfloat16),
+        preferred_element_type=jnp.float32,
+    )
+    position = jnp.sum(before * named, axis=0, keepdims=True).astype(jnp.int32)
+    slot = lax.broadcasted_iota(jnp.int32, (blocks * ROWS, tokens), 0)
+    row = slot % ROWS
+    mine = (slot // ROWS) ^ me == routes
+    main = mine & (position == row)
+    spill = mine & (position == ROWS + row // pieces)
+    return main, spill, row % pieces
+
+
+def ones(mask):
+    return jnp.where(mask, 1.0, 0.0).astype(jnp.bfloat16)
+
+
+def send_kernel(scaled, blocks, me_ref, routes_ref, gates_ref, values_ref, *outs):
+    tokens, width = values_ref.shape
+    pieces, step = cut(width)
+    main, spill, piece = slot_masks(me_ref[0], routes_ref[...], blocks, width)
+    rows = jnp.dot(ones(main), values_ref[...], preferred_element_type=jnp.float32)
+    extra = jnp.zeros((blocks * ROWS, step), jnp.float32)
+    for at in range(pieces):
+        extra += jnp.dot(
+            ones(spill & (piece == at)),
+            values_ref[:, at * step : (at + 1) * step],
+            preferred_element_type=jnp.float32,
+        )
+    if scaled:
+        gates = gates_ref[...]
+        rows = rows * jnp.sum(jnp.where(main, gates, 0.0), axis=1, keepdims=True)
+        extra = extra * jnp.sum(jnp.where(spill, gates, 0.0), axis=1, keepdims=True)
+    rows = rows.astype(jnp.bfloat16)
+    extra = extra.astype(jnp.bfloat16)
+    for block in range(blocks):
+        part = slice(block * ROWS, (block + 1) * ROWS)
+        outs[block][:, :width] = rows[part]
+        outs[block][:, width:] = extra[part]
+
+
+def pack(scaled, blocks, me, routes, gates, values):
+    tokens, width = values.shape
+    _, step = cut(width)
+    shape = jax.ShapeDtypeStruct((ROWS, width + step), jnp.bfloat16)
+
+    def kernel(*refs):
+        send_kernel(scaled, blocks, *refs)
+
+    return pl.pallas_call(
+        kernel,
+        out_shape=[shape] * blocks,
+        in_specs=[pl.BlockSpec(memory_space=pltpu.SMEM)] + whole(3),
+        out_specs=whole(blocks),
+        compiler_params=params(),
+        cost_estimate=cost(4 * blocks * ROWS * tokens * width, 4 * tokens * width),
+        name="pack",
+    )(me, routes, gates, values)
+
+
+def spill_picks(blocks, pieces, at):
+    slot = lax.broadcasted_iota(jnp.int32, (blocks * (MOST - ROWS), blocks * ROWS), 0)
+    row = lax.broadcasted_iota(jnp.int32, (blocks * (MOST - ROWS), blocks * ROWS), 1)
+    return ones(row == slot * pieces + at)
+
+
+def unpack(blocks, width):
+    tail = []
+    extra = jnp.concatenate([block[:, width:] for block in blocks], 0)
+    pieces, _ = cut(width)
+    for at in range(pieces):
+        tail.append(
+            jnp.dot(
+                spill_picks(len(blocks), pieces, at), extra, preferred_element_type=jnp.float32
+            ).astype(jnp.bfloat16)
+        )
+    return jnp.concatenate([block[:, :width] for block in blocks], 0), jnp.concatenate(tail, 1)
+
+
+def join(blocks):
+    count = len(blocks)
+    width = blocks[0].shape[1] * (ROWS // (MOST - ROWS)) // (ROWS // (MOST - ROWS) + 1)
+    slots = count * MOST
+
+    def kernel(*refs):
+        rows, extra = unpack(refs[:count], width)
+        refs[count][: count * ROWS, :] = rows
+        refs[count][count * ROWS :, :] = extra
+
+    return pl.pallas_call(
+        kernel,
+        out_shape=jax.ShapeDtypeStruct((slots, width), jnp.bfloat16),
+        in_specs=whole(count),
+        out_specs=pl.BlockSpec(memory_space=pltpu.VMEM),
+        compiler_params=params(),
+        cost_estimate=cost(0, 4 * slots * width),
+        name="join",
+    )(*blocks)
+
+
+BY_WIDTH = (((1,), (1,)), ((), ()))
+BY_ROWS = (((0,), (0,)), ((), ()))
+
+
+def dot(left, right, dims=(((1,), (0,)), ((), ()))):
+    return lax.dot_general(left, right, dims, preferred_element_type=jnp.float32)
+
+
+def slice_grads(rows, scaled, gate_cols, up_cols, down_rows):
+    pre_gate = dot(rows, gate_cols)
+    pre_up = dot(rows, up_cols)
+    d_hidden = dot(scaled, down_rows, BY_WIDTH)
+    sig = jax.nn.sigmoid(pre_gate)
+    silu = pre_gate * sig
+    hidden = (silu * pre_up).astype(jnp.bfloat16)
+    d_gate = (d_hidden * pre_up * sig * (1.0 + pre_gate * (1.0 - sig))).astype(jnp.bfloat16)
+    d_up = (d_hidden * silu).astype(jnp.bfloat16)
+    return hidden, d_gate, d_up
+
+
+def weight_specs(width, tile):
+    return [
+        pl.BlockSpec((width, tile), lambda i: (0, i)),
+        pl.BlockSpec((width, tile), lambda i: (0, i)),
+        pl.BlockSpec((tile, width), lambda i: (i, 0)),
+    ]
+
+
+def back(blocks, tile, rows, scaled, gate_proj, up_proj, down_proj):
+    slots, width = rows.shape
+    hid = gate_proj.shape[1]
+    pieces, step = cut(width)
+    extras = blocks * (MOST - ROWS)
+
+    def kernel(x_ref, dy_ref, gate_ref, up_ref, down_ref, *rest):
+        outs, total = rest[:blocks], rest[blocks]
+        gate, up = gate_ref[...], up_ref[...]
+        _, d_gate, d_up = slice_grads(x_ref[...], dy_ref[...], gate, up, down_ref[...])
+        part = dot(d_gate, gate, BY_WIDTH) + dot(d_up, up, BY_WIDTH)
+
+        @pl.when(pl.program_id(0) == 0)
+        def _():
+            total[...] = part
+
+        @pl.when(pl.program_id(0) > 0)
+        def _():
+            total[...] += part
+
+        @pl.when(pl.program_id(0) == hid // tile - 1)
+        def _():
+            done = total[...].astype(jnp.bfloat16)
+            extra = jnp.zeros((blocks * ROWS, step), jnp.float32)
+            for at in range(pieces):
+                extra += dot(
+                    spill_picks(blocks, pieces, at),
+                    done[blocks * ROWS :, at * step : (at + 1) * step],
+                    BY_ROWS,
+                )
+            extra = extra.astype(jnp.bfloat16)
+            for block in range(blocks):
+                part_of = slice(block * ROWS, (block + 1) * ROWS)
+                outs[block][:, :width] = done[part_of]
+                outs[block][:, width:] = extra[part_of]
+
+    shape = jax.ShapeDtypeStruct((ROWS, width + step), jnp.bfloat16)
+    same = pl.BlockSpec((slots, width), lambda i: (0, 0))
+    return pl.pallas_call(
+        kernel,
+        grid=(hid // tile,),
+        out_shape=[shape] * blocks,
+        in_specs=[same, same] + weight_specs(width, tile),
+        out_specs=[pl.BlockSpec((ROWS, width + step), lambda i: (0, 0))] * blocks,
+        scratch_shapes=[pltpu.VMEM((slots, width), jnp.float32)],
+        compiler_params=params(),
+        cost_estimate=cost(10 * slots * width * hid, 6 * width * hid),
+        name="back",
+    )(rows, scaled, gate_proj, up_proj, down_proj)
+
+
+def weight_grads(tile, part, rows, scaled, gate_proj, up_proj, down_proj):
+    groups = len(rows)
+    slots, width = rows[0].shape
+    hid = gate_proj.shape[1]
+    own = width // groups
+    total = groups * slots
+
+    def kernel(part_ref, *refs):
+        sources = refs[: 2 * groups]
+        gate_ref, up_ref, down_ref, d_gate_ref, d_up_ref, d_down_ref = refs[
+            2 * groups : 2 * groups + 6
+        ]
+        x_all, dy_all, arrived = refs[2 * groups + 6 :]
+
+        @pl.when(pl.program_id(0) == 0)
+        def _():
+            copies = []
+            for at in range(2 * groups):
+                target = x_all if at < groups else dy_all
+                begin = (at % groups) * slots
+                copies.append(
+                    pltpu.make_async_copy(
+                        sources[at], target.at[begin : begin + slots, :], arrived.at[at]
+                    )
+                )
+            for copy in copies:
+                copy.start()
+            for copy in copies:
+                copy.wait()
+
+        hidden, d_gate, d_up = slice_grads(
+            x_all[...], dy_all[...], gate_ref[...], up_ref[...], down_ref[...]
+        )
+        columns = pl.ds(pl.multiple_of(part_ref[0] * own, own), own)
+        both = dot(x_all[:, columns], jnp.concatenate([d_gate, d_up], 1), BY_ROWS)
+        d_gate_ref[...] = both[:, :tile]
+        d_up_ref[...] = both[:, tile:]
+        d_down_ref[...] = dot(hidden, dy_all[:, columns], BY_ROWS)
+
+    return pl.pallas_call(
+        kernel,
+        grid=(hid // tile,),
+        out_shape=[
+            jax.ShapeDtypeStruct((own, hid), jnp.float32),
+            jax.ShapeDtypeStruct((own, hid), jnp.float32),
+            jax.ShapeDtypeStruct((hid, own), jnp.float32),
+        ],
+        in_specs=[pl.BlockSpec(memory_space=pltpu.SMEM)]
+        + [pl.BlockSpec(memory_space=pl.ANY)] * (2 * groups)
+        + weight_specs(width, tile),
+        out_specs=[
+            pl.BlockSpec((own, tile), lambda i: (0, i)),
+            pl.BlockSpec((own, tile), lambda i: (0, i)),
+            pl.BlockSpec((tile, own), lambda i: (i, 0)),
+        ],
+        scratch_shapes=[
+            pltpu.VMEM((total, width), jnp.bfloat16),
+            pltpu.VMEM((total, width), jnp.bfloat16),
+            pltpu.SemaphoreType.DMA((2 * groups,)),
+        ],
+        compiler_params=params(),
+        cost_estimate=cost(
+            6 * total * width * hid + 6 * total * own * hid, 6 * width * hid + 4 * total * width
+        ),
+        name="weight_grads",
+    )(part, *rows, *scaled, gate_proj, up_proj, down_proj)
+
+
+def merge(me, routes, returned):
+    blocks = len(returned)
+    tokens = routes.shape[1]
+    width = returned[0].shape[1] * (ROWS // (MOST - ROWS)) // (ROWS // (MOST - ROWS) + 1)
+    pieces, step = cut(width)
+
+    def kernel(me_ref, routes_ref, *refs):
+        out = refs[blocks]
+        main, spill, piece = slot_masks(me_ref[0], routes_ref[...], blocks, width)
+        rows = jnp.concatenate([ref[:, :width] for ref in refs[:blocks]], 0)
+        extra = jnp.concatenate([ref[:, width:] for ref in refs[:blocks]], 0)
+        picked = dot(ones(main), rows, BY_ROWS)
+        for at in range(pieces):
+            columns = slice(at * step, (at + 1) * step)
+            out[:, columns] = (
+                picked[:, columns] + dot(ones(spill & (piece == at)), extra, BY_ROWS)
+            ).astype(jnp.bfloat16)
+
+    return pl.pallas_call(
+        kernel,
+        out_shape=jax.ShapeDtypeStruct((tokens, width), jnp.bfloat16),
+        in_specs=[pl.BlockSpec(memory_space=pltpu.SMEM)] + whole(1 + blocks),
+        out_specs=pl.BlockSpec(memory_space=pltpu.VMEM),
+        compiler_params=params(),
+        cost_estimate=cost(4 * blocks * ROWS * tokens * width, 4 * tokens * width),
+        name="merge",
+    )(me, routes, *returned)
+
+
+def swap(value, axis, distance):
+    size = lax.axis_size(axis)
+    return lax.ppermute(value, axis, [(at, at ^ distance) for at in range(size)])
+
+
+def exchange(blocks, axis):
+    out = list(blocks)
+    for distance in reversed(range(1, len(blocks))):
+        out[distance] = swap(blocks[distance], axis, distance)
+    return out
+
+
+def collect(value, axis):
+    values = [value]
+    distance = lax.axis_size(axis) // 2
+    while distance > 0:
+        values = values + [swap(one, axis, distance) for one in values]
+        distance //= 2
+    return values
+
+
+def gather_body(tokens, cotangent, routes, expert_gates, gate_proj, up_proj, down_proj):
+    blocks = lax.axis_size("expert")
+    tile = 256
+    me = lax.axis_index("expert").astype(jnp.int32).reshape(1)
+    part = lax.axis_index("dp").astype(jnp.int32).reshape(1)
+    routes = routes.reshape(1, -1)
+    gates = expert_gates.reshape(1, -1)
+    rows = join(exchange(pack(False, blocks, me, routes, gates, tokens), "expert"))
+    all_rows = collect(rows, "dp")
+    scaled = join(exchange(pack(True, blocks, me, routes, gates, cotangent), "expert"))
+    all_scaled = collect(scaled, "dp")
+    sent = back(blocks, tile, rows, scaled, gate_proj, up_proj, down_proj)
+    grad_input = merge(me, routes, exchange(sent, "expert"))
+    grads = weight_grads(tile, part, all_rows, all_scaled, gate_proj, up_proj, down_proj)
+    return (grad_input, *grads)
+
+
+def body(tokens, cotangent, routes, expert_gates, gate_proj, up_proj, down_proj):
+    groups, blocks = lax.axis_size("dp"), lax.axis_size("expert")
+    width, hid = gate_proj.shape
+    rows_sent = (groups - 1) * 2 * blocks * MOST * width
+    grads_sent = 3 * width * hid * (groups - 1) // groups
+    fits = blocks == EXPERTS and groups & (groups - 1) == 0 and hid % 256 == 0
+    fits = fits and tokens.shape[0] == 128 and routes.shape[1] == 1 and width // groups % 128 == 0
+    chosen = gather_body if fits and rows_sent < grads_sent else scatter_body
+    return chosen(tokens, cotangent, routes, expert_gates, gate_proj, up_proj, down_proj)
+
+
 def solution(mesh):
     in_specs = (
         P(("dp", "expert"), None),

time: 209 us -> 127 us (0.61)
  waiting for transfers between devices: 113 us -> 50.6 us
  Pallas kernels: 0 us -> 30.3 us
  starting transfers between devices: 15.8 us -> 41.6 us
  matrix products: 24 us -> 0 us
  local copies, waits for them, and re-layouts: 25.6 us -> 3.55 us
  other arithmetic: 16.2 us -> 0 us
  between operations: 13.9 us -> 0.71 us
    reduce_scatter x3 -> x0, waiting for transfers between devices: 65.2 us -> none  [the longest x1 38.1 us: body(): lax.psum_scatter(grad_up.astype(jnp.bfloat16), 'dp', scatter_dimension=0,...]
    ppermute x0 -> x27, waiting for transfers between devices: none -> 50.6 us  [swap(): lax.ppermute(value, axis, [(at, at ^ distance) for at in range(size)])]
    all_to_all x3 -> x0, waiting for transfers between devices: 47.6 us -> none  [the longest x1 20.2 us: body(): lax.all_to_all(partial_value.reshape(expert_devs, capacity, model_dim), '...]
    ppermute x0 -> x27, starting transfers between devices: none -> 41.6 us  [swap(): lax.ppermute(value, axis, [(at, at ^ distance) for at in range(size)])]
    pallas_call x0 -> x7, Pallas kernels: none -> 30.3 us  [the longest x1 17.1 us: weight_grads(): pl.pallas_call(kernel, grid=(hid // tile,), out_shape=[jax.ShapeDtypeStru...]
    dot_general x7 -> x0, matrix products: 24 us -> none  [the longest x1 6.2 us: body(): lax.dot_general(joined_grads, joined_proj, by_width, preferred_element_ty...]
    all_to_all x3 -> x0, starting transfers between devices: 15.7 us -> none  [the longest x1 7.25 us: body(): lax.all_to_all(copies(dy_slots), 'expert', split_axis=0, concat_axis=0, t...]
    convert_element_type x6 -> x0, other arithmetic: 12.5 us -> none  [the longest x3 7.34 us: body(): grad_gate, grad_up, grad_down = (lax.psum_scatter(grad_gate.astype(jnp.bf...]
  transfers between devices with their start and end apart: 6 -> 27, of which waited for: 5 -> 11; matrix products, arithmetic and copies ran while one was open for 20% -> 0% of each run, Pallas kernels for 0% -> 10%
where the time goes in v1:
time: 127 us
  waiting for transfers between devices  50.6 us (40%)
  starting transfers between devices  41.6 us (33%)
  Pallas kernels  30.3 us (24%)
  local copies, waits for them, and re-layouts  3.55 us (3%)
    ppermute x27, waiting for transfers between devices, swap(): lax.ppermute(value, axis, [(at, at ^ distance) for at in range(size)])  50.6 us
    ppermute x27, starting transfers between devices, swap(): lax.ppermute(value, axis, [(at, at ^ distance) for at in range(size)])  41.6 us
    pallas_call x1, Pallas kernels, weight_grads(): pl.pallas_call(kernel, grid=(hid // tile,), out_shape=[jax.ShapeDtypeStru...  17.1 us
    pallas_call x1, Pallas kernels, back(): pl.pallas_call(kernel, grid=(hid // tile,), out_shape=[shape] * blocks, i...  8.67 us
    unnamed x12, local copies, waits for them, and re-layouts  3.55 us
  transfers between devices with their start and end apart: 27, of which 11 were waited for; matrix products, arithmetic and copies ran while one was open for 0% of the time, Pallas kernels for 10%

profile of v1, /device:TPU:0, one launch (start us, length us, event | category | flops | bytes accessed | tf_op | source)
XLA Modules:
  0.0 126.8 jit_solution(4577281183981104607)
XLA Ops:
  3.7 4.1 %collective-permute-start.10 = (bf16[16,2304]{1,0:T(8,128)(2,1)S(1)}, bf16[16,2304]{1,0:T(8,128)(2,1)S(1)}, u32[]{:S(2)}, u32[]{:S(2)}) collective-permute-start(bf16[16,2304]{1,0:T(8,128)(2,1)S(1)} %get-tuple-element.43), channel_id=1, source_target_pairs={{0,4},{1,5},{2,6},{3,7},{4,0},{5,1},{6,2},{7,3},{8,12},{9,13},{10,... | collective-permute-start | bytes 221192 | tf_op jit(solution)/shard_map/ppermute | solution.py:402
  9.1 3.6 %collective-permute-start.12 = (bf16[16,2304]{1,0:T(8,128)(2,1)S(1)}, bf16[16,2304]{1,0:T(8,128)(2,1)S(1)}, u32[]{:S(2)}, u32[]{:S(2)}) collective-permute-start(bf16[16,2304]{1,0:T(8,128)(2,1)S(1)} %get-tuple-element.45), channel_id=1, source_target_pairs={{0,6},{1,7},{2,4},{3,5},{4,2},{5,3},{6,0},{7,1},{8,14},{9,15},{10,... | collective-permute-start | bytes 221192 | tf_op jit(solution)/shard_map/ppermute | solution.py:402
  12.7 1.7 %collective-permute-start.7 = (bf16[16,2304]{1,0:T(8,128)(2,1)S(1)}, bf16[16,2304]{1,0:T(8,128)(2,1)S(1)}, u32[]{:S(2)}, u32[]{:S(2)}) collective-permute-start(bf16[16,2304]{1,0:T(8,128)(2,1)S(1)} %get-tuple-element.40), channel_id=1, source_target_pairs={{0,1},{1,0},{2,3},{3,2},{4,5},{5,4},{6,7},{7,6},{8,9},{9,8},{10,11... | collective-permute-start | bytes 221192 | tf_op jit(solution)/shard_map/ppermute | solution.py:402
  17.0 1.8 %collective-permute-done.11.refs_5_ = bf16[16,2304]{1,0:T(8,128)(2,1)S(1)} collective-permute-done((bf16[16,2304]{1,0:T(8,128)(2,1)S(1)}, bf16[16,2304]{1,0:T(8,128)(2,1)S(1)}, u32[]{:S(2)}, u32[]{:S(2)}) %collective-permute-start.11) | collective-permute-done | bytes 73760 | tf_op jit(solution)/shard_map/ppermute | solution.py:402
  20.8 2.7 %collective-permute-start.1 = (bf16[16,2304]{1,0:T(8,128)(2,1)S(1)}, bf16[16,2304]{1,0:T(8,128)(2,1)S(1)}, u32[]{:S(2)}, u32[]{:S(2)}) collective-permute-start(bf16[16,2304]{1,0:T(8,128)(2,1)S(1)} %get-tuple-element.33), channel_id=1, source_target_pairs={{0,2},{1,3},{2,0},{3,1},{4,6},{5,7},{6,4},{7,5},{8,10},{9,11},{10,... | collective-permute-start | bytes 221192 | tf_op jit(solution)/shard_map/ppermute | solution.py:402
  23.8 3.0 %collective-permute-start.3 = (bf16[16,2304]{1,0:T(8,128)(2,1)S(1)}, bf16[16,2304]{1,0:T(8,128)(2,1)S(1)}, u32[]{:S(2)}, u32[]{:S(2)}) collective-permute-start(bf16[16,2304]{1,0:T(8,128)(2,1)S(1)} %get-tuple-element.35), channel_id=1, source_target_pairs={{0,4},{1,5},{2,6},{3,7},{4,0},{5,1},{6,2},{7,3},{8,12},{9,13},{10,... | collective-permute-start | bytes 221192 | tf_op jit(solution)/shard_map/ppermute | solution.py:402
  26.7 1.8 %collective-permute-start.4 = (bf16[16,2304]{1,0:T(8,128)(2,1)S(1)}, bf16[16,2304]{1,0:T(8,128)(2,1)S(1)}, u32[]{:S(2)}, u32[]{:S(2)}) collective-permute-start(bf16[16,2304]{1,0:T(8,128)(2,1)S(1)} %get-tuple-element.36), channel_id=1, source_target_pairs={{0,5},{1,4},{2,7},{3,6},{4,1},{5,0},{6,3},{7,2},{8,13},{9,12},{10,... | collective-permute-start | bytes 221192 | tf_op jit(solution)/shard_map/ppermute | solution.py:402
  28.6 2.3 %collective-permute-start.5 = (bf16[16,2304]{1,0:T(8,128)(2,1)S(1)}, bf16[16,2304]{1,0:T(8,128)(2,1)S(1)}, u32[]{:S(2)}, u32[]{:S(2)}) collective-permute-start(bf16[16,2304]{1,0:T(8,128)(2,1)S(1)} %get-tuple-element.37), channel_id=1, source_target_pairs={{0,6},{1,7},{2,4},{3,5},{4,2},{5,3},{6,0},{7,1},{8,14},{9,15},{10,... | collective-permute-start | bytes 221192 | tf_op jit(solution)/shard_map/ppermute | solution.py:402
  34.9 4.0 %collective-permute-done.4.refs_5_ = bf16[16,2304]{1,0:T(8,128)(2,1)S(1)} collective-permute-done((bf16[16,2304]{1,0:T(8,128)(2,1)S(1)}, bf16[16,2304]{1,0:T(8,128)(2,1)S(1)}, u32[]{:S(2)}, u32[]{:S(2)}) %collective-permute-start.4) | collective-permute-done | bytes 73760 | tf_op jit(solution)/shard_map/ppermute | solution.py:402
  42.0 8.0 %collective-permute-done.24.refs_5_ = bf16[144,2048]{1,0:T(8,128)(2,1)} collective-permute-done((bf16[144,2048]{1,0:T(8,128)(2,1)}, bf16[144,2048]{1,0:T(8,128)(2,1)}, u32[]{:S(2)}, u32[]{:S(2)}) %collective-permute-start.24) | collective-permute-done | bytes 589856 | tf_op jit(solution)/shard_map/ppermute | solution.py:402
  50.0 9.8 %collective-permute-done.21.refs_1_ = bf16[144,2048]{1,0:T(8,128)(2,1)} collective-permute-done((bf16[144,2048]{1,0:T(8,128)(2,1)}, bf16[144,2048]{1,0:T(8,128)(2,1)}, u32[]{:S(2)}, u32[]{:S(2)}) %collective-permute-start.21) | collective-permute-done | bytes 589856 | tf_op jit(solution)/shard_map/ppermute | solution.py:402
  59.9 8.7 %back.1 = (bf16[16,2304]{1,0:T(8,128)(2,1)S(1)}, bf16[16,2304]{1,0:T(8,128)(2,1)S(1)}, bf16[16,2304]{1,0:T(8,128)(2,1)S(1)}, bf16[16,2304]{1,0:T(8,128)(2,1)S(1)...) custom-call(bf16[144,2048]{1,0:T(8,128)(2,1)} %join.2.x_ref.refs_0_,, ...), custom_call_target="tpu_custom_call" | custom-call | flops 2264924160 | bytes 9437184 | tf_op jit(solution)/shard_map/back/pallas_call | solution.py:290
  68.5 1.5 %collective-permute-start.14 = (bf16[16,2304]{1,0:T(8,128)(2,1)S(1)}, bf16[16,2304]{1,0:T(8,128)(2,1)S(1)}, u32[]{:S(2)}, u32[]{:S(2)}) collective-permute-start(bf16[16,2304]{1,0:T(8,128)(2,1)S(1)} %get-tuple-element.48), channel_id=1, source_target_pairs={{0,1},{1,0},{2,3},{3,2},{4,5},{5,4},{6,7},{7,6},{8,9},{9,8},{10,11... | collective-permute-start | bytes 221192 | tf_op jit(solution)/shard_map/ppermute | solution.py:402
  70.1 3.2 %collective-permute-done.14.refs_1_ = bf16[16,2304]{1,0:T(8,128)(2,1)S(1)} collective-permute-done((bf16[16,2304]{1,0:T(8,128)(2,1)S(1)}, bf16[16,2304]{1,0:T(8,128)(2,1)S(1)}, u32[]{:S(2)}, u32[]{:S(2)}) %collective-permute-start.14) | collective-permute-done | bytes 73760 | tf_op jit(solution)/shard_map/ppermute | solution.py:402
  73.3 4.3 %collective-permute-done.15.refs_2_ = bf16[16,2304]{1,0:T(8,128)(2,1)S(1)} collective-permute-done((bf16[16,2304]{1,0:T(8,128)(2,1)S(1)}, bf16[16,2304]{1,0:T(8,128)(2,1)S(1)}, u32[]{:S(2)}, u32[]{:S(2)}) %collective-permute-start.15) | collective-permute-done | bytes 73760 | tf_op jit(solution)/shard_map/ppermute | solution.py:402
  78.5 4.3 %collective-permute-done.16.refs_3_ = bf16[16,2304]{1,0:T(8,128)(2,1)S(1)} collective-permute-done((bf16[16,2304]{1,0:T(8,128)(2,1)S(1)}, bf16[16,2304]{1,0:T(8,128)(2,1)S(1)}, u32[]{:S(2)}, u32[]{:S(2)}) %collective-permute-start.16) | collective-permute-done | bytes 73760 | tf_op jit(solution)/shard_map/ppermute | solution.py:402
  83.8 4.6 %collective-permute-done.17.refs_4_ = bf16[16,2304]{1,0:T(8,128)(2,1)S(1)} collective-permute-done((bf16[16,2304]{1,0:T(8,128)(2,1)S(1)}, bf16[16,2304]{1,0:T(8,128)(2,1)S(1)}, u32[]{:S(2)}, u32[]{:S(2)}) %collective-permute-start.17) | collective-permute-done | bytes 73760 | tf_op jit(solution)/shard_map/ppermute | solution.py:402
  88.4 1.5 %collective-permute-start.18 = (bf16[16,2304]{1,0:T(8,128)(2,1)S(1)}, bf16[16,2304]{1,0:T(8,128)(2,1)S(1)}, u32[]{:S(2)}, u32[]{:S(2)}) collective-permute-start(bf16[16,2304]{1,0:T(8,128)(2,1)S(1)} %get-tuple-element.52), channel_id=1, source_target_pairs={{0,5},{1,4},{2,7},{3,6},{4,1},{5,0},{6,3},{7,2},{8,13},{9,12},{10,... | collective-permute-start | bytes 221192 | tf_op jit(solution)/shard_map/ppermute | solution.py:402
  89.9 4.6 %collective-permute-done.18.refs_5_ = bf16[16,2304]{1,0:T(8,128)(2,1)S(1)} collective-permute-done((bf16[16,2304]{1,0:T(8,128)(2,1)S(1)}, bf16[16,2304]{1,0:T(8,128)(2,1)S(1)}, u32[]{:S(2)}, u32[]{:S(2)}) %collective-permute-start.18) | collective-permute-done | bytes 73760 | tf_op jit(solution)/shard_map/ppermute | solution.py:402
  94.5 2.8 %collective-permute-start.19 = (bf16[16,2304]{1,0:T(8,128)(2,1)S(1)}, bf16[16,2304]{1,0:T(8,128)(2,1)S(1)}, u32[]{:S(2)}, u32[]{:S(2)}) collective-permute-start(bf16[16,2304]{1,0:T(8,128)(2,1)S(1)} %get-tuple-element.53), channel_id=1, source_target_pairs={{0,6},{1,7},{2,4},{3,5},{4,2},{5,3},{6,0},{7,1},{8,14},{9,15},{10,... | collective-permute-start | bytes 221192 | tf_op jit(solution)/shard_map/ppermute | solution.py:402
  97.3 3.4 %collective-permute-done.19.refs_6_ = bf16[16,2304]{1,0:T(8,128)(2,1)S(1)} collective-permute-done((bf16[16,2304]{1,0:T(8,128)(2,1)S(1)}, bf16[16,2304]{1,0:T(8,128)(2,1)S(1)}, u32[]{:S(2)}, u32[]{:S(2)}) %collective-permute-start.19) | collective-permute-done | bytes 73760 | tf_op jit(solution)/shard_map/ppermute | solution.py:402
  100.8 5.2 %collective-permute-start.20 = (bf16[16,2304]{1,0:T(8,128)(2,1)S(1)}, bf16[16,2304]{1,0:T(8,128)(2,1)S(1)}, u32[]{:S(2)}, u32[]{:S(2)}) collective-permute-start(bf16[16,2304]{1,0:T(8,128)(2,1)S(1)} %get-tuple-element.54), channel_id=1, source_target_pairs={{0,7},{1,6},{2,5},{3,4},{4,3},{5,2},{6,1},{7,0},{8,15},{9,14},{10,... | collective-permute-start | bytes 221192 | tf_op jit(solution)/shard_map/ppermute | solution.py:402
  106.0 2.3 %collective-permute-done.20.refs_7_ = bf16[16,2304]{1,0:T(8,128)(2,1)S(1)} collective-permute-done((bf16[16,2304]{1,0:T(8,128)(2,1)S(1)}, bf16[16,2304]{1,0:T(8,128)(2,1)S(1)}, u32[]{:S(2)}, u32[]{:S(2)}) %collective-permute-start.20) | collective-permute-done | bytes 73760 | tf_op jit(solution)/shard_map/ppermute | solution.py:402
  109.8 17.1 %weight_grads.1 = (f32[512,768]{1,0:T(8,128)}, f32[512,768]{1,0:T(8,128)}, f32[768,512]{1,0:T(8,128)}) custom-call(s32[1]{0:T(128)} %bitcast.3.part_ref, bf16[144,2048]{1,0:T(8,128)(2,1)} %join.2.x_ref.refs_0_, bf16[144,2048]{1,0:T(8,128)(2,1)} %collective-permute-done.21.refs_1_, bf16[144,2048]{1,0:T(8,128)(2,1)} %collective-permute-done.22.refs_2_, ...), custom_call_target="tpu_custom_call" | custom-call | flops 6794772480 | bytes 14155776 | tf_op jit(solution)/shard_map/weight_grads/pallas_call | solution.py:342
  (49 shorter events, 19.6 us)
Async XLA Ops:
  3.7 12.3 %collective-permute-start.10 = (bf16[16,2304]{1,0:T(8,128)(2,1)S(1)}, bf16[16,2304]{1,0:T(8,128)(2,1)S(1)}, u32[]{:S(2)}, u32[]{:S(2)}) collective-permute-start(bf16[16,2304]{1,0:T(8,128)(2,1)S(1)} %get-tuple-element.43), channel_id=1, source_target_pairs={{0,4},{1,5},{2,6},{3,7},{4,0},{5,1},{6,2},{7,3},{8,12},{9,13},{10,... | collective-permute-start | bytes 221192 | tf_op jit(solution)/shard_map/ppermute | solution.py:402
  7.8 11.0 %collective-permute-start.11 = (bf16[16,2304]{1,0:T(8,128)(2,1)S(1)}, bf16[16,2304]{1,0:T(8,128)(2,1)S(1)}, u32[]{:S(2)}, u32[]{:S(2)}) collective-permute-start(bf16[16,2304]{1,0:T(8,128)(2,1)S(1)} %get-tuple-element.44), channel_id=1, source_target_pairs={{0,5},{1,4},{2,7},{3,6},{4,1},{5,0},{6,3},{7,2},{8,13},{9,12},{10,... | collective-permute-start | bytes 221192 | tf_op jit(solution)/shard_map/ppermute | solution.py:402
  9.1 10.7 %collective-permute-start.12 = (bf16[16,2304]{1,0:T(8,128)(2,1)S(1)}, bf16[16,2304]{1,0:T(8,128)(2,1)S(1)}, u32[]{:S(2)}, u32[]{:S(2)}) collective-permute-start(bf16[16,2304]{1,0:T(8,128)(2,1)S(1)} %get-tuple-element.45), channel_id=1, source_target_pairs={{0,6},{1,7},{2,4},{3,5},{4,2},{5,3},{6,0},{7,1},{8,14},{9,15},{10,... | collective-permute-start | bytes 221192 | tf_op jit(solution)/shard_map/ppermute | solution.py:402
  12.7 8.1 %collective-permute-start.13 = (bf16[16,2304]{1,0:T(8,128)(2,1)S(1)}, bf16[16,2304]{1,0:T(8,128)(2,1)S(1)}, u32[]{:S(2)}, u32[]{:S(2)}) collective-permute-start(bf16[16,2304]{1,0:T(8,128)(2,1)S(1)} %get-tuple-element.46), channel_id=1, source_target_pairs={{0,7},{1,6},{2,5},{3,4},{4,3},{5,2},{6,1},{7,0},{8,15},{9,14},{10,... | collective-permute-start | bytes 221192 | tf_op jit(solution)/shard_map/ppermute | solution.py:402
  12.7 10.7 %collective-permute-start.7 = (bf16[16,2304]{1,0:T(8,128)(2,1)S(1)}, bf16[16,2304]{1,0:T(8,128)(2,1)S(1)}, u32[]{:S(2)}, u32[]{:S(2)}) collective-permute-start(bf16[16,2304]{1,0:T(8,128)(2,1)S(1)} %get-tuple-element.40), channel_id=1, source_target_pairs={{0,1},{1,0},{2,3},{3,2},{4,5},{5,4},{6,7},{7,6},{8,9},{9,8},{10,11... | collective-permute-start | bytes 221192 | tf_op jit(solution)/shard_map/ppermute | solution.py:402
  16.0 7.8 %collective-permute-start.8 = (bf16[16,2304]{1,0:T(8,128)(2,1)S(1)}, bf16[16,2304]{1,0:T(8,128)(2,1)S(1)}, u32[]{:S(2)}, u32[]{:S(2)}) collective-permute-start(bf16[16,2304]{1,0:T(8,128)(2,1)S(1)} %get-tuple-element.41), channel_id=1, source_target_pairs={{0,2},{1,3},{2,0},{3,1},{4,6},{5,7},{6,4},{7,5},{8,10},{9,11},{10,... | collective-permute-start | bytes 221192 | tf_op jit(solution)/shard_map/ppermute | solution.py:402
  18.9 7.9 %collective-permute-start.9 = (bf16[16,2304]{1,0:T(8,128)(2,1)S(1)}, bf16[16,2304]{1,0:T(8,128)(2,1)S(1)}, u32[]{:S(2)}, u32[]{:S(2)}) collective-permute-start(bf16[16,2304]{1,0:T(8,128)(2,1)S(1)} %get-tuple-element.42), channel_id=1, source_target_pairs={{0,3},{1,2},{2,1},{3,0},{4,7},{5,6},{6,5},{7,4},{8,11},{9,10},{10,... | collective-permute-start | bytes 221192 | tf_op jit(solution)/shard_map/ppermute | solution.py:402
  19.8 8.8 %collective-permute-start = (bf16[16,2304]{1,0:T(8,128)(2,1)S(1)}, bf16[16,2304]{1,0:T(8,128)(2,1)S(1)}, u32[]{:S(2)}, u32[]{:S(2)}) collective-permute-start(bf16[16,2304]{1,0:T(8,128)(2,1)S(1)} %get-tuple-element.32), channel_id=1, source_target_pairs={{0,1},{1,0},{2,3},{3,2},{4,5},{5,4},{6,7},{7,6},{8,9},{9,8},{10,11... | collective-permute-start | bytes 221192 | tf_op jit(solution)/shard_map/ppermute | solution.py:402
  20.8 10.1 %collective-permute-start.1 = (bf16[16,2304]{1,0:T(8,128)(2,1)S(1)}, bf16[16,2304]{1,0:T(8,128)(2,1)S(1)}, u32[]{:S(2)}, u32[]{:S(2)}) collective-permute-start(bf16[16,2304]{1,0:T(8,128)(2,1)S(1)} %get-tuple-element.33), channel_id=1, source_target_pairs={{0,2},{1,3},{2,0},{3,1},{4,6},{5,7},{6,4},{7,5},{8,10},{9,11},{10,... | collective-permute-start | bytes 221192 | tf_op jit(solution)/shard_map/ppermute | solution.py:402
  23.4 10.0 %collective-permute-start.2 = (bf16[16,2304]{1,0:T(8,128)(2,1)S(1)}, bf16[16,2304]{1,0:T(8,128)(2,1)S(1)}, u32[]{:S(2)}, u32[]{:S(2)}) collective-permute-start(bf16[16,2304]{1,0:T(8,128)(2,1)S(1)} %get-tuple-element.34), channel_id=1, source_target_pairs={{0,3},{1,2},{2,1},{3,0},{4,7},{5,6},{6,5},{7,4},{8,11},{9,10},{10,... | collective-permute-start | bytes 221192 | tf_op jit(solution)/shard_map/ppermute | solution.py:402
  23.8 11.2 %collective-permute-start.3 = (bf16[16,2304]{1,0:T(8,128)(2,1)S(1)}, bf16[16,2304]{1,0:T(8,128)(2,1)S(1)}, u32[]{:S(2)}, u32[]{:S(2)}) collective-permute-start(bf16[16,2304]{1,0:T(8,128)(2,1)S(1)} %get-tuple-element.35), channel_id=1, source_target_pairs={{0,4},{1,5},{2,6},{3,7},{4,0},{5,1},{6,2},{7,3},{8,12},{9,13},{10,... | collective-permute-start | bytes 221192 | tf_op jit(solution)/shard_map/ppermute | solution.py:402
  26.7 12.2 %collective-permute-start.4 = (bf16[16,2304]{1,0:T(8,128)(2,1)S(1)}, bf16[16,2304]{1,0:T(8,128)(2,1)S(1)}, u32[]{:S(2)}, u32[]{:S(2)}) collective-permute-start(bf16[16,2304]{1,0:T(8,128)(2,1)S(1)} %get-tuple-element.36), channel_id=1, source_target_pairs={{0,5},{1,4},{2,7},{3,6},{4,1},{5,0},{6,3},{7,2},{8,13},{9,12},{10,... | collective-permute-start | bytes 221192 | tf_op jit(solution)/shard_map/ppermute | solution.py:402
  28.6 10.4 %collective-permute-start.5 = (bf16[16,2304]{1,0:T(8,128)(2,1)S(1)}, bf16[16,2304]{1,0:T(8,128)(2,1)S(1)}, u32[]{:S(2)}, u32[]{:S(2)}) collective-permute-start(bf16[16,2304]{1,0:T(8,128)(2,1)S(1)} %get-tuple-element.37), channel_id=1, source_target_pairs={{0,6},{1,7},{2,4},{3,5},{4,2},{5,3},{6,0},{7,1},{8,14},{9,15},{10,... | collective-permute-start | bytes 221192 | tf_op jit(solution)/shard_map/ppermute | solution.py:402
  30.9 8.1 %collective-permute-start.6 = (bf16[16,2304]{1,0:T(8,128)(2,1)S(1)}, bf16[16,2304]{1,0:T(8,128)(2,1)S(1)}, u32[]{:S(2)}, u32[]{:S(2)}) collective-permute-start(bf16[16,2304]{1,0:T(8,128)(2,1)S(1)} %get-tuple-element.38), channel_id=1, source_target_pairs={{0,7},{1,6},{2,5},{3,4},{4,3},{5,2},{6,1},{7,0},{8,15},{9,14},{10,... | collective-permute-start | bytes 221192 | tf_op jit(solution)/shard_map/ppermute | solution.py:402
  33.4 16.6 %collective-permute-start.24 = (bf16[144,2048]{1,0:T(8,128)(2,1)}, bf16[144,2048]{1,0:T(8,128)(2,1)}, u32[]{:S(2)}, u32[]{:S(2)}) collective-permute-start(bf16[144,2048]{1,0:T(8,128)(2,1)} %join.3.dy_ref.refs_4_), channel_id=1, source_target_pairs={{0,16},{8,24},{16,0},{24,8},{1,17},{9,25},{17,1},{25,9},{2,18},{10... | collective-permute-start | bytes 1769480 | tf_op jit(solution)/shard_map/ppermute | solution.py:402
  40.0 19.9 %collective-permute-start.21 = (bf16[144,2048]{1,0:T(8,128)(2,1)}, bf16[144,2048]{1,0:T(8,128)(2,1)}, u32[]{:S(2)}, u32[]{:S(2)}) collective-permute-start(bf16[144,2048]{1,0:T(8,128)(2,1)} %join.2.x_ref.refs_0_), channel_id=1, source_target_pairs={{0,16},{8,24},{16,0},{24,8},{1,17},{9,25},{17,1},{25,9},{2,18},{10... | collective-permute-start | bytes 1769480 | tf_op jit(solution)/shard_map/ppermute | solution.py:402
  41.5 68.3 %collective-permute-start.25 = (bf16[144,2048]{1,0:T(8,128)(2,1)}, bf16[144,2048]{1,0:T(8,128)(2,1)}, u32[]{:S(2)}, u32[]{:S(2)}) collective-permute-start(bf16[144,2048]{1,0:T(8,128)(2,1)} %join.3.dy_ref.refs_4_), channel_id=1, source_target_pairs={{0,8},{8,0},{16,24},{24,16},{1,9},{9,1},{17,25},{25,17},{2,10},{10... | collective-permute-start | bytes 1769480 | tf_op jit(solution)/shard_map/ppermute | solution.py:402
  41.5 68.3 %collective-permute-start.22 = (bf16[144,2048]{1,0:T(8,128)(2,1)}, bf16[144,2048]{1,0:T(8,128)(2,1)}, u32[]{:S(2)}, u32[]{:S(2)}) collective-permute-start(bf16[144,2048]{1,0:T(8,128)(2,1)} %join.2.x_ref.refs_0_), channel_id=1, source_target_pairs={{0,8},{8,0},{16,24},{24,16},{1,9},{9,1},{17,25},{25,17},{2,10},{10... | collective-permute-start | bytes 1769480 | tf_op jit(solution)/shard_map/ppermute | solution.py:402
  50.0 59.7 %collective-permute-start.26 = (bf16[144,2048]{1,0:T(8,128)(2,1)}, bf16[144,2048]{1,0:T(8,128)(2,1)}, u32[]{:S(2)}, u32[]{:S(2)}) collective-permute-start(bf16[144,2048]{1,0:T(8,128)(2,1)} %collective-permute-done.24.refs_5_), channel_id=1, source_target_pairs={{0,8},{8,0},{16,24},{24,16},{1,9},{9,1},{17,25},{25,17},{2,10},{10... | collective-permute-start | bytes 1769480 | tf_op jit(solution)/shard_map/ppermute | solution.py:402
  59.9 49.9 %collective-permute-start.23 = (bf16[144,2048]{1,0:T(8,128)(2,1)}, bf16[144,2048]{1,0:T(8,128)(2,1)}, u32[]{:S(2)}, u32[]{:S(2)}) collective-permute-start(bf16[144,2048]{1,0:T(8,128)(2,1)} %collective-permute-done.21.refs_1_), channel_id=1, source_target_pairs={{0,8},{8,0},{16,24},{24,16},{1,9},{9,1},{17,25},{25,17},{2,10},{10... | collective-permute-start | bytes 1769480 | tf_op jit(solution)/shard_map/ppermute | solution.py:402
  82.9 5.5 %collective-permute-start.17 = (bf16[16,2304]{1,0:T(8,128)(2,1)S(1)}, bf16[16,2304]{1,0:T(8,128)(2,1)S(1)}, u32[]{:S(2)}, u32[]{:S(2)}) collective-permute-start(bf16[16,2304]{1,0:T(8,128)(2,1)S(1)} %get-tuple-element.51), channel_id=1, source_target_pairs={{0,4},{1,5},{2,6},{3,7},{4,0},{5,1},{6,2},{7,3},{8,12},{9,13},{10,... | collective-permute-start | bytes 221192 | tf_op jit(solution)/shard_map/ppermute | solution.py:402
  88.4 6.2 %collective-permute-start.18 = (bf16[16,2304]{1,0:T(8,128)(2,1)S(1)}, bf16[16,2304]{1,0:T(8,128)(2,1)S(1)}, u32[]{:S(2)}, u32[]{:S(2)}) collective-permute-start(bf16[16,2304]{1,0:T(8,128)(2,1)S(1)} %get-tuple-element.52), channel_id=1, source_target_pairs={{0,5},{1,4},{2,7},{3,6},{4,1},{5,0},{6,3},{7,2},{8,13},{9,12},{10,... | collective-permute-start | bytes 221192 | tf_op jit(solution)/shard_map/ppermute | solution.py:402
  94.5 6.3 %collective-permute-start.19 = (bf16[16,2304]{1,0:T(8,128)(2,1)S(1)}, bf16[16,2304]{1,0:T(8,128)(2,1)S(1)}, u32[]{:S(2)}, u32[]{:S(2)}) collective-permute-start(bf16[16,2304]{1,0:T(8,128)(2,1)S(1)} %get-tuple-element.53), channel_id=1, source_target_pairs={{0,6},{1,7},{2,4},{3,5},{4,2},{5,3},{6,0},{7,1},{8,14},{9,15},{10,... | collective-permute-start | bytes 221192 | tf_op jit(solution)/shard_map/ppermute | solution.py:402
  100.8 7.5 %collective-permute-start.20 = (bf16[16,2304]{1,0:T(8,128)(2,1)S(1)}, bf16[16,2304]{1,0:T(8,128)(2,1)S(1)}, u32[]{:S(2)}, u32[]{:S(2)}) collective-permute-start(bf16[16,2304]{1,0:T(8,128)(2,1)S(1)} %get-tuple-element.54), channel_id=1, source_target_pairs={{0,7},{1,6},{2,5},{3,4},{4,3},{5,2},{6,1},{7,0},{8,15},{9,14},{10,... | collective-permute-start | bytes 221192 | tf_op jit(solution)/shard_map/ppermute | solution.py:402
  (9 other events, 145.5 us)

commit v2 on v0

--- a/solution.py
+++ b/solution.py
@@ -1,10 +1,13 @@
 import jax
 import jax.numpy as jnp
 from jax import lax
+from jax.experimental import pallas as pl
+from jax.experimental.pallas import tpu as pltpu
 from jax.sharding import PartitionSpec as P
 
 EXPERTS = 8
 MOST = 18
+ROWS = 16
 
 
 def build_slots(routes, capacity):
@@ -17,7 +20,7 @@
     return flat_routes * capacity + position
 
 
-def body(tokens, cotangent, routes, expert_gates, gate_proj, up_proj, down_proj):
+def scatter_body(tokens, cotangent, routes, expert_gates, gate_proj, up_proj, down_proj):
     tok_dev, model_dim = tokens.shape
     top_k = routes.shape[1]
     expert_devs = lax.axis_size("expert")
@@ -91,6 +94,433 @@
     return (grad_input.astype(jnp.bfloat16), grad_gate, grad_up, grad_down)
 
 
+BY_WIDTH = (((1,), (1,)), ((), ()))
+BY_ROWS = (((0,), (0,)), ((), ()))
+
+
+def cut(width):
+    pieces = ROWS // (MOST - ROWS)
+    return pieces, width // pieces
+
+
+def cost(flops, moved):
+    return pl.CostEstimate(flops=flops, bytes_accessed=moved, transcendentals=0)
+
+
+def params(mib):
+    return pltpu.CompilerParams(vmem_limit_bytes=mib * 1024 * 1024)
+
+
+def anywhere(count):
+    return [pl.BlockSpec(memory_space=pltpu.HBM)] * count
+
+
+def dot(left, right, dims=(((1,), (0,)), ((), ()))):
+    return lax.dot_general(left, right, dims, preferred_element_type=jnp.float32)
+
+
+def ones(mask):
+    return jnp.where(mask, 1.0, 0.0).astype(jnp.bfloat16)
+
+
+def load(sources, targets, arrived):
+    copies = [
+        pltpu.make_async_copy(source, target, arrived.at[at])
+        for at, (source, target) in enumerate(zip(sources, targets))
+    ]
+    for copy in copies:
+        copy.start()
+    for copy in copies:
+        copy.wait()
+
+
+def slot_masks(routes, blocks, width):
+    tokens = routes.shape[1]
+    pieces, _ = cut(width)
+    experts = lax.broadcasted_iota(jnp.int32, (EXPERTS, tokens), 0)
+    named = jnp.where(experts == routes, 1.0, 0.0)
+    earlier = lax.broadcasted_iota(jnp.int32, (tokens, tokens), 0) < lax.broadcasted_iota(
+        jnp.int32, (tokens, tokens), 1
+    )
+    before = dot(named.astype(jnp.bfloat16), ones(earlier))
+    position = jnp.sum(before * named, axis=0, keepdims=True).astype(jnp.int32)
+    slot = lax.broadcasted_iota(jnp.int32, (blocks * ROWS, tokens), 0)
+    row = slot % ROWS
+    mine = slot // ROWS == routes
+    main = mine & (position == row)
+    spill = mine & (position == ROWS + row // pieces)
+    return main, spill, row % pieces
+
+
+def pack(blocks, routes, values, gates=None):
+    tokens, width = values.shape
+    pieces, step = cut(width)
+    scaled = gates is not None
+    sources = (routes, values) + ((gates,) if scaled else ())
+
+    def kernel(*refs):
+        count = len(sources)
+        out, held, arrived = refs[count], refs[count + 1 : 2 * count + 1], refs[-1]
+        load(refs[:count], held, arrived)
+        main, spill, piece = slot_masks(held[0][...], blocks, width)
+        rows = dot(ones(main), held[1][...])
+        extra = jnp.zeros((blocks * ROWS, step), jnp.float32)
+        for at in range(pieces):
+            extra += dot(ones(spill & (piece == at)), held[1][:, at * step : (at + 1) * step])
+        if scaled:
+            weights = held[2][...]
+            rows = rows * jnp.sum(jnp.where(main, weights, 0.0), axis=1, keepdims=True)
+            extra = extra * jnp.sum(jnp.where(spill, weights, 0.0), axis=1, keepdims=True)
+        rows = rows.astype(jnp.bfloat16)
+        extra = extra.astype(jnp.bfloat16)
+        for block in range(blocks):
+            part = slice(block * ROWS, (block + 1) * ROWS)
+            out[block, :, :width] = rows[part]
+            out[block, :, width:] = extra[part]
+
+    return pl.pallas_call(
+        kernel,
+        out_shape=jax.ShapeDtypeStruct((blocks, ROWS, width + step), jnp.bfloat16),
+        in_specs=anywhere(len(sources)),
+        out_specs=pl.BlockSpec(memory_space=pltpu.VMEM),
+        scratch_shapes=[pltpu.VMEM(source.shape, source.dtype) for source in sources]
+        + [pltpu.SemaphoreType.DMA((len(sources),))],
+        compiler_params=params(16),
+        cost_estimate=cost(4 * blocks * ROWS * tokens * width, 4 * tokens * width),
+        name="pack",
+    )(*sources)
+
+
+def merge(routes, returned):
+    blocks = returned.shape[0]
+    tokens = routes.shape[1]
+    width = width_of(returned)
+    pieces, step = cut(width)
+
+    def kernel(routes_ref, back_ref, out, named, held, arrived):
+        load((routes_ref, back_ref), (named, held), arrived)
+        main, spill, piece = slot_masks(named[...], blocks, width)
+        rows = jnp.concatenate([held[at, :, :width] for at in range(blocks)], 0)
+        extra = jnp.concatenate([held[at, :, width:] for at in range(blocks)], 0)
+        picked = dot(ones(main), rows, BY_ROWS)
+        for at in range(pieces):
+            columns = slice(at * step, (at + 1) * step)
+            out[:, columns] = (
+                picked[:, columns] + dot(ones(spill & (piece == at)), extra, BY_ROWS)
+            ).astype(jnp.bfloat16)
+
+    return pl.pallas_call(
+        kernel,
+        out_shape=jax.ShapeDtypeStruct((tokens, width), jnp.bfloat16),
+        in_specs=anywhere(2),
+        out_specs=pl.BlockSpec(memory_space=pltpu.VMEM),
+        scratch_shapes=[
+            pltpu.VMEM(routes.shape, routes.dtype),
+            pltpu.VMEM(returned.shape, returned.dtype),
+            pltpu.SemaphoreType.DMA((2,)),
+        ],
+        compiler_params=params(16),
+        cost_estimate=cost(4 * blocks * ROWS * tokens * width, 4 * tokens * width),
+        name="merge",
+    )(routes, returned)
+
+
+def width_of(packed):
+    pieces = ROWS // (MOST - ROWS)
+    return packed.shape[2] * pieces // (pieces + 1)
+
+
+def spill_picks(blocks, pieces, at):
+    shape = (blocks * (MOST - ROWS), blocks * ROWS)
+    slot = lax.broadcasted_iota(jnp.int32, shape, 0)
+    row = lax.broadcasted_iota(jnp.int32, shape, 1)
+    return ones(row == slot * pieces + at)
+
+
+def unpack(packed, out, begin):
+    blocks = packed.shape[0]
+    width = width_of(packed)
+    pieces, step = cut(width)
+    for at in range(blocks):
+        out[begin + at * ROWS : begin + (at + 1) * ROWS, :] = packed[at, :, :width]
+    extra = jnp.concatenate([packed[at, :, width:] for at in range(blocks)], 0)
+    first, last = begin + blocks * ROWS, begin + blocks * MOST
+    for at in range(pieces):
+        out[first:last, at * step : (at + 1) * step] = dot(
+            spill_picks(blocks, pieces, at), extra
+        ).astype(jnp.bfloat16)
+
+
+def column_tile(width, tile):
+    return pl.BlockSpec((width, tile), lambda i: (0, i))
+
+
+def row_tile(tile, width):
+    return pl.BlockSpec((tile, width), lambda i: (i, 0))
+
+
+def forward(tile, packed, gate_proj, up_proj):
+    groups = len(packed)
+    blocks = packed[0].shape[0]
+    width, hid = gate_proj.shape
+    slots = blocks * MOST
+
+    def kernel(*refs):
+        gate_ref, up_ref, rows_ref, pre_gate_ref, pre_up_ref = refs[groups : groups + 5]
+        held, arrived = refs[groups + 5 :]
+
+        @pl.when(pl.program_id(0) == 0)
+        def _():
+            load(refs[:groups], [held.at[at] for at in range(groups)], arrived)
+            for at in range(groups):
+                unpack(held.at[at], rows_ref, at * slots)
+
+        pre_gate_ref[...] = dot(rows_ref[...], gate_ref[...])
+        pre_up_ref[...] = dot(rows_ref[...], up_ref[...])
+
+    total = groups * slots
+    return pl.pallas_call(
+        kernel,
+        grid=(hid // tile,),
+        out_shape=[
+            jax.ShapeDtypeStruct((total, width), jnp.bfloat16),
+            jax.ShapeDtypeStruct((total, hid), jnp.float32),
+            jax.ShapeDtypeStruct((total, hid), jnp.float32),
+        ],
+        in_specs=anywhere(groups) + [column_tile(width, tile)] * 2,
+        out_specs=[
+            pl.BlockSpec((total, width), lambda i: (0, 0)),
+            column_tile(total, tile),
+            column_tile(total, tile),
+        ],
+        scratch_shapes=[
+            pltpu.VMEM((groups,) + packed[0].shape, jnp.bfloat16),
+            pltpu.SemaphoreType.DMA((groups,)),
+        ],
+        compiler_params=params(24),
+        cost_estimate=cost(4 * total * width * hid, 4 * width * hid + 4 * total * width),
+        name="forward",
+    )(*packed, gate_proj, up_proj)
+
+
+def hidden_grads(pre_gate, pre_up, d_hidden):
+    sig = jax.nn.sigmoid(pre_gate)
+    silu = pre_gate * sig
+    hidden = (silu * pre_up).astype(jnp.bfloat16)
+    d_gate = (d_hidden * pre_up * sig * (1.0 + pre_gate * (1.0 - sig))).astype(jnp.bfloat16)
+    d_up = (d_hidden * silu).astype(jnp.bfloat16)
+    return hidden, d_gate, d_up
+
+
+def back(tile, packed, pre_gate, pre_up, gate_proj, up_proj, down_proj):
+    blocks = packed.shape[0]
+    width, hid = gate_proj.shape
+    slots = blocks * MOST
+    pieces, step = cut(width)
+
+    def kernel(packed_ref, pre_gate_ref, pre_up_ref, gate_ref, up_ref, down_ref, *rest):
+        out, scaled, hidden_ref, d_gate_ref, d_up_ref, held, total, arrived = rest
+
+        @pl.when(pl.program_id(0) == 0)
+        def _():
+            load([packed_ref], [held], arrived)
+            unpack(held, scaled, 0)
+
+        d_hidden = dot(scaled[...], down_ref[...], BY_WIDTH)
+        hidden, d_gate, d_up = hidden_grads(pre_gate_ref[...], pre_up_ref[...], d_hidden)
+        hidden_ref[...] = hidden
+        d_gate_ref[...] = d_gate
+        d_up_ref[...] = d_up
+        part = dot(d_gate, gate_ref[...], BY_WIDTH) + dot(d_up, up_ref[...], BY_WIDTH)
+
+        @pl.when(pl.program_id(0) == 0)
+        def _():
+            total[...] = part
+
+        @pl.when(pl.program_id(0) > 0)
+        def _():
+            total[...] += part
+
+        @pl.when(pl.program_id(0) == hid // tile - 1)
+        def _():
+            done = total[...].astype(jnp.bfloat16)
+            extra = jnp.zeros((blocks * ROWS, step), jnp.float32)
+            for at in range(pieces):
+                extra += dot(
+                    spill_picks(blocks, pieces, at),
+                    done[blocks * ROWS :, at * step : (at + 1) * step],
+                    BY_ROWS,
+                )
+            extra = extra.astype(jnp.bfloat16)
+            for block in range(blocks):
+                part_of = slice(block * ROWS, (block + 1) * ROWS)
+                out[block, :, :width] = done[part_of]
+                out[block, :, width:] = extra[part_of]
+
+    factor = jax.ShapeDtypeStruct((slots, hid), jnp.bfloat16)
+    return pl.pallas_call(
+        kernel,
+        grid=(hid // tile,),
+        out_shape=[
+            jax.ShapeDtypeStruct(packed.shape, jnp.bfloat16),
+            jax.ShapeDtypeStruct((slots, width), jnp.bfloat16),
+            factor,
+            factor,
+            factor,
+        ],
+        in_specs=anywhere(1)
+        + [column_tile(slots, tile)] * 2
+        + [column_tile(width, tile)] * 2
+        + [row_tile(tile, width)],
+        out_specs=[
+            pl.BlockSpec(packed.shape, lambda i: (0, 0, 0)),
+            pl.BlockSpec((slots, width), lambda i: (0, 0)),
+        ]
+        + [column_tile(slots, tile)] * 3,
+        scratch_shapes=[
+            pltpu.VMEM(packed.shape, jnp.bfloat16),
+            pltpu.VMEM((slots, width), jnp.float32),
+            pltpu.SemaphoreType.DMA((1,)),
+        ],
+        compiler_params=params(24),
+        cost_estimate=cost(6 * slots * width * hid, 6 * width * hid),
+        name="back",
+    )(packed, pre_gate, pre_up, gate_proj, up_proj, down_proj)
+
+
+def weight_grads(tile, groups, part, packed, rows, pre_gate, pre_up, down_proj, own=(), sums=()):
+    others = len(packed)
+    blocks = packed[0].shape[0]
+    hid, width = down_proj.shape
+    slots = blocks * MOST
+    known = slots if own else 0
+    some = others * slots
+    share = width // groups
+    loaded = others + 1 + len(own[:1])
+
+    def kernel(part_ref, *refs):
+        refs = list(refs)
+        sources = [refs.pop(0) for _ in range(loaded)]
+        pre_gate_ref, pre_up_ref, down_ref = [refs.pop(0) for _ in range(3)]
+        factors = [refs.pop(0) for _ in own[1:]]
+        added = [refs.pop(0) for _ in sums]
+        d_gate_ref, d_up_ref, d_down_ref, held, scaled, x_mine, dy_mine, arrived = refs
+
+        @pl.when(pl.program_id(0) == 0)
+        def _():
+            columns = pl.ds(pl.multiple_of(part_ref[0] * share, share), share)
+            here = [source.at[:, columns] for source in sources[others:]]
+            targets = [held.at[at] for at in range(others)] + [x_mine]
+            targets += [dy_mine.at[:known, :]] if own else []
+            load(sources[:others] + here, targets, arrived)
+            for at in range(others):
+                unpack(held.at[at], scaled, at * slots)
+            dy_mine[known:, :] = scaled[:, columns]
+
+        d_hidden = dot(scaled[...], down_ref[...], BY_WIDTH)
+        hidden, d_gate, d_up = hidden_grads(pre_gate_ref[...], pre_up_ref[...], d_hidden)
+        if own:
+            hidden = jnp.concatenate([factors[0][...], hidden], 0)
+            d_gate = jnp.concatenate([factors[1][...], d_gate], 0)
+            d_up = jnp.concatenate([factors[2][...], d_up], 0)
+        both = dot(x_mine[...], jnp.concatenate([d_gate, d_up], 1), BY_ROWS)
+        d_gate, d_up = both[:, :tile], both[:, tile:]
+        d_down = dot(hidden, dy_mine[...], BY_ROWS)
+        if sums:
+            d_gate += added[0][...]
+            d_up += added[1][...]
+            d_down += added[2][...]
+        d_gate_ref[...] = d_gate
+        d_up_ref[...] = d_up
+        d_down_ref[...] = d_down
+
+    at_row = known // some
+    behind = pl.BlockSpec((some, tile), lambda i: (at_row, i))
+    grads = [column_tile(share, tile), column_tile(share, tile), row_tile(tile, share)]
+    return pl.pallas_call(
+        kernel,
+        grid=(hid // tile,),
+        out_shape=[
+            jax.ShapeDtypeStruct((share, hid), jnp.float32),
+            jax.ShapeDtypeStruct((share, hid), jnp.float32),
+            jax.ShapeDtypeStruct((hid, share), jnp.float32),
+        ],
+        in_specs=[pl.BlockSpec(memory_space=pltpu.SMEM)]
+        + anywhere(loaded)
+        + [behind] * 2
+        + [row_tile(tile, width)]
+        + [column_tile(slots, tile)] * len(own[1:])
+        + grads[: len(sums)],
+        out_specs=grads,
+        scratch_shapes=[
+            pltpu.VMEM((others,) + packed[0].shape, jnp.bfloat16),
+            pltpu.VMEM((some, width), jnp.bfloat16),
+            pltpu.VMEM((known + some, share), jnp.bfloat16),
+            pltpu.VMEM((known + some, share), jnp.bfloat16),
+            pltpu.SemaphoreType.DMA((loaded,)),
+        ],
+        compiler_params=params(24),
+        cost_estimate=cost(
+            2 * some * width * hid + 6 * (known + some) * share * hid,
+            2 * width * hid + 4 * some * width,
+        ),
+        name="weight_grads",
+    )(part, *packed, rows, *own[:1], pre_gate, pre_up, down_proj, *own[1:], *sums)
+
+
+def swap(value, axis, distance):
+    size = lax.axis_size(axis)
+    return lax.ppermute(value, axis, [(at, at ^ distance) for at in range(size)])
+
+
+def exchange(blocks):
+    return lax.all_to_all(blocks, "expert", split_axis=0, concat_axis=0, tiled=True)
+
+
+def after(value, *earlier):
+    return lax.optimization_barrier((value, *earlier))[0]
+
+
+def gather_body(tokens, cotangent, routes, expert_gates, gate_proj, up_proj, down_proj):
+    blocks, groups = lax.axis_size("expert"), lax.axis_size("dp")
+    tile = 256
+    part = lax.axis_index("dp").astype(jnp.int32).reshape(1)
+    routes = routes.reshape(1, -1)
+    gates = expert_gates.reshape(1, -1)
+    x_own = exchange(pack(blocks, routes, tokens))
+    x_far = swap(x_own, "dp", 2)
+    x_near = swap(x_own, "dp", 1)
+    dy_own = exchange(after(pack(blocks, routes, cotangent, gates), x_own))
+    rows, pre_gate, pre_up = forward(tile, [x_own, x_near], gate_proj, up_proj)
+    x_last = swap(x_far, "dp", 1)
+    dy_far = swap(dy_own, "dp", 2)
+    dy_near = swap(dy_own, "dp", 1)
+    sent, *own = back(tile, dy_own, pre_gate, pre_up, gate_proj, up_proj, down_proj)
+    returned = exchange(sent)
+    far_rows, far_gate, far_up = forward(
+        tile, [after(x_far, sent), x_last], gate_proj, up_proj
+    )
+    sums = weight_grads(
+        tile, groups, part, [dy_near], rows, pre_gate, pre_up, down_proj, own=own
+    )
+    dy_last = swap(after(dy_far, sent), "dp", 1)
+    grads = weight_grads(
+        tile, groups, part, [dy_far, dy_last], far_rows, far_gate, far_up, down_proj, sums=sums
+    )
+    return (merge(routes, returned), *grads)
+
+
+def body(tokens, cotangent, routes, expert_gates, gate_proj, up_proj, down_proj):
+    groups, blocks = lax.axis_size("dp"), lax.axis_size("expert")
+    width, hid = gate_proj.shape
+    rows_sent = (groups - 1) * 2 * blocks * MOST * width
+    grads_sent = 3 * width * hid * (groups - 1) // groups
+    fits = blocks == EXPERTS and groups == 4 and hid % 256 == 0
+    fits = fits and tokens.shape[0] == 128 and routes.shape[1] == 1 and width // groups % 128 == 0
+    chosen = gather_body if fits and rows_sent < grads_sent else scatter_body
+    return chosen(tokens, cotangent, routes, expert_gates, gate_proj, up_proj, down_proj)
+
+
 def solution(mesh):
     in_specs = (
         P(("dp", "expert"), None),

time: 209 us -> 111 us (0.53)
  waiting for transfers between devices: 113 us -> 29.2 us
  Pallas kernels: 0 us -> 35.2 us
  matrix products: 24 us -> 0 us
  other arithmetic: 16.2 us -> 0 us
  between operations: 13.9 us -> 0.97 us
  starting transfers between devices: 15.8 us -> 19.7 us
    reduce_scatter x3 -> x0, waiting for transfers between devices: 65.2 us -> none  [the longest x1 38.1 us: body(): lax.psum_scatter(grad_up.astype(jnp.bfloat16), 'dp', scatter_dimension=0,...]
    pallas_call x0 -> x8, Pallas kernels: none -> 35.2 us  [the longest x2 14.3 us: weight_grads(): pl.pallas_call(kernel, grid=(hid // tile,), out_shape=[jax.ShapeDtypeStru...]
    unnamed x10 -> x76, local copies, waits for them, and re-layouts: 0.48 us -> 25.2 us
    dot_general x7 -> x0, matrix products: 24 us -> none  [the longest x1 6.2 us: body(): lax.dot_general(joined_grads, joined_proj, by_width, preferred_element_ty...]
    all_to_all x3, waiting for transfers between devices: 47.6 us -> 27.4 us  [exchange(): lax.all_to_all(blocks, 'expert', split_axis=0, concat_axis=0, tiled=True)]
    convert_element_type x6 -> x0, other arithmetic: 12.5 us -> none  [the longest x3 7.34 us: body(): grad_gate, grad_up, grad_down = (lax.psum_scatter(grad_gate.astype(jnp.bf...]
    gather x3 -> x0, local copies, waits for them, and re-layouts: 10.3 us -> none  [the longest x1 3.49 us: body(): jnp.take(cotangent, slot_table, axis=0, mode='fill', fill_value=0)]
    reshape x4 -> x0, local copies, waits for them, and re-layouts: 8.5 us -> none  [the longest x1 2.13 us: body(): scaled = dy_recv.reshape(expert_devs * capacity, model_dim)]
  transfers between devices with their start and end apart: 6 -> 9, of which waited for: 5 -> 3; matrix products, arithmetic and copies ran while one was open for 20% -> 0% of each run, Pallas kernels for 0% -> 24%
where the time goes in v2:
time: 111 us; the launch traced here: 110 us
  Pallas kernels  35.2 us (32%)
  waiting for transfers between devices  29.2 us (26%)
  local copies, waits for them, and re-layouts  25.2 us (23%)
  starting transfers between devices  19.7 us (18%)
    all_to_all x3, waiting for transfers between devices, exchange(): lax.all_to_all(blocks, 'expert', split_axis=0, concat_axis=0, tiled=True)  27.4 us
    unnamed x76, local copies, waits for them, and re-layouts  25.2 us
    all_to_all x3, starting transfers between devices, exchange(): lax.all_to_all(blocks, 'expert', split_axis=0, concat_axis=0, tiled=True)  15.9 us
    pallas_call x2, Pallas kernels, weight_grads(): pl.pallas_call(kernel, grid=(hid // tile,), out_shape=[jax.ShapeDtypeStru...  14.3 us
    pallas_call x2, Pallas kernels, forward(): pl.pallas_call(kernel, grid=(hid // tile,), out_shape=[jax.ShapeDtypeStru...  9.27 us
    pallas_call x1, Pallas kernels, back(): pl.pallas_call(kernel, grid=(hid // tile,), out_shape=[jax.ShapeDtypeStru...  7.81 us
    ppermute x6, starting transfers between devices, swap(): lax.ppermute(value, axis, [(at, at ^ distance) for at in range(size)])  3.82 us
    pallas_call x1, Pallas kernels, merge(): pl.pallas_call(kernel, out_shape=jax.ShapeDtypeStruct((tokens, width), jn...  2.57 us
  transfers between devices with their start and end apart: 9, of which 3 were waited for; matrix products, arithmetic and copies ran while one was open for 0% of the time, Pallas kernels for 24%

profile of v2, /device:TPU:0, one launch (start us, length us, event | category | flops | bytes accessed | tf_op | source)
XLA Modules:
  0.0 110.3 jit_solution(16727361750455511326)
XLA Ops:
  3.8 7.5 %all-to-all-start = ((bf16[8,16,2304]{2,1,0:T(8,128)(2,1)}), bf16[8,16,2304]{2,1,0:T(8,128)(2,1)}, u32[]{:S(2)}, u32[]{:S(2)}) async-start(bf16[8,16,2304]{2,1,0:T(8,128)(2,1)} %copy-done.11), calls=%async_computation | async-start | bytes 1179648 | tf_op jit(solution)/shard_map/all_to_all | solution.py:477
  13.9 13.5 %all-to-all-done.refs_0_ = bf16[8,16,2304]{2,1,0:T(8,128)(2,1)} async-done(((bf16[8,16,2304]{2,1,0:T(8,128)(2,1)}), bf16[8,16,2304]{2,1,0:T(8,128)(2,1)}, u32[]{:S(2)}, u32[]{:S(2)}) %all-to-all-start) | async-done | bytes 589856 | tf_op jit(solution)/shard_map/all_to_all | solution.py:477
  27.3 4.2 %all-to-all-start.1 = ((bf16[8,16,2304]{2,1,0:T(8,128)(2,1)}), bf16[8,16,2304]{2,1,0:T(8,128)(2,1)}, u32[]{:S(2)}, u32[]{:S(2)}) async-start(bf16[8,16,2304]{2,1,0:T(8,128)(2,1)} %copy-done.10), calls=%async_computation.1 | async-start | bytes 1179648 | tf_op jit(solution)/shard_map/all_to_all | solution.py:477
  31.6 1.6 %collective-permute-start.3 = (bf16[8,16,2304]{2,1,0:T(8,128)(2,1)}, bf16[8,16,2304]{2,1,0:T(8,128)(2,1)}, u32[]{:S(2)}, u32[]{:S(2)}) collective-permute-start(bf16[8,16,2304]{2,1,0:T(8,128)(2,1)} %all-to-all-done.refs_0_), channel_id=1, source_target_pairs={{0,16},{8,24},{16,0},{24,8},{1,17},{9,25},{17,1},{25,9},{2,18},{10... | collective-permute-start | bytes 1769480 | tf_op jit(solution)/shard_map/ppermute | solution.py:473
  33.2 14.0 %all-to-all-done.1.packed_ref = bf16[8,16,2304]{2,1,0:T(8,128)(2,1)} async-done(((bf16[8,16,2304]{2,1,0:T(8,128)(2,1)}), bf16[8,16,2304]{2,1,0:T(8,128)(2,1)}, u32[]{:S(2)}, u32[]{:S(2)}) %all-to-all-start.1) | async-done | bytes 589856 | tf_op jit(solution)/shard_map/all_to_all | solution.py:477
  47.2 1.5 %collective-permute-start.1 = (bf16[8,16,2304]{2,1,0:T(8,128)(2,1)}, bf16[8,16,2304]{2,1,0:T(8,128)(2,1)}, u32[]{:S(2)}, u32[]{:S(2)}) collective-permute-start(bf16[8,16,2304]{2,1,0:T(8,128)(2,1)} %all-to-all-done.1.packed_ref), channel_id=1, source_target_pairs={{0,16},{8,24},{16,0},{24,8},{1,17},{9,25},{17,1},{25,9},{2,18},{10... | collective-permute-start | bytes 1769480 | tf_op jit(solution)/shard_map/ppermute | solution.py:473
  48.7 1.9 %copy-done.1 = bf16[2048,768]{1,0:T(8,128)(2,1)S(1)} copy-done((bf16[2048,768]{1,0:T(8,128)(2,1)S(1)}, bf16[2048,768]{1,0:T(8,128)(2,1)}, u32[]{:S(2)}) %copy-start.1) | copy-done | bytes 3145752
  50.6 4.6 %forward.2 = (bf16[288,2048]{1,0:T(8,128)(2,1)S(1)}, f32[288,768]{1,0:T(8,128)S(1)}, f32[288,768]{1,0:T(8,128)S(1)}) custom-call(bf16[8,16,2304]{2,1,0:T(8,128)(2,1)} %all-to-all-done.refs_0_, bf16[8,16,2304]{2,1,0:T(8,128)(2,1)} %collective-permute-done.refs_1_, bf16[2048,768]{1,0:T(8,128)(2,1)S(1)} %copy-done, bf16[2048,768]{1,0:T(8,128)(2,1)S(1)} %copy-done.1), custom_call_target="tpu_custom_call" | custom-call | flops 1811939328 | bytes 8650752 | tf_op jit(solution)/shard_map/forward/pallas_call | solution.py:282
  56.2 7.8 %back.1 = (bf16[8,16,2304]{2,1,0:T(8,128)(2,1)S(1)}, bf16[144,2048]{1,0:T(8,128)(2,1)S(1)}, bf16[144,768]{1,0:T(8,128)(2,1)S(1)}, bf16[144,768]{1,0:T(8,128)(2,1)S(1)}, bf16[144,768]{1,0:T(8,128)(2,1)S(1)}) custom-call(bf16[8,16,2304]{2,1,0:T(8,128)(2,1)} %all-to-all-done.1.packed_ref, f32[288,768]{1,0:T(8,128)S(1)} %get-tuple-element.25.pre_gate_ref.refs_3_, ...), custom_call_target="tpu_custom_call" | custom-call | flops 1358954496 | bytes 9437184 | tf_op jit(solution)/shard_map/back/pallas_call | solution.py:361
  67.1 4.2 %all-to-all-start.2 = ((bf16[8,16,2304]{2,1,0:T(8,128)(2,1)}), bf16[8,16,2304]{2,1,0:T(8,128)(2,1)}, u32[]{:S(2)}, u32[]{:S(2)}) async-start(bf16[8,16,2304]{2,1,0:T(8,128)(2,1)} %copy-done.28), calls=%async_computation.2 | async-start | bytes 1179648 | tf_op jit(solution)/shard_map/all_to_all | solution.py:477
  72.0 1.8 %collective-permute-done.4.refs_1_ = bf16[8,16,2304]{2,1,0:T(8,128)(2,1)} collective-permute-done((bf16[8,16,2304]{2,1,0:T(8,128)(2,1)}, bf16[8,16,2304]{2,1,0:T(8,128)(2,1)}, u32[]{:S(2)}, u32[]{:S(2)}) %collective-permute-start.4) | collective-permute-done | bytes 589856 | tf_op jit(solution)/shard_map/ppermute | solution.py:473
  73.7 1.9 %copy-done.2 = bf16[2048,768]{1,0:T(8,128)(2,1)S(1)} copy-done((bf16[2048,768]{1,0:T(8,128)(2,1)S(1)}, bf16[2048,768]{1,0:T(8,128)(2,1)}, u32[]{:S(2)}) %copy-start.2) | copy-done | bytes 3145752
  75.6 4.7 %forward.3 = (bf16[288,2048]{1,0:T(8,128)(2,1)S(1)}, f32[288,768]{1,0:T(8,128)S(1)}, f32[288,768]{1,0:T(8,128)S(1)}) custom-call(bf16[8,16,2304]{2,1,0:T(8,128)(2,1)} %collective-permute-done.3.refs_0_, bf16[8,16,2304]{2,1,0:T(8,128)(2,1)} %collective-permute-done.4.refs_1_, bf16[2048,768]{1,0:T(8,128)(2,1)S(1)} %copy-done, bf16[2048,768]{1,0:T(8,128)(2,1)S(1)} %copy-done.2), custom_call_target="tpu_custom_call" | custom-call | flops 1811939328 | bytes 8650752 | tf_op jit(solution)/shard_map/forward/pallas_call | solution.py:282
  83.3 6.4 %weight_grads.2 = (f32[512,768]{1,0:T(8,128)S(1)}, f32[512,768]{1,0:T(8,128)S(1)}, f32[768,512]{1,0:T(8,128)S(1)}) custom-call(s32[1]{0:T(128)} %bitcast.2.part_ref, bf16[8,16,2304]{2,1,0:T(8,128)(2,1)} %collective-permute-done.5.refs_0_, bf16[288,2048]{1,0:T(8,128)(2,1)S(1)} %copy-done.19, bf16[144,2048]{1,0:T(8,128)(2,1)S(1)} %copy-done.27, ...), custom_call_target="tpu_custom_call" | custom-call | flops 1132462080 | bytes 4325376 | tf_op jit(solution)/shard_map/weight_grads/pallas_call | solution.py:440
  89.8 1.1 %copy-done.12 = f32[512,768]{1,0:T(8,128)} copy-done((f32[512,768]{1,0:T(8,128)}, f32[512,768]{1,0:T(8,128)S(1)}, u32[]{:S(2)}) %copy-start.12) | copy-done | bytes 1572888
  90.9 1.1 %copy-done.14 = f32[512,768]{1,0:T(8,128)} copy-done((f32[512,768]{1,0:T(8,128)}, f32[512,768]{1,0:T(8,128)S(1)}, u32[]{:S(2)}) %copy-start.14) | copy-done | bytes 1572888
  92.0 1.1 %copy-done.16 = f32[768,512]{1,0:T(8,128)} copy-done((f32[768,512]{1,0:T(8,128)}, f32[768,512]{1,0:T(8,128)S(1)}, u32[]{:S(2)}) %copy-start.16) | copy-done | bytes 1572888
  93.2 2.6 %merge.1 = bf16[128,2048]{1,0:T(8,128)(2,1)} custom-call(s32[1,128]{1,0:T(1,128)S(1)} %bitcast.5, bf16[8,16,2304]{2,1,0:T(8,128)(2,1)} %all-to-all-done.2.back_ref), custom_call_target="tpu_custom_call" | custom-call | flops 134217728 | bytes 1048576 | tf_op jit(solution)/shard_map/merge/pallas_call | solution.py:212
  95.8 1.4 %copy-done.13 = f32[512,768]{1,0:T(8,128)S(1)} copy-done((f32[512,768]{1,0:T(8,128)S(1)}, f32[512,768]{1,0:T(8,128)}, u32[]{:S(2)}) %copy-start.13) | copy-done | bytes 1572888
  97.2 1.4 %copy-done.15 = f32[512,768]{1,0:T(8,128)S(1)} copy-done((f32[512,768]{1,0:T(8,128)S(1)}, f32[512,768]{1,0:T(8,128)}, u32[]{:S(2)}) %copy-start.15) | copy-done | bytes 1572888
  98.6 1.4 %copy-done.17 = f32[768,512]{1,0:T(8,128)S(1)} copy-done((f32[768,512]{1,0:T(8,128)S(1)}, f32[768,512]{1,0:T(8,128)}, u32[]{:S(2)}) %copy-start.17) | copy-done | bytes 1572888
  100.0 1.3 %copy-done.21 = bf16[288,2048]{1,0:T(8,128)(2,1)S(1)} copy-done((bf16[288,2048]{1,0:T(8,128)(2,1)S(1)}, bf16[288,2048]{1,0:T(8,128)(2,1)}, u32[]{:S(2)}) %copy-start.21) | copy-done | bytes 1179672
  101.3 1.2 %copy-done.25 = f32[288,768]{1,0:T(8,128)S(1)} copy-done((f32[288,768]{1,0:T(8,128)S(1)}, f32[288,768]{1,0:T(8,128)}, u32[]{:S(2)}) %copy-start.25) | copy-done | bytes 884760
  102.5 7.8 %weight_grads.3 = (f32[512,768]{1,0:T(8,128)}, f32[512,768]{1,0:T(8,128)}, f32[768,512]{1,0:T(8,128)}) custom-call(s32[1]{0:T(128)} %bitcast.2.part_ref, bf16[8,16,2304]{2,1,0:T(8,128)(2,1)} %collective-permute-done.1.refs_0_, bf16[8,16,2304]{2,1,0:T(8,128)(2,1)} %collective-permute-done.2.refs_1_, bf16[288,2048]{1,0:T(8,128)(2,1)S(1)} %copy-done.21, ...), custom_call_target="tpu_custom_call" | custom-call | flops 1585446912 | bytes 5505024 | tf_op jit(solution)/shard_map/weight_grads/pallas_call | solution.py:440
  (78 shorter events, 13.4 us)
Async XLA Ops:
  0.6 10.7 %copy-start.36 = (s32[128,1]{0,1:T(1,128)S(1)}, s32[128,1]{0,1:T(1,128)}, u32[]{:S(2)}) copy-start(s32[128,1]{0,1:T(1,128)} %param.9) | copy-start | bytes 1540
  0.6 10.7 %copy-start.37 = (f32[128,1]{0,1:T(1,128)S(1)}, f32[128,1]{0,1:T(1,128)}, u32[]{:S(2)}) copy-start(f32[128,1]{0,1:T(1,128)} %param.10) | copy-start | bytes 1540
  3.8 44.9 %copy-start = (bf16[2048,768]{1,0:T(8,128)(2,1)S(1)}, bf16[2048,768]{1,0:T(8,128)(2,1)}, u32[]{:S(2)}) copy-start(bf16[2048,768]{1,0:T(8,128)(2,1)} %refs_2_.3) | copy-start | bytes 9437188
  3.8 23.5 %all-to-all-start = ((bf16[8,16,2304]{2,1,0:T(8,128)(2,1)}), bf16[8,16,2304]{2,1,0:T(8,128)(2,1)}, u32[]{:S(2)}, u32[]{:S(2)}) async-start(bf16[8,16,2304]{2,1,0:T(8,128)(2,1)} %copy-done.11), calls=%async_computation | async-start | bytes 1179648 | tf_op jit(solution)/shard_map/all_to_all | solution.py:477
  27.3 19.8 %all-to-all-start.1 = ((bf16[8,16,2304]{2,1,0:T(8,128)(2,1)}), bf16[8,16,2304]{2,1,0:T(8,128)(2,1)}, u32[]{:S(2)}, u32[]{:S(2)}) async-start(bf16[8,16,2304]{2,1,0:T(8,128)(2,1)} %copy-done.10), calls=%async_computation.1 | async-start | bytes 1179648 | tf_op jit(solution)/shard_map/all_to_all | solution.py:477
  31.5 17.2 %collective-permute-start = (bf16[8,16,2304]{2,1,0:T(8,128)(2,1)}, bf16[8,16,2304]{2,1,0:T(8,128)(2,1)}, u32[]{:S(2)}, u32[]{:S(2)}) collective-permute-start(bf16[8,16,2304]{2,1,0:T(8,128)(2,1)} %all-to-all-done.refs_0_), channel_id=1, source_target_pairs={{0,8},{8,0},{16,24},{24,16},{1,9},{9,1},{17,25},{25,17},{2,10},{10... | collective-permute-start | bytes 1769480 | tf_op jit(solution)/shard_map/ppermute | solution.py:473
  31.6 39.7 %collective-permute-start.3 = (bf16[8,16,2304]{2,1,0:T(8,128)(2,1)}, bf16[8,16,2304]{2,1,0:T(8,128)(2,1)}, u32[]{:S(2)}, u32[]{:S(2)}) collective-permute-start(bf16[8,16,2304]{2,1,0:T(8,128)(2,1)} %all-to-all-done.refs_0_), channel_id=1, source_target_pairs={{0,16},{8,24},{16,0},{24,8},{1,17},{9,25},{17,1},{25,9},{2,18},{10... | collective-permute-start | bytes 1769480 | tf_op jit(solution)/shard_map/ppermute | solution.py:473
  47.2 24.7 %collective-permute-start.1 = (bf16[8,16,2304]{2,1,0:T(8,128)(2,1)}, bf16[8,16,2304]{2,1,0:T(8,128)(2,1)}, u32[]{:S(2)}, u32[]{:S(2)}) collective-permute-start(bf16[8,16,2304]{2,1,0:T(8,128)(2,1)} %all-to-all-done.1.packed_ref), channel_id=1, source_target_pairs={{0,16},{8,24},{16,0},{24,8},{1,17},{9,25},{17,1},{25,9},{2,18},{10... | collective-permute-start | bytes 1769480 | tf_op jit(solution)/shard_map/ppermute | solution.py:473
  50.6 5.6 %copy-start.3 = (bf16[768,2048]{1,0:T(8,128)(2,1)S(1)}, bf16[768,2048]{1,0:T(8,128)(2,1)}, u32[]{:S(2)}) copy-start(bf16[768,2048]{1,0:T(8,128)(2,1)} %refs_5_.3) | copy-start | bytes 9437188
  56.2 7.8 %copy-start.6 = (f32[288,768]{1,0:T(8,128)}, f32[288,768]{1,0:T(8,128)S(1)}, u32[]{:S(2)}) copy-start(f32[288,768]{1,0:T(8,128)S(1)} %get-tuple-element.25.pre_gate_ref.refs_3_) | copy-start | bytes 2654212
  56.2 7.8 %copy-start.8 = (f32[288,768]{1,0:T(8,128)}, f32[288,768]{1,0:T(8,128)S(1)}, u32[]{:S(2)}) copy-start(f32[288,768]{1,0:T(8,128)S(1)} %get-tuple-element.26.pre_up_ref.refs_4_) | copy-start | bytes 2654212
  67.1 26.1 %all-to-all-start.2 = ((bf16[8,16,2304]{2,1,0:T(8,128)(2,1)}), bf16[8,16,2304]{2,1,0:T(8,128)(2,1)}, u32[]{:S(2)}, u32[]{:S(2)}) async-start(bf16[8,16,2304]{2,1,0:T(8,128)(2,1)} %copy-done.28), calls=%async_computation.2 | async-start | bytes 1179648 | tf_op jit(solution)/shard_map/all_to_all | solution.py:477
  71.3 2.4 %collective-permute-start.4 = (bf16[8,16,2304]{2,1,0:T(8,128)(2,1)}, bf16[8,16,2304]{2,1,0:T(8,128)(2,1)}, u32[]{:S(2)}, u32[]{:S(2)}) collective-permute-start(bf16[8,16,2304]{2,1,0:T(8,128)(2,1)} %collective-permute-done.3.refs_0_), channel_id=1, source_target_pairs={{0,8},{8,0},{16,24},{24,16},{1,9},{9,1},{17,25},{25,17},{2,10},{10... | collective-permute-start | bytes 1769480 | tf_op jit(solution)/shard_map/ppermute | solution.py:473
  71.4 11.9 %collective-permute-start.5 = (bf16[8,16,2304]{2,1,0:T(8,128)(2,1)}, bf16[8,16,2304]{2,1,0:T(8,128)(2,1)}, u32[]{:S(2)}, u32[]{:S(2)}) collective-permute-start(bf16[8,16,2304]{2,1,0:T(8,128)(2,1)} %all-to-all-done.1.packed_ref), channel_id=1, source_target_pairs={{0,8},{8,0},{16,24},{24,16},{1,9},{9,1},{17,25},{25,17},{2,10},{10... | collective-permute-start | bytes 1769480 | tf_op jit(solution)/shard_map/ppermute | solution.py:473
  71.9 23.9 %collective-permute-start.2 = (bf16[8,16,2304]{2,1,0:T(8,128)(2,1)}, bf16[8,16,2304]{2,1,0:T(8,128)(2,1)}, u32[]{:S(2)}, u32[]{:S(2)}) collective-permute-start(bf16[8,16,2304]{2,1,0:T(8,128)(2,1)} %collective-permute-done.1.refs_0_), channel_id=1, source_target_pairs={{0,8},{8,0},{16,24},{24,16},{1,9},{9,1},{17,25},{25,17},{2,10},{10... | collective-permute-start | bytes 1769480 | tf_op jit(solution)/shard_map/ppermute | solution.py:473
  75.6 7.7 %copy-start.4 = (bf16[768,2048]{1,0:T(8,128)(2,1)S(1)}, bf16[768,2048]{1,0:T(8,128)(2,1)}, u32[]{:S(2)}) copy-start(bf16[768,2048]{1,0:T(8,128)(2,1)} %refs_5_.3) | copy-start | bytes 9437188
  75.6 7.7 %copy-start.7 = (f32[288,768]{1,0:T(8,128)S(1)}, f32[288,768]{1,0:T(8,128)}, u32[]{:S(2)}) copy-start(f32[288,768]{1,0:T(8,128)} %copy-done.6) | copy-start | bytes 2654212
  75.6 7.7 %copy-start.9 = (f32[288,768]{1,0:T(8,128)S(1)}, f32[288,768]{1,0:T(8,128)}, u32[]{:S(2)}) copy-start(f32[288,768]{1,0:T(8,128)} %copy-done.8) | copy-start | bytes 2654212
  75.6 7.7 %copy-start.19 = (bf16[288,2048]{1,0:T(8,128)(2,1)S(1)}, bf16[288,2048]{1,0:T(8,128)(2,1)}, u32[]{:S(2)}) copy-start(bf16[288,2048]{1,0:T(8,128)(2,1)} %copy-done.18) | copy-start | bytes 3538948
  75.6 7.7 %copy-start.27 = (bf16[144,2048]{1,0:T(8,128)(2,1)S(1)}, bf16[144,2048]{1,0:T(8,128)(2,1)}, u32[]{:S(2)}) copy-start(bf16[144,2048]{1,0:T(8,128)(2,1)} %copy-done.26) | copy-start | bytes 1769476
  75.6 7.7 %copy-start.32 = (bf16[144,768]{1,0:T(8,128)(2,1)S(1)}, bf16[144,768]{1,0:T(8,128)(2,1)}, u32[]{:S(2)}) copy-start(bf16[144,768]{1,0:T(8,128)(2,1)} %copy-done.31) | copy-start | bytes 663556
  75.6 7.7 %copy-start.34 = (bf16[144,768]{1,0:T(8,128)(2,1)S(1)}, bf16[144,768]{1,0:T(8,128)(2,1)}, u32[]{:S(2)}) copy-start(bf16[144,768]{1,0:T(8,128)(2,1)} %copy-done.33) | copy-start | bytes 663556
  83.3 12.5 %copy-start.5 = (bf16[768,2048]{1,0:T(8,128)(2,1)S(1)}, bf16[768,2048]{1,0:T(8,128)(2,1)}, u32[]{:S(2)}) copy-start(bf16[768,2048]{1,0:T(8,128)(2,1)} %refs_5_.3) | copy-start | bytes 9437188
  93.2 2.6 %copy-start.23 = (f32[288,768]{1,0:T(8,128)S(1)}, f32[288,768]{1,0:T(8,128)}, u32[]{:S(2)}) copy-start(f32[288,768]{1,0:T(8,128)} %copy-done.22) | copy-start | bytes 2654212
  (23 other events, 25.2 us)

commit v3 on v2

--- a/solution.py
+++ b/solution.py
@@ -8,6 +8,7 @@
 EXPERTS = 8
 MOST = 18
 ROWS = 16
+VMEM_BYTES = (63 * 1024 + 768) * 1024
 
 
 def build_slots(routes, capacity):
@@ -107,12 +108,12 @@
     return pl.CostEstimate(flops=flops, bytes_accessed=moved, transcendentals=0)
 
 
-def params(mib):
-    return pltpu.CompilerParams(vmem_limit_bytes=mib * 1024 * 1024)
+def params():
+    return pltpu.CompilerParams(vmem_limit_bytes=VMEM_BYTES)
 
 
 def anywhere(count):
-    return [pl.BlockSpec(memory_space=pltpu.HBM)] * count
+    return [pl.BlockSpec(memory_space=pl.ANY)] * count
 
 
 def dot(left, right, dims=(((1,), (0,)), ((), ()))):
@@ -185,7 +186,7 @@
         out_specs=pl.BlockSpec(memory_space=pltpu.VMEM),
         scratch_shapes=[pltpu.VMEM(source.shape, source.dtype) for source in sources]
         + [pltpu.SemaphoreType.DMA((len(sources),))],
-        compiler_params=params(16),
+        compiler_params=params(),
         cost_estimate=cost(4 * blocks * ROWS * tokens * width, 4 * tokens * width),
         name="pack",
     )(*sources)
@@ -219,7 +220,7 @@
             pltpu.VMEM(returned.shape, returned.dtype),
             pltpu.SemaphoreType.DMA((2,)),
         ],
-        compiler_params=params(16),
+        compiler_params=params(),
         cost_estimate=cost(4 * blocks * ROWS * tokens * width, 4 * tokens * width),
         name="merge",
     )(routes, returned)
@@ -297,7 +298,7 @@
             pltpu.VMEM((groups,) + packed[0].shape, jnp.bfloat16),
             pltpu.SemaphoreType.DMA((groups,)),
         ],
-        compiler_params=params(24),
+        compiler_params=params(),
         cost_estimate=cost(4 * total * width * hid, 4 * width * hid + 4 * total * width),
         name="forward",
     )(*packed, gate_proj, up_proj)
@@ -382,7 +383,7 @@
             pltpu.VMEM((slots, width), jnp.float32),
             pltpu.SemaphoreType.DMA((1,)),
         ],
-        compiler_params=params(24),
+        compiler_params=params(),
         cost_estimate=cost(6 * slots * width * hid, 6 * width * hid),
         name="back",
     )(packed, pre_gate, pre_up, gate_proj, up_proj, down_proj)
@@ -459,7 +460,7 @@
             pltpu.VMEM((known + some, share), jnp.bfloat16),
             pltpu.SemaphoreType.DMA((loaded,)),
         ],
-        compiler_params=params(24),
+        compiler_params=params(),
         cost_estimate=cost(
             2 * some * width * hid + 6 * (known + some) * share * hid,
             2 * width * hid + 4 * some * width,
@@ -493,6 +494,7 @@
     dy_own = exchange(after(pack(blocks, routes, cotangent, gates), x_own))
     rows, pre_gate, pre_up = forward(tile, [x_own, x_near], gate_proj, up_proj)
     x_last = swap(x_far, "dp", 1)
+    dy_own = after(dy_own, pre_gate)
     dy_far = swap(dy_own, "dp", 2)
     dy_near = swap(dy_own, "dp", 1)
     sent, *own = back(tile, dy_own, pre_gate, pre_up, gate_proj, up_proj, down_proj)

time: 111 us -> 94.7 us (0.85)
  local copies, waits for them, and re-layouts: 25.2 us -> 0 us
  Pallas kernels: 35.2 us -> 52.3 us
  waiting for transfers between devices: 29.2 us -> 21.4 us
    unnamed x76 -> x0, local copies, waits for them, and re-layouts: 25.2 us -> none
    all_to_all x3, waiting for transfers between devices: 27.4 us -> 18.9 us  [exchange(): lax.all_to_all(blocks, 'expert', split_axis=0, concat_axis=0, tiled=True)]
    pallas_call x2, Pallas kernels: 9.27 us -> 15.6 us  [forward(): pl.pallas_call(kernel, grid=(hid // tile,), out_shape=[jax.ShapeDtypeStru...]
    pallas_call x2, Pallas kernels: 14.3 us -> 18.6 us  [weight_grads(): pl.pallas_call(kernel, grid=(hid // tile,), out_shape=[jax.ShapeDtypeStru...]
    pallas_call x2, Pallas kernels: 1.27 us -> 4.94 us  [pack(): pl.pallas_call(kernel, out_shape=jax.ShapeDtypeStruct((blocks, ROWS, widt...]
    pallas_call x1, Pallas kernels: 7.81 us -> 10.7 us  [back(): pl.pallas_call(kernel, grid=(hid // tile,), out_shape=[jax.ShapeDtypeStru...]
  transfers between devices with their start and end apart: 9 -> 9, of which waited for: 3 -> 4; matrix products, arithmetic and copies ran while one was open for 0% -> 0% of each run, Pallas kernels for 24% -> 42%
where the time goes in v3:
time: 94.7 us; the launch traced here: 94 us
  Pallas kernels  52.3 us (55%)
  waiting for transfers between devices  21.4 us (23%)
  starting transfers between devices  19.5 us (21%)
    all_to_all x3, waiting for transfers between devices, exchange(): lax.all_to_all(blocks, 'expert', split_axis=0, concat_axis=0, tiled=True)  18.9 us
    pallas_call x2, Pallas kernels, weight_grads(): pl.pallas_call(kernel, grid=(hid // tile,), out_shape=[jax.ShapeDtypeStru...  18.6 us
    all_to_all x3, starting transfers between devices, exchange(): lax.all_to_all(blocks, 'expert', split_axis=0, concat_axis=0, tiled=True)  15.7 us
    pallas_call x2, Pallas kernels, forward(): pl.pallas_call(kernel, grid=(hid // tile,), out_shape=[jax.ShapeDtypeStru...  15.6 us
    pallas_call x1, Pallas kernels, back(): pl.pallas_call(kernel, grid=(hid // tile,), out_shape=[jax.ShapeDtypeStru...  10.7 us
    pallas_call x2, Pallas kernels, pack(): pl.pallas_call(kernel, out_shape=jax.ShapeDtypeStruct((blocks, ROWS, widt...  4.94 us
    ppermute x6, starting transfers between devices, swap(): lax.ppermute(value, axis, [(at, at ^ distance) for at in range(size)])  3.83 us
    pallas_call x1, Pallas kernels, merge(): pl.pallas_call(kernel, out_shape=jax.ShapeDtypeStruct((tokens, width), jn...  2.52 us
  transfers between devices with their start and end apart: 9, of which 4 were waited for; matrix products, arithmetic and copies ran while one was open for 0% of the time, Pallas kernels for 42%

profile of v3, /device:TPU:0, one launch (start us, length us, event | category | flops | bytes accessed | tf_op | source)
XLA Modules:
  0.0 94.0 jit_solution(1631450247719614433)
XLA Ops:
  0.6 2.4 %pack.3 = bf16[8,16,2304]{2,1,0:T(8,128)(2,1)} custom-call(s32[1,128]{1,0:T(1,128)} %bitcast.3, bf16[128,2048]{1,0:T(8,128)(2,1)} %refs_1_.3), custom_call_target="tpu_custom_call" | custom-call | flops 134217728 | bytes 1048576 | tf_op jit(solution)/shard_map/pack/pallas_call | solution.py:182
  3.1 7.3 %all-to-all-start = ((bf16[8,16,2304]{2,1,0:T(8,128)(2,1)}), bf16[8,16,2304]{2,1,0:T(8,128)(2,1)}, u32[]{:S(2)}, u32[]{:S(2)}) async-start(bf16[8,16,2304]{2,1,0:T(8,128)(2,1)} %pack.3), calls=%async_computation | async-start | bytes 1179648 | tf_op jit(solution)/shard_map/all_to_all | solution.py:478
  10.4 2.5 %pack.2 = bf16[8,16,2304]{2,1,0:T(8,128)(2,1)} custom-call(s32[1,128]{1,0:T(1,128)} %bitcast.4, bf16[128,2048]{1,0:T(8,128)(2,1)} %refs_1_.2, f32[1,128]{1,0:T(1,128)} %bitcast.6), custom_call_target="tpu_custom_call" | custom-call | flops 134217728 | bytes 1048576 | tf_op jit(solution)/shard_map/pack/pallas_call | solution.py:182
  12.9 13.5 %all-to-all-done.refs_0_ = bf16[8,16,2304]{2,1,0:T(8,128)(2,1)} async-done(((bf16[8,16,2304]{2,1,0:T(8,128)(2,1)}), bf16[8,16,2304]{2,1,0:T(8,128)(2,1)}, u32[]{:S(2)}, u32[]{:S(2)}) %all-to-all-start) | async-done | bytes 589856 | tf_op jit(solution)/shard_map/all_to_all | solution.py:478
  26.4 4.2 %all-to-all-start.1 = ((bf16[8,16,2304]{2,1,0:T(8,128)(2,1)}), bf16[8,16,2304]{2,1,0:T(8,128)(2,1)}, u32[]{:S(2)}, u32[]{:S(2)}) async-start(bf16[8,16,2304]{2,1,0:T(8,128)(2,1)} %pack.2), calls=%async_computation.1 | async-start | bytes 1179648 | tf_op jit(solution)/shard_map/all_to_all | solution.py:478
  30.6 0.1 collective-permute-start
  30.6 1.6 %collective-permute-start.3 = (bf16[8,16,2304]{2,1,0:T(8,128)(2,1)}, bf16[8,16,2304]{2,1,0:T(8,128)(2,1)}, u32[]{:S(2)}, u32[]{:S(2)}) collective-permute-start(bf16[8,16,2304]{2,1,0:T(8,128)(2,1)} %all-to-all-done.refs_0_), channel_id=1, source_target_pairs={{0,16},{8,24},{16,0},{24,8},{1,17},{9,25},{17,1},{25,9},{2,18},{10... | collective-permute-start | bytes 1769480 | tf_op jit(solution)/shard_map/ppermute | solution.py:474
  32.2 0.7 collective-permute-done.refs_1_
  33.0 7.8 %forward.2 = (bf16[288,2048]{1,0:T(8,128)(2,1)}, f32[288,768]{1,0:T(8,128)}, f32[288,768]{1,0:T(8,128)}) custom-call(bf16[8,16,2304]{2,1,0:T(8,128)(2,1)} %all-to-all-done.refs_0_, bf16[8,16,2304]{2,1,0:T(8,128)(2,1)} %collective-permute-done.refs_1_, bf16[2048,768]{1,0:T(8,128)(2,1)} %refs_2_.3, bf16[2048,768]{1,0:T(8,128)(2,1)} %refs_3_.3), custom_call_target="tpu_custom_call" | custom-call | flops 1811939328 | bytes 8650752 | tf_op jit(solution)/shard_map/forward/pallas_call | solution.py:283
  40.8 5.4 %all-to-all-done.1.packed_ref = bf16[8,16,2304]{2,1,0:T(8,128)(2,1)} async-done(((bf16[8,16,2304]{2,1,0:T(8,128)(2,1)}), bf16[8,16,2304]{2,1,0:T(8,128)(2,1)}, u32[]{:S(2)}, u32[]{:S(2)}) %all-to-all-start.1) | async-done | bytes 589856 | tf_op jit(solution)/shard_map/all_to_all | solution.py:478
  46.2 1.5 %collective-permute-start.1 = (bf16[8,16,2304]{2,1,0:T(8,128)(2,1)}, bf16[8,16,2304]{2,1,0:T(8,128)(2,1)}, u32[]{:S(2)}, u32[]{:S(2)}) collective-permute-start(bf16[8,16,2304]{2,1,0:T(8,128)(2,1)} %all-to-all-done.1.packed_ref), channel_id=1, source_target_pairs={{0,16},{8,24},{16,0},{24,8},{1,17},{9,25},{17,1},{25,9},{2,18},{10... | collective-permute-start | bytes 1769480 | tf_op jit(solution)/shard_map/ppermute | solution.py:474
  47.7 10.7 %back.1 = (bf16[8,16,2304]{2,1,0:T(8,128)(2,1)}, bf16[144,2048]{1,0:T(8,128)(2,1)}, bf16[144,768]{1,0:T(8,128)(2,1)}, bf16[144,768]{1,0:T(8,128)(2,1)}, bf16[144,768]{1,0:T(8,128)(2,1)}) custom-call(bf16[8,16,2304]{2,1,0:T(8,128)(2,1)} %all-to-all-done.1.packed_ref, f32[288,768]{1,0:T(8,128)} %get-tuple-element.26.pre_gate_ref.refs_3_, ...), custom_call_target="tpu_custom_call" | custom-call | flops 1358954496 | bytes 9437184 | tf_op jit(solution)/shard_map/back/pallas_call | solution.py:362
  58.4 4.2 %all-to-all-start.2 = ((bf16[8,16,2304]{2,1,0:T(8,128)(2,1)}), bf16[8,16,2304]{2,1,0:T(8,128)(2,1)}, u32[]{:S(2)}, u32[]{:S(2)}) async-start(bf16[8,16,2304]{2,1,0:T(8,128)(2,1)} %get-tuple-element.29), calls=%async_computation.2 | async-start | bytes 1179648 | tf_op jit(solution)/shard_map/all_to_all | solution.py:478
  62.6 0.0 collective-permute-done.3.refs_0_
  62.6 0.1 collective-permute-start.4
  62.7 0.5 collective-permute-start.5
  63.2 0.1 collective-permute-start.2
  63.3 1.8 %collective-permute-done.4.refs_1_ = bf16[8,16,2304]{2,1,0:T(8,128)(2,1)} collective-permute-done((bf16[8,16,2304]{2,1,0:T(8,128)(2,1)}, bf16[8,16,2304]{2,1,0:T(8,128)(2,1)}, u32[]{:S(2)}, u32[]{:S(2)}) %collective-permute-start.4) | collective-permute-done | bytes 589856 | tf_op jit(solution)/shard_map/ppermute | solution.py:474
  65.0 7.8 %forward.3 = (bf16[288,2048]{1,0:T(8,128)(2,1)}, f32[288,768]{1,0:T(8,128)}, f32[288,768]{1,0:T(8,128)}) custom-call(bf16[8,16,2304]{2,1,0:T(8,128)(2,1)} %collective-permute-done.3.refs_0_, bf16[8,16,2304]{2,1,0:T(8,128)(2,1)} %collective-permute-done.4.refs_1_, bf16[2048,768]{1,0:T(8,128)(2,1)} %refs_2_.3, bf16[2048,768]{1,0:T(8,128)(2,1)} %refs_3_.3), custom_call_target="tpu_custom_call" | custom-call | flops 1811939328 | bytes 8650752 | tf_op jit(solution)/shard_map/forward/pallas_call | solution.py:283
  72.9 0.0 collective-permute-done.5.refs_0_
  72.9 8.6 %weight_grads.2 = (f32[512,768]{1,0:T(8,128)}, f32[512,768]{1,0:T(8,128)}, f32[768,512]{1,0:T(8,128)}) custom-call(s32[1]{0:T(128)} %bitcast.2.part_ref, bf16[8,16,2304]{2,1,0:T(8,128)(2,1)} %collective-permute-done.5.refs_0_, bf16[288,2048]{1,0:T(8,128)(2,1)} %get-tuple-element.35.refs_1_, bf16[144,2048]{1,0:T(8,128)(2,1)} %get-tuple-element.36.refs_2_, ...), custom_call_target="tpu_custom_call" | custom-call | flops 1132462080 | bytes 4325376 | tf_op jit(solution)/shard_map/weight_grads/pallas_call | solution.py:441
  81.5 2.5 %merge.1 = bf16[128,2048]{1,0:T(8,128)(2,1)} custom-call(s32[1,128]{1,0:T(1,128)} %bitcast.5, bf16[8,16,2304]{2,1,0:T(8,128)(2,1)} %all-to-all-done.2.back_ref), custom_call_target="tpu_custom_call" | custom-call | flops 134217728 | bytes 1048576 | tf_op jit(solution)/shard_map/merge/pallas_call | solution.py:213
  84.0 0.0 collective-permute-done.2.refs_1_
  84.0 10.0 %weight_grads.3 = (f32[512,768]{1,0:T(8,128)}, f32[512,768]{1,0:T(8,128)}, f32[768,512]{1,0:T(8,128)}) custom-call(s32[1]{0:T(128)} %bitcast.2.part_ref, bf16[8,16,2304]{2,1,0:T(8,128)(2,1)} %collective-permute-done.1.refs_0_, bf16[8,16,2304]{2,1,0:T(8,128)(2,1)} %collective-permute-done.2.refs_1_, bf16[288,2048]{1,0:T(8,128)(2,1)} %get-tuple-element.32.refs_2_, ...), custom_call_target="tpu_custom_call" | custom-call | flops 1585446912 | bytes 5505024 | tf_op jit(solution)/shard_map/weight_grads/pallas_call | solution.py:441
  (2 shorter events, 0.0 us)
Async XLA Ops:
  3.1 23.3 %all-to-all-start = ((bf16[8,16,2304]{2,1,0:T(8,128)(2,1)}), bf16[8,16,2304]{2,1,0:T(8,128)(2,1)}, u32[]{:S(2)}, u32[]{:S(2)}) async-start(bf16[8,16,2304]{2,1,0:T(8,128)(2,1)} %pack.3), calls=%async_computation | async-start | bytes 1179648 | tf_op jit(solution)/shard_map/all_to_all | solution.py:478
  26.4 19.8 %all-to-all-start.1 = ((bf16[8,16,2304]{2,1,0:T(8,128)(2,1)}), bf16[8,16,2304]{2,1,0:T(8,128)(2,1)}, u32[]{:S(2)}, u32[]{:S(2)}) async-start(bf16[8,16,2304]{2,1,0:T(8,128)(2,1)} %pack.2), calls=%async_computation.1 | async-start | bytes 1179648 | tf_op jit(solution)/shard_map/all_to_all | solution.py:478
  30.6 2.4 %collective-permute-start = (bf16[8,16,2304]{2,1,0:T(8,128)(2,1)}, bf16[8,16,2304]{2,1,0:T(8,128)(2,1)}, u32[]{:S(2)}, u32[]{:S(2)}) collective-permute-start(bf16[8,16,2304]{2,1,0:T(8,128)(2,1)} %all-to-all-done.refs_0_), channel_id=1, source_target_pairs={{0,8},{8,0},{16,24},{24,16},{1,9},{9,1},{17,25},{25,17},{2,10},{10... | collective-permute-start | bytes 1769480 | tf_op jit(solution)/shard_map/ppermute | solution.py:474
  30.6 32.0 %collective-permute-start.3 = (bf16[8,16,2304]{2,1,0:T(8,128)(2,1)}, bf16[8,16,2304]{2,1,0:T(8,128)(2,1)}, u32[]{:S(2)}, u32[]{:S(2)}) collective-permute-start(bf16[8,16,2304]{2,1,0:T(8,128)(2,1)} %all-to-all-done.refs_0_), channel_id=1, source_target_pairs={{0,16},{8,24},{16,0},{24,8},{1,17},{9,25},{17,1},{25,9},{2,18},{10... | collective-permute-start | bytes 1769480 | tf_op jit(solution)/shard_map/ppermute | solution.py:474
  46.2 17.0 %collective-permute-start.1 = (bf16[8,16,2304]{2,1,0:T(8,128)(2,1)}, bf16[8,16,2304]{2,1,0:T(8,128)(2,1)}, u32[]{:S(2)}, u32[]{:S(2)}) collective-permute-start(bf16[8,16,2304]{2,1,0:T(8,128)(2,1)} %all-to-all-done.1.packed_ref), channel_id=1, source_target_pairs={{0,16},{8,24},{16,0},{24,8},{1,17},{9,25},{17,1},{25,9},{2,18},{10... | collective-permute-start | bytes 1769480 | tf_op jit(solution)/shard_map/ppermute | solution.py:474
  58.4 23.1 %all-to-all-start.2 = ((bf16[8,16,2304]{2,1,0:T(8,128)(2,1)}), bf16[8,16,2304]{2,1,0:T(8,128)(2,1)}, u32[]{:S(2)}, u32[]{:S(2)}) async-start(bf16[8,16,2304]{2,1,0:T(8,128)(2,1)} %get-tuple-element.29), calls=%async_computation.2 | async-start | bytes 1179648 | tf_op jit(solution)/shard_map/all_to_all | solution.py:478
  62.6 2.4 %collective-permute-start.4 = (bf16[8,16,2304]{2,1,0:T(8,128)(2,1)}, bf16[8,16,2304]{2,1,0:T(8,128)(2,1)}, u32[]{:S(2)}, u32[]{:S(2)}) collective-permute-start(bf16[8,16,2304]{2,1,0:T(8,128)(2,1)} %collective-permute-done.3.refs_0_), channel_id=1, source_target_pairs={{0,8},{8,0},{16,24},{24,16},{1,9},{9,1},{17,25},{25,17},{2,10},{10... | collective-permute-start | bytes 1769480 | tf_op jit(solution)/shard_map/ppermute | solution.py:474
  62.7 10.2 %collective-permute-start.5 = (bf16[8,16,2304]{2,1,0:T(8,128)(2,1)}, bf16[8,16,2304]{2,1,0:T(8,128)(2,1)}, u32[]{:S(2)}, u32[]{:S(2)}) collective-permute-start(bf16[8,16,2304]{2,1,0:T(8,128)(2,1)} %all-to-all-done.1.packed_ref), channel_id=1, source_target_pairs={{0,8},{8,0},{16,24},{24,16},{1,9},{9,1},{17,25},{25,17},{2,10},{10... | collective-permute-start | bytes 1769480 | tf_op jit(solution)/shard_map/ppermute | solution.py:474
  63.2 20.8 %collective-permute-start.2 = (bf16[8,16,2304]{2,1,0:T(8,128)(2,1)}, bf16[8,16,2304]{2,1,0:T(8,128)(2,1)}, u32[]{:S(2)}, u32[]{:S(2)}) collective-permute-start(bf16[8,16,2304]{2,1,0:T(8,128)(2,1)} %collective-permute-done.1.refs_0_), channel_id=1, source_target_pairs={{0,8},{8,0},{16,24},{24,16},{1,9},{9,1},{17,25},{25,17},{2,10},{10... | collective-permute-start | bytes 1769480 | tf_op jit(solution)/shard_map/ppermute | solution.py:474

commit v4 on v0

--- a/solution.py
+++ b/solution.py
@@ -1,10 +1,13 @@
 import jax
 import jax.numpy as jnp
 from jax import lax
+from jax.experimental import pallas as pl
+from jax.experimental.pallas import tpu as pltpu
 from jax.sharding import PartitionSpec as P
 
 EXPERTS = 8
 MOST = 18
+ROWS = 16
 
 
 def build_slots(routes, capacity):
@@ -17,7 +20,7 @@
     return flat_routes * capacity + position
 
 
-def body(tokens, cotangent, routes, expert_gates, gate_proj, up_proj, down_proj):
+def scatter_body(tokens, cotangent, routes, expert_gates, gate_proj, up_proj, down_proj):
     tok_dev, model_dim = tokens.shape
     top_k = routes.shape[1]
     expert_devs = lax.axis_size("expert")
@@ -91,6 +94,391 @@
     return (grad_input.astype(jnp.bfloat16), grad_gate, grad_up, grad_down)
 
 
+BY_WIDTH = (((1,), (1,)), ((), ()))
+BY_ROWS = (((0,), (0,)), ((), ()))
+
+
+def cut(width):
+    pieces = ROWS // (MOST - ROWS)
+    return pieces, width // pieces
+
+
+def width_of(block):
+    pieces = ROWS // (MOST - ROWS)
+    return block.shape[1] * pieces // (pieces + 1)
+
+
+def cost(flops, moved):
+    return pl.CostEstimate(flops=flops, bytes_accessed=moved, transcendentals=0)
+
+
+def params(mib):
+    return pltpu.CompilerParams(vmem_limit_bytes=mib * 1024 * 1024)
+
+
+def inside(count):
+    return [pl.BlockSpec(memory_space=pltpu.VMEM)] * count
+
+
+def dot(left, right, dims=(((1,), (0,)), ((), ()))):
+    return lax.dot_general(left, right, dims, preferred_element_type=jnp.float32)
+
+
+def ones(mask):
+    return jnp.where(mask, 1.0, 0.0).astype(jnp.bfloat16)
+
+
+def slot_masks(me, routes, blocks, width):
+    tokens = routes.shape[1]
+    pieces, _ = cut(width)
+    experts = lax.broadcasted_iota(jnp.int32, (EXPERTS, tokens), 0)
+    named = jnp.where(experts == routes, 1.0, 0.0)
+    earlier = lax.broadcasted_iota(jnp.int32, (tokens, tokens), 0) < lax.broadcasted_iota(
+        jnp.int32, (tokens, tokens), 1
+    )
+    before = dot(named.astype(jnp.bfloat16), ones(earlier))
+    position = jnp.sum(before * named, axis=0, keepdims=True).astype(jnp.int32)
+    slot = lax.broadcasted_iota(jnp.int32, (blocks * ROWS, tokens), 0)
+    row = slot % ROWS
+    mine = (slot // ROWS) ^ me == routes
+    main = mine & (position == row)
+    spill = mine & (position == ROWS + row // pieces)
+    return main, spill, row % pieces
+
+
+def pack(blocks, me, routes, values, gates=None):
+    tokens, width = values.shape
+    pieces, step = cut(width)
+    sources = (routes, values) + (() if gates is None else (gates,))
+
+    def kernel(me_ref, routes_ref, values_ref, *rest):
+        outs = rest[-blocks:]
+        main, spill, piece = slot_masks(me_ref[0], routes_ref[...], blocks, width)
+        rows = dot(ones(main), values_ref[...])
+        extra = jnp.zeros((blocks * ROWS, step), jnp.float32)
+        for at in range(pieces):
+            extra += dot(ones(spill & (piece == at)), values_ref[:, at * step : (at + 1) * step])
+        if gates is not None:
+            weights = rest[0][...]
+            rows = rows * jnp.sum(jnp.where(main, weights, 0.0), axis=1, keepdims=True)
+            extra = extra * jnp.sum(jnp.where(spill, weights, 0.0), axis=1, keepdims=True)
+        rows = rows.astype(jnp.bfloat16)
+        extra = extra.astype(jnp.bfloat16)
+        for block in range(blocks):
+            part = slice(block * ROWS, (block + 1) * ROWS)
+            outs[block][:, :width] = rows[part]
+            outs[block][:, width:] = extra[part]
+
+    return pl.pallas_call(
+        kernel,
+        out_shape=[jax.ShapeDtypeStruct((ROWS, width + step), jnp.bfloat16)] * blocks,
+        in_specs=[pl.BlockSpec(memory_space=pltpu.SMEM)] + inside(len(sources)),
+        out_specs=inside(blocks),
+        compiler_params=params(16),
+        cost_estimate=cost(4 * blocks * ROWS * tokens * width, 4 * tokens * width),
+        name="pack",
+    )(me, *sources)
+
+
+def merge(me, routes, returned):
+    blocks = len(returned)
+    tokens = routes.shape[1]
+    width = width_of(returned[0])
+    pieces, step = cut(width)
+
+    def kernel(me_ref, routes_ref, *refs):
+        out = refs[blocks]
+        main, spill, piece = slot_masks(me_ref[0], routes_ref[...], blocks, width)
+        rows = jnp.concatenate([ref[:, :width] for ref in refs[:blocks]], 0)
+        extra = jnp.concatenate([ref[:, width:] for ref in refs[:blocks]], 0)
+        picked = dot(ones(main), rows, BY_ROWS)
+        for at in range(pieces):
+            columns = slice(at * step, (at + 1) * step)
+            out[:, columns] = (
+                picked[:, columns] + dot(ones(spill & (piece == at)), extra, BY_ROWS)
+            ).astype(jnp.bfloat16)
+
+    return pl.pallas_call(
+        kernel,
+        out_shape=jax.ShapeDtypeStruct((tokens, width), jnp.bfloat16),
+        in_specs=[pl.BlockSpec(memory_space=pltpu.SMEM)] + inside(1 + blocks),
+        out_specs=pl.BlockSpec(memory_space=pltpu.VMEM),
+        compiler_params=params(16),
+        cost_estimate=cost(4 * blocks * ROWS * tokens * width, 4 * tokens * width),
+        name="merge",
+    )(me, routes, *returned)
+
+
+def spill_picks(blocks, pieces, at):
+    shape = (blocks * (MOST - ROWS), blocks * ROWS)
+    slot = lax.broadcasted_iota(jnp.int32, shape, 0)
+    row = lax.broadcasted_iota(jnp.int32, shape, 1)
+    return ones(row == slot * pieces + at)
+
+
+def join(blocks):
+    count = len(blocks)
+    width = width_of(blocks[0])
+    pieces, step = cut(width)
+    first, last = count * ROWS, count * MOST
+
+    def kernel(*refs):
+        out = refs[count]
+        for at in range(count):
+            out[at * ROWS : (at + 1) * ROWS, :] = refs[at][:, :width]
+        extra = jnp.concatenate([ref[:, width:] for ref in refs[:count]], 0)
+        for at in range(pieces):
+            out[first:last, at * step : (at + 1) * step] = dot(
+                spill_picks(count, pieces, at), extra
+            ).astype(jnp.bfloat16)
+
+    return pl.pallas_call(
+        kernel,
+        out_shape=jax.ShapeDtypeStruct((last, width), jnp.bfloat16),
+        in_specs=inside(count),
+        out_specs=pl.BlockSpec(memory_space=pltpu.VMEM),
+        compiler_params=params(16),
+        cost_estimate=cost(0, 4 * last * width),
+        name="join",
+    )(*blocks)
+
+
+def column_tile(width, tile):
+    return pl.BlockSpec((width, tile), lambda i: (0, i))
+
+
+def row_tile(tile, width):
+    return pl.BlockSpec((tile, width), lambda i: (i, 0))
+
+
+def tile_of(tile):
+    return pl.ds(pl.multiple_of(pl.program_id(0) * tile, tile), tile)
+
+
+def forward(tile, rows, gate_proj, up_proj):
+    groups = len(rows)
+    slots = rows[0].shape[0]
+    width, hid = gate_proj.shape
+    total = groups * slots
+
+    def kernel(*refs):
+        gate_ref, up_ref, pre_gate_ref, pre_up_ref, held = refs[groups:]
+
+        @pl.when(pl.program_id(0) == 0)
+        def _():
+            for at in range(groups):
+                held[at * slots : (at + 1) * slots, :] = refs[at][...]
+
+        columns = tile_of(tile)
+        pre_gate_ref[...] = dot(held[...], gate_ref[:, columns])
+        pre_up_ref[...] = dot(held[...], up_ref[:, columns])
+
+    return pl.pallas_call(
+        kernel,
+        grid=(hid // tile,),
+        out_shape=[jax.ShapeDtypeStruct((total, hid), jnp.float32)] * 2,
+        in_specs=inside(groups + 2),
+        out_specs=[column_tile(total, tile)] * 2,
+        scratch_shapes=[pltpu.VMEM((total, width), jnp.bfloat16)],
+        compiler_params=params(20),
+        cost_estimate=cost(4 * total * width * hid, 4 * width * hid + 4 * total * width),
+        name="forward",
+    )(*rows, gate_proj, up_proj)
+
+
+def hidden_grads(pre_gate, pre_up, d_hidden):
+    sig = jax.nn.sigmoid(pre_gate)
+    silu = pre_gate * sig
+    hidden = (silu * pre_up).astype(jnp.bfloat16)
+    d_gate = (d_hidden * pre_up * sig * (1.0 + pre_gate * (1.0 - sig))).astype(jnp.bfloat16)
+    d_up = (d_hidden * silu).astype(jnp.bfloat16)
+    return hidden, d_gate, d_up
+
+
+def back(blocks, tile, scaled, pre_gate, pre_up, gate_proj, up_proj, down_proj):
+    slots, width = scaled.shape
+    hid = gate_proj.shape[1]
+    pieces, step = cut(width)
+
+    def kernel(scaled_ref, gate_ref, up_ref, down_ref, pre_gate_ref, pre_up_ref, *rest):
+        outs = rest[:blocks]
+        hidden_ref, d_gate_ref, d_up_ref, total = rest[blocks:]
+        columns = tile_of(tile)
+        d_hidden = dot(scaled_ref[...], down_ref[columns, :], BY_WIDTH)
+        hidden, d_gate, d_up = hidden_grads(pre_gate_ref[...], pre_up_ref[...], d_hidden)
+        hidden_ref[...] = hidden
+        d_gate_ref[...] = d_gate
+        d_up_ref[...] = d_up
+        part = dot(d_gate, gate_ref[:, columns], BY_WIDTH)
+        part += dot(d_up, up_ref[:, columns], BY_WIDTH)
+
+        @pl.when(pl.program_id(0) == 0)
+        def _():
+            total[...] = part
+
+        @pl.when(pl.program_id(0) > 0)
+        def _():
+            total[...] += part
+
+        @pl.when(pl.program_id(0) == hid // tile - 1)
+        def _():
+            done = total[...].astype(jnp.bfloat16)
+            extra = jnp.zeros((blocks * ROWS, step), jnp.float32)
+            for at in range(pieces):
+                extra += dot(
+                    spill_picks(blocks, pieces, at),
+                    done[blocks * ROWS :, at * step : (at + 1) * step],
+                    BY_ROWS,
+                )
+            extra = extra.astype(jnp.bfloat16)
+            for block in range(blocks):
+                part_of = slice(block * ROWS, (block + 1) * ROWS)
+                outs[block][:, :width] = done[part_of]
+                outs[block][:, width:] = extra[part_of]
+
+    factor = jax.ShapeDtypeStruct((slots, hid), jnp.bfloat16)
+    result = pl.pallas_call(
+        kernel,
+        grid=(hid // tile,),
+        out_shape=[jax.ShapeDtypeStruct((ROWS, width + step), jnp.bfloat16)] * blocks
+        + [factor] * 3,
+        in_specs=inside(4) + [column_tile(slots, tile)] * 2,
+        out_specs=inside(blocks) + [column_tile(slots, tile)] * 3,
+        scratch_shapes=[pltpu.VMEM((slots, width), jnp.float32)],
+        compiler_params=params(20),
+        cost_estimate=cost(6 * slots * width * hid, 6 * width * hid),
+        name="back",
+    )(scaled, gate_proj, up_proj, down_proj, pre_gate, pre_up)
+    return result[:blocks], result[blocks:]
+
+
+def weight_grads(tile, part, rows, scaled, pre_gate, pre_up, down_proj, own):
+    groups = len(rows)
+    slots, width = rows[0].shape
+    hid = down_proj.shape[0]
+    some = (groups - 1) * slots
+    share = width // groups
+
+    def kernel(part_ref, *refs):
+        x_refs, dy_refs = refs[:groups], refs[groups : 2 * groups]
+        down_ref, pre_gate_ref, pre_up_ref, own_hidden, own_gate, own_up = refs[
+            2 * groups : 2 * groups + 6
+        ]
+        d_gate_ref, d_up_ref, d_down_ref, others, x_mine, dy_mine = refs[2 * groups + 6 :]
+
+        @pl.when(pl.program_id(0) == 0)
+        def _():
+            columns = pl.ds(pl.multiple_of(part_ref[0] * share, share), share)
+            for at in range(groups):
+                here = slice(at * slots, (at + 1) * slots)
+                x_mine[here, :] = x_refs[at][:, columns]
+                dy_mine[here, :] = dy_refs[at][:, columns]
+                if at > 0:
+                    others[(at - 1) * slots : at * slots, :] = dy_refs[at][...]
+
+        d_hidden = dot(others[...], down_ref[tile_of(tile), :], BY_WIDTH)
+        hidden, d_gate, d_up = hidden_grads(pre_gate_ref[...], pre_up_ref[...], d_hidden)
+        hidden = jnp.concatenate([own_hidden[...], hidden], 0)
+        d_gate = jnp.concatenate([own_gate[...], d_gate], 0)
+        d_up = jnp.concatenate([own_up[...], d_up], 0)
+        both = dot(x_mine[...], jnp.concatenate([d_gate, d_up], 1), BY_ROWS)
+        d_gate_ref[...] = both[:, :tile]
+        d_up_ref[...] = both[:, tile:]
+        d_down_ref[...] = dot(hidden, dy_mine[...], BY_ROWS)
+
+    return pl.pallas_call(
+        kernel,
+        grid=(hid // tile,),
+        out_shape=[
+            jax.ShapeDtypeStruct((share, hid), jnp.float32),
+            jax.ShapeDtypeStruct((share, hid), jnp.float32),
+            jax.ShapeDtypeStruct((hid, share), jnp.float32),
+        ],
+        in_specs=[pl.BlockSpec(memory_space=pltpu.SMEM)]
+        + inside(2 * groups + 1)
+        + [column_tile(some, tile)] * 2
+        + [column_tile(slots, tile)] * 3,
+        out_specs=[column_tile(share, tile), column_tile(share, tile), row_tile(tile, share)],
+        scratch_shapes=[
+            pltpu.VMEM((some, width), jnp.bfloat16),
+            pltpu.VMEM((groups * slots, share), jnp.bfloat16),
+            pltpu.VMEM((groups * slots, share), jnp.bfloat16),
+        ],
+        compiler_params=params(20),
+        cost_estimate=cost(
+            2 * some * width * hid + 6 * groups * slots * share * hid,
+            2 * width * hid + 4 * groups * slots * width,
+        ),
+        name="weight_grads",
+    )(part, *rows, *scaled, down_proj, pre_gate, pre_up, *own)
+
+
+def swap(value, axis, distance):
+    size = lax.axis_size(axis)
+    return lax.ppermute(value, axis, [(at, at ^ distance) for at in range(size)])
+
+
+def exchange(blocks):
+    out = list(blocks)
+    for distance in reversed(range(1, len(blocks))):
+        out[distance] = swap(blocks[distance], "expert", distance)
+    return out
+
+
+def after(values, *earlier):
+    return lax.optimization_barrier((list(values), *earlier))[0]
+
+
+def gather_body(tokens, cotangent, routes, expert_gates, gate_proj, up_proj, down_proj):
+    blocks = lax.axis_size("expert")
+    tile = 256
+    me = lax.axis_index("expert").astype(jnp.int32).reshape(1)
+    part = lax.axis_index("dp").astype(jnp.int32).reshape(1)
+    routes = routes.reshape(1, -1)
+    gates = expert_gates.reshape(1, -1)
+    weights = (gate_proj, up_proj, down_proj)
+    received = exchange(pack(blocks, me, routes, tokens))
+    packed, *received[-3:] = lax.optimization_barrier(
+        (pack(blocks, me, routes, cotangent, gates), *received[-3:])
+    )
+    rows = join(received)
+    far = swap(rows, "dp", 2)
+    near = swap(rows, "dp", 1)
+    pre = forward(tile, [rows], gate_proj, up_proj)
+    received, far = lax.optimization_barrier((exchange(packed), far, pre))[:2]
+    last = swap(far, "dp", 1)
+    scaled = join(received)
+    dy_far = swap(scaled, "dp", 2)
+    dy_near = swap(scaled, "dp", 1)
+    sent, own = back(blocks, tile, scaled, *pre, *weights)
+    sent, last, dy_near = lax.optimization_barrier((sent, last, dy_near))
+    returned = exchange(sent)
+    others = forward(tile, [near, far, last], gate_proj, up_proj)
+    dy_far = after([dy_far], sent)[0]
+    dy_last = swap(dy_far, "dp", 1)
+    grads = weight_grads(
+        tile,
+        part,
+        [rows, near, far, last],
+        [scaled, dy_near, dy_far, dy_last],
+        *others,
+        down_proj,
+        own,
+    )
+    return (merge(me, routes, returned), *grads)
+
+
+def body(tokens, cotangent, routes, expert_gates, gate_proj, up_proj, down_proj):
+    groups, blocks = lax.axis_size("dp"), lax.axis_size("expert")
+    width, hid = gate_proj.shape
+    rows_sent = (groups - 1) * 2 * blocks * MOST * width
+    grads_sent = 3 * width * hid * (groups - 1) // groups
+    fits = blocks == EXPERTS and groups == 4 and hid % 256 == 0
+    fits = fits and tokens.shape[0] == 128 and routes.shape[1] == 1 and width // groups % 128 == 0
+    chosen = gather_body if fits and rows_sent < grads_sent else scatter_body
+    return chosen(tokens, cotangent, routes, expert_gates, gate_proj, up_proj, down_proj)
+
+
 def solution(mesh):
     in_specs = (
         P(("dp", "expert"), None),

time: 209 us -> 94.2 us (0.45)
  waiting for transfers between devices: 113 us -> 5.65 us
  Pallas kernels: 0 us -> 28.6 us
  starting transfers between devices: 15.8 us -> 41.8 us
  matrix products: 24 us -> 0 us
  other arithmetic: 16.2 us -> 0 us
  between operations: 13.9 us -> 0.88 us
  local copies, waits for them, and re-layouts: 25.6 us -> 16.7 us
    reduce_scatter x3 -> x0, waiting for transfers between devices: 65.2 us -> none  [the longest x1 38.1 us: body(): lax.psum_scatter(grad_up.astype(jnp.bfloat16), 'dp', scatter_dimension=0,...]
    all_to_all x3 -> x0, waiting for transfers between devices: 47.6 us -> none  [the longest x1 20.2 us: body(): lax.all_to_all(partial_value.reshape(expert_devs, capacity, model_dim), '...]
    ppermute x0 -> x27, starting transfers between devices: none -> 41.8 us  [swap(): lax.ppermute(value, axis, [(at, at ^ distance) for at in range(size)])]
    pallas_call x0 -> x9, Pallas kernels: none -> 28.6 us  [the longest x1 9.71 us: weight_grads(): pl.pallas_call(kernel, grid=(hid // tile,), out_shape=[jax.ShapeDtypeStru...]
    dot_general x7 -> x0, matrix products: 24 us -> none  [the longest x1 6.2 us: body(): lax.dot_general(joined_grads, joined_proj, by_width, preferred_element_ty...]
    unnamed x10 -> x54, local copies, waits for them, and re-layouts: 0.48 us -> 16.7 us
    all_to_all x3 -> x0, starting transfers between devices: 15.7 us -> none  [the longest x1 7.25 us: body(): lax.all_to_all(copies(dy_slots), 'expert', split_axis=0, concat_axis=0, t...]
    convert_element_type x6 -> x0, other arithmetic: 12.5 us -> none  [the longest x3 7.34 us: body(): grad_gate, grad_up, grad_down = (lax.psum_scatter(grad_gate.astype(jnp.bf...]
  transfers between devices with their start and end apart: 6 -> 27, of which waited for: 5 -> 4; matrix products, arithmetic and copies ran while one was open for 20% -> 0% of each run, Pallas kernels for 0% -> 18%
where the time goes in v4:
time: 94.2 us; the launch traced here: 93.6 us
  starting transfers between devices  41.8 us (44%)
  Pallas kernels  28.6 us (30%)
  local copies, waits for them, and re-layouts  16.7 us (18%)
  waiting for transfers between devices  5.65 us (6%)
    ppermute x27, starting transfers between devices, swap(): lax.ppermute(value, axis, [(at, at ^ distance) for at in range(size)])  41.8 us
    unnamed x54, local copies, waits for them, and re-layouts  16.7 us
    pallas_call x1, Pallas kernels, weight_grads(): pl.pallas_call(kernel, grid=(hid // tile,), out_shape=[jax.ShapeDtypeStru...  9.71 us
    pallas_call x2, Pallas kernels, forward(): pl.pallas_call(kernel, grid=(hid // tile,), out_shape=[jax.ShapeDtypeStru...  7.68 us
    pallas_call x1, Pallas kernels, back(): pl.pallas_call(kernel, grid=(hid // tile,), out_shape=[jax.ShapeDtypeStru...  6.49 us
    ppermute x27, waiting for transfers between devices, swap(): lax.ppermute(value, axis, [(at, at ^ distance) for at in range(size)])  5.65 us
    pallas_call x1, Pallas kernels, merge(): pl.pallas_call(kernel, out_shape=jax.ShapeDtypeStruct((tokens, width), jn...  2.35 us
  transfers between devices with their start and end apart: 27, of which 4 were waited for; matrix products, arithmetic and copies ran while one was open for 0% of the time, Pallas kernels for 18%

profile of v4, /device:TPU:0, one launch (start us, length us, event | category | flops | bytes accessed | tf_op | source)
XLA Modules:
  0.0 93.6 jit_solution(14180412792927963473)
XLA Ops:
  2.9 5.0 %collective-permute-start = (bf16[16,2304]{1,0:T(8,128)(2,1)S(1)}, bf16[16,2304]{1,0:T(8,128)(2,1)S(1)}, u32[]{:S(2)}, u32[]{:S(2)}) collective-permute-start(bf16[16,2304]{1,0:T(8,128)(2,1)S(1)} %get-tuple-element.77), channel_id=1, source_target_pairs={{0,5},{1,4},{2,7},{3,6},{4,1},{5,0},{6,3},{7,2},{8,13},{9,12},{10,... | collective-permute-start | bytes 221192 | tf_op jit(solution)/shard_map/ppermute | solution.py:418
  7.9 1.3 %collective-permute-start.1 = (bf16[16,2304]{1,0:T(8,128)(2,1)S(1)}, bf16[16,2304]{1,0:T(8,128)(2,1)S(1)}, u32[]{:S(2)}, u32[]{:S(2)}) collective-permute-start(bf16[16,2304]{1,0:T(8,128)(2,1)S(1)} %get-tuple-element.78), channel_id=1, source_target_pairs={{0,6},{1,7},{2,4},{3,5},{4,2},{5,3},{6,0},{7,1},{8,14},{9,15},{10,... | collective-permute-start | bytes 221192 | tf_op jit(solution)/shard_map/ppermute | solution.py:418
  9.3 2.4 %collective-permute-start.2 = (bf16[16,2304]{1,0:T(8,128)(2,1)S(1)}, bf16[16,2304]{1,0:T(8,128)(2,1)S(1)}, u32[]{:S(2)}, u32[]{:S(2)}) collective-permute-start(bf16[16,2304]{1,0:T(8,128)(2,1)S(1)} %get-tuple-element.79), channel_id=1, source_target_pairs={{0,7},{1,6},{2,5},{3,4},{4,3},{5,2},{6,1},{7,0},{8,15},{9,14},{10,... | collective-permute-start | bytes 221192 | tf_op jit(solution)/shard_map/ppermute | solution.py:418
  11.7 1.5 %collective-permute-start.10 = (bf16[16,2304]{1,0:T(8,128)(2,1)S(1)}, bf16[16,2304]{1,0:T(8,128)(2,1)S(1)}, u32[]{:S(2)}, u32[]{:S(2)}) collective-permute-start(bf16[16,2304]{1,0:T(8,128)(2,1)S(1)} %get-tuple-element.89), channel_id=1, source_target_pairs={{0,1},{1,0},{2,3},{3,2},{4,5},{5,4},{6,7},{7,6},{8,9},{9,8},{10,11... | collective-permute-start | bytes 221192 | tf_op jit(solution)/shard_map/ppermute | solution.py:418
  13.2 2.0 %collective-permute-start.12 = (bf16[16,2304]{1,0:T(8,128)(2,1)S(1)}, bf16[16,2304]{1,0:T(8,128)(2,1)S(1)}, u32[]{:S(2)}, u32[]{:S(2)}) collective-permute-start(bf16[16,2304]{1,0:T(8,128)(2,1)S(1)} %get-tuple-element.91), channel_id=1, source_target_pairs={{0,3},{1,2},{2,1},{3,0},{4,7},{5,6},{6,5},{7,4},{8,11},{9,10},{10,... | collective-permute-start | bytes 221192 | tf_op jit(solution)/shard_map/ppermute | solution.py:418
  15.2 5.0 %collective-permute-start.13 = (bf16[16,2304]{1,0:T(8,128)(2,1)S(1)}, bf16[16,2304]{1,0:T(8,128)(2,1)S(1)}, u32[]{:S(2)}, u32[]{:S(2)}) collective-permute-start(bf16[16,2304]{1,0:T(8,128)(2,1)S(1)} %get-tuple-element.92), channel_id=1, source_target_pairs={{0,4},{1,5},{2,6},{3,7},{4,0},{5,1},{6,2},{7,3},{8,12},{9,13},{10,... | collective-permute-start | bytes 221192 | tf_op jit(solution)/shard_map/ppermute | solution.py:418
  24.4 1.5 %collective-permute-start.14 = (bf16[144,2048]{1,0:T(8,128)(2,1)}, bf16[144,2048]{1,0:T(8,128)(2,1)S(1)}, u32[]{:S(2)}, u32[]{:S(2)}) collective-permute-start(bf16[144,2048]{1,0:T(8,128)(2,1)} %join.2.refs_0_), channel_id=1, source_target_pairs={{0,16},{8,24},{16,0},{24,8},{1,17},{9,25},{17,1},{25,9},{2,18},{10... | collective-permute-start | bytes 1769480 | tf_op jit(solution)/shard_map/ppermute | solution.py:418
  26.9 2.4 %collective-permute-start.5 = (bf16[16,2304]{1,0:T(8,128)(2,1)S(1)}, bf16[16,2304]{1,0:T(8,128)(2,1)S(1)}, u32[]{:S(2)}, u32[]{:S(2)}) collective-permute-start(bf16[16,2304]{1,0:T(8,128)(2,1)S(1)} %get-tuple-element.83), channel_id=1, source_target_pairs={{0,3},{1,2},{2,1},{3,0},{4,7},{5,6},{6,5},{7,4},{8,11},{9,10},{10,... | collective-permute-start | bytes 221192 | tf_op jit(solution)/shard_map/ppermute | solution.py:418
  29.4 2.2 %collective-permute-start.6 = (bf16[16,2304]{1,0:T(8,128)(2,1)S(1)}, bf16[16,2304]{1,0:T(8,128)(2,1)S(1)}, u32[]{:S(2)}, u32[]{:S(2)}) collective-permute-start(bf16[16,2304]{1,0:T(8,128)(2,1)S(1)} %get-tuple-element.84), channel_id=1, source_target_pairs={{0,4},{1,5},{2,6},{3,7},{4,0},{5,1},{6,2},{7,3},{8,12},{9,13},{10,... | collective-permute-start | bytes 221192 | tf_op jit(solution)/shard_map/ppermute | solution.py:418
  32.7 2.2 %collective-permute-start.8 = (bf16[16,2304]{1,0:T(8,128)(2,1)S(1)}, bf16[16,2304]{1,0:T(8,128)(2,1)S(1)}, u32[]{:S(2)}, u32[]{:S(2)}) collective-permute-start(bf16[16,2304]{1,0:T(8,128)(2,1)S(1)} %get-tuple-element.86), channel_id=1, source_target_pairs={{0,6},{1,7},{2,4},{3,5},{4,2},{5,3},{6,0},{7,1},{8,14},{9,15},{10,... | collective-permute-start | bytes 221192 | tf_op jit(solution)/shard_map/ppermute | solution.py:418
  34.9 3.4 %collective-permute-start.9 = (bf16[16,2304]{1,0:T(8,128)(2,1)S(1)}, bf16[16,2304]{1,0:T(8,128)(2,1)S(1)}, u32[]{:S(2)}, u32[]{:S(2)}) collective-permute-start(bf16[16,2304]{1,0:T(8,128)(2,1)S(1)} %get-tuple-element.87), channel_id=1, source_target_pairs={{0,7},{1,6},{2,5},{3,4},{4,3},{5,2},{6,1},{7,0},{8,15},{9,14},{10,... | collective-permute-start | bytes 221192 | tf_op jit(solution)/shard_map/ppermute | solution.py:418
  38.3 1.9 %copy-done = bf16[2048,768]{1,0:T(8,128)(2,1)S(1)} copy-done((bf16[2048,768]{1,0:T(8,128)(2,1)S(1)}, bf16[2048,768]{1,0:T(8,128)(2,1)}, u32[]{:S(2)}) %copy-start) | copy-done | bytes 3145752
  40.2 1.9 %copy-done.2 = bf16[2048,768]{1,0:T(8,128)(2,1)S(1)} copy-done((bf16[2048,768]{1,0:T(8,128)(2,1)S(1)}, bf16[2048,768]{1,0:T(8,128)(2,1)}, u32[]{:S(2)}) %copy-start.2) | copy-done | bytes 3145752
  42.1 2.9 %forward.2 = (f32[144,768]{1,0:T(8,128)S(1)}, f32[144,768]{1,0:T(8,128)S(1)}) custom-call(bf16[144,2048]{1,0:T(8,128)(2,1)} %join.2.refs_0_, bf16[2048,768]{1,0:T(8,128)(2,1)S(1)} %copy-done, bf16[2048,768]{1,0:T(8,128)(2,1)S(1)} %copy-done.2), custom_call_target="tpu_custom_call" | custom-call | flops 905969664 | bytes 7471104 | tf_op jit(solution)/shard_map/forward/pallas_call | solution.py:276
  46.4 6.5 %back.1 = (bf16[16,2304]{1,0:T(8,128)(2,1)S(1)}, bf16[16,2304]{1,0:T(8,128)(2,1)}, bf16[16,2304]{1,0:T(8,128)(2,1)}, bf16[16,2304]{1,0:T(8,128)(2,1)}, bf16[16,2...) custom-call(bf16[144,2048]{1,0:T(8,128)(2,1)S(1)} %join.3.scaled_ref, ...), custom_call_target="tpu_custom_call" | custom-call | flops 1358954496 | bytes 9437184 | tf_op jit(solution)/shard_map/back/pallas_call | solution.py:340
  58.4 2.8 %collective-permute-done.25.refs_6_ = bf16[144,2048]{1,0:T(8,128)(2,1)} collective-permute-done((bf16[144,2048]{1,0:T(8,128)(2,1)S(1)}, bf16[144,2048]{1,0:T(8,128)(2,1)}, u32[]{:S(2)}, u32[]{:S(2)}) %collective-permute-start.25) | collective-permute-done | bytes 589856 | tf_op jit(solution)/shard_map/ppermute | solution.py:418
  61.9 2.8 %collective-permute-start.19 = (bf16[16,2304]{1,0:T(8,128)(2,1)}, bf16[16,2304]{1,0:T(8,128)(2,1)}, u32[]{:S(2)}, u32[]{:S(2)}) collective-permute-start(bf16[16,2304]{1,0:T(8,128)(2,1)} %get-tuple-element.118), channel_id=1, source_target_pairs={{0,3},{1,2},{2,1},{3,0},{4,7},{5,6},{6,5},{7,4},{8,11},{9,10},{10,... | collective-permute-start | bytes 221192 | tf_op jit(solution)/shard_map/ppermute | solution.py:418
  67.1 1.8 %collective-permute-start.22 = (bf16[16,2304]{1,0:T(8,128)(2,1)}, bf16[16,2304]{1,0:T(8,128)(2,1)S(1)}, u32[]{:S(2)}, u32[]{:S(2)}) collective-permute-start(bf16[16,2304]{1,0:T(8,128)(2,1)} %copy-done.24), channel_id=1, source_target_pairs={{0,6},{1,7},{2,4},{3,5},{4,2},{5,3},{6,0},{7,1},{8,14},{9,15},{10,... | collective-permute-start | bytes 221192 | tf_op jit(solution)/shard_map/ppermute | solution.py:418
  69.0 1.1 %collective-permute-done.19.refs_3_ = bf16[16,2304]{1,0:T(8,128)(2,1)} collective-permute-done((bf16[16,2304]{1,0:T(8,128)(2,1)}, bf16[16,2304]{1,0:T(8,128)(2,1)}, u32[]{:S(2)}, u32[]{:S(2)}) %collective-permute-start.19) | collective-permute-done | bytes 73760 | tf_op jit(solution)/shard_map/ppermute | solution.py:418
  70.1 2.5 %collective-permute-start.23 = (bf16[16,2304]{1,0:T(8,128)(2,1)}, bf16[16,2304]{1,0:T(8,128)(2,1)S(1)}, u32[]{:S(2)}, u32[]{:S(2)}) collective-permute-start(bf16[16,2304]{1,0:T(8,128)(2,1)} %copy-done.23), channel_id=1, source_target_pairs={{0,7},{1,6},{2,5},{3,4},{4,3},{5,2},{6,1},{7,0},{8,15},{9,14},{10,... | collective-permute-start | bytes 221192 | tf_op jit(solution)/shard_map/ppermute | solution.py:418
  72.6 1.9 %copy-done.3 = bf16[2048,768]{1,0:T(8,128)(2,1)S(1)} copy-done((bf16[2048,768]{1,0:T(8,128)(2,1)S(1)}, bf16[2048,768]{1,0:T(8,128)(2,1)}, u32[]{:S(2)}) %copy-start.3) | copy-done | bytes 3145752
  76.6 4.8 %forward.3 = (f32[432,768]{1,0:T(8,128)S(1)}, f32[432,768]{1,0:T(8,128)S(1)}) custom-call(bf16[144,2048]{1,0:T(8,128)(2,1)} %collective-permute-done.24.refs_0_.refs_1_, bf16[144,2048]{1,0:T(8,128)(2,1)S(1)} %copy-done.9, bf16[144,2048]{1,0:T(8,128)(2,1)S(1)} %copy-done.13, bf16[2048,768]{1,0:T(8,128)(2,1)S(1)} %copy-done.1, bf16[2048,768]{1,0:T(8,128)(2,1)S(1)} %copy-done.3), custom_call_target="tpu_custom_call" | custom-call | flops 2717908992 | bytes 9830400 | tf_op jit(solution)/shard_map/forward/pallas_call | solution.py:276
  81.5 2.3 %merge.1 = bf16[128,2048]{1,0:T(8,128)(2,1)} custom-call(s32[1]{0:T(128)} %bitcast.me_ref, s32[1,128]{1,0:T(1,128)S(1)} %bitcast.6, bf16[16,2304]{1,0:T(8,128)(2,1)S(1)} %get-tuple-element.115.refs_0_, bf16[16,2304]{1,0:T(8,128)(2,1)S(1)} %collective-permute-done.17.refs_1_, bf16[16,2304]{1,0:T(8,128)(2,1)} %collective-permute-done.18.refs_2_, ...), custom_call_target="tpu_custom_call" | custom-call | flops 134217728 | bytes 1048576 | tf_op jit(solution)/shard_map/merge/pallas_call | solution.py:201
  83.9 9.7 %weight_grads.1 = (f32[512,768]{1,0:T(8,128)}, f32[512,768]{1,0:T(8,128)}, f32[768,512]{1,0:T(8,128)}) custom-call(s32[1]{0:T(128)} %bitcast.3.part_ref, bf16[144,2048]{1,0:T(8,128)(2,1)} %join.2.refs_0_, bf16[144,2048]{1,0:T(8,128)(2,1)} %collective-permute-done.24.refs_0_.refs_1_, bf16[144,2048]{1,0:T(8,128)(2,1)S(1)} %copy-done.9, ...), custom_call_target="tpu_custom_call" | custom-call | flops 2717908992 | bytes 7864320 | tf_op jit(solution)/shard_map/weight_grads/pallas_call | solution.py:389
  (93 shorter events, 20.6 us)
Async XLA Ops:
  2.9 10.3 %collective-permute-start = (bf16[16,2304]{1,0:T(8,128)(2,1)S(1)}, bf16[16,2304]{1,0:T(8,128)(2,1)S(1)}, u32[]{:S(2)}, u32[]{:S(2)}) collective-permute-start(bf16[16,2304]{1,0:T(8,128)(2,1)S(1)} %get-tuple-element.77), channel_id=1, source_target_pairs={{0,5},{1,4},{2,7},{3,6},{4,1},{5,0},{6,3},{7,2},{8,13},{9,12},{10,... | collective-permute-start | bytes 221192 | tf_op jit(solution)/shard_map/ppermute | solution.py:418
  7.9 7.3 %collective-permute-start.1 = (bf16[16,2304]{1,0:T(8,128)(2,1)S(1)}, bf16[16,2304]{1,0:T(8,128)(2,1)S(1)}, u32[]{:S(2)}, u32[]{:S(2)}) collective-permute-start(bf16[16,2304]{1,0:T(8,128)(2,1)S(1)} %get-tuple-element.78), channel_id=1, source_target_pairs={{0,6},{1,7},{2,4},{3,5},{4,2},{5,3},{6,0},{7,1},{8,14},{9,15},{10,... | collective-permute-start | bytes 221192 | tf_op jit(solution)/shard_map/ppermute | solution.py:418
  9.3 13.3 %collective-permute-start.2 = (bf16[16,2304]{1,0:T(8,128)(2,1)S(1)}, bf16[16,2304]{1,0:T(8,128)(2,1)S(1)}, u32[]{:S(2)}, u32[]{:S(2)}) collective-permute-start(bf16[16,2304]{1,0:T(8,128)(2,1)S(1)} %get-tuple-element.79), channel_id=1, source_target_pairs={{0,7},{1,6},{2,5},{3,4},{4,3},{5,2},{6,1},{7,0},{8,15},{9,14},{10,... | collective-permute-start | bytes 221192 | tf_op jit(solution)/shard_map/ppermute | solution.py:418
  11.7 10.8 %collective-permute-start.10 = (bf16[16,2304]{1,0:T(8,128)(2,1)S(1)}, bf16[16,2304]{1,0:T(8,128)(2,1)S(1)}, u32[]{:S(2)}, u32[]{:S(2)}) collective-permute-start(bf16[16,2304]{1,0:T(8,128)(2,1)S(1)} %get-tuple-element.89), channel_id=1, source_target_pairs={{0,1},{1,0},{2,3},{3,2},{4,5},{5,4},{6,7},{7,6},{8,9},{9,8},{10,11... | collective-permute-start | bytes 221192 | tf_op jit(solution)/shard_map/ppermute | solution.py:418
  13.2 9.3 %collective-permute-start.11 = (bf16[16,2304]{1,0:T(8,128)(2,1)S(1)}, bf16[16,2304]{1,0:T(8,128)(2,1)S(1)}, u32[]{:S(2)}, u32[]{:S(2)}) collective-permute-start(bf16[16,2304]{1,0:T(8,128)(2,1)S(1)} %get-tuple-element.90), channel_id=1, source_target_pairs={{0,2},{1,3},{2,0},{3,1},{4,6},{5,7},{6,4},{7,5},{8,10},{9,11},{10,... | collective-permute-start | bytes 221192 | tf_op jit(solution)/shard_map/ppermute | solution.py:418
  13.2 9.4 %collective-permute-start.12 = (bf16[16,2304]{1,0:T(8,128)(2,1)S(1)}, bf16[16,2304]{1,0:T(8,128)(2,1)S(1)}, u32[]{:S(2)}, u32[]{:S(2)}) collective-permute-start(bf16[16,2304]{1,0:T(8,128)(2,1)S(1)} %get-tuple-element.91), channel_id=1, source_target_pairs={{0,3},{1,2},{2,1},{3,0},{4,7},{5,6},{6,5},{7,4},{8,11},{9,10},{10,... | collective-permute-start | bytes 221192 | tf_op jit(solution)/shard_map/ppermute | solution.py:418
  15.2 8.1 %collective-permute-start.13 = (bf16[16,2304]{1,0:T(8,128)(2,1)S(1)}, bf16[16,2304]{1,0:T(8,128)(2,1)S(1)}, u32[]{:S(2)}, u32[]{:S(2)}) collective-permute-start(bf16[16,2304]{1,0:T(8,128)(2,1)S(1)} %get-tuple-element.92), channel_id=1, source_target_pairs={{0,4},{1,5},{2,6},{3,7},{4,0},{5,1},{6,2},{7,3},{8,12},{9,13},{10,... | collective-permute-start | bytes 221192 | tf_op jit(solution)/shard_map/ppermute | solution.py:418
  24.4 20.6 %collective-permute-start.14 = (bf16[144,2048]{1,0:T(8,128)(2,1)}, bf16[144,2048]{1,0:T(8,128)(2,1)S(1)}, u32[]{:S(2)}, u32[]{:S(2)}) collective-permute-start(bf16[144,2048]{1,0:T(8,128)(2,1)} %join.2.refs_0_), channel_id=1, source_target_pairs={{0,16},{8,24},{16,0},{24,8},{1,17},{9,25},{17,1},{25,9},{2,18},{10... | collective-permute-start | bytes 1769480 | tf_op jit(solution)/shard_map/ppermute | solution.py:418
  25.9 6.8 %collective-permute-start.4 = (bf16[16,2304]{1,0:T(8,128)(2,1)S(1)}, bf16[16,2304]{1,0:T(8,128)(2,1)S(1)}, u32[]{:S(2)}, u32[]{:S(2)}) collective-permute-start(bf16[16,2304]{1,0:T(8,128)(2,1)S(1)} %get-tuple-element.82), channel_id=1, source_target_pairs={{0,2},{1,3},{2,0},{3,1},{4,6},{5,7},{6,4},{7,5},{8,10},{9,11},{10,... | collective-permute-start | bytes 221192 | tf_op jit(solution)/shard_map/ppermute | solution.py:418
  26.9 7.9 %collective-permute-start.5 = (bf16[16,2304]{1,0:T(8,128)(2,1)S(1)}, bf16[16,2304]{1,0:T(8,128)(2,1)S(1)}, u32[]{:S(2)}, u32[]{:S(2)}) collective-permute-start(bf16[16,2304]{1,0:T(8,128)(2,1)S(1)} %get-tuple-element.83), channel_id=1, source_target_pairs={{0,3},{1,2},{2,1},{3,0},{4,7},{5,6},{6,5},{7,4},{8,11},{9,10},{10,... | collective-permute-start | bytes 221192 | tf_op jit(solution)/shard_map/ppermute | solution.py:418
  29.4 15.6 %collective-permute-start.6 = (bf16[16,2304]{1,0:T(8,128)(2,1)S(1)}, bf16[16,2304]{1,0:T(8,128)(2,1)S(1)}, u32[]{:S(2)}, u32[]{:S(2)}) collective-permute-start(bf16[16,2304]{1,0:T(8,128)(2,1)S(1)} %get-tuple-element.84), channel_id=1, source_target_pairs={{0,4},{1,5},{2,6},{3,7},{4,0},{5,1},{6,2},{7,3},{8,12},{9,13},{10,... | collective-permute-start | bytes 221192 | tf_op jit(solution)/shard_map/ppermute | solution.py:418
  31.6 13.4 %collective-permute-start.7 = (bf16[16,2304]{1,0:T(8,128)(2,1)S(1)}, bf16[16,2304]{1,0:T(8,128)(2,1)S(1)}, u32[]{:S(2)}, u32[]{:S(2)}) collective-permute-start(bf16[16,2304]{1,0:T(8,128)(2,1)S(1)} %get-tuple-element.85), channel_id=1, source_target_pairs={{0,5},{1,4},{2,7},{3,6},{4,1},{5,0},{6,3},{7,2},{8,13},{9,12},{10,... | collective-permute-start | bytes 221192 | tf_op jit(solution)/shard_map/ppermute | solution.py:418
  32.7 12.3 %collective-permute-start.8 = (bf16[16,2304]{1,0:T(8,128)(2,1)S(1)}, bf16[16,2304]{1,0:T(8,128)(2,1)S(1)}, u32[]{:S(2)}, u32[]{:S(2)}) collective-permute-start(bf16[16,2304]{1,0:T(8,128)(2,1)S(1)} %get-tuple-element.86), channel_id=1, source_target_pairs={{0,6},{1,7},{2,4},{3,5},{4,2},{5,3},{6,0},{7,1},{8,14},{9,15},{10,... | collective-permute-start | bytes 221192 | tf_op jit(solution)/shard_map/ppermute | solution.py:418
  34.9 10.1 %collective-permute-start.9 = (bf16[16,2304]{1,0:T(8,128)(2,1)S(1)}, bf16[16,2304]{1,0:T(8,128)(2,1)S(1)}, u32[]{:S(2)}, u32[]{:S(2)}) collective-permute-start(bf16[16,2304]{1,0:T(8,128)(2,1)S(1)} %get-tuple-element.87), channel_id=1, source_target_pairs={{0,7},{1,6},{2,5},{3,4},{4,3},{5,2},{6,1},{7,0},{8,15},{9,14},{10,... | collective-permute-start | bytes 221192 | tf_op jit(solution)/shard_map/ppermute | solution.py:418
  45.2 11.6 %collective-permute-start.16 = (bf16[144,2048]{1,0:T(8,128)(2,1)S(1)}, bf16[144,2048]{1,0:T(8,128)(2,1)S(1)}, u32[]{:S(2)}, u32[]{:S(2)}) collective-permute-start(bf16[144,2048]{1,0:T(8,128)(2,1)S(1)} %join.3.scaled_ref.refs_4_), channel_id=1, source_target_pairs={{0,8},{8,0},{16,24},{24,16},{1,9},{9,1},{17,25},{25,17},{2,10},{10... | collective-permute-start | bytes 1769480 | tf_op jit(solution)/shard_map/ppermute | solution.py:418
  45.3 12.3 %collective-permute-start.15 = (bf16[144,2048]{1,0:T(8,128)(2,1)S(1)}, bf16[144,2048]{1,0:T(8,128)(2,1)S(1)}, u32[]{:S(2)}, u32[]{:S(2)}) collective-permute-start(bf16[144,2048]{1,0:T(8,128)(2,1)S(1)} %collective-permute-done.14.refs_1_.refs_2_), channel_id=1, source_target_pairs={{0,8},{8,0},{16,24},{24,16},{1,9},{9,1},{17,25},{25,17},{2,10},{10... | collective-permute-start | bytes 1769480 | tf_op jit(solution)/shard_map/ppermute | solution.py:418
  45.8 15.4 %collective-permute-start.25 = (bf16[144,2048]{1,0:T(8,128)(2,1)S(1)}, bf16[144,2048]{1,0:T(8,128)(2,1)}, u32[]{:S(2)}, u32[]{:S(2)}) collective-permute-start(bf16[144,2048]{1,0:T(8,128)(2,1)S(1)} %join.3.scaled_ref.refs_4_), channel_id=1, source_target_pairs={{0,16},{8,24},{16,0},{24,8},{1,17},{9,25},{17,1},{25,9},{2,18},{10... | collective-permute-start | bytes 1769480 | tf_op jit(solution)/shard_map/ppermute | solution.py:418
  46.4 18.3 %collective-permute-start.24 = (bf16[144,2048]{1,0:T(8,128)(2,1)}, bf16[144,2048]{1,0:T(8,128)(2,1)}, u32[]{:S(2)}, u32[]{:S(2)}) collective-permute-start(bf16[144,2048]{1,0:T(8,128)(2,1)} %join.2.refs_0_), channel_id=1, source_target_pairs={{0,8},{8,0},{16,24},{24,16},{1,9},{9,1},{17,25},{25,17},{2,10},{10... | collective-permute-start | bytes 1769480 | tf_op jit(solution)/shard_map/ppermute | solution.py:418
  61.2 22.7 %collective-permute-start.26 = (bf16[144,2048]{1,0:T(8,128)(2,1)}, bf16[144,2048]{1,0:T(8,128)(2,1)}, u32[]{:S(2)}, u32[]{:S(2)}) collective-permute-start(bf16[144,2048]{1,0:T(8,128)(2,1)} %collective-permute-done.25.refs_6_), channel_id=1, source_target_pairs={{0,8},{8,0},{16,24},{24,16},{1,9},{9,1},{17,25},{25,17},{2,10},{10... | collective-permute-start | bytes 1769480 | tf_op jit(solution)/shard_map/ppermute | solution.py:418
  61.9 8.2 %collective-permute-start.19 = (bf16[16,2304]{1,0:T(8,128)(2,1)}, bf16[16,2304]{1,0:T(8,128)(2,1)}, u32[]{:S(2)}, u32[]{:S(2)}) collective-permute-start(bf16[16,2304]{1,0:T(8,128)(2,1)} %get-tuple-element.118), channel_id=1, source_target_pairs={{0,3},{1,2},{2,1},{3,0},{4,7},{5,6},{6,5},{7,4},{8,11},{9,10},{10,... | collective-permute-start | bytes 221192 | tf_op jit(solution)/shard_map/ppermute | solution.py:418
  64.7 16.8 %collective-permute-start.20 = (bf16[16,2304]{1,0:T(8,128)(2,1)}, bf16[16,2304]{1,0:T(8,128)(2,1)S(1)}, u32[]{:S(2)}, u32[]{:S(2)}) collective-permute-start(bf16[16,2304]{1,0:T(8,128)(2,1)} %copy-done.26), channel_id=1, source_target_pairs={{0,4},{1,5},{2,6},{3,7},{4,0},{5,1},{6,2},{7,3},{8,12},{9,13},{10,... | collective-permute-start | bytes 221192 | tf_op jit(solution)/shard_map/ppermute | solution.py:418
  66.1 15.4 %collective-permute-start.21 = (bf16[16,2304]{1,0:T(8,128)(2,1)}, bf16[16,2304]{1,0:T(8,128)(2,1)S(1)}, u32[]{:S(2)}, u32[]{:S(2)}) collective-permute-start(bf16[16,2304]{1,0:T(8,128)(2,1)} %copy-done.25), channel_id=1, source_target_pairs={{0,5},{1,4},{2,7},{3,6},{4,1},{5,0},{6,3},{7,2},{8,13},{9,12},{10,... | collective-permute-start | bytes 221192 | tf_op jit(solution)/shard_map/ppermute | solution.py:418
  67.1 14.4 %collective-permute-start.22 = (bf16[16,2304]{1,0:T(8,128)(2,1)}, bf16[16,2304]{1,0:T(8,128)(2,1)S(1)}, u32[]{:S(2)}, u32[]{:S(2)}) collective-permute-start(bf16[16,2304]{1,0:T(8,128)(2,1)} %copy-done.24), channel_id=1, source_target_pairs={{0,6},{1,7},{2,4},{3,5},{4,2},{5,3},{6,0},{7,1},{8,14},{9,15},{10,... | collective-permute-start | bytes 221192 | tf_op jit(solution)/shard_map/ppermute | solution.py:418
  70.1 11.4 %collective-permute-start.23 = (bf16[16,2304]{1,0:T(8,128)(2,1)}, bf16[16,2304]{1,0:T(8,128)(2,1)S(1)}, u32[]{:S(2)}, u32[]{:S(2)}) collective-permute-start(bf16[16,2304]{1,0:T(8,128)(2,1)} %copy-done.23), channel_id=1, source_target_pairs={{0,7},{1,6},{2,5},{3,4},{4,3},{5,2},{6,1},{7,0},{8,15},{9,14},{10,... | collective-permute-start | bytes 221192 | tf_op jit(solution)/shard_map/ppermute | solution.py:418
  (30 other events, 133.6 us)

commit v5 on v3

--- a/solution.py
+++ b/solution.py
@@ -104,6 +104,11 @@
     return pieces, width // pieces
 
 
+def width_of(packed):
+    pieces = ROWS // (MOST - ROWS)
+    return packed.shape[2] * pieces // (pieces + 1)
+
+
 def cost(flops, moved):
     return pl.CostEstimate(flops=flops, bytes_accessed=moved, transcendentals=0)
 
@@ -124,15 +129,15 @@
     return jnp.where(mask, 1.0, 0.0).astype(jnp.bfloat16)
 
 
-def load(sources, targets, arrived):
-    copies = [
-        pltpu.make_async_copy(source, target, arrived.at[at])
-        for at, (source, target) in enumerate(zip(sources, targets))
-    ]
-    for copy in copies:
-        copy.start()
-    for copy in copies:
-        copy.wait()
+def start(pairs, arrived):
+    for at, (source, target) in enumerate(pairs):
+        pltpu.make_async_copy(source, target, arrived.at[at]).start()
+
+
+def wait(pairs, arrived, first=0):
+    for at, (source, target) in enumerate(pairs):
+        if at >= first:
+            pltpu.make_async_copy(source, target, arrived.at[at]).wait()
 
 
 def slot_masks(routes, blocks, width):
@@ -156,22 +161,27 @@
 def pack(blocks, routes, values, gates=None):
     tokens, width = values.shape
     pieces, step = cut(width)
-    scaled = gates is not None
-    sources = (routes, values) + ((gates,) if scaled else ())
+    sources = (routes,) + (() if gates is None else (gates,)) + (values,)
+    count = len(sources)
 
     def kernel(*refs):
-        count = len(sources)
         out, held, arrived = refs[count], refs[count + 1 : 2 * count + 1], refs[-1]
-        load(refs[:count], held, arrived)
+        pairs = list(zip(refs[:count], held))
+        start(pairs, arrived)
+        wait(pairs[:-1], arrived)
         main, spill, piece = slot_masks(held[0][...], blocks, width)
-        rows = dot(ones(main), held[1][...])
+        picks = [ones(spill & (piece == at)) for at in range(pieces)]
+        if gates is not None:
+            weights = held[1][...]
+            main_scale = jnp.sum(jnp.where(main, weights, 0.0), axis=1, keepdims=True)
+            spill_scale = jnp.sum(jnp.where(spill, weights, 0.0), axis=1, keepdims=True)
+        wait(pairs, arrived, count - 1)
+        rows = dot(ones(main), held[-1][...])
         extra = jnp.zeros((blocks * ROWS, step), jnp.float32)
         for at in range(pieces):
-            extra += dot(ones(spill & (piece == at)), held[1][:, at * step : (at + 1) * step])
-        if scaled:
-            weights = held[2][...]
-            rows = rows * jnp.sum(jnp.where(main, weights, 0.0), axis=1, keepdims=True)
-            extra = extra * jnp.sum(jnp.where(spill, weights, 0.0), axis=1, keepdims=True)
+            extra += dot(picks[at], held[-1][:, at * step : (at + 1) * step])
+        if gates is not None:
+            rows, extra = rows * main_scale, extra * spill_scale
         rows = rows.astype(jnp.bfloat16)
         extra = extra.astype(jnp.bfloat16)
         for block in range(blocks):
@@ -182,10 +192,10 @@
     return pl.pallas_call(
         kernel,
         out_shape=jax.ShapeDtypeStruct((blocks, ROWS, width + step), jnp.bfloat16),
-        in_specs=anywhere(len(sources)),
+        in_specs=anywhere(count),
         out_specs=pl.BlockSpec(memory_space=pltpu.VMEM),
         scratch_shapes=[pltpu.VMEM(source.shape, source.dtype) for source in sources]
-        + [pltpu.SemaphoreType.DMA((len(sources),))],
+        + [pltpu.SemaphoreType.DMA((count,))],
         compiler_params=params(),
         cost_estimate=cost(4 * blocks * ROWS * tokens * width, 4 * tokens * width),
         name="pack",
@@ -199,16 +209,21 @@
     pieces, step = cut(width)
 
     def kernel(routes_ref, back_ref, out, named, held, arrived):
-        load((routes_ref, back_ref), (named, held), arrived)
+        pairs = [(routes_ref, named), (back_ref, held)]
+        start(pairs, arrived)
+        wait(pairs[:1], arrived)
         main, spill, piece = slot_masks(named[...], blocks, width)
+        mains = ones(main)
+        picks = [ones(spill & (piece == at)) for at in range(pieces)]
+        wait(pairs, arrived, 1)
         rows = jnp.concatenate([held[at, :, :width] for at in range(blocks)], 0)
         extra = jnp.concatenate([held[at, :, width:] for at in range(blocks)], 0)
-        picked = dot(ones(main), rows, BY_ROWS)
+        picked = dot(mains, rows, BY_ROWS)
         for at in range(pieces):
             columns = slice(at * step, (at + 1) * step)
-            out[:, columns] = (
-                picked[:, columns] + dot(ones(spill & (piece == at)), extra, BY_ROWS)
-            ).astype(jnp.bfloat16)
+            out[:, columns] = (picked[:, columns] + dot(picks[at], extra, BY_ROWS)).astype(
+                jnp.bfloat16
+            )
 
     return pl.pallas_call(
         kernel,
@@ -226,11 +241,6 @@
     )(routes, returned)
 
 
-def width_of(packed):
-    pieces = ROWS // (MOST - ROWS)
-    return packed.shape[2] * pieces // (pieces + 1)
-
-
 def spill_picks(blocks, pieces, at):
     shape = (blocks * (MOST - ROWS), blocks * ROWS)
     slot = lax.broadcasted_iota(jnp.int32, shape, 0)
@@ -238,17 +248,16 @@
     return ones(row == slot * pieces + at)
 
 
-def unpack(packed, out, begin):
-    blocks = packed.shape[0]
-    width = width_of(packed)
-    pieces, step = cut(width)
+def unpack(main, tail, pieces, begin, first, out):
+    blocks = main.shape[0]
+    step = tail.shape[2]
     for at in range(blocks):
-        out[begin + at * ROWS : begin + (at + 1) * ROWS, :] = packed[at, :, :width]
-    extra = jnp.concatenate([packed[at, :, width:] for at in range(blocks)], 0)
-    first, last = begin + blocks * ROWS, begin + blocks * MOST
-    for at in range(pieces):
-        out[first:last, at * step : (at + 1) * step] = dot(
-            spill_picks(blocks, pieces, at), extra
+        out[first + at * ROWS : first + (at + 1) * ROWS, :] = main[at]
+    extra = jnp.concatenate([tail[at] for at in range(blocks)], 0)
+    spill = slice(first + blocks * ROWS, first + blocks * MOST)
+    for at in range(out.shape[1] // step):
+        out[spill, at * step : (at + 1) * step] = dot(
+            spill_picks(blocks, pieces, begin + at), extra
         ).astype(jnp.bfloat16)
 
 
@@ -258,45 +267,64 @@
 
 def row_tile(tile, width):
     return pl.BlockSpec((tile, width), lambda i: (i, 0))
+
+
+def tile_of(index, tile):
+    return pl.ds(pl.multiple_of(index * tile, tile), tile)
+
+
+def weight_copy(source, target, arrived, index, axis, tile):
+    here = tile_of(index, tile)
+    view = source.at[:, here] if axis else source.at[here, :]
+    return pltpu.make_async_copy(view, target.at[index], arrived.at[index])
 
 
 def forward(tile, packed, gate_proj, up_proj):
     groups = len(packed)
     blocks = packed[0].shape[0]
     width, hid = gate_proj.shape
+    pieces, _ = cut(width)
     slots = blocks * MOST
+    total = groups * slots
+    tiles = hid // tile
 
     def kernel(*refs):
-        gate_ref, up_ref, rows_ref, pre_gate_ref, pre_up_ref = refs[groups : groups + 5]
-        held, arrived = refs[groups + 5 :]
-
-        @pl.when(pl.program_id(0) == 0)
+        gate_ref, up_ref, pre_gate_ref, pre_up_ref = refs[groups : groups + 4]
+        held, rows, gate, up, arrived, gate_in, up_in = refs[groups + 4 :]
+        now = pl.program_id(0)
+
+        @pl.when(now == 0)
         def _():
-            load(refs[:groups], [held.at[at] for at in range(groups)], arrived)
+            pairs = [(refs[at], held.at[at]) for at in range(groups)]
+            start(pairs, arrived)
+            for at in range(tiles):
+                weight_copy(gate_ref, gate, gate_in, at, 1, tile).start()
+                weight_copy(up_ref, up, up_in, at, 1, tile).start()
+            wait(pairs, arrived)
             for at in range(groups):
-                unpack(held.at[at], rows_ref, at * slots)
-
-        pre_gate_ref[...] = dot(rows_ref[...], gate_ref[...])
-        pre_up_ref[...] = dot(rows_ref[...], up_ref[...])
-
-    total = groups * slots
+                unpack(
+                    held.at[at, :, :, :width], held.at[at, :, :, width:], pieces, 0, at * slots, rows
+                )
+
+        weight_copy(gate_ref, gate, gate_in, now, 1, tile).wait()
+        pre_gate_ref[...] = dot(rows[...], gate[now])
+        weight_copy(up_ref, up, up_in, now, 1, tile).wait()
+        pre_up_ref[...] = dot(rows[...], up[now])
+
     return pl.pallas_call(
         kernel,
-        grid=(hid // tile,),
-        out_shape=[
-            jax.ShapeDtypeStruct((total, width), jnp.bfloat16),
-            jax.ShapeDtypeStruct((total, hid), jnp.float32),
-            jax.ShapeDtypeStruct((total, hid), jnp.float32),
-        ],
-        in_specs=anywhere(groups) + [column_tile(width, tile)] * 2,
-        out_specs=[
-            pl.BlockSpec((total, width), lambda i: (0, 0)),
-            column_tile(total, tile),
-            column_tile(total, tile),
-        ],
+        grid=(tiles,),
+        out_shape=[jax.ShapeDtypeStruct((total, hid), jnp.float32)] * 2,
+        in_specs=anywhere(groups + 2),
+        out_specs=[column_tile(total, tile)] * 2,
         scratch_shapes=[
             pltpu.VMEM((groups,) + packed[0].shape, jnp.bfloat16),
+            pltpu.VMEM((total, width), jnp.bfloat16),
+            pltpu.VMEM((tiles, width, tile), jnp.bfloat16),
+            pltpu.VMEM((tiles, width, tile), jnp.bfloat16),
             pltpu.SemaphoreType.DMA((groups,)),
+            pltpu.SemaphoreType.DMA((tiles,)),
+            pltpu.SemaphoreType.DMA((tiles,)),
         ],
         compiler_params=params(),
         cost_estimate=cost(4 * total * width * hid, 4 * width * hid + 4 * total * width),
@@ -318,31 +346,42 @@
     width, hid = gate_proj.shape
     slots = blocks * MOST
     pieces, step = cut(width)
-
-    def kernel(packed_ref, pre_gate_ref, pre_up_ref, gate_ref, up_ref, down_ref, *rest):
-        out, scaled, hidden_ref, d_gate_ref, d_up_ref, held, total, arrived = rest
-
-        @pl.when(pl.program_id(0) == 0)
+    tiles = hid // tile
+
+    def kernel(packed_ref, gate_ref, up_ref, down_ref, pre_gate_ref, pre_up_ref, *rest):
+        out, hidden_ref, d_gate_ref, d_up_ref, held, scaled, total, gate, up, down = rest[:10]
+        arrived, gate_in, up_in, down_in = rest[10:]
+        now = pl.program_id(0)
+
+        @pl.when(now == 0)
         def _():
-            load([packed_ref], [held], arrived)
-            unpack(held, scaled, 0)
-
-        d_hidden = dot(scaled[...], down_ref[...], BY_WIDTH)
+            start([(packed_ref, held)], arrived)
+            for at in range(tiles):
+                weight_copy(down_ref, down, down_in, at, 0, tile).start()
+                weight_copy(gate_ref, gate, gate_in, at, 1, tile).start()
+                weight_copy(up_ref, up, up_in, at, 1, tile).start()
+            wait([(packed_ref, held)], arrived)
+            unpack(held.at[:, :, :width], held.at[:, :, width:], pieces, 0, 0, scaled)
+
+        weight_copy(down_ref, down, down_in, now, 0, tile).wait()
+        d_hidden = dot(scaled[...], down[now], BY_WIDTH)
         hidden, d_gate, d_up = hidden_grads(pre_gate_ref[...], pre_up_ref[...], d_hidden)
         hidden_ref[...] = hidden
         d_gate_ref[...] = d_gate
         d_up_ref[...] = d_up
-        part = dot(d_gate, gate_ref[...], BY_WIDTH) + dot(d_up, up_ref[...], BY_WIDTH)
-
-        @pl.when(pl.program_id(0) == 0)
+        weight_copy(gate_ref, gate, gate_in, now, 1, tile).wait()
+        weight_copy(up_ref, up, up_in, now, 1, tile).wait()
+        part = dot(d_gate, gate[now], BY_WIDTH) + dot(d_up, up[now], BY_WIDTH)
+
+        @pl.when(now == 0)
         def _():
             total[...] = part
 
-        @pl.when(pl.program_id(0) > 0)
+        @pl.when(now > 0)
         def _():
             total[...] += part
 
-        @pl.when(pl.program_id(0) == hid // tile - 1)
+        @pl.when(now == tiles - 1)
         def _():
             done = total[...].astype(jnp.bfloat16)
             extra = jnp.zeros((blocks * ROWS, step), jnp.float32)
@@ -359,114 +398,126 @@
                 out[block, :, width:] = extra[part_of]
 
     factor = jax.ShapeDtypeStruct((slots, hid), jnp.bfloat16)
-    return pl.pallas_call(
+    sent, *own = pl.pallas_call(
         kernel,
-        grid=(hid // tile,),
-        out_shape=[
-            jax.ShapeDtypeStruct(packed.shape, jnp.bfloat16),
-            jax.ShapeDtypeStruct((slots, width), jnp.bfloat16),
-            factor,
-            factor,
-            factor,
-        ],
-        in_specs=anywhere(1)
-        + [column_tile(slots, tile)] * 2
-        + [column_tile(width, tile)] * 2
-        + [row_tile(tile, width)],
-        out_specs=[
-            pl.BlockSpec(packed.shape, lambda i: (0, 0, 0)),
-            pl.BlockSpec((slots, width), lambda i: (0, 0)),
-        ]
+        grid=(tiles,),
+        out_shape=[jax.ShapeDtypeStruct(packed.shape, jnp.bfloat16)] + [factor] * 3,
+        in_specs=anywhere(4) + [column_tile(slots, tile)] * 2,
+        out_specs=[pl.BlockSpec(packed.shape, lambda i: (0, 0, 0))]
         + [column_tile(slots, tile)] * 3,
         scratch_shapes=[
             pltpu.VMEM(packed.shape, jnp.bfloat16),
+            pltpu.VMEM((slots, width), jnp.bfloat16),
             pltpu.VMEM((slots, width), jnp.float32),
+            pltpu.VMEM((tiles, width, tile), jnp.bfloat16),
+            pltpu.VMEM((tiles, width, tile), jnp.bfloat16),
+            pltpu.VMEM((tiles, tile, width), jnp.bfloat16),
             pltpu.SemaphoreType.DMA((1,)),
+            pltpu.SemaphoreType.DMA((tiles,)),
+            pltpu.SemaphoreType.DMA((tiles,)),
+            pltpu.SemaphoreType.DMA((tiles,)),
         ],
         compiler_params=params(),
         cost_estimate=cost(6 * slots * width * hid, 6 * width * hid),
         name="back",
-    )(packed, pre_gate, pre_up, gate_proj, up_proj, down_proj)
-
-
-def weight_grads(tile, groups, part, packed, rows, pre_gate, pre_up, down_proj, own=(), sums=()):
-    others = len(packed)
-    blocks = packed[0].shape[0]
+    )(packed, gate_proj, up_proj, down_proj, pre_gate, pre_up)
+    return sent, own
+
+
+def weight_grads(tile, part, rows, scaled, pre_gate, pre_up, down_proj, own):
+    groups = len(rows)
+    blocks = rows[0].shape[0]
     hid, width = down_proj.shape
+    pieces, step = cut(width)
     slots = blocks * MOST
-    known = slots if own else 0
-    some = others * slots
+    some = (groups - 1) * slots
     share = width // groups
-    loaded = others + 1 + len(own[:1])
+    tiles = hid // tile
 
     def kernel(part_ref, *refs):
-        refs = list(refs)
-        sources = [refs.pop(0) for _ in range(loaded)]
-        pre_gate_ref, pre_up_ref, down_ref = [refs.pop(0) for _ in range(3)]
-        factors = [refs.pop(0) for _ in own[1:]]
-        added = [refs.pop(0) for _ in sums]
-        d_gate_ref, d_up_ref, d_down_ref, held, scaled, x_mine, dy_mine, arrived = refs
-
-        @pl.when(pl.program_id(0) == 0)
+        x_refs, dy_refs = refs[:groups], refs[groups : 2 * groups]
+        down_ref, pre_gate_ref, pre_up_ref, own_hidden, own_gate, own_up = refs[
+            2 * groups : 2 * groups + 6
+        ]
+        d_gate_ref, d_up_ref, d_down_ref = refs[2 * groups + 6 : 2 * groups + 9]
+        held, mains, tails, others, x_mine, dy_mine, down = refs[2 * groups + 9 : 2 * groups + 16]
+        held_in, mains_in, tails_in, down_in = refs[2 * groups + 16 :]
+        now = pl.program_id(0)
+
+        @pl.when(now == 0)
         def _():
             columns = pl.ds(pl.multiple_of(part_ref[0] * share, share), share)
-            here = [source.at[:, columns] for source in sources[others:]]
-            targets = [held.at[at] for at in range(others)] + [x_mine]
-            targets += [dy_mine.at[:known, :]] if own else []
-            load(sources[:others] + here, targets, arrived)
-            for at in range(others):
-                unpack(held.at[at], scaled, at * slots)
-            dy_mine[known:, :] = scaled[:, columns]
-
-        d_hidden = dot(scaled[...], down_ref[...], BY_WIDTH)
+            begin = part_ref[0] * (share // step)
+            whole = [(dy_refs[at], held.at[at - 1]) for at in range(1, groups)]
+            sources = list(x_refs) + [dy_refs[0]]
+            cuts = [(ref.at[:, :, columns], mains.at[at]) for at, ref in enumerate(sources)]
+            ends = [(ref.at[:, :, width:], tails.at[at]) for at, ref in enumerate(sources)]
+            start(whole, held_in)
+            for at in range(tiles):
+                weight_copy(down_ref, down, down_in, at, 0, tile).start()
+            start(cuts, mains_in)
+            start(ends, tails_in)
+            wait(whole, held_in)
+            for at in range(groups - 1):
+                unpack(
+                    held.at[at, :, :, :width],
+                    held.at[at, :, :, width:],
+                    pieces,
+                    0,
+                    at * slots,
+                    others,
+                )
+            dy_mine[slots:, :] = others[:, columns]
+            wait(cuts, mains_in)
+            wait(ends, tails_in)
+            for at in range(groups):
+                unpack(mains.at[at], tails.at[at], pieces, begin, at * slots, x_mine)
+            unpack(mains.at[groups], tails.at[groups], pieces, begin, 0, dy_mine)
+
+        weight_copy(down_ref, down, down_in, now, 0, tile).wait()
+        d_hidden = dot(others[...], down[now], BY_WIDTH)
         hidden, d_gate, d_up = hidden_grads(pre_gate_ref[...], pre_up_ref[...], d_hidden)
-        if own:
-            hidden = jnp.concatenate([factors[0][...], hidden], 0)
-            d_gate = jnp.concatenate([factors[1][...], d_gate], 0)
-            d_up = jnp.concatenate([factors[2][...], d_up], 0)
+        hidden = jnp.concatenate([own_hidden[...], hidden], 0)
+        d_gate = jnp.concatenate([own_gate[...], d_gate], 0)
+        d_up = jnp.concatenate([own_up[...], d_up], 0)
         both = dot(x_mine[...], jnp.concatenate([d_gate, d_up], 1), BY_ROWS)
-        d_gate, d_up = both[:, :tile], both[:, tile:]
-        d_down = dot(hidden, dy_mine[...], BY_ROWS)
-        if sums:
-            d_gate += added[0][...]
-            d_up += added[1][...]
-            d_down += added[2][...]
-        d_gate_ref[...] = d_gate
-        d_up_ref[...] = d_up
-        d_down_ref[...] = d_down
-
-    at_row = known // some
-    behind = pl.BlockSpec((some, tile), lambda i: (at_row, i))
-    grads = [column_tile(share, tile), column_tile(share, tile), row_tile(tile, share)]
+        d_gate_ref[...] = both[:, :tile]
+        d_up_ref[...] = both[:, tile:]
+        d_down_ref[...] = dot(hidden, dy_mine[...], BY_ROWS)
+
     return pl.pallas_call(
         kernel,
-        grid=(hid // tile,),
+        grid=(tiles,),
         out_shape=[
             jax.ShapeDtypeStruct((share, hid), jnp.float32),
             jax.ShapeDtypeStruct((share, hid), jnp.float32),
             jax.ShapeDtypeStruct((hid, share), jnp.float32),
         ],
         in_specs=[pl.BlockSpec(memory_space=pltpu.SMEM)]
-        + anywhere(loaded)
-        + [behind] * 2
-        + [row_tile(tile, width)]
-        + [column_tile(slots, tile)] * len(own[1:])
-        + grads[: len(sums)],
-        out_specs=grads,
+        + anywhere(2 * groups + 1)
+        + [column_tile(some, tile)] * 2
+        + [column_tile(slots, tile)] * 3,
+        out_specs=[column_tile(share, tile), column_tile(share, tile), row_tile(tile, share)],
         scratch_shapes=[
-            pltpu.VMEM((others,) + packed[0].shape, jnp.bfloat16),
+            pltpu.VMEM((groups - 1,) + rows[0].shape, jnp.bfloat16),
+            pltpu.VMEM((groups + 1, blocks, ROWS, share), jnp.bfloat16),
+            pltpu.VMEM((groups + 1, blocks, ROWS, step), jnp.bfloat16),
             pltpu.VMEM((some, width), jnp.bfloat16),
-            pltpu.VMEM((known + some, share), jnp.bfloat16),
-            pltpu.VMEM((known + some, share), jnp.bfloat16),
-            pltpu.SemaphoreType.DMA((loaded,)),
+            pltpu.VMEM((groups * slots, share), jnp.bfloat16),
+            pltpu.VMEM((groups * slots, share), jnp.bfloat16),
+            pltpu.VMEM((tiles, tile, width), jnp.bfloat16),
+            pltpu.SemaphoreType.DMA((groups - 1,)),
+            pltpu.SemaphoreType.DMA((groups + 1,)),
+            pltpu.SemaphoreType.DMA((groups + 1,)),
+            pltpu.SemaphoreType.DMA((tiles,)),
         ],
         compiler_params=params(),
         cost_estimate=cost(
-            2 * some * width * hid + 6 * (known + some) * share * hid,
-            2 * width * hid + 4 * some * width,
+            2 * some * width * hid + 6 * groups * slots * share * hid,
+            2 * width * hid + 4 * groups * slots * width,
         ),
         name="weight_grads",
-    )(part, *packed, rows, *own[:1], pre_gate, pre_up, down_proj, *own[1:], *sums)
+    )(part, *rows, *scaled, down_proj, pre_gate, pre_up, *own)
 
 
 def swap(value, axis, distance):
@@ -483,31 +534,33 @@
 
 
 def gather_body(tokens, cotangent, routes, expert_gates, gate_proj, up_proj, down_proj):
-    blocks, groups = lax.axis_size("expert"), lax.axis_size("dp")
+    blocks = lax.axis_size("expert")
     tile = 256
     part = lax.axis_index("dp").astype(jnp.int32).reshape(1)
     routes = routes.reshape(1, -1)
     gates = expert_gates.reshape(1, -1)
-    x_own = exchange(pack(blocks, routes, tokens))
-    x_far = swap(x_own, "dp", 2)
-    x_near = swap(x_own, "dp", 1)
-    dy_own = exchange(after(pack(blocks, routes, cotangent, gates), x_own))
-    rows, pre_gate, pre_up = forward(tile, [x_own, x_near], gate_proj, up_proj)
-    x_last = swap(x_far, "dp", 1)
-    dy_own = after(dy_own, pre_gate)
-    dy_far = swap(dy_own, "dp", 2)
-    dy_near = swap(dy_own, "dp", 1)
-    sent, *own = back(tile, dy_own, pre_gate, pre_up, gate_proj, up_proj, down_proj)
+    packed = pack(blocks, routes, tokens)
+    rows = exchange(packed)
+    scaled = exchange(pack(blocks, routes, after(cotangent, packed), gates))
+    far = swap(rows, "dp", 2)
+    near = swap(rows, "dp", 1)
+    pre = forward(tile, [rows], gate_proj, up_proj)
+    scaled = after(scaled, *pre)
+    dy_far = swap(scaled, "dp", 2)
+    dy_near = swap(scaled, "dp", 1)
+    sent, own = back(tile, scaled, *pre, gate_proj, up_proj, down_proj)
     returned = exchange(sent)
-    far_rows, far_gate, far_up = forward(
-        tile, [after(x_far, sent), x_last], gate_proj, up_proj
-    )
-    sums = weight_grads(
-        tile, groups, part, [dy_near], rows, pre_gate, pre_up, down_proj, own=own
-    )
+    last = swap(after(far, pre[0]), "dp", 1)
+    others = forward(tile, [after(near, sent), far, last], gate_proj, up_proj)
     dy_last = swap(after(dy_far, sent), "dp", 1)
     grads = weight_grads(
-        tile, groups, part, [dy_far, dy_last], far_rows, far_gate, far_up, down_proj, sums=sums
+        tile,
+        part,
+        [rows, near, far, last],
+        [scaled, dy_near, dy_far, dy_last],
+        *others,
+        down_proj,
+        own,
     )
     return (merge(routes, returned), *grads)
 

time: 94.7 us -> 103 us (1.088)
  waiting for transfers between devices: 21.4 us -> 35.1 us
  Pallas kernels: 52.3 us -> 47.4 us
    ppermute x6, waiting for transfers between devices: 2.51 us -> 12.6 us  [swap(): lax.ppermute(value, axis, [(at, at ^ distance) for at in range(size)])]
    pallas_call x5 -> x4, Pallas kernels: 44.9 us -> 40.3 us  [the longest x2 16.5 us: forward(): pl.pallas_call(kernel, grid=(tiles,), out_shape=[jax.ShapeDtypeStruct((to...]
    all_to_all x3, waiting for transfers between devices: 18.9 us -> 22.5 us  [exchange(): lax.all_to_all(blocks, 'expert', split_axis=0, concat_axis=0, tiled=True)]
  transfers between devices with their start and end apart: 9 -> 9, of which waited for: 4 -> 4; matrix products, arithmetic and copies ran while one was open for 0% -> 0% of each run, Pallas kernels for 42% -> 32%
where the time goes in v5:
time: 103 us
  Pallas kernels  47.4 us (46%)
  waiting for transfers between devices  35.1 us (34%)
  starting transfers between devices  19.3 us (19%)
    all_to_all x3, waiting for transfers between devices, exchange(): lax.all_to_all(blocks, 'expert', split_axis=0, concat_axis=0, tiled=True)  22.5 us
    pallas_call x2, Pallas kernels, forward(): pl.pallas_call(kernel, grid=(tiles,), out_shape=[jax.ShapeDtypeStruct((to...  16.5 us
    all_to_all x3, starting transfers between devices, exchange(): lax.all_to_all(blocks, 'expert', split_axis=0, concat_axis=0, tiled=True)  15.7 us
    ppermute x6, waiting for transfers between devices, swap(): lax.ppermute(value, axis, [(at, at ^ distance) for at in range(size)])  12.6 us
    pallas_call x1, Pallas kernels, weight_grads(): pl.pallas_call(kernel, grid=(tiles,), out_shape=[jax.ShapeDtypeStruct((sh...  12.1 us
    pallas_call x1, Pallas kernels, back(): pl.pallas_call(kernel, grid=(tiles,), out_shape=[jax.ShapeDtypeStruct(pac...  11.7 us
    pallas_call x2, Pallas kernels, pack(): pl.pallas_call(kernel, out_shape=jax.ShapeDtypeStruct((blocks, ROWS, widt...  4.66 us
    ppermute x6, starting transfers between devices, swap(): lax.ppermute(value, axis, [(at, at ^ distance) for at in range(size)])  3.68 us
  transfers between devices with their start and end apart: 9, of which 4 were waited for; matrix products, arithmetic and copies ran while one was open for 0% of the time, Pallas kernels for 32%

profile of v5, /device:TPU:0, one launch (start us, length us, event | category | flops | bytes accessed | tf_op | source)
XLA Modules:
  0.0 102.6 jit_solution(2001402981882944094)
XLA Ops:
  0.6 2.3 %pack.2 = bf16[8,16,2304]{2,1,0:T(8,128)(2,1)} custom-call(s32[1,128]{1,0:T(1,128)} %bitcast.3, bf16[128,2048]{1,0:T(8,128)(2,1)} %refs_1_.2), custom_call_target="tpu_custom_call" | custom-call | flops 134217728 | bytes 1048576 | tf_op jit(solution)/shard_map/pack/pallas_call | solution.py:192
  3.0 7.3 %all-to-all-start.1 = ((bf16[8,16,2304]{2,1,0:T(8,128)(2,1)}), bf16[8,16,2304]{2,1,0:T(8,128)(2,1)}, u32[]{:S(2)}, u32[]{:S(2)}) async-start(bf16[8,16,2304]{2,1,0:T(8,128)(2,1)} %pack.2), calls=%async_computation.1 | async-start | bytes 1179648 | tf_op jit(solution)/shard_map/all_to_all | solution.py:529
  10.2 2.3 %pack.3 = bf16[8,16,2304]{2,1,0:T(8,128)(2,1)} custom-call(s32[1,128]{1,0:T(1,128)} %bitcast.4, f32[1,128]{1,0:T(1,128)} %bitcast.6, bf16[128,2048]{1,0:T(8,128)(2,1)} %refs_2_.1), custom_call_target="tpu_custom_call" | custom-call | flops 134217728 | bytes 1048576 | tf_op jit(solution)/shard_map/pack/pallas_call | solution.py:192
  12.6 13.6 %all-to-all-done.1.refs_0_ = bf16[8,16,2304]{2,1,0:T(8,128)(2,1)} async-done(((bf16[8,16,2304]{2,1,0:T(8,128)(2,1)}), bf16[8,16,2304]{2,1,0:T(8,128)(2,1)}, u32[]{:S(2)}, u32[]{:S(2)}) %all-to-all-start.1) | async-done | bytes 589856 | tf_op jit(solution)/shard_map/all_to_all | solution.py:529
  26.2 4.2 %all-to-all-start = ((bf16[8,16,2304]{2,1,0:T(8,128)(2,1)}), bf16[8,16,2304]{2,1,0:T(8,128)(2,1)}, u32[]{:S(2)}, u32[]{:S(2)}) async-start(bf16[8,16,2304]{2,1,0:T(8,128)(2,1)} %pack.3), calls=%async_computation | async-start | bytes 1179648 | tf_op jit(solution)/shard_map/all_to_all | solution.py:529
  30.4 1.6 %collective-permute-start.1 = (bf16[8,16,2304]{2,1,0:T(8,128)(2,1)}, bf16[8,16,2304]{2,1,0:T(8,128)(2,1)}, u32[]{:S(2)}, u32[]{:S(2)}) collective-permute-start(bf16[8,16,2304]{2,1,0:T(8,128)(2,1)} %all-to-all-done.1.refs_0_), channel_id=1, source_target_pairs={{0,16},{8,24},{16,0},{24,8},{1,17},{9,25},{17,1},{25,9},{2,18},{10... | collective-permute-start | bytes 1769480 | tf_op jit(solution)/shard_map/ppermute | solution.py:525
  32.0 6.1 %forward.2 = (f32[144,768]{1,0:T(8,128)}, f32[144,768]{1,0:T(8,128)}) custom-call(bf16[8,16,2304]{2,1,0:T(8,128)(2,1)} %all-to-all-done.1.refs_0_, bf16[2048,768]{1,0:T(8,128)(2,1)} %refs_3_.1, bf16[2048,768]{1,0:T(8,128)(2,1)} %refs_4_.1), custom_call_target="tpu_custom_call" | custom-call | flops 905969664 | bytes 7471104 | tf_op jit(solution)/shard_map/forward/pallas_call | solution.py:314
  38.1 8.0 %all-to-all-done.packed_ref.refs_4_ = bf16[8,16,2304]{2,1,0:T(8,128)(2,1)} async-done(((bf16[8,16,2304]{2,1,0:T(8,128)(2,1)}), bf16[8,16,2304]{2,1,0:T(8,128)(2,1)}, u32[]{:S(2)}, u32[]{:S(2)}) %all-to-all-start) | async-done | bytes 589856 | tf_op jit(solution)/shard_map/all_to_all | solution.py:529
  46.1 11.7 %back.1 = (bf16[8,16,2304]{2,1,0:T(8,128)(2,1)}, bf16[144,768]{1,0:T(8,128)(2,1)}, bf16[144,768]{1,0:T(8,128)(2,1)}, bf16[144,768]{1,0:T(8,128)(2,1)}) custom-call(bf16[8,16,2304]{2,1,0:T(8,128)(2,1)} %all-to-all-done.packed_ref.refs_4_, bf16[2048,768]{1,0:T(8,128)(2,1)} %refs_3_.1, bf16[2048,768]{1,0:T(8,128)(2,1)} %refs_4_.1, bf16[768,2048]{1,0:T(8,128)(2,1)} %refs_8_.1, ...), custom_call_target="tpu_custom_call" | custom-call | flops 1358954496 | bytes 9437184 | tf_op jit(solution)/shard_map/back/pallas_call | solution.py:401
  57.8 4.2 %all-to-all-start.2 = ((bf16[8,16,2304]{2,1,0:T(8,128)(2,1)}), bf16[8,16,2304]{2,1,0:T(8,128)(2,1)}, u32[]{:S(2)}, u32[]{:S(2)}) async-start(bf16[8,16,2304]{2,1,0:T(8,128)(2,1)} %get-tuple-element.24), calls=%async_computation.2 | async-start | bytes 1179648 | tf_op jit(solution)/shard_map/all_to_all | solution.py:529
  62.0 1.6 %collective-permute-start.4 = (bf16[8,16,2304]{2,1,0:T(8,128)(2,1)}, bf16[8,16,2304]{2,1,0:T(8,128)(2,1)}, u32[]{:S(2)}, u32[]{:S(2)}) collective-permute-start(bf16[8,16,2304]{2,1,0:T(8,128)(2,1)} %all-to-all-done.packed_ref.refs_4_), channel_id=1, source_target_pairs={{0,16},{8,24},{16,0},{24,8},{1,17},{9,25},{17,1},{25,9},{2,18},{10... | collective-permute-start | bytes 1769480 | tf_op jit(solution)/shard_map/ppermute | solution.py:525
  63.6 0.0 collective-permute-start
  63.6 0.0 collective-permute-done.1.refs_1_.refs_2_
  63.6 0.5 collective-permute-start.2
  64.1 0.0 collective-permute-start.3
  64.1 12.6 %collective-permute-done.4.refs_6_ = bf16[8,16,2304]{2,1,0:T(8,128)(2,1)} collective-permute-done((bf16[8,16,2304]{2,1,0:T(8,128)(2,1)}, bf16[8,16,2304]{2,1,0:T(8,128)(2,1)}, u32[]{:S(2)}, u32[]{:S(2)}) %collective-permute-start.4) | collective-permute-done | bytes 589856 | tf_op jit(solution)/shard_map/ppermute | solution.py:525
  76.7 0.0 collective-permute-start.5
  76.7 0.0 collective-permute-done.refs_0_.refs_1_
  76.7 0.9 all-to-all-done.2.back_ref
  77.6 2.4 %merge.1 = bf16[128,2048]{1,0:T(8,128)(2,1)} custom-call(s32[1,128]{1,0:T(1,128)} %bitcast.5, bf16[8,16,2304]{2,1,0:T(8,128)(2,1)} %all-to-all-done.2.back_ref), custom_call_target="tpu_custom_call" | custom-call | flops 134217728 | bytes 1048576 | tf_op jit(solution)/shard_map/merge/pallas_call | solution.py:228
  80.0 0.0 collective-permute-done.2.refs_2_.refs_3_
  80.0 10.4 %forward.3 = (f32[432,768]{1,0:T(8,128)}, f32[432,768]{1,0:T(8,128)}) custom-call(bf16[8,16,2304]{2,1,0:T(8,128)(2,1)} %collective-permute-done.refs_0_.refs_1_, bf16[8,16,2304]{2,1,0:T(8,128)(2,1)} %collective-permute-done.1.refs_1_.refs_2_, bf16[8,16,2304]{2,1,0:T(8,128)(2,1)} %collective-permute-done.2.refs_2_.refs_3_, bf16[2048,768]{1,0:T(8,128)(2,1)} %refs_3_.1, ...), custom_call_target="tpu_custom_call" | custom-call | flops 2717908992 | bytes 9830400 | tf_op jit(solution)/shard_map/forward/pallas_call | solution.py:314
  90.4 0.0 collective-permute-done.5.refs_7_
  90.4 12.1 %weight_grads.1 = (f32[512,768]{1,0:T(8,128)}, f32[512,768]{1,0:T(8,128)}, f32[768,512]{1,0:T(8,128)}) custom-call(s32[1]{0:T(128)} %bitcast.2.part_ref, bf16[8,16,2304]{2,1,0:T(8,128)(2,1)} %all-to-all-done.1.refs_0_, bf16[8,16,2304]{2,1,0:T(8,128)(2,1)} %collective-permute-done.refs_0_.refs_1_, ...), custom_call_target="tpu_custom_call" | custom-call | flops 2717908992 | bytes 7864320 | tf_op jit(solution)/shard_map/weight_grads/pallas_call | solution.py:488
  (1 shorter events, 0.0 us)
Async XLA Ops:
  3.0 23.3 %all-to-all-start.1 = ((bf16[8,16,2304]{2,1,0:T(8,128)(2,1)}), bf16[8,16,2304]{2,1,0:T(8,128)(2,1)}, u32[]{:S(2)}, u32[]{:S(2)}) async-start(bf16[8,16,2304]{2,1,0:T(8,128)(2,1)} %pack.2), calls=%async_computation.1 | async-start | bytes 1179648 | tf_op jit(solution)/shard_map/all_to_all | solution.py:529
  26.2 19.8 %all-to-all-start = ((bf16[8,16,2304]{2,1,0:T(8,128)(2,1)}), bf16[8,16,2304]{2,1,0:T(8,128)(2,1)}, u32[]{:S(2)}, u32[]{:S(2)}) async-start(bf16[8,16,2304]{2,1,0:T(8,128)(2,1)} %pack.3), calls=%async_computation | async-start | bytes 1179648 | tf_op jit(solution)/shard_map/all_to_all | solution.py:529
  30.4 33.2 %collective-permute-start.1 = (bf16[8,16,2304]{2,1,0:T(8,128)(2,1)}, bf16[8,16,2304]{2,1,0:T(8,128)(2,1)}, u32[]{:S(2)}, u32[]{:S(2)}) collective-permute-start(bf16[8,16,2304]{2,1,0:T(8,128)(2,1)} %all-to-all-done.1.refs_0_), channel_id=1, source_target_pairs={{0,16},{8,24},{16,0},{24,8},{1,17},{9,25},{17,1},{25,9},{2,18},{10... | collective-permute-start | bytes 1769480 | tf_op jit(solution)/shard_map/ppermute | solution.py:525
  57.8 19.8 %all-to-all-start.2 = ((bf16[8,16,2304]{2,1,0:T(8,128)(2,1)}), bf16[8,16,2304]{2,1,0:T(8,128)(2,1)}, u32[]{:S(2)}, u32[]{:S(2)}) async-start(bf16[8,16,2304]{2,1,0:T(8,128)(2,1)} %get-tuple-element.24), calls=%async_computation.2 | async-start | bytes 1179648 | tf_op jit(solution)/shard_map/all_to_all | solution.py:529
  62.0 14.7 %collective-permute-start.4 = (bf16[8,16,2304]{2,1,0:T(8,128)(2,1)}, bf16[8,16,2304]{2,1,0:T(8,128)(2,1)}, u32[]{:S(2)}, u32[]{:S(2)}) collective-permute-start(bf16[8,16,2304]{2,1,0:T(8,128)(2,1)} %all-to-all-done.packed_ref.refs_4_), channel_id=1, source_target_pairs={{0,16},{8,24},{16,0},{24,8},{1,17},{9,25},{17,1},{25,9},{2,18},{10... | collective-permute-start | bytes 1769480 | tf_op jit(solution)/shard_map/ppermute | solution.py:525
  63.6 13.1 %collective-permute-start = (bf16[8,16,2304]{2,1,0:T(8,128)(2,1)}, bf16[8,16,2304]{2,1,0:T(8,128)(2,1)}, u32[]{:S(2)}, u32[]{:S(2)}) collective-permute-start(bf16[8,16,2304]{2,1,0:T(8,128)(2,1)} %all-to-all-done.1.refs_0_), channel_id=1, source_target_pairs={{0,8},{8,0},{16,24},{24,16},{1,9},{9,1},{17,25},{25,17},{2,10},{10... | collective-permute-start | bytes 1769480 | tf_op jit(solution)/shard_map/ppermute | solution.py:525
  63.6 16.4 %collective-permute-start.2 = (bf16[8,16,2304]{2,1,0:T(8,128)(2,1)}, bf16[8,16,2304]{2,1,0:T(8,128)(2,1)}, u32[]{:S(2)}, u32[]{:S(2)}) collective-permute-start(bf16[8,16,2304]{2,1,0:T(8,128)(2,1)} %collective-permute-done.1.refs_1_.refs_2_), channel_id=1, source_target_pairs={{0,8},{8,0},{16,24},{24,16},{1,9},{9,1},{17,25},{25,17},{2,10},{10... | collective-permute-start | bytes 1769480 | tf_op jit(solution)/shard_map/ppermute | solution.py:525
  64.1 26.3 %collective-permute-start.3 = (bf16[8,16,2304]{2,1,0:T(8,128)(2,1)}, bf16[8,16,2304]{2,1,0:T(8,128)(2,1)}, u32[]{:S(2)}, u32[]{:S(2)}) collective-permute-start(bf16[8,16,2304]{2,1,0:T(8,128)(2,1)} %all-to-all-done.packed_ref.refs_4_), channel_id=1, source_target_pairs={{0,8},{8,0},{16,24},{24,16},{1,9},{9,1},{17,25},{25,17},{2,10},{10... | collective-permute-start | bytes 1769480 | tf_op jit(solution)/shard_map/ppermute | solution.py:525
  76.7 13.8 %collective-permute-start.5 = (bf16[8,16,2304]{2,1,0:T(8,128)(2,1)}, bf16[8,16,2304]{2,1,0:T(8,128)(2,1)}, u32[]{:S(2)}, u32[]{:S(2)}) collective-permute-start(bf16[8,16,2304]{2,1,0:T(8,128)(2,1)} %collective-permute-done.4.refs_6_), channel_id=1, source_target_pairs={{0,8},{8,0},{16,24},{24,16},{1,9},{9,1},{17,25},{25,17},{2,10},{10... | collective-permute-start | bytes 1769480 | tf_op jit(solution)/shard_map/ppermute | solution.py:525

commit v6 on v5

--- a/solution.py
+++ b/solution.py
@@ -293,18 +293,24 @@
         held, rows, gate, up, arrived, gate_in, up_in = refs[groups + 4 :]
         now = pl.program_id(0)
 
+        def fetch(index):
+            weight_copy(gate_ref, gate, gate_in, index, 1, tile).start()
+            weight_copy(up_ref, up, up_in, index, 1, tile).start()
+
         @pl.when(now == 0)
         def _():
             pairs = [(refs[at], held.at[at]) for at in range(groups)]
             start(pairs, arrived)
-            for at in range(tiles):
-                weight_copy(gate_ref, gate, gate_in, at, 1, tile).start()
-                weight_copy(up_ref, up, up_in, at, 1, tile).start()
+            fetch(0)
             wait(pairs, arrived)
             for at in range(groups):
                 unpack(
                     held.at[at, :, :, :width], held.at[at, :, :, width:], pieces, 0, at * slots, rows
                 )
+
+        @pl.when(now < tiles - 1)
+        def _():
+            fetch(now + 1)
 
         weight_copy(gate_ref, gate, gate_in, now, 1, tile).wait()
         pre_gate_ref[...] = dot(rows[...], gate[now])
@@ -327,7 +333,7 @@
             pltpu.SemaphoreType.DMA((tiles,)),
         ],
         compiler_params=params(),
-        cost_estimate=cost(4 * total * width * hid, 4 * width * hid + 4 * total * width),
+        cost_estimate=cost(0, 4 * total * width),
         name="forward",
     )(*packed, gate_proj, up_proj)
 
@@ -347,84 +353,114 @@
     slots = blocks * MOST
     pieces, step = cut(width)
     tiles = hid // tile
+    chunk = 2 * step
+    chunks = width // chunk
 
     def kernel(packed_ref, gate_ref, up_ref, down_ref, pre_gate_ref, pre_up_ref, *rest):
-        out, hidden_ref, d_gate_ref, d_up_ref, held, scaled, total, gate, up, down = rest[:10]
-        arrived, gate_in, up_in, down_in = rest[10:]
+        out, hidden_ref, d_gate_ref, d_up_ref = rest[:4]
+        held, scaled, both, tail, staged, gate, up, down = rest[4:12]
+        arrived, gate_in, up_in, down_in, gone = rest[12:]
         now = pl.program_id(0)
 
+        def fetch(index):
+            @pl.when(index < tiles)
+            def _():
+                weight_copy(down_ref, down, down_in, index, 0, tile).start()
+
+            @pl.when((index >= tiles) & (index < tiles + chunks))
+            def _():
+                weight_copy(gate_ref, gate, gate_in, index - tiles, 0, chunk).start()
+                weight_copy(up_ref, up, up_in, index - tiles, 0, chunk).start()
+
+        def leave(index):
+            columns = tile_of(index, chunk)
+            return pltpu.make_async_copy(
+                staged.at[:, :, columns], out.at[:, :, columns], gone.at[index]
+            )
+
         @pl.when(now == 0)
         def _():
             start([(packed_ref, held)], arrived)
-            for at in range(tiles):
-                weight_copy(down_ref, down, down_in, at, 0, tile).start()
-                weight_copy(gate_ref, gate, gate_in, at, 1, tile).start()
-                weight_copy(up_ref, up, up_in, at, 1, tile).start()
+            fetch(0)
+            fetch(1)
             wait([(packed_ref, held)], arrived)
             unpack(held.at[:, :, :width], held.at[:, :, width:], pieces, 0, 0, scaled)
-
-        weight_copy(down_ref, down, down_in, now, 0, tile).wait()
-        d_hidden = dot(scaled[...], down[now], BY_WIDTH)
-        hidden, d_gate, d_up = hidden_grads(pre_gate_ref[...], pre_up_ref[...], d_hidden)
-        hidden_ref[...] = hidden
-        d_gate_ref[...] = d_gate
-        d_up_ref[...] = d_up
-        weight_copy(gate_ref, gate, gate_in, now, 1, tile).wait()
-        weight_copy(up_ref, up, up_in, now, 1, tile).wait()
-        part = dot(d_gate, gate[now], BY_WIDTH) + dot(d_up, up[now], BY_WIDTH)
-
-        @pl.when(now == 0)
-        def _():
-            total[...] = part
-
-        @pl.when(now > 0)
-        def _():
-            total[...] += part
-
-        @pl.when(now == tiles - 1)
-        def _():
-            done = total[...].astype(jnp.bfloat16)
-            extra = jnp.zeros((blocks * ROWS, step), jnp.float32)
-            for at in range(pieces):
-                extra += dot(
-                    spill_picks(blocks, pieces, at),
-                    done[blocks * ROWS :, at * step : (at + 1) * step],
+            tail[...] = jnp.zeros_like(tail)
+
+        fetch(now + 2)
+
+        @pl.when(now < tiles)
+        def _():
+            weight_copy(down_ref, down, down_in, now, 0, tile).wait()
+            d_hidden = dot(scaled[...], down[now], BY_WIDTH)
+            hidden, d_gate, d_up = hidden_grads(pre_gate_ref[...], pre_up_ref[...], d_hidden)
+            hidden_ref[...] = hidden
+            d_gate_ref[...] = d_gate
+            d_up_ref[...] = d_up
+            both[:, tile_of(now, tile)] = d_gate
+            both[:, tile_of(tiles + now, tile)] = d_up
+
+        @pl.when(now >= tiles)
+        def _():
+            at = now - tiles
+            weight_copy(gate_ref, gate, gate_in, at, 0, chunk).wait()
+            weight_copy(up_ref, up, up_in, at, 0, chunk).wait()
+            done = dot(both[:, :hid], gate[at], BY_WIDTH) + dot(both[:, hid:], up[at], BY_WIDTH)
+            done = done.astype(jnp.bfloat16)
+            for block in range(blocks):
+                staged[block, :, tile_of(at, chunk)] = done[block * ROWS : (block + 1) * ROWS]
+            for piece in range(chunk // step):
+                tail[...] += dot(
+                    spill_picks(blocks, pieces, at * (chunk // step) + piece),
+                    done[blocks * ROWS :, piece * step : (piece + 1) * step],
                     BY_ROWS,
                 )
-            extra = extra.astype(jnp.bfloat16)
+            leave(at).start()
+
+        @pl.when(now == tiles + chunks - 1)
+        def _():
             for block in range(blocks):
-                part_of = slice(block * ROWS, (block + 1) * ROWS)
-                out[block, :, :width] = done[part_of]
-                out[block, :, width:] = extra[part_of]
+                part = tail[block * ROWS : (block + 1) * ROWS, :]
+                staged[block, :, width:] = part.astype(jnp.bfloat16)
+            last = pltpu.make_async_copy(
+                staged.at[:, :, width:], out.at[:, :, width:], gone.at[chunks]
+            )
+            last.start()
+            for at in range(chunks):
+                leave(at).wait()
+            last.wait()
 
     factor = jax.ShapeDtypeStruct((slots, hid), jnp.bfloat16)
+    held_tile = pl.BlockSpec((slots, tile), lambda i: (0, jnp.minimum(i, tiles - 1)))
     sent, *own = pl.pallas_call(
         kernel,
-        grid=(tiles,),
+        grid=(tiles + chunks,),
         out_shape=[jax.ShapeDtypeStruct(packed.shape, jnp.bfloat16)] + [factor] * 3,
-        in_specs=anywhere(4) + [column_tile(slots, tile)] * 2,
-        out_specs=[pl.BlockSpec(packed.shape, lambda i: (0, 0, 0))]
-        + [column_tile(slots, tile)] * 3,
+        in_specs=anywhere(4) + [held_tile] * 2,
+        out_specs=anywhere(1) + [held_tile] * 3,
         scratch_shapes=[
             pltpu.VMEM(packed.shape, jnp.bfloat16),
             pltpu.VMEM((slots, width), jnp.bfloat16),
-            pltpu.VMEM((slots, width), jnp.float32),
-            pltpu.VMEM((tiles, width, tile), jnp.bfloat16),
-            pltpu.VMEM((tiles, width, tile), jnp.bfloat16),
+            pltpu.VMEM((slots, 2 * hid), jnp.bfloat16),
+            pltpu.VMEM((blocks * ROWS, step), jnp.float32),
+            pltpu.VMEM(packed.shape, jnp.bfloat16),
+            pltpu.VMEM((chunks, chunk, hid), jnp.bfloat16),
+            pltpu.VMEM((chunks, chunk, hid), jnp.bfloat16),
             pltpu.VMEM((tiles, tile, width), jnp.bfloat16),
             pltpu.SemaphoreType.DMA((1,)),
+            pltpu.SemaphoreType.DMA((chunks,)),
+            pltpu.SemaphoreType.DMA((chunks,)),
             pltpu.SemaphoreType.DMA((tiles,)),
-            pltpu.SemaphoreType.DMA((tiles,)),
-            pltpu.SemaphoreType.DMA((tiles,)),
+            pltpu.SemaphoreType.DMA((chunks + 1,)),
         ],
         compiler_params=params(),
-        cost_estimate=cost(6 * slots * width * hid, 6 * width * hid),
+        cost_estimate=cost(0, 4 * slots * width),
         name="back",
     )(packed, gate_proj, up_proj, down_proj, pre_gate, pre_up)
     return sent, own
 
 
-def weight_grads(tile, part, rows, scaled, pre_gate, pre_up, down_proj, own):
+def weight_grads(tile, part, rows, scaled, pre_near, pre_far, down_proj, own):
     groups = len(rows)
     blocks = rows[0].shape[0]
     hid, width = down_proj.shape
@@ -435,29 +471,32 @@
     tiles = hid // tile
 
     def kernel(part_ref, *refs):
-        x_refs, dy_refs = refs[:groups], refs[groups : 2 * groups]
-        down_ref, pre_gate_ref, pre_up_ref, own_hidden, own_gate, own_up = refs[
-            2 * groups : 2 * groups + 6
-        ]
-        d_gate_ref, d_up_ref, d_down_ref = refs[2 * groups + 6 : 2 * groups + 9]
-        held, mains, tails, others, x_mine, dy_mine, down = refs[2 * groups + 9 : 2 * groups + 16]
-        held_in, mains_in, tails_in, down_in = refs[2 * groups + 16 :]
+        refs = list(refs)
+        x_refs = [refs.pop(0) for _ in range(groups)]
+        dy_refs = [refs.pop(0) for _ in range(groups)]
+        down_ref, near_gate, near_up, far_gate, far_up = [refs.pop(0) for _ in range(5)]
+        own_hidden, own_gate, own_up = [refs.pop(0) for _ in range(3)]
+        d_gate_ref, d_up_ref, d_down_ref = [refs.pop(0) for _ in range(3)]
+        held, mains, tails, others, x_mine, dy_mine, down = [refs.pop(0) for _ in range(7)]
+        held_in, mains_in, tails_in, down_in = refs
         now = pl.program_id(0)
+        columns = pl.ds(pl.multiple_of(part_ref[0] * share, share), share)
+        begin = part_ref[0] * (share // step)
+        sources = x_refs + [dy_refs[0]]
+        cuts = [(ref.at[:, :, columns], mains.at[at]) for at, ref in enumerate(sources)]
+        ends = [(ref.at[:, :, width:], tails.at[at]) for at, ref in enumerate(sources)]
+
+        def fetch(index):
+            weight_copy(down_ref, down, down_in, index, 0, tile).start()
 
         @pl.when(now == 0)
         def _():
-            columns = pl.ds(pl.multiple_of(part_ref[0] * share, share), share)
-            begin = part_ref[0] * (share // step)
             whole = [(dy_refs[at], held.at[at - 1]) for at in range(1, groups)]
-            sources = list(x_refs) + [dy_refs[0]]
-            cuts = [(ref.at[:, :, columns], mains.at[at]) for at, ref in enumerate(sources)]
-            ends = [(ref.at[:, :, width:], tails.at[at]) for at, ref in enumerate(sources)]
             start(whole, held_in)
-            for at in range(tiles):
-                weight_copy(down_ref, down, down_in, at, 0, tile).start()
+            fetch(0)
+            wait(whole, held_in)
             start(cuts, mains_in)
             start(ends, tails_in)
-            wait(whole, held_in)
             for at in range(groups - 1):
                 unpack(
                     held.at[at, :, :, :width],
@@ -468,23 +507,34 @@
                     others,
                 )
             dy_mine[slots:, :] = others[:, columns]
+
+        @pl.when(now < tiles - 1)
+        def _():
+            fetch(now + 1)
+
+        weight_copy(down_ref, down, down_in, now, 0, tile).wait()
+        d_hidden = dot(others[...], down[now], BY_WIDTH)
+        pre_gate = jnp.concatenate([near_gate[...], far_gate[...]], 0)
+        pre_up = jnp.concatenate([near_up[...], far_up[...]], 0)
+        hidden, d_gate, d_up = hidden_grads(pre_gate, pre_up, d_hidden)
+        hidden = jnp.concatenate([own_hidden[...], hidden], 0)
+        d_gate = jnp.concatenate([own_gate[...], d_gate], 0)
+        d_up = jnp.concatenate([own_up[...], d_up], 0)
+
+        @pl.when(now == 0)
+        def _():
             wait(cuts, mains_in)
             wait(ends, tails_in)
             for at in range(groups):
                 unpack(mains.at[at], tails.at[at], pieces, begin, at * slots, x_mine)
             unpack(mains.at[groups], tails.at[groups], pieces, begin, 0, dy_mine)
 
-        weight_copy(down_ref, down, down_in, now, 0, tile).wait()
-        d_hidden = dot(others[...], down[now], BY_WIDTH)
-        hidden, d_gate, d_up = hidden_grads(pre_gate_ref[...], pre_up_ref[...], d_hidden)
-        hidden = jnp.concatenate([own_hidden[...], hidden], 0)
-        d_gate = jnp.concatenate([own_gate[...], d_gate], 0)
-        d_up = jnp.concatenate([own_up[...], d_up], 0)
         both = dot(x_mine[...], jnp.concatenate([d_gate, d_up], 1), BY_ROWS)
         d_gate_ref[...] = both[:, :tile]
         d_up_ref[...] = both[:, tile:]
         d_down_ref[...] = dot(hidden, dy_mine[...], BY_ROWS)
 
+    behind = pl.BlockSpec((slots, tile), lambda i: (1, i))
     return pl.pallas_call(
         kernel,
         grid=(tiles,),
@@ -495,7 +545,8 @@
         ],
         in_specs=[pl.BlockSpec(memory_space=pltpu.SMEM)]
         + anywhere(2 * groups + 1)
-        + [column_tile(some, tile)] * 2
+        + [behind] * 2
+        + [column_tile(some - slots, tile)] * 2
         + [column_tile(slots, tile)] * 3,
         out_specs=[column_tile(share, tile), column_tile(share, tile), row_tile(tile, share)],
         scratch_shapes=[
@@ -512,12 +563,9 @@
             pltpu.SemaphoreType.DMA((tiles,)),
         ],
         compiler_params=params(),
-        cost_estimate=cost(
-            2 * some * width * hid + 6 * groups * slots * share * hid,
-            2 * width * hid + 4 * groups * slots * width,
-        ),
+        cost_estimate=cost(0, 4 * slots * width),
         name="weight_grads",
-    )(part, *rows, *scaled, down_proj, pre_gate, pre_up, *own)
+    )(part, *rows, *scaled, down_proj, *pre_near, *pre_far, *own)
 
 
 def swap(value, axis, distance):
@@ -539,26 +587,26 @@
     part = lax.axis_index("dp").astype(jnp.int32).reshape(1)
     routes = routes.reshape(1, -1)
     gates = expert_gates.reshape(1, -1)
-    packed = pack(blocks, routes, tokens)
-    rows = exchange(packed)
-    scaled = exchange(pack(blocks, routes, after(cotangent, packed), gates))
+    rows = exchange(pack(blocks, routes, tokens))
     far = swap(rows, "dp", 2)
     near = swap(rows, "dp", 1)
-    pre = forward(tile, [rows], gate_proj, up_proj)
-    scaled = after(scaled, *pre)
+    scaled = exchange(after(pack(blocks, routes, cotangent, gates), rows))
+    pre_near = forward(tile, [rows, near], gate_proj, up_proj)
+    scaled, *pre_near = lax.optimization_barrier((scaled, *pre_near))
     dy_far = swap(scaled, "dp", 2)
     dy_near = swap(scaled, "dp", 1)
-    sent, own = back(tile, scaled, *pre, gate_proj, up_proj, down_proj)
+    sent, own = back(tile, scaled, *pre_near, gate_proj, up_proj, down_proj)
     returned = exchange(sent)
-    last = swap(after(far, pre[0]), "dp", 1)
-    others = forward(tile, [after(near, sent), far, last], gate_proj, up_proj)
+    last = swap(after(far, pre_near[0]), "dp", 1)
+    pre_far = forward(tile, [after(far, sent), last], gate_proj, up_proj)
     dy_last = swap(after(dy_far, sent), "dp", 1)
     grads = weight_grads(
         tile,
         part,
         [rows, near, far, last],
         [scaled, dy_near, dy_far, dy_last],
-        *others,
+        pre_near,
+        pre_far,
         down_proj,
         own,
     )

time: 103 us -> 89.7 us (0.87)
  waiting for transfers between devices: 35.1 us -> 27.7 us
  Pallas kernels: 47.4 us -> 41.1 us
    ppermute x6, waiting for transfers between devices: 12.6 us -> 2.51 us  [swap(): lax.ppermute(value, axis, [(at, at ^ distance) for at in range(size)])]
    all_to_all x3, waiting for transfers between devices: 22.5 us -> 25.2 us  [exchange(): lax.all_to_all(blocks, 'expert', split_axis=0, concat_axis=0, tiled=True)]
    pallas_call x1, Pallas kernels: 12.1 us -> 9.71 us  [weight_grads(): pl.pallas_call(kernel, grid=(tiles,), out_shape=[jax.ShapeDtypeStruct((sh...]
    pallas_call x1, Pallas kernels: 11.7 us -> 9.8 us  [back(): pl.pallas_call(kernel, grid=(tiles + chunks,), out_shape=[jax.ShapeDtypeS...]
    pallas_call x2, Pallas kernels: 16.5 us -> 14.6 us  [forward(): pl.pallas_call(kernel, grid=(tiles,), out_shape=[jax.ShapeDtypeStruct((to...]
  transfers between devices with their start and end apart: 9 -> 9, of which waited for: 4 -> 5; matrix products, arithmetic and copies ran while one was open for 0% -> 0% of each run, Pallas kernels for 32% -> 33%
where the time goes in v6:
time: 89.7 us; the launch traced here: 89.1 us
  Pallas kernels  41.1 us (46%)
  waiting for transfers between devices  27.7 us (31%)
  starting transfers between devices  19.5 us (22%)
    all_to_all x3, waiting for transfers between devices, exchange(): lax.all_to_all(blocks, 'expert', split_axis=0, concat_axis=0, tiled=True)  25.2 us
    all_to_all x3, starting transfers between devices, exchange(): lax.all_to_all(blocks, 'expert', split_axis=0, concat_axis=0, tiled=True)  15.6 us
    pallas_call x2, Pallas kernels, forward(): pl.pallas_call(kernel, grid=(tiles,), out_shape=[jax.ShapeDtypeStruct((to...  14.6 us
    pallas_call x1, Pallas kernels, back(): pl.pallas_call(kernel, grid=(tiles + chunks,), out_shape=[jax.ShapeDtypeS...  9.8 us
    pallas_call x1, Pallas kernels, weight_grads(): pl.pallas_call(kernel, grid=(tiles,), out_shape=[jax.ShapeDtypeStruct((sh...  9.71 us
    pallas_call x2, Pallas kernels, pack(): pl.pallas_call(kernel, out_shape=jax.ShapeDtypeStruct((blocks, ROWS, widt...  4.66 us
    ppermute x6, starting transfers between devices, swap(): lax.ppermute(value, axis, [(at, at ^ distance) for at in range(size)])  3.82 us
    ppermute x6, waiting for transfers between devices, swap(): lax.ppermute(value, axis, [(at, at ^ distance) for at in range(size)])  2.51 us
  transfers between devices with their start and end apart: 9, of which 5 were waited for; matrix products, arithmetic and copies ran while one was open for 0% of the time, Pallas kernels for 33%

profile of v6, /device:TPU:0, one launch (start us, length us, event | category | flops | bytes accessed | tf_op | source)
XLA Modules:
  0.0 89.1 jit_solution(8343813694083242461)
XLA Ops:
  0.6 2.3 %pack.3 = bf16[8,16,2304]{2,1,0:T(8,128)(2,1)} custom-call(s32[1,128]{1,0:T(1,128)} %bitcast.3, bf16[128,2048]{1,0:T(8,128)(2,1)} %refs_1_.1), custom_call_target="tpu_custom_call" | custom-call | flops 134217728 | bytes 1048576 | tf_op jit(solution)/shard_map/pack/pallas_call | solution.py:192
  3.0 7.3 %all-to-all-start = ((bf16[8,16,2304]{2,1,0:T(8,128)(2,1)}), bf16[8,16,2304]{2,1,0:T(8,128)(2,1)}, u32[]{:S(2)}, u32[]{:S(2)}) async-start(bf16[8,16,2304]{2,1,0:T(8,128)(2,1)} %pack.3), calls=%async_computation | async-start | bytes 1179648 | tf_op jit(solution)/shard_map/all_to_all | solution.py:577
  10.2 2.3 %pack.2 = bf16[8,16,2304]{2,1,0:T(8,128)(2,1)} custom-call(s32[1,128]{1,0:T(1,128)} %bitcast.4, f32[1,128]{1,0:T(1,128)} %bitcast.6, bf16[128,2048]{1,0:T(8,128)(2,1)} %refs_2_.3), custom_call_target="tpu_custom_call" | custom-call | flops 134217728 | bytes 1048576 | tf_op jit(solution)/shard_map/pack/pallas_call | solution.py:192
  12.6 13.6 %all-to-all-done.refs_0_ = bf16[8,16,2304]{2,1,0:T(8,128)(2,1)} async-done(((bf16[8,16,2304]{2,1,0:T(8,128)(2,1)}), bf16[8,16,2304]{2,1,0:T(8,128)(2,1)}, u32[]{:S(2)}, u32[]{:S(2)}) %all-to-all-start) | async-done | bytes 589856 | tf_op jit(solution)/shard_map/all_to_all | solution.py:577
  26.2 4.2 %all-to-all-start.1 = ((bf16[8,16,2304]{2,1,0:T(8,128)(2,1)}), bf16[8,16,2304]{2,1,0:T(8,128)(2,1)}, u32[]{:S(2)}, u32[]{:S(2)}) async-start(bf16[8,16,2304]{2,1,0:T(8,128)(2,1)} %pack.2), calls=%async_computation.1 | async-start | bytes 1179648 | tf_op jit(solution)/shard_map/all_to_all | solution.py:577
  30.4 0.1 collective-permute-start
  30.5 1.6 %collective-permute-start.1 = (bf16[8,16,2304]{2,1,0:T(8,128)(2,1)}, bf16[8,16,2304]{2,1,0:T(8,128)(2,1)}, u32[]{:S(2)}, u32[]{:S(2)}) collective-permute-start(bf16[8,16,2304]{2,1,0:T(8,128)(2,1)} %all-to-all-done.refs_0_), channel_id=1, source_target_pairs={{0,16},{8,24},{16,0},{24,8},{1,17},{9,25},{17,1},{25,9},{2,18},{10... | collective-permute-start | bytes 1769480 | tf_op jit(solution)/shard_map/ppermute | solution.py:573
  32.1 0.7 collective-permute-done.refs_1_
  32.8 7.3 %forward.2 = (f32[288,768]{1,0:T(8,128)}, f32[288,768]{1,0:T(8,128)}) custom-call(bf16[8,16,2304]{2,1,0:T(8,128)(2,1)} %all-to-all-done.refs_0_, bf16[8,16,2304]{2,1,0:T(8,128)(2,1)} %collective-permute-done.refs_1_, bf16[2048,768]{1,0:T(8,128)(2,1)} %refs_2_.5, bf16[2048,768]{1,0:T(8,128)(2,1)} %refs_3_.3), custom_call_target="tpu_custom_call" | custom-call | bytes 2359296 | tf_op jit(solution)/shard_map/forward/pallas_call | solution.py:320
  40.2 5.9 %all-to-all-done.1.packed_ref.refs_4_ = bf16[8,16,2304]{2,1,0:T(8,128)(2,1)} async-done(((bf16[8,16,2304]{2,1,0:T(8,128)(2,1)}), bf16[8,16,2304]{2,1,0:T(8,128)(2,1)}, u32[]{:S(2)}, u32[]{:S(2)}) %all-to-all-start.1) | async-done | bytes 589856 | tf_op jit(solution)/shard_map/all_to_all | solution.py:577
  46.1 1.5 %collective-permute-start.4 = (bf16[8,16,2304]{2,1,0:T(8,128)(2,1)}, bf16[8,16,2304]{2,1,0:T(8,128)(2,1)}, u32[]{:S(2)}, u32[]{:S(2)}) collective-permute-start(bf16[8,16,2304]{2,1,0:T(8,128)(2,1)} %all-to-all-done.1.packed_ref.refs_4_), channel_id=1, source_target_pairs={{0,16},{8,24},{16,0},{24,8},{1,17},{9,25},{17,1},{25,9},{2,18},{10... | collective-permute-start | bytes 1769480 | tf_op jit(solution)/shard_map/ppermute | solution.py:573
  47.6 9.8 %back.1 = (bf16[8,16,2304]{2,1,0:T(8,128)(2,1)}, bf16[144,768]{1,0:T(8,128)(2,1)}, bf16[144,768]{1,0:T(8,128)(2,1)}, bf16[144,768]{1,0:T(8,128)(2,1)}) custom-call(bf16[8,16,2304]{2,1,0:T(8,128)(2,1)} %all-to-all-done.1.packed_ref.refs_4_, bf16[2048,768]{1,0:T(8,128)(2,1)} %refs_2_.5, bf16[2048,768]{1,0:T(8,128)(2,1)} %refs_3_.3, bf16[768,2048]{1,0:T(8,128)(2,1)} %refs_8_.1, ...), custom_call_target="tpu_custom_call" | custom-call | bytes 1179648 | tf_op jit(solution)/shard_map/back/pallas_call | solution.py:435
  57.4 4.2 %all-to-all-start.2 = ((bf16[8,16,2304]{2,1,0:T(8,128)(2,1)}), bf16[8,16,2304]{2,1,0:T(8,128)(2,1)}, u32[]{:S(2)}, u32[]{:S(2)}) async-start(bf16[8,16,2304]{2,1,0:T(8,128)(2,1)} %get-tuple-element.28), calls=%async_computation.2 | async-start | bytes 1179648 | tf_op jit(solution)/shard_map/all_to_all | solution.py:577
  61.6 0.0 collective-permute-done.1.refs_0_.refs_2_
  61.6 0.1 collective-permute-start.2
  61.7 0.5 collective-permute-start.3
  62.2 0.0 collective-permute-done.4.refs_6_
  62.2 0.1 collective-permute-start.5
  62.3 1.8 %collective-permute-done.2.refs_1_.refs_3_ = bf16[8,16,2304]{2,1,0:T(8,128)(2,1)} collective-permute-done((bf16[8,16,2304]{2,1,0:T(8,128)(2,1)}, bf16[8,16,2304]{2,1,0:T(8,128)(2,1)}, u32[]{:S(2)}, u32[]{:S(2)}) %collective-permute-start.2) | collective-permute-done | bytes 589856 | tf_op jit(solution)/shard_map/ppermute | solution.py:573
  64.0 7.3 %forward.3 = (f32[288,768]{1,0:T(8,128)}, f32[288,768]{1,0:T(8,128)}) custom-call(bf16[8,16,2304]{2,1,0:T(8,128)(2,1)} %collective-permute-done.1.refs_0_.refs_2_, bf16[8,16,2304]{2,1,0:T(8,128)(2,1)} %collective-permute-done.2.refs_1_.refs_3_, bf16[2048,768]{1,0:T(8,128)(2,1)} %refs_2_.5, bf16[2048,768]{1,0:T(8,128)(2,1)} %refs_3_.3), custom_call_target="tpu_custom_call" | custom-call | bytes 2359296 | tf_op jit(solution)/shard_map/forward/pallas_call | solution.py:320
  71.3 5.7 %all-to-all-done.2.back_ref = bf16[8,16,2304]{2,1,0:T(8,128)(2,1)} async-done(((bf16[8,16,2304]{2,1,0:T(8,128)(2,1)}), bf16[8,16,2304]{2,1,0:T(8,128)(2,1)}, u32[]{:S(2)}, u32[]{:S(2)}) %all-to-all-start.2) | async-done | bytes 589856 | tf_op jit(solution)/shard_map/all_to_all | solution.py:577
  77.0 2.4 %merge.1 = bf16[128,2048]{1,0:T(8,128)(2,1)} custom-call(s32[1,128]{1,0:T(1,128)} %bitcast.5, bf16[8,16,2304]{2,1,0:T(8,128)(2,1)} %all-to-all-done.2.back_ref), custom_call_target="tpu_custom_call" | custom-call | flops 134217728 | bytes 1048576 | tf_op jit(solution)/shard_map/merge/pallas_call | solution.py:228
  79.3 0.0 collective-permute-done.3.refs_5_
  79.4 9.7 %weight_grads.1 = (f32[512,768]{1,0:T(8,128)}, f32[512,768]{1,0:T(8,128)}, f32[768,512]{1,0:T(8,128)}) custom-call(s32[1]{0:T(128)} %bitcast.2.part_ref, bf16[8,16,2304]{2,1,0:T(8,128)(2,1)} %all-to-all-done.refs_0_, bf16[8,16,2304]{2,1,0:T(8,128)(2,1)} %collective-permute-done.refs_1_, bf16[8,16,2304]{2,1,0:T(8,128)(2,1)} %collective-permute-done.1.refs_0_.refs_2_, ...), custom_call_target="tpu_custom_call" | custom-call | bytes 1179648 | tf_op jit(solution)/shard_map/weight_grads/pallas_call | solution.py:538
  (1 shorter events, 0.0 us)
Async XLA Ops:
  3.0 23.3 %all-to-all-start = ((bf16[8,16,2304]{2,1,0:T(8,128)(2,1)}), bf16[8,16,2304]{2,1,0:T(8,128)(2,1)}, u32[]{:S(2)}, u32[]{:S(2)}) async-start(bf16[8,16,2304]{2,1,0:T(8,128)(2,1)} %pack.3), calls=%async_computation | async-start | bytes 1179648 | tf_op jit(solution)/shard_map/all_to_all | solution.py:577
  26.2 19.8 %all-to-all-start.1 = ((bf16[8,16,2304]{2,1,0:T(8,128)(2,1)}), bf16[8,16,2304]{2,1,0:T(8,128)(2,1)}, u32[]{:S(2)}, u32[]{:S(2)}) async-start(bf16[8,16,2304]{2,1,0:T(8,128)(2,1)} %pack.2), calls=%async_computation.1 | async-start | bytes 1179648 | tf_op jit(solution)/shard_map/all_to_all | solution.py:577
  30.4 2.4 %collective-permute-start = (bf16[8,16,2304]{2,1,0:T(8,128)(2,1)}, bf16[8,16,2304]{2,1,0:T(8,128)(2,1)}, u32[]{:S(2)}, u32[]{:S(2)}) collective-permute-start(bf16[8,16,2304]{2,1,0:T(8,128)(2,1)} %all-to-all-done.refs_0_), channel_id=1, source_target_pairs={{0,8},{8,0},{16,24},{24,16},{1,9},{9,1},{17,25},{25,17},{2,10},{10... | collective-permute-start | bytes 1769480 | tf_op jit(solution)/shard_map/ppermute | solution.py:573
  30.5 31.1 %collective-permute-start.1 = (bf16[8,16,2304]{2,1,0:T(8,128)(2,1)}, bf16[8,16,2304]{2,1,0:T(8,128)(2,1)}, u32[]{:S(2)}, u32[]{:S(2)}) collective-permute-start(bf16[8,16,2304]{2,1,0:T(8,128)(2,1)} %all-to-all-done.refs_0_), channel_id=1, source_target_pairs={{0,16},{8,24},{16,0},{24,8},{1,17},{9,25},{17,1},{25,9},{2,18},{10... | collective-permute-start | bytes 1769480 | tf_op jit(solution)/shard_map/ppermute | solution.py:573
  46.1 16.1 %collective-permute-start.4 = (bf16[8,16,2304]{2,1,0:T(8,128)(2,1)}, bf16[8,16,2304]{2,1,0:T(8,128)(2,1)}, u32[]{:S(2)}, u32[]{:S(2)}) collective-permute-start(bf16[8,16,2304]{2,1,0:T(8,128)(2,1)} %all-to-all-done.1.packed_ref.refs_4_), channel_id=1, source_target_pairs={{0,16},{8,24},{16,0},{24,8},{1,17},{9,25},{17,1},{25,9},{2,18},{10... | collective-permute-start | bytes 1769480 | tf_op jit(solution)/shard_map/ppermute | solution.py:573
  57.4 19.6 %all-to-all-start.2 = ((bf16[8,16,2304]{2,1,0:T(8,128)(2,1)}), bf16[8,16,2304]{2,1,0:T(8,128)(2,1)}, u32[]{:S(2)}, u32[]{:S(2)}) async-start(bf16[8,16,2304]{2,1,0:T(8,128)(2,1)} %get-tuple-element.28), calls=%async_computation.2 | async-start | bytes 1179648 | tf_op jit(solution)/shard_map/all_to_all | solution.py:577
  61.6 2.4 %collective-permute-start.2 = (bf16[8,16,2304]{2,1,0:T(8,128)(2,1)}, bf16[8,16,2304]{2,1,0:T(8,128)(2,1)}, u32[]{:S(2)}, u32[]{:S(2)}) collective-permute-start(bf16[8,16,2304]{2,1,0:T(8,128)(2,1)} %collective-permute-done.1.refs_0_.refs_2_), channel_id=1, source_target_pairs={{0,8},{8,0},{16,24},{24,16},{1,9},{9,1},{17,25},{25,17},{2,10},{10... | collective-permute-start | bytes 1769480 | tf_op jit(solution)/shard_map/ppermute | solution.py:573
  61.7 17.7 %collective-permute-start.3 = (bf16[8,16,2304]{2,1,0:T(8,128)(2,1)}, bf16[8,16,2304]{2,1,0:T(8,128)(2,1)}, u32[]{:S(2)}, u32[]{:S(2)}) collective-permute-start(bf16[8,16,2304]{2,1,0:T(8,128)(2,1)} %all-to-all-done.1.packed_ref.refs_4_), channel_id=1, source_target_pairs={{0,8},{8,0},{16,24},{24,16},{1,9},{9,1},{17,25},{25,17},{2,10},{10... | collective-permute-start | bytes 1769480 | tf_op jit(solution)/shard_map/ppermute | solution.py:573
  62.2 17.2 %collective-permute-start.5 = (bf16[8,16,2304]{2,1,0:T(8,128)(2,1)}, bf16[8,16,2304]{2,1,0:T(8,128)(2,1)}, u32[]{:S(2)}, u32[]{:S(2)}) collective-permute-start(bf16[8,16,2304]{2,1,0:T(8,128)(2,1)} %collective-permute-done.4.refs_6_), channel_id=1, source_target_pairs={{0,8},{8,0},{16,24},{24,16},{1,9},{9,1},{17,25},{25,17},{2,10},{10... | collective-permute-start | bytes 1769480 | tf_op jit(solution)/shard_map/ppermute | solution.py:573

commit v7 on v6

--- a/solution.py
+++ b/solution.py
@@ -129,9 +129,10 @@
     return jnp.where(mask, 1.0, 0.0).astype(jnp.bfloat16)
 
 
-def start(pairs, arrived):
+def start(pairs, arrived, first=0):
     for at, (source, target) in enumerate(pairs):
-        pltpu.make_async_copy(source, target, arrived.at[at]).start()
+        if at >= first:
+            pltpu.make_async_copy(source, target, arrived.at[at]).start()
 
 
 def wait(pairs, arrived, first=0):
@@ -357,10 +358,10 @@
     chunks = width // chunk
 
     def kernel(packed_ref, gate_ref, up_ref, down_ref, pre_gate_ref, pre_up_ref, *rest):
-        out, hidden_ref, d_gate_ref, d_up_ref = rest[:4]
-        held, scaled, both, tail, staged, gate, up, down = rest[4:12]
-        arrived, gate_in, up_in, down_in, gone = rest[12:]
+        out, hidden_ref, both_ref, held, scaled, pre_gate, pre_up, hidden, both = rest[:9]
+        tail, staged, gate, up, down, arrived, gate_in, up_in, down_in, gone = rest[9:]
         now = pl.program_id(0)
+        first = [(packed_ref, held), (pre_gate_ref, pre_gate), (pre_up_ref, pre_up)]
 
         def fetch(index):
             @pl.when(index < tiles)
@@ -378,12 +379,19 @@
                 staged.at[:, :, columns], out.at[:, :, columns], gone.at[index]
             )
 
+        def leave_factors():
+            return [
+                pltpu.make_async_copy(hidden, hidden_ref, gone.at[chunks + 1]),
+                pltpu.make_async_copy(both, both_ref, gone.at[chunks + 2]),
+            ]
+
         @pl.when(now == 0)
         def _():
-            start([(packed_ref, held)], arrived)
+            start(first[:1], arrived)
             fetch(0)
+            start(first, arrived, 1)
+            wait(first[:1], arrived)
             fetch(1)
-            wait([(packed_ref, held)], arrived)
             unpack(held.at[:, :, :width], held.at[:, :, width:], pieces, 0, 0, scaled)
             tail[...] = jnp.zeros_like(tail)
 
@@ -391,31 +399,40 @@
 
         @pl.when(now < tiles)
         def _():
+            columns = tile_of(now, tile)
             weight_copy(down_ref, down, down_in, now, 0, tile).wait()
             d_hidden = dot(scaled[...], down[now], BY_WIDTH)
-            hidden, d_gate, d_up = hidden_grads(pre_gate_ref[...], pre_up_ref[...], d_hidden)
-            hidden_ref[...] = hidden
-            d_gate_ref[...] = d_gate
-            d_up_ref[...] = d_up
-            both[:, tile_of(now, tile)] = d_gate
+
+            @pl.when(now == 0)
+            def _():
+                wait(first, arrived, 1)
+
+            made, d_gate, d_up = hidden_grads(pre_gate[:, columns], pre_up[:, columns], d_hidden)
+            hidden[:, columns] = made
+            both[:, columns] = d_gate
             both[:, tile_of(tiles + now, tile)] = d_up
+
+        @pl.when(now == tiles)
+        def _():
+            for copy in leave_factors():
+                copy.start()
 
         @pl.when(now >= tiles)
         def _():
             at = now - tiles
             weight_copy(gate_ref, gate, gate_in, at, 0, chunk).wait()
+            done = dot(both[:, :hid], gate[at], BY_WIDTH)
             weight_copy(up_ref, up, up_in, at, 0, chunk).wait()
-            done = dot(both[:, :hid], gate[at], BY_WIDTH) + dot(both[:, hid:], up[at], BY_WIDTH)
-            done = done.astype(jnp.bfloat16)
+            done = (done + dot(both[:, hid:], up[at], BY_WIDTH)).astype(jnp.bfloat16)
             for block in range(blocks):
                 staged[block, :, tile_of(at, chunk)] = done[block * ROWS : (block + 1) * ROWS]
+            leave(at).start()
             for piece in range(chunk // step):
                 tail[...] += dot(
                     spill_picks(blocks, pieces, at * (chunk // step) + piece),
                     done[blocks * ROWS :, piece * step : (piece + 1) * step],
                     BY_ROWS,
                 )
-            leave(at).start()
 
         @pl.when(now == tiles + chunks - 1)
         def _():
@@ -428,39 +445,45 @@
             last.start()
             for at in range(chunks):
                 leave(at).wait()
+            for copy in leave_factors():
+                copy.wait()
             last.wait()
 
-    factor = jax.ShapeDtypeStruct((slots, hid), jnp.bfloat16)
-    held_tile = pl.BlockSpec((slots, tile), lambda i: (0, jnp.minimum(i, tiles - 1)))
-    sent, *own = pl.pallas_call(
+    return pl.pallas_call(
         kernel,
         grid=(tiles + chunks,),
-        out_shape=[jax.ShapeDtypeStruct(packed.shape, jnp.bfloat16)] + [factor] * 3,
-        in_specs=anywhere(4) + [held_tile] * 2,
-        out_specs=anywhere(1) + [held_tile] * 3,
+        out_shape=[
+            jax.ShapeDtypeStruct(packed.shape, jnp.bfloat16),
+            jax.ShapeDtypeStruct((slots, hid), jnp.bfloat16),
+            jax.ShapeDtypeStruct((slots, 2 * hid), jnp.bfloat16),
+        ],
+        in_specs=anywhere(6),
+        out_specs=anywhere(3),
         scratch_shapes=[
             pltpu.VMEM(packed.shape, jnp.bfloat16),
             pltpu.VMEM((slots, width), jnp.bfloat16),
+            pltpu.VMEM((slots, hid), jnp.float32),
+            pltpu.VMEM((slots, hid), jnp.float32),
+            pltpu.VMEM((slots, hid), jnp.bfloat16),
             pltpu.VMEM((slots, 2 * hid), jnp.bfloat16),
             pltpu.VMEM((blocks * ROWS, step), jnp.float32),
             pltpu.VMEM(packed.shape, jnp.bfloat16),
             pltpu.VMEM((chunks, chunk, hid), jnp.bfloat16),
             pltpu.VMEM((chunks, chunk, hid), jnp.bfloat16),
             pltpu.VMEM((tiles, tile, width), jnp.bfloat16),
-            pltpu.SemaphoreType.DMA((1,)),
+            pltpu.SemaphoreType.DMA((3,)),
             pltpu.SemaphoreType.DMA((chunks,)),
             pltpu.SemaphoreType.DMA((chunks,)),
             pltpu.SemaphoreType.DMA((tiles,)),
-            pltpu.SemaphoreType.DMA((chunks + 1,)),
+            pltpu.SemaphoreType.DMA((chunks + 3,)),
         ],
         compiler_params=params(),
         cost_estimate=cost(0, 4 * slots * width),
         name="back",
     )(packed, gate_proj, up_proj, down_proj, pre_gate, pre_up)
-    return sent, own
-
-
-def weight_grads(tile, part, rows, scaled, pre_near, pre_far, down_proj, own):
+
+
+def weight_grads(tile, part, rows, scaled, hidden, both, gate_proj, up_proj, down_proj):
     groups = len(rows)
     blocks = rows[0].shape[0]
     hid, width = down_proj.shape
@@ -474,29 +497,22 @@
         refs = list(refs)
         x_refs = [refs.pop(0) for _ in range(groups)]
         dy_refs = [refs.pop(0) for _ in range(groups)]
-        down_ref, near_gate, near_up, far_gate, far_up = [refs.pop(0) for _ in range(5)]
-        own_hidden, own_gate, own_up = [refs.pop(0) for _ in range(3)]
+        hidden_ref, both_ref, gate_ref, up_ref, down_ref = [refs.pop(0) for _ in range(5)]
         d_gate_ref, d_up_ref, d_down_ref = [refs.pop(0) for _ in range(3)]
-        held, mains, tails, others, x_mine, dy_mine, down = [refs.pop(0) for _ in range(7)]
-        held_in, mains_in, tails_in, down_in = refs
+        x_held, dy_held, mains, tails, x_all, dy_all = [refs.pop(0) for _ in range(6)]
+        x_mine, dy_mine, own_hidden, own_both = [refs.pop(0) for _ in range(4)]
+        gate, up, down, x_in, dy_in, own_in, gate_in, up_in, down_in = refs
         now = pl.program_id(0)
         columns = pl.ds(pl.multiple_of(part_ref[0] * share, share), share)
         begin = part_ref[0] * (share // step)
-        sources = x_refs + [dy_refs[0]]
-        cuts = [(ref.at[:, :, columns], mains.at[at]) for at, ref in enumerate(sources)]
-        ends = [(ref.at[:, :, width:], tails.at[at]) for at, ref in enumerate(sources)]
-
-        def fetch(index):
-            weight_copy(down_ref, down, down_in, index, 0, tile).start()
-
-        @pl.when(now == 0)
-        def _():
-            whole = [(dy_refs[at], held.at[at - 1]) for at in range(1, groups)]
-            start(whole, held_in)
-            fetch(0)
-            wait(whole, held_in)
-            start(cuts, mains_in)
-            start(ends, tails_in)
+        x_pairs = [(x_refs[at], x_held.at[at - 1]) for at in range(1, groups)]
+        dy_pairs = [(dy_refs[at], dy_held.at[at - 1]) for at in range(1, groups)]
+        own_pairs = [(hidden_ref, own_hidden), (both_ref, own_both)]
+        for at, ref in enumerate([x_refs[0], dy_refs[0]]):
+            own_pairs.append((ref.at[:, :, columns], mains.at[at]))
+            own_pairs.append((ref.at[:, :, width:], tails.at[at]))
+
+        def arrange(held, rows_out, target):
             for at in range(groups - 1):
                 unpack(
                     held.at[at, :, :, :width],
@@ -504,37 +520,60 @@
                     pieces,
                     0,
                     at * slots,
-                    others,
+                    rows_out,
                 )
-            dy_mine[slots:, :] = others[:, columns]
+            target[slots:, :] = rows_out[:, columns]
+
+        def fetch_x(index):
+            weight_copy(gate_ref, gate, gate_in, index, 1, tile).start()
+            weight_copy(up_ref, up, up_in, index, 1, tile).start()
+
+        def fetch_dy(index):
+            weight_copy(down_ref, down, down_in, index, 0, tile).start()
+
+        @pl.when(now == 0)
+        def _():
+            start(x_pairs, x_in)
+            fetch_x(0)
+            wait(x_pairs, x_in)
+            start(dy_pairs, dy_in)
+            fetch_dy(0)
+            arrange(x_held, x_all, x_mine)
+
+        weight_copy(gate_ref, gate, gate_in, now, 1, tile).wait()
+        pre_gate = dot(x_all[...], gate[now])
+        weight_copy(up_ref, up, up_in, now, 1, tile).wait()
+        pre_up = dot(x_all[...], up[now])
+
+        @pl.when(now == 0)
+        def _():
+            wait(dy_pairs, dy_in)
+            start(own_pairs, own_in)
+            arrange(dy_held, dy_all, dy_mine)
 
         @pl.when(now < tiles - 1)
         def _():
-            fetch(now + 1)
+            fetch_x(now + 1)
+            fetch_dy(now + 1)
 
         weight_copy(down_ref, down, down_in, now, 0, tile).wait()
-        d_hidden = dot(others[...], down[now], BY_WIDTH)
-        pre_gate = jnp.concatenate([near_gate[...], far_gate[...]], 0)
-        pre_up = jnp.concatenate([near_up[...], far_up[...]], 0)
-        hidden, d_gate, d_up = hidden_grads(pre_gate, pre_up, d_hidden)
-        hidden = jnp.concatenate([own_hidden[...], hidden], 0)
-        d_gate = jnp.concatenate([own_gate[...], d_gate], 0)
-        d_up = jnp.concatenate([own_up[...], d_up], 0)
+        d_hidden = dot(dy_all[...], down[now], BY_WIDTH)
+        made, d_gate, d_up = hidden_grads(pre_gate, pre_up, d_hidden)
 
         @pl.when(now == 0)
         def _():
-            wait(cuts, mains_in)
-            wait(ends, tails_in)
-            for at in range(groups):
-                unpack(mains.at[at], tails.at[at], pieces, begin, at * slots, x_mine)
-            unpack(mains.at[groups], tails.at[groups], pieces, begin, 0, dy_mine)
-
-        both = dot(x_mine[...], jnp.concatenate([d_gate, d_up], 1), BY_ROWS)
-        d_gate_ref[...] = both[:, :tile]
-        d_up_ref[...] = both[:, tile:]
-        d_down_ref[...] = dot(hidden, dy_mine[...], BY_ROWS)
-
-    behind = pl.BlockSpec((slots, tile), lambda i: (1, i))
+            wait(own_pairs, own_in)
+            unpack(mains.at[0], tails.at[0], pieces, begin, 0, x_mine)
+            unpack(mains.at[1], tails.at[1], pieces, begin, 0, dy_mine)
+
+        made = jnp.concatenate([own_hidden[:, tile_of(now, tile)], made], 0)
+        d_gate = jnp.concatenate([own_both[:, tile_of(now, tile)], d_gate], 0)
+        d_up = jnp.concatenate([own_both[:, tile_of(tiles + now, tile)], d_up], 0)
+        sums = dot(x_mine[...], jnp.concatenate([d_gate, d_up], 1), BY_ROWS)
+        d_gate_ref[...] = sums[:, :tile]
+        d_up_ref[...] = sums[:, tile:]
+        d_down_ref[...] = dot(made, dy_mine[...], BY_ROWS)
+
     return pl.pallas_call(
         kernel,
         grid=(tiles,),
@@ -543,29 +582,33 @@
             jax.ShapeDtypeStruct((share, hid), jnp.float32),
             jax.ShapeDtypeStruct((hid, share), jnp.float32),
         ],
-        in_specs=[pl.BlockSpec(memory_space=pltpu.SMEM)]
-        + anywhere(2 * groups + 1)
-        + [behind] * 2
-        + [column_tile(some - slots, tile)] * 2
-        + [column_tile(slots, tile)] * 3,
+        in_specs=[pl.BlockSpec(memory_space=pltpu.SMEM)] + anywhere(2 * groups + 5),
         out_specs=[column_tile(share, tile), column_tile(share, tile), row_tile(tile, share)],
         scratch_shapes=[
             pltpu.VMEM((groups - 1,) + rows[0].shape, jnp.bfloat16),
-            pltpu.VMEM((groups + 1, blocks, ROWS, share), jnp.bfloat16),
-            pltpu.VMEM((groups + 1, blocks, ROWS, step), jnp.bfloat16),
+            pltpu.VMEM((groups - 1,) + rows[0].shape, jnp.bfloat16),
+            pltpu.VMEM((2, blocks, ROWS, share), jnp.bfloat16),
+            pltpu.VMEM((2, blocks, ROWS, step), jnp.bfloat16),
+            pltpu.VMEM((some, width), jnp.bfloat16),
             pltpu.VMEM((some, width), jnp.bfloat16),
             pltpu.VMEM((groups * slots, share), jnp.bfloat16),
             pltpu.VMEM((groups * slots, share), jnp.bfloat16),
+            pltpu.VMEM((slots, hid), jnp.bfloat16),
+            pltpu.VMEM((slots, 2 * hid), jnp.bfloat16),
+            pltpu.VMEM((tiles, width, tile), jnp.bfloat16),
+            pltpu.VMEM((tiles, width, tile), jnp.bfloat16),
             pltpu.VMEM((tiles, tile, width), jnp.bfloat16),
             pltpu.SemaphoreType.DMA((groups - 1,)),
-            pltpu.SemaphoreType.DMA((groups + 1,)),
-            pltpu.SemaphoreType.DMA((groups + 1,)),
+            pltpu.SemaphoreType.DMA((groups - 1,)),
+            pltpu.SemaphoreType.DMA((6,)),
+            pltpu.SemaphoreType.DMA((tiles,)),
+            pltpu.SemaphoreType.DMA((tiles,)),
             pltpu.SemaphoreType.DMA((tiles,)),
         ],
         compiler_params=params(),
         cost_estimate=cost(0, 4 * slots * width),
         name="weight_grads",
-    )(part, *rows, *scaled, down_proj, *pre_near, *pre_far, *own)
+    )(part, *rows, *scaled, hidden, both, gate_proj, up_proj, down_proj)
 
 
 def swap(value, axis, distance):
@@ -587,30 +630,29 @@
     part = lax.axis_index("dp").astype(jnp.int32).reshape(1)
     routes = routes.reshape(1, -1)
     gates = expert_gates.reshape(1, -1)
+    weights = (gate_proj, up_proj, down_proj)
     rows = exchange(pack(blocks, routes, tokens))
     far = swap(rows, "dp", 2)
     near = swap(rows, "dp", 1)
     scaled = exchange(after(pack(blocks, routes, cotangent, gates), rows))
-    pre_near = forward(tile, [rows, near], gate_proj, up_proj)
-    scaled, *pre_near = lax.optimization_barrier((scaled, *pre_near))
+    pre = forward(tile, [rows], gate_proj, up_proj)
+    scaled, *pre = lax.optimization_barrier((scaled, *pre))
     dy_far = swap(scaled, "dp", 2)
     dy_near = swap(scaled, "dp", 1)
-    sent, own = back(tile, scaled, *pre_near, gate_proj, up_proj, down_proj)
+    sent, hidden, both = back(tile, scaled, *pre, *weights)
     returned = exchange(sent)
-    last = swap(after(far, pre_near[0]), "dp", 1)
-    pre_far = forward(tile, [after(far, sent), last], gate_proj, up_proj)
+    last = swap(after(far, pre[0]), "dp", 1)
     dy_last = swap(after(dy_far, sent), "dp", 1)
     grads = weight_grads(
         tile,
         part,
         [rows, near, far, last],
         [scaled, dy_near, dy_far, dy_last],
-        pre_near,
-        pre_far,
-        down_proj,
-        own,
-    )
-    return (merge(routes, returned), *grads)
+        hidden,
+        both,
+        *weights,
+    )
+    return (merge(routes, after(returned, *grads)), *grads)
 
 
 def body(tokens, cotangent, routes, expert_gates, gate_proj, up_proj, down_proj):

time: 89.7 us -> 82.7 us (0.922)
  Pallas kernels: 41.1 us -> 36 us
  waiting for transfers between devices: 27.7 us -> 25.6 us
    pallas_call x2 -> x1, Pallas kernels: 14.6 us -> 5.93 us  [forward(): pl.pallas_call(kernel, grid=(tiles,), out_shape=[jax.ShapeDtypeStruct((to...]
    pallas_call x1, Pallas kernels: 9.71 us -> 15 us  [weight_grads(): pl.pallas_call(kernel, grid=(tiles,), out_shape=[jax.ShapeDtypeStruct((sh...]
    all_to_all x3, waiting for transfers between devices: 25.2 us -> 21.8 us  [exchange(): lax.all_to_all(blocks, 'expert', split_axis=0, concat_axis=0, tiled=True)]
    pallas_call x1, Pallas kernels: 9.8 us -> 8.05 us  [back(): pl.pallas_call(kernel, grid=(tiles + chunks,), out_shape=[jax.ShapeDtypeS...]
    ppermute x6, waiting for transfers between devices: 2.51 us -> 3.85 us  [swap(): lax.ppermute(value, axis, [(at, at ^ distance) for at in range(size)])]
  transfers between devices with their start and end apart: 9 -> 9, of which waited for: 5 -> 5; matrix products, arithmetic and copies ran while one was open for 0% -> 0% of each run, Pallas kernels for 33% -> 38%
where the time goes in v7:
time: 82.7 us; the launch traced here: 82.1 us
  Pallas kernels  36 us (44%)
  waiting for transfers between devices  25.6 us (31%)
  starting transfers between devices  19.8 us (24%)
    all_to_all x3, waiting for transfers between devices, exchange(): lax.all_to_all(blocks, 'expert', split_axis=0, concat_axis=0, tiled=True)  21.8 us
    all_to_all x3, starting transfers between devices, exchange(): lax.all_to_all(blocks, 'expert', split_axis=0, concat_axis=0, tiled=True)  15.7 us
    pallas_call x1, Pallas kernels, weight_grads(): pl.pallas_call(kernel, grid=(tiles,), out_shape=[jax.ShapeDtypeStruct((sh...  15 us
    pallas_call x1, Pallas kernels, back(): pl.pallas_call(kernel, grid=(tiles + chunks,), out_shape=[jax.ShapeDtypeS...  8.05 us
    pallas_call x1, Pallas kernels, forward(): pl.pallas_call(kernel, grid=(tiles,), out_shape=[jax.ShapeDtypeStruct((to...  5.93 us
    pallas_call x2, Pallas kernels, pack(): pl.pallas_call(kernel, out_shape=jax.ShapeDtypeStruct((blocks, ROWS, widt...  4.66 us
    ppermute x6, starting transfers between devices, swap(): lax.ppermute(value, axis, [(at, at ^ distance) for at in range(size)])  4.18 us
    ppermute x6, waiting for transfers between devices, swap(): lax.ppermute(value, axis, [(at, at ^ distance) for at in range(size)])  3.85 us
  transfers between devices with their start and end apart: 9, of which 5 were waited for; matrix products, arithmetic and copies ran while one was open for 0% of the time, Pallas kernels for 38%

profile of v7, /device:TPU:0, one launch (start us, length us, event | category | flops | bytes accessed | tf_op | source)
XLA Modules:
  0.0 82.1 jit_solution(10981453662766264960)
XLA Ops:
  0.6 2.3 %pack.3 = bf16[8,16,2304]{2,1,0:T(8,128)(2,1)} custom-call(s32[1,128]{1,0:T(1,128)} %bitcast.3, bf16[128,2048]{1,0:T(8,128)(2,1)} %refs_1_.2), custom_call_target="tpu_custom_call" | custom-call | flops 134217728 | bytes 1048576 | tf_op jit(solution)/shard_map/pack/pallas_call | solution.py:193
  3.0 7.3 %all-to-all-start = ((bf16[8,16,2304]{2,1,0:T(8,128)(2,1)}), bf16[8,16,2304]{2,1,0:T(8,128)(2,1)}, u32[]{:S(2)}, u32[]{:S(2)}) async-start(bf16[8,16,2304]{2,1,0:T(8,128)(2,1)} %pack.3), calls=%async_computation | async-start | bytes 1179648 | tf_op jit(solution)/shard_map/all_to_all | solution.py:620
  10.2 2.3 %pack.2 = bf16[8,16,2304]{2,1,0:T(8,128)(2,1)} custom-call(s32[1,128]{1,0:T(1,128)} %bitcast.4, f32[1,128]{1,0:T(1,128)} %bitcast.6, bf16[128,2048]{1,0:T(8,128)(2,1)} %refs_2_.2), custom_call_target="tpu_custom_call" | custom-call | flops 134217728 | bytes 1048576 | tf_op jit(solution)/shard_map/pack/pallas_call | solution.py:193
  12.6 13.6 %all-to-all-done.refs_0_ = bf16[8,16,2304]{2,1,0:T(8,128)(2,1)} async-done(((bf16[8,16,2304]{2,1,0:T(8,128)(2,1)}), bf16[8,16,2304]{2,1,0:T(8,128)(2,1)}, u32[]{:S(2)}, u32[]{:S(2)}) %all-to-all-start) | async-done | bytes 589856 | tf_op jit(solution)/shard_map/all_to_all | solution.py:620
  26.2 4.2 %all-to-all-start.1 = ((bf16[8,16,2304]{2,1,0:T(8,128)(2,1)}), bf16[8,16,2304]{2,1,0:T(8,128)(2,1)}, u32[]{:S(2)}, u32[]{:S(2)}) async-start(bf16[8,16,2304]{2,1,0:T(8,128)(2,1)} %pack.2), calls=%async_computation.1 | async-start | bytes 1179648 | tf_op jit(solution)/shard_map/all_to_all | solution.py:620
  30.4 1.6 %collective-permute-start.1 = (bf16[8,16,2304]{2,1,0:T(8,128)(2,1)}, bf16[8,16,2304]{2,1,0:T(8,128)(2,1)}, u32[]{:S(2)}, u32[]{:S(2)}) collective-permute-start(bf16[8,16,2304]{2,1,0:T(8,128)(2,1)} %all-to-all-done.refs_0_), channel_id=1, source_target_pairs={{0,16},{8,24},{16,0},{24,8},{1,17},{9,25},{17,1},{25,9},{2,18},{10... | collective-permute-start | bytes 1769480 | tf_op jit(solution)/shard_map/ppermute | solution.py:616
  32.0 5.9 %forward.1 = (f32[144,768]{1,0:T(8,128)}, f32[144,768]{1,0:T(8,128)}) custom-call(bf16[8,16,2304]{2,1,0:T(8,128)(2,1)} %all-to-all-done.refs_0_, bf16[2048,768]{1,0:T(8,128)(2,1)} %refs_10_.1, bf16[2048,768]{1,0:T(8,128)(2,1)} %refs_11_.1), custom_call_target="tpu_custom_call" | custom-call | bytes 1179648 | tf_op jit(solution)/shard_map/forward/pallas_call | solution.py:321
  38.0 8.1 %all-to-all-done.1.packed_ref.refs_4_ = bf16[8,16,2304]{2,1,0:T(8,128)(2,1)} async-done(((bf16[8,16,2304]{2,1,0:T(8,128)(2,1)}), bf16[8,16,2304]{2,1,0:T(8,128)(2,1)}, u32[]{:S(2)}, u32[]{:S(2)}) %all-to-all-start.1) | async-done | bytes 589856 | tf_op jit(solution)/shard_map/all_to_all | solution.py:620
  46.1 1.5 %collective-permute-start.4 = (bf16[8,16,2304]{2,1,0:T(8,128)(2,1)}, bf16[8,16,2304]{2,1,0:T(8,128)(2,1)}, u32[]{:S(2)}, u32[]{:S(2)}) collective-permute-start(bf16[8,16,2304]{2,1,0:T(8,128)(2,1)} %all-to-all-done.1.packed_ref.refs_4_), channel_id=1, source_target_pairs={{0,16},{8,24},{16,0},{24,8},{1,17},{9,25},{17,1},{25,9},{2,18},{10... | collective-permute-start | bytes 1769480 | tf_op jit(solution)/shard_map/ppermute | solution.py:616
  47.6 8.1 %back.1 = (bf16[8,16,2304]{2,1,0:T(8,128)(2,1)}, bf16[144,768]{1,0:T(8,128)(2,1)}, bf16[144,1536]{1,0:T(8,128)(2,1)}) custom-call(bf16[8,16,2304]{2,1,0:T(8,128)(2,1)} %all-to-all-done.1.packed_ref.refs_4_, bf16[2048,768]{1,0:T(8,128)(2,1)} %refs_10_.1, bf16[2048,768]{1,0:T(8,128)(2,1)} %refs_11_.1, bf16[768,2048]{1,0:T(8,128)(2,1)} %refs_12_.1, ...), custom_call_target="tpu_custom_call" | custom-call | bytes 1179648 | tf_op jit(solution)/shard_map/back/pallas_call | solution.py:452
  55.6 4.2 %all-to-all-start.2 = ((bf16[8,16,2304]{2,1,0:T(8,128)(2,1)}), bf16[8,16,2304]{2,1,0:T(8,128)(2,1)}, u32[]{:S(2)}, u32[]{:S(2)}) async-start(bf16[8,16,2304]{2,1,0:T(8,128)(2,1)} %get-tuple-element.25), calls=%async_computation.2 | async-start | bytes 1179648 | tf_op jit(solution)/shard_map/all_to_all | solution.py:620
  59.8 0.1 collective-permute-start
  59.9 0.5 collective-permute-start.3
  60.4 0.0 collective-permute-done.1.refs_2_
  60.4 0.1 collective-permute-start.2
  60.5 0.0 collective-permute-done.4.refs_6_
  60.5 0.4 collective-permute-start.5
  60.9 1.3 %collective-permute-done.refs_1_ = bf16[8,16,2304]{2,1,0:T(8,128)(2,1)} collective-permute-done((bf16[8,16,2304]{2,1,0:T(8,128)(2,1)}, bf16[8,16,2304]{2,1,0:T(8,128)(2,1)}, u32[]{:S(2)}, u32[]{:S(2)}) %collective-permute-start) | collective-permute-done | bytes 589856 | tf_op jit(solution)/shard_map/ppermute | solution.py:616
  62.3 1.7 %collective-permute-done.2.refs_3_ = bf16[8,16,2304]{2,1,0:T(8,128)(2,1)} collective-permute-done((bf16[8,16,2304]{2,1,0:T(8,128)(2,1)}, bf16[8,16,2304]{2,1,0:T(8,128)(2,1)}, u32[]{:S(2)}, u32[]{:S(2)}) %collective-permute-start.2) | collective-permute-done | bytes 589856 | tf_op jit(solution)/shard_map/ppermute | solution.py:616
  63.9 0.0 collective-permute-done.3.refs_5_
  63.9 0.8 %collective-permute-done.5.refs_7_ = bf16[8,16,2304]{2,1,0:T(8,128)(2,1)} collective-permute-done((bf16[8,16,2304]{2,1,0:T(8,128)(2,1)}, bf16[8,16,2304]{2,1,0:T(8,128)(2,1)}, u32[]{:S(2)}, u32[]{:S(2)}) %collective-permute-start.5) | collective-permute-done | bytes 589856 | tf_op jit(solution)/shard_map/ppermute | solution.py:616
  64.8 15.0 %weight_grads.1 = (f32[512,768]{1,0:T(8,128)}, f32[512,768]{1,0:T(8,128)}, f32[768,512]{1,0:T(8,128)}) custom-call(s32[1]{0:T(128)} %bitcast.2.part_ref, bf16[8,16,2304]{2,1,0:T(8,128)(2,1)} %all-to-all-done.refs_0_, bf16[8,16,2304]{2,1,0:T(8,128)(2,1)} %collective-permute-done.refs_1_, bf16[8,16,2304]{2,1,0:T(8,128)(2,1)} %collective-permute-done.1.refs_2_, ...), custom_call_target="tpu_custom_call" | custom-call | bytes 1179648 | tf_op jit(solution)/shard_map/weight_grads/pallas_call | solution.py:577
  79.8 0.0 all-to-all-done.2.back_ref
  79.8 2.4 %merge.1 = bf16[128,2048]{1,0:T(8,128)(2,1)} custom-call(s32[1,128]{1,0:T(1,128)} %bitcast.5, bf16[8,16,2304]{2,1,0:T(8,128)(2,1)} %all-to-all-done.2.back_ref), custom_call_target="tpu_custom_call" | custom-call | flops 134217728 | bytes 1048576 | tf_op jit(solution)/shard_map/merge/pallas_call | solution.py:229
Async XLA Ops:
  3.0 23.3 %all-to-all-start = ((bf16[8,16,2304]{2,1,0:T(8,128)(2,1)}), bf16[8,16,2304]{2,1,0:T(8,128)(2,1)}, u32[]{:S(2)}, u32[]{:S(2)}) async-start(bf16[8,16,2304]{2,1,0:T(8,128)(2,1)} %pack.3), calls=%async_computation | async-start | bytes 1179648 | tf_op jit(solution)/shard_map/all_to_all | solution.py:620
  26.2 19.8 %all-to-all-start.1 = ((bf16[8,16,2304]{2,1,0:T(8,128)(2,1)}), bf16[8,16,2304]{2,1,0:T(8,128)(2,1)}, u32[]{:S(2)}, u32[]{:S(2)}) async-start(bf16[8,16,2304]{2,1,0:T(8,128)(2,1)} %pack.2), calls=%async_computation.1 | async-start | bytes 1179648 | tf_op jit(solution)/shard_map/all_to_all | solution.py:620
  30.4 30.0 %collective-permute-start.1 = (bf16[8,16,2304]{2,1,0:T(8,128)(2,1)}, bf16[8,16,2304]{2,1,0:T(8,128)(2,1)}, u32[]{:S(2)}, u32[]{:S(2)}) collective-permute-start(bf16[8,16,2304]{2,1,0:T(8,128)(2,1)} %all-to-all-done.refs_0_), channel_id=1, source_target_pairs={{0,16},{8,24},{16,0},{24,8},{1,17},{9,25},{17,1},{25,9},{2,18},{10... | collective-permute-start | bytes 1769480 | tf_op jit(solution)/shard_map/ppermute | solution.py:616
  46.1 14.4 %collective-permute-start.4 = (bf16[8,16,2304]{2,1,0:T(8,128)(2,1)}, bf16[8,16,2304]{2,1,0:T(8,128)(2,1)}, u32[]{:S(2)}, u32[]{:S(2)}) collective-permute-start(bf16[8,16,2304]{2,1,0:T(8,128)(2,1)} %all-to-all-done.1.packed_ref.refs_4_), channel_id=1, source_target_pairs={{0,16},{8,24},{16,0},{24,8},{1,17},{9,25},{17,1},{25,9},{2,18},{10... | collective-permute-start | bytes 1769480 | tf_op jit(solution)/shard_map/ppermute | solution.py:616
  55.6 24.1 %all-to-all-start.2 = ((bf16[8,16,2304]{2,1,0:T(8,128)(2,1)}), bf16[8,16,2304]{2,1,0:T(8,128)(2,1)}, u32[]{:S(2)}, u32[]{:S(2)}) async-start(bf16[8,16,2304]{2,1,0:T(8,128)(2,1)} %get-tuple-element.25), calls=%async_computation.2 | async-start | bytes 1179648 | tf_op jit(solution)/shard_map/all_to_all | solution.py:620
  59.8 2.4 %collective-permute-start = (bf16[8,16,2304]{2,1,0:T(8,128)(2,1)}, bf16[8,16,2304]{2,1,0:T(8,128)(2,1)}, u32[]{:S(2)}, u32[]{:S(2)}) collective-permute-start(bf16[8,16,2304]{2,1,0:T(8,128)(2,1)} %all-to-all-done.refs_0_), channel_id=1, source_target_pairs={{0,8},{8,0},{16,24},{24,16},{1,9},{9,1},{17,25},{25,17},{2,10},{10... | collective-permute-start | bytes 1769480 | tf_op jit(solution)/shard_map/ppermute | solution.py:616
  59.9 4.0 %collective-permute-start.3 = (bf16[8,16,2304]{2,1,0:T(8,128)(2,1)}, bf16[8,16,2304]{2,1,0:T(8,128)(2,1)}, u32[]{:S(2)}, u32[]{:S(2)}) collective-permute-start(bf16[8,16,2304]{2,1,0:T(8,128)(2,1)} %all-to-all-done.1.packed_ref.refs_4_), channel_id=1, source_target_pairs={{0,8},{8,0},{16,24},{24,16},{1,9},{9,1},{17,25},{25,17},{2,10},{10... | collective-permute-start | bytes 1769480 | tf_op jit(solution)/shard_map/ppermute | solution.py:616
  60.4 3.5 %collective-permute-start.2 = (bf16[8,16,2304]{2,1,0:T(8,128)(2,1)}, bf16[8,16,2304]{2,1,0:T(8,128)(2,1)}, u32[]{:S(2)}, u32[]{:S(2)}) collective-permute-start(bf16[8,16,2304]{2,1,0:T(8,128)(2,1)} %collective-permute-done.1.refs_2_), channel_id=1, source_target_pairs={{0,8},{8,0},{16,24},{24,16},{1,9},{9,1},{17,25},{25,17},{2,10},{10... | collective-permute-start | bytes 1769480 | tf_op jit(solution)/shard_map/ppermute | solution.py:616
  60.5 4.3 %collective-permute-start.5 = (bf16[8,16,2304]{2,1,0:T(8,128)(2,1)}, bf16[8,16,2304]{2,1,0:T(8,128)(2,1)}, u32[]{:S(2)}, u32[]{:S(2)}) collective-permute-start(bf16[8,16,2304]{2,1,0:T(8,128)(2,1)} %collective-permute-done.4.refs_6_), channel_id=1, source_target_pairs={{0,8},{8,0},{16,24},{24,16},{1,9},{9,1},{17,25},{25,17},{2,10},{10... | collective-permute-start | bytes 1769480 | tf_op jit(solution)/shard_map/ppermute | solution.py:616

commit v8 on v7

--- a/solution.py
+++ b/solution.py
@@ -358,8 +358,8 @@
     chunks = width // chunk
 
     def kernel(packed_ref, gate_ref, up_ref, down_ref, pre_gate_ref, pre_up_ref, *rest):
-        out, hidden_ref, both_ref, held, scaled, pre_gate, pre_up, hidden, both = rest[:9]
-        tail, staged, gate, up, down, arrived, gate_in, up_in, down_in, gone = rest[9:]
+        out, factors_ref, held, scaled, pre_gate, pre_up, factors = rest[:7]
+        tail, staged, gate, up, down, arrived, gate_in, up_in, down_in, gone = rest[7:]
         now = pl.program_id(0)
         first = [(packed_ref, held), (pre_gate_ref, pre_gate), (pre_up_ref, pre_up)]
 
@@ -380,10 +380,7 @@
             )
 
         def leave_factors():
-            return [
-                pltpu.make_async_copy(hidden, hidden_ref, gone.at[chunks + 1]),
-                pltpu.make_async_copy(both, both_ref, gone.at[chunks + 2]),
-            ]
+            return pltpu.make_async_copy(factors, factors_ref, gone.at[chunks + 1])
 
         @pl.when(now == 0)
         def _():
@@ -408,22 +405,21 @@
                 wait(first, arrived, 1)
 
             made, d_gate, d_up = hidden_grads(pre_gate[:, columns], pre_up[:, columns], d_hidden)
-            hidden[:, columns] = made
-            both[:, columns] = d_gate
-            both[:, tile_of(tiles + now, tile)] = d_up
+            factors[:, columns] = made
+            factors[:, tile_of(tiles + now, tile)] = d_gate
+            factors[:, tile_of(2 * tiles + now, tile)] = d_up
 
         @pl.when(now == tiles)
         def _():
-            for copy in leave_factors():
-                copy.start()
+            leave_factors().start()
 
         @pl.when(now >= tiles)
         def _():
             at = now - tiles
             weight_copy(gate_ref, gate, gate_in, at, 0, chunk).wait()
-            done = dot(both[:, :hid], gate[at], BY_WIDTH)
+            done = dot(factors[:, hid : 2 * hid], gate[at], BY_WIDTH)
             weight_copy(up_ref, up, up_in, at, 0, chunk).wait()
-            done = (done + dot(both[:, hid:], up[at], BY_WIDTH)).astype(jnp.bfloat16)
+            done = (done + dot(factors[:, 2 * hid :], up[at], BY_WIDTH)).astype(jnp.bfloat16)
             for block in range(blocks):
                 staged[block, :, tile_of(at, chunk)] = done[block * ROWS : (block + 1) * ROWS]
             leave(at).start()
@@ -445,8 +441,7 @@
             last.start()
             for at in range(chunks):
                 leave(at).wait()
-            for copy in leave_factors():
-                copy.wait()
+            leave_factors().wait()
             last.wait()
 
     return pl.pallas_call(
@@ -454,18 +449,16 @@
         grid=(tiles + chunks,),
         out_shape=[
             jax.ShapeDtypeStruct(packed.shape, jnp.bfloat16),
-            jax.ShapeDtypeStruct((slots, hid), jnp.bfloat16),
-            jax.ShapeDtypeStruct((slots, 2 * hid), jnp.bfloat16),
+            jax.ShapeDtypeStruct((slots, 3 * hid), jnp.bfloat16),
         ],
         in_specs=anywhere(6),
-        out_specs=anywhere(3),
+        out_specs=anywhere(2),
         scratch_shapes=[
             pltpu.VMEM(packed.shape, jnp.bfloat16),
             pltpu.VMEM((slots, width), jnp.bfloat16),
             pltpu.VMEM((slots, hid), jnp.float32),
             pltpu.VMEM((slots, hid), jnp.float32),
-            pltpu.VMEM((slots, hid), jnp.bfloat16),
-            pltpu.VMEM((slots, 2 * hid), jnp.bfloat16),
+            pltpu.VMEM((slots, 3 * hid), jnp.bfloat16),
             pltpu.VMEM((blocks * ROWS, step), jnp.float32),
             pltpu.VMEM(packed.shape, jnp.bfloat16),
             pltpu.VMEM((chunks, chunk, hid), jnp.bfloat16),
@@ -475,7 +468,7 @@
             pltpu.SemaphoreType.DMA((chunks,)),
             pltpu.SemaphoreType.DMA((chunks,)),
             pltpu.SemaphoreType.DMA((tiles,)),
-            pltpu.SemaphoreType.DMA((chunks + 3,)),
+            pltpu.SemaphoreType.DMA((chunks + 2,)),
         ],
         compiler_params=params(),
         cost_estimate=cost(0, 4 * slots * width),
@@ -483,13 +476,14 @@
     )(packed, gate_proj, up_proj, down_proj, pre_gate, pre_up)
 
 
-def weight_grads(tile, part, rows, scaled, hidden, both, gate_proj, up_proj, down_proj):
+def weight_grads(tile, part, rows, scaled, factors, gate_proj, up_proj, down_proj):
     groups = len(rows)
     blocks = rows[0].shape[0]
     hid, width = down_proj.shape
     pieces, step = cut(width)
     slots = blocks * MOST
-    some = (groups - 1) * slots
+    given = len(factors)
+    some = (groups - given) * slots
     share = width // groups
     tiles = hid // tile
 
@@ -497,23 +491,26 @@
         refs = list(refs)
         x_refs = [refs.pop(0) for _ in range(groups)]
         dy_refs = [refs.pop(0) for _ in range(groups)]
-        hidden_ref, both_ref, gate_ref, up_ref, down_ref = [refs.pop(0) for _ in range(5)]
+        factor_refs = [refs.pop(0) for _ in range(given)]
+        gate_ref, up_ref, down_ref = [refs.pop(0) for _ in range(3)]
         d_gate_ref, d_up_ref, d_down_ref = [refs.pop(0) for _ in range(3)]
         x_held, dy_held, mains, tails, x_all, dy_all = [refs.pop(0) for _ in range(6)]
-        x_mine, dy_mine, own_hidden, own_both = [refs.pop(0) for _ in range(4)]
-        gate, up, down, x_in, dy_in, own_in, gate_in, up_in, down_in = refs
+        x_mine, dy_mine, known = [refs.pop(0) for _ in range(3)]
+        gate, up, down, x_in, dy_in, known_in, gate_in, up_in, down_in = refs
         now = pl.program_id(0)
         columns = pl.ds(pl.multiple_of(part_ref[0] * share, share), share)
         begin = part_ref[0] * (share // step)
-        x_pairs = [(x_refs[at], x_held.at[at - 1]) for at in range(1, groups)]
-        dy_pairs = [(dy_refs[at], dy_held.at[at - 1]) for at in range(1, groups)]
-        own_pairs = [(hidden_ref, own_hidden), (both_ref, own_both)]
-        for at, ref in enumerate([x_refs[0], dy_refs[0]]):
-            own_pairs.append((ref.at[:, :, columns], mains.at[at]))
-            own_pairs.append((ref.at[:, :, width:], tails.at[at]))
+        x_pairs = [(x_refs[at], x_held.at[at - given]) for at in range(given, groups)]
+        dy_pairs = [(dy_refs[at], dy_held.at[at - given]) for at in range(given, groups)]
+        known_pairs = []
+        for at in range(given):
+            known_pairs.append((factor_refs[at], known.at[at * slots : (at + 1) * slots, :]))
+        for at, ref in enumerate(x_refs[:given] + dy_refs[:given]):
+            known_pairs.append((ref.at[:, :, columns], mains.at[at]))
+            known_pairs.append((ref.at[:, :, width:], tails.at[at]))
 
         def arrange(held, rows_out, target):
-            for at in range(groups - 1):
+            for at in range(groups - given):
                 unpack(
                     held.at[at, :, :, :width],
                     held.at[at, :, :, width:],
@@ -522,7 +519,7 @@
                     at * slots,
                     rows_out,
                 )
-            target[slots:, :] = rows_out[:, columns]
+            target[given * slots :, :] = rows_out[:, columns]
 
         def fetch_x(index):
             weight_copy(gate_ref, gate, gate_in, index, 1, tile).start()
@@ -548,7 +545,7 @@
         @pl.when(now == 0)
         def _():
             wait(dy_pairs, dy_in)
-            start(own_pairs, own_in)
+            start(known_pairs, known_in)
             arrange(dy_held, dy_all, dy_mine)
 
         @pl.when(now < tiles - 1)
@@ -562,13 +559,15 @@
 
         @pl.when(now == 0)
         def _():
-            wait(own_pairs, own_in)
-            unpack(mains.at[0], tails.at[0], pieces, begin, 0, x_mine)
-            unpack(mains.at[1], tails.at[1], pieces, begin, 0, dy_mine)
-
-        made = jnp.concatenate([own_hidden[:, tile_of(now, tile)], made], 0)
-        d_gate = jnp.concatenate([own_both[:, tile_of(now, tile)], d_gate], 0)
-        d_up = jnp.concatenate([own_both[:, tile_of(tiles + now, tile)], d_up], 0)
+            wait(known_pairs, known_in)
+            for at in range(given):
+                unpack(mains.at[at], tails.at[at], pieces, begin, at * slots, x_mine)
+                behind = given + at
+                unpack(mains.at[behind], tails.at[behind], pieces, begin, at * slots, dy_mine)
+
+        made = jnp.concatenate([known[:, tile_of(now, tile)], made], 0)
+        d_gate = jnp.concatenate([known[:, tile_of(tiles + now, tile)], d_gate], 0)
+        d_up = jnp.concatenate([known[:, tile_of(2 * tiles + now, tile)], d_up], 0)
         sums = dot(x_mine[...], jnp.concatenate([d_gate, d_up], 1), BY_ROWS)
         d_gate_ref[...] = sums[:, :tile]
         d_up_ref[...] = sums[:, tile:]
@@ -582,25 +581,24 @@
             jax.ShapeDtypeStruct((share, hid), jnp.float32),
             jax.ShapeDtypeStruct((hid, share), jnp.float32),
         ],
-        in_specs=[pl.BlockSpec(memory_space=pltpu.SMEM)] + anywhere(2 * groups + 5),
+        in_specs=[pl.BlockSpec(memory_space=pltpu.SMEM)] + anywhere(2 * groups + given + 3),
         out_specs=[column_tile(share, tile), column_tile(share, tile), row_tile(tile, share)],
         scratch_shapes=[
-            pltpu.VMEM((groups - 1,) + rows[0].shape, jnp.bfloat16),
-            pltpu.VMEM((groups - 1,) + rows[0].shape, jnp.bfloat16),
-            pltpu.VMEM((2, blocks, ROWS, share), jnp.bfloat16),
-            pltpu.VMEM((2, blocks, ROWS, step), jnp.bfloat16),
+            pltpu.VMEM((groups - given,) + rows[0].shape, jnp.bfloat16),
+            pltpu.VMEM((groups - given,) + rows[0].shape, jnp.bfloat16),
+            pltpu.VMEM((2 * given, blocks, ROWS, share), jnp.bfloat16),
+            pltpu.VMEM((2 * given, blocks, ROWS, step), jnp.bfloat16),
             pltpu.VMEM((some, width), jnp.bfloat16),
             pltpu.VMEM((some, width), jnp.bfloat16),
             pltpu.VMEM((groups * slots, share), jnp.bfloat16),
             pltpu.VMEM((groups * slots, share), jnp.bfloat16),
-            pltpu.VMEM((slots, hid), jnp.bfloat16),
-            pltpu.VMEM((slots, 2 * hid), jnp.bfloat16),
+            pltpu.VMEM((given * slots, 3 * hid), jnp.bfloat16),
             pltpu.VMEM((tiles, width, tile), jnp.bfloat16),
             pltpu.VMEM((tiles, width, tile), jnp.bfloat16),
             pltpu.VMEM((tiles, tile, width), jnp.bfloat16),
-            pltpu.SemaphoreType.DMA((groups - 1,)),
-            pltpu.SemaphoreType.DMA((groups - 1,)),
-            pltpu.SemaphoreType.DMA((6,)),
+            pltpu.SemaphoreType.DMA((groups - given,)),
+            pltpu.SemaphoreType.DMA((groups - given,)),
+            pltpu.SemaphoreType.DMA((5 * given,)),
             pltpu.SemaphoreType.DMA((tiles,)),
             pltpu.SemaphoreType.DMA((tiles,)),
             pltpu.SemaphoreType.DMA((tiles,)),
@@ -608,7 +606,7 @@
         compiler_params=params(),
         cost_estimate=cost(0, 4 * slots * width),
         name="weight_grads",
-    )(part, *rows, *scaled, hidden, both, gate_proj, up_proj, down_proj)
+    )(part, *rows, *scaled, *factors, gate_proj, up_proj, down_proj)
 
 
 def swap(value, axis, distance):
@@ -636,20 +634,20 @@
     near = swap(rows, "dp", 1)
     scaled = exchange(after(pack(blocks, routes, cotangent, gates), rows))
     pre = forward(tile, [rows], gate_proj, up_proj)
-    scaled, *pre = lax.optimization_barrier((scaled, *pre))
+    scaled, far, near, *pre = lax.optimization_barrier((scaled, far, near, *pre))
+    last = swap(far, "dp", 1)
     dy_far = swap(scaled, "dp", 2)
     dy_near = swap(scaled, "dp", 1)
-    sent, hidden, both = back(tile, scaled, *pre, *weights)
+    sent, factors = back(tile, scaled, *pre, *weights)
+    sent, factors, last, dy_near = lax.optimization_barrier((sent, factors, last, dy_near))
     returned = exchange(sent)
-    last = swap(after(far, pre[0]), "dp", 1)
     dy_last = swap(after(dy_far, sent), "dp", 1)
     grads = weight_grads(
         tile,
         part,
         [rows, near, far, last],
         [scaled, dy_near, dy_far, dy_last],
-        hidden,
-        both,
+        [factors, swap(factors, "dp", 1)],
         *weights,
     )
     return (merge(routes, after(returned, *grads)), *grads)

time: 82.7 us -> 81.6 us (0.987)
  Pallas kernels: 36 us -> 33.8 us
  starting transfers between devices: 19.8 us -> 21.4 us
    all_to_all x3, waiting for transfers between devices: 21.8 us -> 13.7 us  [exchange(): lax.all_to_all(blocks, 'expert', split_axis=0, concat_axis=0, tiled=True)]
    ppermute x6 -> x7, waiting for transfers between devices: 3.85 us -> 11.4 us  [swap(): lax.ppermute(value, axis, [(at, at ^ distance) for at in range(size)])]
    pallas_call x1, Pallas kernels: 15 us -> 12.8 us  [weight_grads(): pl.pallas_call(kernel, grid=(tiles,), out_shape=[jax.ShapeDtypeStruct((sh...]
    all_to_all x3, starting transfers between devices: 15.7 us -> 17.3 us  [exchange(): lax.all_to_all(blocks, 'expert', split_axis=0, concat_axis=0, tiled=True)]
    ppermute x6 -> x7, starting transfers between devices: 4.18 us -> 4.1 us  [swap(): lax.ppermute(value, axis, [(at, at ^ distance) for at in range(size)])]
  transfers between devices with their start and end apart: 9 -> 10, of which waited for: 5 -> 4; matrix products, arithmetic and copies ran while one was open for 0% -> 0% of each run, Pallas kernels for 38% -> 36%
where the time goes in v8:
time: 81.6 us; the launch traced here: 81 us
  Pallas kernels  33.8 us (41%)
  waiting for transfers between devices  25.1 us (31%)
  starting transfers between devices  21.4 us (26%)
    all_to_all x3, starting transfers between devices, exchange(): lax.all_to_all(blocks, 'expert', split_axis=0, concat_axis=0, tiled=True)  17.3 us
    all_to_all x3, waiting for transfers between devices, exchange(): lax.all_to_all(blocks, 'expert', split_axis=0, concat_axis=0, tiled=True)  13.7 us
    pallas_call x1, Pallas kernels, weight_grads(): pl.pallas_call(kernel, grid=(tiles,), out_shape=[jax.ShapeDtypeStruct((sh...  12.8 us
    ppermute x7, waiting for transfers between devices, swap(): lax.ppermute(value, axis, [(at, at ^ distance) for at in range(size)])  11.4 us
    pallas_call x1, Pallas kernels, back(): pl.pallas_call(kernel, grid=(tiles + chunks,), out_shape=[jax.ShapeDtypeS...  8.06 us
    pallas_call x1, Pallas kernels, forward(): pl.pallas_call(kernel, grid=(tiles,), out_shape=[jax.ShapeDtypeStruct((to...  5.93 us
    pallas_call x2, Pallas kernels, pack(): pl.pallas_call(kernel, out_shape=jax.ShapeDtypeStruct((blocks, ROWS, widt...  4.66 us
    ppermute x7, starting transfers between devices, swap(): lax.ppermute(value, axis, [(at, at ^ distance) for at in range(size)])  4.1 us
  transfers between devices with their start and end apart: 10, of which 4 were waited for; matrix products, arithmetic and copies ran while one was open for 0% of the time, Pallas kernels for 36%

profile of v8, /device:TPU:0, one launch (start us, length us, event | category | flops | bytes accessed | tf_op | source)
XLA Modules:
  0.0 81.0 jit_solution(2812737611036127390)
XLA Ops:
  0.6 2.3 %pack.3 = bf16[8,16,2304]{2,1,0:T(8,128)(2,1)} custom-call(s32[1,128]{1,0:T(1,128)} %bitcast.3, bf16[128,2048]{1,0:T(8,128)(2,1)} %refs_1_.2), custom_call_target="tpu_custom_call" | custom-call | flops 134217728 | bytes 1048576 | tf_op jit(solution)/shard_map/pack/pallas_call | solution.py:193
  3.0 7.3 %all-to-all-start = ((bf16[8,16,2304]{2,1,0:T(8,128)(2,1)}), bf16[8,16,2304]{2,1,0:T(8,128)(2,1)}, u32[]{:S(2)}, u32[]{:S(2)}) async-start(bf16[8,16,2304]{2,1,0:T(8,128)(2,1)} %pack.3), calls=%async_computation | async-start | bytes 1179648 | tf_op jit(solution)/shard_map/all_to_all | solution.py:618
  10.2 2.3 %pack.2 = bf16[8,16,2304]{2,1,0:T(8,128)(2,1)} custom-call(s32[1,128]{1,0:T(1,128)} %bitcast.4, f32[1,128]{1,0:T(1,128)} %bitcast.6, bf16[128,2048]{1,0:T(8,128)(2,1)} %refs_2_.2), custom_call_target="tpu_custom_call" | custom-call | flops 134217728 | bytes 1048576 | tf_op jit(solution)/shard_map/pack/pallas_call | solution.py:193
  12.6 13.6 %all-to-all-done.refs_0_ = bf16[8,16,2304]{2,1,0:T(8,128)(2,1)} async-done(((bf16[8,16,2304]{2,1,0:T(8,128)(2,1)}), bf16[8,16,2304]{2,1,0:T(8,128)(2,1)}, u32[]{:S(2)}, u32[]{:S(2)}) %all-to-all-start) | async-done | bytes 589856 | tf_op jit(solution)/shard_map/all_to_all | solution.py:618
  26.2 4.2 %all-to-all-start.1 = ((bf16[8,16,2304]{2,1,0:T(8,128)(2,1)}), bf16[8,16,2304]{2,1,0:T(8,128)(2,1)}, u32[]{:S(2)}, u32[]{:S(2)}) async-start(bf16[8,16,2304]{2,1,0:T(8,128)(2,1)} %pack.2), calls=%async_computation.1 | async-start | bytes 1179648 | tf_op jit(solution)/shard_map/all_to_all | solution.py:618
  30.4 0.1 collective-permute-start.1
  30.5 1.6 %collective-permute-start = (bf16[8,16,2304]{2,1,0:T(8,128)(2,1)}, bf16[8,16,2304]{2,1,0:T(8,128)(2,1)}, u32[]{:S(2)}, u32[]{:S(2)}) collective-permute-start(bf16[8,16,2304]{2,1,0:T(8,128)(2,1)} %all-to-all-done.refs_0_), channel_id=1, source_target_pairs={{0,16},{8,24},{16,0},{24,8},{1,17},{9,25},{17,1},{25,9},{2,18},{10... | collective-permute-start | bytes 1769480 | tf_op jit(solution)/shard_map/ppermute | solution.py:614
  32.1 5.9 %forward.1 = (f32[144,768]{1,0:T(8,128)}, f32[144,768]{1,0:T(8,128)}) custom-call(bf16[8,16,2304]{2,1,0:T(8,128)(2,1)} %all-to-all-done.refs_0_, bf16[2048,768]{1,0:T(8,128)(2,1)} %refs_10_.1, bf16[2048,768]{1,0:T(8,128)(2,1)} %refs_11_.1), custom_call_target="tpu_custom_call" | custom-call | bytes 1179648 | tf_op jit(solution)/shard_map/forward/pallas_call | solution.py:321
  38.0 0.0 collective-permute-done.1.refs_1_
  38.0 8.5 %collective-permute-done.refs_2_ = bf16[8,16,2304]{2,1,0:T(8,128)(2,1)} collective-permute-done((bf16[8,16,2304]{2,1,0:T(8,128)(2,1)}, bf16[8,16,2304]{2,1,0:T(8,128)(2,1)}, u32[]{:S(2)}, u32[]{:S(2)}) %collective-permute-start) | collective-permute-done | bytes 589856 | tf_op jit(solution)/shard_map/ppermute | solution.py:614
  46.6 0.0 all-to-all-done.1.packed_ref.refs_4_
  46.6 0.0 collective-permute-start.2
  46.6 0.5 collective-permute-start.3
  47.1 1.5 %collective-permute-start.4 = (bf16[8,16,2304]{2,1,0:T(8,128)(2,1)}, bf16[8,16,2304]{2,1,0:T(8,128)(2,1)}, u32[]{:S(2)}, u32[]{:S(2)}) collective-permute-start(bf16[8,16,2304]{2,1,0:T(8,128)(2,1)} %all-to-all-done.1.packed_ref.refs_4_), channel_id=1, source_target_pairs={{0,16},{8,24},{16,0},{24,8},{1,17},{9,25},{17,1},{25,9},{2,18},{10... | collective-permute-start | bytes 1769480 | tf_op jit(solution)/shard_map/ppermute | solution.py:614
  48.6 8.1 %back.1 = (bf16[8,16,2304]{2,1,0:T(8,128)(2,1)}, bf16[144,2304]{1,0:T(8,128)(2,1)}) custom-call(bf16[8,16,2304]{2,1,0:T(8,128)(2,1)} %all-to-all-done.1.packed_ref.refs_4_, bf16[2048,768]{1,0:T(8,128)(2,1)} %refs_10_.1, bf16[2048,768]{1,0:T(8,128)(2,1)} %refs_11_.1, bf16[768,2048]{1,0:T(8,128)(2,1)} %refs_12_.1, f32[144,768]{1,0:T(8,128)} %get-tuple-element.27.pre_gate_ref, ...), custom_call_target="tpu_custom_call" | custom-call | bytes 1179648 | tf_op jit(solution)/shard_map/back/pallas_call | solution.py:447
  56.7 0.0 collective-permute-done.3.refs_5_
  56.7 5.8 %all-to-all-start.2 = ((bf16[8,16,2304]{2,1,0:T(8,128)(2,1)}), bf16[8,16,2304]{2,1,0:T(8,128)(2,1)}, u32[]{:S(2)}, u32[]{:S(2)}) async-start(bf16[8,16,2304]{2,1,0:T(8,128)(2,1)} %get-tuple-element.32), calls=%async_computation.2 | async-start | bytes 1179648 | tf_op jit(solution)/shard_map/all_to_all | solution.py:618
  62.5 0.0 collective-permute-start.6
  62.5 0.1 collective-permute-done.4.refs_6_
  62.6 0.4 collective-permute-start.5
  63.0 2.8 %collective-permute-done.5.refs_7_ = bf16[8,16,2304]{2,1,0:T(8,128)(2,1)} collective-permute-done((bf16[8,16,2304]{2,1,0:T(8,128)(2,1)}, bf16[8,16,2304]{2,1,0:T(8,128)(2,1)}, u32[]{:S(2)}, u32[]{:S(2)}) %collective-permute-start.5) | collective-permute-done | bytes 589856 | tf_op jit(solution)/shard_map/ppermute | solution.py:614
  65.8 12.8 %weight_grads.1 = (f32[512,768]{1,0:T(8,128)}, f32[512,768]{1,0:T(8,128)}, f32[768,512]{1,0:T(8,128)}) custom-call(s32[1]{0:T(128)} %bitcast.2.part_ref, bf16[8,16,2304]{2,1,0:T(8,128)(2,1)} %all-to-all-done.refs_0_, bf16[8,16,2304]{2,1,0:T(8,128)(2,1)} %collective-permute-done.1.refs_1_, bf16[8,16,2304]{2,1,0:T(8,128)(2,1)} %collective-permute-done.refs_2_, ...), custom_call_target="tpu_custom_call" | custom-call | bytes 1179648 | tf_op jit(solution)/shard_map/weight_grads/pallas_call | solution.py:576
  78.7 0.0 all-to-all-done.2.back_ref
  78.7 2.4 %merge.1 = bf16[128,2048]{1,0:T(8,128)(2,1)} custom-call(s32[1,128]{1,0:T(1,128)} %bitcast.5, bf16[8,16,2304]{2,1,0:T(8,128)(2,1)} %all-to-all-done.2.back_ref), custom_call_target="tpu_custom_call" | custom-call | flops 134217728 | bytes 1048576 | tf_op jit(solution)/shard_map/merge/pallas_call | solution.py:229
  (2 shorter events, 0.0 us)
Async XLA Ops:
  3.0 23.3 %all-to-all-start = ((bf16[8,16,2304]{2,1,0:T(8,128)(2,1)}), bf16[8,16,2304]{2,1,0:T(8,128)(2,1)}, u32[]{:S(2)}, u32[]{:S(2)}) async-start(bf16[8,16,2304]{2,1,0:T(8,128)(2,1)} %pack.3), calls=%async_computation | async-start | bytes 1179648 | tf_op jit(solution)/shard_map/all_to_all | solution.py:618
  26.2 20.3 %all-to-all-start.1 = ((bf16[8,16,2304]{2,1,0:T(8,128)(2,1)}), bf16[8,16,2304]{2,1,0:T(8,128)(2,1)}, u32[]{:S(2)}, u32[]{:S(2)}) async-start(bf16[8,16,2304]{2,1,0:T(8,128)(2,1)} %pack.2), calls=%async_computation.1 | async-start | bytes 1179648 | tf_op jit(solution)/shard_map/all_to_all | solution.py:618
  30.4 7.6 %collective-permute-start.1 = (bf16[8,16,2304]{2,1,0:T(8,128)(2,1)}, bf16[8,16,2304]{2,1,0:T(8,128)(2,1)}, u32[]{:S(2)}, u32[]{:S(2)}) collective-permute-start(bf16[8,16,2304]{2,1,0:T(8,128)(2,1)} %all-to-all-done.refs_0_), channel_id=1, source_target_pairs={{0,8},{8,0},{16,24},{24,16},{1,9},{9,1},{17,25},{25,17},{2,10},{10... | collective-permute-start | bytes 1769480 | tf_op jit(solution)/shard_map/ppermute | solution.py:614
  30.5 16.1 %collective-permute-start = (bf16[8,16,2304]{2,1,0:T(8,128)(2,1)}, bf16[8,16,2304]{2,1,0:T(8,128)(2,1)}, u32[]{:S(2)}, u32[]{:S(2)}) collective-permute-start(bf16[8,16,2304]{2,1,0:T(8,128)(2,1)} %all-to-all-done.refs_0_), channel_id=1, source_target_pairs={{0,16},{8,24},{16,0},{24,8},{1,17},{9,25},{17,1},{25,9},{2,18},{10... | collective-permute-start | bytes 1769480 | tf_op jit(solution)/shard_map/ppermute | solution.py:614
  46.6 10.1 %collective-permute-start.2 = (bf16[8,16,2304]{2,1,0:T(8,128)(2,1)}, bf16[8,16,2304]{2,1,0:T(8,128)(2,1)}, u32[]{:S(2)}, u32[]{:S(2)}) collective-permute-start(bf16[8,16,2304]{2,1,0:T(8,128)(2,1)} %collective-permute-done.refs_2_), channel_id=1, source_target_pairs={{0,8},{8,0},{16,24},{24,16},{1,9},{9,1},{17,25},{25,17},{2,10},{10... | collective-permute-start | bytes 1769480 | tf_op jit(solution)/shard_map/ppermute | solution.py:614
  46.6 10.1 %collective-permute-start.3 = (bf16[8,16,2304]{2,1,0:T(8,128)(2,1)}, bf16[8,16,2304]{2,1,0:T(8,128)(2,1)}, u32[]{:S(2)}, u32[]{:S(2)}) collective-permute-start(bf16[8,16,2304]{2,1,0:T(8,128)(2,1)} %all-to-all-done.1.packed_ref.refs_4_), channel_id=1, source_target_pairs={{0,8},{8,0},{16,24},{24,16},{1,9},{9,1},{17,25},{25,17},{2,10},{10... | collective-permute-start | bytes 1769480 | tf_op jit(solution)/shard_map/ppermute | solution.py:614
  47.1 15.6 %collective-permute-start.4 = (bf16[8,16,2304]{2,1,0:T(8,128)(2,1)}, bf16[8,16,2304]{2,1,0:T(8,128)(2,1)}, u32[]{:S(2)}, u32[]{:S(2)}) collective-permute-start(bf16[8,16,2304]{2,1,0:T(8,128)(2,1)} %all-to-all-done.1.packed_ref.refs_4_), channel_id=1, source_target_pairs={{0,16},{8,24},{16,0},{24,8},{1,17},{9,25},{17,1},{25,9},{2,18},{10... | collective-permute-start | bytes 1769480 | tf_op jit(solution)/shard_map/ppermute | solution.py:614
  56.7 22.0 %all-to-all-start.2 = ((bf16[8,16,2304]{2,1,0:T(8,128)(2,1)}), bf16[8,16,2304]{2,1,0:T(8,128)(2,1)}, u32[]{:S(2)}, u32[]{:S(2)}) async-start(bf16[8,16,2304]{2,1,0:T(8,128)(2,1)} %get-tuple-element.32), calls=%async_computation.2 | async-start | bytes 1179648 | tf_op jit(solution)/shard_map/all_to_all | solution.py:618
  62.5 3.3 %collective-permute-start.6 = (bf16[144,2304]{1,0:T(8,128)(2,1)}, bf16[144,2304]{1,0:T(8,128)(2,1)}, u32[]{:S(2)}, u32[]{:S(2)}) collective-permute-start(bf16[144,2304]{1,0:T(8,128)(2,1)} %get-tuple-element.37.refs_8_), channel_id=1, source_target_pairs={{0,8},{8,0},{16,24},{24,16},{1,9},{9,1},{17,25},{25,17},{2,10},{10... | collective-permute-start | bytes 1990664 | tf_op jit(solution)/shard_map/ppermute | solution.py:614
  62.6 3.2 %collective-permute-start.5 = (bf16[8,16,2304]{2,1,0:T(8,128)(2,1)}, bf16[8,16,2304]{2,1,0:T(8,128)(2,1)}, u32[]{:S(2)}, u32[]{:S(2)}) collective-permute-start(bf16[8,16,2304]{2,1,0:T(8,128)(2,1)} %collective-permute-done.4.refs_6_), channel_id=1, source_target_pairs={{0,8},{8,0},{16,24},{24,16},{1,9},{9,1},{17,25},{25,17},{2,10},{10... | collective-permute-start | bytes 1769480 | tf_op jit(solution)/shard_map/ppermute | solution.py:614

commit v9 on v8

--- a/solution.py
+++ b/solution.py
@@ -141,7 +141,7 @@
             pltpu.make_async_copy(source, target, arrived.at[at]).wait()
 
 
-def slot_masks(routes, blocks, width):
+def slot_masks(routes, blocks, width, me=0):
     tokens = routes.shape[1]
     pieces, _ = cut(width)
     experts = lax.broadcasted_iota(jnp.int32, (EXPERTS, tokens), 0)
@@ -153,24 +153,31 @@
     position = jnp.sum(before * named, axis=0, keepdims=True).astype(jnp.int32)
     slot = lax.broadcasted_iota(jnp.int32, (blocks * ROWS, tokens), 0)
     row = slot % ROWS
-    mine = slot // ROWS == routes
+    mine = (slot // ROWS) ^ me == routes
     main = mine & (position == row)
     spill = mine & (position == ROWS + row // pieces)
     return main, spill, row % pieces
 
 
-def pack(blocks, routes, values, gates=None):
+def pack(blocks, routes, values, gates=None, me=None):
     tokens, width = values.shape
     pieces, step = cut(width)
     sources = (routes,) + (() if gates is None else (gates,)) + (values,)
     count = len(sources)
+    apart = me is not None
+    whole = jax.ShapeDtypeStruct((blocks, ROWS, width + step), jnp.bfloat16)
+    alone = jax.ShapeDtypeStruct((ROWS, width + step), jnp.bfloat16)
 
     def kernel(*refs):
-        out, held, arrived = refs[count], refs[count + 1 : 2 * count + 1], refs[-1]
-        pairs = list(zip(refs[:count], held))
+        refs = list(refs)
+        index = refs.pop(0)[0] if apart else 0
+        given = [refs.pop(0) for _ in range(count)]
+        outs = [refs.pop(0) for _ in range(blocks if apart else 1)]
+        held, arrived = refs[:-1], refs[-1]
+        pairs = list(zip(given, held))
         start(pairs, arrived)
         wait(pairs[:-1], arrived)
-        main, spill, piece = slot_masks(held[0][...], blocks, width)
+        main, spill, piece = slot_masks(held[0][...], blocks, width, index)
         picks = [ones(spill & (piece == at)) for at in range(pieces)]
         if gates is not None:
             weights = held[1][...]
@@ -187,20 +194,43 @@
         extra = extra.astype(jnp.bfloat16)
         for block in range(blocks):
             part = slice(block * ROWS, (block + 1) * ROWS)
-            out[block, :, :width] = rows[part]
-            out[block, :, width:] = extra[part]
-
+            out = outs[block] if apart else outs[0].at[block]
+            out[:, :width] = rows[part]
+            out[:, width:] = extra[part]
+
+    inside = pl.BlockSpec(memory_space=pltpu.VMEM)
     return pl.pallas_call(
         kernel,
-        out_shape=jax.ShapeDtypeStruct((blocks, ROWS, width + step), jnp.bfloat16),
-        in_specs=anywhere(count),
-        out_specs=pl.BlockSpec(memory_space=pltpu.VMEM),
+        out_shape=[alone] * blocks if apart else whole,
+        in_specs=[pl.BlockSpec(memory_space=pltpu.SMEM)] * apart + anywhere(count),
+        out_specs=[inside] * blocks if apart else inside,
         scratch_shapes=[pltpu.VMEM(source.shape, source.dtype) for source in sources]
         + [pltpu.SemaphoreType.DMA((count,))],
         compiler_params=params(),
         cost_estimate=cost(4 * blocks * ROWS * tokens * width, 4 * tokens * width),
         name="pack",
-    )(*sources)
+    )(*((me,) if apart else ()), *sources)
+
+
+def join(me, received):
+    count = len(received)
+
+    def kernel(me_ref, *refs):
+        arrived = refs[-1]
+        pairs = [(refs[at], refs[count].at[me_ref[0] ^ at]) for at in range(count)]
+        start(pairs, arrived)
+        wait(pairs, arrived)
+
+    return pl.pallas_call(
+        kernel,
+        out_shape=jax.ShapeDtypeStruct((count,) + received[0].shape, jnp.bfloat16),
+        in_specs=[pl.BlockSpec(memory_space=pltpu.SMEM)] + anywhere(count),
+        out_specs=pl.BlockSpec(memory_space=pl.ANY),
+        scratch_shapes=[pltpu.SemaphoreType.DMA((count,))],
+        compiler_params=params(),
+        cost_estimate=cost(0, 4 * received[0].size * count),
+        name="join",
+    )(me, *received)
 
 
 def merge(routes, returned):
@@ -629,10 +659,16 @@
     routes = routes.reshape(1, -1)
     gates = expert_gates.reshape(1, -1)
     weights = (gate_proj, up_proj, down_proj)
-    rows = exchange(pack(blocks, routes, tokens))
+    me = lax.axis_index("expert").astype(jnp.int32).reshape(1)
+    received = list(pack(blocks, routes, tokens, me=me))
+    for distance in reversed(range(1, blocks)):
+        received[distance] = swap(received[distance], "expert", distance)
+    packed = pack(blocks, routes, cotangent, gates)
+    packed, received[-1] = lax.optimization_barrier((packed, received[-1]))
+    scaled = exchange(packed)
+    rows = join(me, received)
     far = swap(rows, "dp", 2)
     near = swap(rows, "dp", 1)
-    scaled = exchange(after(pack(blocks, routes, cotangent, gates), rows))
     pre = forward(tile, [rows], gate_proj, up_proj)
     scaled, far, near, *pre = lax.optimization_barrier((scaled, far, near, *pre))
     last = swap(far, "dp", 1)

time: 81.6 us -> 111 us (1.36)
  Pallas kernels: 33.8 us -> 52.8 us
  starting transfers between devices: 21.4 us -> 31.1 us
    pallas_call x2 -> x3, Pallas kernels: 4.66 us -> 23.7 us  [the longest x1 19 us: join(): pl.pallas_call(kernel, out_shape=jax.ShapeDtypeStruct((count,) + received...]
    ppermute x7 -> x14, starting transfers between devices: 4.1 us -> 20.9 us  [swap(): lax.ppermute(value, axis, [(at, at ^ distance) for at in range(size)])]
    ppermute x7 -> x14, waiting for transfers between devices: 11.4 us -> 26.1 us  [swap(): lax.ppermute(value, axis, [(at, at ^ distance) for at in range(size)])]
    all_to_all x3 -> x2, waiting for transfers between devices: 13.7 us -> 0.01 us  [exchange(): lax.all_to_all(blocks, 'expert', split_axis=0, concat_axis=0, tiled=True)]
    all_to_all x3 -> x2, starting transfers between devices: 17.3 us -> 10.2 us  [exchange(): lax.all_to_all(blocks, 'expert', split_axis=0, concat_axis=0, tiled=True)]
  transfers between devices with their start and end apart: 10 -> 16, of which waited for: 4 -> 8; matrix products, arithmetic and copies ran while one was open for 0% -> 0% of each run, Pallas kernels for 36% -> 43%
where the time goes in v9:
time: 111 us
  Pallas kernels  52.8 us (48%)
  starting transfers between devices  31.1 us (28%)
  waiting for transfers between devices  26.1 us (24%)
    ppermute x14, waiting for transfers between devices, swap(): lax.ppermute(value, axis, [(at, at ^ distance) for at in range(size)])  26.1 us
    ppermute x14, starting transfers between devices, swap(): lax.ppermute(value, axis, [(at, at ^ distance) for at in range(size)])  20.9 us
    pallas_call x1, Pallas kernels, join(): pl.pallas_call(kernel, out_shape=jax.ShapeDtypeStruct((count,) + received...  19 us
    pallas_call x1, Pallas kernels, weight_grads(): pl.pallas_call(kernel, grid=(tiles,), out_shape=[jax.ShapeDtypeStruct((sh...  12.8 us
    all_to_all x2, starting transfers between devices, exchange(): lax.all_to_all(blocks, 'expert', split_axis=0, concat_axis=0, tiled=True)  10.2 us
    pallas_call x1, Pallas kernels, back(): pl.pallas_call(kernel, grid=(tiles + chunks,), out_shape=[jax.ShapeDtypeS...  8.03 us
    pallas_call x1, Pallas kernels, forward(): pl.pallas_call(kernel, grid=(tiles,), out_shape=[jax.ShapeDtypeStruct((to...  5.93 us
    pallas_call x2, Pallas kernels, pack(): pl.pallas_call(kernel, out_shape=[alone] * blocks if apart else whole, in...  4.62 us
  transfers between devices with their start and end apart: 16, of which 8 were waited for; matrix products, arithmetic and copies ran while one was open for 0% of the time, Pallas kernels for 43%

profile of v9, /device:TPU:0, one launch (start us, length us, event | category | flops | bytes accessed | tf_op | source)
XLA Modules:
  0.0 110.8 jit_solution(9292266157890579414)
XLA Ops:
  0.6 2.3 %pack.3 = (bf16[16,2304]{1,0:T(8,128)(2,1)}, bf16[16,2304]{1,0:T(8,128)(2,1)}, bf16[16,2304]{1,0:T(8,128)(2,1)}, bf16[16,2304]{1,0:T(8,128)(2,1)}, bf16[16,2304]...) custom-call(s32[1]{0:T(128)} %bitcast.2.refs_0_.me_ref, ...), custom_call_target="tpu_custom_call" | custom-call | flops 134217728 | bytes 1048576 | tf_op jit(solution)/shard_map/pack/pallas_call | solution.py:202
  2.9 6.0 %collective-permute-start = (bf16[16,2304]{1,0:T(8,128)(2,1)}, bf16[16,2304]{1,0:T(8,128)(2,1)S(1)}, u32[]{:S(2)}, u32[]{:S(2)}) collective-permute-start(bf16[16,2304]{1,0:T(8,128)(2,1)} %get-tuple-element.32), channel_id=1, source_target_pairs={{0,7},{1,6},{2,5},{3,4},{4,3},{5,2},{6,1},{7,0},{8,15},{9,14},{10,... | collective-permute-start | bytes 221192 | tf_op jit(solution)/shard_map/ppermute | solution.py:644
  9.0 2.3 %pack.2 = bf16[8,16,2304]{2,1,0:T(8,128)(2,1)} custom-call(s32[1,128]{1,0:T(1,128)} %bitcast.5, f32[1,128]{1,0:T(1,128)} %bitcast.7, bf16[128,2048]{1,0:T(8,128)(2,1)} %refs_2_.3), custom_call_target="tpu_custom_call" | custom-call | flops 134217728 | bytes 1048576 | tf_op jit(solution)/shard_map/pack/pallas_call | solution.py:202
  11.5 6.0 %all-to-all-start = ((bf16[8,16,2304]{2,1,0:T(8,128)(2,1)}), bf16[8,16,2304]{2,1,0:T(8,128)(2,1)}, u32[]{:S(2)}, u32[]{:S(2)}) async-start(bf16[8,16,2304]{2,1,0:T(8,128)(2,1)} %pack.2), calls=%async_computation | async-start | bytes 1179648 | tf_op jit(solution)/shard_map/all_to_all | solution.py:648
  17.5 2.0 %collective-permute-start.1 = (bf16[16,2304]{1,0:T(8,128)(2,1)}, bf16[16,2304]{1,0:T(8,128)(2,1)S(1)}, u32[]{:S(2)}, u32[]{:S(2)}) collective-permute-start(bf16[16,2304]{1,0:T(8,128)(2,1)} %get-tuple-element.35), channel_id=1, source_target_pairs={{0,1},{1,0},{2,3},{3,2},{4,5},{5,4},{6,7},{7,6},{8,9},{9,8},{10,11... | collective-permute-start | bytes 221192 | tf_op jit(solution)/shard_map/ppermute | solution.py:644
  19.5 1.5 %collective-permute-start.2 = (bf16[16,2304]{1,0:T(8,128)(2,1)}, bf16[16,2304]{1,0:T(8,128)(2,1)}, u32[]{:S(2)}, u32[]{:S(2)}) collective-permute-start(bf16[16,2304]{1,0:T(8,128)(2,1)} %get-tuple-element.36), channel_id=1, source_target_pairs={{0,2},{1,3},{2,0},{3,1},{4,6},{5,7},{6,4},{7,5},{8,10},{9,11},{10,... | collective-permute-start | bytes 221192 | tf_op jit(solution)/shard_map/ppermute | solution.py:644
  21.0 2.9 %collective-permute-start.4 = (bf16[16,2304]{1,0:T(8,128)(2,1)}, bf16[16,2304]{1,0:T(8,128)(2,1)}, u32[]{:S(2)}, u32[]{:S(2)}) collective-permute-start(bf16[16,2304]{1,0:T(8,128)(2,1)} %get-tuple-element.38), channel_id=1, source_target_pairs={{0,4},{1,5},{2,6},{3,7},{4,0},{5,1},{6,2},{7,3},{8,12},{9,13},{10,... | collective-permute-start | bytes 221192 | tf_op jit(solution)/shard_map/ppermute | solution.py:644
  23.9 1.5 %collective-permute-start.5 = (bf16[16,2304]{1,0:T(8,128)(2,1)}, bf16[16,2304]{1,0:T(8,128)(2,1)}, u32[]{:S(2)}, u32[]{:S(2)}) collective-permute-start(bf16[16,2304]{1,0:T(8,128)(2,1)} %get-tuple-element.39), channel_id=1, source_target_pairs={{0,5},{1,4},{2,7},{3,6},{4,1},{5,0},{6,3},{7,2},{8,13},{9,12},{10,... | collective-permute-start | bytes 221192 | tf_op jit(solution)/shard_map/ppermute | solution.py:644
  25.4 3.3 %collective-permute-start.6 = (bf16[16,2304]{1,0:T(8,128)(2,1)}, bf16[16,2304]{1,0:T(8,128)(2,1)}, u32[]{:S(2)}, u32[]{:S(2)}) collective-permute-start(bf16[16,2304]{1,0:T(8,128)(2,1)} %get-tuple-element.40), channel_id=1, source_target_pairs={{0,6},{1,7},{2,4},{3,5},{4,2},{5,3},{6,0},{7,1},{8,14},{9,15},{10,... | collective-permute-start | bytes 221192 | tf_op jit(solution)/shard_map/ppermute | solution.py:644
  28.6 1.4 %collective-permute-done.2.refs_2_ = bf16[16,2304]{1,0:T(8,128)(2,1)} collective-permute-done((bf16[16,2304]{1,0:T(8,128)(2,1)}, bf16[16,2304]{1,0:T(8,128)(2,1)}, u32[]{:S(2)}, u32[]{:S(2)}) %collective-permute-start.2) | collective-permute-done | bytes 73760 | tf_op jit(solution)/shard_map/ppermute | solution.py:644
  30.1 2.1 %collective-permute-done.3.refs_3_ = bf16[16,2304]{1,0:T(8,128)(2,1)} collective-permute-done((bf16[16,2304]{1,0:T(8,128)(2,1)}, bf16[16,2304]{1,0:T(8,128)(2,1)}, u32[]{:S(2)}, u32[]{:S(2)}) %collective-permute-start.3) | collective-permute-done | bytes 73760 | tf_op jit(solution)/shard_map/ppermute | solution.py:644
  32.2 8.1 %collective-permute-done.4.refs_4_ = bf16[16,2304]{1,0:T(8,128)(2,1)} collective-permute-done((bf16[16,2304]{1,0:T(8,128)(2,1)}, bf16[16,2304]{1,0:T(8,128)(2,1)}, u32[]{:S(2)}, u32[]{:S(2)}) %collective-permute-start.4) | collective-permute-done | bytes 73760 | tf_op jit(solution)/shard_map/ppermute | solution.py:644
  40.3 1.7 %collective-permute-done.5.refs_5_ = bf16[16,2304]{1,0:T(8,128)(2,1)} collective-permute-done((bf16[16,2304]{1,0:T(8,128)(2,1)}, bf16[16,2304]{1,0:T(8,128)(2,1)}, u32[]{:S(2)}, u32[]{:S(2)}) %collective-permute-start.5) | collective-permute-done | bytes 73760 | tf_op jit(solution)/shard_map/ppermute | solution.py:644
  42.0 19.0 %join.1.refs_0_ = bf16[8,16,2304]{2,1,0:T(8,128)(2,1)} custom-call(s32[1]{0:T(128)} %bitcast.2.refs_0_.me_ref, bf16[16,2304]{1,0:T(8,128)(2,1)} %get-tuple-element.34.refs_0_, bf16[16,2304]{1,0:T(8,128)(2,1)} %copy-done.1, bf16[16,2304]{1,0:T(8,128)(2,1)} %collective-permute-done.2.refs_2_, bf16[16,2304]{1,0:T(8,128)(2,1)} %collective-permute-done.3.refs_3_, ...), custom_call_target="tpu_custom_call" | custom-call | bytes 1179648 | tf_op jit(solution)/shard_map/join/pallas_call | solution.py:224
  61.1 1.6 %collective-permute-start.7 = (bf16[8,16,2304]{2,1,0:T(8,128)(2,1)}, bf16[8,16,2304]{2,1,0:T(8,128)(2,1)}, u32[]{:S(2)}, u32[]{:S(2)}) collective-permute-start(bf16[8,16,2304]{2,1,0:T(8,128)(2,1)} %join.1.refs_0_), channel_id=1, source_target_pairs={{0,16},{8,24},{16,0},{24,8},{1,17},{9,25},{17,1},{25,9},{2,18},{10... | collective-permute-start | bytes 1769480 | tf_op jit(solution)/shard_map/ppermute | solution.py:644
  62.7 5.9 %forward.1 = (f32[144,768]{1,0:T(8,128)}, f32[144,768]{1,0:T(8,128)}) custom-call(bf16[8,16,2304]{2,1,0:T(8,128)(2,1)} %join.1.refs_0_, bf16[2048,768]{1,0:T(8,128)(2,1)} %refs_10_.1, bf16[2048,768]{1,0:T(8,128)(2,1)} %refs_11_.1), custom_call_target="tpu_custom_call" | custom-call | bytes 1179648 | tf_op jit(solution)/shard_map/forward/pallas_call | solution.py:351
  68.6 8.5 %collective-permute-done.7.refs_2_ = bf16[8,16,2304]{2,1,0:T(8,128)(2,1)} collective-permute-done((bf16[8,16,2304]{2,1,0:T(8,128)(2,1)}, bf16[8,16,2304]{2,1,0:T(8,128)(2,1)}, u32[]{:S(2)}, u32[]{:S(2)}) %collective-permute-start.7) | collective-permute-done | bytes 589856 | tf_op jit(solution)/shard_map/ppermute | solution.py:644
  77.7 1.5 %collective-permute-start.11 = (bf16[8,16,2304]{2,1,0:T(8,128)(2,1)}, bf16[8,16,2304]{2,1,0:T(8,128)(2,1)}, u32[]{:S(2)}, u32[]{:S(2)}) collective-permute-start(bf16[8,16,2304]{2,1,0:T(8,128)(2,1)} %all-to-all-done.packed_ref.refs_4_), channel_id=1, source_target_pairs={{0,16},{8,24},{16,0},{24,8},{1,17},{9,25},{17,1},{25,9},{2,18},{10... | collective-permute-start | bytes 1769480 | tf_op jit(solution)/shard_map/ppermute | solution.py:644
  79.2 8.0 %back.1 = (bf16[8,16,2304]{2,1,0:T(8,128)(2,1)}, bf16[144,2304]{1,0:T(8,128)(2,1)}) custom-call(bf16[8,16,2304]{2,1,0:T(8,128)(2,1)} %all-to-all-done.packed_ref.refs_4_, bf16[2048,768]{1,0:T(8,128)(2,1)} %refs_10_.1, bf16[2048,768]{1,0:T(8,128)(2,1)} %refs_11_.1, bf16[768,2048]{1,0:T(8,128)(2,1)} %refs_12_.1, f32[144,768]{1,0:T(8,128)} %get-tuple-element.45.pre_gate_ref, ...), custom_call_target="tpu_custom_call" | custom-call | bytes 1179648 | tf_op jit(solution)/shard_map/back/pallas_call | solution.py:477
  87.2 4.2 %all-to-all-start.1 = ((bf16[8,16,2304]{2,1,0:T(8,128)(2,1)}), bf16[8,16,2304]{2,1,0:T(8,128)(2,1)}, u32[]{:S(2)}, u32[]{:S(2)}) async-start(bf16[8,16,2304]{2,1,0:T(8,128)(2,1)} %get-tuple-element.50), calls=%async_computation.1 | async-start | bytes 1179648 | tf_op jit(solution)/shard_map/all_to_all | solution.py:648
  91.5 1.7 %collective-permute-done.11.refs_6_ = bf16[8,16,2304]{2,1,0:T(8,128)(2,1)} collective-permute-done((bf16[8,16,2304]{2,1,0:T(8,128)(2,1)}, bf16[8,16,2304]{2,1,0:T(8,128)(2,1)}, u32[]{:S(2)}, u32[]{:S(2)}) %collective-permute-start.11) | collective-permute-done | bytes 589856 | tf_op jit(solution)/shard_map/ppermute | solution.py:644
  93.2 2.3 %collective-permute-done.12.refs_7_ = bf16[8,16,2304]{2,1,0:T(8,128)(2,1)} collective-permute-done((bf16[8,16,2304]{2,1,0:T(8,128)(2,1)}, bf16[8,16,2304]{2,1,0:T(8,128)(2,1)}, u32[]{:S(2)}, u32[]{:S(2)}) %collective-permute-start.12) | collective-permute-done | bytes 589856 | tf_op jit(solution)/shard_map/ppermute | solution.py:644
  95.6 12.8 %weight_grads.1 = (f32[512,768]{1,0:T(8,128)}, f32[512,768]{1,0:T(8,128)}, f32[768,512]{1,0:T(8,128)}) custom-call(s32[1]{0:T(128)} %bitcast.3.part_ref, bf16[8,16,2304]{2,1,0:T(8,128)(2,1)} %join.1.refs_0_, bf16[8,16,2304]{2,1,0:T(8,128)(2,1)} %collective-permute-done.8.refs_1_, bf16[8,16,2304]{2,1,0:T(8,128)(2,1)} %collective-permute-done.7.refs_2_, ...), custom_call_target="tpu_custom_call" | custom-call | bytes 1179648 | tf_op jit(solution)/shard_map/weight_grads/pallas_call | solution.py:606
  108.4 2.4 %merge.1 = bf16[128,2048]{1,0:T(8,128)(2,1)} custom-call(s32[1,128]{1,0:T(1,128)} %bitcast.6, bf16[8,16,2304]{2,1,0:T(8,128)(2,1)} %all-to-all-done.1.back_ref), custom_call_target="tpu_custom_call" | custom-call | flops 134217728 | bytes 1048576 | tf_op jit(solution)/shard_map/merge/pallas_call | solution.py:259
  (19 shorter events, 0.9 us)
Async XLA Ops:
  2.9 8.6 %collective-permute-start = (bf16[16,2304]{1,0:T(8,128)(2,1)}, bf16[16,2304]{1,0:T(8,128)(2,1)S(1)}, u32[]{:S(2)}, u32[]{:S(2)}) collective-permute-start(bf16[16,2304]{1,0:T(8,128)(2,1)} %get-tuple-element.32), channel_id=1, source_target_pairs={{0,7},{1,6},{2,5},{3,4},{4,3},{5,2},{6,1},{7,0},{8,15},{9,14},{10,... | collective-permute-start | bytes 221192 | tf_op jit(solution)/shard_map/ppermute | solution.py:644
  11.5 30.4 %copy-start = (bf16[16,2304]{1,0:T(8,128)(2,1)}, bf16[16,2304]{1,0:T(8,128)(2,1)S(1)}, u32[]{:S(2)}) copy-start(bf16[16,2304]{1,0:T(8,128)(2,1)S(1)} %collective-permute-done.refs_7_) | copy-start | bytes 221188
  11.5 65.6 %all-to-all-start = ((bf16[8,16,2304]{2,1,0:T(8,128)(2,1)}), bf16[8,16,2304]{2,1,0:T(8,128)(2,1)}, u32[]{:S(2)}, u32[]{:S(2)}) async-start(bf16[8,16,2304]{2,1,0:T(8,128)(2,1)} %pack.2), calls=%async_computation | async-start | bytes 1179648 | tf_op jit(solution)/shard_map/all_to_all | solution.py:648
  17.5 7.9 %collective-permute-start.1 = (bf16[16,2304]{1,0:T(8,128)(2,1)}, bf16[16,2304]{1,0:T(8,128)(2,1)S(1)}, u32[]{:S(2)}, u32[]{:S(2)}) collective-permute-start(bf16[16,2304]{1,0:T(8,128)(2,1)} %get-tuple-element.35), channel_id=1, source_target_pairs={{0,1},{1,0},{2,3},{3,2},{4,5},{5,4},{6,7},{7,6},{8,9},{9,8},{10,11... | collective-permute-start | bytes 221192 | tf_op jit(solution)/shard_map/ppermute | solution.py:644
  19.5 10.5 %collective-permute-start.2 = (bf16[16,2304]{1,0:T(8,128)(2,1)}, bf16[16,2304]{1,0:T(8,128)(2,1)}, u32[]{:S(2)}, u32[]{:S(2)}) collective-permute-start(bf16[16,2304]{1,0:T(8,128)(2,1)} %get-tuple-element.36), channel_id=1, source_target_pairs={{0,2},{1,3},{2,0},{3,1},{4,6},{5,7},{6,4},{7,5},{8,10},{9,11},{10,... | collective-permute-start | bytes 221192 | tf_op jit(solution)/shard_map/ppermute | solution.py:644
  21.0 11.2 %collective-permute-start.3 = (bf16[16,2304]{1,0:T(8,128)(2,1)}, bf16[16,2304]{1,0:T(8,128)(2,1)}, u32[]{:S(2)}, u32[]{:S(2)}) collective-permute-start(bf16[16,2304]{1,0:T(8,128)(2,1)} %get-tuple-element.37), channel_id=1, source_target_pairs={{0,3},{1,2},{2,1},{3,0},{4,7},{5,6},{6,5},{7,4},{8,11},{9,10},{10,... | collective-permute-start | bytes 221192 | tf_op jit(solution)/shard_map/ppermute | solution.py:644
  21.0 19.2 %collective-permute-start.4 = (bf16[16,2304]{1,0:T(8,128)(2,1)}, bf16[16,2304]{1,0:T(8,128)(2,1)}, u32[]{:S(2)}, u32[]{:S(2)}) collective-permute-start(bf16[16,2304]{1,0:T(8,128)(2,1)} %get-tuple-element.38), channel_id=1, source_target_pairs={{0,4},{1,5},{2,6},{3,7},{4,0},{5,1},{6,2},{7,3},{8,12},{9,13},{10,... | collective-permute-start | bytes 221192 | tf_op jit(solution)/shard_map/ppermute | solution.py:644
  23.9 18.0 %collective-permute-start.5 = (bf16[16,2304]{1,0:T(8,128)(2,1)}, bf16[16,2304]{1,0:T(8,128)(2,1)}, u32[]{:S(2)}, u32[]{:S(2)}) collective-permute-start(bf16[16,2304]{1,0:T(8,128)(2,1)} %get-tuple-element.39), channel_id=1, source_target_pairs={{0,5},{1,4},{2,7},{3,6},{4,1},{5,0},{6,3},{7,2},{8,13},{9,12},{10,... | collective-permute-start | bytes 221192 | tf_op jit(solution)/shard_map/ppermute | solution.py:644
  25.4 16.6 %copy-start.1 = (bf16[16,2304]{1,0:T(8,128)(2,1)}, bf16[16,2304]{1,0:T(8,128)(2,1)S(1)}, u32[]{:S(2)}) copy-start(bf16[16,2304]{1,0:T(8,128)(2,1)S(1)} %collective-permute-done.1.refs_1_) | copy-start | bytes 221188
  25.4 16.6 %collective-permute-start.6 = (bf16[16,2304]{1,0:T(8,128)(2,1)}, bf16[16,2304]{1,0:T(8,128)(2,1)}, u32[]{:S(2)}, u32[]{:S(2)}) collective-permute-start(bf16[16,2304]{1,0:T(8,128)(2,1)} %get-tuple-element.40), channel_id=1, source_target_pairs={{0,6},{1,7},{2,4},{3,5},{4,2},{5,3},{6,0},{7,1},{8,14},{9,15},{10,... | collective-permute-start | bytes 221192 | tf_op jit(solution)/shard_map/ppermute | solution.py:644
  61.0 7.6 %collective-permute-start.8 = (bf16[8,16,2304]{2,1,0:T(8,128)(2,1)}, bf16[8,16,2304]{2,1,0:T(8,128)(2,1)}, u32[]{:S(2)}, u32[]{:S(2)}) collective-permute-start(bf16[8,16,2304]{2,1,0:T(8,128)(2,1)} %join.1.refs_0_), channel_id=1, source_target_pairs={{0,8},{8,0},{16,24},{24,16},{1,9},{9,1},{17,25},{25,17},{2,10},{10... | collective-permute-start | bytes 1769480 | tf_op jit(solution)/shard_map/ppermute | solution.py:644
  61.1 16.1 %collective-permute-start.7 = (bf16[8,16,2304]{2,1,0:T(8,128)(2,1)}, bf16[8,16,2304]{2,1,0:T(8,128)(2,1)}, u32[]{:S(2)}, u32[]{:S(2)}) collective-permute-start(bf16[8,16,2304]{2,1,0:T(8,128)(2,1)} %join.1.refs_0_), channel_id=1, source_target_pairs={{0,16},{8,24},{16,0},{24,8},{1,17},{9,25},{17,1},{25,9},{2,18},{10... | collective-permute-start | bytes 1769480 | tf_op jit(solution)/shard_map/ppermute | solution.py:644
  77.2 10.1 %collective-permute-start.9 = (bf16[8,16,2304]{2,1,0:T(8,128)(2,1)}, bf16[8,16,2304]{2,1,0:T(8,128)(2,1)}, u32[]{:S(2)}, u32[]{:S(2)}) collective-permute-start(bf16[8,16,2304]{2,1,0:T(8,128)(2,1)} %collective-permute-done.7.refs_2_), channel_id=1, source_target_pairs={{0,8},{8,0},{16,24},{24,16},{1,9},{9,1},{17,25},{25,17},{2,10},{10... | collective-permute-start | bytes 1769480 | tf_op jit(solution)/shard_map/ppermute | solution.py:644
  77.2 10.1 %collective-permute-start.10 = (bf16[8,16,2304]{2,1,0:T(8,128)(2,1)}, bf16[8,16,2304]{2,1,0:T(8,128)(2,1)}, u32[]{:S(2)}, u32[]{:S(2)}) collective-permute-start(bf16[8,16,2304]{2,1,0:T(8,128)(2,1)} %all-to-all-done.packed_ref.refs_4_), channel_id=1, source_target_pairs={{0,8},{8,0},{16,24},{24,16},{1,9},{9,1},{17,25},{25,17},{2,10},{10... | collective-permute-start | bytes 1769480 | tf_op jit(solution)/shard_map/ppermute | solution.py:644
  77.7 15.6 %collective-permute-start.11 = (bf16[8,16,2304]{2,1,0:T(8,128)(2,1)}, bf16[8,16,2304]{2,1,0:T(8,128)(2,1)}, u32[]{:S(2)}, u32[]{:S(2)}) collective-permute-start(bf16[8,16,2304]{2,1,0:T(8,128)(2,1)} %all-to-all-done.packed_ref.refs_4_), channel_id=1, source_target_pairs={{0,16},{8,24},{16,0},{24,8},{1,17},{9,25},{17,1},{25,9},{2,18},{10... | collective-permute-start | bytes 1769480 | tf_op jit(solution)/shard_map/ppermute | solution.py:644
  87.2 21.2 %all-to-all-start.1 = ((bf16[8,16,2304]{2,1,0:T(8,128)(2,1)}), bf16[8,16,2304]{2,1,0:T(8,128)(2,1)}, u32[]{:S(2)}, u32[]{:S(2)}) async-start(bf16[8,16,2304]{2,1,0:T(8,128)(2,1)} %get-tuple-element.50), calls=%async_computation.1 | async-start | bytes 1179648 | tf_op jit(solution)/shard_map/all_to_all | solution.py:648
  91.5 4.1 %collective-permute-start.13 = (bf16[144,2304]{1,0:T(8,128)(2,1)}, bf16[144,2304]{1,0:T(8,128)(2,1)}, u32[]{:S(2)}, u32[]{:S(2)}) collective-permute-start(bf16[144,2304]{1,0:T(8,128)(2,1)} %get-tuple-element.55.refs_8_), channel_id=1, source_target_pairs={{0,8},{8,0},{16,24},{24,16},{1,9},{9,1},{17,25},{25,17},{2,10},{10... | collective-permute-start | bytes 1990664 | tf_op jit(solution)/shard_map/ppermute | solution.py:644
  93.2 2.3 %collective-permute-start.12 = (bf16[8,16,2304]{2,1,0:T(8,128)(2,1)}, bf16[8,16,2304]{2,1,0:T(8,128)(2,1)}, u32[]{:S(2)}, u32[]{:S(2)}) collective-permute-start(bf16[8,16,2304]{2,1,0:T(8,128)(2,1)} %collective-permute-done.11.refs_6_), channel_id=1, source_target_pairs={{0,8},{8,0},{16,24},{24,16},{1,9},{9,1},{17,25},{25,17},{2,10},{10... | collective-permute-start | bytes 1769480 | tf_op jit(solution)/shard_map/ppermute | solution.py:644

commit v10 on v8

--- a/solution.py
+++ b/solution.py
@@ -141,7 +141,7 @@
             pltpu.make_async_copy(source, target, arrived.at[at]).wait()
 
 
-def slot_masks(routes, blocks, width):
+def slot_masks(routes, blocks, width, me=0):
     tokens = routes.shape[1]
     pieces, _ = cut(width)
     experts = lax.broadcasted_iota(jnp.int32, (EXPERTS, tokens), 0)
@@ -153,54 +153,76 @@
     position = jnp.sum(before * named, axis=0, keepdims=True).astype(jnp.int32)
     slot = lax.broadcasted_iota(jnp.int32, (blocks * ROWS, tokens), 0)
     row = slot % ROWS
-    mine = slot // ROWS == routes
+    mine = (slot // ROWS) ^ me == routes
     main = mine & (position == row)
     spill = mine & (position == ROWS + row // pieces)
     return main, spill, row % pieces
 
 
-def pack(blocks, routes, values, gates=None):
-    tokens, width = values.shape
+def pack(blocks, me, routes, gates, tokens, cotangent):
+    count, width = tokens.shape
     pieces, step = cut(width)
-    sources = (routes,) + (() if gates is None else (gates,)) + (values,)
-    count = len(sources)
-
-    def kernel(*refs):
-        out, held, arrived = refs[count], refs[count + 1 : 2 * count + 1], refs[-1]
-        pairs = list(zip(refs[:count], held))
+    sources = (routes, gates, tokens, cotangent)
+
+    def kernel(me_ref, *refs):
+        outs, held, arrived = refs[4 : 4 + blocks], refs[4 + blocks : 8 + blocks], refs[-1]
+        pairs = list(zip(refs[:4], held))
         start(pairs, arrived)
-        wait(pairs[:-1], arrived)
-        main, spill, piece = slot_masks(held[0][...], blocks, width)
+        wait(pairs[:2], arrived)
+        main, spill, piece = slot_masks(held[0][...], blocks, width, me_ref[0])
+        mains = ones(main)
         picks = [ones(spill & (piece == at)) for at in range(pieces)]
-        if gates is not None:
-            weights = held[1][...]
-            main_scale = jnp.sum(jnp.where(main, weights, 0.0), axis=1, keepdims=True)
-            spill_scale = jnp.sum(jnp.where(spill, weights, 0.0), axis=1, keepdims=True)
-        wait(pairs, arrived, count - 1)
-        rows = dot(ones(main), held[-1][...])
-        extra = jnp.zeros((blocks * ROWS, step), jnp.float32)
-        for at in range(pieces):
-            extra += dot(picks[at], held[-1][:, at * step : (at + 1) * step])
-        if gates is not None:
-            rows, extra = rows * main_scale, extra * spill_scale
-        rows = rows.astype(jnp.bfloat16)
-        extra = extra.astype(jnp.bfloat16)
-        for block in range(blocks):
-            part = slice(block * ROWS, (block + 1) * ROWS)
-            out[block, :, :width] = rows[part]
-            out[block, :, width:] = extra[part]
-
+        main_scale = jnp.sum(jnp.where(main, held[1][...], 0.0), axis=1, keepdims=True)
+        spill_scale = jnp.sum(jnp.where(spill, held[1][...], 0.0), axis=1, keepdims=True)
+        for half in range(2):
+            wait(pairs[: 3 + half], arrived, 2 + half)
+            values = held[2 + half]
+            rows = dot(mains, values[...])
+            extra = jnp.zeros((blocks * ROWS, step), jnp.float32)
+            for at in range(pieces):
+                extra += dot(picks[at], values[:, at * step : (at + 1) * step])
+            if half > 0:
+                rows, extra = rows * main_scale, extra * spill_scale
+            rows = rows.astype(jnp.bfloat16)
+            extra = extra.astype(jnp.bfloat16)
+            here = slice(half * ROWS, (half + 1) * ROWS)
+            for block in range(blocks):
+                part = slice(block * ROWS, (block + 1) * ROWS)
+                outs[block][here, :width] = rows[part]
+                outs[block][here, width:] = extra[part]
+
+    inside = pl.BlockSpec(memory_space=pltpu.VMEM)
     return pl.pallas_call(
         kernel,
-        out_shape=jax.ShapeDtypeStruct((blocks, ROWS, width + step), jnp.bfloat16),
+        out_shape=[jax.ShapeDtypeStruct((2 * ROWS, width + step), jnp.bfloat16)] * blocks,
+        in_specs=[pl.BlockSpec(memory_space=pltpu.SMEM)] + anywhere(4),
+        out_specs=[inside] * blocks,
+        scratch_shapes=[pltpu.VMEM(source.shape, source.dtype) for source in sources]
+        + [pltpu.SemaphoreType.DMA((4,))],
+        compiler_params=params(),
+        cost_estimate=cost(8 * blocks * ROWS * count * width, 8 * count * width),
+        name="pack",
+    )(me, *sources)
+
+
+def join(received):
+    count = len(received)
+
+    def kernel(*refs):
+        pairs = [(refs[at], refs[count].at[at]) for at in range(count)]
+        start(pairs, refs[-1])
+        wait(pairs, refs[-1])
+
+    return pl.pallas_call(
+        kernel,
+        out_shape=jax.ShapeDtypeStruct((count,) + received[0].shape, jnp.bfloat16),
         in_specs=anywhere(count),
         out_specs=pl.BlockSpec(memory_space=pltpu.VMEM),
-        scratch_shapes=[pltpu.VMEM(source.shape, source.dtype) for source in sources]
-        + [pltpu.SemaphoreType.DMA((count,))],
+        scratch_shapes=[pltpu.SemaphoreType.DMA((count,))],
         compiler_params=params(),
-        cost_estimate=cost(4 * blocks * ROWS * tokens * width, 4 * tokens * width),
-        name="pack",
-    )(*sources)
+        cost_estimate=cost(0, 4 * received[0].size * count),
+        name="join",
+    )(*received)
 
 
 def merge(routes, returned):
@@ -280,63 +302,13 @@
     return pltpu.make_async_copy(view, target.at[index], arrived.at[index])
 
 
-def forward(tile, packed, gate_proj, up_proj):
-    groups = len(packed)
-    blocks = packed[0].shape[0]
-    width, hid = gate_proj.shape
-    pieces, _ = cut(width)
-    slots = blocks * MOST
-    total = groups * slots
-    tiles = hid // tile
-
-    def kernel(*refs):
-        gate_ref, up_ref, pre_gate_ref, pre_up_ref = refs[groups : groups + 4]
-        held, rows, gate, up, arrived, gate_in, up_in = refs[groups + 4 :]
-        now = pl.program_id(0)
-
-        def fetch(index):
-            weight_copy(gate_ref, gate, gate_in, index, 1, tile).start()
-            weight_copy(up_ref, up, up_in, index, 1, tile).start()
-
-        @pl.when(now == 0)
-        def _():
-            pairs = [(refs[at], held.at[at]) for at in range(groups)]
-            start(pairs, arrived)
-            fetch(0)
-            wait(pairs, arrived)
-            for at in range(groups):
-                unpack(
-                    held.at[at, :, :, :width], held.at[at, :, :, width:], pieces, 0, at * slots, rows
-                )
-
-        @pl.when(now < tiles - 1)
-        def _():
-            fetch(now + 1)
-
-        weight_copy(gate_ref, gate, gate_in, now, 1, tile).wait()
-        pre_gate_ref[...] = dot(rows[...], gate[now])
-        weight_copy(up_ref, up, up_in, now, 1, tile).wait()
-        pre_up_ref[...] = dot(rows[...], up[now])
-
-    return pl.pallas_call(
-        kernel,
-        grid=(tiles,),
-        out_shape=[jax.ShapeDtypeStruct((total, hid), jnp.float32)] * 2,
-        in_specs=anywhere(groups + 2),
-        out_specs=[column_tile(total, tile)] * 2,
-        scratch_shapes=[
-            pltpu.VMEM((groups,) + packed[0].shape, jnp.bfloat16),
-            pltpu.VMEM((total, width), jnp.bfloat16),
-            pltpu.VMEM((tiles, width, tile), jnp.bfloat16),
-            pltpu.VMEM((tiles, width, tile), jnp.bfloat16),
-            pltpu.SemaphoreType.DMA((groups,)),
-            pltpu.SemaphoreType.DMA((tiles,)),
-            pltpu.SemaphoreType.DMA((tiles,)),
-        ],
-        compiler_params=params(),
-        cost_estimate=cost(0, 4 * total * width),
-        name="forward",
-    )(*packed, gate_proj, up_proj)
+def halves(parts, half, out):
+    here = slice(half * ROWS, (half + 1) * ROWS)
+    count = parts[0].shape[0]
+    return [
+        (part.at[:, here, :], out.at[at * count : (at + 1) * count])
+        for at, part in enumerate(parts)
+    ]
 
 
 def hidden_grads(pre_gate, pre_up, d_hidden):
@@ -348,30 +320,39 @@
     return hidden, d_gate, d_up
 
 
-def back(tile, packed, pre_gate, pre_up, gate_proj, up_proj, down_proj):
-    blocks = packed.shape[0]
+def back(tile, me, parts, gate_proj, up_proj, down_proj):
+    count = len(parts)
+    blocks = count * parts[0].shape[0]
     width, hid = gate_proj.shape
     slots = blocks * MOST
     pieces, step = cut(width)
     tiles = hid // tile
     chunk = 2 * step
     chunks = width // chunk
-
-    def kernel(packed_ref, gate_ref, up_ref, down_ref, pre_gate_ref, pre_up_ref, *rest):
-        out, factors_ref, held, scaled, pre_gate, pre_up, factors = rest[:7]
-        tail, staged, gate, up, down, arrived, gate_in, up_in, down_in, gone = rest[7:]
+    shape = (blocks, ROWS, width + step)
+
+    def kernel(me_ref, *refs):
+        refs = list(refs)
+        part_refs = [refs.pop(0) for _ in range(count)]
+        gate_ref, up_ref, down_ref, out, factors_ref = [refs.pop(0) for _ in range(5)]
+        x_held, dy_held, rows, scaled, factors = [refs.pop(0) for _ in range(5)]
+        tail, staged, gate, up, down = [refs.pop(0) for _ in range(5)]
+        x_in, dy_in, gate_in, up_in, down_in, gone = refs
         now = pl.program_id(0)
-        first = [(packed_ref, held), (pre_gate_ref, pre_gate), (pre_up_ref, pre_up)]
-
-        def fetch(index):
-            @pl.when(index < tiles)
-            def _():
-                weight_copy(down_ref, down, down_in, index, 0, tile).start()
-
-            @pl.when((index >= tiles) & (index < tiles + chunks))
-            def _():
-                weight_copy(gate_ref, gate, gate_in, index - tiles, 0, chunk).start()
-                weight_copy(up_ref, up, up_in, index - tiles, 0, chunk).start()
+        x_pairs, dy_pairs = halves(part_refs, 0, x_held), halves(part_refs, 1, dy_held)
+
+        def column_copy(source, target, arrived, index):
+            here = tile_of(index, tile)
+            return pltpu.make_async_copy(
+                source.at[:, here], target.at[:, here], arrived.at[index]
+            )
+
+        def fetch_x(index):
+            column_copy(gate_ref, gate, gate_in, index).start()
+            column_copy(up_ref, up, up_in, index).start()
+
+        def fetch_dy(index):
+            weight_copy(down_ref, down, down_in, index, 0, tile).start()
 
         def leave(index):
             columns = tile_of(index, chunk)
@@ -384,27 +365,39 @@
 
         @pl.when(now == 0)
         def _():
-            start(first[:1], arrived)
-            fetch(0)
-            start(first, arrived, 1)
-            wait(first[:1], arrived)
-            fetch(1)
-            unpack(held.at[:, :, :width], held.at[:, :, width:], pieces, 0, 0, scaled)
+            start(x_pairs, x_in)
+            fetch_x(0)
+            wait(x_pairs, x_in)
+            start(dy_pairs, dy_in)
+            fetch_dy(0)
+            unpack(x_held.at[:, :, :width], x_held.at[:, :, width:], pieces, 0, 0, rows)
             tail[...] = jnp.zeros_like(tail)
 
-        fetch(now + 2)
-
         @pl.when(now < tiles)
         def _():
             columns = tile_of(now, tile)
+            column_copy(gate_ref, gate, gate_in, now).wait()
+            pre_gate = dot(rows[...], gate[:, columns])
+
+            @pl.when(now < tiles - 1)
+            def _():
+                fetch_x(now + 1)
+
+            column_copy(up_ref, up, up_in, now).wait()
+            pre_up = dot(rows[...], up[:, columns])
+
+            @pl.when(now == 0)
+            def _():
+                wait(dy_pairs, dy_in)
+                unpack(dy_held.at[:, :, :width], dy_held.at[:, :, width:], pieces, 0, 0, scaled)
+
+            @pl.when(now < tiles - 1)
+            def _():
+                fetch_dy(now + 1)
+
             weight_copy(down_ref, down, down_in, now, 0, tile).wait()
             d_hidden = dot(scaled[...], down[now], BY_WIDTH)
-
-            @pl.when(now == 0)
-            def _():
-                wait(first, arrived, 1)
-
-            made, d_gate, d_up = hidden_grads(pre_gate[:, columns], pre_up[:, columns], d_hidden)
+            made, d_gate, d_up = hidden_grads(pre_gate, pre_up, d_hidden)
             factors[:, columns] = made
             factors[:, tile_of(tiles + now, tile)] = d_gate
             factors[:, tile_of(2 * tiles + now, tile)] = d_up
@@ -416,12 +409,12 @@
         @pl.when(now >= tiles)
         def _():
             at = now - tiles
-            weight_copy(gate_ref, gate, gate_in, at, 0, chunk).wait()
-            done = dot(factors[:, hid : 2 * hid], gate[at], BY_WIDTH)
-            weight_copy(up_ref, up, up_in, at, 0, chunk).wait()
-            done = (done + dot(factors[:, 2 * hid :], up[at], BY_WIDTH)).astype(jnp.bfloat16)
+            here = tile_of(at, chunk)
+            done = dot(factors[:, hid : 2 * hid], gate[here, :], BY_WIDTH)
+            done += dot(factors[:, 2 * hid :], up[here, :], BY_WIDTH)
+            done = done.astype(jnp.bfloat16)
             for block in range(blocks):
-                staged[block, :, tile_of(at, chunk)] = done[block * ROWS : (block + 1) * ROWS]
+                staged[me_ref[0] ^ block, :, here] = done[block * ROWS : (block + 1) * ROWS]
             leave(at).start()
             for piece in range(chunk // step):
                 tail[...] += dot(
@@ -434,7 +427,7 @@
         def _():
             for block in range(blocks):
                 part = tail[block * ROWS : (block + 1) * ROWS, :]
-                staged[block, :, width:] = part.astype(jnp.bfloat16)
+                staged[me_ref[0] ^ block, :, width:] = part.astype(jnp.bfloat16)
             last = pltpu.make_async_copy(
                 staged.at[:, :, width:], out.at[:, :, width:], gone.at[chunks]
             )
@@ -448,37 +441,39 @@
         kernel,
         grid=(tiles + chunks,),
         out_shape=[
-            jax.ShapeDtypeStruct(packed.shape, jnp.bfloat16),
+            jax.ShapeDtypeStruct(shape, jnp.bfloat16),
             jax.ShapeDtypeStruct((slots, 3 * hid), jnp.bfloat16),
         ],
-        in_specs=anywhere(6),
+        in_specs=[pl.BlockSpec(memory_space=pltpu.SMEM)] + anywhere(count + 3),
         out_specs=anywhere(2),
         scratch_shapes=[
-            pltpu.VMEM(packed.shape, jnp.bfloat16),
+            pltpu.VMEM(shape, jnp.bfloat16),
+            pltpu.VMEM(shape, jnp.bfloat16),
             pltpu.VMEM((slots, width), jnp.bfloat16),
-            pltpu.VMEM((slots, hid), jnp.float32),
-            pltpu.VMEM((slots, hid), jnp.float32),
+            pltpu.VMEM((slots, width), jnp.bfloat16),
             pltpu.VMEM((slots, 3 * hid), jnp.bfloat16),
             pltpu.VMEM((blocks * ROWS, step), jnp.float32),
-            pltpu.VMEM(packed.shape, jnp.bfloat16),
-            pltpu.VMEM((chunks, chunk, hid), jnp.bfloat16),
-            pltpu.VMEM((chunks, chunk, hid), jnp.bfloat16),
+            pltpu.VMEM(shape, jnp.bfloat16),
+            pltpu.VMEM((width, hid), jnp.bfloat16),
+            pltpu.VMEM((width, hid), jnp.bfloat16),
             pltpu.VMEM((tiles, tile, width), jnp.bfloat16),
-            pltpu.SemaphoreType.DMA((3,)),
-            pltpu.SemaphoreType.DMA((chunks,)),
-            pltpu.SemaphoreType.DMA((chunks,)),
+            pltpu.SemaphoreType.DMA((count,)),
+            pltpu.SemaphoreType.DMA((count,)),
+            pltpu.SemaphoreType.DMA((tiles,)),
+            pltpu.SemaphoreType.DMA((tiles,)),
             pltpu.SemaphoreType.DMA((tiles,)),
             pltpu.SemaphoreType.DMA((chunks + 2,)),
         ],
         compiler_params=params(),
         cost_estimate=cost(0, 4 * slots * width),
         name="back",
-    )(packed, gate_proj, up_proj, down_proj, pre_gate, pre_up)
-
-
-def weight_grads(tile, part, rows, scaled, factors, gate_proj, up_proj, down_proj):
-    groups = len(rows)
-    blocks = rows[0].shape[0]
+    )(me, *parts, gate_proj, up_proj, down_proj)
+
+
+def weight_grads(tile, part, parts, factors, gate_proj, up_proj, down_proj):
+    groups, count = len(parts), len(parts[0])
+    each = parts[0][0].shape[0]
+    blocks = count * each
     hid, width = down_proj.shape
     pieces, step = cut(width)
     slots = blocks * MOST
@@ -489,8 +484,7 @@
 
     def kernel(part_ref, *refs):
         refs = list(refs)
-        x_refs = [refs.pop(0) for _ in range(groups)]
-        dy_refs = [refs.pop(0) for _ in range(groups)]
+        part_refs = [[refs.pop(0) for _ in range(count)] for _ in range(groups)]
         factor_refs = [refs.pop(0) for _ in range(given)]
         gate_ref, up_ref, down_ref = [refs.pop(0) for _ in range(3)]
         d_gate_ref, d_up_ref, d_down_ref = [refs.pop(0) for _ in range(3)]
@@ -500,14 +494,19 @@
         now = pl.program_id(0)
         columns = pl.ds(pl.multiple_of(part_ref[0] * share, share), share)
         begin = part_ref[0] * (share // step)
-        x_pairs = [(x_refs[at], x_held.at[at - given]) for at in range(given, groups)]
-        dy_pairs = [(dy_refs[at], dy_held.at[at - given]) for at in range(given, groups)]
-        known_pairs = []
+        x_pairs, dy_pairs, known_pairs = [], [], []
+        for at in range(given, groups):
+            x_pairs += halves(part_refs[at], 0, x_held.at[at - given])
+            dy_pairs += halves(part_refs[at], 1, dy_held.at[at - given])
         for at in range(given):
             known_pairs.append((factor_refs[at], known.at[at * slots : (at + 1) * slots, :]))
-        for at, ref in enumerate(x_refs[:given] + dy_refs[:given]):
-            known_pairs.append((ref.at[:, :, columns], mains.at[at]))
-            known_pairs.append((ref.at[:, :, width:], tails.at[at]))
+            for half in range(2):
+                here = slice(half * ROWS, (half + 1) * ROWS)
+                behind = half * given + at
+                for number, ref in enumerate(part_refs[at]):
+                    some_blocks = slice(number * each, (number + 1) * each)
+                    known_pairs.append((ref.at[:, here, columns], mains.at[behind, some_blocks]))
+                    known_pairs.append((ref.at[:, here, width:], tails.at[behind, some_blocks]))
 
         def arrange(held, rows_out, target):
             for at in range(groups - given):
@@ -581,11 +580,11 @@
             jax.ShapeDtypeStruct((share, hid), jnp.float32),
             jax.ShapeDtypeStruct((hid, share), jnp.float32),
         ],
-        in_specs=[pl.BlockSpec(memory_space=pltpu.SMEM)] + anywhere(2 * groups + given + 3),
+        in_specs=[pl.BlockSpec(memory_space=pltpu.SMEM)] + anywhere(groups * count + given + 3),
         out_specs=[column_tile(share, tile), column_tile(share, tile), row_tile(tile, share)],
         scratch_shapes=[
-            pltpu.VMEM((groups - given,) + rows[0].shape, jnp.bfloat16),
-            pltpu.VMEM((groups - given,) + rows[0].shape, jnp.bfloat16),
+            pltpu.VMEM((groups - given, blocks, ROWS, width + step), jnp.bfloat16),
+            pltpu.VMEM((groups - given, blocks, ROWS, width + step), jnp.bfloat16),
             pltpu.VMEM((2 * given, blocks, ROWS, share), jnp.bfloat16),
             pltpu.VMEM((2 * given, blocks, ROWS, step), jnp.bfloat16),
             pltpu.VMEM((some, width), jnp.bfloat16),
@@ -596,9 +595,9 @@
             pltpu.VMEM((tiles, width, tile), jnp.bfloat16),
             pltpu.VMEM((tiles, width, tile), jnp.bfloat16),
             pltpu.VMEM((tiles, tile, width), jnp.bfloat16),
-            pltpu.SemaphoreType.DMA((groups - given,)),
-            pltpu.SemaphoreType.DMA((groups - given,)),
-            pltpu.SemaphoreType.DMA((5 * given,)),
+            pltpu.SemaphoreType.DMA(((groups - given) * count,)),
+            pltpu.SemaphoreType.DMA(((groups - given) * count,)),
+            pltpu.SemaphoreType.DMA(((1 + 4 * count) * given,)),
             pltpu.SemaphoreType.DMA((tiles,)),
             pltpu.SemaphoreType.DMA((tiles,)),
             pltpu.SemaphoreType.DMA((tiles,)),
@@ -606,7 +605,7 @@
         compiler_params=params(),
         cost_estimate=cost(0, 4 * slots * width),
         name="weight_grads",
-    )(part, *rows, *scaled, *factors, gate_proj, up_proj, down_proj)
+    )(part, *[one for group in parts for one in group], *factors, gate_proj, up_proj, down_proj)
 
 
 def swap(value, axis, distance):
@@ -625,28 +624,37 @@
 def gather_body(tokens, cotangent, routes, expert_gates, gate_proj, up_proj, down_proj):
     blocks = lax.axis_size("expert")
     tile = 256
+    me = lax.axis_index("expert").astype(jnp.int32).reshape(1)
     part = lax.axis_index("dp").astype(jnp.int32).reshape(1)
     routes = routes.reshape(1, -1)
     gates = expert_gates.reshape(1, -1)
     weights = (gate_proj, up_proj, down_proj)
-    rows = exchange(pack(blocks, routes, tokens))
-    far = swap(rows, "dp", 2)
-    near = swap(rows, "dp", 1)
-    scaled = exchange(after(pack(blocks, routes, cotangent, gates), rows))
-    pre = forward(tile, [rows], gate_proj, up_proj)
-    scaled, far, near, *pre = lax.optimization_barrier((scaled, far, near, *pre))
+    received = list(pack(blocks, me, routes, gates, tokens, cotangent))
+    half = blocks // 2
+    order = [7, 6, 3, 2, 1, 5, 4]
+    for distance in order:
+        received[distance] = swap(received[distance], "expert", distance)
+    *received[1:half], received[6], received[7] = lax.optimization_barrier(
+        (*received[1:half], received[6], received[7])
+    )
+    first = join(received[:half])
+    far = swap(first, "dp", 2)
+    near = swap(first, "dp", 1)
+    *received[half:], far, near = lax.optimization_barrier((*received[half:], far, near))
     last = swap(far, "dp", 1)
-    dy_far = swap(scaled, "dp", 2)
-    dy_near = swap(scaled, "dp", 1)
-    sent, factors = back(tile, scaled, *pre, *weights)
-    sent, factors, last, dy_near = lax.optimization_barrier((sent, factors, last, dy_near))
+    second = join(received[half:])
+    second_far = swap(second, "dp", 2)
+    second_near = swap(second, "dp", 1)
+    sent, factors = back(tile, me, [first, second], *weights)
+    sent, factors, last, second_near = lax.optimization_barrier(
+        (sent, factors, last, second_near)
+    )
     returned = exchange(sent)
-    dy_last = swap(after(dy_far, sent), "dp", 1)
+    second_last = swap(after(second_far, sent), "dp", 1)
     grads = weight_grads(
         tile,
         part,
-        [rows, near, far, last],
-        [scaled, dy_near, dy_far, dy_last],
+        [[first, second], [near, second_near], [far, second_far], [last, second_last]],
         [factors, swap(factors, "dp", 1)],
         *weights,
     )

time: 81.6 us -> 81.7 us (level)
  waiting for transfers between devices: 25.1 us -> 27.7 us
  Pallas kernels: 33.8 us -> 32.4 us
  starting transfers between devices: 21.4 us -> 20.5 us
    ppermute x7 -> x14, waiting for transfers between devices: 11.4 us -> 27.5 us  [swap(): lax.ppermute(value, axis, [(at, at ^ distance) for at in range(size)])]
    all_to_all x3 -> x1, waiting for transfers between devices: 13.7 us -> 0.18 us  [exchange(): lax.all_to_all(blocks, 'expert', split_axis=0, concat_axis=0, tiled=True)]
    all_to_all x3 -> x1, starting transfers between devices: 17.3 us -> 4.21 us  [exchange(): lax.all_to_all(blocks, 'expert', split_axis=0, concat_axis=0, tiled=True)]
    ppermute x7 -> x14, starting transfers between devices: 4.1 us -> 16.3 us  [swap(): lax.ppermute(value, axis, [(at, at ^ distance) for at in range(size)])]
    pallas_call x3, Pallas kernels: 10.6 us -> 6.96 us  [the longest x2 3.97 us: join(): pl.pallas_call(kernel, out_shape=jax.ShapeDtypeStruct((count,) + received...]
    pallas_call x1, Pallas kernels: 8.06 us -> 10.5 us  [back(): pl.pallas_call(kernel, grid=(tiles + chunks,), out_shape=[jax.ShapeDtypeS...]
  transfers between devices with their start and end apart: 10 -> 15, of which waited for: 4 -> 9; matrix products, arithmetic and copies ran while one was open for 0% -> 0% of each run, Pallas kernels for 36% -> 28%
where the time goes in v10:
time: 81.7 us; the launch traced here: 81.4 us
  Pallas kernels  32.4 us (40%)
  waiting for transfers between devices  27.7 us (34%)
  starting transfers between devices  20.5 us (25%)
    ppermute x14, waiting for transfers between devices, swap(): lax.ppermute(value, axis, [(at, at ^ distance) for at in range(size)])  27.5 us
    ppermute x14, starting transfers between devices, swap(): lax.ppermute(value, axis, [(at, at ^ distance) for at in range(size)])  16.3 us
    pallas_call x1, Pallas kernels, weight_grads(): pl.pallas_call(kernel, grid=(tiles,), out_shape=[jax.ShapeDtypeStruct((sh...  12.6 us
    pallas_call x1, Pallas kernels, back(): pl.pallas_call(kernel, grid=(tiles + chunks,), out_shape=[jax.ShapeDtypeS...  10.5 us
    all_to_all x1, starting transfers between devices, exchange(): lax.all_to_all(blocks, 'expert', split_axis=0, concat_axis=0, tiled=True)  4.21 us
    pallas_call x2, Pallas kernels, join(): pl.pallas_call(kernel, out_shape=jax.ShapeDtypeStruct((count,) + received...  3.97 us
    pallas_call x1, Pallas kernels, pack(): pl.pallas_call(kernel, out_shape=[jax.ShapeDtypeStruct((2 * ROWS, width +...  2.99 us
    pallas_call x1, Pallas kernels, merge(): pl.pallas_call(kernel, out_shape=jax.ShapeDtypeStruct((tokens, width), jn...  2.35 us
  transfers between devices with their start and end apart: 15, of which 9 were waited for; matrix products, arithmetic and copies ran while one was open for 0% of the time, Pallas kernels for 28%

profile of v10, /device:TPU:0, one launch (start us, length us, event | category | flops | bytes accessed | tf_op | source)
XLA Modules:
  0.0 81.4 jit_solution(13859023539500723604)
XLA Ops:
  0.6 3.0 %pack.1 = (bf16[32,2304]{1,0:T(8,128)(2,1)}, bf16[32,2304]{1,0:T(8,128)(2,1)}, bf16[32,2304]{1,0:T(8,128)(2,1)}, bf16[32,2304]{1,0:T(8,128)(2,1)}, bf16[32,2304]...) custom-call(s32[1]{0:T(128)} %bitcast.1.me_ref, ...), custom_call_target="tpu_custom_call" | custom-call | flops 268435456 | bytes 2097152 | tf_op jit(solution)/shard_map/pack/pallas_call | solution.py:195
  3.6 3.0 %collective-permute-start = (bf16[32,2304]{1,0:T(8,128)(2,1)}, bf16[32,2304]{1,0:T(8,128)(2,1)S(1)}, u32[]{:S(2)}, u32[]{:S(2)}) collective-permute-start(bf16[32,2304]{1,0:T(8,128)(2,1)} %get-tuple-element.35), channel_id=1, source_target_pairs={{0,1},{1,0},{2,3},{3,2},{4,5},{5,4},{6,7},{7,6},{8,9},{9,8},{10,11... | collective-permute-start | bytes 442376 | tf_op jit(solution)/shard_map/ppermute | solution.py:613
  6.6 1.6 %collective-permute-start.1 = (bf16[32,2304]{1,0:T(8,128)(2,1)}, bf16[32,2304]{1,0:T(8,128)(2,1)S(1)}, u32[]{:S(2)}, u32[]{:S(2)}) collective-permute-start(bf16[32,2304]{1,0:T(8,128)(2,1)} %get-tuple-element.36), channel_id=1, source_target_pairs={{0,2},{1,3},{2,0},{3,1},{4,6},{5,7},{6,4},{7,5},{8,10},{9,11},{10,... | collective-permute-start | bytes 442376 | tf_op jit(solution)/shard_map/ppermute | solution.py:613
  8.2 4.0 %collective-permute-start.3 = (bf16[32,2304]{1,0:T(8,128)(2,1)}, bf16[32,2304]{1,0:T(8,128)(2,1)S(1)}, u32[]{:S(2)}, u32[]{:S(2)}) collective-permute-start(bf16[32,2304]{1,0:T(8,128)(2,1)} %get-tuple-element.38), channel_id=1, source_target_pairs={{0,6},{1,7},{2,4},{3,5},{4,2},{5,3},{6,0},{7,1},{8,14},{9,15},{10,... | collective-permute-start | bytes 442376 | tf_op jit(solution)/shard_map/ppermute | solution.py:613
  12.2 1.2 %collective-permute-start.4 = (bf16[32,2304]{1,0:T(8,128)(2,1)}, bf16[32,2304]{1,0:T(8,128)(2,1)}, u32[]{:S(2)}, u32[]{:S(2)}) collective-permute-start(bf16[32,2304]{1,0:T(8,128)(2,1)} %get-tuple-element.39), channel_id=1, source_target_pairs={{0,7},{1,6},{2,5},{3,4},{4,3},{5,2},{6,1},{7,0},{8,15},{9,14},{10,... | collective-permute-start | bytes 442376 | tf_op jit(solution)/shard_map/ppermute | solution.py:613
  13.4 0.2 collective-permute-done.1.refs_2_
  13.6 2.4 %collective-permute-done.2.refs_3_ = bf16[32,2304]{1,0:T(8,128)(2,1)S(1)} collective-permute-done((bf16[32,2304]{1,0:T(8,128)(2,1)}, bf16[32,2304]{1,0:T(8,128)(2,1)S(1)}, u32[]{:S(2)}, u32[]{:S(2)}) %collective-permute-start.2) | collective-permute-done | bytes 147488 | tf_op jit(solution)/shard_map/ppermute | solution.py:613
  16.0 6.1 %collective-permute-done.3.refs_2_ = bf16[32,2304]{1,0:T(8,128)(2,1)S(1)} collective-permute-done((bf16[32,2304]{1,0:T(8,128)(2,1)}, bf16[32,2304]{1,0:T(8,128)(2,1)S(1)}, u32[]{:S(2)}, u32[]{:S(2)}) %collective-permute-start.3) | collective-permute-done | bytes 147488 | tf_op jit(solution)/shard_map/ppermute | solution.py:613
  22.1 2.1 %collective-permute-done.4.refs_3_ = bf16[32,2304]{1,0:T(8,128)(2,1)} collective-permute-done((bf16[32,2304]{1,0:T(8,128)(2,1)}, bf16[32,2304]{1,0:T(8,128)(2,1)}, u32[]{:S(2)}, u32[]{:S(2)}) %collective-permute-start.4) | collective-permute-done | bytes 147488 | tf_op jit(solution)/shard_map/ppermute | solution.py:613
  24.1 2.0 %join.2.refs_0_ = bf16[4,32,2304]{2,1,0:T(8,128)(2,1)} custom-call(bf16[32,2304]{1,0:T(8,128)(2,1)} %get-tuple-element.34.refs_0_, bf16[32,2304]{1,0:T(8,128)(2,1)} %copy-done.1, bf16[32,2304]{1,0:T(8,128)(2,1)} %copy-done.2, bf16[32,2304]{1,0:T(8,128)(2,1)} %copy-done.3), custom_call_target="tpu_custom_call" | custom-call | bytes 1179648 | tf_op jit(solution)/shard_map/join/pallas_call | solution.py:216
  26.2 1.6 %collective-permute-start.7 = (bf16[4,32,2304]{2,1,0:T(8,128)(2,1)}, bf16[4,32,2304]{2,1,0:T(8,128)(2,1)}, u32[]{:S(2)}, u32[]{:S(2)}) collective-permute-start(bf16[4,32,2304]{2,1,0:T(8,128)(2,1)} %join.2.refs_0_), channel_id=1, source_target_pairs={{0,16},{8,24},{16,0},{24,8},{1,17},{9,25},{17,1},{25,9},{2,18},{10... | collective-permute-start | bytes 1769480 | tf_op jit(solution)/shard_map/ppermute | solution.py:613
  27.8 2.6 %collective-permute-start.5 = (bf16[32,2304]{1,0:T(8,128)(2,1)}, bf16[32,2304]{1,0:T(8,128)(2,1)}, u32[]{:S(2)}, u32[]{:S(2)}) collective-permute-start(bf16[32,2304]{1,0:T(8,128)(2,1)} %get-tuple-element.43), channel_id=1, source_target_pairs={{0,4},{1,5},{2,6},{3,7},{4,0},{5,1},{6,2},{7,3},{8,12},{9,13},{10,... | collective-permute-start | bytes 442376 | tf_op jit(solution)/shard_map/ppermute | solution.py:613
  30.4 1.0 %collective-permute-start.6 = (bf16[32,2304]{1,0:T(8,128)(2,1)}, bf16[32,2304]{1,0:T(8,128)(2,1)}, u32[]{:S(2)}, u32[]{:S(2)}) collective-permute-start(bf16[32,2304]{1,0:T(8,128)(2,1)} %get-tuple-element.44), channel_id=1, source_target_pairs={{0,5},{1,4},{2,7},{3,6},{4,1},{5,0},{6,3},{7,2},{8,13},{9,12},{10,... | collective-permute-start | bytes 442376 | tf_op jit(solution)/shard_map/ppermute | solution.py:613
  31.4 10.7 %collective-permute-done.5.refs_0_ = bf16[32,2304]{1,0:T(8,128)(2,1)} collective-permute-done((bf16[32,2304]{1,0:T(8,128)(2,1)}, bf16[32,2304]{1,0:T(8,128)(2,1)}, u32[]{:S(2)}, u32[]{:S(2)}) %collective-permute-start.5) | collective-permute-done | bytes 147488 | tf_op jit(solution)/shard_map/ppermute | solution.py:613
  42.0 3.0 %collective-permute-done.6.refs_1_ = bf16[32,2304]{1,0:T(8,128)(2,1)} collective-permute-done((bf16[32,2304]{1,0:T(8,128)(2,1)}, bf16[32,2304]{1,0:T(8,128)(2,1)}, u32[]{:S(2)}, u32[]{:S(2)}) %collective-permute-start.6) | collective-permute-done | bytes 147488 | tf_op jit(solution)/shard_map/ppermute | solution.py:613
  45.1 2.0 %join.3.refs_1_ = bf16[4,32,2304]{2,1,0:T(8,128)(2,1)} custom-call(bf16[32,2304]{1,0:T(8,128)(2,1)} %collective-permute-done.5.refs_0_, bf16[32,2304]{1,0:T(8,128)(2,1)} %collective-permute-done.6.refs_1_, bf16[32,2304]{1,0:T(8,128)(2,1)} %copy-done, bf16[32,2304]{1,0:T(8,128)(2,1)} %collective-permute-done.4.refs_3_), custom_call_target="tpu_custom_call" | custom-call | bytes 1179648 | tf_op jit(solution)/shard_map/join/pallas_call | solution.py:216
  47.1 0.5 collective-permute-start.9
  47.6 0.5 collective-permute-start.11
  48.1 10.5 %back.1 = (bf16[8,16,2304]{2,1,0:T(8,128)(2,1)}, bf16[144,2304]{1,0:T(8,128)(2,1)}) custom-call(s32[1]{0:T(128)} %bitcast.1.me_ref, bf16[4,32,2304]{2,1,0:T(8,128)(2,1)} %join.2.refs_0_, bf16[4,32,2304]{2,1,0:T(8,128)(2,1)} %join.3.refs_1_, bf16[2048,768]{1,0:T(8,128)(2,1)} %refs_10_.1, bf16[2048,768]{1,0:T(8,128)(2,1)} %refs_11_.1, bf16[768,2048]{1,0:T(8,128)(2,1)} %refs_12_.1), custom_call_target="tpu_custom_call" | custom-call | bytes 1179648 | tf_op jit(solution)/shard_map/back/pallas_call | solution.py:440
  58.6 4.2 %all-to-all-start = ((bf16[8,16,2304]{2,1,0:T(8,128)(2,1)}), bf16[8,16,2304]{2,1,0:T(8,128)(2,1)}, u32[]{:S(2)}, u32[]{:S(2)}) async-start(bf16[8,16,2304]{2,1,0:T(8,128)(2,1)} %get-tuple-element.54), calls=%async_computation | async-start | bytes 1179648 | tf_op jit(solution)/shard_map/all_to_all | solution.py:617
  62.9 0.3 collective-permute-done.11.refs_5_
  63.4 2.8 %collective-permute-done.12.refs_7_ = bf16[4,32,2304]{2,1,0:T(8,128)(2,1)} collective-permute-done((bf16[4,32,2304]{2,1,0:T(8,128)(2,1)}, bf16[4,32,2304]{2,1,0:T(8,128)(2,1)}, u32[]{:S(2)}, u32[]{:S(2)}) %collective-permute-start.12) | collective-permute-done | bytes 589856 | tf_op jit(solution)/shard_map/ppermute | solution.py:613
  66.2 12.6 %weight_grads.1 = (f32[512,768]{1,0:T(8,128)}, f32[512,768]{1,0:T(8,128)}, f32[768,512]{1,0:T(8,128)}) custom-call(s32[1]{0:T(128)} %bitcast.3.part_ref, bf16[4,32,2304]{2,1,0:T(8,128)(2,1)} %join.2.refs_0_, bf16[4,32,2304]{2,1,0:T(8,128)(2,1)} %join.3.refs_1_, bf16[4,32,2304]{2,1,0:T(8,128)(2,1)} %collective-permute-done.8.refs_2_, ...), custom_call_target="tpu_custom_call" | custom-call | bytes 1179648 | tf_op jit(solution)/shard_map/weight_grads/pallas_call | solution.py:575
  79.0 2.4 %merge.1 = bf16[128,2048]{1,0:T(8,128)(2,1)} custom-call(s32[1,128]{1,0:T(1,128)} %bitcast.5, bf16[8,16,2304]{2,1,0:T(8,128)(2,1)} %all-to-all-done.back_ref), custom_call_target="tpu_custom_call" | custom-call | flops 134217728 | bytes 1048576 | tf_op jit(solution)/shard_map/merge/pallas_call | solution.py:251
  (20 shorter events, 0.6 us)
Async XLA Ops:
  3.6 9.8 %collective-permute-start = (bf16[32,2304]{1,0:T(8,128)(2,1)}, bf16[32,2304]{1,0:T(8,128)(2,1)S(1)}, u32[]{:S(2)}, u32[]{:S(2)}) collective-permute-start(bf16[32,2304]{1,0:T(8,128)(2,1)} %get-tuple-element.35), channel_id=1, source_target_pairs={{0,1},{1,0},{2,3},{3,2},{4,5},{5,4},{6,7},{7,6},{8,9},{9,8},{10,11... | collective-permute-start | bytes 442376 | tf_op jit(solution)/shard_map/ppermute | solution.py:613
  6.6 7.0 %collective-permute-start.1 = (bf16[32,2304]{1,0:T(8,128)(2,1)}, bf16[32,2304]{1,0:T(8,128)(2,1)S(1)}, u32[]{:S(2)}, u32[]{:S(2)}) collective-permute-start(bf16[32,2304]{1,0:T(8,128)(2,1)} %get-tuple-element.36), channel_id=1, source_target_pairs={{0,2},{1,3},{2,0},{3,1},{4,6},{5,7},{6,4},{7,5},{8,10},{9,11},{10,... | collective-permute-start | bytes 442376 | tf_op jit(solution)/shard_map/ppermute | solution.py:613
  8.2 7.8 %collective-permute-start.2 = (bf16[32,2304]{1,0:T(8,128)(2,1)}, bf16[32,2304]{1,0:T(8,128)(2,1)S(1)}, u32[]{:S(2)}, u32[]{:S(2)}) collective-permute-start(bf16[32,2304]{1,0:T(8,128)(2,1)} %get-tuple-element.37), channel_id=1, source_target_pairs={{0,3},{1,2},{2,1},{3,0},{4,7},{5,6},{6,5},{7,4},{8,11},{9,10},{10,... | collective-permute-start | bytes 442376 | tf_op jit(solution)/shard_map/ppermute | solution.py:613
  8.2 13.8 %collective-permute-start.3 = (bf16[32,2304]{1,0:T(8,128)(2,1)}, bf16[32,2304]{1,0:T(8,128)(2,1)S(1)}, u32[]{:S(2)}, u32[]{:S(2)}) collective-permute-start(bf16[32,2304]{1,0:T(8,128)(2,1)} %get-tuple-element.38), channel_id=1, source_target_pairs={{0,6},{1,7},{2,4},{3,5},{4,2},{5,3},{6,0},{7,1},{8,14},{9,15},{10,... | collective-permute-start | bytes 442376 | tf_op jit(solution)/shard_map/ppermute | solution.py:613
  12.2 11.9 %collective-permute-start.4 = (bf16[32,2304]{1,0:T(8,128)(2,1)}, bf16[32,2304]{1,0:T(8,128)(2,1)}, u32[]{:S(2)}, u32[]{:S(2)}) collective-permute-start(bf16[32,2304]{1,0:T(8,128)(2,1)} %get-tuple-element.39), channel_id=1, source_target_pairs={{0,7},{1,6},{2,5},{3,4},{4,3},{5,2},{6,1},{7,0},{8,15},{9,14},{10,... | collective-permute-start | bytes 442376 | tf_op jit(solution)/shard_map/ppermute | solution.py:613
  13.4 8.7 %copy-start.1 = (bf16[32,2304]{1,0:T(8,128)(2,1)}, bf16[32,2304]{1,0:T(8,128)(2,1)S(1)}, u32[]{:S(2)}) copy-start(bf16[32,2304]{1,0:T(8,128)(2,1)S(1)} %collective-permute-done.refs_1_) | copy-start | bytes 442372
  13.6 10.5 %copy-start.2 = (bf16[32,2304]{1,0:T(8,128)(2,1)}, bf16[32,2304]{1,0:T(8,128)(2,1)S(1)}, u32[]{:S(2)}) copy-start(bf16[32,2304]{1,0:T(8,128)(2,1)S(1)} %collective-permute-done.1.refs_2_) | copy-start | bytes 442372
  16.0 8.2 %copy-start.3 = (bf16[32,2304]{1,0:T(8,128)(2,1)}, bf16[32,2304]{1,0:T(8,128)(2,1)S(1)}, u32[]{:S(2)}) copy-start(bf16[32,2304]{1,0:T(8,128)(2,1)S(1)} %collective-permute-done.2.refs_3_) | copy-start | bytes 442372
  22.1 23.0 %copy-start = (bf16[32,2304]{1,0:T(8,128)(2,1)}, bf16[32,2304]{1,0:T(8,128)(2,1)S(1)}, u32[]{:S(2)}) copy-start(bf16[32,2304]{1,0:T(8,128)(2,1)S(1)} %collective-permute-done.3.refs_2_) | copy-start | bytes 442372
  26.1 18.9 %collective-permute-start.8 = (bf16[4,32,2304]{2,1,0:T(8,128)(2,1)}, bf16[4,32,2304]{2,1,0:T(8,128)(2,1)}, u32[]{:S(2)}, u32[]{:S(2)}) collective-permute-start(bf16[4,32,2304]{2,1,0:T(8,128)(2,1)} %join.2.refs_0_), channel_id=1, source_target_pairs={{0,8},{8,0},{16,24},{24,16},{1,9},{9,1},{17,25},{25,17},{2,10},{10... | collective-permute-start | bytes 1769480 | tf_op jit(solution)/shard_map/ppermute | solution.py:613
  26.2 18.8 %collective-permute-start.7 = (bf16[4,32,2304]{2,1,0:T(8,128)(2,1)}, bf16[4,32,2304]{2,1,0:T(8,128)(2,1)}, u32[]{:S(2)}, u32[]{:S(2)}) collective-permute-start(bf16[4,32,2304]{2,1,0:T(8,128)(2,1)} %join.2.refs_0_), channel_id=1, source_target_pairs={{0,16},{8,24},{16,0},{24,8},{1,17},{9,25},{17,1},{25,9},{2,18},{10... | collective-permute-start | bytes 1769480 | tf_op jit(solution)/shard_map/ppermute | solution.py:613
  27.8 14.2 %collective-permute-start.5 = (bf16[32,2304]{1,0:T(8,128)(2,1)}, bf16[32,2304]{1,0:T(8,128)(2,1)}, u32[]{:S(2)}, u32[]{:S(2)}) collective-permute-start(bf16[32,2304]{1,0:T(8,128)(2,1)} %get-tuple-element.43), channel_id=1, source_target_pairs={{0,4},{1,5},{2,6},{3,7},{4,0},{5,1},{6,2},{7,3},{8,12},{9,13},{10,... | collective-permute-start | bytes 442376 | tf_op jit(solution)/shard_map/ppermute | solution.py:613
  30.4 14.7 %collective-permute-start.6 = (bf16[32,2304]{1,0:T(8,128)(2,1)}, bf16[32,2304]{1,0:T(8,128)(2,1)}, u32[]{:S(2)}, u32[]{:S(2)}) collective-permute-start(bf16[32,2304]{1,0:T(8,128)(2,1)} %get-tuple-element.44), channel_id=1, source_target_pairs={{0,5},{1,4},{2,7},{3,6},{4,1},{5,0},{6,3},{7,2},{8,13},{9,12},{10,... | collective-permute-start | bytes 442376 | tf_op jit(solution)/shard_map/ppermute | solution.py:613
  47.0 11.6 %collective-permute-start.10 = (bf16[4,32,2304]{2,1,0:T(8,128)(2,1)}, bf16[4,32,2304]{2,1,0:T(8,128)(2,1)}, u32[]{:S(2)}, u32[]{:S(2)}) collective-permute-start(bf16[4,32,2304]{2,1,0:T(8,128)(2,1)} %join.3.refs_1_), channel_id=1, source_target_pairs={{0,8},{8,0},{16,24},{24,16},{1,9},{9,1},{17,25},{25,17},{2,10},{10... | collective-permute-start | bytes 1769480 | tf_op jit(solution)/shard_map/ppermute | solution.py:613
  47.1 11.5 %collective-permute-start.9 = (bf16[4,32,2304]{2,1,0:T(8,128)(2,1)}, bf16[4,32,2304]{2,1,0:T(8,128)(2,1)}, u32[]{:S(2)}, u32[]{:S(2)}) collective-permute-start(bf16[4,32,2304]{2,1,0:T(8,128)(2,1)} %collective-permute-done.7.refs_4_), channel_id=1, source_target_pairs={{0,8},{8,0},{16,24},{24,16},{1,9},{9,1},{17,25},{25,17},{2,10},{10... | collective-permute-start | bytes 1769480 | tf_op jit(solution)/shard_map/ppermute | solution.py:613
  47.6 15.6 %collective-permute-start.11 = (bf16[4,32,2304]{2,1,0:T(8,128)(2,1)}, bf16[4,32,2304]{2,1,0:T(8,128)(2,1)}, u32[]{:S(2)}, u32[]{:S(2)}) collective-permute-start(bf16[4,32,2304]{2,1,0:T(8,128)(2,1)} %join.3.refs_1_), channel_id=1, source_target_pairs={{0,16},{8,24},{16,0},{24,8},{1,17},{9,25},{17,1},{25,9},{2,18},{10... | collective-permute-start | bytes 1769480 | tf_op jit(solution)/shard_map/ppermute | solution.py:613
  58.6 20.4 %all-to-all-start = ((bf16[8,16,2304]{2,1,0:T(8,128)(2,1)}), bf16[8,16,2304]{2,1,0:T(8,128)(2,1)}, u32[]{:S(2)}, u32[]{:S(2)}) async-start(bf16[8,16,2304]{2,1,0:T(8,128)(2,1)} %get-tuple-element.54), calls=%async_computation | async-start | bytes 1179648 | tf_op jit(solution)/shard_map/all_to_all | solution.py:617
  62.9 3.4 %collective-permute-start.13 = (bf16[144,2304]{1,0:T(8,128)(2,1)}, bf16[144,2304]{1,0:T(8,128)(2,1)}, u32[]{:S(2)}, u32[]{:S(2)}) collective-permute-start(bf16[144,2304]{1,0:T(8,128)(2,1)} %get-tuple-element.59.refs_8_), channel_id=1, source_target_pairs={{0,8},{8,0},{16,24},{24,16},{1,9},{9,1},{17,25},{25,17},{2,10},{10... | collective-permute-start | bytes 1990664 | tf_op jit(solution)/shard_map/ppermute | solution.py:613
  63.3 3.0 %collective-permute-start.12 = (bf16[4,32,2304]{2,1,0:T(8,128)(2,1)}, bf16[4,32,2304]{2,1,0:T(8,128)(2,1)}, u32[]{:S(2)}, u32[]{:S(2)}) collective-permute-start(bf16[4,32,2304]{2,1,0:T(8,128)(2,1)} %collective-permute-done.11.refs_5_), channel_id=1, source_target_pairs={{0,8},{8,0},{16,24},{24,16},{1,9},{9,1},{17,25},{25,17},{2,10},{10... | collective-permute-start | bytes 1769480 | tf_op jit(solution)/shard_map/ppermute | solution.py:613

commit v11 on v10

--- a/solution.py
+++ b/solution.py
@@ -205,26 +205,6 @@
     )(me, *sources)
 
 
-def join(received):
-    count = len(received)
-
-    def kernel(*refs):
-        pairs = [(refs[at], refs[count].at[at]) for at in range(count)]
-        start(pairs, refs[-1])
-        wait(pairs, refs[-1])
-
-    return pl.pallas_call(
-        kernel,
-        out_shape=jax.ShapeDtypeStruct((count,) + received[0].shape, jnp.bfloat16),
-        in_specs=anywhere(count),
-        out_specs=pl.BlockSpec(memory_space=pltpu.VMEM),
-        scratch_shapes=[pltpu.SemaphoreType.DMA((count,))],
-        compiler_params=params(),
-        cost_estimate=cost(0, 4 * received[0].size * count),
-        name="join",
-    )(*received)
-
-
 def merge(routes, returned):
     blocks = returned.shape[0]
     tokens = routes.shape[1]
@@ -302,13 +282,9 @@
     return pltpu.make_async_copy(view, target.at[index], arrived.at[index])
 
 
-def halves(parts, half, out):
+def halves(group, half, out):
     here = slice(half * ROWS, (half + 1) * ROWS)
-    count = parts[0].shape[0]
-    return [
-        (part.at[:, here, :], out.at[at * count : (at + 1) * count])
-        for at, part in enumerate(parts)
-    ]
+    return [(block.at[here, :], out.at[at]) for at, block in enumerate(group)]
 
 
 def hidden_grads(pre_gate, pre_up, d_hidden):
@@ -320,9 +296,8 @@
     return hidden, d_gate, d_up
 
 
-def back(tile, me, parts, gate_proj, up_proj, down_proj):
-    count = len(parts)
-    blocks = count * parts[0].shape[0]
+def back(tile, share, me, part, group, gate_proj, up_proj, down_proj):
+    blocks = len(group)
     width, hid = gate_proj.shape
     slots = blocks * MOST
     pieces, step = cut(width)
@@ -330,16 +305,17 @@
     chunk = 2 * step
     chunks = width // chunk
     shape = (blocks, ROWS, width + step)
-
-    def kernel(me_ref, *refs):
+    given = 3 * hid + 2 * share
+
+    def kernel(me_ref, part_ref, *refs):
         refs = list(refs)
-        part_refs = [refs.pop(0) for _ in range(count)]
-        gate_ref, up_ref, down_ref, out, factors_ref = [refs.pop(0) for _ in range(5)]
-        x_held, dy_held, rows, scaled, factors = [refs.pop(0) for _ in range(5)]
+        group_refs = [refs.pop(0) for _ in range(blocks)]
+        gate_ref, up_ref, down_ref, out, kept, handed = [refs.pop(0) for _ in range(6)]
+        x_held, dy_held, rows, scaled, factors, cuts = [refs.pop(0) for _ in range(6)]
         tail, staged, gate, up, down = [refs.pop(0) for _ in range(5)]
-        x_in, dy_in, gate_in, up_in, down_in, gone = refs
+        x_in, dy_in, gate_in, up_in, down_in, gone, cut_in = refs
         now = pl.program_id(0)
-        x_pairs, dy_pairs = halves(part_refs, 0, x_held), halves(part_refs, 1, dy_held)
+        x_pairs, dy_pairs = halves(group_refs, 0, x_held), halves(group_refs, 1, dy_held)
 
         def column_copy(source, target, arrived, index):
             here = tile_of(index, tile)
@@ -361,7 +337,9 @@
             )
 
         def leave_factors():
-            return pltpu.make_async_copy(factors, factors_ref, gone.at[chunks + 1])
+            first, behind = slice(0, 3 * hid), slice(3 * hid, given)
+            pairs = [(factors, kept.at[:, first]), (cuts.at[0], kept.at[:, behind])]
+            return pairs + [(factors, handed.at[:, first]), (cuts.at[1], handed.at[:, behind])]
 
         @pl.when(now == 0)
         def _():
@@ -404,7 +382,11 @@
 
         @pl.when(now == tiles)
         def _():
-            leave_factors().start()
+            for at in range(2):
+                columns = tile_of(part_ref[0] ^ at, share)
+                cuts[at, :, :share] = rows[:, columns]
+                cuts[at, :, share:] = scaled[:, columns]
+            start(leave_factors(), cut_in)
 
         @pl.when(now >= tiles)
         def _():
@@ -434,7 +416,7 @@
             last.start()
             for at in range(chunks):
                 leave(at).wait()
-            leave_factors().wait()
+            wait(leave_factors(), cut_in)
             last.wait()
 
     return pl.pallas_call(
@@ -442,74 +424,72 @@
         grid=(tiles + chunks,),
         out_shape=[
             jax.ShapeDtypeStruct(shape, jnp.bfloat16),
-            jax.ShapeDtypeStruct((slots, 3 * hid), jnp.bfloat16),
+            jax.ShapeDtypeStruct((slots, given), jnp.bfloat16),
+            jax.ShapeDtypeStruct((slots, given), jnp.bfloat16),
         ],
-        in_specs=[pl.BlockSpec(memory_space=pltpu.SMEM)] + anywhere(count + 3),
-        out_specs=anywhere(2),
+        in_specs=[pl.BlockSpec(memory_space=pltpu.SMEM)] * 2 + anywhere(blocks + 3),
+        out_specs=anywhere(3),
         scratch_shapes=[
             pltpu.VMEM(shape, jnp.bfloat16),
             pltpu.VMEM(shape, jnp.bfloat16),
             pltpu.VMEM((slots, width), jnp.bfloat16),
             pltpu.VMEM((slots, width), jnp.bfloat16),
             pltpu.VMEM((slots, 3 * hid), jnp.bfloat16),
+            pltpu.VMEM((2, slots, 2 * share), jnp.bfloat16),
             pltpu.VMEM((blocks * ROWS, step), jnp.float32),
             pltpu.VMEM(shape, jnp.bfloat16),
             pltpu.VMEM((width, hid), jnp.bfloat16),
             pltpu.VMEM((width, hid), jnp.bfloat16),
             pltpu.VMEM((tiles, tile, width), jnp.bfloat16),
-            pltpu.SemaphoreType.DMA((count,)),
-            pltpu.SemaphoreType.DMA((count,)),
+            pltpu.SemaphoreType.DMA((blocks,)),
+            pltpu.SemaphoreType.DMA((blocks,)),
             pltpu.SemaphoreType.DMA((tiles,)),
             pltpu.SemaphoreType.DMA((tiles,)),
             pltpu.SemaphoreType.DMA((tiles,)),
-            pltpu.SemaphoreType.DMA((chunks + 2,)),
+            pltpu.SemaphoreType.DMA((chunks + 1,)),
+            pltpu.SemaphoreType.DMA((4,)),
         ],
         compiler_params=params(),
         cost_estimate=cost(0, 4 * slots * width),
         name="back",
-    )(me, *parts, gate_proj, up_proj, down_proj)
-
-
-def weight_grads(tile, part, parts, factors, gate_proj, up_proj, down_proj):
-    groups, count = len(parts), len(parts[0])
-    each = parts[0][0].shape[0]
-    blocks = count * each
+    )(me, part, *group, gate_proj, up_proj, down_proj)
+
+
+def weight_grads(tile, share, part, known, groups, gate_proj, up_proj, down_proj):
+    count, blocks = len(groups), len(groups[0])
+    given = len(known)
     hid, width = down_proj.shape
     pieces, step = cut(width)
     slots = blocks * MOST
-    given = len(factors)
-    some = (groups - given) * slots
-    share = width // groups
+    total = (given + count) * slots
     tiles = hid // tile
 
     def kernel(part_ref, *refs):
         refs = list(refs)
-        part_refs = [[refs.pop(0) for _ in range(count)] for _ in range(groups)]
-        factor_refs = [refs.pop(0) for _ in range(given)]
+        known_refs = [refs.pop(0) for _ in range(given)]
+        group_refs = [[refs.pop(0) for _ in range(blocks)] for _ in range(count)]
         gate_ref, up_ref, down_ref = [refs.pop(0) for _ in range(3)]
         d_gate_ref, d_up_ref, d_down_ref = [refs.pop(0) for _ in range(3)]
-        x_held, dy_held, mains, tails, x_all, dy_all = [refs.pop(0) for _ in range(6)]
-        x_mine, dy_mine, known = [refs.pop(0) for _ in range(3)]
+        x_held, dy_held, x_all, dy_all = [refs.pop(0) for _ in range(4)]
+        x_mine, dy_mine, factors = [refs.pop(0) for _ in range(3)]
         gate, up, down, x_in, dy_in, known_in, gate_in, up_in, down_in = refs
         now = pl.program_id(0)
-        columns = pl.ds(pl.multiple_of(part_ref[0] * share, share), share)
-        begin = part_ref[0] * (share // step)
+        columns = tile_of(part_ref[0], share)
         x_pairs, dy_pairs, known_pairs = [], [], []
-        for at in range(given, groups):
-            x_pairs += halves(part_refs[at], 0, x_held.at[at - given])
-            dy_pairs += halves(part_refs[at], 1, dy_held.at[at - given])
+        for at in range(count):
+            x_pairs += halves(group_refs[at], 0, x_held.at[at])
+            dy_pairs += halves(group_refs[at], 1, dy_held.at[at])
         for at in range(given):
-            known_pairs.append((factor_refs[at], known.at[at * slots : (at + 1) * slots, :]))
-            for half in range(2):
-                here = slice(half * ROWS, (half + 1) * ROWS)
-                behind = half * given + at
-                for number, ref in enumerate(part_refs[at]):
-                    some_blocks = slice(number * each, (number + 1) * each)
-                    known_pairs.append((ref.at[:, here, columns], mains.at[behind, some_blocks]))
-                    known_pairs.append((ref.at[:, here, width:], tails.at[behind, some_blocks]))
+            here = slice(at * slots, (at + 1) * slots)
+            behind = 3 * hid
+            known_pairs += [
+                (known_refs[at].at[:, :behind], factors.at[here, :]),
+                (known_refs[at].at[:, behind : behind + share], x_mine.at[here, :]),
+                (known_refs[at].at[:, behind + share :], dy_mine.at[here, :]),
+            ]
 
         def arrange(held, rows_out, target):
-            for at in range(groups - given):
+            for at in range(count):
                 unpack(
                     held.at[at, :, :, :width],
                     held.at[at, :, :, width:],
@@ -559,19 +539,18 @@
         @pl.when(now == 0)
         def _():
             wait(known_pairs, known_in)
-            for at in range(given):
-                unpack(mains.at[at], tails.at[at], pieces, begin, at * slots, x_mine)
-                behind = given + at
-                unpack(mains.at[behind], tails.at[behind], pieces, begin, at * slots, dy_mine)
-
-        made = jnp.concatenate([known[:, tile_of(now, tile)], made], 0)
-        d_gate = jnp.concatenate([known[:, tile_of(tiles + now, tile)], d_gate], 0)
-        d_up = jnp.concatenate([known[:, tile_of(2 * tiles + now, tile)], d_up], 0)
+
+        made = jnp.concatenate([factors[:, tile_of(now, tile)], made], 0)
+        d_gate = jnp.concatenate([factors[:, tile_of(tiles + now, tile)], d_gate], 0)
+        d_up = jnp.concatenate([factors[:, tile_of(2 * tiles + now, tile)], d_up], 0)
         sums = dot(x_mine[...], jnp.concatenate([d_gate, d_up], 1), BY_ROWS)
         d_gate_ref[...] = sums[:, :tile]
         d_up_ref[...] = sums[:, tile:]
         d_down_ref[...] = dot(made, dy_mine[...], BY_ROWS)
 
+    held = pltpu.VMEM((count, blocks, ROWS, width + step), jnp.bfloat16)
+    arranged = pltpu.VMEM((count * slots, width), jnp.bfloat16)
+    mine = pltpu.VMEM((total, share), jnp.bfloat16)
     return pl.pallas_call(
         kernel,
         grid=(tiles,),
@@ -580,24 +559,22 @@
             jax.ShapeDtypeStruct((share, hid), jnp.float32),
             jax.ShapeDtypeStruct((hid, share), jnp.float32),
         ],
-        in_specs=[pl.BlockSpec(memory_space=pltpu.SMEM)] + anywhere(groups * count + given + 3),
+        in_specs=[pl.BlockSpec(memory_space=pltpu.SMEM)] + anywhere(given + count * blocks + 3),
         out_specs=[column_tile(share, tile), column_tile(share, tile), row_tile(tile, share)],
         scratch_shapes=[
-            pltpu.VMEM((groups - given, blocks, ROWS, width + step), jnp.bfloat16),
-            pltpu.VMEM((groups - given, blocks, ROWS, width + step), jnp.bfloat16),
-            pltpu.VMEM((2 * given, blocks, ROWS, share), jnp.bfloat16),
-            pltpu.VMEM((2 * given, blocks, ROWS, step), jnp.bfloat16),
-            pltpu.VMEM((some, width), jnp.bfloat16),
-            pltpu.VMEM((some, width), jnp.bfloat16),
-            pltpu.VMEM((groups * slots, share), jnp.bfloat16),
-            pltpu.VMEM((groups * slots, share), jnp.bfloat16),
+            held,
+            held,
+            arranged,
+            arranged,
+            mine,
+            mine,
             pltpu.VMEM((given * slots, 3 * hid), jnp.bfloat16),
             pltpu.VMEM((tiles, width, tile), jnp.bfloat16),
             pltpu.VMEM((tiles, width, tile), jnp.bfloat16),
             pltpu.VMEM((tiles, tile, width), jnp.bfloat16),
-            pltpu.SemaphoreType.DMA(((groups - given) * count,)),
-            pltpu.SemaphoreType.DMA(((groups - given) * count,)),
-            pltpu.SemaphoreType.DMA(((1 + 4 * count) * given,)),
+            pltpu.SemaphoreType.DMA((count * blocks,)),
+            pltpu.SemaphoreType.DMA((count * blocks,)),
+            pltpu.SemaphoreType.DMA((3 * given,)),
             pltpu.SemaphoreType.DMA((tiles,)),
             pltpu.SemaphoreType.DMA((tiles,)),
             pltpu.SemaphoreType.DMA((tiles,)),
@@ -605,7 +582,7 @@
         compiler_params=params(),
         cost_estimate=cost(0, 4 * slots * width),
         name="weight_grads",
-    )(part, *[one for group in parts for one in group], *factors, gate_proj, up_proj, down_proj)
+    )(part, *known, *[block for group in groups for block in group], gate_proj, up_proj, down_proj)
 
 
 def swap(value, axis, distance):
@@ -623,41 +600,22 @@
 
 def gather_body(tokens, cotangent, routes, expert_gates, gate_proj, up_proj, down_proj):
     blocks = lax.axis_size("expert")
-    tile = 256
+    tile, share = 256, tokens.shape[1] // lax.axis_size("dp")
     me = lax.axis_index("expert").astype(jnp.int32).reshape(1)
     part = lax.axis_index("dp").astype(jnp.int32).reshape(1)
     routes = routes.reshape(1, -1)
     gates = expert_gates.reshape(1, -1)
     weights = (gate_proj, up_proj, down_proj)
     received = list(pack(blocks, me, routes, gates, tokens, cotangent))
-    half = blocks // 2
-    order = [7, 6, 3, 2, 1, 5, 4]
-    for distance in order:
+    for distance in reversed(range(1, blocks)):
         received[distance] = swap(received[distance], "expert", distance)
-    *received[1:half], received[6], received[7] = lax.optimization_barrier(
-        (*received[1:half], received[6], received[7])
-    )
-    first = join(received[:half])
-    far = swap(first, "dp", 2)
-    near = swap(first, "dp", 1)
-    *received[half:], far, near = lax.optimization_barrier((*received[half:], far, near))
-    last = swap(far, "dp", 1)
-    second = join(received[half:])
-    second_far = swap(second, "dp", 2)
-    second_near = swap(second, "dp", 1)
-    sent, factors = back(tile, me, [first, second], *weights)
-    sent, factors, last, second_near = lax.optimization_barrier(
-        (sent, factors, last, second_near)
-    )
+    far = [swap(block, "dp", 2) for block in received]
+    sent, kept, handed = back(tile, share, me, part, received, *weights)
     returned = exchange(sent)
-    second_last = swap(after(second_far, sent), "dp", 1)
-    grads = weight_grads(
-        tile,
-        part,
-        [[first, second], [near, second_near], [far, second_far], [last, second_last]],
-        [factors, swap(factors, "dp", 1)],
-        *weights,
-    )
+    far[4:] = after(far[4:], sent)
+    last = [swap(block, "dp", 1) for block in far]
+    known = [kept, swap(handed, "dp", 1)]
+    grads = weight_grads(tile, share, part, known, [far, last], *weights)
     return (merge(routes, after(returned, *grads)), *grads)
 
 

time: 81.7 us -> 101 us (1.24)
  starting transfers between devices: 20.5 us -> 33.2 us
  waiting for transfers between devices: 27.7 us -> 35.5 us
  Pallas kernels: 32.4 us -> 30.1 us
  local copies, waits for them, and re-layouts: 0.01 us -> 1.28 us
    ppermute x14 -> x24, starting transfers between devices: 16.3 us -> 25 us  [swap(): lax.ppermute(value, axis, [(at, at ^ distance) for at in range(size)])]
    ppermute x14 -> x24, waiting for transfers between devices: 27.5 us -> 35.5 us  [swap(): lax.ppermute(value, axis, [(at, at ^ distance) for at in range(size)])]
    pallas_call x2 -> x0, Pallas kernels: 3.97 us -> none  [join(): pl.pallas_call(kernel, out_shape=jax.ShapeDtypeStruct((count,) + received...]
    all_to_all x1, starting transfers between devices: 4.21 us -> 8.14 us  [exchange(): lax.all_to_all(blocks, 'expert', split_axis=0, concat_axis=0, tiled=True)]
    pallas_call x1, Pallas kernels: 12.6 us -> 14 us  [weight_grads(): pl.pallas_call(kernel, grid=(tiles,), out_shape=[jax.ShapeDtypeStruct((sh...]
    unnamed x8 -> x42, local copies, waits for them, and re-layouts: 0.01 us -> 1.28 us
  transfers between devices with their start and end apart: 15 -> 25, of which waited for: 9 -> 16; matrix products, arithmetic and copies ran while one was open for 0% -> 0% of each run, Pallas kernels for 28% -> 14%
where the time goes in v11:
time: 101 us
  waiting for transfers between devices  35.5 us (35%)
  starting transfers between devices  33.2 us (33%)
  Pallas kernels  30.1 us (30%)
  local copies, waits for them, and re-layouts  1.28 us (1%)
    ppermute x24, waiting for transfers between devices, swap(): lax.ppermute(value, axis, [(at, at ^ distance) for at in range(size)])  35.5 us
    ppermute x24, starting transfers between devices, swap(): lax.ppermute(value, axis, [(at, at ^ distance) for at in range(size)])  25 us
    pallas_call x1, Pallas kernels, weight_grads(): pl.pallas_call(kernel, grid=(tiles,), out_shape=[jax.ShapeDtypeStruct((sh...  14 us
    pallas_call x1, Pallas kernels, back(): pl.pallas_call(kernel, grid=(tiles + chunks,), out_shape=[jax.ShapeDtypeS...  10.8 us
    all_to_all x1, starting transfers between devices, exchange(): lax.all_to_all(blocks, 'expert', split_axis=0, concat_axis=0, tiled=True)  8.14 us
    pallas_call x1, Pallas kernels, pack(): pl.pallas_call(kernel, out_shape=[jax.ShapeDtypeStruct((2 * ROWS, width +...  2.99 us
    pallas_call x1, Pallas kernels, merge(): pl.pallas_call(kernel, out_shape=jax.ShapeDtypeStruct((tokens, width), jn...  2.36 us
  transfers between devices with their start and end apart: 25, of which 16 were waited for; matrix products, arithmetic and copies ran while one was open for 0% of the time, Pallas kernels for 14%

profile of v11, /device:TPU:0, one launch (start us, length us, event | category | flops | bytes accessed | tf_op | source)
XLA Modules:
  0.0 100.8 jit_solution(1574667905698308975)
XLA Ops:
  0.6 3.0 %pack.1 = (bf16[32,2304]{1,0:T(8,128)(2,1)}, bf16[32,2304]{1,0:T(8,128)(2,1)}, bf16[32,2304]{1,0:T(8,128)(2,1)}, bf16[32,2304]{1,0:T(8,128)(2,1)}, bf16[32,2304]...) custom-call(s32[1]{0:T(128)} %bitcast.1.me_ref, ...), custom_call_target="tpu_custom_call" | custom-call | flops 268435456 | bytes 2097152 | tf_op jit(solution)/shard_map/pack/pallas_call | solution.py:195
  3.6 3.0 %collective-permute-start = (bf16[32,2304]{1,0:T(8,128)(2,1)}, bf16[32,2304]{1,0:T(8,128)(2,1)S(1)}, u32[]{:S(2)}, u32[]{:S(2)}) collective-permute-start(bf16[32,2304]{1,0:T(8,128)(2,1)} %get-tuple-element.24), channel_id=1, source_target_pairs={{0,1},{1,0},{2,3},{3,2},{4,5},{5,4},{6,7},{7,6},{8,9},{9,8},{10,11... | collective-permute-start | bytes 442376 | tf_op jit(solution)/shard_map/ppermute | solution.py:590
  6.6 1.6 %collective-permute-start.1 = (bf16[32,2304]{1,0:T(8,128)(2,1)}, bf16[32,2304]{1,0:T(8,128)(2,1)S(1)}, u32[]{:S(2)}, u32[]{:S(2)}) collective-permute-start(bf16[32,2304]{1,0:T(8,128)(2,1)} %get-tuple-element.25), channel_id=1, source_target_pairs={{0,2},{1,3},{2,0},{3,1},{4,6},{5,7},{6,4},{7,5},{8,10},{9,11},{10,... | collective-permute-start | bytes 442376 | tf_op jit(solution)/shard_map/ppermute | solution.py:590
  8.2 3.0 %collective-permute-start.3 = (bf16[32,2304]{1,0:T(8,128)(2,1)}, bf16[32,2304]{1,0:T(8,128)(2,1)S(1)}, u32[]{:S(2)}, u32[]{:S(2)}) collective-permute-start(bf16[32,2304]{1,0:T(8,128)(2,1)} %get-tuple-element.27), channel_id=1, source_target_pairs={{0,4},{1,5},{2,6},{3,7},{4,0},{5,1},{6,2},{7,3},{8,12},{9,13},{10,... | collective-permute-start | bytes 442376 | tf_op jit(solution)/shard_map/ppermute | solution.py:590
  12.5 3.6 %collective-permute-start.5 = (bf16[32,2304]{1,0:T(8,128)(2,1)}, bf16[32,2304]{1,0:T(8,128)(2,1)}, u32[]{:S(2)}, u32[]{:S(2)}) collective-permute-start(bf16[32,2304]{1,0:T(8,128)(2,1)} %get-tuple-element.29), channel_id=1, source_target_pairs={{0,6},{1,7},{2,4},{3,5},{4,2},{5,3},{6,0},{7,1},{8,14},{9,15},{10,... | collective-permute-start | bytes 442376 | tf_op jit(solution)/shard_map/ppermute | solution.py:590
  16.1 2.7 %collective-permute-done.1.refs_2_ = bf16[32,2304]{1,0:T(8,128)(2,1)S(1)} collective-permute-done((bf16[32,2304]{1,0:T(8,128)(2,1)}, bf16[32,2304]{1,0:T(8,128)(2,1)S(1)}, u32[]{:S(2)}, u32[]{:S(2)}) %collective-permute-start.1) | collective-permute-done | bytes 147488 | tf_op jit(solution)/shard_map/ppermute | solution.py:590
  19.9 13.0 %collective-permute-done.4.refs_5_ = bf16[32,2304]{1,0:T(8,128)(2,1)S(1)} collective-permute-done((bf16[32,2304]{1,0:T(8,128)(2,1)}, bf16[32,2304]{1,0:T(8,128)(2,1)S(1)}, u32[]{:S(2)}, u32[]{:S(2)}) %collective-permute-start.4) | collective-permute-done | bytes 147488 | tf_op jit(solution)/shard_map/ppermute | solution.py:590
  33.5 10.8 %back.1 = (bf16[8,16,2304]{2,1,0:T(8,128)(2,1)}, bf16[144,3328]{1,0:T(8,128)(2,1)}, bf16[144,3328]{1,0:T(8,128)(2,1)}) custom-call(s32[1]{0:T(128)} %bitcast.1.me_ref, s32[1]{0:T(128)} %bitcast.2.part_ref, bf16[32,2304]{1,0:T(8,128)(2,1)} %get-tuple-element.23.refs_0_, bf16[32,2304]{1,0:T(8,128)(2,1)} %copy-done.10, bf16[32,2304]{1,0:T(8,128)(2,1)} %copy-done.9, ...), custom_call_target="tpu_custom_call" | custom-call | bytes 1179648 | tf_op jit(solution)/shard_map/back/pallas_call | solution.py:422
  44.3 8.1 %all-to-all-start = ((bf16[8,16,2304]{2,1,0:T(8,128)(2,1)}), bf16[8,16,2304]{2,1,0:T(8,128)(2,1)}, u32[]{:S(2)}, u32[]{:S(2)}) async-start(bf16[8,16,2304]{2,1,0:T(8,128)(2,1)} %get-tuple-element.31), calls=%async_computation | async-start | bytes 1179648 | tf_op jit(solution)/shard_map/all_to_all | solution.py:594
  52.5 1.6 %collective-permute-start.8 = (bf16[32,2304]{1,0:T(8,128)(2,1)}, bf16[32,2304]{1,0:T(8,128)(2,1)S(1)}, u32[]{:S(2)}, u32[]{:S(2)}) collective-permute-start(bf16[32,2304]{1,0:T(8,128)(2,1)} %get-tuple-element.23.refs_0_), channel_id=1, source_target_pairs={{0,16},{8,24},{16,0},{24,8},{1,17},{9,25},{17,1},{25,9},{2,18},{10... | collective-permute-start | bytes 442376 | tf_op jit(solution)/shard_map/ppermute | solution.py:590
  54.6 1.6 %collective-permute-start.10 = (bf16[32,2304]{1,0:T(8,128)(2,1)}, bf16[32,2304]{1,0:T(8,128)(2,1)S(1)}, u32[]{:S(2)}, u32[]{:S(2)}) collective-permute-start(bf16[32,2304]{1,0:T(8,128)(2,1)} %copy-done.9), channel_id=1, source_target_pairs={{0,16},{8,24},{16,0},{24,8},{1,17},{9,25},{17,1},{25,9},{2,18},{10... | collective-permute-start | bytes 442376 | tf_op jit(solution)/shard_map/ppermute | solution.py:590
  56.6 2.8 %collective-permute-done.8.refs_2_ = bf16[32,2304]{1,0:T(8,128)(2,1)S(1)} collective-permute-done((bf16[32,2304]{1,0:T(8,128)(2,1)}, bf16[32,2304]{1,0:T(8,128)(2,1)S(1)}, u32[]{:S(2)}, u32[]{:S(2)}) %collective-permute-start.8) | collective-permute-done | bytes 147488 | tf_op jit(solution)/shard_map/ppermute | solution.py:590
  59.4 1.6 %collective-permute-start.12 = (bf16[32,2304]{1,0:T(8,128)(2,1)}, bf16[32,2304]{1,0:T(8,128)(2,1)S(1)}, u32[]{:S(2)}, u32[]{:S(2)}) collective-permute-start(bf16[32,2304]{1,0:T(8,128)(2,1)} %copy-done.6), channel_id=1, source_target_pairs={{0,16},{8,24},{16,0},{24,8},{1,17},{9,25},{17,1},{25,9},{2,18},{10... | collective-permute-start | bytes 442376 | tf_op jit(solution)/shard_map/ppermute | solution.py:590
  61.0 1.6 %collective-permute-done.9.refs_3_ = bf16[32,2304]{1,0:T(8,128)(2,1)S(1)} collective-permute-done((bf16[32,2304]{1,0:T(8,128)(2,1)}, bf16[32,2304]{1,0:T(8,128)(2,1)S(1)}, u32[]{:S(2)}, u32[]{:S(2)}) %collective-permute-start.9) | collective-permute-done | bytes 147488 | tf_op jit(solution)/shard_map/ppermute | solution.py:590
  62.6 1.6 %collective-permute-start.13 = (bf16[32,2304]{1,0:T(8,128)(2,1)}, bf16[32,2304]{1,0:T(8,128)(2,1)S(1)}, u32[]{:S(2)}, u32[]{:S(2)}) collective-permute-start(bf16[32,2304]{1,0:T(8,128)(2,1)} %copy-done.4), channel_id=1, source_target_pairs={{0,16},{8,24},{16,0},{24,8},{1,17},{9,25},{17,1},{25,9},{2,18},{10... | collective-permute-start | bytes 442376 | tf_op jit(solution)/shard_map/ppermute | solution.py:590
  64.1 1.6 %collective-permute-done.10.refs_4_ = bf16[32,2304]{1,0:T(8,128)(2,1)S(1)} collective-permute-done((bf16[32,2304]{1,0:T(8,128)(2,1)}, bf16[32,2304]{1,0:T(8,128)(2,1)S(1)}, u32[]{:S(2)}, u32[]{:S(2)}) %collective-permute-start.10) | collective-permute-done | bytes 147488 | tf_op jit(solution)/shard_map/ppermute | solution.py:590
  65.7 1.6 %collective-permute-start.14 = (bf16[32,2304]{1,0:T(8,128)(2,1)}, bf16[32,2304]{1,0:T(8,128)(2,1)S(1)}, u32[]{:S(2)}, u32[]{:S(2)}) collective-permute-start(bf16[32,2304]{1,0:T(8,128)(2,1)} %collective-permute-done.5.refs_6_), channel_id=1, source_target_pairs={{0,16},{8,24},{16,0},{24,8},{1,17},{9,25},{17,1},{25,9},{2,18},{10... | collective-permute-start | bytes 442376 | tf_op jit(solution)/shard_map/ppermute | solution.py:590
  67.3 1.6 %collective-permute-done.11.refs_5_ = bf16[32,2304]{1,0:T(8,128)(2,1)S(1)} collective-permute-done((bf16[32,2304]{1,0:T(8,128)(2,1)}, bf16[32,2304]{1,0:T(8,128)(2,1)S(1)}, u32[]{:S(2)}, u32[]{:S(2)}) %collective-permute-start.11) | collective-permute-done | bytes 147488 | tf_op jit(solution)/shard_map/ppermute | solution.py:590
  70.5 1.6 %collective-permute-done.12.refs_6_ = bf16[32,2304]{1,0:T(8,128)(2,1)S(1)} collective-permute-done((bf16[32,2304]{1,0:T(8,128)(2,1)}, bf16[32,2304]{1,0:T(8,128)(2,1)S(1)}, u32[]{:S(2)}, u32[]{:S(2)}) %collective-permute-start.12) | collective-permute-done | bytes 147488 | tf_op jit(solution)/shard_map/ppermute | solution.py:590
  72.1 3.2 %collective-permute-done.13.refs_7_ = bf16[32,2304]{1,0:T(8,128)(2,1)S(1)} collective-permute-done((bf16[32,2304]{1,0:T(8,128)(2,1)}, bf16[32,2304]{1,0:T(8,128)(2,1)S(1)}, u32[]{:S(2)}, u32[]{:S(2)}) %collective-permute-start.13) | collective-permute-done | bytes 147488 | tf_op jit(solution)/shard_map/ppermute | solution.py:590
  75.2 3.2 %collective-permute-done.14.refs_8_ = bf16[32,2304]{1,0:T(8,128)(2,1)S(1)} collective-permute-done((bf16[32,2304]{1,0:T(8,128)(2,1)}, bf16[32,2304]{1,0:T(8,128)(2,1)S(1)}, u32[]{:S(2)}, u32[]{:S(2)}) %collective-permute-start.14) | collective-permute-done | bytes 147488 | tf_op jit(solution)/shard_map/ppermute | solution.py:590
  78.4 2.7 %collective-permute-done.15.refs_9_ = bf16[32,2304]{1,0:T(8,128)(2,1)S(1)} collective-permute-done((bf16[32,2304]{1,0:T(8,128)(2,1)}, bf16[32,2304]{1,0:T(8,128)(2,1)S(1)}, u32[]{:S(2)}, u32[]{:S(2)}) %collective-permute-start.15) | collective-permute-done | bytes 147488 | tf_op jit(solution)/shard_map/ppermute | solution.py:590
  84.5 14.0 %weight_grads.1 = (f32[512,768]{1,0:T(8,128)}, f32[512,768]{1,0:T(8,128)}, f32[768,512]{1,0:T(8,128)}) custom-call(s32[1]{0:T(128)} %bitcast.2.part_ref, bf16[144,3328]{1,0:T(8,128)(2,1)} %get-tuple-element.32.refs_0_, bf16[144,3328]{1,0:T(8,128)(2,1)} %collective-permute-done.7.refs_1_, bf16[32,2304]{1,0:T(8,128)(2,1)} %copy-done, ...), custom_call_target="tpu_custom_call" | custom-call | bytes 1179648 | tf_op jit(solution)/shard_map/weight_grads/pallas_call | solution.py:554
  98.5 2.4 %merge.1 = bf16[128,2048]{1,0:T(8,128)(2,1)} custom-call(s32[1,128]{1,0:T(1,128)} %bitcast.5, bf16[8,16,2304]{2,1,0:T(8,128)(2,1)} %all-to-all-done.back_ref), custom_call_target="tpu_custom_call" | custom-call | flops 134217728 | bytes 1048576 | tf_op jit(solution)/shard_map/merge/pallas_call | solution.py:231
  (72 shorter events, 8.8 us)
Async XLA Ops:
  3.6 8.9 %collective-permute-start = (bf16[32,2304]{1,0:T(8,128)(2,1)}, bf16[32,2304]{1,0:T(8,128)(2,1)S(1)}, u32[]{:S(2)}, u32[]{:S(2)}) collective-permute-start(bf16[32,2304]{1,0:T(8,128)(2,1)} %get-tuple-element.24), channel_id=1, source_target_pairs={{0,1},{1,0},{2,3},{3,2},{4,5},{5,4},{6,7},{7,6},{8,9},{9,8},{10,11... | collective-permute-start | bytes 442376 | tf_op jit(solution)/shard_map/ppermute | solution.py:590
  6.6 12.2 %collective-permute-start.1 = (bf16[32,2304]{1,0:T(8,128)(2,1)}, bf16[32,2304]{1,0:T(8,128)(2,1)S(1)}, u32[]{:S(2)}, u32[]{:S(2)}) collective-permute-start(bf16[32,2304]{1,0:T(8,128)(2,1)} %get-tuple-element.25), channel_id=1, source_target_pairs={{0,2},{1,3},{2,0},{3,1},{4,6},{5,7},{6,4},{7,5},{8,10},{9,11},{10,... | collective-permute-start | bytes 442376 | tf_op jit(solution)/shard_map/ppermute | solution.py:590
  8.2 11.7 %collective-permute-start.2 = (bf16[32,2304]{1,0:T(8,128)(2,1)}, bf16[32,2304]{1,0:T(8,128)(2,1)S(1)}, u32[]{:S(2)}, u32[]{:S(2)}) collective-permute-start(bf16[32,2304]{1,0:T(8,128)(2,1)} %get-tuple-element.26), channel_id=1, source_target_pairs={{0,3},{1,2},{2,1},{3,0},{4,7},{5,6},{6,5},{7,4},{8,11},{9,10},{10,... | collective-permute-start | bytes 442376 | tf_op jit(solution)/shard_map/ppermute | solution.py:590
  8.2 11.7 %collective-permute-start.3 = (bf16[32,2304]{1,0:T(8,128)(2,1)}, bf16[32,2304]{1,0:T(8,128)(2,1)S(1)}, u32[]{:S(2)}, u32[]{:S(2)}) collective-permute-start(bf16[32,2304]{1,0:T(8,128)(2,1)} %get-tuple-element.27), channel_id=1, source_target_pairs={{0,4},{1,5},{2,6},{3,7},{4,0},{5,1},{6,2},{7,3},{8,12},{9,13},{10,... | collective-permute-start | bytes 442376 | tf_op jit(solution)/shard_map/ppermute | solution.py:590
  11.2 21.7 %collective-permute-start.4 = (bf16[32,2304]{1,0:T(8,128)(2,1)}, bf16[32,2304]{1,0:T(8,128)(2,1)S(1)}, u32[]{:S(2)}, u32[]{:S(2)}) collective-permute-start(bf16[32,2304]{1,0:T(8,128)(2,1)} %get-tuple-element.28), channel_id=1, source_target_pairs={{0,5},{1,4},{2,7},{3,6},{4,1},{5,0},{6,3},{7,2},{8,13},{9,12},{10,... | collective-permute-start | bytes 442376 | tf_op jit(solution)/shard_map/ppermute | solution.py:590
  12.5 20.4 %collective-permute-start.5 = (bf16[32,2304]{1,0:T(8,128)(2,1)}, bf16[32,2304]{1,0:T(8,128)(2,1)}, u32[]{:S(2)}, u32[]{:S(2)}) collective-permute-start(bf16[32,2304]{1,0:T(8,128)(2,1)} %get-tuple-element.29), channel_id=1, source_target_pairs={{0,6},{1,7},{2,4},{3,5},{4,2},{5,3},{6,0},{7,1},{8,14},{9,15},{10,... | collective-permute-start | bytes 442376 | tf_op jit(solution)/shard_map/ppermute | solution.py:590
  18.8 14.1 %collective-permute-start.6 = (bf16[32,2304]{1,0:T(8,128)(2,1)}, bf16[32,2304]{1,0:T(8,128)(2,1)}, u32[]{:S(2)}, u32[]{:S(2)}) collective-permute-start(bf16[32,2304]{1,0:T(8,128)(2,1)} %get-tuple-element.30), channel_id=1, source_target_pairs={{0,7},{1,6},{2,5},{3,4},{4,3},{5,2},{6,1},{7,0},{8,15},{9,14},{10,... | collective-permute-start | bytes 442376 | tf_op jit(solution)/shard_map/ppermute | solution.py:590
  44.3 54.1 %all-to-all-start = ((bf16[8,16,2304]{2,1,0:T(8,128)(2,1)}), bf16[8,16,2304]{2,1,0:T(8,128)(2,1)}, u32[]{:S(2)}, u32[]{:S(2)}) async-start(bf16[8,16,2304]{2,1,0:T(8,128)(2,1)} %get-tuple-element.31), calls=%async_computation | async-start | bytes 1179648 | tf_op jit(solution)/shard_map/all_to_all | solution.py:594
  52.5 31.4 %collective-permute-start.7 = (bf16[144,3328]{1,0:T(8,128)(2,1)}, bf16[144,3328]{1,0:T(8,128)(2,1)}, u32[]{:S(2)}, u32[]{:S(2)}) collective-permute-start(bf16[144,3328]{1,0:T(8,128)(2,1)} %get-tuple-element.33), channel_id=1, source_target_pairs={{0,8},{8,0},{16,24},{24,16},{1,9},{9,1},{17,25},{25,17},{2,10},{10... | collective-permute-start | bytes 2875400 | tf_op jit(solution)/shard_map/ppermute | solution.py:590
  52.5 6.9 %collective-permute-start.8 = (bf16[32,2304]{1,0:T(8,128)(2,1)}, bf16[32,2304]{1,0:T(8,128)(2,1)S(1)}, u32[]{:S(2)}, u32[]{:S(2)}) collective-permute-start(bf16[32,2304]{1,0:T(8,128)(2,1)} %get-tuple-element.23.refs_0_), channel_id=1, source_target_pairs={{0,16},{8,24},{16,0},{24,8},{1,17},{9,25},{17,1},{25,9},{2,18},{10... | collective-permute-start | bytes 442376 | tf_op jit(solution)/shard_map/ppermute | solution.py:590
  54.1 8.5 %collective-permute-start.9 = (bf16[32,2304]{1,0:T(8,128)(2,1)}, bf16[32,2304]{1,0:T(8,128)(2,1)S(1)}, u32[]{:S(2)}, u32[]{:S(2)}) collective-permute-start(bf16[32,2304]{1,0:T(8,128)(2,1)} %copy-done.10), channel_id=1, source_target_pairs={{0,16},{8,24},{16,0},{24,8},{1,17},{9,25},{17,1},{25,9},{2,18},{10... | collective-permute-start | bytes 442376 | tf_op jit(solution)/shard_map/ppermute | solution.py:590
  54.6 11.2 %collective-permute-start.10 = (bf16[32,2304]{1,0:T(8,128)(2,1)}, bf16[32,2304]{1,0:T(8,128)(2,1)S(1)}, u32[]{:S(2)}, u32[]{:S(2)}) collective-permute-start(bf16[32,2304]{1,0:T(8,128)(2,1)} %copy-done.9), channel_id=1, source_target_pairs={{0,16},{8,24},{16,0},{24,8},{1,17},{9,25},{17,1},{25,9},{2,18},{10... | collective-permute-start | bytes 442376 | tf_op jit(solution)/shard_map/ppermute | solution.py:590
  56.1 12.8 %collective-permute-start.11 = (bf16[32,2304]{1,0:T(8,128)(2,1)}, bf16[32,2304]{1,0:T(8,128)(2,1)S(1)}, u32[]{:S(2)}, u32[]{:S(2)}) collective-permute-start(bf16[32,2304]{1,0:T(8,128)(2,1)} %copy-done.7), channel_id=1, source_target_pairs={{0,16},{8,24},{16,0},{24,8},{1,17},{9,25},{17,1},{25,9},{2,18},{10... | collective-permute-start | bytes 442376 | tf_op jit(solution)/shard_map/ppermute | solution.py:590
  59.4 12.6 %collective-permute-start.12 = (bf16[32,2304]{1,0:T(8,128)(2,1)}, bf16[32,2304]{1,0:T(8,128)(2,1)S(1)}, u32[]{:S(2)}, u32[]{:S(2)}) collective-permute-start(bf16[32,2304]{1,0:T(8,128)(2,1)} %copy-done.6), channel_id=1, source_target_pairs={{0,16},{8,24},{16,0},{24,8},{1,17},{9,25},{17,1},{25,9},{2,18},{10... | collective-permute-start | bytes 442376 | tf_op jit(solution)/shard_map/ppermute | solution.py:590
  62.6 12.6 %collective-permute-start.13 = (bf16[32,2304]{1,0:T(8,128)(2,1)}, bf16[32,2304]{1,0:T(8,128)(2,1)S(1)}, u32[]{:S(2)}, u32[]{:S(2)}) collective-permute-start(bf16[32,2304]{1,0:T(8,128)(2,1)} %copy-done.4), channel_id=1, source_target_pairs={{0,16},{8,24},{16,0},{24,8},{1,17},{9,25},{17,1},{25,9},{2,18},{10... | collective-permute-start | bytes 442376 | tf_op jit(solution)/shard_map/ppermute | solution.py:590
  65.7 12.6 %collective-permute-start.14 = (bf16[32,2304]{1,0:T(8,128)(2,1)}, bf16[32,2304]{1,0:T(8,128)(2,1)S(1)}, u32[]{:S(2)}, u32[]{:S(2)}) collective-permute-start(bf16[32,2304]{1,0:T(8,128)(2,1)} %collective-permute-done.5.refs_6_), channel_id=1, source_target_pairs={{0,16},{8,24},{16,0},{24,8},{1,17},{9,25},{17,1},{25,9},{2,18},{10... | collective-permute-start | bytes 442376 | tf_op jit(solution)/shard_map/ppermute | solution.py:590
  68.9 12.2 %collective-permute-start.15 = (bf16[32,2304]{1,0:T(8,128)(2,1)}, bf16[32,2304]{1,0:T(8,128)(2,1)S(1)}, u32[]{:S(2)}, u32[]{:S(2)}) collective-permute-start(bf16[32,2304]{1,0:T(8,128)(2,1)} %collective-permute-done.6.refs_7_), channel_id=1, source_target_pairs={{0,16},{8,24},{16,0},{24,8},{1,17},{9,25},{17,1},{25,9},{2,18},{10... | collective-permute-start | bytes 442376 | tf_op jit(solution)/shard_map/ppermute | solution.py:590
  72.1 9.0 %collective-permute-start.16 = (bf16[32,2304]{1,0:T(8,128)(2,1)S(1)}, bf16[32,2304]{1,0:T(8,128)(2,1)S(1)}, u32[]{:S(2)}, u32[]{:S(2)}) collective-permute-start(bf16[32,2304]{1,0:T(8,128)(2,1)S(1)} %collective-permute-done.8.refs_2_), channel_id=1, source_target_pairs={{0,8},{8,0},{16,24},{24,16},{1,9},{9,1},{17,25},{25,17},{2,10},{10... | collective-permute-start | bytes 442376 | tf_op jit(solution)/shard_map/ppermute | solution.py:590
  75.2 6.4 %collective-permute-start.17 = (bf16[32,2304]{1,0:T(8,128)(2,1)S(1)}, bf16[32,2304]{1,0:T(8,128)(2,1)S(1)}, u32[]{:S(2)}, u32[]{:S(2)}) collective-permute-start(bf16[32,2304]{1,0:T(8,128)(2,1)S(1)} %collective-permute-done.9.refs_3_), channel_id=1, source_target_pairs={{0,8},{8,0},{16,24},{24,16},{1,9},{9,1},{17,25},{25,17},{2,10},{10... | collective-permute-start | bytes 442376 | tf_op jit(solution)/shard_map/ppermute | solution.py:590
  78.4 3.4 %collective-permute-start.18 = (bf16[32,2304]{1,0:T(8,128)(2,1)S(1)}, bf16[32,2304]{1,0:T(8,128)(2,1)S(1)}, u32[]{:S(2)}, u32[]{:S(2)}) collective-permute-start(bf16[32,2304]{1,0:T(8,128)(2,1)S(1)} %collective-permute-done.10.refs_4_), channel_id=1, source_target_pairs={{0,8},{8,0},{16,24},{24,16},{1,9},{9,1},{17,25},{25,17},{2,10},{10... | collective-permute-start | bytes 442376 | tf_op jit(solution)/shard_map/ppermute | solution.py:590
  81.1 1.6 %collective-permute-start.20 = (bf16[32,2304]{1,0:T(8,128)(2,1)S(1)}, bf16[32,2304]{1,0:T(8,128)(2,1)S(1)}, u32[]{:S(2)}, u32[]{:S(2)}) collective-permute-start(bf16[32,2304]{1,0:T(8,128)(2,1)S(1)} %collective-permute-done.12.refs_6_), channel_id=1, source_target_pairs={{0,8},{8,0},{16,24},{24,16},{1,9},{9,1},{17,25},{25,17},{2,10},{10... | collective-permute-start | bytes 442376 | tf_op jit(solution)/shard_map/ppermute | solution.py:590
  81.7 1.4 %collective-permute-start.21 = (bf16[32,2304]{1,0:T(8,128)(2,1)S(1)}, bf16[32,2304]{1,0:T(8,128)(2,1)S(1)}, u32[]{:S(2)}, u32[]{:S(2)}) collective-permute-start(bf16[32,2304]{1,0:T(8,128)(2,1)S(1)} %collective-permute-done.13.refs_7_), channel_id=1, source_target_pairs={{0,8},{8,0},{16,24},{24,16},{1,9},{9,1},{17,25},{25,17},{2,10},{10... | collective-permute-start | bytes 442376 | tf_op jit(solution)/shard_map/ppermute | solution.py:590
  81.8 1.5 %collective-permute-start.22 = (bf16[32,2304]{1,0:T(8,128)(2,1)S(1)}, bf16[32,2304]{1,0:T(8,128)(2,1)S(1)}, u32[]{:S(2)}, u32[]{:S(2)}) collective-permute-start(bf16[32,2304]{1,0:T(8,128)(2,1)S(1)} %collective-permute-done.14.refs_8_), channel_id=1, source_target_pairs={{0,8},{8,0},{16,24},{24,16},{1,9},{9,1},{17,25},{25,17},{2,10},{10... | collective-permute-start | bytes 442376 | tf_op jit(solution)/shard_map/ppermute | solution.py:590
  82.5 1.4 %collective-permute-start.23 = (bf16[32,2304]{1,0:T(8,128)(2,1)S(1)}, bf16[32,2304]{1,0:T(8,128)(2,1)S(1)}, u32[]{:S(2)}, u32[]{:S(2)}) collective-permute-start(bf16[32,2304]{1,0:T(8,128)(2,1)S(1)} %collective-permute-done.15.refs_9_), channel_id=1, source_target_pairs={{0,8},{8,0},{16,24},{24,16},{1,9},{9,1},{17,25},{25,17},{2,10},{10... | collective-permute-start | bytes 442376 | tf_op jit(solution)/shard_map/ppermute | solution.py:590
  (22 other events, 171.5 us)

commit v12 on v11

--- a/solution.py
+++ b/solution.py
@@ -205,6 +205,26 @@
     )(me, *sources)
 
 
+def join(received):
+    count = len(received)
+
+    def kernel(*refs):
+        pairs = [(refs[at], refs[count].at[at]) for at in range(count)]
+        start(pairs, refs[-1])
+        wait(pairs, refs[-1])
+
+    return pl.pallas_call(
+        kernel,
+        out_shape=jax.ShapeDtypeStruct((count,) + received[0].shape, jnp.bfloat16),
+        in_specs=anywhere(count),
+        out_specs=pl.BlockSpec(memory_space=pltpu.VMEM),
+        scratch_shapes=[pltpu.SemaphoreType.DMA((count,))],
+        compiler_params=params(),
+        cost_estimate=cost(0, 4 * received[0].size * count),
+        name="join",
+    )(*received)
+
+
 def merge(routes, returned):
     blocks = returned.shape[0]
     tokens = routes.shape[1]
@@ -284,7 +304,15 @@
 
 def halves(group, half, out):
     here = slice(half * ROWS, (half + 1) * ROWS)
-    return [(block.at[here, :], out.at[at]) for at, block in enumerate(group)]
+    pairs, at = [], 0
+    for item in group:
+        if len(item.shape) == 2:
+            pairs.append((item.at[here, :], out.at[at]))
+            at += 1
+        else:
+            pairs.append((item.at[:, here, :], out.at[at : at + item.shape[0]]))
+            at += item.shape[0]
+    return pairs
 
 
 def hidden_grads(pre_gate, pre_up, d_hidden):
@@ -450,13 +478,14 @@
             pltpu.SemaphoreType.DMA((4,)),
         ],
         compiler_params=params(),
-        cost_estimate=cost(0, 4 * slots * width),
+        cost_estimate=cost(10 * slots * width * hid, 4 * slots * width),
         name="back",
     )(me, part, *group, gate_proj, up_proj, down_proj)
 
 
 def weight_grads(tile, share, part, known, groups, gate_proj, up_proj, down_proj):
-    count, blocks = len(groups), len(groups[0])
+    count, items = len(groups), len(groups[0])
+    blocks = sum(item.shape[0] if item.ndim == 3 else 1 for item in groups[0])
     given = len(known)
     hid, width = down_proj.shape
     pieces, step = cut(width)
@@ -467,7 +496,7 @@
     def kernel(part_ref, *refs):
         refs = list(refs)
         known_refs = [refs.pop(0) for _ in range(given)]
-        group_refs = [[refs.pop(0) for _ in range(blocks)] for _ in range(count)]
+        group_refs = [[refs.pop(0) for _ in range(items)] for _ in range(count)]
         gate_ref, up_ref, down_ref = [refs.pop(0) for _ in range(3)]
         d_gate_ref, d_up_ref, d_down_ref = [refs.pop(0) for _ in range(3)]
         x_held, dy_held, x_all, dy_all = [refs.pop(0) for _ in range(4)]
@@ -559,7 +588,7 @@
             jax.ShapeDtypeStruct((share, hid), jnp.float32),
             jax.ShapeDtypeStruct((hid, share), jnp.float32),
         ],
-        in_specs=[pl.BlockSpec(memory_space=pltpu.SMEM)] + anywhere(given + count * blocks + 3),
+        in_specs=[pl.BlockSpec(memory_space=pltpu.SMEM)] + anywhere(given + count * items + 3),
         out_specs=[column_tile(share, tile), column_tile(share, tile), row_tile(tile, share)],
         scratch_shapes=[
             held,
@@ -572,8 +601,8 @@
             pltpu.VMEM((tiles, width, tile), jnp.bfloat16),
             pltpu.VMEM((tiles, width, tile), jnp.bfloat16),
             pltpu.VMEM((tiles, tile, width), jnp.bfloat16),
-            pltpu.SemaphoreType.DMA((count * blocks,)),
-            pltpu.SemaphoreType.DMA((count * blocks,)),
+            pltpu.SemaphoreType.DMA((count * items,)),
+            pltpu.SemaphoreType.DMA((count * items,)),
             pltpu.SemaphoreType.DMA((3 * given,)),
             pltpu.SemaphoreType.DMA((tiles,)),
             pltpu.SemaphoreType.DMA((tiles,)),
@@ -582,7 +611,7 @@
         compiler_params=params(),
         cost_estimate=cost(0, 4 * slots * width),
         name="weight_grads",
-    )(part, *known, *[block for group in groups for block in group], gate_proj, up_proj, down_proj)
+    )(part, *known, *[item for group in groups for item in group], gate_proj, up_proj, down_proj)
 
 
 def swap(value, axis, distance):
@@ -609,11 +638,14 @@
     received = list(pack(blocks, me, routes, gates, tokens, cotangent))
     for distance in reversed(range(1, blocks)):
         received[distance] = swap(received[distance], "expert", distance)
-    far = [swap(block, "dp", 2) for block in received]
+    half = blocks // 2
+    far = swap(join(received[:half]), "dp", 2)
+    far_half = swap(join(received[half:]), "dp", 2)
     sent, kept, handed = back(tile, share, me, part, received, *weights)
+    sent, far = lax.optimization_barrier((sent, far))
     returned = exchange(sent)
-    far[4:] = after(far[4:], sent)
-    last = [swap(block, "dp", 1) for block in far]
+    far = [far, after(far_half, sent)]
+    last = [swap(item, "dp", 1) for item in far]
     known = [kept, swap(handed, "dp", 1)]
     grads = weight_grads(tile, share, part, known, [far, last], *weights)
     return (merge(routes, after(returned, *grads)), *grads)

time: 101 us -> 85.5 us (0.85)
  starting transfers between devices: 33.2 us -> 24.2 us
  waiting for transfers between devices: 35.5 us -> 26.6 us
  Pallas kernels: 30.1 us -> 33.6 us
  local copies, waits for them, and re-layouts: 1.28 us -> 0.01 us
    ppermute x24 -> x12, starting transfers between devices: 25 us -> 15.1 us  [swap(): lax.ppermute(value, axis, [(at, at ^ distance) for at in range(size)])]
    ppermute x24 -> x12, waiting for transfers between devices: 35.5 us -> 26.6 us  [swap(): lax.ppermute(value, axis, [(at, at ^ distance) for at in range(size)])]
    pallas_call x0 -> x2, Pallas kernels: none -> 3.94 us  [join(): pl.pallas_call(kernel, out_shape=jax.ShapeDtypeStruct((count,) + received...]
    unnamed x42 -> x4, local copies, waits for them, and re-layouts: 1.28 us -> 0.01 us
  transfers between devices with their start and end apart: 25 -> 13, of which waited for: 16 -> 8; matrix products, arithmetic and copies ran while one was open for 0% -> 0% of each run, Pallas kernels for 14% -> 31%
where the time goes in v12:
time: 85.5 us; the launch traced here: 85.2 us
  Pallas kernels  33.6 us (39%)
  waiting for transfers between devices  26.6 us (31%)
  starting transfers between devices  24.2 us (28%)
    ppermute x12, waiting for transfers between devices, swap(): lax.ppermute(value, axis, [(at, at ^ distance) for at in range(size)])  26.6 us
    ppermute x12, starting transfers between devices, swap(): lax.ppermute(value, axis, [(at, at ^ distance) for at in range(size)])  15.1 us
    pallas_call x1, Pallas kernels, weight_grads(): pl.pallas_call(kernel, grid=(tiles,), out_shape=[jax.ShapeDtypeStruct((sh...  13.6 us
    pallas_call x1, Pallas kernels, back(): pl.pallas_call(kernel, grid=(tiles + chunks,), out_shape=[jax.ShapeDtypeS...  10.8 us
    all_to_all x1, starting transfers between devices, exchange(): lax.all_to_all(blocks, 'expert', split_axis=0, concat_axis=0, tiled=True)  9.1 us
    pallas_call x2, Pallas kernels, join(): pl.pallas_call(kernel, out_shape=jax.ShapeDtypeStruct((count,) + received...  3.94 us
    pallas_call x1, Pallas kernels, pack(): pl.pallas_call(kernel, out_shape=[jax.ShapeDtypeStruct((2 * ROWS, width +...  3 us
    pallas_call x1, Pallas kernels, merge(): pl.pallas_call(kernel, out_shape=jax.ShapeDtypeStruct((tokens, width), jn...  2.36 us
  transfers between devices with their start and end apart: 13, of which 8 were waited for; matrix products, arithmetic and copies ran while one was open for 0% of the time, Pallas kernels for 31%

profile of v12, /device:TPU:0, one launch (start us, length us, event | category | flops | bytes accessed | tf_op | source)
XLA Modules:
  0.0 85.2 jit_solution(3124594560604022590)
XLA Ops:
  0.6 3.0 %pack.1 = (bf16[32,2304]{1,0:T(8,128)(2,1)}, bf16[32,2304]{1,0:T(8,128)(2,1)}, bf16[32,2304]{1,0:T(8,128)(2,1)}, bf16[32,2304]{1,0:T(8,128)(2,1)}, bf16[32,2304]...) custom-call(s32[1]{0:T(128)} %bitcast.1.me_ref, ...), custom_call_target="tpu_custom_call" | custom-call | flops 268435456 | bytes 2097152 | tf_op jit(solution)/shard_map/pack/pallas_call | solution.py:195
  3.6 3.0 %collective-permute-start = (bf16[32,2304]{1,0:T(8,128)(2,1)}, bf16[32,2304]{1,0:T(8,128)(2,1)S(1)}, u32[]{:S(2)}, u32[]{:S(2)}) collective-permute-start(bf16[32,2304]{1,0:T(8,128)(2,1)} %get-tuple-element.23), channel_id=1, source_target_pairs={{0,1},{1,0},{2,3},{3,2},{4,5},{5,4},{6,7},{7,6},{8,9},{9,8},{10,11... | collective-permute-start | bytes 442376 | tf_op jit(solution)/shard_map/ppermute | solution.py:619
  6.6 1.6 %collective-permute-start.1 = (bf16[32,2304]{1,0:T(8,128)(2,1)}, bf16[32,2304]{1,0:T(8,128)(2,1)}, u32[]{:S(2)}, u32[]{:S(2)}) collective-permute-start(bf16[32,2304]{1,0:T(8,128)(2,1)} %get-tuple-element.24), channel_id=1, source_target_pairs={{0,2},{1,3},{2,0},{3,1},{4,6},{5,7},{6,4},{7,5},{8,10},{9,11},{10,... | collective-permute-start | bytes 442376 | tf_op jit(solution)/shard_map/ppermute | solution.py:619
  8.2 2.5 %collective-permute-done.refs_1_ = bf16[32,2304]{1,0:T(8,128)(2,1)S(1)} collective-permute-done((bf16[32,2304]{1,0:T(8,128)(2,1)}, bf16[32,2304]{1,0:T(8,128)(2,1)S(1)}, u32[]{:S(2)}, u32[]{:S(2)}) %collective-permute-start) | collective-permute-done | bytes 147488 | tf_op jit(solution)/shard_map/ppermute | solution.py:619
  10.7 3.0 %collective-permute-done.1.refs_2_ = bf16[32,2304]{1,0:T(8,128)(2,1)} collective-permute-done((bf16[32,2304]{1,0:T(8,128)(2,1)}, bf16[32,2304]{1,0:T(8,128)(2,1)}, u32[]{:S(2)}, u32[]{:S(2)}) %collective-permute-start.1) | collective-permute-done | bytes 147488 | tf_op jit(solution)/shard_map/ppermute | solution.py:619
  13.7 1.5 %collective-permute-done.2.refs_3_ = bf16[32,2304]{1,0:T(8,128)(2,1)} collective-permute-done((bf16[32,2304]{1,0:T(8,128)(2,1)}, bf16[32,2304]{1,0:T(8,128)(2,1)}, u32[]{:S(2)}, u32[]{:S(2)}) %collective-permute-start.2) | collective-permute-done | bytes 147488 | tf_op jit(solution)/shard_map/ppermute | solution.py:619
  15.2 2.0 %join.2 = bf16[4,32,2304]{2,1,0:T(8,128)(2,1)} custom-call(bf16[32,2304]{1,0:T(8,128)(2,1)} %get-tuple-element.22.refs_0_, bf16[32,2304]{1,0:T(8,128)(2,1)} %copy-done, bf16[32,2304]{1,0:T(8,128)(2,1)} %collective-permute-done.1.refs_2_, bf16[32,2304]{1,0:T(8,128)(2,1)} %collective-permute-done.2.refs_3_), custom_call_target="tpu_custom_call" | custom-call | bytes 1179648 | tf_op jit(solution)/shard_map/join/pallas_call | solution.py:216
  17.2 1.8 %collective-permute-start.7 = (bf16[4,32,2304]{2,1,0:T(8,128)(2,1)}, bf16[4,32,2304]{2,1,0:T(8,128)(2,1)}, u32[]{:S(2)}, u32[]{:S(2)}) collective-permute-start(bf16[4,32,2304]{2,1,0:T(8,128)(2,1)} %join.2), channel_id=1, source_target_pairs={{0,16},{8,24},{16,0},{24,8},{1,17},{9,25},{17,1},{25,9},{2,18},{10... | collective-permute-start | bytes 1769480 | tf_op jit(solution)/shard_map/ppermute | solution.py:619
  19.0 2.6 %collective-permute-start.3 = (bf16[32,2304]{1,0:T(8,128)(2,1)}, bf16[32,2304]{1,0:T(8,128)(2,1)S(1)}, u32[]{:S(2)}, u32[]{:S(2)}) collective-permute-start(bf16[32,2304]{1,0:T(8,128)(2,1)} %get-tuple-element.26), channel_id=1, source_target_pairs={{0,4},{1,5},{2,6},{3,7},{4,0},{5,1},{6,2},{7,3},{8,12},{9,13},{10,... | collective-permute-start | bytes 442376 | tf_op jit(solution)/shard_map/ppermute | solution.py:619
  21.6 1.3 %collective-permute-start.4 = (bf16[32,2304]{1,0:T(8,128)(2,1)}, bf16[32,2304]{1,0:T(8,128)(2,1)}, u32[]{:S(2)}, u32[]{:S(2)}) collective-permute-start(bf16[32,2304]{1,0:T(8,128)(2,1)} %get-tuple-element.27), channel_id=1, source_target_pairs={{0,5},{1,4},{2,7},{3,6},{4,1},{5,0},{6,3},{7,2},{8,13},{9,12},{10,... | collective-permute-start | bytes 442376 | tf_op jit(solution)/shard_map/ppermute | solution.py:619
  22.8 3.6 %collective-permute-start.5 = (bf16[32,2304]{1,0:T(8,128)(2,1)}, bf16[32,2304]{1,0:T(8,128)(2,1)}, u32[]{:S(2)}, u32[]{:S(2)}) collective-permute-start(bf16[32,2304]{1,0:T(8,128)(2,1)} %get-tuple-element.28), channel_id=1, source_target_pairs={{0,6},{1,7},{2,4},{3,5},{4,2},{5,3},{6,0},{7,1},{8,14},{9,15},{10,... | collective-permute-start | bytes 442376 | tf_op jit(solution)/shard_map/ppermute | solution.py:619
  26.4 0.2 collective-permute-start.6
  26.6 11.4 %collective-permute-done.3.refs_4_.refs_0_ = bf16[32,2304]{1,0:T(8,128)(2,1)S(1)} collective-permute-done((bf16[32,2304]{1,0:T(8,128)(2,1)}, bf16[32,2304]{1,0:T(8,128)(2,1)S(1)}, u32[]{:S(2)}, u32[]{:S(2)}) %collective-permute-start.3) | collective-permute-done | bytes 147488 | tf_op jit(solution)/shard_map/ppermute | solution.py:619
  38.0 4.2 %collective-permute-done.4.refs_5_.refs_1_ = bf16[32,2304]{1,0:T(8,128)(2,1)} collective-permute-done((bf16[32,2304]{1,0:T(8,128)(2,1)}, bf16[32,2304]{1,0:T(8,128)(2,1)}, u32[]{:S(2)}, u32[]{:S(2)}) %collective-permute-start.4) | collective-permute-done | bytes 147488 | tf_op jit(solution)/shard_map/ppermute | solution.py:619
  42.2 2.0 %join.3 = bf16[4,32,2304]{2,1,0:T(8,128)(2,1)} custom-call(bf16[32,2304]{1,0:T(8,128)(2,1)} %copy-done.1, bf16[32,2304]{1,0:T(8,128)(2,1)} %collective-permute-done.4.refs_5_.refs_1_, bf16[32,2304]{1,0:T(8,128)(2,1)} %collective-permute-done.5.refs_6_.refs_2_, bf16[32,2304]{1,0:T(8,128)(2,1)} %collective-permute-done.6.refs_7_.refs_3_), custom_call_target="tpu_custom_call" | custom-call | bytes 1179648 | tf_op jit(solution)/shard_map/join/pallas_call | solution.py:216
  44.2 0.6 collective-permute-start.9
  44.8 10.8 %back.1 = (bf16[8,16,2304]{2,1,0:T(8,128)(2,1)}, bf16[144,3328]{1,0:T(8,128)(2,1)}, bf16[144,3328]{1,0:T(8,128)(2,1)}) custom-call(s32[1]{0:T(128)} %bitcast.1.me_ref, s32[1]{0:T(128)} %bitcast.2.part_ref, bf16[32,2304]{1,0:T(8,128)(2,1)} %get-tuple-element.22.refs_0_, bf16[32,2304]{1,0:T(8,128)(2,1)} %copy-done, ...), custom_call_target="tpu_custom_call" | custom-call | flops 2264924160 | bytes 1179648 | tf_op jit(solution)/shard_map/back/pallas_call | solution.py:450
  55.5 9.1 %all-to-all-start = ((bf16[8,16,2304]{2,1,0:T(8,128)(2,1)}), bf16[8,16,2304]{2,1,0:T(8,128)(2,1)}, u32[]{:S(2)}, u32[]{:S(2)}) async-start(bf16[8,16,2304]{2,1,0:T(8,128)(2,1)} %get-tuple-element.31), calls=%async_computation | async-start | bytes 1179648 | tf_op jit(solution)/shard_map/all_to_all | solution.py:623
  64.7 0.5 collective-permute-start.11
  65.2 2.3 %collective-permute-done.8.refs_1_ = bf16[144,3328]{1,0:T(8,128)(2,1)} collective-permute-done((bf16[144,3328]{1,0:T(8,128)(2,1)}, bf16[144,3328]{1,0:T(8,128)(2,1)}, u32[]{:S(2)}, u32[]{:S(2)}) %collective-permute-start.8) | collective-permute-done | bytes 958496 | tf_op jit(solution)/shard_map/ppermute | solution.py:619
  67.5 0.8 collective-permute-done.11.refs_5_
  68.4 0.8 collective-permute-done.10.refs_4_
  69.2 13.6 %weight_grads.1 = (f32[512,768]{1,0:T(8,128)}, f32[512,768]{1,0:T(8,128)}, f32[768,512]{1,0:T(8,128)}) custom-call(s32[1]{0:T(128)} %bitcast.2.part_ref, bf16[144,3328]{1,0:T(8,128)(2,1)} %get-tuple-element.32.refs_0_, bf16[144,3328]{1,0:T(8,128)(2,1)} %collective-permute-done.8.refs_1_, bf16[4,32,2304]{2,1,0:T(8,128)(2,1)} %collective-permute-done.7.refs_2_, ...), custom_call_target="tpu_custom_call" | custom-call | bytes 1179648 | tf_op jit(solution)/shard_map/weight_grads/pallas_call | solution.py:583
  82.8 2.4 %merge.1 = bf16[128,2048]{1,0:T(8,128)(2,1)} custom-call(s32[1,128]{1,0:T(1,128)} %bitcast.5, bf16[8,16,2304]{2,1,0:T(8,128)(2,1)} %all-to-all-done.back_ref), custom_call_target="tpu_custom_call" | custom-call | flops 134217728 | bytes 1048576 | tf_op jit(solution)/shard_map/merge/pallas_call | solution.py:251
  (12 shorter events, 0.1 us)
Async XLA Ops:
  3.6 7.1 %collective-permute-start = (bf16[32,2304]{1,0:T(8,128)(2,1)}, bf16[32,2304]{1,0:T(8,128)(2,1)S(1)}, u32[]{:S(2)}, u32[]{:S(2)}) collective-permute-start(bf16[32,2304]{1,0:T(8,128)(2,1)} %get-tuple-element.23), channel_id=1, source_target_pairs={{0,1},{1,0},{2,3},{3,2},{4,5},{5,4},{6,7},{7,6},{8,9},{9,8},{10,11... | collective-permute-start | bytes 442376 | tf_op jit(solution)/shard_map/ppermute | solution.py:619
  6.6 7.1 %collective-permute-start.1 = (bf16[32,2304]{1,0:T(8,128)(2,1)}, bf16[32,2304]{1,0:T(8,128)(2,1)}, u32[]{:S(2)}, u32[]{:S(2)}) collective-permute-start(bf16[32,2304]{1,0:T(8,128)(2,1)} %get-tuple-element.24), channel_id=1, source_target_pairs={{0,2},{1,3},{2,0},{3,1},{4,6},{5,7},{6,4},{7,5},{8,10},{9,11},{10,... | collective-permute-start | bytes 442376 | tf_op jit(solution)/shard_map/ppermute | solution.py:619
  8.2 7.0 %collective-permute-start.2 = (bf16[32,2304]{1,0:T(8,128)(2,1)}, bf16[32,2304]{1,0:T(8,128)(2,1)}, u32[]{:S(2)}, u32[]{:S(2)}) collective-permute-start(bf16[32,2304]{1,0:T(8,128)(2,1)} %get-tuple-element.25), channel_id=1, source_target_pairs={{0,3},{1,2},{2,1},{3,0},{4,7},{5,6},{6,5},{7,4},{8,11},{9,10},{10,... | collective-permute-start | bytes 442376 | tf_op jit(solution)/shard_map/ppermute | solution.py:619
  10.7 4.5 %copy-start = (bf16[32,2304]{1,0:T(8,128)(2,1)}, bf16[32,2304]{1,0:T(8,128)(2,1)S(1)}, u32[]{:S(2)}) copy-start(bf16[32,2304]{1,0:T(8,128)(2,1)S(1)} %collective-permute-done.refs_1_) | copy-start | bytes 442372
  17.2 38.3 %collective-permute-start.7 = (bf16[4,32,2304]{2,1,0:T(8,128)(2,1)}, bf16[4,32,2304]{2,1,0:T(8,128)(2,1)}, u32[]{:S(2)}, u32[]{:S(2)}) collective-permute-start(bf16[4,32,2304]{2,1,0:T(8,128)(2,1)} %join.2), channel_id=1, source_target_pairs={{0,16},{8,24},{16,0},{24,8},{1,17},{9,25},{17,1},{25,9},{2,18},{10... | collective-permute-start | bytes 1769480 | tf_op jit(solution)/shard_map/ppermute | solution.py:619
  19.0 19.0 %collective-permute-start.3 = (bf16[32,2304]{1,0:T(8,128)(2,1)}, bf16[32,2304]{1,0:T(8,128)(2,1)S(1)}, u32[]{:S(2)}, u32[]{:S(2)}) collective-permute-start(bf16[32,2304]{1,0:T(8,128)(2,1)} %get-tuple-element.26), channel_id=1, source_target_pairs={{0,4},{1,5},{2,6},{3,7},{4,0},{5,1},{6,2},{7,3},{8,12},{9,13},{10,... | collective-permute-start | bytes 442376 | tf_op jit(solution)/shard_map/ppermute | solution.py:619
  21.6 20.6 %collective-permute-start.4 = (bf16[32,2304]{1,0:T(8,128)(2,1)}, bf16[32,2304]{1,0:T(8,128)(2,1)}, u32[]{:S(2)}, u32[]{:S(2)}) collective-permute-start(bf16[32,2304]{1,0:T(8,128)(2,1)} %get-tuple-element.27), channel_id=1, source_target_pairs={{0,5},{1,4},{2,7},{3,6},{4,1},{5,0},{6,3},{7,2},{8,13},{9,12},{10,... | collective-permute-start | bytes 442376 | tf_op jit(solution)/shard_map/ppermute | solution.py:619
  22.8 19.4 %collective-permute-start.5 = (bf16[32,2304]{1,0:T(8,128)(2,1)}, bf16[32,2304]{1,0:T(8,128)(2,1)}, u32[]{:S(2)}, u32[]{:S(2)}) collective-permute-start(bf16[32,2304]{1,0:T(8,128)(2,1)} %get-tuple-element.28), channel_id=1, source_target_pairs={{0,6},{1,7},{2,4},{3,5},{4,2},{5,3},{6,0},{7,1},{8,14},{9,15},{10,... | collective-permute-start | bytes 442376 | tf_op jit(solution)/shard_map/ppermute | solution.py:619
  26.4 15.8 %collective-permute-start.6 = (bf16[32,2304]{1,0:T(8,128)(2,1)}, bf16[32,2304]{1,0:T(8,128)(2,1)}, u32[]{:S(2)}, u32[]{:S(2)}) collective-permute-start(bf16[32,2304]{1,0:T(8,128)(2,1)} %get-tuple-element.29), channel_id=1, source_target_pairs={{0,7},{1,6},{2,5},{3,4},{4,3},{5,2},{6,1},{7,0},{8,15},{9,14},{10,... | collective-permute-start | bytes 442376 | tf_op jit(solution)/shard_map/ppermute | solution.py:619
  38.0 4.2 %copy-start.1 = (bf16[32,2304]{1,0:T(8,128)(2,1)}, bf16[32,2304]{1,0:T(8,128)(2,1)S(1)}, u32[]{:S(2)}) copy-start(bf16[32,2304]{1,0:T(8,128)(2,1)S(1)} %collective-permute-done.3.refs_4_.refs_0_) | copy-start | bytes 442372
  44.2 20.5 %collective-permute-start.9 = (bf16[4,32,2304]{2,1,0:T(8,128)(2,1)}, bf16[4,32,2304]{2,1,0:T(8,128)(2,1)}, u32[]{:S(2)}, u32[]{:S(2)}) collective-permute-start(bf16[4,32,2304]{2,1,0:T(8,128)(2,1)} %join.3), channel_id=1, source_target_pairs={{0,16},{8,24},{16,0},{24,8},{1,17},{9,25},{17,1},{25,9},{2,18},{10... | collective-permute-start | bytes 1769480 | tf_op jit(solution)/shard_map/ppermute | solution.py:619
  55.5 27.3 %all-to-all-start = ((bf16[8,16,2304]{2,1,0:T(8,128)(2,1)}), bf16[8,16,2304]{2,1,0:T(8,128)(2,1)}, u32[]{:S(2)}, u32[]{:S(2)}) async-start(bf16[8,16,2304]{2,1,0:T(8,128)(2,1)} %get-tuple-element.31), calls=%async_computation | async-start | bytes 1179648 | tf_op jit(solution)/shard_map/all_to_all | solution.py:623
  64.6 2.9 %collective-permute-start.8 = (bf16[144,3328]{1,0:T(8,128)(2,1)}, bf16[144,3328]{1,0:T(8,128)(2,1)}, u32[]{:S(2)}, u32[]{:S(2)}) collective-permute-start(bf16[144,3328]{1,0:T(8,128)(2,1)} %get-tuple-element.33), channel_id=1, source_target_pairs={{0,8},{8,0},{16,24},{24,16},{1,9},{9,1},{17,25},{25,17},{2,10},{10... | collective-permute-start | bytes 2875400 | tf_op jit(solution)/shard_map/ppermute | solution.py:619
  64.7 3.7 %collective-permute-start.11 = (bf16[4,32,2304]{2,1,0:T(8,128)(2,1)}, bf16[4,32,2304]{2,1,0:T(8,128)(2,1)}, u32[]{:S(2)}, u32[]{:S(2)}) collective-permute-start(bf16[4,32,2304]{2,1,0:T(8,128)(2,1)} %collective-permute-done.9.refs_3_), channel_id=1, source_target_pairs={{0,8},{8,0},{16,24},{24,16},{1,9},{9,1},{17,25},{25,17},{2,10},{10... | collective-permute-start | bytes 1769480 | tf_op jit(solution)/shard_map/ppermute | solution.py:619
  65.2 4.0 %collective-permute-start.10 = (bf16[4,32,2304]{2,1,0:T(8,128)(2,1)}, bf16[4,32,2304]{2,1,0:T(8,128)(2,1)}, u32[]{:S(2)}, u32[]{:S(2)}) collective-permute-start(bf16[4,32,2304]{2,1,0:T(8,128)(2,1)} %collective-permute-done.7.refs_2_), channel_id=1, source_target_pairs={{0,8},{8,0},{16,24},{24,16},{1,9},{9,1},{17,25},{25,17},{2,10},{10... | collective-permute-start | bytes 1769480 | tf_op jit(solution)/shard_map/ppermute | solution.py:619

commit v13 on v12

--- a/solution.py
+++ b/solution.py
@@ -478,7 +478,7 @@
             pltpu.SemaphoreType.DMA((4,)),
         ],
         compiler_params=params(),
-        cost_estimate=cost(10 * slots * width * hid, 4 * slots * width),
+        cost_estimate=cost(50 * slots * width * hid, 4 * slots * width),
         name="back",
     )(me, part, *group, gate_proj, up_proj, down_proj)
 

time: 85.5 us -> 76.9 us (0.90)
  waiting for transfers between devices: 26.6 us -> 16.2 us
  starting transfers between devices: 24.2 us -> 25.9 us
    ppermute x12, waiting for transfers between devices: 26.6 us -> 16.2 us  [swap(): lax.ppermute(value, axis, [(at, at ^ distance) for at in range(size)])]
    ppermute x12, starting transfers between devices: 15.1 us -> 17.3 us  [swap(): lax.ppermute(value, axis, [(at, at ^ distance) for at in range(size)])]
  transfers between devices with their start and end apart: 13 -> 13, of which waited for: 8 -> 6; matrix products, arithmetic and copies ran while one was open for 0% -> 0% of each run, Pallas kernels for 31% -> 37%
where the time goes in v13:
time: 76.9 us; the launch traced here: 76.5 us
  Pallas kernels  33.6 us (44%)
  starting transfers between devices  25.9 us (34%)
  waiting for transfers between devices  16.2 us (21%)
    ppermute x12, starting transfers between devices, swap(): lax.ppermute(value, axis, [(at, at ^ distance) for at in range(size)])  17.3 us
    ppermute x12, waiting for transfers between devices, swap(): lax.ppermute(value, axis, [(at, at ^ distance) for at in range(size)])  16.2 us
    pallas_call x1, Pallas kernels, weight_grads(): pl.pallas_call(kernel, grid=(tiles,), out_shape=[jax.ShapeDtypeStruct((sh...  13.6 us
    pallas_call x1, Pallas kernels, back(): pl.pallas_call(kernel, grid=(tiles + chunks,), out_shape=[jax.ShapeDtypeS...  10.8 us
    all_to_all x1, starting transfers between devices, exchange(): lax.all_to_all(blocks, 'expert', split_axis=0, concat_axis=0, tiled=True)  8.65 us
    pallas_call x2, Pallas kernels, join(): pl.pallas_call(kernel, out_shape=jax.ShapeDtypeStruct((count,) + received...  3.94 us
    pallas_call x1, Pallas kernels, pack(): pl.pallas_call(kernel, out_shape=[jax.ShapeDtypeStruct((2 * ROWS, width +...  2.99 us
    pallas_call x1, Pallas kernels, merge(): pl.pallas_call(kernel, out_shape=jax.ShapeDtypeStruct((tokens, width), jn...  2.36 us
  transfers between devices with their start and end apart: 13, of which 6 were waited for; matrix products, arithmetic and copies ran while one was open for 0% of the time, Pallas kernels for 37%

profile of v13, /device:TPU:0, one launch (start us, length us, event | category | flops | bytes accessed | tf_op | source)
XLA Modules:
  0.0 76.5 jit_solution(3161119714482380747)
XLA Ops:
  0.6 3.0 %pack.1 = (bf16[32,2304]{1,0:T(8,128)(2,1)}, bf16[32,2304]{1,0:T(8,128)(2,1)}, bf16[32,2304]{1,0:T(8,128)(2,1)}, bf16[32,2304]{1,0:T(8,128)(2,1)}, bf16[32,2304]...) custom-call(s32[1]{0:T(128)} %bitcast.1.me_ref, ...), custom_call_target="tpu_custom_call" | custom-call | flops 268435456 | bytes 2097152 | tf_op jit(solution)/shard_map/pack/pallas_call | solution.py:195
  3.6 3.0 %collective-permute-start = (bf16[32,2304]{1,0:T(8,128)(2,1)}, bf16[32,2304]{1,0:T(8,128)(2,1)S(1)}, u32[]{:S(2)}, u32[]{:S(2)}) collective-permute-start(bf16[32,2304]{1,0:T(8,128)(2,1)} %get-tuple-element.23), channel_id=1, source_target_pairs={{0,1},{1,0},{2,3},{3,2},{4,5},{5,4},{6,7},{7,6},{8,9},{9,8},{10,11... | collective-permute-start | bytes 442376 | tf_op jit(solution)/shard_map/ppermute | solution.py:619
  6.6 1.6 %collective-permute-start.1 = (bf16[32,2304]{1,0:T(8,128)(2,1)}, bf16[32,2304]{1,0:T(8,128)(2,1)}, u32[]{:S(2)}, u32[]{:S(2)}) collective-permute-start(bf16[32,2304]{1,0:T(8,128)(2,1)} %get-tuple-element.24), channel_id=1, source_target_pairs={{0,2},{1,3},{2,0},{3,1},{4,6},{5,7},{6,4},{7,5},{8,10},{9,11},{10,... | collective-permute-start | bytes 442376 | tf_op jit(solution)/shard_map/ppermute | solution.py:619
  8.2 0.0 collective-permute-start.2
  8.2 3.0 %collective-permute-start.3 = (bf16[32,2304]{1,0:T(8,128)(2,1)}, bf16[32,2304]{1,0:T(8,128)(2,1)}, u32[]{:S(2)}, u32[]{:S(2)}) collective-permute-start(bf16[32,2304]{1,0:T(8,128)(2,1)} %get-tuple-element.26), channel_id=1, source_target_pairs={{0,4},{1,5},{2,6},{3,7},{4,0},{5,1},{6,2},{7,3},{8,12},{9,13},{10,... | collective-permute-start | bytes 442376 | tf_op jit(solution)/shard_map/ppermute | solution.py:619
  11.2 1.3 %collective-permute-start.4 = (bf16[32,2304]{1,0:T(8,128)(2,1)}, bf16[32,2304]{1,0:T(8,128)(2,1)}, u32[]{:S(2)}, u32[]{:S(2)}) collective-permute-start(bf16[32,2304]{1,0:T(8,128)(2,1)} %get-tuple-element.27), channel_id=1, source_target_pairs={{0,5},{1,4},{2,7},{3,6},{4,1},{5,0},{6,3},{7,2},{8,13},{9,12},{10,... | collective-permute-start | bytes 442376 | tf_op jit(solution)/shard_map/ppermute | solution.py:619
  12.5 3.6 %collective-permute-start.5 = (bf16[32,2304]{1,0:T(8,128)(2,1)}, bf16[32,2304]{1,0:T(8,128)(2,1)}, u32[]{:S(2)}, u32[]{:S(2)}) collective-permute-start(bf16[32,2304]{1,0:T(8,128)(2,1)} %get-tuple-element.28), channel_id=1, source_target_pairs={{0,6},{1,7},{2,4},{3,5},{4,2},{5,3},{6,0},{7,1},{8,14},{9,15},{10,... | collective-permute-start | bytes 442376 | tf_op jit(solution)/shard_map/ppermute | solution.py:619
  16.1 2.8 %collective-permute-done.1.refs_2_ = bf16[32,2304]{1,0:T(8,128)(2,1)} collective-permute-done((bf16[32,2304]{1,0:T(8,128)(2,1)}, bf16[32,2304]{1,0:T(8,128)(2,1)}, u32[]{:S(2)}, u32[]{:S(2)}) %collective-permute-start.1) | collective-permute-done | bytes 147488 | tf_op jit(solution)/shard_map/ppermute | solution.py:619
  18.9 0.9 %collective-permute-start.6 = (bf16[32,2304]{1,0:T(8,128)(2,1)}, bf16[32,2304]{1,0:T(8,128)(2,1)}, u32[]{:S(2)}, u32[]{:S(2)}) collective-permute-start(bf16[32,2304]{1,0:T(8,128)(2,1)} %get-tuple-element.29), channel_id=1, source_target_pairs={{0,7},{1,6},{2,5},{3,4},{4,3},{5,2},{6,1},{7,0},{8,15},{9,14},{10,... | collective-permute-start | bytes 442376 | tf_op jit(solution)/shard_map/ppermute | solution.py:619
  19.9 0.1 collective-permute-done.2.refs_3_
  20.0 2.0 %join.2 = bf16[4,32,2304]{2,1,0:T(8,128)(2,1)} custom-call(bf16[32,2304]{1,0:T(8,128)(2,1)} %get-tuple-element.22.refs_0_, bf16[32,2304]{1,0:T(8,128)(2,1)} %copy-done, bf16[32,2304]{1,0:T(8,128)(2,1)} %collective-permute-done.1.refs_2_, bf16[32,2304]{1,0:T(8,128)(2,1)} %collective-permute-done.2.refs_3_), custom_call_target="tpu_custom_call" | custom-call | bytes 1179648 | tf_op jit(solution)/shard_map/join/pallas_call | solution.py:216
  22.0 1.8 %collective-permute-start.7 = (bf16[4,32,2304]{2,1,0:T(8,128)(2,1)}, bf16[4,32,2304]{2,1,0:T(8,128)(2,1)}, u32[]{:S(2)}, u32[]{:S(2)}) collective-permute-start(bf16[4,32,2304]{2,1,0:T(8,128)(2,1)} %join.2), channel_id=1, source_target_pairs={{0,16},{8,24},{16,0},{24,8},{1,17},{9,25},{17,1},{25,9},{2,18},{10... | collective-permute-start | bytes 1769480 | tf_op jit(solution)/shard_map/ppermute | solution.py:619
  23.7 9.3 %collective-permute-done.4.refs_5_.refs_1_ = bf16[32,2304]{1,0:T(8,128)(2,1)} collective-permute-done((bf16[32,2304]{1,0:T(8,128)(2,1)}, bf16[32,2304]{1,0:T(8,128)(2,1)}, u32[]{:S(2)}, u32[]{:S(2)}) %collective-permute-start.4) | collective-permute-done | bytes 147488 | tf_op jit(solution)/shard_map/ppermute | solution.py:619
  33.0 2.0 %join.3 = bf16[4,32,2304]{2,1,0:T(8,128)(2,1)} custom-call(bf16[32,2304]{1,0:T(8,128)(2,1)} %collective-permute-done.3.refs_4_.refs_0_, bf16[32,2304]{1,0:T(8,128)(2,1)} %collective-permute-done.4.refs_5_.refs_1_, bf16[32,2304]{1,0:T(8,128)(2,1)} %collective-permute-done.5.refs_6_.refs_2_, bf16[32,2304]{1,0:T(8,128)(2,1)} %collective-permute-done.6.refs_7_.refs_3_), custom_call_target="tpu_custom_call" | custom-call | bytes 1179648 | tf_op jit(solution)/shard_map/join/pallas_call | solution.py:216
  35.0 1.6 %collective-permute-start.9 = (bf16[4,32,2304]{2,1,0:T(8,128)(2,1)}, bf16[4,32,2304]{2,1,0:T(8,128)(2,1)}, u32[]{:S(2)}, u32[]{:S(2)}) collective-permute-start(bf16[4,32,2304]{2,1,0:T(8,128)(2,1)} %join.3), channel_id=1, source_target_pairs={{0,16},{8,24},{16,0},{24,8},{1,17},{9,25},{17,1},{25,9},{2,18},{10... | collective-permute-start | bytes 1769480 | tf_op jit(solution)/shard_map/ppermute | solution.py:619
  36.6 10.8 %back.1 = (bf16[8,16,2304]{2,1,0:T(8,128)(2,1)}, bf16[144,3328]{1,0:T(8,128)(2,1)}, bf16[144,3328]{1,0:T(8,128)(2,1)}) custom-call(s32[1]{0:T(128)} %bitcast.1.me_ref, s32[1]{0:T(128)} %bitcast.2.part_ref, bf16[32,2304]{1,0:T(8,128)(2,1)} %get-tuple-element.22.refs_0_, bf16[32,2304]{1,0:T(8,128)(2,1)} %copy-done, ...), custom_call_target="tpu_custom_call" | custom-call | flops 11324620800 | bytes 1179648 | tf_op jit(solution)/shard_map/back/pallas_call | solution.py:450
  47.3 8.6 %all-to-all-start = ((bf16[8,16,2304]{2,1,0:T(8,128)(2,1)}), bf16[8,16,2304]{2,1,0:T(8,128)(2,1)}, u32[]{:S(2)}, u32[]{:S(2)}) async-start(bf16[8,16,2304]{2,1,0:T(8,128)(2,1)} %get-tuple-element.31), calls=%async_computation | async-start | bytes 1179648 | tf_op jit(solution)/shard_map/all_to_all | solution.py:623
  56.0 0.5 collective-permute-start.11
  56.5 0.1 collective-permute-start.10
  56.6 2.3 %collective-permute-done.8.refs_1_ = bf16[144,3328]{1,0:T(8,128)(2,1)} collective-permute-done((bf16[144,3328]{1,0:T(8,128)(2,1)}, bf16[144,3328]{1,0:T(8,128)(2,1)}, u32[]{:S(2)}, u32[]{:S(2)}) %collective-permute-start.8) | collective-permute-done | bytes 958496 | tf_op jit(solution)/shard_map/ppermute | solution.py:619
  58.9 0.8 %collective-permute-done.11.refs_5_ = bf16[4,32,2304]{2,1,0:T(8,128)(2,1)} collective-permute-done((bf16[4,32,2304]{2,1,0:T(8,128)(2,1)}, bf16[4,32,2304]{2,1,0:T(8,128)(2,1)}, u32[]{:S(2)}, u32[]{:S(2)}) %collective-permute-start.11) | collective-permute-done | bytes 589856 | tf_op jit(solution)/shard_map/ppermute | solution.py:619
  59.7 0.8 %collective-permute-done.10.refs_4_ = bf16[4,32,2304]{2,1,0:T(8,128)(2,1)} collective-permute-done((bf16[4,32,2304]{2,1,0:T(8,128)(2,1)}, bf16[4,32,2304]{2,1,0:T(8,128)(2,1)}, u32[]{:S(2)}, u32[]{:S(2)}) %collective-permute-start.10) | collective-permute-done | bytes 589856 | tf_op jit(solution)/shard_map/ppermute | solution.py:619
  60.6 13.6 %weight_grads.1 = (f32[512,768]{1,0:T(8,128)}, f32[512,768]{1,0:T(8,128)}, f32[768,512]{1,0:T(8,128)}) custom-call(s32[1]{0:T(128)} %bitcast.2.part_ref, bf16[144,3328]{1,0:T(8,128)(2,1)} %get-tuple-element.32.refs_0_, bf16[144,3328]{1,0:T(8,128)(2,1)} %collective-permute-done.8.refs_1_, bf16[4,32,2304]{2,1,0:T(8,128)(2,1)} %collective-permute-done.7.refs_2_, ...), custom_call_target="tpu_custom_call" | custom-call | bytes 1179648 | tf_op jit(solution)/shard_map/weight_grads/pallas_call | solution.py:583
  74.2 2.4 %merge.1 = bf16[128,2048]{1,0:T(8,128)(2,1)} custom-call(s32[1,128]{1,0:T(1,128)} %bitcast.5, bf16[8,16,2304]{2,1,0:T(8,128)(2,1)} %all-to-all-done.back_ref), custom_call_target="tpu_custom_call" | custom-call | flops 134217728 | bytes 1048576 | tf_op jit(solution)/shard_map/merge/pallas_call | solution.py:251
  (10 shorter events, 0.0 us)
Async XLA Ops:
  3.6 8.9 %collective-permute-start = (bf16[32,2304]{1,0:T(8,128)(2,1)}, bf16[32,2304]{1,0:T(8,128)(2,1)S(1)}, u32[]{:S(2)}, u32[]{:S(2)}) collective-permute-start(bf16[32,2304]{1,0:T(8,128)(2,1)} %get-tuple-element.23), channel_id=1, source_target_pairs={{0,1},{1,0},{2,3},{3,2},{4,5},{5,4},{6,7},{7,6},{8,9},{9,8},{10,11... | collective-permute-start | bytes 442376 | tf_op jit(solution)/shard_map/ppermute | solution.py:619
  6.6 12.3 %collective-permute-start.1 = (bf16[32,2304]{1,0:T(8,128)(2,1)}, bf16[32,2304]{1,0:T(8,128)(2,1)}, u32[]{:S(2)}, u32[]{:S(2)}) collective-permute-start(bf16[32,2304]{1,0:T(8,128)(2,1)} %get-tuple-element.24), channel_id=1, source_target_pairs={{0,2},{1,3},{2,0},{3,1},{4,6},{5,7},{6,4},{7,5},{8,10},{9,11},{10,... | collective-permute-start | bytes 442376 | tf_op jit(solution)/shard_map/ppermute | solution.py:619
  8.2 11.8 %collective-permute-start.2 = (bf16[32,2304]{1,0:T(8,128)(2,1)}, bf16[32,2304]{1,0:T(8,128)(2,1)}, u32[]{:S(2)}, u32[]{:S(2)}) collective-permute-start(bf16[32,2304]{1,0:T(8,128)(2,1)} %get-tuple-element.25), channel_id=1, source_target_pairs={{0,3},{1,2},{2,1},{3,0},{4,7},{5,6},{6,5},{7,4},{8,11},{9,10},{10,... | collective-permute-start | bytes 442376 | tf_op jit(solution)/shard_map/ppermute | solution.py:619
  8.2 15.5 %collective-permute-start.3 = (bf16[32,2304]{1,0:T(8,128)(2,1)}, bf16[32,2304]{1,0:T(8,128)(2,1)}, u32[]{:S(2)}, u32[]{:S(2)}) collective-permute-start(bf16[32,2304]{1,0:T(8,128)(2,1)} %get-tuple-element.26), channel_id=1, source_target_pairs={{0,4},{1,5},{2,6},{3,7},{4,0},{5,1},{6,2},{7,3},{8,12},{9,13},{10,... | collective-permute-start | bytes 442376 | tf_op jit(solution)/shard_map/ppermute | solution.py:619
  11.2 21.8 %collective-permute-start.4 = (bf16[32,2304]{1,0:T(8,128)(2,1)}, bf16[32,2304]{1,0:T(8,128)(2,1)}, u32[]{:S(2)}, u32[]{:S(2)}) collective-permute-start(bf16[32,2304]{1,0:T(8,128)(2,1)} %get-tuple-element.27), channel_id=1, source_target_pairs={{0,5},{1,4},{2,7},{3,6},{4,1},{5,0},{6,3},{7,2},{8,13},{9,12},{10,... | collective-permute-start | bytes 442376 | tf_op jit(solution)/shard_map/ppermute | solution.py:619
  12.5 7.5 %copy-start = (bf16[32,2304]{1,0:T(8,128)(2,1)}, bf16[32,2304]{1,0:T(8,128)(2,1)S(1)}, u32[]{:S(2)}) copy-start(bf16[32,2304]{1,0:T(8,128)(2,1)S(1)} %collective-permute-done.refs_1_) | copy-start | bytes 442372
  12.5 20.5 %collective-permute-start.5 = (bf16[32,2304]{1,0:T(8,128)(2,1)}, bf16[32,2304]{1,0:T(8,128)(2,1)}, u32[]{:S(2)}, u32[]{:S(2)}) collective-permute-start(bf16[32,2304]{1,0:T(8,128)(2,1)} %get-tuple-element.28), channel_id=1, source_target_pairs={{0,6},{1,7},{2,4},{3,5},{4,2},{5,3},{6,0},{7,1},{8,14},{9,15},{10,... | collective-permute-start | bytes 442376 | tf_op jit(solution)/shard_map/ppermute | solution.py:619
  18.9 14.1 %collective-permute-start.6 = (bf16[32,2304]{1,0:T(8,128)(2,1)}, bf16[32,2304]{1,0:T(8,128)(2,1)}, u32[]{:S(2)}, u32[]{:S(2)}) collective-permute-start(bf16[32,2304]{1,0:T(8,128)(2,1)} %get-tuple-element.29), channel_id=1, source_target_pairs={{0,7},{1,6},{2,5},{3,4},{4,3},{5,2},{6,1},{7,0},{8,15},{9,14},{10,... | collective-permute-start | bytes 442376 | tf_op jit(solution)/shard_map/ppermute | solution.py:619
  22.0 25.4 %collective-permute-start.7 = (bf16[4,32,2304]{2,1,0:T(8,128)(2,1)}, bf16[4,32,2304]{2,1,0:T(8,128)(2,1)}, u32[]{:S(2)}, u32[]{:S(2)}) collective-permute-start(bf16[4,32,2304]{2,1,0:T(8,128)(2,1)} %join.2), channel_id=1, source_target_pairs={{0,16},{8,24},{16,0},{24,8},{1,17},{9,25},{17,1},{25,9},{2,18},{10... | collective-permute-start | bytes 1769480 | tf_op jit(solution)/shard_map/ppermute | solution.py:619
  35.0 21.0 %collective-permute-start.9 = (bf16[4,32,2304]{2,1,0:T(8,128)(2,1)}, bf16[4,32,2304]{2,1,0:T(8,128)(2,1)}, u32[]{:S(2)}, u32[]{:S(2)}) collective-permute-start(bf16[4,32,2304]{2,1,0:T(8,128)(2,1)} %join.3), channel_id=1, source_target_pairs={{0,16},{8,24},{16,0},{24,8},{1,17},{9,25},{17,1},{25,9},{2,18},{10... | collective-permute-start | bytes 1769480 | tf_op jit(solution)/shard_map/ppermute | solution.py:619
  47.3 26.8 %all-to-all-start = ((bf16[8,16,2304]{2,1,0:T(8,128)(2,1)}), bf16[8,16,2304]{2,1,0:T(8,128)(2,1)}, u32[]{:S(2)}, u32[]{:S(2)}) async-start(bf16[8,16,2304]{2,1,0:T(8,128)(2,1)} %get-tuple-element.31), calls=%async_computation | async-start | bytes 1179648 | tf_op jit(solution)/shard_map/all_to_all | solution.py:623
  56.0 2.9 %collective-permute-start.8 = (bf16[144,3328]{1,0:T(8,128)(2,1)}, bf16[144,3328]{1,0:T(8,128)(2,1)}, u32[]{:S(2)}, u32[]{:S(2)}) collective-permute-start(bf16[144,3328]{1,0:T(8,128)(2,1)} %get-tuple-element.33), channel_id=1, source_target_pairs={{0,8},{8,0},{16,24},{24,16},{1,9},{9,1},{17,25},{25,17},{2,10},{10... | collective-permute-start | bytes 2875400 | tf_op jit(solution)/shard_map/ppermute | solution.py:619
  56.0 3.7 %collective-permute-start.11 = (bf16[4,32,2304]{2,1,0:T(8,128)(2,1)}, bf16[4,32,2304]{2,1,0:T(8,128)(2,1)}, u32[]{:S(2)}, u32[]{:S(2)}) collective-permute-start(bf16[4,32,2304]{2,1,0:T(8,128)(2,1)} %collective-permute-done.9.refs_3_), channel_id=1, source_target_pairs={{0,8},{8,0},{16,24},{24,16},{1,9},{9,1},{17,25},{25,17},{2,10},{10... | collective-permute-start | bytes 1769480 | tf_op jit(solution)/shard_map/ppermute | solution.py:619
  56.5 4.0 %collective-permute-start.10 = (bf16[4,32,2304]{2,1,0:T(8,128)(2,1)}, bf16[4,32,2304]{2,1,0:T(8,128)(2,1)}, u32[]{:S(2)}, u32[]{:S(2)}) collective-permute-start(bf16[4,32,2304]{2,1,0:T(8,128)(2,1)} %collective-permute-done.7.refs_2_), channel_id=1, source_target_pairs={{0,8},{8,0},{16,24},{24,16},{1,9},{9,1},{17,25},{25,17},{2,10},{10... | collective-permute-start | bytes 1769480 | tf_op jit(solution)/shard_map/ppermute | solution.py:619

commit v14 on v13

--- a/solution.py
+++ b/solution.py
@@ -284,14 +284,6 @@
         ).astype(jnp.bfloat16)
 
 
-def column_tile(width, tile):
-    return pl.BlockSpec((width, tile), lambda i: (0, i))
-
-
-def row_tile(tile, width):
-    return pl.BlockSpec((tile, width), lambda i: (i, 0))
-
-
 def tile_of(index, tile):
     return pl.ds(pl.multiple_of(index * tile, tile), tile)
 
@@ -316,10 +308,10 @@
 
 
 def hidden_grads(pre_gate, pre_up, d_hidden):
-    sig = jax.nn.sigmoid(pre_gate)
+    sig = 0.5 * jnp.tanh(0.5 * pre_gate) + 0.5
     silu = pre_gate * sig
     hidden = (silu * pre_up).astype(jnp.bfloat16)
-    d_gate = (d_hidden * pre_up * sig * (1.0 + pre_gate * (1.0 - sig))).astype(jnp.bfloat16)
+    d_gate = (d_hidden * pre_up * (sig + silu * (1.0 - sig))).astype(jnp.bfloat16)
     d_up = (d_hidden * silu).astype(jnp.bfloat16)
     return hidden, d_gate, d_up
 
@@ -501,7 +493,8 @@
         d_gate_ref, d_up_ref, d_down_ref = [refs.pop(0) for _ in range(3)]
         x_held, dy_held, x_all, dy_all = [refs.pop(0) for _ in range(4)]
         x_mine, dy_mine, factors = [refs.pop(0) for _ in range(3)]
-        gate, up, down, x_in, dy_in, known_in, gate_in, up_in, down_in = refs
+        gate, up, down, x_in, dy_in, known_in, gate_in, up_in, down_in = refs[:9]
+        made_gate, made_up, made_down, gate_out, up_out, down_out = refs[9:]
         now = pl.program_id(0)
         columns = tile_of(part_ref[0], share)
         x_pairs, dy_pairs, known_pairs = [], [], []
@@ -529,6 +522,11 @@
                 )
             target[given * slots :, :] = rows_out[:, columns]
 
+        def leave(source, target, gone, index, axis):
+            here = tile_of(index, tile)
+            view = target.at[:, here] if axis else target.at[here, :]
+            return pltpu.make_async_copy(source.at[index], view, gone.at[index])
+
         def fetch_x(index):
             weight_copy(gate_ref, gate, gate_in, index, 1, tile).start()
             weight_copy(up_ref, up, up_in, index, 1, tile).start()
@@ -573,9 +571,19 @@
         d_gate = jnp.concatenate([factors[:, tile_of(tiles + now, tile)], d_gate], 0)
         d_up = jnp.concatenate([factors[:, tile_of(2 * tiles + now, tile)], d_up], 0)
         sums = dot(x_mine[...], jnp.concatenate([d_gate, d_up], 1), BY_ROWS)
-        d_gate_ref[...] = sums[:, :tile]
-        d_up_ref[...] = sums[:, tile:]
-        d_down_ref[...] = dot(made, dy_mine[...], BY_ROWS)
+        made_gate[now] = sums[:, :tile]
+        made_up[now] = sums[:, tile:]
+        leave(made_gate, d_gate_ref, gate_out, now, 1).start()
+        leave(made_up, d_up_ref, up_out, now, 1).start()
+        made_down[now] = dot(made, dy_mine[...], BY_ROWS)
+        leave(made_down, d_down_ref, down_out, now, 0).start()
+
+        @pl.when(now == tiles - 1)
+        def _():
+            for at in range(tiles):
+                leave(made_gate, d_gate_ref, gate_out, at, 1).wait()
+                leave(made_up, d_up_ref, up_out, at, 1).wait()
+                leave(made_down, d_down_ref, down_out, at, 0).wait()
 
     held = pltpu.VMEM((count, blocks, ROWS, width + step), jnp.bfloat16)
     arranged = pltpu.VMEM((count * slots, width), jnp.bfloat16)
@@ -589,7 +597,7 @@
             jax.ShapeDtypeStruct((hid, share), jnp.float32),
         ],
         in_specs=[pl.BlockSpec(memory_space=pltpu.SMEM)] + anywhere(given + count * items + 3),
-        out_specs=[column_tile(share, tile), column_tile(share, tile), row_tile(tile, share)],
+        out_specs=anywhere(3),
         scratch_shapes=[
             held,
             held,
@@ -604,6 +612,12 @@
             pltpu.SemaphoreType.DMA((count * items,)),
             pltpu.SemaphoreType.DMA((count * items,)),
             pltpu.SemaphoreType.DMA((3 * given,)),
+            pltpu.SemaphoreType.DMA((tiles,)),
+            pltpu.SemaphoreType.DMA((tiles,)),
+            pltpu.SemaphoreType.DMA((tiles,)),
+            pltpu.VMEM((tiles, share, tile), jnp.float32),
+            pltpu.VMEM((tiles, share, tile), jnp.float32),
+            pltpu.VMEM((tiles, tile, share), jnp.float32),
             pltpu.SemaphoreType.DMA((tiles,)),
             pltpu.SemaphoreType.DMA((tiles,)),
             pltpu.SemaphoreType.DMA((tiles,)),

time: 76.9 us -> 76.9 us (level)
  no operation moved by 1% of the time
where the time goes in v14:
time: 76.9 us; the launch traced here: 76.6 us
  Pallas kernels  33.7 us (44%)
  starting transfers between devices  26 us (34%)
  waiting for transfers between devices  16.2 us (21%)
    ppermute x12, starting transfers between devices, swap(): lax.ppermute(value, axis, [(at, at ^ distance) for at in range(size)])  17.3 us
    ppermute x12, waiting for transfers between devices, swap(): lax.ppermute(value, axis, [(at, at ^ distance) for at in range(size)])  16.2 us
    pallas_call x1, Pallas kernels, weight_grads(): pl.pallas_call(kernel, grid=(tiles,), out_shape=[jax.ShapeDtypeStruct((sh...  13.6 us
    pallas_call x1, Pallas kernels, back(): pl.pallas_call(kernel, grid=(tiles + chunks,), out_shape=[jax.ShapeDtypeS...  10.8 us
    all_to_all x1, starting transfers between devices, exchange(): lax.all_to_all(blocks, 'expert', split_axis=0, concat_axis=0, tiled=True)  8.68 us
    pallas_call x2, Pallas kernels, join(): pl.pallas_call(kernel, out_shape=jax.ShapeDtypeStruct((count,) + received...  3.94 us
    pallas_call x1, Pallas kernels, pack(): pl.pallas_call(kernel, out_shape=[jax.ShapeDtypeStruct((2 * ROWS, width +...  2.99 us
    pallas_call x1, Pallas kernels, merge(): pl.pallas_call(kernel, out_shape=jax.ShapeDtypeStruct((tokens, width), jn...  2.36 us
  transfers between devices with their start and end apart: 13, of which 6 were waited for; matrix products, arithmetic and copies ran while one was open for 0% of the time, Pallas kernels for 37%

profile of v14, /device:TPU:0, one launch (start us, length us, event | category | flops | bytes accessed | tf_op | source)
XLA Modules:
  0.0 76.6 jit_solution(16597743133054808858)
XLA Ops:
  0.6 3.0 %pack.1 = (bf16[32,2304]{1,0:T(8,128)(2,1)}, bf16[32,2304]{1,0:T(8,128)(2,1)}, bf16[32,2304]{1,0:T(8,128)(2,1)}, bf16[32,2304]{1,0:T(8,128)(2,1)}, bf16[32,2304]...) custom-call(s32[1]{0:T(128)} %bitcast.1.me_ref, ...), custom_call_target="tpu_custom_call" | custom-call | flops 268435456 | bytes 2097152 | tf_op jit(solution)/shard_map/pack/pallas_call | solution.py:195
  3.6 3.0 %collective-permute-start = (bf16[32,2304]{1,0:T(8,128)(2,1)}, bf16[32,2304]{1,0:T(8,128)(2,1)S(1)}, u32[]{:S(2)}, u32[]{:S(2)}) collective-permute-start(bf16[32,2304]{1,0:T(8,128)(2,1)} %get-tuple-element.23), channel_id=1, source_target_pairs={{0,1},{1,0},{2,3},{3,2},{4,5},{5,4},{6,7},{7,6},{8,9},{9,8},{10,11... | collective-permute-start | bytes 442376 | tf_op jit(solution)/shard_map/ppermute | solution.py:633
  6.6 1.6 %collective-permute-start.1 = (bf16[32,2304]{1,0:T(8,128)(2,1)}, bf16[32,2304]{1,0:T(8,128)(2,1)}, u32[]{:S(2)}, u32[]{:S(2)}) collective-permute-start(bf16[32,2304]{1,0:T(8,128)(2,1)} %get-tuple-element.24), channel_id=1, source_target_pairs={{0,2},{1,3},{2,0},{3,1},{4,6},{5,7},{6,4},{7,5},{8,10},{9,11},{10,... | collective-permute-start | bytes 442376 | tf_op jit(solution)/shard_map/ppermute | solution.py:633
  8.2 3.0 %collective-permute-start.3 = (bf16[32,2304]{1,0:T(8,128)(2,1)}, bf16[32,2304]{1,0:T(8,128)(2,1)}, u32[]{:S(2)}, u32[]{:S(2)}) collective-permute-start(bf16[32,2304]{1,0:T(8,128)(2,1)} %get-tuple-element.26), channel_id=1, source_target_pairs={{0,4},{1,5},{2,6},{3,7},{4,0},{5,1},{6,2},{7,3},{8,12},{9,13},{10,... | collective-permute-start | bytes 442376 | tf_op jit(solution)/shard_map/ppermute | solution.py:633
  11.2 1.3 %collective-permute-start.4 = (bf16[32,2304]{1,0:T(8,128)(2,1)}, bf16[32,2304]{1,0:T(8,128)(2,1)}, u32[]{:S(2)}, u32[]{:S(2)}) collective-permute-start(bf16[32,2304]{1,0:T(8,128)(2,1)} %get-tuple-element.27), channel_id=1, source_target_pairs={{0,5},{1,4},{2,7},{3,6},{4,1},{5,0},{6,3},{7,2},{8,13},{9,12},{10,... | collective-permute-start | bytes 442376 | tf_op jit(solution)/shard_map/ppermute | solution.py:633
  12.5 0.0 collective-permute-done.refs_1_
  12.5 3.6 %collective-permute-start.5 = (bf16[32,2304]{1,0:T(8,128)(2,1)}, bf16[32,2304]{1,0:T(8,128)(2,1)}, u32[]{:S(2)}, u32[]{:S(2)}) collective-permute-start(bf16[32,2304]{1,0:T(8,128)(2,1)} %get-tuple-element.28), channel_id=1, source_target_pairs={{0,6},{1,7},{2,4},{3,5},{4,2},{5,3},{6,0},{7,1},{8,14},{9,15},{10,... | collective-permute-start | bytes 442376 | tf_op jit(solution)/shard_map/ppermute | solution.py:633
  16.1 2.8 %collective-permute-done.1.refs_2_ = bf16[32,2304]{1,0:T(8,128)(2,1)} collective-permute-done((bf16[32,2304]{1,0:T(8,128)(2,1)}, bf16[32,2304]{1,0:T(8,128)(2,1)}, u32[]{:S(2)}, u32[]{:S(2)}) %collective-permute-start.1) | collective-permute-done | bytes 147488 | tf_op jit(solution)/shard_map/ppermute | solution.py:633
  18.9 0.9 %collective-permute-start.6 = (bf16[32,2304]{1,0:T(8,128)(2,1)}, bf16[32,2304]{1,0:T(8,128)(2,1)}, u32[]{:S(2)}, u32[]{:S(2)}) collective-permute-start(bf16[32,2304]{1,0:T(8,128)(2,1)} %get-tuple-element.29), channel_id=1, source_target_pairs={{0,7},{1,6},{2,5},{3,4},{4,3},{5,2},{6,1},{7,0},{8,15},{9,14},{10,... | collective-permute-start | bytes 442376 | tf_op jit(solution)/shard_map/ppermute | solution.py:633
  19.9 0.1 collective-permute-done.2.refs_3_
  20.0 2.0 %join.2 = bf16[4,32,2304]{2,1,0:T(8,128)(2,1)} custom-call(bf16[32,2304]{1,0:T(8,128)(2,1)} %get-tuple-element.22.refs_0_, bf16[32,2304]{1,0:T(8,128)(2,1)} %copy-done, bf16[32,2304]{1,0:T(8,128)(2,1)} %collective-permute-done.1.refs_2_, bf16[32,2304]{1,0:T(8,128)(2,1)} %collective-permute-done.2.refs_3_), custom_call_target="tpu_custom_call" | custom-call | bytes 1179648 | tf_op jit(solution)/shard_map/join/pallas_call | solution.py:216
  22.0 1.8 %collective-permute-start.7 = (bf16[4,32,2304]{2,1,0:T(8,128)(2,1)}, bf16[4,32,2304]{2,1,0:T(8,128)(2,1)}, u32[]{:S(2)}, u32[]{:S(2)}) collective-permute-start(bf16[4,32,2304]{2,1,0:T(8,128)(2,1)} %join.2), channel_id=1, source_target_pairs={{0,16},{8,24},{16,0},{24,8},{1,17},{9,25},{17,1},{25,9},{2,18},{10... | collective-permute-start | bytes 1769480 | tf_op jit(solution)/shard_map/ppermute | solution.py:633
  23.7 9.3 %collective-permute-done.4.refs_5_.refs_1_ = bf16[32,2304]{1,0:T(8,128)(2,1)} collective-permute-done((bf16[32,2304]{1,0:T(8,128)(2,1)}, bf16[32,2304]{1,0:T(8,128)(2,1)}, u32[]{:S(2)}, u32[]{:S(2)}) %collective-permute-start.4) | collective-permute-done | bytes 147488 | tf_op jit(solution)/shard_map/ppermute | solution.py:633
  33.0 2.0 %join.3 = bf16[4,32,2304]{2,1,0:T(8,128)(2,1)} custom-call(bf16[32,2304]{1,0:T(8,128)(2,1)} %collective-permute-done.3.refs_4_.refs_0_, bf16[32,2304]{1,0:T(8,128)(2,1)} %collective-permute-done.4.refs_5_.refs_1_, bf16[32,2304]{1,0:T(8,128)(2,1)} %collective-permute-done.5.refs_6_.refs_2_, bf16[32,2304]{1,0:T(8,128)(2,1)} %collective-permute-done.6.refs_7_.refs_3_), custom_call_target="tpu_custom_call" | custom-call | bytes 1179648 | tf_op jit(solution)/shard_map/join/pallas_call | solution.py:216
  35.0 1.6 %collective-permute-start.9 = (bf16[4,32,2304]{2,1,0:T(8,128)(2,1)}, bf16[4,32,2304]{2,1,0:T(8,128)(2,1)}, u32[]{:S(2)}, u32[]{:S(2)}) collective-permute-start(bf16[4,32,2304]{2,1,0:T(8,128)(2,1)} %join.3), channel_id=1, source_target_pairs={{0,16},{8,24},{16,0},{24,8},{1,17},{9,25},{17,1},{25,9},{2,18},{10... | collective-permute-start | bytes 1769480 | tf_op jit(solution)/shard_map/ppermute | solution.py:633
  36.6 10.8 %back.1 = (bf16[8,16,2304]{2,1,0:T(8,128)(2,1)}, bf16[144,3328]{1,0:T(8,128)(2,1)}, bf16[144,3328]{1,0:T(8,128)(2,1)}) custom-call(s32[1]{0:T(128)} %bitcast.1.me_ref, s32[1]{0:T(128)} %bitcast.2.part_ref, bf16[32,2304]{1,0:T(8,128)(2,1)} %get-tuple-element.22.refs_0_, bf16[32,2304]{1,0:T(8,128)(2,1)} %copy-done, ...), custom_call_target="tpu_custom_call" | custom-call | flops 11324620800 | bytes 1179648 | tf_op jit(solution)/shard_map/back/pallas_call | solution.py:442
  47.3 8.7 %all-to-all-start = ((bf16[8,16,2304]{2,1,0:T(8,128)(2,1)}), bf16[8,16,2304]{2,1,0:T(8,128)(2,1)}, u32[]{:S(2)}, u32[]{:S(2)}) async-start(bf16[8,16,2304]{2,1,0:T(8,128)(2,1)} %get-tuple-element.31), calls=%async_computation | async-start | bytes 1179648 | tf_op jit(solution)/shard_map/all_to_all | solution.py:637
  56.0 0.5 collective-permute-start.11
  56.5 0.1 collective-permute-start.10
  56.6 2.3 %collective-permute-done.8.refs_1_ = bf16[144,3328]{1,0:T(8,128)(2,1)} collective-permute-done((bf16[144,3328]{1,0:T(8,128)(2,1)}, bf16[144,3328]{1,0:T(8,128)(2,1)}, u32[]{:S(2)}, u32[]{:S(2)}) %collective-permute-start.8) | collective-permute-done | bytes 958496 | tf_op jit(solution)/shard_map/ppermute | solution.py:633
  58.9 0.8 %collective-permute-done.11.refs_5_ = bf16[4,32,2304]{2,1,0:T(8,128)(2,1)} collective-permute-done((bf16[4,32,2304]{2,1,0:T(8,128)(2,1)}, bf16[4,32,2304]{2,1,0:T(8,128)(2,1)}, u32[]{:S(2)}, u32[]{:S(2)}) %collective-permute-start.11) | collective-permute-done | bytes 589856 | tf_op jit(solution)/shard_map/ppermute | solution.py:633
  59.7 0.8 %collective-permute-done.10.refs_4_ = bf16[4,32,2304]{2,1,0:T(8,128)(2,1)} collective-permute-done((bf16[4,32,2304]{2,1,0:T(8,128)(2,1)}, bf16[4,32,2304]{2,1,0:T(8,128)(2,1)}, u32[]{:S(2)}, u32[]{:S(2)}) %collective-permute-start.10) | collective-permute-done | bytes 589856 | tf_op jit(solution)/shard_map/ppermute | solution.py:633
  60.6 13.6 %weight_grads.1 = (f32[512,768]{1,0:T(8,128)}, f32[512,768]{1,0:T(8,128)}, f32[768,512]{1,0:T(8,128)}) custom-call(s32[1]{0:T(128)} %bitcast.2.part_ref, bf16[144,3328]{1,0:T(8,128)(2,1)} %get-tuple-element.32.refs_0_, bf16[144,3328]{1,0:T(8,128)(2,1)} %collective-permute-done.8.refs_1_, bf16[4,32,2304]{2,1,0:T(8,128)(2,1)} %collective-permute-done.7.refs_2_, ...), custom_call_target="tpu_custom_call" | custom-call | bytes 1179648 | tf_op jit(solution)/shard_map/weight_grads/pallas_call | solution.py:591
  74.2 2.4 %merge.1 = bf16[128,2048]{1,0:T(8,128)(2,1)} custom-call(s32[1,128]{1,0:T(1,128)} %bitcast.5, bf16[8,16,2304]{2,1,0:T(8,128)(2,1)} %all-to-all-done.back_ref), custom_call_target="tpu_custom_call" | custom-call | flops 134217728 | bytes 1048576 | tf_op jit(solution)/shard_map/merge/pallas_call | solution.py:251
  (10 shorter events, 0.0 us)
Async XLA Ops:
  3.6 8.9 %collective-permute-start = (bf16[32,2304]{1,0:T(8,128)(2,1)}, bf16[32,2304]{1,0:T(8,128)(2,1)S(1)}, u32[]{:S(2)}, u32[]{:S(2)}) collective-permute-start(bf16[32,2304]{1,0:T(8,128)(2,1)} %get-tuple-element.23), channel_id=1, source_target_pairs={{0,1},{1,0},{2,3},{3,2},{4,5},{5,4},{6,7},{7,6},{8,9},{9,8},{10,11... | collective-permute-start | bytes 442376 | tf_op jit(solution)/shard_map/ppermute | solution.py:633
  6.6 12.3 %collective-permute-start.1 = (bf16[32,2304]{1,0:T(8,128)(2,1)}, bf16[32,2304]{1,0:T(8,128)(2,1)}, u32[]{:S(2)}, u32[]{:S(2)}) collective-permute-start(bf16[32,2304]{1,0:T(8,128)(2,1)} %get-tuple-element.24), channel_id=1, source_target_pairs={{0,2},{1,3},{2,0},{3,1},{4,6},{5,7},{6,4},{7,5},{8,10},{9,11},{10,... | collective-permute-start | bytes 442376 | tf_op jit(solution)/shard_map/ppermute | solution.py:633
  8.2 11.8 %collective-permute-start.2 = (bf16[32,2304]{1,0:T(8,128)(2,1)}, bf16[32,2304]{1,0:T(8,128)(2,1)}, u32[]{:S(2)}, u32[]{:S(2)}) collective-permute-start(bf16[32,2304]{1,0:T(8,128)(2,1)} %get-tuple-element.25), channel_id=1, source_target_pairs={{0,3},{1,2},{2,1},{3,0},{4,7},{5,6},{6,5},{7,4},{8,11},{9,10},{10,... | collective-permute-start | bytes 442376 | tf_op jit(solution)/shard_map/ppermute | solution.py:633
  8.2 15.5 %collective-permute-start.3 = (bf16[32,2304]{1,0:T(8,128)(2,1)}, bf16[32,2304]{1,0:T(8,128)(2,1)}, u32[]{:S(2)}, u32[]{:S(2)}) collective-permute-start(bf16[32,2304]{1,0:T(8,128)(2,1)} %get-tuple-element.26), channel_id=1, source_target_pairs={{0,4},{1,5},{2,6},{3,7},{4,0},{5,1},{6,2},{7,3},{8,12},{9,13},{10,... | collective-permute-start | bytes 442376 | tf_op jit(solution)/shard_map/ppermute | solution.py:633
  11.2 21.8 %collective-permute-start.4 = (bf16[32,2304]{1,0:T(8,128)(2,1)}, bf16[32,2304]{1,0:T(8,128)(2,1)}, u32[]{:S(2)}, u32[]{:S(2)}) collective-permute-start(bf16[32,2304]{1,0:T(8,128)(2,1)} %get-tuple-element.27), channel_id=1, source_target_pairs={{0,5},{1,4},{2,7},{3,6},{4,1},{5,0},{6,3},{7,2},{8,13},{9,12},{10,... | collective-permute-start | bytes 442376 | tf_op jit(solution)/shard_map/ppermute | solution.py:633
  12.5 7.5 %copy-start = (bf16[32,2304]{1,0:T(8,128)(2,1)}, bf16[32,2304]{1,0:T(8,128)(2,1)S(1)}, u32[]{:S(2)}) copy-start(bf16[32,2304]{1,0:T(8,128)(2,1)S(1)} %collective-permute-done.refs_1_) | copy-start | bytes 442372
  12.5 20.5 %collective-permute-start.5 = (bf16[32,2304]{1,0:T(8,128)(2,1)}, bf16[32,2304]{1,0:T(8,128)(2,1)}, u32[]{:S(2)}, u32[]{:S(2)}) collective-permute-start(bf16[32,2304]{1,0:T(8,128)(2,1)} %get-tuple-element.28), channel_id=1, source_target_pairs={{0,6},{1,7},{2,4},{3,5},{4,2},{5,3},{6,0},{7,1},{8,14},{9,15},{10,... | collective-permute-start | bytes 442376 | tf_op jit(solution)/shard_map/ppermute | solution.py:633
  18.9 14.1 %collective-permute-start.6 = (bf16[32,2304]{1,0:T(8,128)(2,1)}, bf16[32,2304]{1,0:T(8,128)(2,1)}, u32[]{:S(2)}, u32[]{:S(2)}) collective-permute-start(bf16[32,2304]{1,0:T(8,128)(2,1)} %get-tuple-element.29), channel_id=1, source_target_pairs={{0,7},{1,6},{2,5},{3,4},{4,3},{5,2},{6,1},{7,0},{8,15},{9,14},{10,... | collective-permute-start | bytes 442376 | tf_op jit(solution)/shard_map/ppermute | solution.py:633
  22.0 25.4 %collective-permute-start.7 = (bf16[4,32,2304]{2,1,0:T(8,128)(2,1)}, bf16[4,32,2304]{2,1,0:T(8,128)(2,1)}, u32[]{:S(2)}, u32[]{:S(2)}) collective-permute-start(bf16[4,32,2304]{2,1,0:T(8,128)(2,1)} %join.2), channel_id=1, source_target_pairs={{0,16},{8,24},{16,0},{24,8},{1,17},{9,25},{17,1},{25,9},{2,18},{10... | collective-permute-start | bytes 1769480 | tf_op jit(solution)/shard_map/ppermute | solution.py:633
  35.0 21.1 %collective-permute-start.9 = (bf16[4,32,2304]{2,1,0:T(8,128)(2,1)}, bf16[4,32,2304]{2,1,0:T(8,128)(2,1)}, u32[]{:S(2)}, u32[]{:S(2)}) collective-permute-start(bf16[4,32,2304]{2,1,0:T(8,128)(2,1)} %join.3), channel_id=1, source_target_pairs={{0,16},{8,24},{16,0},{24,8},{1,17},{9,25},{17,1},{25,9},{2,18},{10... | collective-permute-start | bytes 1769480 | tf_op jit(solution)/shard_map/ppermute | solution.py:633
  47.3 26.9 %all-to-all-start = ((bf16[8,16,2304]{2,1,0:T(8,128)(2,1)}), bf16[8,16,2304]{2,1,0:T(8,128)(2,1)}, u32[]{:S(2)}, u32[]{:S(2)}) async-start(bf16[8,16,2304]{2,1,0:T(8,128)(2,1)} %get-tuple-element.31), calls=%async_computation | async-start | bytes 1179648 | tf_op jit(solution)/shard_map/all_to_all | solution.py:637
  56.0 2.9 %collective-permute-start.8 = (bf16[144,3328]{1,0:T(8,128)(2,1)}, bf16[144,3328]{1,0:T(8,128)(2,1)}, u32[]{:S(2)}, u32[]{:S(2)}) collective-permute-start(bf16[144,3328]{1,0:T(8,128)(2,1)} %get-tuple-element.33), channel_id=1, source_target_pairs={{0,8},{8,0},{16,24},{24,16},{1,9},{9,1},{17,25},{25,17},{2,10},{10... | collective-permute-start | bytes 2875400 | tf_op jit(solution)/shard_map/ppermute | solution.py:633
  56.0 3.7 %collective-permute-start.11 = (bf16[4,32,2304]{2,1,0:T(8,128)(2,1)}, bf16[4,32,2304]{2,1,0:T(8,128)(2,1)}, u32[]{:S(2)}, u32[]{:S(2)}) collective-permute-start(bf16[4,32,2304]{2,1,0:T(8,128)(2,1)} %collective-permute-done.9.refs_3_), channel_id=1, source_target_pairs={{0,8},{8,0},{16,24},{24,16},{1,9},{9,1},{17,25},{25,17},{2,10},{10... | collective-permute-start | bytes 1769480 | tf_op jit(solution)/shard_map/ppermute | solution.py:633
  56.5 4.0 %collective-permute-start.10 = (bf16[4,32,2304]{2,1,0:T(8,128)(2,1)}, bf16[4,32,2304]{2,1,0:T(8,128)(2,1)}, u32[]{:S(2)}, u32[]{:S(2)}) collective-permute-start(bf16[4,32,2304]{2,1,0:T(8,128)(2,1)} %collective-permute-done.7.refs_2_), channel_id=1, source_target_pairs={{0,8},{8,0},{16,24},{24,16},{1,9},{9,1},{17,25},{25,17},{2,10},{10... | collective-permute-start | bytes 1769480 | tf_op jit(solution)/shard_map/ppermute | solution.py:633

commit v15 on v14

--- a/solution.py
+++ b/solution.py
@@ -333,7 +333,7 @@
         gate_ref, up_ref, down_ref, out, kept, handed = [refs.pop(0) for _ in range(6)]
         x_held, dy_held, rows, scaled, factors, cuts = [refs.pop(0) for _ in range(6)]
         tail, staged, gate, up, down = [refs.pop(0) for _ in range(5)]
-        x_in, dy_in, gate_in, up_in, down_in, gone, cut_in = refs
+        x_in, dy_in, gate_in, up_in, down_in, gone, cut_in, turned = refs
         now = pl.program_id(0)
         x_pairs, dy_pairs = halves(group_refs, 0, x_held), halves(group_refs, 1, dy_held)
 
@@ -407,14 +407,14 @@
                 cuts[at, :, :share] = rows[:, columns]
                 cuts[at, :, share:] = scaled[:, columns]
             start(leave_factors(), cut_in)
+            turned[...] = factors[:, hid:].T
 
         @pl.when(now >= tiles)
         def _():
             at = now - tiles
             here = tile_of(at, chunk)
-            done = dot(factors[:, hid : 2 * hid], gate[here, :], BY_WIDTH)
-            done += dot(factors[:, 2 * hid :], up[here, :], BY_WIDTH)
-            done = done.astype(jnp.bfloat16)
+            done = dot(gate[here, :], turned[:hid, :]) + dot(up[here, :], turned[hid:, :])
+            done = done.T.astype(jnp.bfloat16)
             for block in range(blocks):
                 staged[me_ref[0] ^ block, :, here] = done[block * ROWS : (block + 1) * ROWS]
             leave(at).start()
@@ -468,6 +468,7 @@
             pltpu.SemaphoreType.DMA((tiles,)),
             pltpu.SemaphoreType.DMA((chunks + 1,)),
             pltpu.SemaphoreType.DMA((4,)),
+            pltpu.VMEM((2 * hid, slots), jnp.bfloat16),
         ],
         compiler_params=params(),
         cost_estimate=cost(50 * slots * width * hid, 4 * slots * width),
@@ -494,7 +495,7 @@
         x_held, dy_held, x_all, dy_all = [refs.pop(0) for _ in range(4)]
         x_mine, dy_mine, factors = [refs.pop(0) for _ in range(3)]
         gate, up, down, x_in, dy_in, known_in, gate_in, up_in, down_in = refs[:9]
-        made_gate, made_up, made_down, gate_out, up_out, down_out = refs[9:]
+        made_gate, made_up, made_down, gate_out, up_out, down_out, x_turned = refs[9:]
         now = pl.program_id(0)
         columns = tile_of(part_ref[0], share)
         x_pairs, dy_pairs, known_pairs = [], [], []
@@ -566,11 +567,12 @@
         @pl.when(now == 0)
         def _():
             wait(known_pairs, known_in)
+            x_turned[...] = x_mine[...].T
 
         made = jnp.concatenate([factors[:, tile_of(now, tile)], made], 0)
         d_gate = jnp.concatenate([factors[:, tile_of(tiles + now, tile)], d_gate], 0)
         d_up = jnp.concatenate([factors[:, tile_of(2 * tiles + now, tile)], d_up], 0)
-        sums = dot(x_mine[...], jnp.concatenate([d_gate, d_up], 1), BY_ROWS)
+        sums = dot(x_turned[...], jnp.concatenate([d_gate, d_up], 1))
         made_gate[now] = sums[:, :tile]
         made_up[now] = sums[:, tile:]
         leave(made_gate, d_gate_ref, gate_out, now, 1).start()
@@ -621,6 +623,7 @@
             pltpu.SemaphoreType.DMA((tiles,)),
             pltpu.SemaphoreType.DMA((tiles,)),
             pltpu.SemaphoreType.DMA((tiles,)),
+            pltpu.VMEM((share, total), jnp.bfloat16),
         ],
         compiler_params=params(),
         cost_estimate=cost(0, 4 * slots * width),

time: 76.9 us -> 77.3 us (level)
  no operation moved by 1% of the time
where the time goes in v15:
time: 77.3 us; the launch traced here: 76.9 us
  Pallas kernels  34 us (44%)
  starting transfers between devices  26 us (34%)
  waiting for transfers between devices  16.2 us (21%)
    ppermute x12, starting transfers between devices, swap(): lax.ppermute(value, axis, [(at, at ^ distance) for at in range(size)])  17.3 us
    ppermute x12, waiting for transfers between devices, swap(): lax.ppermute(value, axis, [(at, at ^ distance) for at in range(size)])  16.2 us
    pallas_call x1, Pallas kernels, weight_grads(): pl.pallas_call(kernel, grid=(tiles,), out_shape=[jax.ShapeDtypeStruct((sh...  13.8 us
    pallas_call x1, Pallas kernels, back(): pl.pallas_call(kernel, grid=(tiles + chunks,), out_shape=[jax.ShapeDtypeS...  10.9 us
    all_to_all x1, starting transfers between devices, exchange(): lax.all_to_all(blocks, 'expert', split_axis=0, concat_axis=0, tiled=True)  8.68 us
    pallas_call x2, Pallas kernels, join(): pl.pallas_call(kernel, out_shape=jax.ShapeDtypeStruct((count,) + received...  3.94 us
    pallas_call x1, Pallas kernels, pack(): pl.pallas_call(kernel, out_shape=[jax.ShapeDtypeStruct((2 * ROWS, width +...  2.99 us
    pallas_call x1, Pallas kernels, merge(): pl.pallas_call(kernel, out_shape=jax.ShapeDtypeStruct((tokens, width), jn...  2.36 us
  transfers between devices with their start and end apart: 13, of which 6 were waited for; matrix products, arithmetic and copies ran while one was open for 0% of the time, Pallas kernels for 37%

profile of v15, /device:TPU:0, one launch (start us, length us, event | category | flops | bytes accessed | tf_op | source)
XLA Modules:
  0.0 76.9 jit_solution(16124933060988258487)
XLA Ops:
  0.6 3.0 %pack.1 = (bf16[32,2304]{1,0:T(8,128)(2,1)}, bf16[32,2304]{1,0:T(8,128)(2,1)}, bf16[32,2304]{1,0:T(8,128)(2,1)}, bf16[32,2304]{1,0:T(8,128)(2,1)}, bf16[32,2304]...) custom-call(s32[1]{0:T(128)} %bitcast.1.me_ref, ...), custom_call_target="tpu_custom_call" | custom-call | flops 268435456 | bytes 2097152 | tf_op jit(solution)/shard_map/pack/pallas_call | solution.py:195
  3.6 3.0 %collective-permute-start = (bf16[32,2304]{1,0:T(8,128)(2,1)}, bf16[32,2304]{1,0:T(8,128)(2,1)S(1)}, u32[]{:S(2)}, u32[]{:S(2)}) collective-permute-start(bf16[32,2304]{1,0:T(8,128)(2,1)} %get-tuple-element.23), channel_id=1, source_target_pairs={{0,1},{1,0},{2,3},{3,2},{4,5},{5,4},{6,7},{7,6},{8,9},{9,8},{10,11... | collective-permute-start | bytes 442376 | tf_op jit(solution)/shard_map/ppermute | solution.py:636
  6.6 1.6 %collective-permute-start.1 = (bf16[32,2304]{1,0:T(8,128)(2,1)}, bf16[32,2304]{1,0:T(8,128)(2,1)}, u32[]{:S(2)}, u32[]{:S(2)}) collective-permute-start(bf16[32,2304]{1,0:T(8,128)(2,1)} %get-tuple-element.24), channel_id=1, source_target_pairs={{0,2},{1,3},{2,0},{3,1},{4,6},{5,7},{6,4},{7,5},{8,10},{9,11},{10,... | collective-permute-start | bytes 442376 | tf_op jit(solution)/shard_map/ppermute | solution.py:636
  8.2 0.0 collective-permute-start.2
  8.2 3.0 %collective-permute-start.3 = (bf16[32,2304]{1,0:T(8,128)(2,1)}, bf16[32,2304]{1,0:T(8,128)(2,1)}, u32[]{:S(2)}, u32[]{:S(2)}) collective-permute-start(bf16[32,2304]{1,0:T(8,128)(2,1)} %get-tuple-element.26), channel_id=1, source_target_pairs={{0,4},{1,5},{2,6},{3,7},{4,0},{5,1},{6,2},{7,3},{8,12},{9,13},{10,... | collective-permute-start | bytes 442376 | tf_op jit(solution)/shard_map/ppermute | solution.py:636
  11.2 1.3 %collective-permute-start.4 = (bf16[32,2304]{1,0:T(8,128)(2,1)}, bf16[32,2304]{1,0:T(8,128)(2,1)}, u32[]{:S(2)}, u32[]{:S(2)}) collective-permute-start(bf16[32,2304]{1,0:T(8,128)(2,1)} %get-tuple-element.27), channel_id=1, source_target_pairs={{0,5},{1,4},{2,7},{3,6},{4,1},{5,0},{6,3},{7,2},{8,13},{9,12},{10,... | collective-permute-start | bytes 442376 | tf_op jit(solution)/shard_map/ppermute | solution.py:636
  12.5 3.6 %collective-permute-start.5 = (bf16[32,2304]{1,0:T(8,128)(2,1)}, bf16[32,2304]{1,0:T(8,128)(2,1)}, u32[]{:S(2)}, u32[]{:S(2)}) collective-permute-start(bf16[32,2304]{1,0:T(8,128)(2,1)} %get-tuple-element.28), channel_id=1, source_target_pairs={{0,6},{1,7},{2,4},{3,5},{4,2},{5,3},{6,0},{7,1},{8,14},{9,15},{10,... | collective-permute-start | bytes 442376 | tf_op jit(solution)/shard_map/ppermute | solution.py:636
  16.1 2.8 %collective-permute-done.1.refs_2_ = bf16[32,2304]{1,0:T(8,128)(2,1)} collective-permute-done((bf16[32,2304]{1,0:T(8,128)(2,1)}, bf16[32,2304]{1,0:T(8,128)(2,1)}, u32[]{:S(2)}, u32[]{:S(2)}) %collective-permute-start.1) | collective-permute-done | bytes 147488 | tf_op jit(solution)/shard_map/ppermute | solution.py:636
  18.9 0.9 %collective-permute-start.6 = (bf16[32,2304]{1,0:T(8,128)(2,1)}, bf16[32,2304]{1,0:T(8,128)(2,1)}, u32[]{:S(2)}, u32[]{:S(2)}) collective-permute-start(bf16[32,2304]{1,0:T(8,128)(2,1)} %get-tuple-element.29), channel_id=1, source_target_pairs={{0,7},{1,6},{2,5},{3,4},{4,3},{5,2},{6,1},{7,0},{8,15},{9,14},{10,... | collective-permute-start | bytes 442376 | tf_op jit(solution)/shard_map/ppermute | solution.py:636
  19.9 0.1 collective-permute-done.2.refs_3_
  20.0 2.0 %join.2 = bf16[4,32,2304]{2,1,0:T(8,128)(2,1)} custom-call(bf16[32,2304]{1,0:T(8,128)(2,1)} %get-tuple-element.22.refs_0_, bf16[32,2304]{1,0:T(8,128)(2,1)} %copy-done, bf16[32,2304]{1,0:T(8,128)(2,1)} %collective-permute-done.1.refs_2_, bf16[32,2304]{1,0:T(8,128)(2,1)} %collective-permute-done.2.refs_3_), custom_call_target="tpu_custom_call" | custom-call | bytes 1179648 | tf_op jit(solution)/shard_map/join/pallas_call | solution.py:216
  22.0 1.8 %collective-permute-start.7 = (bf16[4,32,2304]{2,1,0:T(8,128)(2,1)}, bf16[4,32,2304]{2,1,0:T(8,128)(2,1)}, u32[]{:S(2)}, u32[]{:S(2)}) collective-permute-start(bf16[4,32,2304]{2,1,0:T(8,128)(2,1)} %join.2), channel_id=1, source_target_pairs={{0,16},{8,24},{16,0},{24,8},{1,17},{9,25},{17,1},{25,9},{2,18},{10... | collective-permute-start | bytes 1769480 | tf_op jit(solution)/shard_map/ppermute | solution.py:636
  23.7 9.3 %collective-permute-done.4.refs_5_.refs_1_ = bf16[32,2304]{1,0:T(8,128)(2,1)} collective-permute-done((bf16[32,2304]{1,0:T(8,128)(2,1)}, bf16[32,2304]{1,0:T(8,128)(2,1)}, u32[]{:S(2)}, u32[]{:S(2)}) %collective-permute-start.4) | collective-permute-done | bytes 147488 | tf_op jit(solution)/shard_map/ppermute | solution.py:636
  33.0 2.0 %join.3 = bf16[4,32,2304]{2,1,0:T(8,128)(2,1)} custom-call(bf16[32,2304]{1,0:T(8,128)(2,1)} %collective-permute-done.3.refs_4_.refs_0_, bf16[32,2304]{1,0:T(8,128)(2,1)} %collective-permute-done.4.refs_5_.refs_1_, bf16[32,2304]{1,0:T(8,128)(2,1)} %collective-permute-done.5.refs_6_.refs_2_, bf16[32,2304]{1,0:T(8,128)(2,1)} %collective-permute-done.6.refs_7_.refs_3_), custom_call_target="tpu_custom_call" | custom-call | bytes 1179648 | tf_op jit(solution)/shard_map/join/pallas_call | solution.py:216
  35.0 1.6 %collective-permute-start.9 = (bf16[4,32,2304]{2,1,0:T(8,128)(2,1)}, bf16[4,32,2304]{2,1,0:T(8,128)(2,1)}, u32[]{:S(2)}, u32[]{:S(2)}) collective-permute-start(bf16[4,32,2304]{2,1,0:T(8,128)(2,1)} %join.3), channel_id=1, source_target_pairs={{0,16},{8,24},{16,0},{24,8},{1,17},{9,25},{17,1},{25,9},{2,18},{10... | collective-permute-start | bytes 1769480 | tf_op jit(solution)/shard_map/ppermute | solution.py:636
  36.6 10.9 %back.1 = (bf16[8,16,2304]{2,1,0:T(8,128)(2,1)}, bf16[144,3328]{1,0:T(8,128)(2,1)}, bf16[144,3328]{1,0:T(8,128)(2,1)}) custom-call(s32[1]{0:T(128)} %bitcast.1.me_ref, s32[1]{0:T(128)} %bitcast.2.part_ref, bf16[32,2304]{1,0:T(8,128)(2,1)} %get-tuple-element.22.refs_0_, bf16[32,2304]{1,0:T(8,128)(2,1)} %copy-done, ...), custom_call_target="tpu_custom_call" | custom-call | flops 11324620800 | bytes 1179648 | tf_op jit(solution)/shard_map/back/pallas_call | solution.py:442
  47.5 8.7 %all-to-all-start = ((bf16[8,16,2304]{2,1,0:T(8,128)(2,1)}), bf16[8,16,2304]{2,1,0:T(8,128)(2,1)}, u32[]{:S(2)}, u32[]{:S(2)}) async-start(bf16[8,16,2304]{2,1,0:T(8,128)(2,1)} %get-tuple-element.31), calls=%async_computation | async-start | bytes 1179648 | tf_op jit(solution)/shard_map/all_to_all | solution.py:640
  56.2 0.5 collective-permute-start.11
  56.7 0.1 collective-permute-start.10
  56.8 2.3 %collective-permute-done.8.refs_1_ = bf16[144,3328]{1,0:T(8,128)(2,1)} collective-permute-done((bf16[144,3328]{1,0:T(8,128)(2,1)}, bf16[144,3328]{1,0:T(8,128)(2,1)}, u32[]{:S(2)}, u32[]{:S(2)}) %collective-permute-start.8) | collective-permute-done | bytes 958496 | tf_op jit(solution)/shard_map/ppermute | solution.py:636
  59.1 0.8 %collective-permute-done.11.refs_5_ = bf16[4,32,2304]{2,1,0:T(8,128)(2,1)} collective-permute-done((bf16[4,32,2304]{2,1,0:T(8,128)(2,1)}, bf16[4,32,2304]{2,1,0:T(8,128)(2,1)}, u32[]{:S(2)}, u32[]{:S(2)}) %collective-permute-start.11) | collective-permute-done | bytes 589856 | tf_op jit(solution)/shard_map/ppermute | solution.py:636
  59.9 0.8 %collective-permute-done.10.refs_4_ = bf16[4,32,2304]{2,1,0:T(8,128)(2,1)} collective-permute-done((bf16[4,32,2304]{2,1,0:T(8,128)(2,1)}, bf16[4,32,2304]{2,1,0:T(8,128)(2,1)}, u32[]{:S(2)}, u32[]{:S(2)}) %collective-permute-start.10) | collective-permute-done | bytes 589856 | tf_op jit(solution)/shard_map/ppermute | solution.py:636
  60.8 13.8 %weight_grads.1 = (f32[512,768]{1,0:T(8,128)}, f32[512,768]{1,0:T(8,128)}, f32[768,512]{1,0:T(8,128)}) custom-call(s32[1]{0:T(128)} %bitcast.2.part_ref, bf16[144,3328]{1,0:T(8,128)(2,1)} %get-tuple-element.32.refs_0_, bf16[144,3328]{1,0:T(8,128)(2,1)} %collective-permute-done.8.refs_1_, bf16[4,32,2304]{2,1,0:T(8,128)(2,1)} %collective-permute-done.7.refs_2_, ...), custom_call_target="tpu_custom_call" | custom-call | bytes 1179648 | tf_op jit(solution)/shard_map/weight_grads/pallas_call | solution.py:593
  74.6 2.4 %merge.1 = bf16[128,2048]{1,0:T(8,128)(2,1)} custom-call(s32[1,128]{1,0:T(1,128)} %bitcast.5, bf16[8,16,2304]{2,1,0:T(8,128)(2,1)} %all-to-all-done.back_ref), custom_call_target="tpu_custom_call" | custom-call | flops 134217728 | bytes 1048576 | tf_op jit(solution)/shard_map/merge/pallas_call | solution.py:251
  (10 shorter events, 0.0 us)
Async XLA Ops:
  3.6 8.9 %collective-permute-start = (bf16[32,2304]{1,0:T(8,128)(2,1)}, bf16[32,2304]{1,0:T(8,128)(2,1)S(1)}, u32[]{:S(2)}, u32[]{:S(2)}) collective-permute-start(bf16[32,2304]{1,0:T(8,128)(2,1)} %get-tuple-element.23), channel_id=1, source_target_pairs={{0,1},{1,0},{2,3},{3,2},{4,5},{5,4},{6,7},{7,6},{8,9},{9,8},{10,11... | collective-permute-start | bytes 442376 | tf_op jit(solution)/shard_map/ppermute | solution.py:636
  6.6 12.3 %collective-permute-start.1 = (bf16[32,2304]{1,0:T(8,128)(2,1)}, bf16[32,2304]{1,0:T(8,128)(2,1)}, u32[]{:S(2)}, u32[]{:S(2)}) collective-permute-start(bf16[32,2304]{1,0:T(8,128)(2,1)} %get-tuple-element.24), channel_id=1, source_target_pairs={{0,2},{1,3},{2,0},{3,1},{4,6},{5,7},{6,4},{7,5},{8,10},{9,11},{10,... | collective-permute-start | bytes 442376 | tf_op jit(solution)/shard_map/ppermute | solution.py:636
  8.2 11.8 %collective-permute-start.2 = (bf16[32,2304]{1,0:T(8,128)(2,1)}, bf16[32,2304]{1,0:T(8,128)(2,1)}, u32[]{:S(2)}, u32[]{:S(2)}) collective-permute-start(bf16[32,2304]{1,0:T(8,128)(2,1)} %get-tuple-element.25), channel_id=1, source_target_pairs={{0,3},{1,2},{2,1},{3,0},{4,7},{5,6},{6,5},{7,4},{8,11},{9,10},{10,... | collective-permute-start | bytes 442376 | tf_op jit(solution)/shard_map/ppermute | solution.py:636
  8.2 15.5 %collective-permute-start.3 = (bf16[32,2304]{1,0:T(8,128)(2,1)}, bf16[32,2304]{1,0:T(8,128)(2,1)}, u32[]{:S(2)}, u32[]{:S(2)}) collective-permute-start(bf16[32,2304]{1,0:T(8,128)(2,1)} %get-tuple-element.26), channel_id=1, source_target_pairs={{0,4},{1,5},{2,6},{3,7},{4,0},{5,1},{6,2},{7,3},{8,12},{9,13},{10,... | collective-permute-start | bytes 442376 | tf_op jit(solution)/shard_map/ppermute | solution.py:636
  11.2 21.8 %collective-permute-start.4 = (bf16[32,2304]{1,0:T(8,128)(2,1)}, bf16[32,2304]{1,0:T(8,128)(2,1)}, u32[]{:S(2)}, u32[]{:S(2)}) collective-permute-start(bf16[32,2304]{1,0:T(8,128)(2,1)} %get-tuple-element.27), channel_id=1, source_target_pairs={{0,5},{1,4},{2,7},{3,6},{4,1},{5,0},{6,3},{7,2},{8,13},{9,12},{10,... | collective-permute-start | bytes 442376 | tf_op jit(solution)/shard_map/ppermute | solution.py:636
  12.5 7.5 %copy-start = (bf16[32,2304]{1,0:T(8,128)(2,1)}, bf16[32,2304]{1,0:T(8,128)(2,1)S(1)}, u32[]{:S(2)}) copy-start(bf16[32,2304]{1,0:T(8,128)(2,1)S(1)} %collective-permute-done.refs_1_) | copy-start | bytes 442372
  12.5 20.5 %collective-permute-start.5 = (bf16[32,2304]{1,0:T(8,128)(2,1)}, bf16[32,2304]{1,0:T(8,128)(2,1)}, u32[]{:S(2)}, u32[]{:S(2)}) collective-permute-start(bf16[32,2304]{1,0:T(8,128)(2,1)} %get-tuple-element.28), channel_id=1, source_target_pairs={{0,6},{1,7},{2,4},{3,5},{4,2},{5,3},{6,0},{7,1},{8,14},{9,15},{10,... | collective-permute-start | bytes 442376 | tf_op jit(solution)/shard_map/ppermute | solution.py:636
  18.9 14.1 %collective-permute-start.6 = (bf16[32,2304]{1,0:T(8,128)(2,1)}, bf16[32,2304]{1,0:T(8,128)(2,1)}, u32[]{:S(2)}, u32[]{:S(2)}) collective-permute-start(bf16[32,2304]{1,0:T(8,128)(2,1)} %get-tuple-element.29), channel_id=1, source_target_pairs={{0,7},{1,6},{2,5},{3,4},{4,3},{5,2},{6,1},{7,0},{8,15},{9,14},{10,... | collective-permute-start | bytes 442376 | tf_op jit(solution)/shard_map/ppermute | solution.py:636
  22.0 25.6 %collective-permute-start.7 = (bf16[4,32,2304]{2,1,0:T(8,128)(2,1)}, bf16[4,32,2304]{2,1,0:T(8,128)(2,1)}, u32[]{:S(2)}, u32[]{:S(2)}) collective-permute-start(bf16[4,32,2304]{2,1,0:T(8,128)(2,1)} %join.2), channel_id=1, source_target_pairs={{0,16},{8,24},{16,0},{24,8},{1,17},{9,25},{17,1},{25,9},{2,18},{10... | collective-permute-start | bytes 1769480 | tf_op jit(solution)/shard_map/ppermute | solution.py:636
  35.0 21.2 %collective-permute-start.9 = (bf16[4,32,2304]{2,1,0:T(8,128)(2,1)}, bf16[4,32,2304]{2,1,0:T(8,128)(2,1)}, u32[]{:S(2)}, u32[]{:S(2)}) collective-permute-start(bf16[4,32,2304]{2,1,0:T(8,128)(2,1)} %join.3), channel_id=1, source_target_pairs={{0,16},{8,24},{16,0},{24,8},{1,17},{9,25},{17,1},{25,9},{2,18},{10... | collective-permute-start | bytes 1769480 | tf_op jit(solution)/shard_map/ppermute | solution.py:636
  47.5 27.0 %all-to-all-start = ((bf16[8,16,2304]{2,1,0:T(8,128)(2,1)}), bf16[8,16,2304]{2,1,0:T(8,128)(2,1)}, u32[]{:S(2)}, u32[]{:S(2)}) async-start(bf16[8,16,2304]{2,1,0:T(8,128)(2,1)} %get-tuple-element.31), calls=%async_computation | async-start | bytes 1179648 | tf_op jit(solution)/shard_map/all_to_all | solution.py:640
  56.2 2.9 %collective-permute-start.8 = (bf16[144,3328]{1,0:T(8,128)(2,1)}, bf16[144,3328]{1,0:T(8,128)(2,1)}, u32[]{:S(2)}, u32[]{:S(2)}) collective-permute-start(bf16[144,3328]{1,0:T(8,128)(2,1)} %get-tuple-element.33), channel_id=1, source_target_pairs={{0,8},{8,0},{16,24},{24,16},{1,9},{9,1},{17,25},{25,17},{2,10},{10... | collective-permute-start | bytes 2875400 | tf_op jit(solution)/shard_map/ppermute | solution.py:636
  56.2 3.7 %collective-permute-start.11 = (bf16[4,32,2304]{2,1,0:T(8,128)(2,1)}, bf16[4,32,2304]{2,1,0:T(8,128)(2,1)}, u32[]{:S(2)}, u32[]{:S(2)}) collective-permute-start(bf16[4,32,2304]{2,1,0:T(8,128)(2,1)} %collective-permute-done.9.refs_3_), channel_id=1, source_target_pairs={{0,8},{8,0},{16,24},{24,16},{1,9},{9,1},{17,25},{25,17},{2,10},{10... | collective-permute-start | bytes 1769480 | tf_op jit(solution)/shard_map/ppermute | solution.py:636
  56.7 4.0 %collective-permute-start.10 = (bf16[4,32,2304]{2,1,0:T(8,128)(2,1)}, bf16[4,32,2304]{2,1,0:T(8,128)(2,1)}, u32[]{:S(2)}, u32[]{:S(2)}) collective-permute-start(bf16[4,32,2304]{2,1,0:T(8,128)(2,1)} %collective-permute-done.7.refs_2_), channel_id=1, source_target_pairs={{0,8},{8,0},{16,24},{24,16},{1,9},{9,1},{17,25},{25,17},{2,10},{10... | collective-permute-start | bytes 1769480 | tf_op jit(solution)/shard_map/ppermute | solution.py:636

commit v16 on v14

--- a/solution.py
+++ b/solution.py
@@ -264,24 +264,25 @@
     )(routes, returned)
 
 
-def spill_picks(blocks, pieces, at):
-    shape = (blocks * (MOST - ROWS), blocks * ROWS)
-    slot = lax.broadcasted_iota(jnp.int32, shape, 0)
+def spill_picks(blocks, pieces):
+    extras = blocks * (MOST - ROWS)
+    shape = (pieces * extras, blocks * ROWS)
+    index = lax.broadcasted_iota(jnp.int32, shape, 0)
     row = lax.broadcasted_iota(jnp.int32, shape, 1)
-    return ones(row == slot * pieces + at)
-
-
-def unpack(main, tail, pieces, begin, first, out):
-    blocks = main.shape[0]
-    step = tail.shape[2]
+    return ones(row == (index % extras) * pieces + index // extras)
+
+
+def unpack(packed, first, out):
+    blocks, width = packed.shape[0], out.shape[1]
+    pieces, step = cut(width)
+    extras = blocks * (MOST - ROWS)
     for at in range(blocks):
-        out[first + at * ROWS : first + (at + 1) * ROWS, :] = main[at]
-    extra = jnp.concatenate([tail[at] for at in range(blocks)], 0)
+        out[first + at * ROWS : first + (at + 1) * ROWS, :] = packed[at, :, :width]
+    tails = jnp.concatenate([packed[at, :, width:] for at in range(blocks)], 0)
+    placed = dot(spill_picks(blocks, pieces), tails).astype(jnp.bfloat16)
     spill = slice(first + blocks * ROWS, first + blocks * MOST)
-    for at in range(out.shape[1] // step):
-        out[spill, at * step : (at + 1) * step] = dot(
-            spill_picks(blocks, pieces, begin + at), extra
-        ).astype(jnp.bfloat16)
+    for at in range(pieces):
+        out[spill, at * step : (at + 1) * step] = placed[at * extras : (at + 1) * extras]
 
 
 def tile_of(index, tile):
@@ -332,13 +333,12 @@
         group_refs = [refs.pop(0) for _ in range(blocks)]
         gate_ref, up_ref, down_ref, out, kept, handed = [refs.pop(0) for _ in range(6)]
         x_held, dy_held, rows, scaled, factors, cuts = [refs.pop(0) for _ in range(6)]
-        tail, staged, gate, up, down = [refs.pop(0) for _ in range(5)]
+        staged, gate, up, down = [refs.pop(0) for _ in range(4)]
         x_in, dy_in, gate_in, up_in, down_in, gone, cut_in = refs
-        now = pl.program_id(0)
         x_pairs, dy_pairs = halves(group_refs, 0, x_held), halves(group_refs, 1, dy_held)
 
         def column_copy(source, target, arrived, index):
-            here = tile_of(index, tile)
+            here = slice(index * tile, (index + 1) * tile)
             return pltpu.make_async_copy(
                 source.at[:, here], target.at[:, here], arrived.at[index]
             )
@@ -351,97 +351,71 @@
             weight_copy(down_ref, down, down_in, index, 0, tile).start()
 
         def leave(index):
-            columns = tile_of(index, chunk)
+            columns = slice(index * chunk, (index + 1) * chunk)
             return pltpu.make_async_copy(
                 staged.at[:, :, columns], out.at[:, :, columns], gone.at[index]
             )
 
-        def leave_factors():
-            first, behind = slice(0, 3 * hid), slice(3 * hid, given)
-            pairs = [(factors, kept.at[:, first]), (cuts.at[0], kept.at[:, behind])]
-            return pairs + [(factors, handed.at[:, first]), (cuts.at[1], handed.at[:, behind])]
-
-        @pl.when(now == 0)
-        def _():
-            start(x_pairs, x_in)
-            fetch_x(0)
-            wait(x_pairs, x_in)
-            start(dy_pairs, dy_in)
-            fetch_dy(0)
-            unpack(x_held.at[:, :, :width], x_held.at[:, :, width:], pieces, 0, 0, rows)
-            tail[...] = jnp.zeros_like(tail)
-
-        @pl.when(now < tiles)
-        def _():
-            columns = tile_of(now, tile)
+        first, behind = slice(0, 3 * hid), slice(3 * hid, given)
+        leaving = [(factors, kept.at[:, first]), (cuts.at[0], kept.at[:, behind])]
+        leaving += [(factors, handed.at[:, first]), (cuts.at[1], handed.at[:, behind])]
+
+        start(x_pairs, x_in)
+        fetch_x(0)
+        wait(x_pairs, x_in)
+        start(dy_pairs, dy_in)
+        fetch_dy(0)
+        unpack(x_held, 0, rows)
+        for now in range(tiles):
+            columns = slice(now * tile, (now + 1) * tile)
             column_copy(gate_ref, gate, gate_in, now).wait()
             pre_gate = dot(rows[...], gate[:, columns])
-
-            @pl.when(now < tiles - 1)
-            def _():
+            if now < tiles - 1:
                 fetch_x(now + 1)
-
             column_copy(up_ref, up, up_in, now).wait()
             pre_up = dot(rows[...], up[:, columns])
-
-            @pl.when(now == 0)
-            def _():
+            if now == 0:
                 wait(dy_pairs, dy_in)
-                unpack(dy_held.at[:, :, :width], dy_held.at[:, :, width:], pieces, 0, 0, scaled)
-
-            @pl.when(now < tiles - 1)
-            def _():
+                unpack(dy_held, 0, scaled)
+            if now < tiles - 1:
                 fetch_dy(now + 1)
-
             weight_copy(down_ref, down, down_in, now, 0, tile).wait()
             d_hidden = dot(scaled[...], down[now], BY_WIDTH)
             made, d_gate, d_up = hidden_grads(pre_gate, pre_up, d_hidden)
             factors[:, columns] = made
-            factors[:, tile_of(tiles + now, tile)] = d_gate
-            factors[:, tile_of(2 * tiles + now, tile)] = d_up
-
-        @pl.when(now == tiles)
-        def _():
-            for at in range(2):
-                columns = tile_of(part_ref[0] ^ at, share)
-                cuts[at, :, :share] = rows[:, columns]
-                cuts[at, :, share:] = scaled[:, columns]
-            start(leave_factors(), cut_in)
-
-        @pl.when(now >= tiles)
-        def _():
-            at = now - tiles
-            here = tile_of(at, chunk)
+            factors[:, hid + now * tile : hid + (now + 1) * tile] = d_gate
+            factors[:, 2 * hid + now * tile : 2 * hid + (now + 1) * tile] = d_up
+
+        for at in range(2):
+            columns = tile_of(part_ref[0] ^ at, share)
+            cuts[at, :, :share] = rows[:, columns]
+            cuts[at, :, share:] = scaled[:, columns]
+        start(leaving, cut_in)
+        extras = []
+        for at in range(chunks):
+            here = slice(at * chunk, (at + 1) * chunk)
             done = dot(factors[:, hid : 2 * hid], gate[here, :], BY_WIDTH)
             done += dot(factors[:, 2 * hid :], up[here, :], BY_WIDTH)
             done = done.astype(jnp.bfloat16)
             for block in range(blocks):
                 staged[me_ref[0] ^ block, :, here] = done[block * ROWS : (block + 1) * ROWS]
             leave(at).start()
-            for piece in range(chunk // step):
-                tail[...] += dot(
-                    spill_picks(blocks, pieces, at * (chunk // step) + piece),
-                    done[blocks * ROWS :, piece * step : (piece + 1) * step],
-                    BY_ROWS,
-                )
-
-        @pl.when(now == tiles + chunks - 1)
-        def _():
-            for block in range(blocks):
-                part = tail[block * ROWS : (block + 1) * ROWS, :]
-                staged[me_ref[0] ^ block, :, width:] = part.astype(jnp.bfloat16)
-            last = pltpu.make_async_copy(
-                staged.at[:, :, width:], out.at[:, :, width:], gone.at[chunks]
-            )
-            last.start()
-            for at in range(chunks):
-                leave(at).wait()
-            wait(leave_factors(), cut_in)
-            last.wait()
+            extras += [done[blocks * ROWS :, :step], done[blocks * ROWS :, step:]]
+        tail = dot(spill_picks(blocks, pieces), jnp.concatenate(extras, 0), BY_ROWS)
+        tail = tail.astype(jnp.bfloat16)
+        for block in range(blocks):
+            staged[me_ref[0] ^ block, :, width:] = tail[block * ROWS : (block + 1) * ROWS]
+        last = pltpu.make_async_copy(
+            staged.at[:, :, width:], out.at[:, :, width:], gone.at[chunks]
+        )
+        last.start()
+        for at in range(chunks):
+            leave(at).wait()
+        wait(leaving, cut_in)
+        last.wait()
 
     return pl.pallas_call(
         kernel,
-        grid=(tiles + chunks,),
         out_shape=[
             jax.ShapeDtypeStruct(shape, jnp.bfloat16),
             jax.ShapeDtypeStruct((slots, given), jnp.bfloat16),
@@ -456,7 +430,6 @@
             pltpu.VMEM((slots, width), jnp.bfloat16),
             pltpu.VMEM((slots, 3 * hid), jnp.bfloat16),
             pltpu.VMEM((2, slots, 2 * share), jnp.bfloat16),
-            pltpu.VMEM((blocks * ROWS, step), jnp.float32),
             pltpu.VMEM(shape, jnp.bfloat16),
             pltpu.VMEM((width, hid), jnp.bfloat16),
             pltpu.VMEM((width, hid), jnp.bfloat16),
@@ -512,14 +485,7 @@
 
         def arrange(held, rows_out, target):
             for at in range(count):
-                unpack(
-                    held.at[at, :, :, :width],
-                    held.at[at, :, :, width:],
-                    pieces,
-                    0,
-                    at * slots,
-                    rows_out,
-                )
+                unpack(held.at[at], at * slots, rows_out)
             target[given * slots :, :] = rows_out[:, columns]
 
         def leave(source, target, gone, index, axis):

time: 76.9 us -> 76.1 us (0.990)
  Pallas kernels: 33.7 us -> 32.8 us
    pallas_call x1, Pallas kernels: 10.8 us -> 9.93 us  [back(): pl.pallas_call(kernel, out_shape=[jax.ShapeDtypeStruct(shape, jnp.bfloat1...]
  transfers between devices with their start and end apart: 13 -> 13, of which waited for: 6 -> 6; matrix products, arithmetic and copies ran while one was open for 0% -> 0% of each run, Pallas kernels for 37% -> 36%
where the time goes in v16:
time: 76.1 us; the launch traced here: 75.8 us
  Pallas kernels  32.8 us (43%)
  starting transfers between devices  26 us (34%)
  waiting for transfers between devices  16.2 us (21%)
    ppermute x12, starting transfers between devices, swap(): lax.ppermute(value, axis, [(at, at ^ distance) for at in range(size)])  17.3 us
    ppermute x12, waiting for transfers between devices, swap(): lax.ppermute(value, axis, [(at, at ^ distance) for at in range(size)])  16.2 us
    pallas_call x1, Pallas kernels, weight_grads(): pl.pallas_call(kernel, grid=(tiles,), out_shape=[jax.ShapeDtypeStruct((sh...  13.6 us
    pallas_call x1, Pallas kernels, back(): pl.pallas_call(kernel, out_shape=[jax.ShapeDtypeStruct(shape, jnp.bfloat1...  9.93 us
    all_to_all x1, starting transfers between devices, exchange(): lax.all_to_all(blocks, 'expert', split_axis=0, concat_axis=0, tiled=True)  8.68 us
    pallas_call x2, Pallas kernels, join(): pl.pallas_call(kernel, out_shape=jax.ShapeDtypeStruct((count,) + received...  3.94 us
    pallas_call x1, Pallas kernels, pack(): pl.pallas_call(kernel, out_shape=[jax.ShapeDtypeStruct((2 * ROWS, width +...  2.99 us
    pallas_call x1, Pallas kernels, merge(): pl.pallas_call(kernel, out_shape=jax.ShapeDtypeStruct((tokens, width), jn...  2.36 us
  transfers between devices with their start and end apart: 13, of which 6 were waited for; matrix products, arithmetic and copies ran while one was open for 0% of the time, Pallas kernels for 36%

profile of v16, /device:TPU:0, one launch (start us, length us, event | category | flops | bytes accessed | tf_op | source)
XLA Modules:
  0.0 75.8 jit_solution(5740603772980270234)
XLA Ops:
  0.6 3.0 %pack.1 = (bf16[32,2304]{1,0:T(8,128)(2,1)}, bf16[32,2304]{1,0:T(8,128)(2,1)}, bf16[32,2304]{1,0:T(8,128)(2,1)}, bf16[32,2304]{1,0:T(8,128)(2,1)}, bf16[32,2304]...) custom-call(s32[1]{0:T(128)} %bitcast.1.me_ref, ...), custom_call_target="tpu_custom_call" | custom-call | flops 268435456 | bytes 2097152 | tf_op jit(solution)/shard_map/pack/pallas_call | solution.py:195
  3.6 3.0 %collective-permute-start = (bf16[32,2304]{1,0:T(8,128)(2,1)}, bf16[32,2304]{1,0:T(8,128)(2,1)S(1)}, u32[]{:S(2)}, u32[]{:S(2)}) collective-permute-start(bf16[32,2304]{1,0:T(8,128)(2,1)} %get-tuple-element.23), channel_id=1, source_target_pairs={{0,1},{1,0},{2,3},{3,2},{4,5},{5,4},{6,7},{7,6},{8,9},{9,8},{10,11... | collective-permute-start | bytes 442376 | tf_op jit(solution)/shard_map/ppermute | solution.py:599
  6.6 1.6 %collective-permute-start.1 = (bf16[32,2304]{1,0:T(8,128)(2,1)}, bf16[32,2304]{1,0:T(8,128)(2,1)}, u32[]{:S(2)}, u32[]{:S(2)}) collective-permute-start(bf16[32,2304]{1,0:T(8,128)(2,1)} %get-tuple-element.24), channel_id=1, source_target_pairs={{0,2},{1,3},{2,0},{3,1},{4,6},{5,7},{6,4},{7,5},{8,10},{9,11},{10,... | collective-permute-start | bytes 442376 | tf_op jit(solution)/shard_map/ppermute | solution.py:599
  8.2 3.0 %collective-permute-start.3 = (bf16[32,2304]{1,0:T(8,128)(2,1)}, bf16[32,2304]{1,0:T(8,128)(2,1)}, u32[]{:S(2)}, u32[]{:S(2)}) collective-permute-start(bf16[32,2304]{1,0:T(8,128)(2,1)} %get-tuple-element.26), channel_id=1, source_target_pairs={{0,4},{1,5},{2,6},{3,7},{4,0},{5,1},{6,2},{7,3},{8,12},{9,13},{10,... | collective-permute-start | bytes 442376 | tf_op jit(solution)/shard_map/ppermute | solution.py:599
  11.2 1.3 %collective-permute-start.4 = (bf16[32,2304]{1,0:T(8,128)(2,1)}, bf16[32,2304]{1,0:T(8,128)(2,1)}, u32[]{:S(2)}, u32[]{:S(2)}) collective-permute-start(bf16[32,2304]{1,0:T(8,128)(2,1)} %get-tuple-element.27), channel_id=1, source_target_pairs={{0,5},{1,4},{2,7},{3,6},{4,1},{5,0},{6,3},{7,2},{8,13},{9,12},{10,... | collective-permute-start | bytes 442376 | tf_op jit(solution)/shard_map/ppermute | solution.py:599
  12.5 0.0 collective-permute-done.refs_1_
  12.5 3.6 %collective-permute-start.5 = (bf16[32,2304]{1,0:T(8,128)(2,1)}, bf16[32,2304]{1,0:T(8,128)(2,1)}, u32[]{:S(2)}, u32[]{:S(2)}) collective-permute-start(bf16[32,2304]{1,0:T(8,128)(2,1)} %get-tuple-element.28), channel_id=1, source_target_pairs={{0,6},{1,7},{2,4},{3,5},{4,2},{5,3},{6,0},{7,1},{8,14},{9,15},{10,... | collective-permute-start | bytes 442376 | tf_op jit(solution)/shard_map/ppermute | solution.py:599
  16.1 2.8 %collective-permute-done.1.refs_2_ = bf16[32,2304]{1,0:T(8,128)(2,1)} collective-permute-done((bf16[32,2304]{1,0:T(8,128)(2,1)}, bf16[32,2304]{1,0:T(8,128)(2,1)}, u32[]{:S(2)}, u32[]{:S(2)}) %collective-permute-start.1) | collective-permute-done | bytes 147488 | tf_op jit(solution)/shard_map/ppermute | solution.py:599
  18.9 0.9 %collective-permute-start.6 = (bf16[32,2304]{1,0:T(8,128)(2,1)}, bf16[32,2304]{1,0:T(8,128)(2,1)}, u32[]{:S(2)}, u32[]{:S(2)}) collective-permute-start(bf16[32,2304]{1,0:T(8,128)(2,1)} %get-tuple-element.29), channel_id=1, source_target_pairs={{0,7},{1,6},{2,5},{3,4},{4,3},{5,2},{6,1},{7,0},{8,15},{9,14},{10,... | collective-permute-start | bytes 442376 | tf_op jit(solution)/shard_map/ppermute | solution.py:599
  19.9 0.1 collective-permute-done.2.refs_3_
  20.0 2.0 %join.2 = bf16[4,32,2304]{2,1,0:T(8,128)(2,1)} custom-call(bf16[32,2304]{1,0:T(8,128)(2,1)} %get-tuple-element.22.refs_0_, bf16[32,2304]{1,0:T(8,128)(2,1)} %copy-done, bf16[32,2304]{1,0:T(8,128)(2,1)} %collective-permute-done.1.refs_2_, bf16[32,2304]{1,0:T(8,128)(2,1)} %collective-permute-done.2.refs_3_), custom_call_target="tpu_custom_call" | custom-call | bytes 1179648 | tf_op jit(solution)/shard_map/join/pallas_call | solution.py:216
  22.0 1.8 %collective-permute-start.7 = (bf16[4,32,2304]{2,1,0:T(8,128)(2,1)}, bf16[4,32,2304]{2,1,0:T(8,128)(2,1)}, u32[]{:S(2)}, u32[]{:S(2)}) collective-permute-start(bf16[4,32,2304]{2,1,0:T(8,128)(2,1)} %join.2), channel_id=1, source_target_pairs={{0,16},{8,24},{16,0},{24,8},{1,17},{9,25},{17,1},{25,9},{2,18},{10... | collective-permute-start | bytes 1769480 | tf_op jit(solution)/shard_map/ppermute | solution.py:599
  23.7 9.3 %collective-permute-done.4.refs_5_.refs_1_ = bf16[32,2304]{1,0:T(8,128)(2,1)} collective-permute-done((bf16[32,2304]{1,0:T(8,128)(2,1)}, bf16[32,2304]{1,0:T(8,128)(2,1)}, u32[]{:S(2)}, u32[]{:S(2)}) %collective-permute-start.4) | collective-permute-done | bytes 147488 | tf_op jit(solution)/shard_map/ppermute | solution.py:599
  33.0 2.0 %join.3 = bf16[4,32,2304]{2,1,0:T(8,128)(2,1)} custom-call(bf16[32,2304]{1,0:T(8,128)(2,1)} %collective-permute-done.3.refs_4_.refs_0_, bf16[32,2304]{1,0:T(8,128)(2,1)} %collective-permute-done.4.refs_5_.refs_1_, bf16[32,2304]{1,0:T(8,128)(2,1)} %collective-permute-done.5.refs_6_.refs_2_, bf16[32,2304]{1,0:T(8,128)(2,1)} %collective-permute-done.6.refs_7_.refs_3_), custom_call_target="tpu_custom_call" | custom-call | bytes 1179648 | tf_op jit(solution)/shard_map/join/pallas_call | solution.py:216
  35.0 1.6 %collective-permute-start.9 = (bf16[4,32,2304]{2,1,0:T(8,128)(2,1)}, bf16[4,32,2304]{2,1,0:T(8,128)(2,1)}, u32[]{:S(2)}, u32[]{:S(2)}) collective-permute-start(bf16[4,32,2304]{2,1,0:T(8,128)(2,1)} %join.3), channel_id=1, source_target_pairs={{0,16},{8,24},{16,0},{24,8},{1,17},{9,25},{17,1},{25,9},{2,18},{10... | collective-permute-start | bytes 1769480 | tf_op jit(solution)/shard_map/ppermute | solution.py:599
  36.6 9.9 %back.1 = (bf16[8,16,2304]{2,1,0:T(8,128)(2,1)}, bf16[144,3328]{1,0:T(8,128)(2,1)}, bf16[144,3328]{1,0:T(8,128)(2,1)}) custom-call(s32[1]{0:T(128)} %bitcast.1.me_ref, s32[1]{0:T(128)} %bitcast.2.part_ref, bf16[32,2304]{1,0:T(8,128)(2,1)} %get-tuple-element.22.refs_0_, bf16[32,2304]{1,0:T(8,128)(2,1)} %copy-done, ...), custom_call_target="tpu_custom_call" | custom-call | flops 11324620800 | bytes 1179648 | tf_op jit(solution)/shard_map/back/pallas_call | solution.py:417
  46.5 8.7 %all-to-all-start = ((bf16[8,16,2304]{2,1,0:T(8,128)(2,1)}), bf16[8,16,2304]{2,1,0:T(8,128)(2,1)}, u32[]{:S(2)}, u32[]{:S(2)}) async-start(bf16[8,16,2304]{2,1,0:T(8,128)(2,1)} %get-tuple-element.31), calls=%async_computation | async-start | bytes 1179648 | tf_op jit(solution)/shard_map/all_to_all | solution.py:603
  55.2 0.5 collective-permute-start.11
  55.7 0.1 collective-permute-start.10
  55.8 2.3 %collective-permute-done.8.refs_1_ = bf16[144,3328]{1,0:T(8,128)(2,1)} collective-permute-done((bf16[144,3328]{1,0:T(8,128)(2,1)}, bf16[144,3328]{1,0:T(8,128)(2,1)}, u32[]{:S(2)}, u32[]{:S(2)}) %collective-permute-start.8) | collective-permute-done | bytes 958496 | tf_op jit(solution)/shard_map/ppermute | solution.py:599
  58.1 0.8 %collective-permute-done.11.refs_5_ = bf16[4,32,2304]{2,1,0:T(8,128)(2,1)} collective-permute-done((bf16[4,32,2304]{2,1,0:T(8,128)(2,1)}, bf16[4,32,2304]{2,1,0:T(8,128)(2,1)}, u32[]{:S(2)}, u32[]{:S(2)}) %collective-permute-start.11) | collective-permute-done | bytes 589856 | tf_op jit(solution)/shard_map/ppermute | solution.py:599
  58.9 0.8 %collective-permute-done.10.refs_4_ = bf16[4,32,2304]{2,1,0:T(8,128)(2,1)} collective-permute-done((bf16[4,32,2304]{2,1,0:T(8,128)(2,1)}, bf16[4,32,2304]{2,1,0:T(8,128)(2,1)}, u32[]{:S(2)}, u32[]{:S(2)}) %collective-permute-start.10) | collective-permute-done | bytes 589856 | tf_op jit(solution)/shard_map/ppermute | solution.py:599
  59.8 13.6 %weight_grads.1 = (f32[512,768]{1,0:T(8,128)}, f32[512,768]{1,0:T(8,128)}, f32[768,512]{1,0:T(8,128)}) custom-call(s32[1]{0:T(128)} %bitcast.2.part_ref, bf16[144,3328]{1,0:T(8,128)(2,1)} %get-tuple-element.32.refs_0_, bf16[144,3328]{1,0:T(8,128)(2,1)} %collective-permute-done.8.refs_1_, bf16[4,32,2304]{2,1,0:T(8,128)(2,1)} %collective-permute-done.7.refs_2_, ...), custom_call_target="tpu_custom_call" | custom-call | bytes 1179648 | tf_op jit(solution)/shard_map/weight_grads/pallas_call | solution.py:557
  73.4 2.4 %merge.1 = bf16[128,2048]{1,0:T(8,128)(2,1)} custom-call(s32[1,128]{1,0:T(1,128)} %bitcast.5, bf16[8,16,2304]{2,1,0:T(8,128)(2,1)} %all-to-all-done.back_ref), custom_call_target="tpu_custom_call" | custom-call | flops 134217728 | bytes 1048576 | tf_op jit(solution)/shard_map/merge/pallas_call | solution.py:251
  (10 shorter events, 0.0 us)
Async XLA Ops:
  3.6 8.9 %collective-permute-start = (bf16[32,2304]{1,0:T(8,128)(2,1)}, bf16[32,2304]{1,0:T(8,128)(2,1)S(1)}, u32[]{:S(2)}, u32[]{:S(2)}) collective-permute-start(bf16[32,2304]{1,0:T(8,128)(2,1)} %get-tuple-element.23), channel_id=1, source_target_pairs={{0,1},{1,0},{2,3},{3,2},{4,5},{5,4},{6,7},{7,6},{8,9},{9,8},{10,11... | collective-permute-start | bytes 442376 | tf_op jit(solution)/shard_map/ppermute | solution.py:599
  6.6 12.3 %collective-permute-start.1 = (bf16[32,2304]{1,0:T(8,128)(2,1)}, bf16[32,2304]{1,0:T(8,128)(2,1)}, u32[]{:S(2)}, u32[]{:S(2)}) collective-permute-start(bf16[32,2304]{1,0:T(8,128)(2,1)} %get-tuple-element.24), channel_id=1, source_target_pairs={{0,2},{1,3},{2,0},{3,1},{4,6},{5,7},{6,4},{7,5},{8,10},{9,11},{10,... | collective-permute-start | bytes 442376 | tf_op jit(solution)/shard_map/ppermute | solution.py:599
  8.2 11.8 %collective-permute-start.2 = (bf16[32,2304]{1,0:T(8,128)(2,1)}, bf16[32,2304]{1,0:T(8,128)(2,1)}, u32[]{:S(2)}, u32[]{:S(2)}) collective-permute-start(bf16[32,2304]{1,0:T(8,128)(2,1)} %get-tuple-element.25), channel_id=1, source_target_pairs={{0,3},{1,2},{2,1},{3,0},{4,7},{5,6},{6,5},{7,4},{8,11},{9,10},{10,... | collective-permute-start | bytes 442376 | tf_op jit(solution)/shard_map/ppermute | solution.py:599
  8.2 15.5 %collective-permute-start.3 = (bf16[32,2304]{1,0:T(8,128)(2,1)}, bf16[32,2304]{1,0:T(8,128)(2,1)}, u32[]{:S(2)}, u32[]{:S(2)}) collective-permute-start(bf16[32,2304]{1,0:T(8,128)(2,1)} %get-tuple-element.26), channel_id=1, source_target_pairs={{0,4},{1,5},{2,6},{3,7},{4,0},{5,1},{6,2},{7,3},{8,12},{9,13},{10,... | collective-permute-start | bytes 442376 | tf_op jit(solution)/shard_map/ppermute | solution.py:599
  11.2 21.8 %collective-permute-start.4 = (bf16[32,2304]{1,0:T(8,128)(2,1)}, bf16[32,2304]{1,0:T(8,128)(2,1)}, u32[]{:S(2)}, u32[]{:S(2)}) collective-permute-start(bf16[32,2304]{1,0:T(8,128)(2,1)} %get-tuple-element.27), channel_id=1, source_target_pairs={{0,5},{1,4},{2,7},{3,6},{4,1},{5,0},{6,3},{7,2},{8,13},{9,12},{10,... | collective-permute-start | bytes 442376 | tf_op jit(solution)/shard_map/ppermute | solution.py:599
  12.5 7.5 %copy-start = (bf16[32,2304]{1,0:T(8,128)(2,1)}, bf16[32,2304]{1,0:T(8,128)(2,1)S(1)}, u32[]{:S(2)}) copy-start(bf16[32,2304]{1,0:T(8,128)(2,1)S(1)} %collective-permute-done.refs_1_) | copy-start | bytes 442372
  12.5 20.5 %collective-permute-start.5 = (bf16[32,2304]{1,0:T(8,128)(2,1)}, bf16[32,2304]{1,0:T(8,128)(2,1)}, u32[]{:S(2)}, u32[]{:S(2)}) collective-permute-start(bf16[32,2304]{1,0:T(8,128)(2,1)} %get-tuple-element.28), channel_id=1, source_target_pairs={{0,6},{1,7},{2,4},{3,5},{4,2},{5,3},{6,0},{7,1},{8,14},{9,15},{10,... | collective-permute-start | bytes 442376 | tf_op jit(solution)/shard_map/ppermute | solution.py:599
  18.9 14.1 %collective-permute-start.6 = (bf16[32,2304]{1,0:T(8,128)(2,1)}, bf16[32,2304]{1,0:T(8,128)(2,1)}, u32[]{:S(2)}, u32[]{:S(2)}) collective-permute-start(bf16[32,2304]{1,0:T(8,128)(2,1)} %get-tuple-element.29), channel_id=1, source_target_pairs={{0,7},{1,6},{2,5},{3,4},{4,3},{5,2},{6,1},{7,0},{8,15},{9,14},{10,... | collective-permute-start | bytes 442376 | tf_op jit(solution)/shard_map/ppermute | solution.py:599
  22.0 24.5 %collective-permute-start.7 = (bf16[4,32,2304]{2,1,0:T(8,128)(2,1)}, bf16[4,32,2304]{2,1,0:T(8,128)(2,1)}, u32[]{:S(2)}, u32[]{:S(2)}) collective-permute-start(bf16[4,32,2304]{2,1,0:T(8,128)(2,1)} %join.2), channel_id=1, source_target_pairs={{0,16},{8,24},{16,0},{24,8},{1,17},{9,25},{17,1},{25,9},{2,18},{10... | collective-permute-start | bytes 1769480 | tf_op jit(solution)/shard_map/ppermute | solution.py:599
  35.0 20.2 %collective-permute-start.9 = (bf16[4,32,2304]{2,1,0:T(8,128)(2,1)}, bf16[4,32,2304]{2,1,0:T(8,128)(2,1)}, u32[]{:S(2)}, u32[]{:S(2)}) collective-permute-start(bf16[4,32,2304]{2,1,0:T(8,128)(2,1)} %join.3), channel_id=1, source_target_pairs={{0,16},{8,24},{16,0},{24,8},{1,17},{9,25},{17,1},{25,9},{2,18},{10... | collective-permute-start | bytes 1769480 | tf_op jit(solution)/shard_map/ppermute | solution.py:599
  46.5 26.9 %all-to-all-start = ((bf16[8,16,2304]{2,1,0:T(8,128)(2,1)}), bf16[8,16,2304]{2,1,0:T(8,128)(2,1)}, u32[]{:S(2)}, u32[]{:S(2)}) async-start(bf16[8,16,2304]{2,1,0:T(8,128)(2,1)} %get-tuple-element.31), calls=%async_computation | async-start | bytes 1179648 | tf_op jit(solution)/shard_map/all_to_all | solution.py:603
  55.2 2.9 %collective-permute-start.8 = (bf16[144,3328]{1,0:T(8,128)(2,1)}, bf16[144,3328]{1,0:T(8,128)(2,1)}, u32[]{:S(2)}, u32[]{:S(2)}) collective-permute-start(bf16[144,3328]{1,0:T(8,128)(2,1)} %get-tuple-element.33), channel_id=1, source_target_pairs={{0,8},{8,0},{16,24},{24,16},{1,9},{9,1},{17,25},{25,17},{2,10},{10... | collective-permute-start | bytes 2875400 | tf_op jit(solution)/shard_map/ppermute | solution.py:599
  55.2 3.7 %collective-permute-start.11 = (bf16[4,32,2304]{2,1,0:T(8,128)(2,1)}, bf16[4,32,2304]{2,1,0:T(8,128)(2,1)}, u32[]{:S(2)}, u32[]{:S(2)}) collective-permute-start(bf16[4,32,2304]{2,1,0:T(8,128)(2,1)} %collective-permute-done.9.refs_3_), channel_id=1, source_target_pairs={{0,8},{8,0},{16,24},{24,16},{1,9},{9,1},{17,25},{25,17},{2,10},{10... | collective-permute-start | bytes 1769480 | tf_op jit(solution)/shard_map/ppermute | solution.py:599
  55.7 4.0 %collective-permute-start.10 = (bf16[4,32,2304]{2,1,0:T(8,128)(2,1)}, bf16[4,32,2304]{2,1,0:T(8,128)(2,1)}, u32[]{:S(2)}, u32[]{:S(2)}) collective-permute-start(bf16[4,32,2304]{2,1,0:T(8,128)(2,1)} %collective-permute-done.7.refs_2_), channel_id=1, source_target_pairs={{0,8},{8,0},{16,24},{24,16},{1,9},{9,1},{17,25},{25,17},{2,10},{10... | collective-permute-start | bytes 1769480 | tf_op jit(solution)/shard_map/ppermute | solution.py:599

commit v17 on v16

--- a/solution.py
+++ b/solution.py
@@ -468,7 +468,6 @@
         x_mine, dy_mine, factors = [refs.pop(0) for _ in range(3)]
         gate, up, down, x_in, dy_in, known_in, gate_in, up_in, down_in = refs[:9]
         made_gate, made_up, made_down, gate_out, up_out, down_out = refs[9:]
-        now = pl.program_id(0)
         columns = tile_of(part_ref[0], share)
         x_pairs, dy_pairs, known_pairs = [], [], []
         for at in range(count):
@@ -500,63 +499,52 @@
         def fetch_dy(index):
             weight_copy(down_ref, down, down_in, index, 0, tile).start()
 
-        @pl.when(now == 0)
-        def _():
-            start(x_pairs, x_in)
-            fetch_x(0)
-            wait(x_pairs, x_in)
-            start(dy_pairs, dy_in)
-            fetch_dy(0)
-            arrange(x_held, x_all, x_mine)
-
-        weight_copy(gate_ref, gate, gate_in, now, 1, tile).wait()
-        pre_gate = dot(x_all[...], gate[now])
-        weight_copy(up_ref, up, up_in, now, 1, tile).wait()
-        pre_up = dot(x_all[...], up[now])
-
-        @pl.when(now == 0)
-        def _():
-            wait(dy_pairs, dy_in)
-            start(known_pairs, known_in)
-            arrange(dy_held, dy_all, dy_mine)
-
-        @pl.when(now < tiles - 1)
-        def _():
-            fetch_x(now + 1)
-            fetch_dy(now + 1)
-
-        weight_copy(down_ref, down, down_in, now, 0, tile).wait()
-        d_hidden = dot(dy_all[...], down[now], BY_WIDTH)
-        made, d_gate, d_up = hidden_grads(pre_gate, pre_up, d_hidden)
-
-        @pl.when(now == 0)
-        def _():
-            wait(known_pairs, known_in)
-
-        made = jnp.concatenate([factors[:, tile_of(now, tile)], made], 0)
-        d_gate = jnp.concatenate([factors[:, tile_of(tiles + now, tile)], d_gate], 0)
-        d_up = jnp.concatenate([factors[:, tile_of(2 * tiles + now, tile)], d_up], 0)
-        sums = dot(x_mine[...], jnp.concatenate([d_gate, d_up], 1), BY_ROWS)
-        made_gate[now] = sums[:, :tile]
-        made_up[now] = sums[:, tile:]
-        leave(made_gate, d_gate_ref, gate_out, now, 1).start()
-        leave(made_up, d_up_ref, up_out, now, 1).start()
-        made_down[now] = dot(made, dy_mine[...], BY_ROWS)
-        leave(made_down, d_down_ref, down_out, now, 0).start()
-
-        @pl.when(now == tiles - 1)
-        def _():
-            for at in range(tiles):
-                leave(made_gate, d_gate_ref, gate_out, at, 1).wait()
-                leave(made_up, d_up_ref, up_out, at, 1).wait()
-                leave(made_down, d_down_ref, down_out, at, 0).wait()
+        start(x_pairs, x_in)
+        fetch_x(0)
+        wait(x_pairs, x_in)
+        start(dy_pairs, dy_in)
+        fetch_dy(0)
+        arrange(x_held, x_all, x_mine)
+        for now in range(tiles):
+            here = slice(now * tile, (now + 1) * tile)
+            weight_copy(gate_ref, gate, gate_in, now, 1, tile).wait()
+            pre_gate = dot(x_all[...], gate[now])
+            weight_copy(up_ref, up, up_in, now, 1, tile).wait()
+            pre_up = dot(x_all[...], up[now])
+            if now == 0:
+                wait(dy_pairs, dy_in)
+                start(known_pairs, known_in)
+                arrange(dy_held, dy_all, dy_mine)
+            if now < tiles - 1:
+                fetch_x(now + 1)
+                fetch_dy(now + 1)
+            weight_copy(down_ref, down, down_in, now, 0, tile).wait()
+            d_hidden = dot(dy_all[...], down[now], BY_WIDTH)
+            made, d_gate, d_up = hidden_grads(pre_gate, pre_up, d_hidden)
+            if now == 0:
+                wait(known_pairs, known_in)
+            made = jnp.concatenate([factors[:, here], made], 0)
+            d_gate = jnp.concatenate([factors[:, hid + here.start : hid + here.stop], d_gate], 0)
+            d_up = jnp.concatenate(
+                [factors[:, 2 * hid + here.start : 2 * hid + here.stop], d_up], 0
+            )
+            sums = dot(x_mine[...], jnp.concatenate([d_gate, d_up], 1), BY_ROWS)
+            made_gate[now] = sums[:, :tile]
+            made_up[now] = sums[:, tile:]
+            leave(made_gate, d_gate_ref, gate_out, now, 1).start()
+            leave(made_up, d_up_ref, up_out, now, 1).start()
+            made_down[now] = dot(made, dy_mine[...], BY_ROWS)
+            leave(made_down, d_down_ref, down_out, now, 0).start()
+        for at in range(tiles):
+            leave(made_gate, d_gate_ref, gate_out, at, 1).wait()
+            leave(made_up, d_up_ref, up_out, at, 1).wait()
+            leave(made_down, d_down_ref, down_out, at, 0).wait()
 
     held = pltpu.VMEM((count, blocks, ROWS, width + step), jnp.bfloat16)
     arranged = pltpu.VMEM((count * slots, width), jnp.bfloat16)
     mine = pltpu.VMEM((total, share), jnp.bfloat16)
     return pl.pallas_call(
         kernel,
-        grid=(tiles,),
         out_shape=[
             jax.ShapeDtypeStruct((share, hid), jnp.float32),
             jax.ShapeDtypeStruct((share, hid), jnp.float32),

time: 76.1 us -> 75.6 us (level)
  no operation moved by 1% of the time
where the time goes in v17:
time: 75.6 us; the launch traced here: 75.3 us
  Pallas kernels  32.2 us (43%)
  starting transfers between devices  26 us (34%)
  waiting for transfers between devices  16.2 us (21%)
  between operations  0.88 us (1%)
    ppermute x12, starting transfers between devices, swap(): lax.ppermute(value, axis, [(at, at ^ distance) for at in range(size)])  17.3 us
    ppermute x12, waiting for transfers between devices, swap(): lax.ppermute(value, axis, [(at, at ^ distance) for at in range(size)])  16.2 us
    pallas_call x1, Pallas kernels, weight_grads(): pl.pallas_call(kernel, out_shape=[jax.ShapeDtypeStruct((share, hid), jnp....  13 us
    pallas_call x1, Pallas kernels, back(): pl.pallas_call(kernel, out_shape=[jax.ShapeDtypeStruct(shape, jnp.bfloat1...  9.93 us
    all_to_all x1, starting transfers between devices, exchange(): lax.all_to_all(blocks, 'expert', split_axis=0, concat_axis=0, tiled=True)  8.69 us
    pallas_call x2, Pallas kernels, join(): pl.pallas_call(kernel, out_shape=jax.ShapeDtypeStruct((count,) + received...  3.94 us
    pallas_call x1, Pallas kernels, pack(): pl.pallas_call(kernel, out_shape=[jax.ShapeDtypeStruct((2 * ROWS, width +...  2.99 us
    pallas_call x1, Pallas kernels, merge(): pl.pallas_call(kernel, out_shape=jax.ShapeDtypeStruct((tokens, width), jn...  2.36 us
  transfers between devices with their start and end apart: 13, of which 6 were waited for; matrix products, arithmetic and copies ran while one was open for 0% of the time, Pallas kernels for 36%

profile of v17, /device:TPU:0, one launch (start us, length us, event | category | flops | bytes accessed | tf_op | source)
XLA Modules:
  0.0 75.3 jit_solution(11834720865143628258)
XLA Ops:
  0.6 3.0 %pack.1 = (bf16[32,2304]{1,0:T(8,128)(2,1)}, bf16[32,2304]{1,0:T(8,128)(2,1)}, bf16[32,2304]{1,0:T(8,128)(2,1)}, bf16[32,2304]{1,0:T(8,128)(2,1)}, bf16[32,2304]...) custom-call(s32[1]{0:T(128)} %bitcast.1.me_ref, ...), custom_call_target="tpu_custom_call" | custom-call | flops 268435456 | bytes 2097152 | tf_op jit(solution)/shard_map/pack/pallas_call | solution.py:195
  3.6 3.0 %collective-permute-start = (bf16[32,2304]{1,0:T(8,128)(2,1)}, bf16[32,2304]{1,0:T(8,128)(2,1)S(1)}, u32[]{:S(2)}, u32[]{:S(2)}) collective-permute-start(bf16[32,2304]{1,0:T(8,128)(2,1)} %get-tuple-element.23), channel_id=1, source_target_pairs={{0,1},{1,0},{2,3},{3,2},{4,5},{5,4},{6,7},{7,6},{8,9},{9,8},{10,11... | collective-permute-start | bytes 442376 | tf_op jit(solution)/shard_map/ppermute | solution.py:587
  6.6 1.6 %collective-permute-start.1 = (bf16[32,2304]{1,0:T(8,128)(2,1)}, bf16[32,2304]{1,0:T(8,128)(2,1)}, u32[]{:S(2)}, u32[]{:S(2)}) collective-permute-start(bf16[32,2304]{1,0:T(8,128)(2,1)} %get-tuple-element.24), channel_id=1, source_target_pairs={{0,2},{1,3},{2,0},{3,1},{4,6},{5,7},{6,4},{7,5},{8,10},{9,11},{10,... | collective-permute-start | bytes 442376 | tf_op jit(solution)/shard_map/ppermute | solution.py:587
  8.2 0.0 collective-permute-start.2
  8.2 3.0 %collective-permute-start.3 = (bf16[32,2304]{1,0:T(8,128)(2,1)}, bf16[32,2304]{1,0:T(8,128)(2,1)}, u32[]{:S(2)}, u32[]{:S(2)}) collective-permute-start(bf16[32,2304]{1,0:T(8,128)(2,1)} %get-tuple-element.26), channel_id=1, source_target_pairs={{0,4},{1,5},{2,6},{3,7},{4,0},{5,1},{6,2},{7,3},{8,12},{9,13},{10,... | collective-permute-start | bytes 442376 | tf_op jit(solution)/shard_map/ppermute | solution.py:587
  11.2 1.3 %collective-permute-start.4 = (bf16[32,2304]{1,0:T(8,128)(2,1)}, bf16[32,2304]{1,0:T(8,128)(2,1)}, u32[]{:S(2)}, u32[]{:S(2)}) collective-permute-start(bf16[32,2304]{1,0:T(8,128)(2,1)} %get-tuple-element.27), channel_id=1, source_target_pairs={{0,5},{1,4},{2,7},{3,6},{4,1},{5,0},{6,3},{7,2},{8,13},{9,12},{10,... | collective-permute-start | bytes 442376 | tf_op jit(solution)/shard_map/ppermute | solution.py:587
  12.5 3.6 %collective-permute-start.5 = (bf16[32,2304]{1,0:T(8,128)(2,1)}, bf16[32,2304]{1,0:T(8,128)(2,1)}, u32[]{:S(2)}, u32[]{:S(2)}) collective-permute-start(bf16[32,2304]{1,0:T(8,128)(2,1)} %get-tuple-element.28), channel_id=1, source_target_pairs={{0,6},{1,7},{2,4},{3,5},{4,2},{5,3},{6,0},{7,1},{8,14},{9,15},{10,... | collective-permute-start | bytes 442376 | tf_op jit(solution)/shard_map/ppermute | solution.py:587
  16.1 2.8 %collective-permute-done.1.refs_2_ = bf16[32,2304]{1,0:T(8,128)(2,1)} collective-permute-done((bf16[32,2304]{1,0:T(8,128)(2,1)}, bf16[32,2304]{1,0:T(8,128)(2,1)}, u32[]{:S(2)}, u32[]{:S(2)}) %collective-permute-start.1) | collective-permute-done | bytes 147488 | tf_op jit(solution)/shard_map/ppermute | solution.py:587
  18.9 0.9 %collective-permute-start.6 = (bf16[32,2304]{1,0:T(8,128)(2,1)}, bf16[32,2304]{1,0:T(8,128)(2,1)}, u32[]{:S(2)}, u32[]{:S(2)}) collective-permute-start(bf16[32,2304]{1,0:T(8,128)(2,1)} %get-tuple-element.29), channel_id=1, source_target_pairs={{0,7},{1,6},{2,5},{3,4},{4,3},{5,2},{6,1},{7,0},{8,15},{9,14},{10,... | collective-permute-start | bytes 442376 | tf_op jit(solution)/shard_map/ppermute | solution.py:587
  19.9 0.1 collective-permute-done.2.refs_3_
  20.0 2.0 %join.2 = bf16[4,32,2304]{2,1,0:T(8,128)(2,1)} custom-call(bf16[32,2304]{1,0:T(8,128)(2,1)} %get-tuple-element.22.refs_0_, bf16[32,2304]{1,0:T(8,128)(2,1)} %copy-done, bf16[32,2304]{1,0:T(8,128)(2,1)} %collective-permute-done.1.refs_2_, bf16[32,2304]{1,0:T(8,128)(2,1)} %collective-permute-done.2.refs_3_), custom_call_target="tpu_custom_call" | custom-call | bytes 1179648 | tf_op jit(solution)/shard_map/join/pallas_call | solution.py:216
  22.0 1.8 %collective-permute-start.7 = (bf16[4,32,2304]{2,1,0:T(8,128)(2,1)}, bf16[4,32,2304]{2,1,0:T(8,128)(2,1)}, u32[]{:S(2)}, u32[]{:S(2)}) collective-permute-start(bf16[4,32,2304]{2,1,0:T(8,128)(2,1)} %join.2), channel_id=1, source_target_pairs={{0,16},{8,24},{16,0},{24,8},{1,17},{9,25},{17,1},{25,9},{2,18},{10... | collective-permute-start | bytes 1769480 | tf_op jit(solution)/shard_map/ppermute | solution.py:587
  23.7 9.3 %collective-permute-done.4.refs_5_.refs_1_ = bf16[32,2304]{1,0:T(8,128)(2,1)} collective-permute-done((bf16[32,2304]{1,0:T(8,128)(2,1)}, bf16[32,2304]{1,0:T(8,128)(2,1)}, u32[]{:S(2)}, u32[]{:S(2)}) %collective-permute-start.4) | collective-permute-done | bytes 147488 | tf_op jit(solution)/shard_map/ppermute | solution.py:587
  33.0 2.0 %join.3 = bf16[4,32,2304]{2,1,0:T(8,128)(2,1)} custom-call(bf16[32,2304]{1,0:T(8,128)(2,1)} %collective-permute-done.3.refs_4_.refs_0_, bf16[32,2304]{1,0:T(8,128)(2,1)} %collective-permute-done.4.refs_5_.refs_1_, bf16[32,2304]{1,0:T(8,128)(2,1)} %collective-permute-done.5.refs_6_.refs_2_, bf16[32,2304]{1,0:T(8,128)(2,1)} %collective-permute-done.6.refs_7_.refs_3_), custom_call_target="tpu_custom_call" | custom-call | bytes 1179648 | tf_op jit(solution)/shard_map/join/pallas_call | solution.py:216
  35.0 1.6 %collective-permute-start.9 = (bf16[4,32,2304]{2,1,0:T(8,128)(2,1)}, bf16[4,32,2304]{2,1,0:T(8,128)(2,1)}, u32[]{:S(2)}, u32[]{:S(2)}) collective-permute-start(bf16[4,32,2304]{2,1,0:T(8,128)(2,1)} %join.3), channel_id=1, source_target_pairs={{0,16},{8,24},{16,0},{24,8},{1,17},{9,25},{17,1},{25,9},{2,18},{10... | collective-permute-start | bytes 1769480 | tf_op jit(solution)/shard_map/ppermute | solution.py:587
  36.6 9.9 %back.1 = (bf16[8,16,2304]{2,1,0:T(8,128)(2,1)}, bf16[144,3328]{1,0:T(8,128)(2,1)}, bf16[144,3328]{1,0:T(8,128)(2,1)}) custom-call(s32[1]{0:T(128)} %bitcast.1.me_ref, s32[1]{0:T(128)} %bitcast.2.part_ref, bf16[32,2304]{1,0:T(8,128)(2,1)} %get-tuple-element.22.refs_0_, bf16[32,2304]{1,0:T(8,128)(2,1)} %copy-done, ...), custom_call_target="tpu_custom_call" | custom-call | flops 11324620800 | bytes 1179648 | tf_op jit(solution)/shard_map/back/pallas_call | solution.py:417
  46.5 8.7 %all-to-all-start = ((bf16[8,16,2304]{2,1,0:T(8,128)(2,1)}), bf16[8,16,2304]{2,1,0:T(8,128)(2,1)}, u32[]{:S(2)}, u32[]{:S(2)}) async-start(bf16[8,16,2304]{2,1,0:T(8,128)(2,1)} %get-tuple-element.31), calls=%async_computation | async-start | bytes 1179648 | tf_op jit(solution)/shard_map/all_to_all | solution.py:591
  55.2 0.5 collective-permute-start.11
  55.7 0.1 collective-permute-start.10
  55.8 2.3 %collective-permute-done.8.refs_1_ = bf16[144,3328]{1,0:T(8,128)(2,1)} collective-permute-done((bf16[144,3328]{1,0:T(8,128)(2,1)}, bf16[144,3328]{1,0:T(8,128)(2,1)}, u32[]{:S(2)}, u32[]{:S(2)}) %collective-permute-start.8) | collective-permute-done | bytes 958496 | tf_op jit(solution)/shard_map/ppermute | solution.py:587
  58.1 0.8 %collective-permute-done.11.refs_5_ = bf16[4,32,2304]{2,1,0:T(8,128)(2,1)} collective-permute-done((bf16[4,32,2304]{2,1,0:T(8,128)(2,1)}, bf16[4,32,2304]{2,1,0:T(8,128)(2,1)}, u32[]{:S(2)}, u32[]{:S(2)}) %collective-permute-start.11) | collective-permute-done | bytes 589856 | tf_op jit(solution)/shard_map/ppermute | solution.py:587
  58.9 0.8 %collective-permute-done.10.refs_4_ = bf16[4,32,2304]{2,1,0:T(8,128)(2,1)} collective-permute-done((bf16[4,32,2304]{2,1,0:T(8,128)(2,1)}, bf16[4,32,2304]{2,1,0:T(8,128)(2,1)}, u32[]{:S(2)}, u32[]{:S(2)}) %collective-permute-start.10) | collective-permute-done | bytes 589856 | tf_op jit(solution)/shard_map/ppermute | solution.py:587
  59.8 13.0 %weight_grads.1 = (f32[512,768]{1,0:T(8,128)}, f32[512,768]{1,0:T(8,128)}, f32[768,512]{1,0:T(8,128)}) custom-call(s32[1]{0:T(128)} %bitcast.2.part_ref, bf16[144,3328]{1,0:T(8,128)(2,1)} %get-tuple-element.32.refs_0_, bf16[144,3328]{1,0:T(8,128)(2,1)} %collective-permute-done.8.refs_1_, bf16[4,32,2304]{2,1,0:T(8,128)(2,1)} %collective-permute-done.7.refs_2_, ...), custom_call_target="tpu_custom_call" | custom-call | bytes 1179648 | tf_op jit(solution)/shard_map/weight_grads/pallas_call | solution.py:546
  72.7 2.4 %merge.1 = bf16[128,2048]{1,0:T(8,128)(2,1)} custom-call(s32[1,128]{1,0:T(1,128)} %bitcast.5, bf16[8,16,2304]{2,1,0:T(8,128)(2,1)} %all-to-all-done.back_ref), custom_call_target="tpu_custom_call" | custom-call | flops 134217728 | bytes 1048576 | tf_op jit(solution)/shard_map/merge/pallas_call | solution.py:251
  (10 shorter events, 0.0 us)
Async XLA Ops:
  3.6 8.9 %collective-permute-start = (bf16[32,2304]{1,0:T(8,128)(2,1)}, bf16[32,2304]{1,0:T(8,128)(2,1)S(1)}, u32[]{:S(2)}, u32[]{:S(2)}) collective-permute-start(bf16[32,2304]{1,0:T(8,128)(2,1)} %get-tuple-element.23), channel_id=1, source_target_pairs={{0,1},{1,0},{2,3},{3,2},{4,5},{5,4},{6,7},{7,6},{8,9},{9,8},{10,11... | collective-permute-start | bytes 442376 | tf_op jit(solution)/shard_map/ppermute | solution.py:587
  6.6 12.3 %collective-permute-start.1 = (bf16[32,2304]{1,0:T(8,128)(2,1)}, bf16[32,2304]{1,0:T(8,128)(2,1)}, u32[]{:S(2)}, u32[]{:S(2)}) collective-permute-start(bf16[32,2304]{1,0:T(8,128)(2,1)} %get-tuple-element.24), channel_id=1, source_target_pairs={{0,2},{1,3},{2,0},{3,1},{4,6},{5,7},{6,4},{7,5},{8,10},{9,11},{10,... | collective-permute-start | bytes 442376 | tf_op jit(solution)/shard_map/ppermute | solution.py:587
  8.2 11.8 %collective-permute-start.2 = (bf16[32,2304]{1,0:T(8,128)(2,1)}, bf16[32,2304]{1,0:T(8,128)(2,1)}, u32[]{:S(2)}, u32[]{:S(2)}) collective-permute-start(bf16[32,2304]{1,0:T(8,128)(2,1)} %get-tuple-element.25), channel_id=1, source_target_pairs={{0,3},{1,2},{2,1},{3,0},{4,7},{5,6},{6,5},{7,4},{8,11},{9,10},{10,... | collective-permute-start | bytes 442376 | tf_op jit(solution)/shard_map/ppermute | solution.py:587
  8.2 15.5 %collective-permute-start.3 = (bf16[32,2304]{1,0:T(8,128)(2,1)}, bf16[32,2304]{1,0:T(8,128)(2,1)}, u32[]{:S(2)}, u32[]{:S(2)}) collective-permute-start(bf16[32,2304]{1,0:T(8,128)(2,1)} %get-tuple-element.26), channel_id=1, source_target_pairs={{0,4},{1,5},{2,6},{3,7},{4,0},{5,1},{6,2},{7,3},{8,12},{9,13},{10,... | collective-permute-start | bytes 442376 | tf_op jit(solution)/shard_map/ppermute | solution.py:587
  11.2 21.8 %collective-permute-start.4 = (bf16[32,2304]{1,0:T(8,128)(2,1)}, bf16[32,2304]{1,0:T(8,128)(2,1)}, u32[]{:S(2)}, u32[]{:S(2)}) collective-permute-start(bf16[32,2304]{1,0:T(8,128)(2,1)} %get-tuple-element.27), channel_id=1, source_target_pairs={{0,5},{1,4},{2,7},{3,6},{4,1},{5,0},{6,3},{7,2},{8,13},{9,12},{10,... | collective-permute-start | bytes 442376 | tf_op jit(solution)/shard_map/ppermute | solution.py:587
  12.5 7.5 %copy-start = (bf16[32,2304]{1,0:T(8,128)(2,1)}, bf16[32,2304]{1,0:T(8,128)(2,1)S(1)}, u32[]{:S(2)}) copy-start(bf16[32,2304]{1,0:T(8,128)(2,1)S(1)} %collective-permute-done.refs_1_) | copy-start | bytes 442372
  12.5 20.5 %collective-permute-start.5 = (bf16[32,2304]{1,0:T(8,128)(2,1)}, bf16[32,2304]{1,0:T(8,128)(2,1)}, u32[]{:S(2)}, u32[]{:S(2)}) collective-permute-start(bf16[32,2304]{1,0:T(8,128)(2,1)} %get-tuple-element.28), channel_id=1, source_target_pairs={{0,6},{1,7},{2,4},{3,5},{4,2},{5,3},{6,0},{7,1},{8,14},{9,15},{10,... | collective-permute-start | bytes 442376 | tf_op jit(solution)/shard_map/ppermute | solution.py:587
  18.9 14.1 %collective-permute-start.6 = (bf16[32,2304]{1,0:T(8,128)(2,1)}, bf16[32,2304]{1,0:T(8,128)(2,1)}, u32[]{:S(2)}, u32[]{:S(2)}) collective-permute-start(bf16[32,2304]{1,0:T(8,128)(2,1)} %get-tuple-element.29), channel_id=1, source_target_pairs={{0,7},{1,6},{2,5},{3,4},{4,3},{5,2},{6,1},{7,0},{8,15},{9,14},{10,... | collective-permute-start | bytes 442376 | tf_op jit(solution)/shard_map/ppermute | solution.py:587
  22.0 24.5 %collective-permute-start.7 = (bf16[4,32,2304]{2,1,0:T(8,128)(2,1)}, bf16[4,32,2304]{2,1,0:T(8,128)(2,1)}, u32[]{:S(2)}, u32[]{:S(2)}) collective-permute-start(bf16[4,32,2304]{2,1,0:T(8,128)(2,1)} %join.2), channel_id=1, source_target_pairs={{0,16},{8,24},{16,0},{24,8},{1,17},{9,25},{17,1},{25,9},{2,18},{10... | collective-permute-start | bytes 1769480 | tf_op jit(solution)/shard_map/ppermute | solution.py:587
  35.0 20.2 %collective-permute-start.9 = (bf16[4,32,2304]{2,1,0:T(8,128)(2,1)}, bf16[4,32,2304]{2,1,0:T(8,128)(2,1)}, u32[]{:S(2)}, u32[]{:S(2)}) collective-permute-start(bf16[4,32,2304]{2,1,0:T(8,128)(2,1)} %join.3), channel_id=1, source_target_pairs={{0,16},{8,24},{16,0},{24,8},{1,17},{9,25},{17,1},{25,9},{2,18},{10... | collective-permute-start | bytes 1769480 | tf_op jit(solution)/shard_map/ppermute | solution.py:587
  46.5 26.2 %all-to-all-start = ((bf16[8,16,2304]{2,1,0:T(8,128)(2,1)}), bf16[8,16,2304]{2,1,0:T(8,128)(2,1)}, u32[]{:S(2)}, u32[]{:S(2)}) async-start(bf16[8,16,2304]{2,1,0:T(8,128)(2,1)} %get-tuple-element.31), calls=%async_computation | async-start | bytes 1179648 | tf_op jit(solution)/shard_map/all_to_all | solution.py:591
  55.2 2.9 %collective-permute-start.8 = (bf16[144,3328]{1,0:T(8,128)(2,1)}, bf16[144,3328]{1,0:T(8,128)(2,1)}, u32[]{:S(2)}, u32[]{:S(2)}) collective-permute-start(bf16[144,3328]{1,0:T(8,128)(2,1)} %get-tuple-element.33), channel_id=1, source_target_pairs={{0,8},{8,0},{16,24},{24,16},{1,9},{9,1},{17,25},{25,17},{2,10},{10... | collective-permute-start | bytes 2875400 | tf_op jit(solution)/shard_map/ppermute | solution.py:587
  55.2 3.7 %collective-permute-start.11 = (bf16[4,32,2304]{2,1,0:T(8,128)(2,1)}, bf16[4,32,2304]{2,1,0:T(8,128)(2,1)}, u32[]{:S(2)}, u32[]{:S(2)}) collective-permute-start(bf16[4,32,2304]{2,1,0:T(8,128)(2,1)} %collective-permute-done.9.refs_3_), channel_id=1, source_target_pairs={{0,8},{8,0},{16,24},{24,16},{1,9},{9,1},{17,25},{25,17},{2,10},{10... | collective-permute-start | bytes 1769480 | tf_op jit(solution)/shard_map/ppermute | solution.py:587
  55.7 4.0 %collective-permute-start.10 = (bf16[4,32,2304]{2,1,0:T(8,128)(2,1)}, bf16[4,32,2304]{2,1,0:T(8,128)(2,1)}, u32[]{:S(2)}, u32[]{:S(2)}) collective-permute-start(bf16[4,32,2304]{2,1,0:T(8,128)(2,1)} %collective-permute-done.7.refs_2_), channel_id=1, source_target_pairs={{0,8},{8,0},{16,24},{24,16},{1,9},{9,1},{17,25},{25,17},{2,10},{10... | collective-permute-start | bytes 1769480 | tf_op jit(solution)/shard_map/ppermute | solution.py:587

commit v18 on v17

--- a/solution.py
+++ b/solution.py
@@ -163,24 +163,26 @@
     count, width = tokens.shape
     pieces, step = cut(width)
     sources = (routes, gates, tokens, cotangent)
+    block_shape = (2 * ROWS, width + step)
 
     def kernel(me_ref, *refs):
-        outs, held, arrived = refs[4 : 4 + blocks], refs[4 + blocks : 8 + blocks], refs[-1]
+        outs, held = refs[4 : 4 + blocks], refs[4 + blocks : 8 + blocks]
+        staged, arrived, gone = refs[8 + blocks :]
         pairs = list(zip(refs[:4], held))
         start(pairs, arrived)
         wait(pairs[:2], arrived)
         main, spill, piece = slot_masks(held[0][...], blocks, width, me_ref[0])
         mains = ones(main)
-        picks = [ones(spill & (piece == at)) for at in range(pieces)]
+        picks = jnp.concatenate([ones(spill & (piece == at)) for at in range(pieces)], 1)
         main_scale = jnp.sum(jnp.where(main, held[1][...], 0.0), axis=1, keepdims=True)
         spill_scale = jnp.sum(jnp.where(spill, held[1][...], 0.0), axis=1, keepdims=True)
+        leaving = []
         for half in range(2):
             wait(pairs[: 3 + half], arrived, 2 + half)
             values = held[2 + half]
             rows = dot(mains, values[...])
-            extra = jnp.zeros((blocks * ROWS, step), jnp.float32)
-            for at in range(pieces):
-                extra += dot(picks[at], values[:, at * step : (at + 1) * step])
+            cuts = [values[:, at * step : (at + 1) * step] for at in range(pieces)]
+            extra = dot(picks, jnp.concatenate(cuts, 0))
             if half > 0:
                 rows, extra = rows * main_scale, extra * spill_scale
             rows = rows.astype(jnp.bfloat16)
@@ -188,17 +190,24 @@
             here = slice(half * ROWS, (half + 1) * ROWS)
             for block in range(blocks):
                 part = slice(block * ROWS, (block + 1) * ROWS)
-                outs[block][here, :width] = rows[part]
-                outs[block][here, width:] = extra[part]
-
-    inside = pl.BlockSpec(memory_space=pltpu.VMEM)
+                staged[block, here, :width] = rows[part]
+                staged[block, here, width:] = extra[part]
+            sent = [(staged.at[at, here], outs[at].at[here, :]) for at in range(blocks)]
+            leaving += sent
+            start(leaving, gone, half * blocks)
+        wait(leaving, gone)
+
     return pl.pallas_call(
         kernel,
-        out_shape=[jax.ShapeDtypeStruct((2 * ROWS, width + step), jnp.bfloat16)] * blocks,
+        out_shape=[jax.ShapeDtypeStruct(block_shape, jnp.bfloat16)] * blocks,
         in_specs=[pl.BlockSpec(memory_space=pltpu.SMEM)] + anywhere(4),
-        out_specs=[inside] * blocks,
+        out_specs=anywhere(blocks),
         scratch_shapes=[pltpu.VMEM(source.shape, source.dtype) for source in sources]
-        + [pltpu.SemaphoreType.DMA((4,))],
+        + [
+            pltpu.VMEM((blocks,) + block_shape, jnp.bfloat16),
+            pltpu.SemaphoreType.DMA((4,)),
+            pltpu.SemaphoreType.DMA((2 * blocks,)),
+        ],
         compiler_params=params(),
         cost_estimate=cost(8 * blocks * ROWS * count * width, 8 * count * width),
         name="pack",
@@ -207,18 +216,28 @@
 
 def join(received):
     count = len(received)
+    shape = (count,) + received[0].shape
 
     def kernel(*refs):
-        pairs = [(refs[at], refs[count].at[at]) for at in range(count)]
-        start(pairs, refs[-1])
-        wait(pairs, refs[-1])
+        out, held, arrived, gone = refs[count:]
+        pairs = [(refs[at], held.at[at]) for at in range(count)]
+        leaving = [(held.at[at], out.at[at]) for at in range(count)]
+        start(pairs, arrived)
+        for at in range(count):
+            wait(pairs[: at + 1], arrived, at)
+            start(leaving[: at + 1], gone, at)
+        wait(leaving, gone)
 
     return pl.pallas_call(
         kernel,
-        out_shape=jax.ShapeDtypeStruct((count,) + received[0].shape, jnp.bfloat16),
+        out_shape=jax.ShapeDtypeStruct(shape, jnp.bfloat16),
         in_specs=anywhere(count),
-        out_specs=pl.BlockSpec(memory_space=pltpu.VMEM),
-        scratch_shapes=[pltpu.SemaphoreType.DMA((count,))],
+        out_specs=pl.BlockSpec(memory_space=pl.ANY),
+        scratch_shapes=[
+            pltpu.VMEM(shape, jnp.bfloat16),
+            pltpu.SemaphoreType.DMA((count,)),
+            pltpu.SemaphoreType.DMA((count,)),
+        ],
         compiler_params=params(),
         cost_estimate=cost(0, 4 * received[0].size * count),
         name="join",
@@ -230,33 +249,43 @@
     tokens = routes.shape[1]
     width = width_of(returned)
     pieces, step = cut(width)
-
-    def kernel(routes_ref, back_ref, out, named, held, arrived):
-        pairs = [(routes_ref, named), (back_ref, held)]
+    chunk = 2 * step
+
+    def kernel(routes_ref, back_ref, out, named, held, made, arrived, gone):
+        spans = [slice(width, width + step)]
+        spans += [slice(at, at + chunk) for at in range(0, width, chunk)]
+        pairs = [(routes_ref, named)]
+        pairs += [(back_ref.at[:, :, span], held.at[:, :, span]) for span in spans]
+        leaving = [(made.at[:, span], out.at[:, span]) for span in spans[1:]]
         start(pairs, arrived)
         wait(pairs[:1], arrived)
         main, spill, piece = slot_masks(named[...], blocks, width)
         mains = ones(main)
-        picks = [ones(spill & (piece == at)) for at in range(pieces)]
-        wait(pairs, arrived, 1)
-        rows = jnp.concatenate([held[at, :, :width] for at in range(blocks)], 0)
-        extra = jnp.concatenate([held[at, :, width:] for at in range(blocks)], 0)
-        picked = dot(mains, rows, BY_ROWS)
-        for at in range(pieces):
-            columns = slice(at * step, (at + 1) * step)
-            out[:, columns] = (picked[:, columns] + dot(picks[at], extra, BY_ROWS)).astype(
-                jnp.bfloat16
-            )
-
+        picks = jnp.concatenate([ones(spill & (piece == at)) for at in range(pieces)], 1)
+        wait(pairs[:2], arrived, 1)
+        tails = jnp.concatenate([held[at, :, width:] for at in range(blocks)], 0)
+        extra = dot(picks, tails, BY_ROWS)
+        for at, span in enumerate(spans[1:]):
+            wait(pairs[: at + 3], arrived, at + 2)
+            rows = jnp.concatenate([held[block, :, span] for block in range(blocks)], 0)
+            here = [extra[(2 * at + side) * tokens :][:tokens] for side in range(2)]
+            picked = dot(mains, rows, BY_ROWS) + jnp.concatenate(here, 1)
+            made[:, span] = picked.astype(jnp.bfloat16)
+            start(leaving[: at + 1], gone, at)
+        wait(leaving, gone)
+
+    chunks = width // chunk
     return pl.pallas_call(
         kernel,
         out_shape=jax.ShapeDtypeStruct((tokens, width), jnp.bfloat16),
         in_specs=anywhere(2),
-        out_specs=pl.BlockSpec(memory_space=pltpu.VMEM),
+        out_specs=pl.BlockSpec(memory_space=pl.ANY),
         scratch_shapes=[
             pltpu.VMEM(routes.shape, routes.dtype),
             pltpu.VMEM(returned.shape, returned.dtype),
-            pltpu.SemaphoreType.DMA((2,)),
+            pltpu.VMEM((tokens, width), jnp.bfloat16),
+            pltpu.SemaphoreType.DMA((chunks + 2,)),
+            pltpu.SemaphoreType.DMA((chunks,)),
         ],
         compiler_params=params(),
         cost_estimate=cost(4 * blocks * ROWS * tokens * width, 4 * tokens * width),

time: 75.6 us -> 75.8 us (level)
  transfers between devices with their start and end apart: 13 -> 13, of which waited for: 6 -> 6; matrix products, arithmetic and copies ran while one was open for 0% -> 0% of each run, Pallas kernels for 36% -> 35%
where the time goes in v18:
time: 75.8 us; the launch traced here: 75.5 us
  Pallas kernels  32.3 us (43%)
  starting transfers between devices  26 us (34%)
  waiting for transfers between devices  16.3 us (22%)
  between operations  0.88 us (1%)
    ppermute x12, starting transfers between devices, swap(): lax.ppermute(value, axis, [(at, at ^ distance) for at in range(size)])  17.3 us
    ppermute x12, waiting for transfers between devices, swap(): lax.ppermute(value, axis, [(at, at ^ distance) for at in range(size)])  16.3 us
    pallas_call x1, Pallas kernels, weight_grads(): pl.pallas_call(kernel, out_shape=[jax.ShapeDtypeStruct((share, hid), jnp....  13 us
    pallas_call x1, Pallas kernels, back(): pl.pallas_call(kernel, out_shape=[jax.ShapeDtypeStruct(shape, jnp.bfloat1...  9.93 us
    all_to_all x1, starting transfers between devices, exchange(): lax.all_to_all(blocks, 'expert', split_axis=0, concat_axis=0, tiled=True)  8.68 us
    pallas_call x2, Pallas kernels, join(): pl.pallas_call(kernel, out_shape=jax.ShapeDtypeStruct(shape, jnp.bfloat16...  3.7 us
    pallas_call x1, Pallas kernels, merge(): pl.pallas_call(kernel, out_shape=jax.ShapeDtypeStruct((tokens, width), jn...  2.88 us
    pallas_call x1, Pallas kernels, pack(): pl.pallas_call(kernel, out_shape=[jax.ShapeDtypeStruct(block_shape, jnp.b...  2.82 us
  transfers between devices with their start and end apart: 13, of which 6 were waited for; matrix products, arithmetic and copies ran while one was open for 0% of the time, Pallas kernels for 35%

profile of v18, /device:TPU:0, one launch (start us, length us, event | category | flops | bytes accessed | tf_op | source)
XLA Modules:
  0.0 75.5 jit_solution(13161848142747195035)
XLA Ops:
  0.6 2.8 %pack.1 = (bf16[32,2304]{1,0:T(8,128)(2,1)}, bf16[32,2304]{1,0:T(8,128)(2,1)}, bf16[32,2304]{1,0:T(8,128)(2,1)}, bf16[32,2304]{1,0:T(8,128)(2,1)}, bf16[32,2304]...) custom-call(s32[1]{0:T(128)} %bitcast.1.me_ref, ...), custom_call_target="tpu_custom_call" | custom-call | flops 268435456 | bytes 2097152 | tf_op jit(solution)/shard_map/pack/pallas_call | solution.py:200
  3.5 3.0 %collective-permute-start = (bf16[32,2304]{1,0:T(8,128)(2,1)}, bf16[32,2304]{1,0:T(8,128)(2,1)S(1)}, u32[]{:S(2)}, u32[]{:S(2)}) collective-permute-start(bf16[32,2304]{1,0:T(8,128)(2,1)} %get-tuple-element.23), channel_id=1, source_target_pairs={{0,1},{1,0},{2,3},{3,2},{4,5},{5,4},{6,7},{7,6},{8,9},{9,8},{10,11... | collective-permute-start | bytes 442376 | tf_op jit(solution)/shard_map/ppermute | solution.py:616
  6.5 1.6 %collective-permute-start.1 = (bf16[32,2304]{1,0:T(8,128)(2,1)}, bf16[32,2304]{1,0:T(8,128)(2,1)}, u32[]{:S(2)}, u32[]{:S(2)}) collective-permute-start(bf16[32,2304]{1,0:T(8,128)(2,1)} %get-tuple-element.24), channel_id=1, source_target_pairs={{0,2},{1,3},{2,0},{3,1},{4,6},{5,7},{6,4},{7,5},{8,10},{9,11},{10,... | collective-permute-start | bytes 442376 | tf_op jit(solution)/shard_map/ppermute | solution.py:616
  8.0 0.0 collective-permute-start.2
  8.1 3.0 %collective-permute-start.3 = (bf16[32,2304]{1,0:T(8,128)(2,1)}, bf16[32,2304]{1,0:T(8,128)(2,1)}, u32[]{:S(2)}, u32[]{:S(2)}) collective-permute-start(bf16[32,2304]{1,0:T(8,128)(2,1)} %get-tuple-element.26), channel_id=1, source_target_pairs={{0,4},{1,5},{2,6},{3,7},{4,0},{5,1},{6,2},{7,3},{8,12},{9,13},{10,... | collective-permute-start | bytes 442376 | tf_op jit(solution)/shard_map/ppermute | solution.py:616
  11.1 1.3 %collective-permute-start.4 = (bf16[32,2304]{1,0:T(8,128)(2,1)}, bf16[32,2304]{1,0:T(8,128)(2,1)}, u32[]{:S(2)}, u32[]{:S(2)}) collective-permute-start(bf16[32,2304]{1,0:T(8,128)(2,1)} %get-tuple-element.27), channel_id=1, source_target_pairs={{0,5},{1,4},{2,7},{3,6},{4,1},{5,0},{6,3},{7,2},{8,13},{9,12},{10,... | collective-permute-start | bytes 442376 | tf_op jit(solution)/shard_map/ppermute | solution.py:616
  12.3 3.6 %collective-permute-start.5 = (bf16[32,2304]{1,0:T(8,128)(2,1)}, bf16[32,2304]{1,0:T(8,128)(2,1)}, u32[]{:S(2)}, u32[]{:S(2)}) collective-permute-start(bf16[32,2304]{1,0:T(8,128)(2,1)} %get-tuple-element.28), channel_id=1, source_target_pairs={{0,6},{1,7},{2,4},{3,5},{4,2},{5,3},{6,0},{7,1},{8,14},{9,15},{10,... | collective-permute-start | bytes 442376 | tf_op jit(solution)/shard_map/ppermute | solution.py:616
  15.9 2.8 %collective-permute-done.1.refs_2_ = bf16[32,2304]{1,0:T(8,128)(2,1)} collective-permute-done((bf16[32,2304]{1,0:T(8,128)(2,1)}, bf16[32,2304]{1,0:T(8,128)(2,1)}, u32[]{:S(2)}, u32[]{:S(2)}) %collective-permute-start.1) | collective-permute-done | bytes 147488 | tf_op jit(solution)/shard_map/ppermute | solution.py:616
  18.8 0.9 %collective-permute-start.6 = (bf16[32,2304]{1,0:T(8,128)(2,1)}, bf16[32,2304]{1,0:T(8,128)(2,1)}, u32[]{:S(2)}, u32[]{:S(2)}) collective-permute-start(bf16[32,2304]{1,0:T(8,128)(2,1)} %get-tuple-element.29), channel_id=1, source_target_pairs={{0,7},{1,6},{2,5},{3,4},{4,3},{5,2},{6,1},{7,0},{8,15},{9,14},{10,... | collective-permute-start | bytes 442376 | tf_op jit(solution)/shard_map/ppermute | solution.py:616
  19.7 0.1 collective-permute-done.2.refs_3_
  19.8 1.9 %join.2 = bf16[4,32,2304]{2,1,0:T(8,128)(2,1)} custom-call(bf16[32,2304]{1,0:T(8,128)(2,1)} %get-tuple-element.22.refs_0_, bf16[32,2304]{1,0:T(8,128)(2,1)} %copy-done, bf16[32,2304]{1,0:T(8,128)(2,1)} %collective-permute-done.1.refs_2_, bf16[32,2304]{1,0:T(8,128)(2,1)} %collective-permute-done.2.refs_3_), custom_call_target="tpu_custom_call" | custom-call | bytes 1179648 | tf_op jit(solution)/shard_map/join/pallas_call | solution.py:231
  21.7 1.7 %collective-permute-start.7 = (bf16[4,32,2304]{2,1,0:T(8,128)(2,1)}, bf16[4,32,2304]{2,1,0:T(8,128)(2,1)}, u32[]{:S(2)}, u32[]{:S(2)}) collective-permute-start(bf16[4,32,2304]{2,1,0:T(8,128)(2,1)} %join.2), channel_id=1, source_target_pairs={{0,16},{8,24},{16,0},{24,8},{1,17},{9,25},{17,1},{25,9},{2,18},{10... | collective-permute-start | bytes 1769480 | tf_op jit(solution)/shard_map/ppermute | solution.py:616
  23.4 9.4 %collective-permute-done.4.refs_5_.refs_1_ = bf16[32,2304]{1,0:T(8,128)(2,1)} collective-permute-done((bf16[32,2304]{1,0:T(8,128)(2,1)}, bf16[32,2304]{1,0:T(8,128)(2,1)}, u32[]{:S(2)}, u32[]{:S(2)}) %collective-permute-start.4) | collective-permute-done | bytes 147488 | tf_op jit(solution)/shard_map/ppermute | solution.py:616
  32.8 1.9 %join.3 = bf16[4,32,2304]{2,1,0:T(8,128)(2,1)} custom-call(bf16[32,2304]{1,0:T(8,128)(2,1)} %collective-permute-done.3.refs_4_.refs_0_, bf16[32,2304]{1,0:T(8,128)(2,1)} %collective-permute-done.4.refs_5_.refs_1_, bf16[32,2304]{1,0:T(8,128)(2,1)} %collective-permute-done.5.refs_6_.refs_2_, bf16[32,2304]{1,0:T(8,128)(2,1)} %collective-permute-done.6.refs_7_.refs_3_), custom_call_target="tpu_custom_call" | custom-call | bytes 1179648 | tf_op jit(solution)/shard_map/join/pallas_call | solution.py:231
  34.7 1.6 %collective-permute-start.9 = (bf16[4,32,2304]{2,1,0:T(8,128)(2,1)}, bf16[4,32,2304]{2,1,0:T(8,128)(2,1)}, u32[]{:S(2)}, u32[]{:S(2)}) collective-permute-start(bf16[4,32,2304]{2,1,0:T(8,128)(2,1)} %join.3), channel_id=1, source_target_pairs={{0,16},{8,24},{16,0},{24,8},{1,17},{9,25},{17,1},{25,9},{2,18},{10... | collective-permute-start | bytes 1769480 | tf_op jit(solution)/shard_map/ppermute | solution.py:616
  36.3 9.9 %back.1 = (bf16[8,16,2304]{2,1,0:T(8,128)(2,1)}, bf16[144,3328]{1,0:T(8,128)(2,1)}, bf16[144,3328]{1,0:T(8,128)(2,1)}) custom-call(s32[1]{0:T(128)} %bitcast.1.me_ref, s32[1]{0:T(128)} %bitcast.2.part_ref, bf16[32,2304]{1,0:T(8,128)(2,1)} %get-tuple-element.22.refs_0_, bf16[32,2304]{1,0:T(8,128)(2,1)} %copy-done, ...), custom_call_target="tpu_custom_call" | custom-call | flops 11324620800 | bytes 1179648 | tf_op jit(solution)/shard_map/back/pallas_call | solution.py:446
  46.2 8.7 %all-to-all-start = ((bf16[8,16,2304]{2,1,0:T(8,128)(2,1)}), bf16[8,16,2304]{2,1,0:T(8,128)(2,1)}, u32[]{:S(2)}, u32[]{:S(2)}) async-start(bf16[8,16,2304]{2,1,0:T(8,128)(2,1)} %get-tuple-element.31), calls=%async_computation | async-start | bytes 1179648 | tf_op jit(solution)/shard_map/all_to_all | solution.py:620
  54.9 0.5 collective-permute-start.11
  55.4 0.1 collective-permute-start.10
  55.5 2.3 %collective-permute-done.8.refs_1_ = bf16[144,3328]{1,0:T(8,128)(2,1)} collective-permute-done((bf16[144,3328]{1,0:T(8,128)(2,1)}, bf16[144,3328]{1,0:T(8,128)(2,1)}, u32[]{:S(2)}, u32[]{:S(2)}) %collective-permute-start.8) | collective-permute-done | bytes 958496 | tf_op jit(solution)/shard_map/ppermute | solution.py:616
  57.8 0.8 %collective-permute-done.11.refs_5_ = bf16[4,32,2304]{2,1,0:T(8,128)(2,1)} collective-permute-done((bf16[4,32,2304]{2,1,0:T(8,128)(2,1)}, bf16[4,32,2304]{2,1,0:T(8,128)(2,1)}, u32[]{:S(2)}, u32[]{:S(2)}) %collective-permute-start.11) | collective-permute-done | bytes 589856 | tf_op jit(solution)/shard_map/ppermute | solution.py:616
  58.6 0.8 %collective-permute-done.10.refs_4_ = bf16[4,32,2304]{2,1,0:T(8,128)(2,1)} collective-permute-done((bf16[4,32,2304]{2,1,0:T(8,128)(2,1)}, bf16[4,32,2304]{2,1,0:T(8,128)(2,1)}, u32[]{:S(2)}, u32[]{:S(2)}) %collective-permute-start.10) | collective-permute-done | bytes 589856 | tf_op jit(solution)/shard_map/ppermute | solution.py:616
  59.5 13.0 %weight_grads.1 = (f32[512,768]{1,0:T(8,128)}, f32[512,768]{1,0:T(8,128)}, f32[768,512]{1,0:T(8,128)}) custom-call(s32[1]{0:T(128)} %bitcast.2.part_ref, bf16[144,3328]{1,0:T(8,128)(2,1)} %get-tuple-element.32.refs_0_, bf16[144,3328]{1,0:T(8,128)(2,1)} %collective-permute-done.8.refs_1_, bf16[4,32,2304]{2,1,0:T(8,128)(2,1)} %collective-permute-done.7.refs_2_, ...), custom_call_target="tpu_custom_call" | custom-call | bytes 1179648 | tf_op jit(solution)/shard_map/weight_grads/pallas_call | solution.py:575
  72.4 2.9 %merge.1 = bf16[128,2048]{1,0:T(8,128)(2,1)} custom-call(s32[1,128]{1,0:T(1,128)} %bitcast.5, bf16[8,16,2304]{2,1,0:T(8,128)(2,1)} %all-to-all-done.back_ref), custom_call_target="tpu_custom_call" | custom-call | flops 134217728 | bytes 1048576 | tf_op jit(solution)/shard_map/merge/pallas_call | solution.py:278
  (10 shorter events, 0.0 us)
Async XLA Ops:
  3.5 8.9 %collective-permute-start = (bf16[32,2304]{1,0:T(8,128)(2,1)}, bf16[32,2304]{1,0:T(8,128)(2,1)S(1)}, u32[]{:S(2)}, u32[]{:S(2)}) collective-permute-start(bf16[32,2304]{1,0:T(8,128)(2,1)} %get-tuple-element.23), channel_id=1, source_target_pairs={{0,1},{1,0},{2,3},{3,2},{4,5},{5,4},{6,7},{7,6},{8,9},{9,8},{10,11... | collective-permute-start | bytes 442376 | tf_op jit(solution)/shard_map/ppermute | solution.py:616
  6.5 12.3 %collective-permute-start.1 = (bf16[32,2304]{1,0:T(8,128)(2,1)}, bf16[32,2304]{1,0:T(8,128)(2,1)}, u32[]{:S(2)}, u32[]{:S(2)}) collective-permute-start(bf16[32,2304]{1,0:T(8,128)(2,1)} %get-tuple-element.24), channel_id=1, source_target_pairs={{0,2},{1,3},{2,0},{3,1},{4,6},{5,7},{6,4},{7,5},{8,10},{9,11},{10,... | collective-permute-start | bytes 442376 | tf_op jit(solution)/shard_map/ppermute | solution.py:616
  8.0 11.8 %collective-permute-start.2 = (bf16[32,2304]{1,0:T(8,128)(2,1)}, bf16[32,2304]{1,0:T(8,128)(2,1)}, u32[]{:S(2)}, u32[]{:S(2)}) collective-permute-start(bf16[32,2304]{1,0:T(8,128)(2,1)} %get-tuple-element.25), channel_id=1, source_target_pairs={{0,3},{1,2},{2,1},{3,0},{4,7},{5,6},{6,5},{7,4},{8,11},{9,10},{10,... | collective-permute-start | bytes 442376 | tf_op jit(solution)/shard_map/ppermute | solution.py:616
  8.1 15.4 %collective-permute-start.3 = (bf16[32,2304]{1,0:T(8,128)(2,1)}, bf16[32,2304]{1,0:T(8,128)(2,1)}, u32[]{:S(2)}, u32[]{:S(2)}) collective-permute-start(bf16[32,2304]{1,0:T(8,128)(2,1)} %get-tuple-element.26), channel_id=1, source_target_pairs={{0,4},{1,5},{2,6},{3,7},{4,0},{5,1},{6,2},{7,3},{8,12},{9,13},{10,... | collective-permute-start | bytes 442376 | tf_op jit(solution)/shard_map/ppermute | solution.py:616
  11.1 21.8 %collective-permute-start.4 = (bf16[32,2304]{1,0:T(8,128)(2,1)}, bf16[32,2304]{1,0:T(8,128)(2,1)}, u32[]{:S(2)}, u32[]{:S(2)}) collective-permute-start(bf16[32,2304]{1,0:T(8,128)(2,1)} %get-tuple-element.27), channel_id=1, source_target_pairs={{0,5},{1,4},{2,7},{3,6},{4,1},{5,0},{6,3},{7,2},{8,13},{9,12},{10,... | collective-permute-start | bytes 442376 | tf_op jit(solution)/shard_map/ppermute | solution.py:616
  12.3 7.5 %copy-start = (bf16[32,2304]{1,0:T(8,128)(2,1)}, bf16[32,2304]{1,0:T(8,128)(2,1)S(1)}, u32[]{:S(2)}) copy-start(bf16[32,2304]{1,0:T(8,128)(2,1)S(1)} %collective-permute-done.refs_1_) | copy-start | bytes 442372
  12.3 20.5 %collective-permute-start.5 = (bf16[32,2304]{1,0:T(8,128)(2,1)}, bf16[32,2304]{1,0:T(8,128)(2,1)}, u32[]{:S(2)}, u32[]{:S(2)}) collective-permute-start(bf16[32,2304]{1,0:T(8,128)(2,1)} %get-tuple-element.28), channel_id=1, source_target_pairs={{0,6},{1,7},{2,4},{3,5},{4,2},{5,3},{6,0},{7,1},{8,14},{9,15},{10,... | collective-permute-start | bytes 442376 | tf_op jit(solution)/shard_map/ppermute | solution.py:616
  18.8 14.1 %collective-permute-start.6 = (bf16[32,2304]{1,0:T(8,128)(2,1)}, bf16[32,2304]{1,0:T(8,128)(2,1)}, u32[]{:S(2)}, u32[]{:S(2)}) collective-permute-start(bf16[32,2304]{1,0:T(8,128)(2,1)} %get-tuple-element.29), channel_id=1, source_target_pairs={{0,7},{1,6},{2,5},{3,4},{4,3},{5,2},{6,1},{7,0},{8,15},{9,14},{10,... | collective-permute-start | bytes 442376 | tf_op jit(solution)/shard_map/ppermute | solution.py:616
  21.7 24.5 %collective-permute-start.7 = (bf16[4,32,2304]{2,1,0:T(8,128)(2,1)}, bf16[4,32,2304]{2,1,0:T(8,128)(2,1)}, u32[]{:S(2)}, u32[]{:S(2)}) collective-permute-start(bf16[4,32,2304]{2,1,0:T(8,128)(2,1)} %join.2), channel_id=1, source_target_pairs={{0,16},{8,24},{16,0},{24,8},{1,17},{9,25},{17,1},{25,9},{2,18},{10... | collective-permute-start | bytes 1769480 | tf_op jit(solution)/shard_map/ppermute | solution.py:616
  34.7 20.2 %collective-permute-start.9 = (bf16[4,32,2304]{2,1,0:T(8,128)(2,1)}, bf16[4,32,2304]{2,1,0:T(8,128)(2,1)}, u32[]{:S(2)}, u32[]{:S(2)}) collective-permute-start(bf16[4,32,2304]{2,1,0:T(8,128)(2,1)} %join.3), channel_id=1, source_target_pairs={{0,16},{8,24},{16,0},{24,8},{1,17},{9,25},{17,1},{25,9},{2,18},{10... | collective-permute-start | bytes 1769480 | tf_op jit(solution)/shard_map/ppermute | solution.py:616
  46.2 26.2 %all-to-all-start = ((bf16[8,16,2304]{2,1,0:T(8,128)(2,1)}), bf16[8,16,2304]{2,1,0:T(8,128)(2,1)}, u32[]{:S(2)}, u32[]{:S(2)}) async-start(bf16[8,16,2304]{2,1,0:T(8,128)(2,1)} %get-tuple-element.31), calls=%async_computation | async-start | bytes 1179648 | tf_op jit(solution)/shard_map/all_to_all | solution.py:620
  54.9 2.9 %collective-permute-start.8 = (bf16[144,3328]{1,0:T(8,128)(2,1)}, bf16[144,3328]{1,0:T(8,128)(2,1)}, u32[]{:S(2)}, u32[]{:S(2)}) collective-permute-start(bf16[144,3328]{1,0:T(8,128)(2,1)} %get-tuple-element.33), channel_id=1, source_target_pairs={{0,8},{8,0},{16,24},{24,16},{1,9},{9,1},{17,25},{25,17},{2,10},{10... | collective-permute-start | bytes 2875400 | tf_op jit(solution)/shard_map/ppermute | solution.py:616
  54.9 3.7 %collective-permute-start.11 = (bf16[4,32,2304]{2,1,0:T(8,128)(2,1)}, bf16[4,32,2304]{2,1,0:T(8,128)(2,1)}, u32[]{:S(2)}, u32[]{:S(2)}) collective-permute-start(bf16[4,32,2304]{2,1,0:T(8,128)(2,1)} %collective-permute-done.9.refs_3_), channel_id=1, source_target_pairs={{0,8},{8,0},{16,24},{24,16},{1,9},{9,1},{17,25},{25,17},{2,10},{10... | collective-permute-start | bytes 1769480 | tf_op jit(solution)/shard_map/ppermute | solution.py:616
  55.4 4.0 %collective-permute-start.10 = (bf16[4,32,2304]{2,1,0:T(8,128)(2,1)}, bf16[4,32,2304]{2,1,0:T(8,128)(2,1)}, u32[]{:S(2)}, u32[]{:S(2)}) collective-permute-start(bf16[4,32,2304]{2,1,0:T(8,128)(2,1)} %collective-permute-done.7.refs_2_), channel_id=1, source_target_pairs={{0,8},{8,0},{16,24},{24,16},{1,9},{9,1},{17,25},{25,17},{2,10},{10... | collective-permute-start | bytes 1769480 | tf_op jit(solution)/shard_map/ppermute | solution.py:616

commit v19 on v18

--- a/solution.py
+++ b/solution.py
@@ -214,7 +214,7 @@
     )(me, *sources)
 
 
-def join(received):
+def join(received, flops=0):
     count = len(received)
     shape = (count,) + received[0].shape
 
@@ -239,7 +239,7 @@
             pltpu.SemaphoreType.DMA((count,)),
         ],
         compiler_params=params(),
-        cost_estimate=cost(0, 4 * received[0].size * count),
+        cost_estimate=cost(flops, 4 * received[0].size * count),
         name="join",
     )(*received)
 
@@ -249,43 +249,33 @@
     tokens = routes.shape[1]
     width = width_of(returned)
     pieces, step = cut(width)
-    chunk = 2 * step
-
-    def kernel(routes_ref, back_ref, out, named, held, made, arrived, gone):
-        spans = [slice(width, width + step)]
-        spans += [slice(at, at + chunk) for at in range(0, width, chunk)]
-        pairs = [(routes_ref, named)]
-        pairs += [(back_ref.at[:, :, span], held.at[:, :, span]) for span in spans]
-        leaving = [(made.at[:, span], out.at[:, span]) for span in spans[1:]]
+
+    def kernel(routes_ref, back_ref, out, named, held, arrived):
+        pairs = [(routes_ref, named), (back_ref, held)]
         start(pairs, arrived)
         wait(pairs[:1], arrived)
         main, spill, piece = slot_masks(named[...], blocks, width)
         mains = ones(main)
-        picks = jnp.concatenate([ones(spill & (piece == at)) for at in range(pieces)], 1)
-        wait(pairs[:2], arrived, 1)
-        tails = jnp.concatenate([held[at, :, width:] for at in range(blocks)], 0)
-        extra = dot(picks, tails, BY_ROWS)
-        for at, span in enumerate(spans[1:]):
-            wait(pairs[: at + 3], arrived, at + 2)
-            rows = jnp.concatenate([held[block, :, span] for block in range(blocks)], 0)
-            here = [extra[(2 * at + side) * tokens :][:tokens] for side in range(2)]
-            picked = dot(mains, rows, BY_ROWS) + jnp.concatenate(here, 1)
-            made[:, span] = picked.astype(jnp.bfloat16)
-            start(leaving[: at + 1], gone, at)
-        wait(leaving, gone)
-
-    chunks = width // chunk
+        picks = [ones(spill & (piece == at)) for at in range(pieces)]
+        wait(pairs, arrived, 1)
+        rows = jnp.concatenate([held[at, :, :width] for at in range(blocks)], 0)
+        extra = jnp.concatenate([held[at, :, width:] for at in range(blocks)], 0)
+        picked = dot(mains, rows, BY_ROWS)
+        for at in range(pieces):
+            columns = slice(at * step, (at + 1) * step)
+            out[:, columns] = (picked[:, columns] + dot(picks[at], extra, BY_ROWS)).astype(
+                jnp.bfloat16
+            )
+
     return pl.pallas_call(
         kernel,
         out_shape=jax.ShapeDtypeStruct((tokens, width), jnp.bfloat16),
         in_specs=anywhere(2),
-        out_specs=pl.BlockSpec(memory_space=pl.ANY),
+        out_specs=pl.BlockSpec(memory_space=pltpu.VMEM),
         scratch_shapes=[
             pltpu.VMEM(routes.shape, routes.dtype),
             pltpu.VMEM(returned.shape, returned.dtype),
-            pltpu.VMEM((tokens, width), jnp.bfloat16),
-            pltpu.SemaphoreType.DMA((chunks + 2,)),
-            pltpu.SemaphoreType.DMA((chunks,)),
+            pltpu.SemaphoreType.DMA((2,)),
         ],
         compiler_params=params(),
         cost_estimate=cost(4 * blocks * ROWS * tokens * width, 4 * tokens * width),
@@ -637,12 +627,14 @@
         received[distance] = swap(received[distance], "expert", distance)
     half = blocks // 2
     far = swap(join(received[:half]), "dp", 2)
-    far_half = swap(join(received[half:]), "dp", 2)
+    work = 50 * blocks * MOST * gate_proj.size
+    far_half = swap(join(received[half:], work), "dp", 2)
     sent, kept, handed = back(tile, share, me, part, received, *weights)
-    sent, far = lax.optimization_barrier((sent, far))
+    last = swap(far, "dp", 1)
+    sent, last = lax.optimization_barrier((sent, last))
     returned = exchange(sent)
     far = [far, after(far_half, sent)]
-    last = [swap(item, "dp", 1) for item in far]
+    last = [last, swap(far[1], "dp", 1)]
     known = [kept, swap(handed, "dp", 1)]
     grads = weight_grads(tile, share, part, known, [far, last], *weights)
     return (merge(routes, after(returned, *grads)), *grads)

time: 75.8 us -> 75.2 us (level)
  starting transfers between devices: 26 us -> 24.2 us
  waiting for transfers between devices: 16.3 us -> 18 us
    all_to_all x1, starting transfers between devices: 8.68 us -> 6.92 us  [exchange(): lax.all_to_all(blocks, 'expert', split_axis=0, concat_axis=0, tiled=True)]
    ppermute x12, waiting for transfers between devices: 16.3 us -> 17.3 us  [swap(): lax.ppermute(value, axis, [(at, at ^ distance) for at in range(size)])]
  transfers between devices with their start and end apart: 13 -> 13, of which waited for: 6 -> 7; matrix products, arithmetic and copies ran while one was open for 0% -> 0% of each run, Pallas kernels for 35% -> 36%
where the time goes in v19:
time: 75.2 us; the launch traced here: 74.8 us
  Pallas kernels  31.8 us (42%)
  starting transfers between devices  24.2 us (32%)
  waiting for transfers between devices  18 us (24%)
  between operations  0.86 us (1%)
    ppermute x12, waiting for transfers between devices, swap(): lax.ppermute(value, axis, [(at, at ^ distance) for at in range(size)])  17.3 us
    ppermute x12, starting transfers between devices, swap(): lax.ppermute(value, axis, [(at, at ^ distance) for at in range(size)])  17.2 us
    pallas_call x1, Pallas kernels, weight_grads(): pl.pallas_call(kernel, out_shape=[jax.ShapeDtypeStruct((share, hid), jnp....  13 us
    pallas_call x1, Pallas kernels, back(): pl.pallas_call(kernel, out_shape=[jax.ShapeDtypeStruct(shape, jnp.bfloat1...  9.93 us
    all_to_all x1, starting transfers between devices, exchange(): lax.all_to_all(blocks, 'expert', split_axis=0, concat_axis=0, tiled=True)  6.92 us
    pallas_call x2, Pallas kernels, join(): pl.pallas_call(kernel, out_shape=jax.ShapeDtypeStruct(shape, jnp.bfloat16...  3.7 us
    pallas_call x1, Pallas kernels, pack(): pl.pallas_call(kernel, out_shape=[jax.ShapeDtypeStruct(block_shape, jnp.b...  2.82 us
    pallas_call x1, Pallas kernels, merge(): pl.pallas_call(kernel, out_shape=jax.ShapeDtypeStruct((tokens, width), jn...  2.35 us
  transfers between devices with their start and end apart: 13, of which 7 were waited for; matrix products, arithmetic and copies ran while one was open for 0% of the time, Pallas kernels for 36%

profile of v19, /device:TPU:0, one launch (start us, length us, event | category | flops | bytes accessed | tf_op | source)
XLA Modules:
  0.0 74.8 jit_solution(3121854605316958939)
XLA Ops:
  0.6 2.8 %pack.1 = (bf16[32,2304]{1,0:T(8,128)(2,1)}, bf16[32,2304]{1,0:T(8,128)(2,1)}, bf16[32,2304]{1,0:T(8,128)(2,1)}, bf16[32,2304]{1,0:T(8,128)(2,1)}, bf16[32,2304]...) custom-call(s32[1]{0:T(128)} %bitcast.1.me_ref, ...), custom_call_target="tpu_custom_call" | custom-call | flops 268435456 | bytes 2097152 | tf_op jit(solution)/shard_map/pack/pallas_call | solution.py:200
  3.5 3.0 %collective-permute-start = (bf16[32,2304]{1,0:T(8,128)(2,1)}, bf16[32,2304]{1,0:T(8,128)(2,1)S(1)}, u32[]{:S(2)}, u32[]{:S(2)}) collective-permute-start(bf16[32,2304]{1,0:T(8,128)(2,1)} %get-tuple-element.23), channel_id=1, source_target_pairs={{0,1},{1,0},{2,3},{3,2},{4,5},{5,4},{6,7},{7,6},{8,9},{9,8},{10,11... | collective-permute-start | bytes 442376 | tf_op jit(solution)/shard_map/ppermute | solution.py:606
  6.5 1.6 %collective-permute-start.1 = (bf16[32,2304]{1,0:T(8,128)(2,1)}, bf16[32,2304]{1,0:T(8,128)(2,1)}, u32[]{:S(2)}, u32[]{:S(2)}) collective-permute-start(bf16[32,2304]{1,0:T(8,128)(2,1)} %get-tuple-element.24), channel_id=1, source_target_pairs={{0,2},{1,3},{2,0},{3,1},{4,6},{5,7},{6,4},{7,5},{8,10},{9,11},{10,... | collective-permute-start | bytes 442376 | tf_op jit(solution)/shard_map/ppermute | solution.py:606
  8.1 3.0 %collective-permute-start.3 = (bf16[32,2304]{1,0:T(8,128)(2,1)}, bf16[32,2304]{1,0:T(8,128)(2,1)}, u32[]{:S(2)}, u32[]{:S(2)}) collective-permute-start(bf16[32,2304]{1,0:T(8,128)(2,1)} %get-tuple-element.26), channel_id=1, source_target_pairs={{0,4},{1,5},{2,6},{3,7},{4,0},{5,1},{6,2},{7,3},{8,12},{9,13},{10,... | collective-permute-start | bytes 442376 | tf_op jit(solution)/shard_map/ppermute | solution.py:606
  11.1 1.3 %collective-permute-start.4 = (bf16[32,2304]{1,0:T(8,128)(2,1)}, bf16[32,2304]{1,0:T(8,128)(2,1)}, u32[]{:S(2)}, u32[]{:S(2)}) collective-permute-start(bf16[32,2304]{1,0:T(8,128)(2,1)} %get-tuple-element.27), channel_id=1, source_target_pairs={{0,5},{1,4},{2,7},{3,6},{4,1},{5,0},{6,3},{7,2},{8,13},{9,12},{10,... | collective-permute-start | bytes 442376 | tf_op jit(solution)/shard_map/ppermute | solution.py:606
  12.3 3.6 %collective-permute-start.5 = (bf16[32,2304]{1,0:T(8,128)(2,1)}, bf16[32,2304]{1,0:T(8,128)(2,1)}, u32[]{:S(2)}, u32[]{:S(2)}) collective-permute-start(bf16[32,2304]{1,0:T(8,128)(2,1)} %get-tuple-element.28), channel_id=1, source_target_pairs={{0,6},{1,7},{2,4},{3,5},{4,2},{5,3},{6,0},{7,1},{8,14},{9,15},{10,... | collective-permute-start | bytes 442376 | tf_op jit(solution)/shard_map/ppermute | solution.py:606
  15.9 2.8 %collective-permute-done.1.refs_2_ = bf16[32,2304]{1,0:T(8,128)(2,1)} collective-permute-done((bf16[32,2304]{1,0:T(8,128)(2,1)}, bf16[32,2304]{1,0:T(8,128)(2,1)}, u32[]{:S(2)}, u32[]{:S(2)}) %collective-permute-start.1) | collective-permute-done | bytes 147488 | tf_op jit(solution)/shard_map/ppermute | solution.py:606
  18.8 0.9 %collective-permute-start.6 = (bf16[32,2304]{1,0:T(8,128)(2,1)}, bf16[32,2304]{1,0:T(8,128)(2,1)}, u32[]{:S(2)}, u32[]{:S(2)}) collective-permute-start(bf16[32,2304]{1,0:T(8,128)(2,1)} %get-tuple-element.29), channel_id=1, source_target_pairs={{0,7},{1,6},{2,5},{3,4},{4,3},{5,2},{6,1},{7,0},{8,15},{9,14},{10,... | collective-permute-start | bytes 442376 | tf_op jit(solution)/shard_map/ppermute | solution.py:606
  19.7 0.1 collective-permute-done.2.refs_3_
  19.8 1.9 %join.2 = bf16[4,32,2304]{2,1,0:T(8,128)(2,1)} custom-call(bf16[32,2304]{1,0:T(8,128)(2,1)} %get-tuple-element.22.refs_0_, bf16[32,2304]{1,0:T(8,128)(2,1)} %copy-done, bf16[32,2304]{1,0:T(8,128)(2,1)} %collective-permute-done.1.refs_2_, bf16[32,2304]{1,0:T(8,128)(2,1)} %collective-permute-done.2.refs_3_), custom_call_target="tpu_custom_call" | custom-call | bytes 1179648 | tf_op jit(solution)/shard_map/join/pallas_call | solution.py:231
  21.7 1.7 %collective-permute-start.7 = (bf16[4,32,2304]{2,1,0:T(8,128)(2,1)}, bf16[4,32,2304]{2,1,0:T(8,128)(2,1)}, u32[]{:S(2)}, u32[]{:S(2)}) collective-permute-start(bf16[4,32,2304]{2,1,0:T(8,128)(2,1)} %join.2), channel_id=1, source_target_pairs={{0,16},{8,24},{16,0},{24,8},{1,17},{9,25},{17,1},{25,9},{2,18},{10... | collective-permute-start | bytes 1769480 | tf_op jit(solution)/shard_map/ppermute | solution.py:606
  23.4 9.4 %collective-permute-done.4.refs_5_.refs_1_ = bf16[32,2304]{1,0:T(8,128)(2,1)} collective-permute-done((bf16[32,2304]{1,0:T(8,128)(2,1)}, bf16[32,2304]{1,0:T(8,128)(2,1)}, u32[]{:S(2)}, u32[]{:S(2)}) %collective-permute-start.4) | collective-permute-done | bytes 147488 | tf_op jit(solution)/shard_map/ppermute | solution.py:606
  32.8 1.9 %join.3 = bf16[4,32,2304]{2,1,0:T(8,128)(2,1)} custom-call(bf16[32,2304]{1,0:T(8,128)(2,1)} %collective-permute-done.3.refs_4_.refs_0_, bf16[32,2304]{1,0:T(8,128)(2,1)} %collective-permute-done.4.refs_5_.refs_1_, bf16[32,2304]{1,0:T(8,128)(2,1)} %collective-permute-done.5.refs_6_.refs_2_, bf16[32,2304]{1,0:T(8,128)(2,1)} %collective-permute-done.6.refs_7_.refs_3_), custom_call_target="tpu_custom_call" | custom-call | flops 11324620800 | bytes 1179648 | tf_op jit(solution)/shard_map/join/pallas_call | solution.py:231
  34.7 1.6 %collective-permute-start.10 = (bf16[4,32,2304]{2,1,0:T(8,128)(2,1)}, bf16[4,32,2304]{2,1,0:T(8,128)(2,1)}, u32[]{:S(2)}, u32[]{:S(2)}) collective-permute-start(bf16[4,32,2304]{2,1,0:T(8,128)(2,1)} %join.3), channel_id=1, source_target_pairs={{0,16},{8,24},{16,0},{24,8},{1,17},{9,25},{17,1},{25,9},{2,18},{10... | collective-permute-start | bytes 1769480 | tf_op jit(solution)/shard_map/ppermute | solution.py:606
  36.3 1.8 %collective-permute-done.7.refs_2_ = bf16[4,32,2304]{2,1,0:T(8,128)(2,1)} collective-permute-done((bf16[4,32,2304]{2,1,0:T(8,128)(2,1)}, bf16[4,32,2304]{2,1,0:T(8,128)(2,1)}, u32[]{:S(2)}, u32[]{:S(2)}) %collective-permute-start.7) | collective-permute-done | bytes 589856 | tf_op jit(solution)/shard_map/ppermute | solution.py:606
  38.0 9.9 %back.1 = (bf16[8,16,2304]{2,1,0:T(8,128)(2,1)}, bf16[144,3328]{1,0:T(8,128)(2,1)}, bf16[144,3328]{1,0:T(8,128)(2,1)}) custom-call(s32[1]{0:T(128)} %bitcast.1.me_ref, s32[1]{0:T(128)} %bitcast.2.part_ref, bf16[32,2304]{1,0:T(8,128)(2,1)} %get-tuple-element.22.refs_0_, bf16[32,2304]{1,0:T(8,128)(2,1)} %copy-done, ...), custom_call_target="tpu_custom_call" | custom-call | flops 11324620800 | bytes 1179648 | tf_op jit(solution)/shard_map/back/pallas_call | solution.py:436
  48.0 6.9 %all-to-all-start = ((bf16[8,16,2304]{2,1,0:T(8,128)(2,1)}), bf16[8,16,2304]{2,1,0:T(8,128)(2,1)}, u32[]{:S(2)}, u32[]{:S(2)}) async-start(bf16[8,16,2304]{2,1,0:T(8,128)(2,1)} %get-tuple-element.31), calls=%async_computation | async-start | bytes 1179648 | tf_op jit(solution)/shard_map/all_to_all | solution.py:610
  54.9 0.2 collective-permute-start.9
  55.2 0.3 collective-permute-start.11
  55.4 2.4 %collective-permute-done.9.refs_1_ = bf16[144,3328]{1,0:T(8,128)(2,1)} collective-permute-done((bf16[144,3328]{1,0:T(8,128)(2,1)}, bf16[144,3328]{1,0:T(8,128)(2,1)}, u32[]{:S(2)}, u32[]{:S(2)}) %collective-permute-start.9) | collective-permute-done | bytes 958496 | tf_op jit(solution)/shard_map/ppermute | solution.py:606
  57.8 0.8 %collective-permute-done.11.refs_5_ = bf16[4,32,2304]{2,1,0:T(8,128)(2,1)} collective-permute-done((bf16[4,32,2304]{2,1,0:T(8,128)(2,1)}, bf16[4,32,2304]{2,1,0:T(8,128)(2,1)}, u32[]{:S(2)}, u32[]{:S(2)}) %collective-permute-start.11) | collective-permute-done | bytes 589856 | tf_op jit(solution)/shard_map/ppermute | solution.py:606
  58.6 13.0 %weight_grads.1 = (f32[512,768]{1,0:T(8,128)}, f32[512,768]{1,0:T(8,128)}, f32[768,512]{1,0:T(8,128)}) custom-call(s32[1]{0:T(128)} %bitcast.2.part_ref, bf16[144,3328]{1,0:T(8,128)(2,1)} %get-tuple-element.32.refs_0_, bf16[144,3328]{1,0:T(8,128)(2,1)} %collective-permute-done.9.refs_1_, bf16[4,32,2304]{2,1,0:T(8,128)(2,1)} %collective-permute-done.7.refs_2_, ...), custom_call_target="tpu_custom_call" | custom-call | bytes 1179648 | tf_op jit(solution)/shard_map/weight_grads/pallas_call | solution.py:565
  71.6 0.7 all-to-all-done.back_ref
  72.3 2.4 %merge.1 = bf16[128,2048]{1,0:T(8,128)(2,1)} custom-call(s32[1,128]{1,0:T(1,128)} %bitcast.5, bf16[8,16,2304]{2,1,0:T(8,128)(2,1)} %all-to-all-done.back_ref), custom_call_target="tpu_custom_call" | custom-call | flops 134217728 | bytes 1048576 | tf_op jit(solution)/shard_map/merge/pallas_call | solution.py:270
  (10 shorter events, 0.0 us)
Async XLA Ops:
  3.5 8.9 %collective-permute-start = (bf16[32,2304]{1,0:T(8,128)(2,1)}, bf16[32,2304]{1,0:T(8,128)(2,1)S(1)}, u32[]{:S(2)}, u32[]{:S(2)}) collective-permute-start(bf16[32,2304]{1,0:T(8,128)(2,1)} %get-tuple-element.23), channel_id=1, source_target_pairs={{0,1},{1,0},{2,3},{3,2},{4,5},{5,4},{6,7},{7,6},{8,9},{9,8},{10,11... | collective-permute-start | bytes 442376 | tf_op jit(solution)/shard_map/ppermute | solution.py:606
  6.5 12.3 %collective-permute-start.1 = (bf16[32,2304]{1,0:T(8,128)(2,1)}, bf16[32,2304]{1,0:T(8,128)(2,1)}, u32[]{:S(2)}, u32[]{:S(2)}) collective-permute-start(bf16[32,2304]{1,0:T(8,128)(2,1)} %get-tuple-element.24), channel_id=1, source_target_pairs={{0,2},{1,3},{2,0},{3,1},{4,6},{5,7},{6,4},{7,5},{8,10},{9,11},{10,... | collective-permute-start | bytes 442376 | tf_op jit(solution)/shard_map/ppermute | solution.py:606
  8.0 11.8 %collective-permute-start.2 = (bf16[32,2304]{1,0:T(8,128)(2,1)}, bf16[32,2304]{1,0:T(8,128)(2,1)}, u32[]{:S(2)}, u32[]{:S(2)}) collective-permute-start(bf16[32,2304]{1,0:T(8,128)(2,1)} %get-tuple-element.25), channel_id=1, source_target_pairs={{0,3},{1,2},{2,1},{3,0},{4,7},{5,6},{6,5},{7,4},{8,11},{9,10},{10,... | collective-permute-start | bytes 442376 | tf_op jit(solution)/shard_map/ppermute | solution.py:606
  8.1 15.4 %collective-permute-start.3 = (bf16[32,2304]{1,0:T(8,128)(2,1)}, bf16[32,2304]{1,0:T(8,128)(2,1)}, u32[]{:S(2)}, u32[]{:S(2)}) collective-permute-start(bf16[32,2304]{1,0:T(8,128)(2,1)} %get-tuple-element.26), channel_id=1, source_target_pairs={{0,4},{1,5},{2,6},{3,7},{4,0},{5,1},{6,2},{7,3},{8,12},{9,13},{10,... | collective-permute-start | bytes 442376 | tf_op jit(solution)/shard_map/ppermute | solution.py:606
  11.1 21.8 %collective-permute-start.4 = (bf16[32,2304]{1,0:T(8,128)(2,1)}, bf16[32,2304]{1,0:T(8,128)(2,1)}, u32[]{:S(2)}, u32[]{:S(2)}) collective-permute-start(bf16[32,2304]{1,0:T(8,128)(2,1)} %get-tuple-element.27), channel_id=1, source_target_pairs={{0,5},{1,4},{2,7},{3,6},{4,1},{5,0},{6,3},{7,2},{8,13},{9,12},{10,... | collective-permute-start | bytes 442376 | tf_op jit(solution)/shard_map/ppermute | solution.py:606
  12.3 7.5 %copy-start = (bf16[32,2304]{1,0:T(8,128)(2,1)}, bf16[32,2304]{1,0:T(8,128)(2,1)S(1)}, u32[]{:S(2)}) copy-start(bf16[32,2304]{1,0:T(8,128)(2,1)S(1)} %collective-permute-done.refs_1_) | copy-start | bytes 442372
  12.3 20.5 %collective-permute-start.5 = (bf16[32,2304]{1,0:T(8,128)(2,1)}, bf16[32,2304]{1,0:T(8,128)(2,1)}, u32[]{:S(2)}, u32[]{:S(2)}) collective-permute-start(bf16[32,2304]{1,0:T(8,128)(2,1)} %get-tuple-element.28), channel_id=1, source_target_pairs={{0,6},{1,7},{2,4},{3,5},{4,2},{5,3},{6,0},{7,1},{8,14},{9,15},{10,... | collective-permute-start | bytes 442376 | tf_op jit(solution)/shard_map/ppermute | solution.py:606
  18.8 14.1 %collective-permute-start.6 = (bf16[32,2304]{1,0:T(8,128)(2,1)}, bf16[32,2304]{1,0:T(8,128)(2,1)}, u32[]{:S(2)}, u32[]{:S(2)}) collective-permute-start(bf16[32,2304]{1,0:T(8,128)(2,1)} %get-tuple-element.29), channel_id=1, source_target_pairs={{0,7},{1,6},{2,5},{3,4},{4,3},{5,2},{6,1},{7,0},{8,15},{9,14},{10,... | collective-permute-start | bytes 442376 | tf_op jit(solution)/shard_map/ppermute | solution.py:606
  21.7 16.4 %collective-permute-start.7 = (bf16[4,32,2304]{2,1,0:T(8,128)(2,1)}, bf16[4,32,2304]{2,1,0:T(8,128)(2,1)}, u32[]{:S(2)}, u32[]{:S(2)}) collective-permute-start(bf16[4,32,2304]{2,1,0:T(8,128)(2,1)} %join.2), channel_id=1, source_target_pairs={{0,16},{8,24},{16,0},{24,8},{1,17},{9,25},{17,1},{25,9},{2,18},{10... | collective-permute-start | bytes 1769480 | tf_op jit(solution)/shard_map/ppermute | solution.py:606
  34.7 20.5 %collective-permute-start.10 = (bf16[4,32,2304]{2,1,0:T(8,128)(2,1)}, bf16[4,32,2304]{2,1,0:T(8,128)(2,1)}, u32[]{:S(2)}, u32[]{:S(2)}) collective-permute-start(bf16[4,32,2304]{2,1,0:T(8,128)(2,1)} %join.3), channel_id=1, source_target_pairs={{0,16},{8,24},{16,0},{24,8},{1,17},{9,25},{17,1},{25,9},{2,18},{10... | collective-permute-start | bytes 1769480 | tf_op jit(solution)/shard_map/ppermute | solution.py:606
  38.0 9.9 %collective-permute-start.8 = (bf16[4,32,2304]{2,1,0:T(8,128)(2,1)}, bf16[4,32,2304]{2,1,0:T(8,128)(2,1)}, u32[]{:S(2)}, u32[]{:S(2)}) collective-permute-start(bf16[4,32,2304]{2,1,0:T(8,128)(2,1)} %collective-permute-done.7.refs_2_), channel_id=1, source_target_pairs={{0,8},{8,0},{16,24},{24,16},{1,9},{9,1},{17,25},{25,17},{2,10},{10... | collective-permute-start | bytes 1769480 | tf_op jit(solution)/shard_map/ppermute | solution.py:606
  48.0 24.3 %all-to-all-start = ((bf16[8,16,2304]{2,1,0:T(8,128)(2,1)}), bf16[8,16,2304]{2,1,0:T(8,128)(2,1)}, u32[]{:S(2)}, u32[]{:S(2)}) async-start(bf16[8,16,2304]{2,1,0:T(8,128)(2,1)} %get-tuple-element.31), calls=%async_computation | async-start | bytes 1179648 | tf_op jit(solution)/shard_map/all_to_all | solution.py:610
  54.9 2.9 %collective-permute-start.9 = (bf16[144,3328]{1,0:T(8,128)(2,1)}, bf16[144,3328]{1,0:T(8,128)(2,1)}, u32[]{:S(2)}, u32[]{:S(2)}) collective-permute-start(bf16[144,3328]{1,0:T(8,128)(2,1)} %get-tuple-element.33), channel_id=1, source_target_pairs={{0,8},{8,0},{16,24},{24,16},{1,9},{9,1},{17,25},{25,17},{2,10},{10... | collective-permute-start | bytes 2875400 | tf_op jit(solution)/shard_map/ppermute | solution.py:606
  55.2 3.5 %collective-permute-start.11 = (bf16[4,32,2304]{2,1,0:T(8,128)(2,1)}, bf16[4,32,2304]{2,1,0:T(8,128)(2,1)}, u32[]{:S(2)}, u32[]{:S(2)}) collective-permute-start(bf16[4,32,2304]{2,1,0:T(8,128)(2,1)} %collective-permute-done.10.refs_3_), channel_id=1, source_target_pairs={{0,8},{8,0},{16,24},{24,16},{1,9},{9,1},{17,25},{25,17},{2,10},{10... | collective-permute-start | bytes 1769480 | tf_op jit(solution)/shard_map/ppermute | solution.py:606

commit v20 on v19

--- a/solution.py
+++ b/solution.py
@@ -336,7 +336,7 @@
     return hidden, d_gate, d_up
 
 
-def back(tile, share, me, part, group, gate_proj, up_proj, down_proj):
+def back(tile, share, me, part, order, group, gate_proj, up_proj, down_proj):
     blocks = len(group)
     width, hid = gate_proj.shape
     slots = blocks * MOST
@@ -417,13 +417,13 @@
             done += dot(factors[:, 2 * hid :], up[here, :], BY_WIDTH)
             done = done.astype(jnp.bfloat16)
             for block in range(blocks):
-                staged[me_ref[0] ^ block, :, here] = done[block * ROWS : (block + 1) * ROWS]
+                staged[me_ref[0] ^ order[block], :, here] = done[block * ROWS : (block + 1) * ROWS]
             leave(at).start()
             extras += [done[blocks * ROWS :, :step], done[blocks * ROWS :, step:]]
         tail = dot(spill_picks(blocks, pieces), jnp.concatenate(extras, 0), BY_ROWS)
         tail = tail.astype(jnp.bfloat16)
         for block in range(blocks):
-            staged[me_ref[0] ^ block, :, width:] = tail[block * ROWS : (block + 1) * ROWS]
+            staged[me_ref[0] ^ order[block], :, width:] = tail[block * ROWS : (block + 1) * ROWS]
         last = pltpu.make_async_copy(
             staged.at[:, :, width:], out.at[:, :, width:], gone.at[chunks]
         )
@@ -625,15 +625,17 @@
     received = list(pack(blocks, me, routes, gates, tokens, cotangent))
     for distance in reversed(range(1, blocks)):
         received[distance] = swap(received[distance], "expert", distance)
-    half = blocks // 2
-    far = swap(join(received[:half]), "dp", 2)
+    order = [0, 1, 2, 4, 5, 6, 7, 3]
+    early = 3
+    received = [received[index] for index in order]
+    far = swap(join(received[:early]), "dp", 2)
     work = 50 * blocks * MOST * gate_proj.size
-    far_half = swap(join(received[half:], work), "dp", 2)
-    sent, kept, handed = back(tile, share, me, part, received, *weights)
+    far_rest = swap(join(received[early:], work), "dp", 2)
+    sent, kept, handed = back(tile, share, me, part, order, received, *weights)
     last = swap(far, "dp", 1)
     sent, last = lax.optimization_barrier((sent, last))
     returned = exchange(sent)
-    far = [far, after(far_half, sent)]
+    far = [far, after(far_rest, sent)]
     last = [last, swap(far[1], "dp", 1)]
     known = [kept, swap(handed, "dp", 1)]
     grads = weight_grads(tile, share, part, known, [far, last], *weights)

time: 75.2 us -> 73.8 us (0.981)
  starting transfers between devices: 24.2 us -> 20.4 us
  waiting for transfers between devices: 18 us -> 20.4 us
    ppermute x12, waiting for transfers between devices: 17.3 us -> 20.4 us  [swap(): lax.ppermute(value, axis, [(at, at ^ distance) for at in range(size)])]
    all_to_all x1, starting transfers between devices: 6.92 us -> 4.49 us  [exchange(): lax.all_to_all(blocks, 'expert', split_axis=0, concat_axis=0, tiled=True)]
    ppermute x12, starting transfers between devices: 17.2 us -> 15.9 us  [swap(): lax.ppermute(value, axis, [(at, at ^ distance) for at in range(size)])]
  transfers between devices with their start and end apart: 13 -> 13, of which waited for: 7 -> 5; matrix products, arithmetic and copies ran while one was open for 0% -> 0% of each run, Pallas kernels for 36% -> 36%
where the time goes in v20:
time: 73.8 us; the launch traced here: 73.5 us
  Pallas kernels  31.9 us (43%)
  starting transfers between devices  20.4 us (28%)
  waiting for transfers between devices  20.4 us (28%)
  between operations  0.87 us (1%)
    ppermute x12, waiting for transfers between devices, swap(): lax.ppermute(value, axis, [(at, at ^ distance) for at in range(size)])  20.4 us
    ppermute x12, starting transfers between devices, swap(): lax.ppermute(value, axis, [(at, at ^ distance) for at in range(size)])  15.9 us
    pallas_call x1, Pallas kernels, weight_grads(): pl.pallas_call(kernel, out_shape=[jax.ShapeDtypeStruct((share, hid), jnp....  13 us
    pallas_call x1, Pallas kernels, back(): pl.pallas_call(kernel, out_shape=[jax.ShapeDtypeStruct(shape, jnp.bfloat1...  9.95 us
    all_to_all x1, starting transfers between devices, exchange(): lax.all_to_all(blocks, 'expert', split_axis=0, concat_axis=0, tiled=True)  4.49 us
    pallas_call x2, Pallas kernels, join(): pl.pallas_call(kernel, out_shape=jax.ShapeDtypeStruct(shape, jnp.bfloat16...  3.71 us
    pallas_call x1, Pallas kernels, pack(): pl.pallas_call(kernel, out_shape=[jax.ShapeDtypeStruct(block_shape, jnp.b...  2.84 us
    pallas_call x1, Pallas kernels, merge(): pl.pallas_call(kernel, out_shape=jax.ShapeDtypeStruct((tokens, width), jn...  2.36 us
  transfers between devices with their start and end apart: 13, of which 5 were waited for; matrix products, arithmetic and copies ran while one was open for 0% of the time, Pallas kernels for 36%

profile of v20, /device:TPU:0, one launch (start us, length us, event | category | flops | bytes accessed | tf_op | source)
XLA Modules:
  0.0 73.5 jit_solution(6870298715516825151)
XLA Ops:
  0.6 2.8 %pack.1 = (bf16[32,2304]{1,0:T(8,128)(2,1)}, bf16[32,2304]{1,0:T(8,128)(2,1)}, bf16[32,2304]{1,0:T(8,128)(2,1)}, bf16[32,2304]{1,0:T(8,128)(2,1)}, bf16[32,2304]...) custom-call(s32[1]{0:T(128)} %bitcast.1.me_ref, ...), custom_call_target="tpu_custom_call" | custom-call | flops 268435456 | bytes 2097152 | tf_op jit(solution)/shard_map/pack/pallas_call | solution.py:200
  3.5 3.0 %collective-permute-start = (bf16[32,2304]{1,0:T(8,128)(2,1)}, bf16[32,2304]{1,0:T(8,128)(2,1)S(1)}, u32[]{:S(2)}, u32[]{:S(2)}) collective-permute-start(bf16[32,2304]{1,0:T(8,128)(2,1)} %get-tuple-element.23), channel_id=1, source_target_pairs={{0,1},{1,0},{2,3},{3,2},{4,5},{5,4},{6,7},{7,6},{8,9},{9,8},{10,11... | collective-permute-start | bytes 442376 | tf_op jit(solution)/shard_map/ppermute | solution.py:606
  6.5 1.6 %collective-permute-start.1 = (bf16[32,2304]{1,0:T(8,128)(2,1)}, bf16[32,2304]{1,0:T(8,128)(2,1)}, u32[]{:S(2)}, u32[]{:S(2)}) collective-permute-start(bf16[32,2304]{1,0:T(8,128)(2,1)} %get-tuple-element.24), channel_id=1, source_target_pairs={{0,2},{1,3},{2,0},{3,1},{4,6},{5,7},{6,4},{7,5},{8,10},{9,11},{10,... | collective-permute-start | bytes 442376 | tf_op jit(solution)/shard_map/ppermute | solution.py:606
  8.1 2.6 %collective-permute-start.2 = (bf16[32,2304]{1,0:T(8,128)(2,1)}, bf16[32,2304]{1,0:T(8,128)(2,1)}, u32[]{:S(2)}, u32[]{:S(2)}) collective-permute-start(bf16[32,2304]{1,0:T(8,128)(2,1)} %get-tuple-element.25), channel_id=1, source_target_pairs={{0,4},{1,5},{2,6},{3,7},{4,0},{5,1},{6,2},{7,3},{8,12},{9,13},{10,... | collective-permute-start | bytes 442376 | tf_op jit(solution)/shard_map/ppermute | solution.py:606
  10.6 0.3 collective-permute-start.3
  11.0 2.5 %collective-permute-start.4 = (bf16[32,2304]{1,0:T(8,128)(2,1)}, bf16[32,2304]{1,0:T(8,128)(2,1)}, u32[]{:S(2)}, u32[]{:S(2)}) collective-permute-start(bf16[32,2304]{1,0:T(8,128)(2,1)} %get-tuple-element.27), channel_id=1, source_target_pairs={{0,6},{1,7},{2,4},{3,5},{4,2},{5,3},{6,0},{7,1},{8,14},{9,15},{10,... | collective-permute-start | bytes 442376 | tf_op jit(solution)/shard_map/ppermute | solution.py:606
  13.4 2.3 %collective-permute-start.5 = (bf16[32,2304]{1,0:T(8,128)(2,1)}, bf16[32,2304]{1,0:T(8,128)(2,1)}, u32[]{:S(2)}, u32[]{:S(2)}) collective-permute-start(bf16[32,2304]{1,0:T(8,128)(2,1)} %get-tuple-element.28), channel_id=1, source_target_pairs={{0,7},{1,6},{2,5},{3,4},{4,3},{5,2},{6,1},{7,0},{8,15},{9,14},{10,... | collective-permute-start | bytes 442376 | tf_op jit(solution)/shard_map/ppermute | solution.py:606
  15.7 0.0 collective-permute-done.1.refs_2_
  15.7 1.8 %join.2 = bf16[3,32,2304]{2,1,0:T(8,128)(2,1)} custom-call(bf16[32,2304]{1,0:T(8,128)(2,1)} %get-tuple-element.22.refs_0_, bf16[32,2304]{1,0:T(8,128)(2,1)} %copy-done, bf16[32,2304]{1,0:T(8,128)(2,1)} %collective-permute-done.1.refs_2_), custom_call_target="tpu_custom_call" | custom-call | bytes 884736 | tf_op jit(solution)/shard_map/join/pallas_call | solution.py:231
  17.5 10.9 %collective-permute-done.2.refs_3_.refs_0_ = bf16[32,2304]{1,0:T(8,128)(2,1)} collective-permute-done((bf16[32,2304]{1,0:T(8,128)(2,1)}, bf16[32,2304]{1,0:T(8,128)(2,1)}, u32[]{:S(2)}, u32[]{:S(2)}) %collective-permute-start.2) | collective-permute-done | bytes 147488 | tf_op jit(solution)/shard_map/ppermute | solution.py:606
  28.4 1.5 %collective-permute-start.7 = (bf16[3,32,2304]{2,1,0:T(8,128)(2,1)}, bf16[3,32,2304]{2,1,0:T(8,128)(2,1)}, u32[]{:S(2)}, u32[]{:S(2)}) collective-permute-start(bf16[3,32,2304]{2,1,0:T(8,128)(2,1)} %join.2), channel_id=1, source_target_pairs={{0,16},{8,24},{16,0},{24,8},{1,17},{9,25},{17,1},{25,9},{2,18},{10... | collective-permute-start | bytes 1327112 | tf_op jit(solution)/shard_map/ppermute | solution.py:606
  29.9 1.0 %collective-permute-done.3.refs_4_.refs_1_ = bf16[32,2304]{1,0:T(8,128)(2,1)} collective-permute-done((bf16[32,2304]{1,0:T(8,128)(2,1)}, bf16[32,2304]{1,0:T(8,128)(2,1)}, u32[]{:S(2)}, u32[]{:S(2)}) %collective-permute-start.3) | collective-permute-done | bytes 147488 | tf_op jit(solution)/shard_map/ppermute | solution.py:606
  30.9 0.0 collective-permute-done.6.refs_7_.refs_4_
  31.0 1.9 %join.3 = bf16[5,32,2304]{2,1,0:T(8,128)(2,1)} custom-call(bf16[32,2304]{1,0:T(8,128)(2,1)} %collective-permute-done.2.refs_3_.refs_0_, bf16[32,2304]{1,0:T(8,128)(2,1)} %collective-permute-done.3.refs_4_.refs_1_, bf16[32,2304]{1,0:T(8,128)(2,1)} %collective-permute-done.4.refs_5_.refs_2_, bf16[32,2304]{1,0:T(8,128)(2,1)} %collective-permute-done.5.refs_6_.refs_3_, ...), custom_call_target="tpu_custom_call" | custom-call | flops 11324620800 | bytes 1474560 | tf_op jit(solution)/shard_map/join/pallas_call | solution.py:231
  32.9 1.6 %collective-permute-start.10 = (bf16[5,32,2304]{2,1,0:T(8,128)(2,1)}, bf16[5,32,2304]{2,1,0:T(8,128)(2,1)}, u32[]{:S(2)}, u32[]{:S(2)}) collective-permute-start(bf16[5,32,2304]{2,1,0:T(8,128)(2,1)} %join.3), channel_id=1, source_target_pairs={{0,16},{8,24},{16,0},{24,8},{1,17},{9,25},{17,1},{25,9},{2,18},{10... | collective-permute-start | bytes 2211848 | tf_op jit(solution)/shard_map/ppermute | solution.py:606
  34.5 5.0 %collective-permute-done.7.refs_2_ = bf16[3,32,2304]{2,1,0:T(8,128)(2,1)} collective-permute-done((bf16[3,32,2304]{2,1,0:T(8,128)(2,1)}, bf16[3,32,2304]{2,1,0:T(8,128)(2,1)}, u32[]{:S(2)}, u32[]{:S(2)}) %collective-permute-start.7) | collective-permute-done | bytes 442400 | tf_op jit(solution)/shard_map/ppermute | solution.py:606
  39.5 10.0 %back.1 = (bf16[8,16,2304]{2,1,0:T(8,128)(2,1)}, bf16[144,3328]{1,0:T(8,128)(2,1)}, bf16[144,3328]{1,0:T(8,128)(2,1)}) custom-call(s32[1]{0:T(128)} %bitcast.1.me_ref, s32[1]{0:T(128)} %bitcast.2.part_ref, bf16[32,2304]{1,0:T(8,128)(2,1)} %get-tuple-element.22.refs_0_, bf16[32,2304]{1,0:T(8,128)(2,1)} %copy-done, ...), custom_call_target="tpu_custom_call" | custom-call | flops 11324620800 | bytes 1179648 | tf_op jit(solution)/shard_map/back/pallas_call | solution.py:436
  49.5 4.5 %all-to-all-start = ((bf16[8,16,2304]{2,1,0:T(8,128)(2,1)}), bf16[8,16,2304]{2,1,0:T(8,128)(2,1)}, u32[]{:S(2)}, u32[]{:S(2)}) async-start(bf16[8,16,2304]{2,1,0:T(8,128)(2,1)} %get-tuple-element.31), calls=%async_computation | async-start | bytes 1179648 | tf_op jit(solution)/shard_map/all_to_all | solution.py:610
  54.0 0.5 collective-permute-start.9
  54.4 0.1 collective-permute-start.11
  54.5 2.4 %collective-permute-done.9.refs_1_ = bf16[144,3328]{1,0:T(8,128)(2,1)} collective-permute-done((bf16[144,3328]{1,0:T(8,128)(2,1)}, bf16[144,3328]{1,0:T(8,128)(2,1)}, u32[]{:S(2)}, u32[]{:S(2)}) %collective-permute-start.9) | collective-permute-done | bytes 958496 | tf_op jit(solution)/shard_map/ppermute | solution.py:606
  56.9 1.1 %collective-permute-done.11.refs_5_ = bf16[5,32,2304]{2,1,0:T(8,128)(2,1)} collective-permute-done((bf16[5,32,2304]{2,1,0:T(8,128)(2,1)}, bf16[5,32,2304]{2,1,0:T(8,128)(2,1)}, u32[]{:S(2)}, u32[]{:S(2)}) %collective-permute-start.11) | collective-permute-done | bytes 737312 | tf_op jit(solution)/shard_map/ppermute | solution.py:606
  58.0 13.0 %weight_grads.1 = (f32[512,768]{1,0:T(8,128)}, f32[512,768]{1,0:T(8,128)}, f32[768,512]{1,0:T(8,128)}) custom-call(s32[1]{0:T(128)} %bitcast.2.part_ref, bf16[144,3328]{1,0:T(8,128)(2,1)} %get-tuple-element.32.refs_0_, bf16[144,3328]{1,0:T(8,128)(2,1)} %collective-permute-done.9.refs_1_, bf16[3,32,2304]{2,1,0:T(8,128)(2,1)} %collective-permute-done.7.refs_2_, ...), custom_call_target="tpu_custom_call" | custom-call | bytes 1179648 | tf_op jit(solution)/shard_map/weight_grads/pallas_call | solution.py:565
  71.0 2.4 %merge.1 = bf16[128,2048]{1,0:T(8,128)(2,1)} custom-call(s32[1,128]{1,0:T(1,128)} %bitcast.5, bf16[8,16,2304]{2,1,0:T(8,128)(2,1)} %all-to-all-done.back_ref), custom_call_target="tpu_custom_call" | custom-call | flops 134217728 | bytes 1048576 | tf_op jit(solution)/shard_map/merge/pallas_call | solution.py:270
  (10 shorter events, 0.0 us)
Async XLA Ops:
  3.5 10.0 %collective-permute-start = (bf16[32,2304]{1,0:T(8,128)(2,1)}, bf16[32,2304]{1,0:T(8,128)(2,1)S(1)}, u32[]{:S(2)}, u32[]{:S(2)}) collective-permute-start(bf16[32,2304]{1,0:T(8,128)(2,1)} %get-tuple-element.23), channel_id=1, source_target_pairs={{0,1},{1,0},{2,3},{3,2},{4,5},{5,4},{6,7},{7,6},{8,9},{9,8},{10,11... | collective-permute-start | bytes 442376 | tf_op jit(solution)/shard_map/ppermute | solution.py:606
  6.5 9.2 %collective-permute-start.1 = (bf16[32,2304]{1,0:T(8,128)(2,1)}, bf16[32,2304]{1,0:T(8,128)(2,1)}, u32[]{:S(2)}, u32[]{:S(2)}) collective-permute-start(bf16[32,2304]{1,0:T(8,128)(2,1)} %get-tuple-element.24), channel_id=1, source_target_pairs={{0,2},{1,3},{2,0},{3,1},{4,6},{5,7},{6,4},{7,5},{8,10},{9,11},{10,... | collective-permute-start | bytes 442376 | tf_op jit(solution)/shard_map/ppermute | solution.py:606
  8.1 20.3 %collective-permute-start.2 = (bf16[32,2304]{1,0:T(8,128)(2,1)}, bf16[32,2304]{1,0:T(8,128)(2,1)}, u32[]{:S(2)}, u32[]{:S(2)}) collective-permute-start(bf16[32,2304]{1,0:T(8,128)(2,1)} %get-tuple-element.25), channel_id=1, source_target_pairs={{0,4},{1,5},{2,6},{3,7},{4,0},{5,1},{6,2},{7,3},{8,12},{9,13},{10,... | collective-permute-start | bytes 442376 | tf_op jit(solution)/shard_map/ppermute | solution.py:606
  10.6 20.3 %collective-permute-start.3 = (bf16[32,2304]{1,0:T(8,128)(2,1)}, bf16[32,2304]{1,0:T(8,128)(2,1)}, u32[]{:S(2)}, u32[]{:S(2)}) collective-permute-start(bf16[32,2304]{1,0:T(8,128)(2,1)} %get-tuple-element.26), channel_id=1, source_target_pairs={{0,5},{1,4},{2,7},{3,6},{4,1},{5,0},{6,3},{7,2},{8,13},{9,12},{10,... | collective-permute-start | bytes 442376 | tf_op jit(solution)/shard_map/ppermute | solution.py:606
  11.0 20.0 %collective-permute-start.4 = (bf16[32,2304]{1,0:T(8,128)(2,1)}, bf16[32,2304]{1,0:T(8,128)(2,1)}, u32[]{:S(2)}, u32[]{:S(2)}) collective-permute-start(bf16[32,2304]{1,0:T(8,128)(2,1)} %get-tuple-element.27), channel_id=1, source_target_pairs={{0,6},{1,7},{2,4},{3,5},{4,2},{5,3},{6,0},{7,1},{8,14},{9,15},{10,... | collective-permute-start | bytes 442376 | tf_op jit(solution)/shard_map/ppermute | solution.py:606
  13.4 2.3 %copy-start = (bf16[32,2304]{1,0:T(8,128)(2,1)}, bf16[32,2304]{1,0:T(8,128)(2,1)S(1)}, u32[]{:S(2)}) copy-start(bf16[32,2304]{1,0:T(8,128)(2,1)S(1)} %collective-permute-done.refs_1_) | copy-start | bytes 442372
  13.4 17.5 %collective-permute-start.5 = (bf16[32,2304]{1,0:T(8,128)(2,1)}, bf16[32,2304]{1,0:T(8,128)(2,1)}, u32[]{:S(2)}, u32[]{:S(2)}) collective-permute-start(bf16[32,2304]{1,0:T(8,128)(2,1)} %get-tuple-element.28), channel_id=1, source_target_pairs={{0,7},{1,6},{2,5},{3,4},{4,3},{5,2},{6,1},{7,0},{8,15},{9,14},{10,... | collective-permute-start | bytes 442376 | tf_op jit(solution)/shard_map/ppermute | solution.py:606
  15.7 15.2 %collective-permute-start.6 = (bf16[32,2304]{1,0:T(8,128)(2,1)}, bf16[32,2304]{1,0:T(8,128)(2,1)}, u32[]{:S(2)}, u32[]{:S(2)}) collective-permute-start(bf16[32,2304]{1,0:T(8,128)(2,1)} %get-tuple-element.29), channel_id=1, source_target_pairs={{0,3},{1,2},{2,1},{3,0},{4,7},{5,6},{6,5},{7,4},{8,11},{9,10},{10,... | collective-permute-start | bytes 442376 | tf_op jit(solution)/shard_map/ppermute | solution.py:606
  28.4 11.1 %collective-permute-start.7 = (bf16[3,32,2304]{2,1,0:T(8,128)(2,1)}, bf16[3,32,2304]{2,1,0:T(8,128)(2,1)}, u32[]{:S(2)}, u32[]{:S(2)}) collective-permute-start(bf16[3,32,2304]{2,1,0:T(8,128)(2,1)} %join.2), channel_id=1, source_target_pairs={{0,16},{8,24},{16,0},{24,8},{1,17},{9,25},{17,1},{25,9},{2,18},{10... | collective-permute-start | bytes 1327112 | tf_op jit(solution)/shard_map/ppermute | solution.py:606
  32.9 21.5 %collective-permute-start.10 = (bf16[5,32,2304]{2,1,0:T(8,128)(2,1)}, bf16[5,32,2304]{2,1,0:T(8,128)(2,1)}, u32[]{:S(2)}, u32[]{:S(2)}) collective-permute-start(bf16[5,32,2304]{2,1,0:T(8,128)(2,1)} %join.3), channel_id=1, source_target_pairs={{0,16},{8,24},{16,0},{24,8},{1,17},{9,25},{17,1},{25,9},{2,18},{10... | collective-permute-start | bytes 2211848 | tf_op jit(solution)/shard_map/ppermute | solution.py:606
  39.5 10.0 %collective-permute-start.8 = (bf16[3,32,2304]{2,1,0:T(8,128)(2,1)}, bf16[3,32,2304]{2,1,0:T(8,128)(2,1)}, u32[]{:S(2)}, u32[]{:S(2)}) collective-permute-start(bf16[3,32,2304]{2,1,0:T(8,128)(2,1)} %collective-permute-done.7.refs_2_), channel_id=1, source_target_pairs={{0,8},{8,0},{16,24},{24,16},{1,9},{9,1},{17,25},{25,17},{2,10},{10... | collective-permute-start | bytes 1327112 | tf_op jit(solution)/shard_map/ppermute | solution.py:606
  49.5 21.5 %all-to-all-start = ((bf16[8,16,2304]{2,1,0:T(8,128)(2,1)}), bf16[8,16,2304]{2,1,0:T(8,128)(2,1)}, u32[]{:S(2)}, u32[]{:S(2)}) async-start(bf16[8,16,2304]{2,1,0:T(8,128)(2,1)} %get-tuple-element.31), calls=%async_computation | async-start | bytes 1179648 | tf_op jit(solution)/shard_map/all_to_all | solution.py:610
  54.0 3.0 %collective-permute-start.9 = (bf16[144,3328]{1,0:T(8,128)(2,1)}, bf16[144,3328]{1,0:T(8,128)(2,1)}, u32[]{:S(2)}, u32[]{:S(2)}) collective-permute-start(bf16[144,3328]{1,0:T(8,128)(2,1)} %get-tuple-element.33), channel_id=1, source_target_pairs={{0,8},{8,0},{16,24},{24,16},{1,9},{9,1},{17,25},{25,17},{2,10},{10... | collective-permute-start | bytes 2875400 | tf_op jit(solution)/shard_map/ppermute | solution.py:606
  54.4 3.6 %collective-permute-start.11 = (bf16[5,32,2304]{2,1,0:T(8,128)(2,1)}, bf16[5,32,2304]{2,1,0:T(8,128)(2,1)}, u32[]{:S(2)}, u32[]{:S(2)}) collective-permute-start(bf16[5,32,2304]{2,1,0:T(8,128)(2,1)} %collective-permute-done.10.refs_3_), channel_id=1, source_target_pairs={{0,8},{8,0},{16,24},{24,16},{1,9},{9,1},{17,25},{25,17},{2,10},{10... | collective-permute-start | bytes 2211848 | tf_op jit(solution)/shard_map/ppermute | solution.py:606

commit v21 on v19

--- a/solution.py
+++ b/solution.py
@@ -160,14 +160,17 @@
 
 
 def pack(blocks, me, routes, gates, tokens, cotangent):
+    near = blocks // 2
     count, width = tokens.shape
     pieces, step = cut(width)
     sources = (routes, gates, tokens, cotangent)
     block_shape = (2 * ROWS, width + step)
 
     def kernel(me_ref, *refs):
-        outs, held = refs[4 : 4 + blocks], refs[4 + blocks : 8 + blocks]
-        staged, arrived, gone = refs[8 + blocks :]
+        outs, held = refs[4 : 5 + near], refs[5 + near : 9 + near]
+        staged, arrived, gone = refs[9 + near :]
+        targets = [outs[0].at[(me_ref[0] & (near - 1)) ^ at] for at in range(near)]
+        targets += outs[1:]
         pairs = list(zip(refs[:4], held))
         start(pairs, arrived)
         wait(pairs[:2], arrived)
@@ -192,16 +195,17 @@
                 part = slice(block * ROWS, (block + 1) * ROWS)
                 staged[block, here, :width] = rows[part]
                 staged[block, here, width:] = extra[part]
-            sent = [(staged.at[at, here], outs[at].at[here, :]) for at in range(blocks)]
+            sent = [(staged.at[at, here], targets[at].at[here, :]) for at in range(blocks)]
             leaving += sent
             start(leaving, gone, half * blocks)
         wait(leaving, gone)
 
     return pl.pallas_call(
         kernel,
-        out_shape=[jax.ShapeDtypeStruct(block_shape, jnp.bfloat16)] * blocks,
+        out_shape=[jax.ShapeDtypeStruct((near,) + block_shape, jnp.bfloat16)]
+        + [jax.ShapeDtypeStruct(block_shape, jnp.bfloat16)] * (blocks - near),
         in_specs=[pl.BlockSpec(memory_space=pltpu.SMEM)] + anywhere(4),
-        out_specs=anywhere(blocks),
+        out_specs=anywhere(1 + blocks - near),
         scratch_shapes=[pltpu.VMEM(source.shape, source.dtype) for source in sources]
         + [
             pltpu.VMEM((blocks,) + block_shape, jnp.bfloat16),
@@ -337,7 +341,8 @@
 
 
 def back(tile, share, me, part, group, gate_proj, up_proj, down_proj):
-    blocks = len(group)
+    items, near = len(group), group[0].shape[0]
+    blocks = near + items - 1
     width, hid = gate_proj.shape
     slots = blocks * MOST
     pieces, step = cut(width)
@@ -349,7 +354,7 @@
 
     def kernel(me_ref, part_ref, *refs):
         refs = list(refs)
-        group_refs = [refs.pop(0) for _ in range(blocks)]
+        group_refs = [refs.pop(0) for _ in range(items)]
         gate_ref, up_ref, down_ref, out, kept, handed = [refs.pop(0) for _ in range(6)]
         x_held, dy_held, rows, scaled, factors, cuts = [refs.pop(0) for _ in range(6)]
         staged, gate, up, down = [refs.pop(0) for _ in range(4)]
@@ -375,6 +380,8 @@
                 staged.at[:, :, columns], out.at[:, :, columns], gone.at[index]
             )
 
+        senders = [me_ref[0] - (me_ref[0] & (near - 1)) + at for at in range(near)]
+        senders += [me_ref[0] ^ at for at in range(near, blocks)]
         first, behind = slice(0, 3 * hid), slice(3 * hid, given)
         leaving = [(factors, kept.at[:, first]), (cuts.at[0], kept.at[:, behind])]
         leaving += [(factors, handed.at[:, first]), (cuts.at[1], handed.at[:, behind])]
@@ -417,13 +424,13 @@
             done += dot(factors[:, 2 * hid :], up[here, :], BY_WIDTH)
             done = done.astype(jnp.bfloat16)
             for block in range(blocks):
-                staged[me_ref[0] ^ block, :, here] = done[block * ROWS : (block + 1) * ROWS]
+                staged[senders[block], :, here] = done[block * ROWS : (block + 1) * ROWS]
             leave(at).start()
             extras += [done[blocks * ROWS :, :step], done[blocks * ROWS :, step:]]
         tail = dot(spill_picks(blocks, pieces), jnp.concatenate(extras, 0), BY_ROWS)
         tail = tail.astype(jnp.bfloat16)
         for block in range(blocks):
-            staged[me_ref[0] ^ block, :, width:] = tail[block * ROWS : (block + 1) * ROWS]
+            staged[senders[block], :, width:] = tail[block * ROWS : (block + 1) * ROWS]
         last = pltpu.make_async_copy(
             staged.at[:, :, width:], out.at[:, :, width:], gone.at[chunks]
         )
@@ -440,7 +447,7 @@
             jax.ShapeDtypeStruct((slots, given), jnp.bfloat16),
             jax.ShapeDtypeStruct((slots, given), jnp.bfloat16),
         ],
-        in_specs=[pl.BlockSpec(memory_space=pltpu.SMEM)] * 2 + anywhere(blocks + 3),
+        in_specs=[pl.BlockSpec(memory_space=pltpu.SMEM)] * 2 + anywhere(items + 3),
         out_specs=anywhere(3),
         scratch_shapes=[
             pltpu.VMEM(shape, jnp.bfloat16),
@@ -453,8 +460,8 @@
             pltpu.VMEM((width, hid), jnp.bfloat16),
             pltpu.VMEM((width, hid), jnp.bfloat16),
             pltpu.VMEM((tiles, tile, width), jnp.bfloat16),
-            pltpu.SemaphoreType.DMA((blocks,)),
-            pltpu.SemaphoreType.DMA((blocks,)),
+            pltpu.SemaphoreType.DMA((items,)),
+            pltpu.SemaphoreType.DMA((items,)),
             pltpu.SemaphoreType.DMA((tiles,)),
             pltpu.SemaphoreType.DMA((tiles,)),
             pltpu.SemaphoreType.DMA((tiles,)),
@@ -606,8 +613,10 @@
     return lax.ppermute(value, axis, [(at, at ^ distance) for at in range(size)])
 
 
-def exchange(blocks):
-    return lax.all_to_all(blocks, "expert", split_axis=0, concat_axis=0, tiled=True)
+def exchange(blocks, groups=None):
+    return lax.all_to_all(
+        blocks, "expert", split_axis=0, concat_axis=0, tiled=True, axis_index_groups=groups
+    )
 
 
 def after(value, *earlier):
@@ -622,18 +631,19 @@
     routes = routes.reshape(1, -1)
     gates = expert_gates.reshape(1, -1)
     weights = (gate_proj, up_proj, down_proj)
-    received = list(pack(blocks, me, routes, gates, tokens, cotangent))
-    for distance in reversed(range(1, blocks)):
-        received[distance] = swap(received[distance], "expert", distance)
+    first, *received = pack(blocks, me, routes, gates, tokens, cotangent)
     half = blocks // 2
-    far = swap(join(received[:half]), "dp", 2)
+    groups = [list(range(at, at + half)) for at in range(0, blocks, half)]
+    first = exchange(first, groups)
+    received = [swap(block, "expert", half + at) for at, block in enumerate(received)]
+    far = swap(first, "dp", 2)
     work = 50 * blocks * MOST * gate_proj.size
-    far_half = swap(join(received[half:], work), "dp", 2)
-    sent, kept, handed = back(tile, share, me, part, received, *weights)
+    far_rest = swap(join(received, work), "dp", 2)
+    sent, kept, handed = back(tile, share, me, part, [first, *received], *weights)
     last = swap(far, "dp", 1)
     sent, last = lax.optimization_barrier((sent, last))
     returned = exchange(sent)
-    far = [far, after(far_half, sent)]
+    far = [far, after(far_rest, sent)]
     last = [last, swap(far[1], "dp", 1)]
     known = [kept, swap(handed, "dp", 1)]
     grads = weight_grads(tile, share, part, known, [far, last], *weights)

time: 75.2 us -> 76.7 us (1.020)
  waiting for transfers between devices: 18 us -> 21.3 us
  Pallas kernels: 31.8 us -> 29.8 us
    all_to_all x1 -> x2, waiting for transfers between devices: 0.72 us -> 7.71 us  [exchange(): lax.all_to_all(blocks, 'expert', split_axis=0, concat_axis=0, tiled=True,...]
    all_to_all x1 -> x2, starting transfers between devices: 6.92 us -> 12.1 us  [exchange(): lax.all_to_all(blocks, 'expert', split_axis=0, concat_axis=0, tiled=True,...]
    ppermute x12 -> x9, starting transfers between devices: 17.2 us -> 12.1 us  [swap(): lax.ppermute(value, axis, [(at, at ^ distance) for at in range(size)])]
    ppermute x12 -> x9, waiting for transfers between devices: 17.3 us -> 13.6 us  [swap(): lax.ppermute(value, axis, [(at, at ^ distance) for at in range(size)])]
    pallas_call x2 -> x1, Pallas kernels: 3.7 us -> 1.85 us  [join(): pl.pallas_call(kernel, out_shape=jax.ShapeDtypeStruct(shape, jnp.bfloat16...]
  transfers between devices with their start and end apart: 13 -> 11, of which waited for: 7 -> 7; matrix products, arithmetic and copies ran while one was open for 0% -> 0% of each run, Pallas kernels for 36% -> 32%
where the time goes in v21:
time: 76.7 us; the launch traced here: 76.3 us
  Pallas kernels  29.8 us (39%)
  starting transfers between devices  24.3 us (32%)
  waiting for transfers between devices  21.3 us (28%)
  between operations  0.85 us (1%)
    ppermute x9, waiting for transfers between devices, swap(): lax.ppermute(value, axis, [(at, at ^ distance) for at in range(size)])  13.6 us
    pallas_call x1, Pallas kernels, weight_grads(): pl.pallas_call(kernel, out_shape=[jax.ShapeDtypeStruct((share, hid), jnp....  13 us
    all_to_all x2, starting transfers between devices, exchange(): lax.all_to_all(blocks, 'expert', split_axis=0, concat_axis=0, tiled=True,...  12.1 us
    ppermute x9, starting transfers between devices, swap(): lax.ppermute(value, axis, [(at, at ^ distance) for at in range(size)])  12.1 us
    pallas_call x1, Pallas kernels, back(): pl.pallas_call(kernel, out_shape=[jax.ShapeDtypeStruct(shape, jnp.bfloat1...  9.85 us
    all_to_all x2, waiting for transfers between devices, exchange(): lax.all_to_all(blocks, 'expert', split_axis=0, concat_axis=0, tiled=True,...  7.71 us
    pallas_call x1, Pallas kernels, pack(): pl.pallas_call(kernel, out_shape=[jax.ShapeDtypeStruct((near,) + block_sh...  2.83 us
    pallas_call x1, Pallas kernels, merge(): pl.pallas_call(kernel, out_shape=jax.ShapeDtypeStruct((tokens, width), jn...  2.35 us
  transfers between devices with their start and end apart: 11, of which 7 were waited for; matrix products, arithmetic and copies ran while one was open for 0% of the time, Pallas kernels for 32%

profile of v21, /device:TPU:0, one launch (start us, length us, event | category | flops | bytes accessed | tf_op | source)
XLA Modules:
  0.0 76.3 jit_solution(3610772737414823002)
XLA Ops:
  0.6 2.8 %pack.1 = (bf16[4,32,2304]{2,1,0:T(8,128)(2,1)}, bf16[32,2304]{1,0:T(8,128)(2,1)}, bf16[32,2304]{1,0:T(8,128)(2,1)}, bf16[32,2304]{1,0:T(8,128)(2,1)}, bf16[32,2304]{1,0:T(8,128)(2,1)}) custom-call(s32[1]{0:T(128)} %bitcast.1.me_ref, s32[1,128]{1,0:T(1,128)} %bitcast.4, f32[1,128]{1,0:T(1,128)} %bitcast.6, bf16[128,2048]{1,0:T(8,128)(2,1)} %refs_2_.1, ...), custom_call_target="tpu_custom_call" | custom-call | flops 268435456 | bytes 2097152 | tf_op jit(solution)/shard_map/pack/pallas_call | solution.py:203
  3.5 5.2 %all-to-all-start = ((bf16[4,32,2304]{2,1,0:T(8,128)(2,1)}), bf16[4,32,2304]{2,1,0:T(8,128)(2,1)}, u32[]{:S(2)}, u32[]{:S(2)}) async-start(bf16[4,32,2304]{2,1,0:T(8,128)(2,1)} %get-tuple-element.19), calls=%async_computation | async-start | bytes 1179648 | tf_op jit(solution)/shard_map/all_to_all | solution.py:617
  8.7 3.0 %collective-permute-start = (bf16[32,2304]{1,0:T(8,128)(2,1)}, bf16[32,2304]{1,0:T(8,128)(2,1)S(1)}, u32[]{:S(2)}, u32[]{:S(2)}) collective-permute-start(bf16[32,2304]{1,0:T(8,128)(2,1)} %get-tuple-element.20), channel_id=1, source_target_pairs={{0,4},{1,5},{2,6},{3,7},{4,0},{5,1},{6,2},{7,3},{8,12},{9,13},{10,... | collective-permute-start | bytes 442376 | tf_op jit(solution)/shard_map/ppermute | solution.py:613
  11.7 1.3 %collective-permute-start.1 = (bf16[32,2304]{1,0:T(8,128)(2,1)}, bf16[32,2304]{1,0:T(8,128)(2,1)}, u32[]{:S(2)}, u32[]{:S(2)}) collective-permute-start(bf16[32,2304]{1,0:T(8,128)(2,1)} %get-tuple-element.21), channel_id=1, source_target_pairs={{0,5},{1,4},{2,7},{3,6},{4,1},{5,0},{6,3},{7,2},{8,13},{9,12},{10,... | collective-permute-start | bytes 442376 | tf_op jit(solution)/shard_map/ppermute | solution.py:613
  13.1 3.8 %collective-permute-start.2 = (bf16[32,2304]{1,0:T(8,128)(2,1)}, bf16[32,2304]{1,0:T(8,128)(2,1)}, u32[]{:S(2)}, u32[]{:S(2)}) collective-permute-start(bf16[32,2304]{1,0:T(8,128)(2,1)} %get-tuple-element.22), channel_id=1, source_target_pairs={{0,6},{1,7},{2,4},{3,5},{4,2},{5,3},{6,0},{7,1},{8,14},{9,15},{10,... | collective-permute-start | bytes 442376 | tf_op jit(solution)/shard_map/ppermute | solution.py:613
  16.9 7.0 %all-to-all-done.refs_0_ = bf16[4,32,2304]{2,1,0:T(8,128)(2,1)} async-done(((bf16[4,32,2304]{2,1,0:T(8,128)(2,1)}), bf16[4,32,2304]{2,1,0:T(8,128)(2,1)}, u32[]{:S(2)}, u32[]{:S(2)}) %all-to-all-start) | async-done | bytes 589856 | tf_op jit(solution)/shard_map/all_to_all | solution.py:617
  23.9 1.7 %collective-permute-start.4 = (bf16[4,32,2304]{2,1,0:T(8,128)(2,1)}, bf16[4,32,2304]{2,1,0:T(8,128)(2,1)}, u32[]{:S(2)}, u32[]{:S(2)}) collective-permute-start(bf16[4,32,2304]{2,1,0:T(8,128)(2,1)} %all-to-all-done.refs_0_), channel_id=1, source_target_pairs={{0,16},{8,24},{16,0},{24,8},{1,17},{9,25},{17,1},{25,9},{2,18},{10... | collective-permute-start | bytes 1769480 | tf_op jit(solution)/shard_map/ppermute | solution.py:613
  25.6 0.0 collective-permute-done.refs_1_.refs_0_
  25.6 0.0 collective-permute-done.1.refs_2_.refs_1_
  25.6 5.3 %collective-permute-done.2.refs_3_.refs_2_ = bf16[32,2304]{1,0:T(8,128)(2,1)} collective-permute-done((bf16[32,2304]{1,0:T(8,128)(2,1)}, bf16[32,2304]{1,0:T(8,128)(2,1)}, u32[]{:S(2)}, u32[]{:S(2)}) %collective-permute-start.2) | collective-permute-done | bytes 147488 | tf_op jit(solution)/shard_map/ppermute | solution.py:613
  30.9 3.0 %collective-permute-done.3.refs_4_.refs_3_ = bf16[32,2304]{1,0:T(8,128)(2,1)} collective-permute-done((bf16[32,2304]{1,0:T(8,128)(2,1)}, bf16[32,2304]{1,0:T(8,128)(2,1)}, u32[]{:S(2)}, u32[]{:S(2)}) %collective-permute-start.3) | collective-permute-done | bytes 147488 | tf_op jit(solution)/shard_map/ppermute | solution.py:613
  33.8 1.9 %join.1 = bf16[4,32,2304]{2,1,0:T(8,128)(2,1)} custom-call(bf16[32,2304]{1,0:T(8,128)(2,1)} %copy-done, bf16[32,2304]{1,0:T(8,128)(2,1)} %collective-permute-done.1.refs_2_.refs_1_, bf16[32,2304]{1,0:T(8,128)(2,1)} %collective-permute-done.2.refs_3_.refs_2_, bf16[32,2304]{1,0:T(8,128)(2,1)} %collective-permute-done.3.refs_4_.refs_3_), custom_call_target="tpu_custom_call" | custom-call | flops 11324620800 | bytes 1179648 | tf_op jit(solution)/shard_map/join/pallas_call | solution.py:235
  35.7 1.7 %collective-permute-start.7 = (bf16[4,32,2304]{2,1,0:T(8,128)(2,1)}, bf16[4,32,2304]{2,1,0:T(8,128)(2,1)}, u32[]{:S(2)}, u32[]{:S(2)}) collective-permute-start(bf16[4,32,2304]{2,1,0:T(8,128)(2,1)} %join.1), channel_id=1, source_target_pairs={{0,16},{8,24},{16,0},{24,8},{1,17},{9,25},{17,1},{25,9},{2,18},{10... | collective-permute-start | bytes 1769480 | tf_op jit(solution)/shard_map/ppermute | solution.py:613
  37.4 2.2 %collective-permute-done.4.refs_2_ = bf16[4,32,2304]{2,1,0:T(8,128)(2,1)} collective-permute-done((bf16[4,32,2304]{2,1,0:T(8,128)(2,1)}, bf16[4,32,2304]{2,1,0:T(8,128)(2,1)}, u32[]{:S(2)}, u32[]{:S(2)}) %collective-permute-start.4) | collective-permute-done | bytes 589856 | tf_op jit(solution)/shard_map/ppermute | solution.py:613
  39.6 9.9 %back.1 = (bf16[8,16,2304]{2,1,0:T(8,128)(2,1)}, bf16[144,3328]{1,0:T(8,128)(2,1)}, bf16[144,3328]{1,0:T(8,128)(2,1)}) custom-call(s32[1]{0:T(128)} %bitcast.1.me_ref, s32[1]{0:T(128)} %bitcast.2.part_ref, bf16[4,32,2304]{2,1,0:T(8,128)(2,1)} %all-to-all-done.refs_0_, bf16[32,2304]{1,0:T(8,128)(2,1)} %copy-done, ...), custom_call_target="tpu_custom_call" | custom-call | flops 11324620800 | bytes 1179648 | tf_op jit(solution)/shard_map/back/pallas_call | solution.py:443
  49.5 0.0 collective-permute-done.5.refs_4_
  49.5 6.9 %all-to-all-start.1 = ((bf16[8,16,2304]{2,1,0:T(8,128)(2,1)}), bf16[8,16,2304]{2,1,0:T(8,128)(2,1)}, u32[]{:S(2)}, u32[]{:S(2)}) async-start(bf16[8,16,2304]{2,1,0:T(8,128)(2,1)} %get-tuple-element.25), calls=%async_computation.1 | async-start | bytes 1179648 | tf_op jit(solution)/shard_map/all_to_all | solution.py:617
  56.4 0.2 collective-permute-start.6
  56.6 0.3 collective-permute-start.8
  56.9 2.4 %collective-permute-done.6.refs_1_ = bf16[144,3328]{1,0:T(8,128)(2,1)} collective-permute-done((bf16[144,3328]{1,0:T(8,128)(2,1)}, bf16[144,3328]{1,0:T(8,128)(2,1)}, u32[]{:S(2)}, u32[]{:S(2)}) %collective-permute-start.6) | collective-permute-done | bytes 958496 | tf_op jit(solution)/shard_map/ppermute | solution.py:613
  59.3 0.8 %collective-permute-done.8.refs_5_ = bf16[4,32,2304]{2,1,0:T(8,128)(2,1)} collective-permute-done((bf16[4,32,2304]{2,1,0:T(8,128)(2,1)}, bf16[4,32,2304]{2,1,0:T(8,128)(2,1)}, u32[]{:S(2)}, u32[]{:S(2)}) %collective-permute-start.8) | collective-permute-done | bytes 589856 | tf_op jit(solution)/shard_map/ppermute | solution.py:613
  60.1 13.0 %weight_grads.1 = (f32[512,768]{1,0:T(8,128)}, f32[512,768]{1,0:T(8,128)}, f32[768,512]{1,0:T(8,128)}) custom-call(s32[1]{0:T(128)} %bitcast.2.part_ref, bf16[144,3328]{1,0:T(8,128)(2,1)} %get-tuple-element.26.refs_0_, bf16[144,3328]{1,0:T(8,128)(2,1)} %collective-permute-done.6.refs_1_, bf16[4,32,2304]{2,1,0:T(8,128)(2,1)} %collective-permute-done.4.refs_2_, ...), custom_call_target="tpu_custom_call" | custom-call | bytes 1179648 | tf_op jit(solution)/shard_map/weight_grads/pallas_call | solution.py:572
  73.1 0.7 all-to-all-done.1.back_ref
  73.8 2.4 %merge.1 = bf16[128,2048]{1,0:T(8,128)(2,1)} custom-call(s32[1,128]{1,0:T(1,128)} %bitcast.5, bf16[8,16,2304]{2,1,0:T(8,128)(2,1)} %all-to-all-done.1.back_ref), custom_call_target="tpu_custom_call" | custom-call | flops 134217728 | bytes 1048576 | tf_op jit(solution)/shard_map/merge/pallas_call | solution.py:274
  (5 shorter events, 0.0 us)
Async XLA Ops:
  3.5 20.4 %all-to-all-start = ((bf16[4,32,2304]{2,1,0:T(8,128)(2,1)}), bf16[4,32,2304]{2,1,0:T(8,128)(2,1)}, u32[]{:S(2)}, u32[]{:S(2)}) async-start(bf16[4,32,2304]{2,1,0:T(8,128)(2,1)} %get-tuple-element.19), calls=%async_computation | async-start | bytes 1179648 | tf_op jit(solution)/shard_map/all_to_all | solution.py:617
  8.7 16.9 %collective-permute-start = (bf16[32,2304]{1,0:T(8,128)(2,1)}, bf16[32,2304]{1,0:T(8,128)(2,1)S(1)}, u32[]{:S(2)}, u32[]{:S(2)}) collective-permute-start(bf16[32,2304]{1,0:T(8,128)(2,1)} %get-tuple-element.20), channel_id=1, source_target_pairs={{0,4},{1,5},{2,6},{3,7},{4,0},{5,1},{6,2},{7,3},{8,12},{9,13},{10,... | collective-permute-start | bytes 442376 | tf_op jit(solution)/shard_map/ppermute | solution.py:613
  11.7 13.8 %collective-permute-start.1 = (bf16[32,2304]{1,0:T(8,128)(2,1)}, bf16[32,2304]{1,0:T(8,128)(2,1)}, u32[]{:S(2)}, u32[]{:S(2)}) collective-permute-start(bf16[32,2304]{1,0:T(8,128)(2,1)} %get-tuple-element.21), channel_id=1, source_target_pairs={{0,5},{1,4},{2,7},{3,6},{4,1},{5,0},{6,3},{7,2},{8,13},{9,12},{10,... | collective-permute-start | bytes 442376 | tf_op jit(solution)/shard_map/ppermute | solution.py:613
  13.1 17.8 %collective-permute-start.2 = (bf16[32,2304]{1,0:T(8,128)(2,1)}, bf16[32,2304]{1,0:T(8,128)(2,1)}, u32[]{:S(2)}, u32[]{:S(2)}) collective-permute-start(bf16[32,2304]{1,0:T(8,128)(2,1)} %get-tuple-element.22), channel_id=1, source_target_pairs={{0,6},{1,7},{2,4},{3,5},{4,2},{5,3},{6,0},{7,1},{8,14},{9,15},{10,... | collective-permute-start | bytes 442376 | tf_op jit(solution)/shard_map/ppermute | solution.py:613
  16.9 16.9 %collective-permute-start.3 = (bf16[32,2304]{1,0:T(8,128)(2,1)}, bf16[32,2304]{1,0:T(8,128)(2,1)}, u32[]{:S(2)}, u32[]{:S(2)}) collective-permute-start(bf16[32,2304]{1,0:T(8,128)(2,1)} %get-tuple-element.23), channel_id=1, source_target_pairs={{0,7},{1,6},{2,5},{3,4},{4,3},{5,2},{6,1},{7,0},{8,15},{9,14},{10,... | collective-permute-start | bytes 442376 | tf_op jit(solution)/shard_map/ppermute | solution.py:613
  23.9 15.7 %collective-permute-start.4 = (bf16[4,32,2304]{2,1,0:T(8,128)(2,1)}, bf16[4,32,2304]{2,1,0:T(8,128)(2,1)}, u32[]{:S(2)}, u32[]{:S(2)}) collective-permute-start(bf16[4,32,2304]{2,1,0:T(8,128)(2,1)} %all-to-all-done.refs_0_), channel_id=1, source_target_pairs={{0,16},{8,24},{16,0},{24,8},{1,17},{9,25},{17,1},{25,9},{2,18},{10... | collective-permute-start | bytes 1769480 | tf_op jit(solution)/shard_map/ppermute | solution.py:613
  25.6 8.2 %copy-start = (bf16[32,2304]{1,0:T(8,128)(2,1)}, bf16[32,2304]{1,0:T(8,128)(2,1)S(1)}, u32[]{:S(2)}) copy-start(bf16[32,2304]{1,0:T(8,128)(2,1)S(1)} %collective-permute-done.refs_1_.refs_0_) | copy-start | bytes 442372
  35.7 20.9 %collective-permute-start.7 = (bf16[4,32,2304]{2,1,0:T(8,128)(2,1)}, bf16[4,32,2304]{2,1,0:T(8,128)(2,1)}, u32[]{:S(2)}, u32[]{:S(2)}) collective-permute-start(bf16[4,32,2304]{2,1,0:T(8,128)(2,1)} %join.1), channel_id=1, source_target_pairs={{0,16},{8,24},{16,0},{24,8},{1,17},{9,25},{17,1},{25,9},{2,18},{10... | collective-permute-start | bytes 1769480 | tf_op jit(solution)/shard_map/ppermute | solution.py:613
  39.6 9.9 %collective-permute-start.5 = (bf16[4,32,2304]{2,1,0:T(8,128)(2,1)}, bf16[4,32,2304]{2,1,0:T(8,128)(2,1)}, u32[]{:S(2)}, u32[]{:S(2)}) collective-permute-start(bf16[4,32,2304]{2,1,0:T(8,128)(2,1)} %collective-permute-done.4.refs_2_), channel_id=1, source_target_pairs={{0,8},{8,0},{16,24},{24,16},{1,9},{9,1},{17,25},{25,17},{2,10},{10... | collective-permute-start | bytes 1769480 | tf_op jit(solution)/shard_map/ppermute | solution.py:613
  49.5 24.3 %all-to-all-start.1 = ((bf16[8,16,2304]{2,1,0:T(8,128)(2,1)}), bf16[8,16,2304]{2,1,0:T(8,128)(2,1)}, u32[]{:S(2)}, u32[]{:S(2)}) async-start(bf16[8,16,2304]{2,1,0:T(8,128)(2,1)} %get-tuple-element.25), calls=%async_computation.1 | async-start | bytes 1179648 | tf_op jit(solution)/shard_map/all_to_all | solution.py:617
  56.4 2.9 %collective-permute-start.6 = (bf16[144,3328]{1,0:T(8,128)(2,1)}, bf16[144,3328]{1,0:T(8,128)(2,1)}, u32[]{:S(2)}, u32[]{:S(2)}) collective-permute-start(bf16[144,3328]{1,0:T(8,128)(2,1)} %get-tuple-element.27), channel_id=1, source_target_pairs={{0,8},{8,0},{16,24},{24,16},{1,9},{9,1},{17,25},{25,17},{2,10},{10... | collective-permute-start | bytes 2875400 | tf_op jit(solution)/shard_map/ppermute | solution.py:613
  56.6 3.5 %collective-permute-start.8 = (bf16[4,32,2304]{2,1,0:T(8,128)(2,1)}, bf16[4,32,2304]{2,1,0:T(8,128)(2,1)}, u32[]{:S(2)}, u32[]{:S(2)}) collective-permute-start(bf16[4,32,2304]{2,1,0:T(8,128)(2,1)} %collective-permute-done.7.refs_3_), channel_id=1, source_target_pairs={{0,8},{8,0},{16,24},{24,16},{1,9},{9,1},{17,25},{25,17},{2,10},{10... | collective-permute-start | bytes 1769480 | tf_op jit(solution)/shard_map/ppermute | solution.py:613

commit v22 on v20

--- a/solution.py
+++ b/solution.py
@@ -625,7 +625,7 @@
     received = list(pack(blocks, me, routes, gates, tokens, cotangent))
     for distance in reversed(range(1, blocks)):
         received[distance] = swap(received[distance], "expert", distance)
-    order = [0, 1, 2, 4, 5, 6, 7, 3]
+    order = [0, 1, 2, 6, 7, 4, 5, 3]
     early = 3
     received = [received[index] for index in order]
     far = swap(join(received[:early]), "dp", 2)

time: 73.8 us -> 75.6 us (1.024)
  waiting for transfers between devices: 20.4 us -> 22.1 us
    ppermute x12, waiting for transfers between devices: 20.4 us -> 22.1 us  [swap(): lax.ppermute(value, axis, [(at, at ^ distance) for at in range(size)])]
  transfers between devices with their start and end apart: 13 -> 13, of which waited for: 5 -> 7; matrix products, arithmetic and copies ran while one was open for 0% -> 0% of each run, Pallas kernels for 36% -> 35%
where the time goes in v22:
time: 75.6 us; the launch traced here: 75.3 us
  Pallas kernels  31.9 us (42%)
  waiting for transfers between devices  22.1 us (29%)
  starting transfers between devices  20.5 us (27%)
  between operations  0.87 us (1%)
    ppermute x12, waiting for transfers between devices, swap(): lax.ppermute(value, axis, [(at, at ^ distance) for at in range(size)])  22.1 us
    ppermute x12, starting transfers between devices, swap(): lax.ppermute(value, axis, [(at, at ^ distance) for at in range(size)])  16.1 us
    pallas_call x1, Pallas kernels, weight_grads(): pl.pallas_call(kernel, out_shape=[jax.ShapeDtypeStruct((share, hid), jnp....  13 us
    pallas_call x1, Pallas kernels, back(): pl.pallas_call(kernel, out_shape=[jax.ShapeDtypeStruct(shape, jnp.bfloat1...  9.94 us
    all_to_all x1, starting transfers between devices, exchange(): lax.all_to_all(blocks, 'expert', split_axis=0, concat_axis=0, tiled=True)  4.39 us
    pallas_call x2, Pallas kernels, join(): pl.pallas_call(kernel, out_shape=jax.ShapeDtypeStruct(shape, jnp.bfloat16...  3.71 us
    pallas_call x1, Pallas kernels, pack(): pl.pallas_call(kernel, out_shape=[jax.ShapeDtypeStruct(block_shape, jnp.b...  2.84 us
    pallas_call x1, Pallas kernels, merge(): pl.pallas_call(kernel, out_shape=jax.ShapeDtypeStruct((tokens, width), jn...  2.36 us
  transfers between devices with their start and end apart: 13, of which 7 were waited for; matrix products, arithmetic and copies ran while one was open for 0% of the time, Pallas kernels for 35%

profile of v22, /device:TPU:0, one launch (start us, length us, event | category | flops | bytes accessed | tf_op | source)
XLA Modules:
  0.0 75.3 jit_solution(3562911503591683608)
XLA Ops:
  0.6 2.8 %pack.1 = (bf16[32,2304]{1,0:T(8,128)(2,1)}, bf16[32,2304]{1,0:T(8,128)(2,1)}, bf16[32,2304]{1,0:T(8,128)(2,1)}, bf16[32,2304]{1,0:T(8,128)(2,1)}, bf16[32,2304]...) custom-call(s32[1]{0:T(128)} %bitcast.1.me_ref, ...), custom_call_target="tpu_custom_call" | custom-call | flops 268435456 | bytes 2097152 | tf_op jit(solution)/shard_map/pack/pallas_call | solution.py:200
  3.5 3.0 %collective-permute-start = (bf16[32,2304]{1,0:T(8,128)(2,1)}, bf16[32,2304]{1,0:T(8,128)(2,1)S(1)}, u32[]{:S(2)}, u32[]{:S(2)}) collective-permute-start(bf16[32,2304]{1,0:T(8,128)(2,1)} %get-tuple-element.23), channel_id=1, source_target_pairs={{0,1},{1,0},{2,3},{3,2},{4,5},{5,4},{6,7},{7,6},{8,9},{9,8},{10,11... | collective-permute-start | bytes 442376 | tf_op jit(solution)/shard_map/ppermute | solution.py:606
  6.5 1.6 %collective-permute-start.1 = (bf16[32,2304]{1,0:T(8,128)(2,1)}, bf16[32,2304]{1,0:T(8,128)(2,1)}, u32[]{:S(2)}, u32[]{:S(2)}) collective-permute-start(bf16[32,2304]{1,0:T(8,128)(2,1)} %get-tuple-element.24), channel_id=1, source_target_pairs={{0,2},{1,3},{2,0},{3,1},{4,6},{5,7},{6,4},{7,5},{8,10},{9,11},{10,... | collective-permute-start | bytes 442376 | tf_op jit(solution)/shard_map/ppermute | solution.py:606
  8.1 2.5 %collective-permute-start.2 = (bf16[32,2304]{1,0:T(8,128)(2,1)}, bf16[32,2304]{1,0:T(8,128)(2,1)}, u32[]{:S(2)}, u32[]{:S(2)}) collective-permute-start(bf16[32,2304]{1,0:T(8,128)(2,1)} %get-tuple-element.25), channel_id=1, source_target_pairs={{0,6},{1,7},{2,4},{3,5},{4,2},{5,3},{6,0},{7,1},{8,14},{9,15},{10,... | collective-permute-start | bytes 442376 | tf_op jit(solution)/shard_map/ppermute | solution.py:606
  10.5 1.3 %collective-permute-start.3 = (bf16[32,2304]{1,0:T(8,128)(2,1)}, bf16[32,2304]{1,0:T(8,128)(2,1)}, u32[]{:S(2)}, u32[]{:S(2)}) collective-permute-start(bf16[32,2304]{1,0:T(8,128)(2,1)} %get-tuple-element.26), channel_id=1, source_target_pairs={{0,7},{1,6},{2,5},{3,4},{4,3},{5,2},{6,1},{7,0},{8,15},{9,14},{10,... | collective-permute-start | bytes 442376 | tf_op jit(solution)/shard_map/ppermute | solution.py:606
  11.9 0.8 %collective-permute-start.4 = (bf16[32,2304]{1,0:T(8,128)(2,1)}, bf16[32,2304]{1,0:T(8,128)(2,1)}, u32[]{:S(2)}, u32[]{:S(2)}) collective-permute-start(bf16[32,2304]{1,0:T(8,128)(2,1)} %get-tuple-element.27), channel_id=1, source_target_pairs={{0,4},{1,5},{2,6},{3,7},{4,0},{5,1},{6,2},{7,3},{8,12},{9,13},{10,... | collective-permute-start | bytes 442376 | tf_op jit(solution)/shard_map/ppermute | solution.py:606
  12.7 3.1 %collective-permute-start.5 = (bf16[32,2304]{1,0:T(8,128)(2,1)}, bf16[32,2304]{1,0:T(8,128)(2,1)}, u32[]{:S(2)}, u32[]{:S(2)}) collective-permute-start(bf16[32,2304]{1,0:T(8,128)(2,1)} %get-tuple-element.28), channel_id=1, source_target_pairs={{0,5},{1,4},{2,7},{3,6},{4,1},{5,0},{6,3},{7,2},{8,13},{9,12},{10,... | collective-permute-start | bytes 442376 | tf_op jit(solution)/shard_map/ppermute | solution.py:606
  15.7 0.2 collective-permute-start.6
  15.9 1.8 %join.2 = bf16[3,32,2304]{2,1,0:T(8,128)(2,1)} custom-call(bf16[32,2304]{1,0:T(8,128)(2,1)} %get-tuple-element.22.refs_0_, bf16[32,2304]{1,0:T(8,128)(2,1)} %copy-done, bf16[32,2304]{1,0:T(8,128)(2,1)} %collective-permute-done.1.refs_2_), custom_call_target="tpu_custom_call" | custom-call | bytes 884736 | tf_op jit(solution)/shard_map/join/pallas_call | solution.py:231
  17.7 1.3 %collective-permute-done.2.refs_3_.refs_0_ = bf16[32,2304]{1,0:T(8,128)(2,1)} collective-permute-done((bf16[32,2304]{1,0:T(8,128)(2,1)}, bf16[32,2304]{1,0:T(8,128)(2,1)}, u32[]{:S(2)}, u32[]{:S(2)}) %collective-permute-start.2) | collective-permute-done | bytes 147488 | tf_op jit(solution)/shard_map/ppermute | solution.py:606
  19.0 1.5 %collective-permute-start.7 = (bf16[3,32,2304]{2,1,0:T(8,128)(2,1)}, bf16[3,32,2304]{2,1,0:T(8,128)(2,1)}, u32[]{:S(2)}, u32[]{:S(2)}) collective-permute-start(bf16[3,32,2304]{2,1,0:T(8,128)(2,1)} %join.2), channel_id=1, source_target_pairs={{0,16},{8,24},{16,0},{24,8},{1,17},{9,25},{17,1},{25,9},{2,18},{10... | collective-permute-start | bytes 1327112 | tf_op jit(solution)/shard_map/ppermute | solution.py:606
  20.5 1.5 %collective-permute-done.3.refs_4_.refs_1_ = bf16[32,2304]{1,0:T(8,128)(2,1)} collective-permute-done((bf16[32,2304]{1,0:T(8,128)(2,1)}, bf16[32,2304]{1,0:T(8,128)(2,1)}, u32[]{:S(2)}, u32[]{:S(2)}) %collective-permute-start.3) | collective-permute-done | bytes 147488 | tf_op jit(solution)/shard_map/ppermute | solution.py:606
  22.0 13.3 %collective-permute-done.4.refs_5_.refs_2_ = bf16[32,2304]{1,0:T(8,128)(2,1)} collective-permute-done((bf16[32,2304]{1,0:T(8,128)(2,1)}, bf16[32,2304]{1,0:T(8,128)(2,1)}, u32[]{:S(2)}, u32[]{:S(2)}) %collective-permute-start.4) | collective-permute-done | bytes 147488 | tf_op jit(solution)/shard_map/ppermute | solution.py:606
  35.3 2.2 %collective-permute-done.5.refs_6_.refs_3_ = bf16[32,2304]{1,0:T(8,128)(2,1)} collective-permute-done((bf16[32,2304]{1,0:T(8,128)(2,1)}, bf16[32,2304]{1,0:T(8,128)(2,1)}, u32[]{:S(2)}, u32[]{:S(2)}) %collective-permute-start.5) | collective-permute-done | bytes 147488 | tf_op jit(solution)/shard_map/ppermute | solution.py:606
  37.5 1.9 %join.3 = bf16[5,32,2304]{2,1,0:T(8,128)(2,1)} custom-call(bf16[32,2304]{1,0:T(8,128)(2,1)} %collective-permute-done.2.refs_3_.refs_0_, bf16[32,2304]{1,0:T(8,128)(2,1)} %collective-permute-done.3.refs_4_.refs_1_, bf16[32,2304]{1,0:T(8,128)(2,1)} %collective-permute-done.4.refs_5_.refs_2_, bf16[32,2304]{1,0:T(8,128)(2,1)} %collective-permute-done.5.refs_6_.refs_3_, ...), custom_call_target="tpu_custom_call" | custom-call | flops 11324620800 | bytes 1474560 | tf_op jit(solution)/shard_map/join/pallas_call | solution.py:231
  39.5 1.6 %collective-permute-start.10 = (bf16[5,32,2304]{2,1,0:T(8,128)(2,1)}, bf16[5,32,2304]{2,1,0:T(8,128)(2,1)}, u32[]{:S(2)}, u32[]{:S(2)}) collective-permute-start(bf16[5,32,2304]{2,1,0:T(8,128)(2,1)} %join.3), channel_id=1, source_target_pairs={{0,16},{8,24},{16,0},{24,8},{1,17},{9,25},{17,1},{25,9},{2,18},{10... | collective-permute-start | bytes 2211848 | tf_op jit(solution)/shard_map/ppermute | solution.py:606
  41.1 9.9 %back.1 = (bf16[8,16,2304]{2,1,0:T(8,128)(2,1)}, bf16[144,3328]{1,0:T(8,128)(2,1)}, bf16[144,3328]{1,0:T(8,128)(2,1)}) custom-call(s32[1]{0:T(128)} %bitcast.1.me_ref, s32[1]{0:T(128)} %bitcast.2.part_ref, bf16[32,2304]{1,0:T(8,128)(2,1)} %get-tuple-element.22.refs_0_, bf16[32,2304]{1,0:T(8,128)(2,1)} %copy-done, ...), custom_call_target="tpu_custom_call" | custom-call | flops 11324620800 | bytes 1179648 | tf_op jit(solution)/shard_map/back/pallas_call | solution.py:436
  51.0 4.4 %all-to-all-start = ((bf16[8,16,2304]{2,1,0:T(8,128)(2,1)}), bf16[8,16,2304]{2,1,0:T(8,128)(2,1)}, u32[]{:S(2)}, u32[]{:S(2)}) async-start(bf16[8,16,2304]{2,1,0:T(8,128)(2,1)} %get-tuple-element.31), calls=%async_computation | async-start | bytes 1179648 | tf_op jit(solution)/shard_map/all_to_all | solution.py:610
  55.4 0.6 collective-permute-start.9
  56.0 1.2 %collective-permute-done.10.refs_3_ = bf16[5,32,2304]{2,1,0:T(8,128)(2,1)} collective-permute-done((bf16[5,32,2304]{2,1,0:T(8,128)(2,1)}, bf16[5,32,2304]{2,1,0:T(8,128)(2,1)}, u32[]{:S(2)}, u32[]{:S(2)}) %collective-permute-start.10) | collective-permute-done | bytes 737312 | tf_op jit(solution)/shard_map/ppermute | solution.py:606
  57.2 1.3 %collective-permute-done.9.refs_1_ = bf16[144,3328]{1,0:T(8,128)(2,1)} collective-permute-done((bf16[144,3328]{1,0:T(8,128)(2,1)}, bf16[144,3328]{1,0:T(8,128)(2,1)}, u32[]{:S(2)}, u32[]{:S(2)}) %collective-permute-start.9) | collective-permute-done | bytes 958496 | tf_op jit(solution)/shard_map/ppermute | solution.py:606
  58.5 1.2 %collective-permute-done.11.refs_5_ = bf16[5,32,2304]{2,1,0:T(8,128)(2,1)} collective-permute-done((bf16[5,32,2304]{2,1,0:T(8,128)(2,1)}, bf16[5,32,2304]{2,1,0:T(8,128)(2,1)}, u32[]{:S(2)}, u32[]{:S(2)}) %collective-permute-start.11) | collective-permute-done | bytes 737312 | tf_op jit(solution)/shard_map/ppermute | solution.py:606
  59.8 13.0 %weight_grads.1 = (f32[512,768]{1,0:T(8,128)}, f32[512,768]{1,0:T(8,128)}, f32[768,512]{1,0:T(8,128)}) custom-call(s32[1]{0:T(128)} %bitcast.2.part_ref, bf16[144,3328]{1,0:T(8,128)(2,1)} %get-tuple-element.32.refs_0_, bf16[144,3328]{1,0:T(8,128)(2,1)} %collective-permute-done.9.refs_1_, bf16[3,32,2304]{2,1,0:T(8,128)(2,1)} %collective-permute-done.7.refs_2_, ...), custom_call_target="tpu_custom_call" | custom-call | bytes 1179648 | tf_op jit(solution)/shard_map/weight_grads/pallas_call | solution.py:565
  72.8 2.4 %merge.1 = bf16[128,2048]{1,0:T(8,128)(2,1)} custom-call(s32[1,128]{1,0:T(1,128)} %bitcast.5, bf16[8,16,2304]{2,1,0:T(8,128)(2,1)} %all-to-all-done.back_ref), custom_call_target="tpu_custom_call" | custom-call | flops 134217728 | bytes 1048576 | tf_op jit(solution)/shard_map/merge/pallas_call | solution.py:270
  (10 shorter events, 0.0 us)
Async XLA Ops:
  3.5 9.2 %collective-permute-start = (bf16[32,2304]{1,0:T(8,128)(2,1)}, bf16[32,2304]{1,0:T(8,128)(2,1)S(1)}, u32[]{:S(2)}, u32[]{:S(2)}) collective-permute-start(bf16[32,2304]{1,0:T(8,128)(2,1)} %get-tuple-element.23), channel_id=1, source_target_pairs={{0,1},{1,0},{2,3},{3,2},{4,5},{5,4},{6,7},{7,6},{8,9},{9,8},{10,11... | collective-permute-start | bytes 442376 | tf_op jit(solution)/shard_map/ppermute | solution.py:606
  6.5 9.2 %collective-permute-start.1 = (bf16[32,2304]{1,0:T(8,128)(2,1)}, bf16[32,2304]{1,0:T(8,128)(2,1)}, u32[]{:S(2)}, u32[]{:S(2)}) collective-permute-start(bf16[32,2304]{1,0:T(8,128)(2,1)} %get-tuple-element.24), channel_id=1, source_target_pairs={{0,2},{1,3},{2,0},{3,1},{4,6},{5,7},{6,4},{7,5},{8,10},{9,11},{10,... | collective-permute-start | bytes 442376 | tf_op jit(solution)/shard_map/ppermute | solution.py:606
  8.1 10.9 %collective-permute-start.2 = (bf16[32,2304]{1,0:T(8,128)(2,1)}, bf16[32,2304]{1,0:T(8,128)(2,1)}, u32[]{:S(2)}, u32[]{:S(2)}) collective-permute-start(bf16[32,2304]{1,0:T(8,128)(2,1)} %get-tuple-element.25), channel_id=1, source_target_pairs={{0,6},{1,7},{2,4},{3,5},{4,2},{5,3},{6,0},{7,1},{8,14},{9,15},{10,... | collective-permute-start | bytes 442376 | tf_op jit(solution)/shard_map/ppermute | solution.py:606
  10.5 11.5 %collective-permute-start.3 = (bf16[32,2304]{1,0:T(8,128)(2,1)}, bf16[32,2304]{1,0:T(8,128)(2,1)}, u32[]{:S(2)}, u32[]{:S(2)}) collective-permute-start(bf16[32,2304]{1,0:T(8,128)(2,1)} %get-tuple-element.26), channel_id=1, source_target_pairs={{0,7},{1,6},{2,5},{3,4},{4,3},{5,2},{6,1},{7,0},{8,15},{9,14},{10,... | collective-permute-start | bytes 442376 | tf_op jit(solution)/shard_map/ppermute | solution.py:606
  11.9 23.4 %collective-permute-start.4 = (bf16[32,2304]{1,0:T(8,128)(2,1)}, bf16[32,2304]{1,0:T(8,128)(2,1)}, u32[]{:S(2)}, u32[]{:S(2)}) collective-permute-start(bf16[32,2304]{1,0:T(8,128)(2,1)} %get-tuple-element.27), channel_id=1, source_target_pairs={{0,4},{1,5},{2,6},{3,7},{4,0},{5,1},{6,2},{7,3},{8,12},{9,13},{10,... | collective-permute-start | bytes 442376 | tf_op jit(solution)/shard_map/ppermute | solution.py:606
  12.7 3.3 %copy-start = (bf16[32,2304]{1,0:T(8,128)(2,1)}, bf16[32,2304]{1,0:T(8,128)(2,1)S(1)}, u32[]{:S(2)}) copy-start(bf16[32,2304]{1,0:T(8,128)(2,1)S(1)} %collective-permute-done.refs_1_) | copy-start | bytes 442372
  12.7 24.9 %collective-permute-start.5 = (bf16[32,2304]{1,0:T(8,128)(2,1)}, bf16[32,2304]{1,0:T(8,128)(2,1)}, u32[]{:S(2)}, u32[]{:S(2)}) collective-permute-start(bf16[32,2304]{1,0:T(8,128)(2,1)} %get-tuple-element.28), channel_id=1, source_target_pairs={{0,5},{1,4},{2,7},{3,6},{4,1},{5,0},{6,3},{7,2},{8,13},{9,12},{10,... | collective-permute-start | bytes 442376 | tf_op jit(solution)/shard_map/ppermute | solution.py:606
  15.7 21.8 %collective-permute-start.6 = (bf16[32,2304]{1,0:T(8,128)(2,1)}, bf16[32,2304]{1,0:T(8,128)(2,1)}, u32[]{:S(2)}, u32[]{:S(2)}) collective-permute-start(bf16[32,2304]{1,0:T(8,128)(2,1)} %get-tuple-element.29), channel_id=1, source_target_pairs={{0,3},{1,2},{2,1},{3,0},{4,7},{5,6},{6,5},{7,4},{8,11},{9,10},{10,... | collective-permute-start | bytes 442376 | tf_op jit(solution)/shard_map/ppermute | solution.py:606
  19.0 22.1 %collective-permute-start.7 = (bf16[3,32,2304]{2,1,0:T(8,128)(2,1)}, bf16[3,32,2304]{2,1,0:T(8,128)(2,1)}, u32[]{:S(2)}, u32[]{:S(2)}) collective-permute-start(bf16[3,32,2304]{2,1,0:T(8,128)(2,1)} %join.2), channel_id=1, source_target_pairs={{0,16},{8,24},{16,0},{24,8},{1,17},{9,25},{17,1},{25,9},{2,18},{10... | collective-permute-start | bytes 1327112 | tf_op jit(solution)/shard_map/ppermute | solution.py:606
  39.5 17.7 %collective-permute-start.10 = (bf16[5,32,2304]{2,1,0:T(8,128)(2,1)}, bf16[5,32,2304]{2,1,0:T(8,128)(2,1)}, u32[]{:S(2)}, u32[]{:S(2)}) collective-permute-start(bf16[5,32,2304]{2,1,0:T(8,128)(2,1)} %join.3), channel_id=1, source_target_pairs={{0,16},{8,24},{16,0},{24,8},{1,17},{9,25},{17,1},{25,9},{2,18},{10... | collective-permute-start | bytes 2211848 | tf_op jit(solution)/shard_map/ppermute | solution.py:606
  41.1 10.0 %collective-permute-start.8 = (bf16[3,32,2304]{2,1,0:T(8,128)(2,1)}, bf16[3,32,2304]{2,1,0:T(8,128)(2,1)}, u32[]{:S(2)}, u32[]{:S(2)}) collective-permute-start(bf16[3,32,2304]{2,1,0:T(8,128)(2,1)} %collective-permute-done.7.refs_2_), channel_id=1, source_target_pairs={{0,8},{8,0},{16,24},{24,16},{1,9},{9,1},{17,25},{25,17},{2,10},{10... | collective-permute-start | bytes 1327112 | tf_op jit(solution)/shard_map/ppermute | solution.py:606
  51.0 21.7 %all-to-all-start = ((bf16[8,16,2304]{2,1,0:T(8,128)(2,1)}), bf16[8,16,2304]{2,1,0:T(8,128)(2,1)}, u32[]{:S(2)}, u32[]{:S(2)}) async-start(bf16[8,16,2304]{2,1,0:T(8,128)(2,1)} %get-tuple-element.31), calls=%async_computation | async-start | bytes 1179648 | tf_op jit(solution)/shard_map/all_to_all | solution.py:610
  55.4 3.1 %collective-permute-start.9 = (bf16[144,3328]{1,0:T(8,128)(2,1)}, bf16[144,3328]{1,0:T(8,128)(2,1)}, u32[]{:S(2)}, u32[]{:S(2)}) collective-permute-start(bf16[144,3328]{1,0:T(8,128)(2,1)} %get-tuple-element.33), channel_id=1, source_target_pairs={{0,8},{8,0},{16,24},{24,16},{1,9},{9,1},{17,25},{25,17},{2,10},{10... | collective-permute-start | bytes 2875400 | tf_op jit(solution)/shard_map/ppermute | solution.py:606
  57.2 2.6 %collective-permute-start.11 = (bf16[5,32,2304]{2,1,0:T(8,128)(2,1)}, bf16[5,32,2304]{2,1,0:T(8,128)(2,1)}, u32[]{:S(2)}, u32[]{:S(2)}) collective-permute-start(bf16[5,32,2304]{2,1,0:T(8,128)(2,1)} %collective-permute-done.10.refs_3_), channel_id=1, source_target_pairs={{0,8},{8,0},{16,24},{24,16},{1,9},{9,1},{17,25},{25,17},{2,10},{10... | collective-permute-start | bytes 2211848 | tf_op jit(solution)/shard_map/ppermute | solution.py:606

commit v23 on v22

--- a/solution.py
+++ b/solution.py
@@ -625,7 +625,7 @@
     received = list(pack(blocks, me, routes, gates, tokens, cotangent))
     for distance in reversed(range(1, blocks)):
         received[distance] = swap(received[distance], "expert", distance)
-    order = [0, 1, 2, 6, 7, 4, 5, 3]
+    order = [0, 1, 2, 6, 4, 7, 5, 3]
     early = 3
     received = [received[index] for index in order]
     far = swap(join(received[:early]), "dp", 2)

time: 75.6 us -> 74.5 us (0.985)
  waiting for transfers between devices: 22.1 us -> 20.8 us
    ppermute x12, waiting for transfers between devices: 22.1 us -> 20.8 us  [swap(): lax.ppermute(value, axis, [(at, at ^ distance) for at in range(size)])]
  transfers between devices with their start and end apart: 13 -> 13, of which waited for: 7 -> 6; matrix products, arithmetic and copies ran while one was open for 0% -> 0% of each run, Pallas kernels for 35% -> 36%
where the time goes in v23:
time: 74.5 us; the launch traced here: 74.2 us
  Pallas kernels  31.8 us (43%)
  waiting for transfers between devices  20.8 us (28%)
  starting transfers between devices  20.7 us (28%)
  between operations  0.86 us (1%)
    ppermute x12, waiting for transfers between devices, swap(): lax.ppermute(value, axis, [(at, at ^ distance) for at in range(size)])  20.8 us
    ppermute x12, starting transfers between devices, swap(): lax.ppermute(value, axis, [(at, at ^ distance) for at in range(size)])  15.8 us
    pallas_call x1, Pallas kernels, weight_grads(): pl.pallas_call(kernel, out_shape=[jax.ShapeDtypeStruct((share, hid), jnp....  13 us
    pallas_call x1, Pallas kernels, back(): pl.pallas_call(kernel, out_shape=[jax.ShapeDtypeStruct(shape, jnp.bfloat1...  9.94 us
    all_to_all x1, starting transfers between devices, exchange(): lax.all_to_all(blocks, 'expert', split_axis=0, concat_axis=0, tiled=True)  4.86 us
    pallas_call x2, Pallas kernels, join(): pl.pallas_call(kernel, out_shape=jax.ShapeDtypeStruct(shape, jnp.bfloat16...  3.71 us
    pallas_call x1, Pallas kernels, pack(): pl.pallas_call(kernel, out_shape=[jax.ShapeDtypeStruct(block_shape, jnp.b...  2.84 us
    pallas_call x1, Pallas kernels, merge(): pl.pallas_call(kernel, out_shape=jax.ShapeDtypeStruct((tokens, width), jn...  2.36 us
  transfers between devices with their start and end apart: 13, of which 6 were waited for; matrix products, arithmetic and copies ran while one was open for 0% of the time, Pallas kernels for 36%

profile of v23, /device:TPU:0, one launch (start us, length us, event | category | flops | bytes accessed | tf_op | source)
XLA Modules:
  0.0 74.2 jit_solution(7665599487354627070)
XLA Ops:
  0.6 2.8 %pack.1 = (bf16[32,2304]{1,0:T(8,128)(2,1)}, bf16[32,2304]{1,0:T(8,128)(2,1)}, bf16[32,2304]{1,0:T(8,128)(2,1)}, bf16[32,2304]{1,0:T(8,128)(2,1)}, bf16[32,2304]...) custom-call(s32[1]{0:T(128)} %bitcast.1.me_ref, ...), custom_call_target="tpu_custom_call" | custom-call | flops 268435456 | bytes 2097152 | tf_op jit(solution)/shard_map/pack/pallas_call | solution.py:200
  3.5 3.0 %collective-permute-start = (bf16[32,2304]{1,0:T(8,128)(2,1)}, bf16[32,2304]{1,0:T(8,128)(2,1)S(1)}, u32[]{:S(2)}, u32[]{:S(2)}) collective-permute-start(bf16[32,2304]{1,0:T(8,128)(2,1)} %get-tuple-element.23), channel_id=1, source_target_pairs={{0,1},{1,0},{2,3},{3,2},{4,5},{5,4},{6,7},{7,6},{8,9},{9,8},{10,11... | collective-permute-start | bytes 442376 | tf_op jit(solution)/shard_map/ppermute | solution.py:606
  6.5 1.6 %collective-permute-start.1 = (bf16[32,2304]{1,0:T(8,128)(2,1)}, bf16[32,2304]{1,0:T(8,128)(2,1)}, u32[]{:S(2)}, u32[]{:S(2)}) collective-permute-start(bf16[32,2304]{1,0:T(8,128)(2,1)} %get-tuple-element.24), channel_id=1, source_target_pairs={{0,2},{1,3},{2,0},{3,1},{4,6},{5,7},{6,4},{7,5},{8,10},{9,11},{10,... | collective-permute-start | bytes 442376 | tf_op jit(solution)/shard_map/ppermute | solution.py:606
  8.1 2.5 %collective-permute-start.2 = (bf16[32,2304]{1,0:T(8,128)(2,1)}, bf16[32,2304]{1,0:T(8,128)(2,1)}, u32[]{:S(2)}, u32[]{:S(2)}) collective-permute-start(bf16[32,2304]{1,0:T(8,128)(2,1)} %get-tuple-element.25), channel_id=1, source_target_pairs={{0,6},{1,7},{2,4},{3,5},{4,2},{5,3},{6,0},{7,1},{8,14},{9,15},{10,... | collective-permute-start | bytes 442376 | tf_op jit(solution)/shard_map/ppermute | solution.py:606
  10.5 0.1 collective-permute-start.3
  10.7 2.9 %collective-permute-start.4 = (bf16[32,2304]{1,0:T(8,128)(2,1)}, bf16[32,2304]{1,0:T(8,128)(2,1)}, u32[]{:S(2)}, u32[]{:S(2)}) collective-permute-start(bf16[32,2304]{1,0:T(8,128)(2,1)} %get-tuple-element.27), channel_id=1, source_target_pairs={{0,7},{1,6},{2,5},{3,4},{4,3},{5,2},{6,1},{7,0},{8,15},{9,14},{10,... | collective-permute-start | bytes 442376 | tf_op jit(solution)/shard_map/ppermute | solution.py:606
  13.5 0.0 collective-permute-done.refs_1_
  13.6 1.3 %collective-permute-start.5 = (bf16[32,2304]{1,0:T(8,128)(2,1)}, bf16[32,2304]{1,0:T(8,128)(2,1)}, u32[]{:S(2)}, u32[]{:S(2)}) collective-permute-start(bf16[32,2304]{1,0:T(8,128)(2,1)} %get-tuple-element.28), channel_id=1, source_target_pairs={{0,5},{1,4},{2,7},{3,6},{4,1},{5,0},{6,3},{7,2},{8,13},{9,12},{10,... | collective-permute-start | bytes 442376 | tf_op jit(solution)/shard_map/ppermute | solution.py:606
  14.8 1.1 %collective-permute-start.6 = (bf16[32,2304]{1,0:T(8,128)(2,1)}, bf16[32,2304]{1,0:T(8,128)(2,1)}, u32[]{:S(2)}, u32[]{:S(2)}) collective-permute-start(bf16[32,2304]{1,0:T(8,128)(2,1)} %get-tuple-element.29), channel_id=1, source_target_pairs={{0,3},{1,2},{2,1},{3,0},{4,7},{5,6},{6,5},{7,4},{8,11},{9,10},{10,... | collective-permute-start | bytes 442376 | tf_op jit(solution)/shard_map/ppermute | solution.py:606
  15.9 1.8 %join.2 = bf16[3,32,2304]{2,1,0:T(8,128)(2,1)} custom-call(bf16[32,2304]{1,0:T(8,128)(2,1)} %get-tuple-element.22.refs_0_, bf16[32,2304]{1,0:T(8,128)(2,1)} %copy-done, bf16[32,2304]{1,0:T(8,128)(2,1)} %collective-permute-done.1.refs_2_), custom_call_target="tpu_custom_call" | custom-call | bytes 884736 | tf_op jit(solution)/shard_map/join/pallas_call | solution.py:231
  17.7 1.2 %collective-permute-done.2.refs_3_.refs_0_ = bf16[32,2304]{1,0:T(8,128)(2,1)} collective-permute-done((bf16[32,2304]{1,0:T(8,128)(2,1)}, bf16[32,2304]{1,0:T(8,128)(2,1)}, u32[]{:S(2)}, u32[]{:S(2)}) %collective-permute-start.2) | collective-permute-done | bytes 147488 | tf_op jit(solution)/shard_map/ppermute | solution.py:606
  18.9 1.5 %collective-permute-start.7 = (bf16[3,32,2304]{2,1,0:T(8,128)(2,1)}, bf16[3,32,2304]{2,1,0:T(8,128)(2,1)}, u32[]{:S(2)}, u32[]{:S(2)}) collective-permute-start(bf16[3,32,2304]{2,1,0:T(8,128)(2,1)} %join.2), channel_id=1, source_target_pairs={{0,16},{8,24},{16,0},{24,8},{1,17},{9,25},{17,1},{25,9},{2,18},{10... | collective-permute-start | bytes 1327112 | tf_op jit(solution)/shard_map/ppermute | solution.py:606
  20.4 10.9 %collective-permute-done.3.refs_4_.refs_1_ = bf16[32,2304]{1,0:T(8,128)(2,1)} collective-permute-done((bf16[32,2304]{1,0:T(8,128)(2,1)}, bf16[32,2304]{1,0:T(8,128)(2,1)}, u32[]{:S(2)}, u32[]{:S(2)}) %collective-permute-start.3) | collective-permute-done | bytes 147488 | tf_op jit(solution)/shard_map/ppermute | solution.py:606
  31.3 5.0 %collective-permute-done.5.refs_6_.refs_3_ = bf16[32,2304]{1,0:T(8,128)(2,1)} collective-permute-done((bf16[32,2304]{1,0:T(8,128)(2,1)}, bf16[32,2304]{1,0:T(8,128)(2,1)}, u32[]{:S(2)}, u32[]{:S(2)}) %collective-permute-start.5) | collective-permute-done | bytes 147488 | tf_op jit(solution)/shard_map/ppermute | solution.py:606
  36.3 1.9 %join.3 = bf16[5,32,2304]{2,1,0:T(8,128)(2,1)} custom-call(bf16[32,2304]{1,0:T(8,128)(2,1)} %collective-permute-done.2.refs_3_.refs_0_, bf16[32,2304]{1,0:T(8,128)(2,1)} %collective-permute-done.3.refs_4_.refs_1_, bf16[32,2304]{1,0:T(8,128)(2,1)} %collective-permute-done.4.refs_5_.refs_2_, bf16[32,2304]{1,0:T(8,128)(2,1)} %collective-permute-done.5.refs_6_.refs_3_, ...), custom_call_target="tpu_custom_call" | custom-call | flops 11324620800 | bytes 1474560 | tf_op jit(solution)/shard_map/join/pallas_call | solution.py:231
  38.3 1.6 %collective-permute-start.10 = (bf16[5,32,2304]{2,1,0:T(8,128)(2,1)}, bf16[5,32,2304]{2,1,0:T(8,128)(2,1)}, u32[]{:S(2)}, u32[]{:S(2)}) collective-permute-start(bf16[5,32,2304]{2,1,0:T(8,128)(2,1)} %join.3), channel_id=1, source_target_pairs={{0,16},{8,24},{16,0},{24,8},{1,17},{9,25},{17,1},{25,9},{2,18},{10... | collective-permute-start | bytes 2211848 | tf_op jit(solution)/shard_map/ppermute | solution.py:606
  39.9 9.9 %back.1 = (bf16[8,16,2304]{2,1,0:T(8,128)(2,1)}, bf16[144,3328]{1,0:T(8,128)(2,1)}, bf16[144,3328]{1,0:T(8,128)(2,1)}) custom-call(s32[1]{0:T(128)} %bitcast.1.me_ref, s32[1]{0:T(128)} %bitcast.2.part_ref, bf16[32,2304]{1,0:T(8,128)(2,1)} %get-tuple-element.22.refs_0_, bf16[32,2304]{1,0:T(8,128)(2,1)} %copy-done, ...), custom_call_target="tpu_custom_call" | custom-call | flops 11324620800 | bytes 1179648 | tf_op jit(solution)/shard_map/back/pallas_call | solution.py:436
  49.8 4.9 %all-to-all-start = ((bf16[8,16,2304]{2,1,0:T(8,128)(2,1)}), bf16[8,16,2304]{2,1,0:T(8,128)(2,1)}, u32[]{:S(2)}, u32[]{:S(2)}) async-start(bf16[8,16,2304]{2,1,0:T(8,128)(2,1)} %get-tuple-element.31), calls=%async_computation | async-start | bytes 1179648 | tf_op jit(solution)/shard_map/all_to_all | solution.py:610
  54.7 0.2 collective-permute-start.9
  55.0 1.0 %collective-permute-done.10.refs_3_ = bf16[5,32,2304]{2,1,0:T(8,128)(2,1)} collective-permute-done((bf16[5,32,2304]{2,1,0:T(8,128)(2,1)}, bf16[5,32,2304]{2,1,0:T(8,128)(2,1)}, u32[]{:S(2)}, u32[]{:S(2)}) %collective-permute-start.10) | collective-permute-done | bytes 737312 | tf_op jit(solution)/shard_map/ppermute | solution.py:606
  55.9 1.6 %collective-permute-done.9.refs_1_ = bf16[144,3328]{1,0:T(8,128)(2,1)} collective-permute-done((bf16[144,3328]{1,0:T(8,128)(2,1)}, bf16[144,3328]{1,0:T(8,128)(2,1)}, u32[]{:S(2)}, u32[]{:S(2)}) %collective-permute-start.9) | collective-permute-done | bytes 958496 | tf_op jit(solution)/shard_map/ppermute | solution.py:606
  57.6 1.1 %collective-permute-done.11.refs_5_ = bf16[5,32,2304]{2,1,0:T(8,128)(2,1)} collective-permute-done((bf16[5,32,2304]{2,1,0:T(8,128)(2,1)}, bf16[5,32,2304]{2,1,0:T(8,128)(2,1)}, u32[]{:S(2)}, u32[]{:S(2)}) %collective-permute-start.11) | collective-permute-done | bytes 737312 | tf_op jit(solution)/shard_map/ppermute | solution.py:606
  58.6 13.0 %weight_grads.1 = (f32[512,768]{1,0:T(8,128)}, f32[512,768]{1,0:T(8,128)}, f32[768,512]{1,0:T(8,128)}) custom-call(s32[1]{0:T(128)} %bitcast.2.part_ref, bf16[144,3328]{1,0:T(8,128)(2,1)} %get-tuple-element.32.refs_0_, bf16[144,3328]{1,0:T(8,128)(2,1)} %collective-permute-done.9.refs_1_, bf16[3,32,2304]{2,1,0:T(8,128)(2,1)} %collective-permute-done.7.refs_2_, ...), custom_call_target="tpu_custom_call" | custom-call | bytes 1179648 | tf_op jit(solution)/shard_map/weight_grads/pallas_call | solution.py:565
  71.7 2.4 %merge.1 = bf16[128,2048]{1,0:T(8,128)(2,1)} custom-call(s32[1,128]{1,0:T(1,128)} %bitcast.5, bf16[8,16,2304]{2,1,0:T(8,128)(2,1)} %all-to-all-done.back_ref), custom_call_target="tpu_custom_call" | custom-call | flops 134217728 | bytes 1048576 | tf_op jit(solution)/shard_map/merge/pallas_call | solution.py:270
  (10 shorter events, 0.0 us)
Async XLA Ops:
  3.5 10.1 %collective-permute-start = (bf16[32,2304]{1,0:T(8,128)(2,1)}, bf16[32,2304]{1,0:T(8,128)(2,1)S(1)}, u32[]{:S(2)}, u32[]{:S(2)}) collective-permute-start(bf16[32,2304]{1,0:T(8,128)(2,1)} %get-tuple-element.23), channel_id=1, source_target_pairs={{0,1},{1,0},{2,3},{3,2},{4,5},{5,4},{6,7},{7,6},{8,9},{9,8},{10,11... | collective-permute-start | bytes 442376 | tf_op jit(solution)/shard_map/ppermute | solution.py:606
  6.5 8.3 %collective-permute-start.1 = (bf16[32,2304]{1,0:T(8,128)(2,1)}, bf16[32,2304]{1,0:T(8,128)(2,1)}, u32[]{:S(2)}, u32[]{:S(2)}) collective-permute-start(bf16[32,2304]{1,0:T(8,128)(2,1)} %get-tuple-element.24), channel_id=1, source_target_pairs={{0,2},{1,3},{2,0},{3,1},{4,6},{5,7},{6,4},{7,5},{8,10},{9,11},{10,... | collective-permute-start | bytes 442376 | tf_op jit(solution)/shard_map/ppermute | solution.py:606
  8.1 10.8 %collective-permute-start.2 = (bf16[32,2304]{1,0:T(8,128)(2,1)}, bf16[32,2304]{1,0:T(8,128)(2,1)}, u32[]{:S(2)}, u32[]{:S(2)}) collective-permute-start(bf16[32,2304]{1,0:T(8,128)(2,1)} %get-tuple-element.25), channel_id=1, source_target_pairs={{0,6},{1,7},{2,4},{3,5},{4,2},{5,3},{6,0},{7,1},{8,14},{9,15},{10,... | collective-permute-start | bytes 442376 | tf_op jit(solution)/shard_map/ppermute | solution.py:606
  10.5 20.8 %collective-permute-start.3 = (bf16[32,2304]{1,0:T(8,128)(2,1)}, bf16[32,2304]{1,0:T(8,128)(2,1)}, u32[]{:S(2)}, u32[]{:S(2)}) collective-permute-start(bf16[32,2304]{1,0:T(8,128)(2,1)} %get-tuple-element.26), channel_id=1, source_target_pairs={{0,4},{1,5},{2,6},{3,7},{4,0},{5,1},{6,2},{7,3},{8,12},{9,13},{10,... | collective-permute-start | bytes 442376 | tf_op jit(solution)/shard_map/ppermute | solution.py:606
  10.7 20.6 %collective-permute-start.4 = (bf16[32,2304]{1,0:T(8,128)(2,1)}, bf16[32,2304]{1,0:T(8,128)(2,1)}, u32[]{:S(2)}, u32[]{:S(2)}) collective-permute-start(bf16[32,2304]{1,0:T(8,128)(2,1)} %get-tuple-element.27), channel_id=1, source_target_pairs={{0,7},{1,6},{2,5},{3,4},{4,3},{5,2},{6,1},{7,0},{8,15},{9,14},{10,... | collective-permute-start | bytes 442376 | tf_op jit(solution)/shard_map/ppermute | solution.py:606
  13.5 2.4 %copy-start = (bf16[32,2304]{1,0:T(8,128)(2,1)}, bf16[32,2304]{1,0:T(8,128)(2,1)S(1)}, u32[]{:S(2)}) copy-start(bf16[32,2304]{1,0:T(8,128)(2,1)S(1)} %collective-permute-done.refs_1_) | copy-start | bytes 442372
  13.6 22.8 %collective-permute-start.5 = (bf16[32,2304]{1,0:T(8,128)(2,1)}, bf16[32,2304]{1,0:T(8,128)(2,1)}, u32[]{:S(2)}, u32[]{:S(2)}) collective-permute-start(bf16[32,2304]{1,0:T(8,128)(2,1)} %get-tuple-element.28), channel_id=1, source_target_pairs={{0,5},{1,4},{2,7},{3,6},{4,1},{5,0},{6,3},{7,2},{8,13},{9,12},{10,... | collective-permute-start | bytes 442376 | tf_op jit(solution)/shard_map/ppermute | solution.py:606
  14.8 21.5 %collective-permute-start.6 = (bf16[32,2304]{1,0:T(8,128)(2,1)}, bf16[32,2304]{1,0:T(8,128)(2,1)}, u32[]{:S(2)}, u32[]{:S(2)}) collective-permute-start(bf16[32,2304]{1,0:T(8,128)(2,1)} %get-tuple-element.29), channel_id=1, source_target_pairs={{0,3},{1,2},{2,1},{3,0},{4,7},{5,6},{6,5},{7,4},{8,11},{9,10},{10,... | collective-permute-start | bytes 442376 | tf_op jit(solution)/shard_map/ppermute | solution.py:606
  18.9 21.0 %collective-permute-start.7 = (bf16[3,32,2304]{2,1,0:T(8,128)(2,1)}, bf16[3,32,2304]{2,1,0:T(8,128)(2,1)}, u32[]{:S(2)}, u32[]{:S(2)}) collective-permute-start(bf16[3,32,2304]{2,1,0:T(8,128)(2,1)} %join.2), channel_id=1, source_target_pairs={{0,16},{8,24},{16,0},{24,8},{1,17},{9,25},{17,1},{25,9},{2,18},{10... | collective-permute-start | bytes 1327112 | tf_op jit(solution)/shard_map/ppermute | solution.py:606
  38.3 17.6 %collective-permute-start.10 = (bf16[5,32,2304]{2,1,0:T(8,128)(2,1)}, bf16[5,32,2304]{2,1,0:T(8,128)(2,1)}, u32[]{:S(2)}, u32[]{:S(2)}) collective-permute-start(bf16[5,32,2304]{2,1,0:T(8,128)(2,1)} %join.3), channel_id=1, source_target_pairs={{0,16},{8,24},{16,0},{24,8},{1,17},{9,25},{17,1},{25,9},{2,18},{10... | collective-permute-start | bytes 2211848 | tf_op jit(solution)/shard_map/ppermute | solution.py:606
  39.9 10.0 %collective-permute-start.8 = (bf16[3,32,2304]{2,1,0:T(8,128)(2,1)}, bf16[3,32,2304]{2,1,0:T(8,128)(2,1)}, u32[]{:S(2)}, u32[]{:S(2)}) collective-permute-start(bf16[3,32,2304]{2,1,0:T(8,128)(2,1)} %collective-permute-done.7.refs_2_), channel_id=1, source_target_pairs={{0,8},{8,0},{16,24},{24,16},{1,9},{9,1},{17,25},{25,17},{2,10},{10... | collective-permute-start | bytes 1327112 | tf_op jit(solution)/shard_map/ppermute | solution.py:606
  49.8 21.8 %all-to-all-start = ((bf16[8,16,2304]{2,1,0:T(8,128)(2,1)}), bf16[8,16,2304]{2,1,0:T(8,128)(2,1)}, u32[]{:S(2)}, u32[]{:S(2)}) async-start(bf16[8,16,2304]{2,1,0:T(8,128)(2,1)} %get-tuple-element.31), calls=%async_computation | async-start | bytes 1179648 | tf_op jit(solution)/shard_map/all_to_all | solution.py:610
  54.7 2.9 %collective-permute-start.9 = (bf16[144,3328]{1,0:T(8,128)(2,1)}, bf16[144,3328]{1,0:T(8,128)(2,1)}, u32[]{:S(2)}, u32[]{:S(2)}) collective-permute-start(bf16[144,3328]{1,0:T(8,128)(2,1)} %get-tuple-element.33), channel_id=1, source_target_pairs={{0,8},{8,0},{16,24},{24,16},{1,9},{9,1},{17,25},{25,17},{2,10},{10... | collective-permute-start | bytes 2875400 | tf_op jit(solution)/shard_map/ppermute | solution.py:606
  55.9 2.7 %collective-permute-start.11 = (bf16[5,32,2304]{2,1,0:T(8,128)(2,1)}, bf16[5,32,2304]{2,1,0:T(8,128)(2,1)}, u32[]{:S(2)}, u32[]{:S(2)}) collective-permute-start(bf16[5,32,2304]{2,1,0:T(8,128)(2,1)} %collective-permute-done.10.refs_3_), channel_id=1, source_target_pairs={{0,8},{8,0},{16,24},{24,16},{1,9},{9,1},{17,25},{25,17},{2,10},{10... | collective-permute-start | bytes 2211848 | tf_op jit(solution)/shard_map/ppermute | solution.py:606

commit v24 on v23

--- a/solution.py
+++ b/solution.py
@@ -625,7 +625,7 @@
     received = list(pack(blocks, me, routes, gates, tokens, cotangent))
     for distance in reversed(range(1, blocks)):
         received[distance] = swap(received[distance], "expert", distance)
-    order = [0, 1, 2, 6, 4, 7, 5, 3]
+    order = [0, 1, 2, 4, 6, 5, 7, 3]
     early = 3
     received = [received[index] for index in order]
     far = swap(join(received[:early]), "dp", 2)

time: 74.5 us -> 73.6 us (0.988)
  waiting for transfers between devices: 20.8 us -> 19 us
  starting transfers between devices: 20.7 us -> 21.6 us
    ppermute x12, waiting for transfers between devices: 20.8 us -> 19 us  [swap(): lax.ppermute(value, axis, [(at, at ^ distance) for at in range(size)])]
  transfers between devices with their start and end apart: 13 -> 13, of which waited for: 6 -> 4; matrix products, arithmetic and copies ran while one was open for 0% -> 0% of each run, Pallas kernels for 36% -> 36%
where the time goes in v24:
time: 73.6 us; the launch traced here: 73.3 us
  Pallas kernels  31.9 us (43%)
  starting transfers between devices  21.6 us (29%)
  waiting for transfers between devices  19 us (26%)
  between operations  0.86 us (1%)
    ppermute x12, waiting for transfers between devices, swap(): lax.ppermute(value, axis, [(at, at ^ distance) for at in range(size)])  19 us
    ppermute x12, starting transfers between devices, swap(): lax.ppermute(value, axis, [(at, at ^ distance) for at in range(size)])  16.2 us
    pallas_call x1, Pallas kernels, weight_grads(): pl.pallas_call(kernel, out_shape=[jax.ShapeDtypeStruct((share, hid), jnp....  13 us
    pallas_call x1, Pallas kernels, back(): pl.pallas_call(kernel, out_shape=[jax.ShapeDtypeStruct(shape, jnp.bfloat1...  9.95 us
    all_to_all x1, starting transfers between devices, exchange(): lax.all_to_all(blocks, 'expert', split_axis=0, concat_axis=0, tiled=True)  5.4 us
    pallas_call x2, Pallas kernels, join(): pl.pallas_call(kernel, out_shape=jax.ShapeDtypeStruct(shape, jnp.bfloat16...  3.71 us
    pallas_call x1, Pallas kernels, pack(): pl.pallas_call(kernel, out_shape=[jax.ShapeDtypeStruct(block_shape, jnp.b...  2.84 us
    pallas_call x1, Pallas kernels, merge(): pl.pallas_call(kernel, out_shape=jax.ShapeDtypeStruct((tokens, width), jn...  2.36 us
  transfers between devices with their start and end apart: 13, of which 4 were waited for; matrix products, arithmetic and copies ran while one was open for 0% of the time, Pallas kernels for 36%

profile of v24, /device:TPU:0, one launch (start us, length us, event | category | flops | bytes accessed | tf_op | source)
XLA Modules:
  0.0 73.3 jit_solution(1951694110369267734)
XLA Ops:
  0.6 2.8 %pack.1 = (bf16[32,2304]{1,0:T(8,128)(2,1)}, bf16[32,2304]{1,0:T(8,128)(2,1)}, bf16[32,2304]{1,0:T(8,128)(2,1)}, bf16[32,2304]{1,0:T(8,128)(2,1)}, bf16[32,2304]...) custom-call(s32[1]{0:T(128)} %bitcast.1.me_ref, ...), custom_call_target="tpu_custom_call" | custom-call | flops 268435456 | bytes 2097152 | tf_op jit(solution)/shard_map/pack/pallas_call | solution.py:200
  3.5 3.0 %collective-permute-start = (bf16[32,2304]{1,0:T(8,128)(2,1)}, bf16[32,2304]{1,0:T(8,128)(2,1)S(1)}, u32[]{:S(2)}, u32[]{:S(2)}) collective-permute-start(bf16[32,2304]{1,0:T(8,128)(2,1)} %get-tuple-element.23), channel_id=1, source_target_pairs={{0,1},{1,0},{2,3},{3,2},{4,5},{5,4},{6,7},{7,6},{8,9},{9,8},{10,11... | collective-permute-start | bytes 442376 | tf_op jit(solution)/shard_map/ppermute | solution.py:606
  6.5 1.6 %collective-permute-start.1 = (bf16[32,2304]{1,0:T(8,128)(2,1)}, bf16[32,2304]{1,0:T(8,128)(2,1)}, u32[]{:S(2)}, u32[]{:S(2)}) collective-permute-start(bf16[32,2304]{1,0:T(8,128)(2,1)} %get-tuple-element.24), channel_id=1, source_target_pairs={{0,2},{1,3},{2,0},{3,1},{4,6},{5,7},{6,4},{7,5},{8,10},{9,11},{10,... | collective-permute-start | bytes 442376 | tf_op jit(solution)/shard_map/ppermute | solution.py:606
  8.1 2.6 %collective-permute-start.2 = (bf16[32,2304]{1,0:T(8,128)(2,1)}, bf16[32,2304]{1,0:T(8,128)(2,1)}, u32[]{:S(2)}, u32[]{:S(2)}) collective-permute-start(bf16[32,2304]{1,0:T(8,128)(2,1)} %get-tuple-element.25), channel_id=1, source_target_pairs={{0,4},{1,5},{2,6},{3,7},{4,0},{5,1},{6,2},{7,3},{8,12},{9,13},{10,... | collective-permute-start | bytes 442376 | tf_op jit(solution)/shard_map/ppermute | solution.py:606
  10.6 0.2 collective-permute-start.3
  10.9 1.7 %collective-permute-start.4 = (bf16[32,2304]{1,0:T(8,128)(2,1)}, bf16[32,2304]{1,0:T(8,128)(2,1)}, u32[]{:S(2)}, u32[]{:S(2)}) collective-permute-start(bf16[32,2304]{1,0:T(8,128)(2,1)} %get-tuple-element.27), channel_id=1, source_target_pairs={{0,5},{1,4},{2,7},{3,6},{4,1},{5,0},{6,3},{7,2},{8,13},{9,12},{10,... | collective-permute-start | bytes 442376 | tf_op jit(solution)/shard_map/ppermute | solution.py:606
  12.5 0.0 collective-permute-done.refs_1_
  12.5 2.8 %collective-permute-start.5 = (bf16[32,2304]{1,0:T(8,128)(2,1)}, bf16[32,2304]{1,0:T(8,128)(2,1)}, u32[]{:S(2)}, u32[]{:S(2)}) collective-permute-start(bf16[32,2304]{1,0:T(8,128)(2,1)} %get-tuple-element.28), channel_id=1, source_target_pairs={{0,7},{1,6},{2,5},{3,4},{4,3},{5,2},{6,1},{7,0},{8,15},{9,14},{10,... | collective-permute-start | bytes 442376 | tf_op jit(solution)/shard_map/ppermute | solution.py:606
  15.3 0.0 collective-permute-done.1.refs_2_
  15.3 0.7 collective-permute-start.6
  16.0 1.8 %join.2 = bf16[3,32,2304]{2,1,0:T(8,128)(2,1)} custom-call(bf16[32,2304]{1,0:T(8,128)(2,1)} %get-tuple-element.22.refs_0_, bf16[32,2304]{1,0:T(8,128)(2,1)} %copy-done, bf16[32,2304]{1,0:T(8,128)(2,1)} %collective-permute-done.1.refs_2_), custom_call_target="tpu_custom_call" | custom-call | bytes 884736 | tf_op jit(solution)/shard_map/join/pallas_call | solution.py:231
  17.8 10.8 %collective-permute-done.2.refs_3_.refs_0_ = bf16[32,2304]{1,0:T(8,128)(2,1)} collective-permute-done((bf16[32,2304]{1,0:T(8,128)(2,1)}, bf16[32,2304]{1,0:T(8,128)(2,1)}, u32[]{:S(2)}, u32[]{:S(2)}) %collective-permute-start.2) | collective-permute-done | bytes 147488 | tf_op jit(solution)/shard_map/ppermute | solution.py:606
  28.6 1.5 %collective-permute-start.7 = (bf16[3,32,2304]{2,1,0:T(8,128)(2,1)}, bf16[3,32,2304]{2,1,0:T(8,128)(2,1)}, u32[]{:S(2)}, u32[]{:S(2)}) collective-permute-start(bf16[3,32,2304]{2,1,0:T(8,128)(2,1)} %join.2), channel_id=1, source_target_pairs={{0,16},{8,24},{16,0},{24,8},{1,17},{9,25},{17,1},{25,9},{2,18},{10... | collective-permute-start | bytes 1327112 | tf_op jit(solution)/shard_map/ppermute | solution.py:606
  30.1 4.7 %collective-permute-done.4.refs_5_.refs_2_ = bf16[32,2304]{1,0:T(8,128)(2,1)} collective-permute-done((bf16[32,2304]{1,0:T(8,128)(2,1)}, bf16[32,2304]{1,0:T(8,128)(2,1)}, u32[]{:S(2)}, u32[]{:S(2)}) %collective-permute-start.4) | collective-permute-done | bytes 147488 | tf_op jit(solution)/shard_map/ppermute | solution.py:606
  34.9 1.9 %join.3 = bf16[5,32,2304]{2,1,0:T(8,128)(2,1)} custom-call(bf16[32,2304]{1,0:T(8,128)(2,1)} %collective-permute-done.2.refs_3_.refs_0_, bf16[32,2304]{1,0:T(8,128)(2,1)} %collective-permute-done.3.refs_4_.refs_1_, bf16[32,2304]{1,0:T(8,128)(2,1)} %collective-permute-done.4.refs_5_.refs_2_, bf16[32,2304]{1,0:T(8,128)(2,1)} %collective-permute-done.5.refs_6_.refs_3_, ...), custom_call_target="tpu_custom_call" | custom-call | flops 11324620800 | bytes 1474560 | tf_op jit(solution)/shard_map/join/pallas_call | solution.py:231
  36.8 1.6 %collective-permute-start.10 = (bf16[5,32,2304]{2,1,0:T(8,128)(2,1)}, bf16[5,32,2304]{2,1,0:T(8,128)(2,1)}, u32[]{:S(2)}, u32[]{:S(2)}) collective-permute-start(bf16[5,32,2304]{2,1,0:T(8,128)(2,1)} %join.3), channel_id=1, source_target_pairs={{0,16},{8,24},{16,0},{24,8},{1,17},{9,25},{17,1},{25,9},{2,18},{10... | collective-permute-start | bytes 2211848 | tf_op jit(solution)/shard_map/ppermute | solution.py:606
  38.4 10.0 %back.1 = (bf16[8,16,2304]{2,1,0:T(8,128)(2,1)}, bf16[144,3328]{1,0:T(8,128)(2,1)}, bf16[144,3328]{1,0:T(8,128)(2,1)}) custom-call(s32[1]{0:T(128)} %bitcast.1.me_ref, s32[1]{0:T(128)} %bitcast.2.part_ref, bf16[32,2304]{1,0:T(8,128)(2,1)} %get-tuple-element.22.refs_0_, bf16[32,2304]{1,0:T(8,128)(2,1)} %copy-done, ...), custom_call_target="tpu_custom_call" | custom-call | flops 11324620800 | bytes 1179648 | tf_op jit(solution)/shard_map/back/pallas_call | solution.py:436
  48.4 5.4 %all-to-all-start = ((bf16[8,16,2304]{2,1,0:T(8,128)(2,1)}), bf16[8,16,2304]{2,1,0:T(8,128)(2,1)}, u32[]{:S(2)}, u32[]{:S(2)}) async-start(bf16[8,16,2304]{2,1,0:T(8,128)(2,1)} %get-tuple-element.31), calls=%async_computation | async-start | bytes 1179648 | tf_op jit(solution)/shard_map/all_to_all | solution.py:610
  53.8 0.2 collective-permute-start.9
  54.0 0.3 collective-permute-start.11
  54.3 2.4 %collective-permute-done.9.refs_1_ = bf16[144,3328]{1,0:T(8,128)(2,1)} collective-permute-done((bf16[144,3328]{1,0:T(8,128)(2,1)}, bf16[144,3328]{1,0:T(8,128)(2,1)}, u32[]{:S(2)}, u32[]{:S(2)}) %collective-permute-start.9) | collective-permute-done | bytes 958496 | tf_op jit(solution)/shard_map/ppermute | solution.py:606
  56.7 1.1 %collective-permute-done.11.refs_5_ = bf16[5,32,2304]{2,1,0:T(8,128)(2,1)} collective-permute-done((bf16[5,32,2304]{2,1,0:T(8,128)(2,1)}, bf16[5,32,2304]{2,1,0:T(8,128)(2,1)}, u32[]{:S(2)}, u32[]{:S(2)}) %collective-permute-start.11) | collective-permute-done | bytes 737312 | tf_op jit(solution)/shard_map/ppermute | solution.py:606
  57.7 13.0 %weight_grads.1 = (f32[512,768]{1,0:T(8,128)}, f32[512,768]{1,0:T(8,128)}, f32[768,512]{1,0:T(8,128)}) custom-call(s32[1]{0:T(128)} %bitcast.2.part_ref, bf16[144,3328]{1,0:T(8,128)(2,1)} %get-tuple-element.32.refs_0_, bf16[144,3328]{1,0:T(8,128)(2,1)} %collective-permute-done.9.refs_1_, bf16[3,32,2304]{2,1,0:T(8,128)(2,1)} %collective-permute-done.7.refs_2_, ...), custom_call_target="tpu_custom_call" | custom-call | bytes 1179648 | tf_op jit(solution)/shard_map/weight_grads/pallas_call | solution.py:565
  70.7 2.4 %merge.1 = bf16[128,2048]{1,0:T(8,128)(2,1)} custom-call(s32[1,128]{1,0:T(1,128)} %bitcast.5, bf16[8,16,2304]{2,1,0:T(8,128)(2,1)} %all-to-all-done.back_ref), custom_call_target="tpu_custom_call" | custom-call | flops 134217728 | bytes 1048576 | tf_op jit(solution)/shard_map/merge/pallas_call | solution.py:270
  (10 shorter events, 0.0 us)
Async XLA Ops:
  3.5 9.1 %collective-permute-start = (bf16[32,2304]{1,0:T(8,128)(2,1)}, bf16[32,2304]{1,0:T(8,128)(2,1)S(1)}, u32[]{:S(2)}, u32[]{:S(2)}) collective-permute-start(bf16[32,2304]{1,0:T(8,128)(2,1)} %get-tuple-element.23), channel_id=1, source_target_pairs={{0,1},{1,0},{2,3},{3,2},{4,5},{5,4},{6,7},{7,6},{8,9},{9,8},{10,11... | collective-permute-start | bytes 442376 | tf_op jit(solution)/shard_map/ppermute | solution.py:606
  6.5 8.8 %collective-permute-start.1 = (bf16[32,2304]{1,0:T(8,128)(2,1)}, bf16[32,2304]{1,0:T(8,128)(2,1)}, u32[]{:S(2)}, u32[]{:S(2)}) collective-permute-start(bf16[32,2304]{1,0:T(8,128)(2,1)} %get-tuple-element.24), channel_id=1, source_target_pairs={{0,2},{1,3},{2,0},{3,1},{4,6},{5,7},{6,4},{7,5},{8,10},{9,11},{10,... | collective-permute-start | bytes 442376 | tf_op jit(solution)/shard_map/ppermute | solution.py:606
  8.1 20.6 %collective-permute-start.2 = (bf16[32,2304]{1,0:T(8,128)(2,1)}, bf16[32,2304]{1,0:T(8,128)(2,1)}, u32[]{:S(2)}, u32[]{:S(2)}) collective-permute-start(bf16[32,2304]{1,0:T(8,128)(2,1)} %get-tuple-element.25), channel_id=1, source_target_pairs={{0,4},{1,5},{2,6},{3,7},{4,0},{5,1},{6,2},{7,3},{8,12},{9,13},{10,... | collective-permute-start | bytes 442376 | tf_op jit(solution)/shard_map/ppermute | solution.py:606
  10.6 19.5 %collective-permute-start.3 = (bf16[32,2304]{1,0:T(8,128)(2,1)}, bf16[32,2304]{1,0:T(8,128)(2,1)}, u32[]{:S(2)}, u32[]{:S(2)}) collective-permute-start(bf16[32,2304]{1,0:T(8,128)(2,1)} %get-tuple-element.26), channel_id=1, source_target_pairs={{0,6},{1,7},{2,4},{3,5},{4,2},{5,3},{6,0},{7,1},{8,14},{9,15},{10,... | collective-permute-start | bytes 442376 | tf_op jit(solution)/shard_map/ppermute | solution.py:606
  10.9 24.0 %collective-permute-start.4 = (bf16[32,2304]{1,0:T(8,128)(2,1)}, bf16[32,2304]{1,0:T(8,128)(2,1)}, u32[]{:S(2)}, u32[]{:S(2)}) collective-permute-start(bf16[32,2304]{1,0:T(8,128)(2,1)} %get-tuple-element.27), channel_id=1, source_target_pairs={{0,5},{1,4},{2,7},{3,6},{4,1},{5,0},{6,3},{7,2},{8,13},{9,12},{10,... | collective-permute-start | bytes 442376 | tf_op jit(solution)/shard_map/ppermute | solution.py:606
  12.5 3.5 %copy-start = (bf16[32,2304]{1,0:T(8,128)(2,1)}, bf16[32,2304]{1,0:T(8,128)(2,1)S(1)}, u32[]{:S(2)}) copy-start(bf16[32,2304]{1,0:T(8,128)(2,1)S(1)} %collective-permute-done.refs_1_) | copy-start | bytes 442372
  12.5 22.3 %collective-permute-start.5 = (bf16[32,2304]{1,0:T(8,128)(2,1)}, bf16[32,2304]{1,0:T(8,128)(2,1)}, u32[]{:S(2)}, u32[]{:S(2)}) collective-permute-start(bf16[32,2304]{1,0:T(8,128)(2,1)} %get-tuple-element.28), channel_id=1, source_target_pairs={{0,7},{1,6},{2,5},{3,4},{4,3},{5,2},{6,1},{7,0},{8,15},{9,14},{10,... | collective-permute-start | bytes 442376 | tf_op jit(solution)/shard_map/ppermute | solution.py:606
  15.3 19.5 %collective-permute-start.6 = (bf16[32,2304]{1,0:T(8,128)(2,1)}, bf16[32,2304]{1,0:T(8,128)(2,1)}, u32[]{:S(2)}, u32[]{:S(2)}) collective-permute-start(bf16[32,2304]{1,0:T(8,128)(2,1)} %get-tuple-element.29), channel_id=1, source_target_pairs={{0,3},{1,2},{2,1},{3,0},{4,7},{5,6},{6,5},{7,4},{8,11},{9,10},{10,... | collective-permute-start | bytes 442376 | tf_op jit(solution)/shard_map/ppermute | solution.py:606
  28.6 9.8 %collective-permute-start.7 = (bf16[3,32,2304]{2,1,0:T(8,128)(2,1)}, bf16[3,32,2304]{2,1,0:T(8,128)(2,1)}, u32[]{:S(2)}, u32[]{:S(2)}) collective-permute-start(bf16[3,32,2304]{2,1,0:T(8,128)(2,1)} %join.2), channel_id=1, source_target_pairs={{0,16},{8,24},{16,0},{24,8},{1,17},{9,25},{17,1},{25,9},{2,18},{10... | collective-permute-start | bytes 1327112 | tf_op jit(solution)/shard_map/ppermute | solution.py:606
  36.8 17.2 %collective-permute-start.10 = (bf16[5,32,2304]{2,1,0:T(8,128)(2,1)}, bf16[5,32,2304]{2,1,0:T(8,128)(2,1)}, u32[]{:S(2)}, u32[]{:S(2)}) collective-permute-start(bf16[5,32,2304]{2,1,0:T(8,128)(2,1)} %join.3), channel_id=1, source_target_pairs={{0,16},{8,24},{16,0},{24,8},{1,17},{9,25},{17,1},{25,9},{2,18},{10... | collective-permute-start | bytes 2211848 | tf_op jit(solution)/shard_map/ppermute | solution.py:606
  38.4 10.0 %collective-permute-start.8 = (bf16[3,32,2304]{2,1,0:T(8,128)(2,1)}, bf16[3,32,2304]{2,1,0:T(8,128)(2,1)}, u32[]{:S(2)}, u32[]{:S(2)}) collective-permute-start(bf16[3,32,2304]{2,1,0:T(8,128)(2,1)} %collective-permute-done.7.refs_2_), channel_id=1, source_target_pairs={{0,8},{8,0},{16,24},{24,16},{1,9},{9,1},{17,25},{25,17},{2,10},{10... | collective-permute-start | bytes 1327112 | tf_op jit(solution)/shard_map/ppermute | solution.py:606
  48.4 22.3 %all-to-all-start = ((bf16[8,16,2304]{2,1,0:T(8,128)(2,1)}), bf16[8,16,2304]{2,1,0:T(8,128)(2,1)}, u32[]{:S(2)}, u32[]{:S(2)}) async-start(bf16[8,16,2304]{2,1,0:T(8,128)(2,1)} %get-tuple-element.31), calls=%async_computation | async-start | bytes 1179648 | tf_op jit(solution)/shard_map/all_to_all | solution.py:610
  53.8 2.9 %collective-permute-start.9 = (bf16[144,3328]{1,0:T(8,128)(2,1)}, bf16[144,3328]{1,0:T(8,128)(2,1)}, u32[]{:S(2)}, u32[]{:S(2)}) collective-permute-start(bf16[144,3328]{1,0:T(8,128)(2,1)} %get-tuple-element.33), channel_id=1, source_target_pairs={{0,8},{8,0},{16,24},{24,16},{1,9},{9,1},{17,25},{25,17},{2,10},{10... | collective-permute-start | bytes 2875400 | tf_op jit(solution)/shard_map/ppermute | solution.py:606
  54.0 3.7 %collective-permute-start.11 = (bf16[5,32,2304]{2,1,0:T(8,128)(2,1)}, bf16[5,32,2304]{2,1,0:T(8,128)(2,1)}, u32[]{:S(2)}, u32[]{:S(2)}) collective-permute-start(bf16[5,32,2304]{2,1,0:T(8,128)(2,1)} %collective-permute-done.10.refs_3_), channel_id=1, source_target_pairs={{0,8},{8,0},{16,24},{24,16},{1,9},{9,1},{17,25},{25,17},{2,10},{10... | collective-permute-start | bytes 2211848 | tf_op jit(solution)/shard_map/ppermute | solution.py:606
